TPU v7x, 32 devices: a whole 2x2x4 slice. The times are simulated.
32 devices in a mesh: grp: 2 (over y), row: 16 (over z, x, core), chan: 1.
Axes of the slice: x: 2, y: 2, z: 4, core: 2. Of those that a mesh axis runs over, the one named last changes fastest.
Arguments:
- pair: bfloat16 [256, 128, 128], P(('grp', 'row'), 'chan'), parts along dimension 0, may hold values from -150 to 150
- cotangent: bfloat16 [256, 128, 128], P(('grp', 'row'), 'chan'), parts along dimension 0, may hold values from -6 to 6
- residue_mask: int32 [256], P('grp'), parts along dimension 0, may hold values from 0 to 1, as said below
- ln_in_gain: float32 [128], replicated, may hold values from 0.5 to 1.5
- ln_in_bias: float32 [128], replicated, may hold values from -3 to 3
- w_proj: bfloat16 [128, 512], replicated, may hold values from -0.5 to 0.5
- w_gate: bfloat16 [128, 128], replicated, may hold values from -0.5 to 0.5
- ln_out_gain: float32 [128], replicated, may hold values from 0.5 to 1.5
- ln_out_bias: float32 [128], replicated, may hold values from -3 to 3
- w_out: bfloat16 [128, 128], replicated, may hold values from -0.5 to 0.5
Outputs:
- grad_pair: bfloat16 [256, 128, 128], P(('grp', 'row'), 'chan'), parts along dimension 0
There are 2 independent parts, one for each index of `grp`. A program takes and returns all parts, laid end to end along the dimension named above; an argument that names none is the same for every part. Nothing has to cross between parts.
Inputs may be any that keep to these rules, and one draw needn't show every extreme that they name: residue_mask is 1 on a leading run of residues and 0 on the rest; the count of ones is a multiple of 8, at least 64 and below 128.
All inputs are finite; a program needn't handle non-finite values.
Results may differ from a plain program's by a relative error of at most 0.0075.
Values may be sent and summed in bfloat16 or wider, within the bound.
No kernel may reach another device: no remote copies, remote signals or barrier semaphores. Data moves between devices by JAX's collectives and lax.ppermute only.
A program may use at most 64 MiB of HBM per device.

v0:
```python
import jax
import jax.numpy as jnp
from jax import lax
from jax.sharding import PartitionSpec as P


def normalize(values, reduce_axis):
    mean_value = jnp.mean(values, axis=reduce_axis, keepdims=True)
    centered = values - mean_value
    variance = jnp.mean(centered * centered, axis=reduce_axis, keepdims=True)
    inv_std = lax.rsqrt(variance + 1e-05)
    return (centered * inv_std, inv_std)


def norm_backward(upstream, normed, inv_std, reduce_axis):
    mean_grad = jnp.mean(upstream, axis=reduce_axis, keepdims=True)
    mean_cross = jnp.mean(upstream * normed, axis=reduce_axis, keepdims=True)
    return inv_std * (upstream - mean_grad - normed * mean_cross)


def shards(
    pair,
    cotangent,
    residue_mask,
    ln_in_gain,
    ln_in_bias,
    w_proj,
    w_gate,
    ln_out_gain,
    ln_out_bias,
    w_out,
):
    local_rows = pair.shape[0]
    local_cols = pair.shape[1]
    hidden = w_out.shape[0]
    chan_index = lax.axis_index("chan")
    row_start = lax.axis_index("row") * local_rows
    col_start = chan_index * local_cols
    mask_float = residue_mask.astype(jnp.float32)
    row_mask = lax.dynamic_slice_in_dim(mask_float, row_start, local_rows)
    col_mask = lax.dynamic_slice_in_dim(mask_float, col_start, local_cols)
    cell_mask = (row_mask[:, None] * col_mask[None, :])[None]
    normed, inv_std = normalize(pair.astype(jnp.float32), -1)
    normed_pair = (normed * ln_in_gain + ln_in_bias).astype(jnp.bfloat16)
    projected = jnp.einsum("rmc,ch->hrm", normed_pair, w_proj, preferred_element_type=jnp.float32)
    left_panel = (
        cell_mask * jax.nn.sigmoid(projected[:hidden]) * projected[hidden : 2 * hidden]
    ).astype(jnp.bfloat16)
    right_panel = (
        cell_mask * jax.nn.sigmoid(projected[2 * hidden : 3 * hidden]) * projected[3 * hidden :]
    ).astype(jnp.bfloat16)
    panels = lax.all_to_all(
        jnp.stack([left_panel, right_panel]), "row", split_axis=1, concat_axis=2, tiled=True
    )
    left_all = panels[0]
    right_all = panels[1]
    right_rows = lax.all_to_all(right_all, "chan", split_axis=1, concat_axis=2, tiled=True)
    partner = right_rows
    tri_part = jnp.einsum(
        "gik,gjk->gij",
        lax.all_gather(left_all, "chan", axis=2, tiled=True),
        partner,
        preferred_element_type=jnp.float32,
    ).astype(jnp.bfloat16)
    tri_cells = lax.all_to_all(tri_part, "row", split_axis=1, concat_axis=0, tiled=True)
    tri_hat, inv_tri = normalize(tri_cells.astype(jnp.float32), 0)
    scaled = (tri_hat * ln_out_gain[:, None, None] + ln_out_bias[:, None, None]).astype(
        jnp.bfloat16
    )
    proj_out = jnp.einsum("hrm,hc->rmc", scaled, w_out, preferred_element_type=jnp.float32)
    gate_value = jax.nn.sigmoid(
        jnp.einsum("rmc,cd->rmd", normed_pair, w_gate, preferred_element_type=jnp.float32)
    )
    cot_float = cotangent.astype(jnp.float32)
    d_gate_pre = (cot_float * proj_out * gate_value * (1.0 - gate_value)).astype(jnp.bfloat16)
    d_scaled = (cot_float * gate_value).astype(jnp.bfloat16)
    d_hat = jnp.einsum("rmc,hc->hrm", d_scaled, w_out, preferred_element_type=jnp.float32)
    d_hat = d_hat * ln_out_gain[:, None, None]
    d_tri = norm_backward(d_hat, tri_hat, inv_tri, 0).astype(jnp.bfloat16)
    d_tri_all = lax.all_to_all(d_tri, "row", split_axis=0, concat_axis=1, tiled=True)
    panel_piece = lax.all_gather(d_tri_all, "chan", axis=2, tiled=True)
    partner = right_all
    d_left = jnp.einsum("gij,gjk->gik", panel_piece, partner, preferred_element_type=jnp.float32)
    contribution = jnp.einsum(
        "gij,gik->gjk", panel_piece, left_all, preferred_element_type=jnp.float32
    )
    d_right = contribution
    d_left, d_right = (d_left, d_right)
    d_stack = jnp.stack([d_left, d_right]).astype(jnp.bfloat16)
    d_panels = lax.all_to_all(d_stack, "row", split_axis=2, concat_axis=1, tiled=True)

    def gating(d_value, gate_proj, value_proj):
        sigmoid_val = jax.nn.sigmoid(gate_proj)
        masked_grad = d_value.astype(jnp.float32) * cell_mask
        return (
            masked_grad * value_proj * sigmoid_val * (1.0 - sigmoid_val),
            masked_grad * sigmoid_val,
        )

    gate_left, value_left = gating(d_panels[0], projected[:hidden], projected[hidden : 2 * hidden])
    gate_right, value_right = gating(
        d_panels[1], projected[2 * hidden : 3 * hidden], projected[3 * hidden :]
    )
    d_proj = jnp.concatenate([gate_left, value_left, gate_right, value_right], axis=0).astype(
        jnp.bfloat16
    )
    d_normed = jnp.einsum("hrm,ch->rmc", d_proj, w_proj, preferred_element_type=jnp.float32)
    d_normed = d_normed + jnp.einsum(
        "rmd,cd->rmc", d_gate_pre, w_gate, preferred_element_type=jnp.float32
    )
    d_input = d_normed * ln_in_gain
    return norm_backward(d_input, normed, inv_std, -1).astype(jnp.bfloat16)


def solution(mesh):
    return jax.shard_map(
        shards,
        mesh=mesh,
        in_specs=(
            P(("grp", "row"), "chan", None),
            P(("grp", "row"), "chan", None),
            P("grp"),
            P(),
            P(),
            P(),
            P(),
            P(),
            P(),
            P(),
        ),
        out_specs=P(("grp", "row"), "chan", None),
        check_vma=False,
    )
```

profile of v0, /device:TPU:0, one launch (start us, length us, event | category | flops | bytes accessed | tf_op | source)
XLA Modules:
  0.0 83.3 jit_solution(11153690040952621570)
XLA Ops:
  0.0 0.7 convert_element_type.69
  0.8 1.1 %copy.54 = bf16[8,128,128]{1,2,0:T(8,128)(2,1)S(1)} copy(bf16[8,128,128]{2,1,0:T(8,128)(2,1)} %param.10) | data formatting | bytes 524288 | tf_op args[0]
  2.2 1.2 %convolution_bitcast_fusion = f32[512,8,128]{0,2,1:T(8,128)S(1)} fusion(bf16[128,512]{1,0:T(8,128)(2,1)S(1)} %copy-done, bf16[8,128,128]{1,2,0:T(8,128)(2,1)S(1)} %copy.54, f32[128]{0:T(128)} %param.14, f32[128]{0:T(128)} %param.13, f32[8,128]{1,0:T(8,128)S(1)} %add_rsqrt_fusion.1, f32[8,128]{1,0:T(8,128)S(1)} %broadcast_multiply_fusion.6), kind=kOutput, calls=%fused_computation | convolution fusion | flops 135004160 | bytes 2499584 | tf_op jit(solution)/shard_map/rmc,ch->hrm/dot_general | solution.py:45
  3.8 0.4 copy.56
  4.2 21.6 %all_to_all.57 = bf16[2,128,8,128]{3,2,0,1:T(8,128)(2,1)S(1)} all-to-all(bf16[2,128,8,128]{3,2,0,1:T(8,128)(2,1)S(1)} %copy.56), channel_id=1, replica_groups=mesh['grp'=2,'row'=16,'chan'=1] {'row'}, dimensions={1} | all-to-all | bytes 1048576 | tf_op jit(solution)/shard_map/all_to_all | solution.py:52
  26.2 0.9 %copy.60 = bf16[8,128,128]{2,0,1:T(8,128)(2,1)} copy(bf16[8,128,128]{2,1,0:T(8,128)(2,1)S(1)} %convolution_convert_fusion.2) | data formatting | bytes 524288 | tf_op jit(solution)/shard_map/convert_element_type | solution.py:64
  27.1 4.1 %all-to-all-start.1 = ((bf16[8,128,128]{2,0,1:T(8,128)(2,1)}), bf16[8,128,128]{2,0,1:T(8,128)(2,1)S(1)}, u32[]{:S(2)}, u32[]{:S(2)}) async-start(bf16[8,128,128]{2,0,1:T(8,128)(2,1)} %copy.60), calls=%async_computation.1 | async-start | bytes 524288 | tf_op jit(solution)/shard_map/all_to_all | solution.py:65
  31.2 2.0 %fusion.4 = f32[8,128,128]{2,1,0:T(8,128)} fusion(bf16[128,128]{1,0:T(8,128)(2,1)} %param.16, bf16[8,128,128]{1,2,0:T(8,128)(2,1)S(1)} %copy.54, f32[128]{0:T(128)S(1)} %copy-done.7, f32[128]{0:T(128)} %param.13, f32[8,128]{1,0:T(8,128)S(1)} %add_rsqrt_fusion.1, f32[8,128]{1,0:T(8,128)S(1)} %broadcast_multiply_fusion.6), kind=kOutput, calls=%fused_computation.9 | convolution fusion | flops 34734080 | bytes 828416 | tf_op jit(solution)/shard_map/rmc,cd->rmd/dot_general | solution.py:72
  33.3 8.0 %all-to-all-done.1 = bf16[8,128,128]{2,0,1:T(8,128)(2,1)S(1)} async-done(((bf16[8,128,128]{2,0,1:T(8,128)(2,1)}), bf16[8,128,128]{2,0,1:T(8,128)(2,1)S(1)}, u32[]{:S(2)}, u32[]{:S(2)}) %all-to-all-start.1) | async-done | bytes 262176 | tf_op jit(solution)/shard_map/all_to_all | solution.py:65
  41.4 0.8 %copy-done.1 = f32[8,128,128]{2,1,0:T(8,128)S(1)} copy-done((f32[8,128,128]{2,1,0:T(8,128)S(1)}, f32[8,128,128]{2,1,0:T(8,128)}, u32[]{:S(2)}) %copy-start.1) | copy-done | bytes 524312
  42.3 1.0 %fusion.78 = (f32[8,128]{1,0:T(8,128)S(1)}, f32[8,128]{1,0:T(8,128)S(1)}, f32[128,8,128]{2,0,1:T(8,128)S(1)}) fusion(f32[8,128]{1,0:T(8,128)S(1)} %add_rsqrt_fusion, f32[8,128]{1,0:T(8,128)S(1)} %broadcast_multiply_fusion.5, f32[128]{0:T(128)} %param.17, bf16[128,128]{1,0:T(8,128)(2,1)} %param.19, f32[8,128,128]{2,1,0:T(8,128)S(1)} %copy-done.1, ...), kind=kOutput, calls=%fused_computation.110 | convolution fusion | flops 34863104 | bytes 1622528 | tf_op jit(solution)/shard_map/rmc,hc->hrm/dot_general | solution.py:77
  43.7 12.8 %all_to_all.58 = bf16[128,8,128]{2,1,0:T(8,128)(2,1)S(1)} all-to-all(bf16[128,8,128]{2,1,0:T(8,128)(2,1)S(1)} %copy.63), channel_id=1, replica_groups=mesh['grp'=2,'row'=16,'chan'=1] {'row'}, dimensions={0} | all-to-all | bytes 524288 | tf_op jit(solution)/shard_map/all_to_all | solution.py:80
  57.1 1.2 %copy.66 = bf16[2,8,128,128]{3,1,0,2:T(8,128)(2,1)} copy(bf16[2,8,128,128]{3,2,1,0:T(8,128)(2,1)S(1)} %pad_maximum_fusion.1) | data formatting | bytes 1048576 | tf_op jit(solution)/shard_map/stack | solution.py:89
  58.2 3.6 %all-to-all-start.3 = ((bf16[2,8,128,128]{3,1,0,2:T(8,128)(2,1)}), bf16[2,8,128,128]{3,1,0,2:T(8,128)(2,1)S(1)}, u32[]{:S(2)}, u32[]{:S(2)}) async-start(bf16[2,8,128,128]{3,1,0,2:T(8,128)(2,1)} %copy.66), calls=%async_computation.3 | async-start | bytes 1048576 | tf_op jit(solution)/shard_map/all_to_all | solution.py:90
  61.8 2.4 %fusion.10 = f32[8,128,128]{1,2,0:T(8,128)} fusion(f32[8,128,128]{2,1,0:T(8,128)} %fusion.4, bf16[8,128,128]{2,1,0:T(8,128)(2,1)S(1)} %copy-done.3, f32[128]{0:T(128)} %param.18, f32[128]{0:T(128)} %param.17, f32[8,128]{1,0:T(8,128)S(1)} %broadcast_multiply_fusion.5, f32[8,128]{1,0:T(8,128)S(1)} %add_rsqrt_fusion, bf16[128,128]{1,0:T(8,128)(2,1)} %param.19, ...), kind=kOutput, calls=%fused_computation.18 | convolution fusion | flops 68681728 | bytes 1647616 | tf_op jit(solution)/shard_map/rmd,cd->rmc/dot_general | solution.py:108
  64.2 12.0 %all-to-all-done.3 = bf16[2,8,128,128]{3,1,0,2:T(8,128)(2,1)S(1)} async-done(((bf16[2,8,128,128]{3,1,0,2:T(8,128)(2,1)}), bf16[2,8,128,128]{3,1,0,2:T(8,128)(2,1)S(1)}, u32[]{:S(2)}, u32[]{:S(2)}) %all-to-all-start.3) | async-done | bytes 524320 | tf_op jit(solution)/shard_map/all_to_all | solution.py:90
  76.5 0.9 %copy.68 = f32[1,16,8,8,128]{4,3,2,1,0:T(8,128)} copy(f32[1,16,8,8,128]{4,3,1,2,0:T(8,128)S(1)} %get-tuple-element.17) | data formatting | bytes 1048576 | tf_op jit(solution)/shard_map/convert_element_type | solution.py:94
  77.3 1.2 %copy.69 = f32[128,8,128]{0,2,1:T(8,128)S(1)} copy(f32[128,8,128]{2,1,0:T(8,128)} %bitcast.92) | data formatting | bytes 1048576 | tf_op jit(solution)/shard_map/convert_element_type | solution.py:94
  78.6 0.9 %copy.70 = f32[1,16,8,8,128]{4,3,2,1,0:T(8,128)} copy(f32[1,16,8,8,128]{4,3,1,2,0:T(8,128)S(1)} %get-tuple-element.18) | data formatting | bytes 1048576 | tf_op jit(solution)/shard_map/convert_element_type | solution.py:94
  79.4 1.2 %copy.71 = f32[128,8,128]{0,2,1:T(8,128)S(1)} copy(f32[128,8,128]{2,1,0:T(8,128)} %bitcast.93) | data formatting | bytes 1048576 | tf_op jit(solution)/shard_map/convert_element_type | solution.py:94
  80.7 0.5 multiply_convert_fusion.3
  81.2 0.5 copy-done.4
  81.7 0.5 fusion.77
  82.4 0.8 %copy.74 = bf16[8,128,128]{2,1,0:T(8,128)(2,1)} copy(bf16[8,128,128]{1,2,0:T(8,128)(2,1)S(1)} %fusion.29) | data formatting | bytes 524288 | tf_op jit(solution)/shard_map/convert_element_type | solution.py:112
  (43 shorter events, 2.5 us)
Async XLA Ops:
  0.0 2.1 %copy-start = (bf16[128,512]{1,0:T(8,128)(2,1)S(1)}, bf16[128,512]{1,0:T(8,128)(2,1)}, u32[]{:S(2)}) copy-start(bf16[128,512]{1,0:T(8,128)(2,1)} %param.15) | copy-start | bytes 393220
  2.1 29.0 %copy-start.5 = (f32[8,128]{1,0:T(8,128)}, f32[8,128]{1,0:T(8,128)S(1)}, u32[]{:S(2)}) copy-start(f32[8,128]{1,0:T(8,128)S(1)} %add_rsqrt_fusion.1) | copy-start | bytes 12292
  25.8 5.4 %copy-start.7 = (f32[128]{0:T(128)S(1)}, f32[128]{0:T(128)}, u32[]{:S(2)}) copy-start(f32[128]{0:T(128)} %param.14) | copy-start | bytes 1540
  27.1 14.2 %all-to-all-start.1 = ((bf16[8,128,128]{2,0,1:T(8,128)(2,1)}), bf16[8,128,128]{2,0,1:T(8,128)(2,1)S(1)}, u32[]{:S(2)}, u32[]{:S(2)}) async-start(bf16[8,128,128]{2,0,1:T(8,128)(2,1)} %copy.60), calls=%async_computation.1 | async-start | bytes 524288 | tf_op jit(solution)/shard_map/all_to_all | solution.py:65
  31.2 10.2 %copy-start.2 = (bf16[8,128,128]{2,1,0:T(8,128)(2,1)S(1)}, bf16[8,128,128]{2,1,0:T(8,128)(2,1)}, u32[]{:S(2)}) copy-start(bf16[8,128,128]{2,1,0:T(8,128)(2,1)} %param.11) | copy-start | bytes 786436
  41.2 1.0 %copy-start.1 = (f32[8,128,128]{2,1,0:T(8,128)S(1)}, f32[8,128,128]{2,1,0:T(8,128)}, u32[]{:S(2)}) copy-start(f32[8,128,128]{2,1,0:T(8,128)} %fusion.4) | copy-start | bytes 1572868
  57.0 4.8 %copy-start.3 = (bf16[8,128,128]{2,1,0:T(8,128)(2,1)S(1)}, bf16[8,128,128]{2,1,0:T(8,128)(2,1)}, u32[]{:S(2)}) copy-start(bf16[8,128,128]{2,1,0:T(8,128)(2,1)} %param.11) | copy-start | bytes 786436
  58.2 18.0 %all-to-all-start.3 = ((bf16[2,8,128,128]{3,1,0,2:T(8,128)(2,1)}), bf16[2,8,128,128]{3,1,0,2:T(8,128)(2,1)S(1)}, u32[]{:S(2)}, u32[]{:S(2)}) async-start(bf16[2,8,128,128]{3,1,0,2:T(8,128)(2,1)} %copy.66), calls=%async_computation.3 | async-start | bytes 1048576 | tf_op jit(solution)/shard_map/all_to_all | solution.py:90
  80.7 1.0 %copy-start.4 = (f32[8,128,128]{1,2,0:T(8,128)S(1)}, f32[8,128,128]{1,2,0:T(8,128)}, u32[]{:S(2)}) copy-start(f32[8,128,128]{1,2,0:T(8,128)} %fusion.10) | copy-start | bytes 1572868
  80.7 1.0 %copy-start.6 = (f32[8,128]{1,0:T(8,128)S(1)}, f32[8,128]{1,0:T(8,128)}, u32[]{:S(2)}) copy-start(f32[8,128]{1,0:T(8,128)} %copy-done.5) | copy-start | bytes 12292
  80.7 1.0 %copy-start.8 = (f32[128]{0:T(128)S(1)}, f32[128]{0:T(128)}, u32[]{:S(2)}) copy-start(f32[128]{0:T(128)} %param.13) | copy-start | bytes 1540
where the time goes:
time: 84 us; the launch traced here: 83.3 us
  blocking collectives  34.4 us (41%)
  waiting for transfers between devices  20 us (24%)
  local copies, waits for them, and re-layouts  10.5 us (12%)
  matrix products  8.02 us (10%)
  starting transfers between devices  7.67 us (9%)
  other arithmetic  2.38 us (3%)
    all_to_all x1, blocking collectives, shards(): lax.all_to_all(jnp.stack([left_panel, right_panel]), 'row', split_axis=1,...  21.6 us
    all_to_all x1, blocking collectives, shards(): lax.all_to_all(d_tri, 'row', split_axis=0, concat_axis=1, tiled=True)  12.8 us
    all_to_all x1, waiting for transfers between devices, shards(): lax.all_to_all(d_stack, 'row', split_axis=2, concat_axis=1, tiled=True)  12 us
    all_to_all x1, waiting for transfers between devices, shards(): lax.all_to_all(tri_part, 'row', split_axis=1, concat_axis=0, tiled=True)  7.97 us
    convert_element_type x4, local copies, waits for them, and re-layouts, gating(): masked_grad = d_value.astype(jnp.float32) * cell_mask  4.2 us
    all_to_all x1, starting transfers between devices, shards(): lax.all_to_all(tri_part, 'row', split_axis=1, concat_axis=0, tiled=True)  4.1 us
    all_to_all x1, starting transfers between devices, shards(): lax.all_to_all(d_stack, 'row', split_axis=2, concat_axis=1, tiled=True)  3.57 us
    unnamed x19, local copies, waits for them, and re-layouts  2.48 us
  transfers between devices with their start and end apart: 2, of which 2 were waited for; matrix products, arithmetic and copies ran while one was open for 5% of the time, Pallas kernels for 0%

commit v1 on v0

--- a/solution.py
+++ b/solution.py
@@ -16,6 +16,25 @@
     mean_grad = jnp.mean(upstream, axis=reduce_axis, keepdims=True)
     mean_cross = jnp.mean(upstream * normed, axis=reduce_axis, keepdims=True)
     return inv_std * (upstream - mean_grad - normed * mean_cross)
+
+
+def exchange(values, split_axis, concat_axis):
+    count = lax.axis_size("row")
+    me = lax.axis_index("row")
+    size = values.shape[split_axis] // count
+    received = [lax.dynamic_slice_in_dim(values, me * size, size, split_axis)]
+    for step in range(1, count):
+        target = lax.rem(me + step, count)
+        piece = lax.dynamic_slice_in_dim(values, target * size, size, split_axis)
+        received.append(lax.ppermute(piece, "row", [(d, (d + step) % count) for d in range(count)]))
+    width = values.shape[concat_axis]
+    shape = list(received[0].shape)
+    shape[concat_axis] = width * count
+    result = jnp.zeros(shape, values.dtype)
+    for step in range(count):
+        source = lax.rem(me - step + count, count)
+        result = lax.dynamic_update_slice_in_dim(result, received[step], source * width, concat_axis)
+    return result
 
 
 def shards(
@@ -49,9 +68,7 @@
     right_panel = (
         cell_mask * jax.nn.sigmoid(projected[2 * hidden : 3 * hidden]) * projected[3 * hidden :]
     ).astype(jnp.bfloat16)
-    panels = lax.all_to_all(
-        jnp.stack([left_panel, right_panel]), "row", split_axis=1, concat_axis=2, tiled=True
-    )
+    panels = exchange(jnp.stack([left_panel, right_panel]), 1, 2)
     left_all = panels[0]
     right_all = panels[1]
     right_rows = lax.all_to_all(right_all, "chan", split_axis=1, concat_axis=2, tiled=True)
@@ -62,7 +79,7 @@
         partner,
         preferred_element_type=jnp.float32,
     ).astype(jnp.bfloat16)
-    tri_cells = lax.all_to_all(tri_part, "row", split_axis=1, concat_axis=0, tiled=True)
+    tri_cells = exchange(tri_part, 1, 0)
     tri_hat, inv_tri = normalize(tri_cells.astype(jnp.float32), 0)
     scaled = (tri_hat * ln_out_gain[:, None, None] + ln_out_bias[:, None, None]).astype(
         jnp.bfloat16
@@ -77,7 +94,7 @@
     d_hat = jnp.einsum("rmc,hc->hrm", d_scaled, w_out, preferred_element_type=jnp.float32)
     d_hat = d_hat * ln_out_gain[:, None, None]
     d_tri = norm_backward(d_hat, tri_hat, inv_tri, 0).astype(jnp.bfloat16)
-    d_tri_all = lax.all_to_all(d_tri, "row", split_axis=0, concat_axis=1, tiled=True)
+    d_tri_all = exchange(d_tri, 0, 1)
     panel_piece = lax.all_gather(d_tri_all, "chan", axis=2, tiled=True)
     partner = right_all
     d_left = jnp.einsum("gij,gjk->gik", panel_piece, partner, preferred_element_type=jnp.float32)
@@ -87,7 +104,7 @@
     d_right = contribution
     d_left, d_right = (d_left, d_right)
     d_stack = jnp.stack([d_left, d_right]).astype(jnp.bfloat16)
-    d_panels = lax.all_to_all(d_stack, "row", split_axis=2, concat_axis=1, tiled=True)
+    d_panels = exchange(d_stack, 2, 1)
 
     def gating(d_value, gate_proj, value_proj):
         sigmoid_val = jax.nn.sigmoid(gate_proj)

time: 84 us -> 681 us (8.11)
  the two profiles are of different devices: /device:TPU:0 before, /device:TPU:27 now
where the time goes in v1:
time: 681 us; the launch traced here: 673 us
  starting transfers between devices  272 us (40%)
  local copies, waits for them, and re-layouts  250 us (37%)
  waiting for transfers between devices  131 us (19%)
  other arithmetic  11.3 us (2%)
  matrix products  7.99 us (1%)
    ppermute x60, starting transfers between devices, exchange(): lax.ppermute(piece, 'row', [(d, (d + step) % count) for d in range(count)])  272 us
    dynamic_update_slice x64, local copies, waits for them, and re-layouts, exchange(): lax.dynamic_update_slice_in_dim(result, received[step], source * width, c...  177 us
    ppermute x60, waiting for transfers between devices, exchange(): lax.ppermute(piece, 'row', [(d, (d + step) % count) for d in range(count)])  131 us
    ppermute x30, local copies, waits for them, and re-layouts, exchange(): lax.ppermute(piece, 'row', [(d, (d + step) % count) for d in range(count)])  44.5 us
    unnamed x59, local copies, waits for them, and re-layouts  25.3 us
  transfers between devices with their start and end apart: 60, of which 15 were waited for; matrix products, arithmetic and copies ran while one was open for 34% of the time, Pallas kernels for 0%

profile of v1, /device:TPU:27, one launch (start us, length us, event | category | flops | bytes accessed | tf_op | source)
XLA Modules:
  0.0 673.3 jit_solution(4378434649666231231)
XLA Ops:
  22.2 9.5 %collective-permute-done.1 = bf16[2,8,8,128]{1,3,2,0:T(8,128)(2,1)} collective-permute-done((bf16[2,8,8,128]{1,3,2,0:T(8,128)(2,1)}, bf16[2,8,8,128]{1,3,2,0:T(8,128)(2,1)}, u32[]{:S(2)}, u32[]{:S(2)}) %collective-permute-start.1) | collective-permute-done | bytes 32800 | tf_op jit(solution)/shard_map/ppermute | solution.py:29
  32.9 7.0 %collective-permute-done.2 = bf16[2,8,8,128]{1,3,2,0:T(8,128)(2,1)} collective-permute-done((bf16[2,8,8,128]{1,3,2,0:T(8,128)(2,1)}, bf16[2,8,8,128]{1,3,2,0:T(8,128)(2,1)}, u32[]{:S(2)}, u32[]{:S(2)}) %collective-permute-start.2) | collective-permute-done | bytes 32800 | tf_op jit(solution)/shard_map/ppermute | solution.py:29
  43.3 10.5 %collective-permute-done.3 = bf16[2,8,8,128]{1,3,2,0:T(8,128)(2,1)} collective-permute-done((bf16[2,8,8,128]{1,3,2,0:T(8,128)(2,1)}, bf16[2,8,8,128]{1,3,2,0:T(8,128)(2,1)}, u32[]{:S(2)}, u32[]{:S(2)}) %collective-permute-start.3) | collective-permute-done | bytes 32800 | tf_op jit(solution)/shard_map/ppermute | solution.py:29
  55.1 7.3 %collective-permute-done.4 = bf16[2,8,8,128]{1,3,2,0:T(8,128)(2,1)} collective-permute-done((bf16[2,8,8,128]{1,3,2,0:T(8,128)(2,1)}, bf16[2,8,8,128]{1,3,2,0:T(8,128)(2,1)}, u32[]{:S(2)}, u32[]{:S(2)}) %collective-permute-start.4) | collective-permute-done | bytes 32800 | tf_op jit(solution)/shard_map/ppermute | solution.py:29
  65.0 8.6 %collective-permute-done.5 = bf16[2,8,8,128]{1,3,2,0:T(8,128)(2,1)} collective-permute-done((bf16[2,8,8,128]{1,3,2,0:T(8,128)(2,1)}, bf16[2,8,8,128]{1,3,2,0:T(8,128)(2,1)}, u32[]{:S(2)}, u32[]{:S(2)}) %collective-permute-start.5) | collective-permute-done | bytes 32800 | tf_op jit(solution)/shard_map/ppermute | solution.py:29
  73.6 36.1 %collective-permute-start.10 = (bf16[2,8,8,128]{1,3,2,0:T(8,128)(2,1)}, bf16[2,8,8,128]{1,3,2,0:T(8,128)(2,1)}, u32[]{:S(2)}, u32[]{:S(2)}) collective-permute-start(bf16[2,8,8,128]{1,3,2,0:T(8,128)(2,1)} %get-tuple-element.45), channel_id=1, source_target_pairs={{0,11},{1,12},{2,13},{3,14},{4,15},{5,0},{6,1},{7,2},{8,3},{9,4},{... | collective-permute-start | bytes 98312 | tf_op jit(solution)/shard_map/ppermute | solution.py:29
  112.3 24.0 %collective-permute-start.11 = (bf16[2,8,8,128]{1,3,2,0:T(8,128)(2,1)}, bf16[2,8,8,128]{1,3,2,0:T(8,128)(2,1)}, u32[]{:S(2)}, u32[]{:S(2)}) collective-permute-start(bf16[2,8,8,128]{1,3,2,0:T(8,128)(2,1)} %get-tuple-element.46), channel_id=1, source_target_pairs={{0,12},{1,13},{2,14},{3,15},{4,0},{5,1},{6,2},{7,3},{8,4},{9,5},{1... | collective-permute-start | bytes 98312 | tf_op jit(solution)/shard_map/ppermute | solution.py:29
  138.9 44.3 %collective-permute-done.7 = bf16[2,8,8,128]{1,3,2,0:T(8,128)(2,1)} collective-permute-done((bf16[2,8,8,128]{1,3,2,0:T(8,128)(2,1)}, bf16[2,8,8,128]{1,3,2,0:T(8,128)(2,1)}, u32[]{:S(2)}, u32[]{:S(2)}) %collective-permute-start.7) | collective-permute-done | bytes 32800 | tf_op jit(solution)/shard_map/ppermute | solution.py:29
  330.9 14.1 %dynamic_update_slice.239 = bf16[8,128,128]{1,2,0:T(8,128)(2,1)S(1)} dynamic-update-slice(bf16[8,128,128]{1,2,0:T(8,128)(2,1)S(1)} %dynamic_update_slice.238, bf16[8,8,128]{1,2,0:T(8,128)(2,1)} %copy.117, s32[]{:T(128)} %constant.139.clone.1, s32[]{:T(128)S(6)} %select_n.36, s32[]{:T(128)} %constant.139.clone.1) | dynamic-update-slice | bytes 32772 | tf_op jit(solution)/shard_map/dynamic_update_slice | solution.py:36
  367.7 8.2 %collective-permute-done.54 = bf16[2,8,8,128]{1,3,2,0:T(8,128)(2,1)} collective-permute-done((bf16[2,8,8,128]{1,3,2,0:T(8,128)(2,1)}, bf16[2,8,8,128]{1,3,2,0:T(8,128)(2,1)}, u32[]{:S(2)}, u32[]{:S(2)}) %collective-permute-start.54) | collective-permute-done | bytes 32800 | tf_op jit(solution)/shard_map/ppermute | solution.py:29
  375.9 28.7 %collective-permute-start.48 = (bf16[2,8,8,128]{1,3,2,0:T(8,128)(2,1)}, bf16[2,8,8,128]{1,3,2,0:T(8,128)(2,1)}, u32[]{:S(2)}, u32[]{:S(2)}) collective-permute-start(bf16[2,8,8,128]{1,3,2,0:T(8,128)(2,1)} %copy.145), channel_id=1, source_target_pairs={{0,4},{1,5},{2,6},{3,7},{4,8},{5,9},{6,10},{7,11},{8,12},{9,13},{1... | collective-permute-start | bytes 98312 | tf_op jit(solution)/shard_map/ppermute | solution.py:29
  409.7 36.9 %collective-permute-start.53 = (bf16[2,8,8,128]{1,3,2,0:T(8,128)(2,1)}, bf16[2,8,8,128]{1,3,2,0:T(8,128)(2,1)}, u32[]{:S(2)}, u32[]{:S(2)}) collective-permute-start(bf16[2,8,8,128]{1,3,2,0:T(8,128)(2,1)} %copy.150), channel_id=1, source_target_pairs={{0,9},{1,10},{2,11},{3,12},{4,13},{5,14},{6,15},{7,0},{8,1},{9,2},... | collective-permute-start | bytes 98312 | tf_op jit(solution)/shard_map/ppermute | solution.py:29
  462.8 44.5 %collective-permute-start.57 = (bf16[2,8,8,128]{1,3,2,0:T(8,128)(2,1)}, bf16[2,8,8,128]{1,3,2,0:T(8,128)(2,1)}, u32[]{:S(2)}, u32[]{:S(2)}) collective-permute-start(bf16[2,8,8,128]{1,3,2,0:T(8,128)(2,1)} %copy.154), channel_id=1, source_target_pairs={{0,13},{1,14},{2,15},{3,0},{4,1},{5,2},{6,3},{7,4},{8,5},{9,6},{10... | collective-permute-start | bytes 98312 | tf_op jit(solution)/shard_map/ppermute | solution.py:29
  507.4 21.7 %collective-permute-done.52 = bf16[2,8,8,128]{1,3,2,0:T(8,128)(2,1)} collective-permute-done((bf16[2,8,8,128]{1,3,2,0:T(8,128)(2,1)}, bf16[2,8,8,128]{1,3,2,0:T(8,128)(2,1)}, u32[]{:S(2)}, u32[]{:S(2)}) %collective-permute-start.52) | collective-permute-done | bytes 32800 | tf_op jit(solution)/shard_map/ppermute | solution.py:29
  529.1 17.0 %collective-permute-start.58 = (bf16[2,8,8,128]{1,3,2,0:T(8,128)(2,1)}, bf16[2,8,8,128]{1,3,2,0:T(8,128)(2,1)}, u32[]{:S(2)}, u32[]{:S(2)}) collective-permute-start(bf16[2,8,8,128]{1,3,2,0:T(8,128)(2,1)} %copy.155), channel_id=1, source_target_pairs={{0,14},{1,15},{2,0},{3,1},{4,2},{5,3},{6,4},{7,5},{8,6},{9,7},{10,... | collective-permute-start | bytes 98312 | tf_op jit(solution)/shard_map/ppermute | solution.py:29
  546.1 17.3 %collective-permute-start.59 = (bf16[2,8,8,128]{1,3,2,0:T(8,128)(2,1)}, bf16[2,8,8,128]{1,3,2,0:T(8,128)(2,1)}, u32[]{:S(2)}, u32[]{:S(2)}) collective-permute-start(bf16[2,8,8,128]{1,3,2,0:T(8,128)(2,1)} %copy.156), channel_id=1, source_target_pairs={{0,15},{1,0},{2,1},{3,2},{4,3},{5,4},{6,5},{7,6},{8,7},{9,8},{10,9... | collective-permute-start | bytes 98312 | tf_op jit(solution)/shard_map/ppermute | solution.py:29
  571.8 6.7 dynamic_update_slice.241
  578.5 6.7 dynamic_update_slice.242
  591.9 6.7 dynamic_update_slice.244
  598.7 6.7 dynamic_update_slice.245
  618.8 6.7 dynamic_update_slice.248
  638.9 6.7 dynamic_update_slice.251
  645.7 6.7 dynamic_update_slice.252
  659.1 6.7 dynamic_update_slice.254
  (290 shorter events, 282.8 us)
Async XLA Ops:
  19.9 53.7 %collective-permute-start.5 = (bf16[2,8,8,128]{1,3,2,0:T(8,128)(2,1)}, bf16[2,8,8,128]{1,3,2,0:T(8,128)(2,1)}, u32[]{:S(2)}, u32[]{:S(2)}) collective-permute-start(bf16[2,8,8,128]{1,3,2,0:T(8,128)(2,1)} %get-tuple-element.39), channel_id=1, source_target_pairs={{0,6},{1,7},{2,8},{3,9},{4,10},{5,11},{6,12},{7,13},{8,14},{9,15},... | collective-permute-start | bytes 98312 | tf_op jit(solution)/shard_map/ppermute | solution.py:29
  31.7 80.6 %collective-permute-start.6 = (bf16[2,8,8,128]{1,3,2,0:T(8,128)(2,1)}, bf16[2,8,8,128]{1,3,2,0:T(8,128)(2,1)}, u32[]{:S(2)}, u32[]{:S(2)}) collective-permute-start(bf16[2,8,8,128]{1,3,2,0:T(8,128)(2,1)} %get-tuple-element.40), channel_id=1, source_target_pairs={{0,7},{1,8},{2,9},{3,10},{4,11},{5,12},{6,13},{7,14},{8,15},{9,0},... | collective-permute-start | bytes 98312 | tf_op jit(solution)/shard_map/ppermute | solution.py:29
  39.9 143.3 %collective-permute-start.7 = (bf16[2,8,8,128]{1,3,2,0:T(8,128)(2,1)}, bf16[2,8,8,128]{1,3,2,0:T(8,128)(2,1)}, u32[]{:S(2)}, u32[]{:S(2)}) collective-permute-start(bf16[2,8,8,128]{1,3,2,0:T(8,128)(2,1)} %get-tuple-element.41), channel_id=1, source_target_pairs={{0,8},{1,9},{2,10},{3,11},{4,12},{5,13},{6,14},{7,15},{8,0},{9,1},... | collective-permute-start | bytes 98312 | tf_op jit(solution)/shard_map/ppermute | solution.py:29
  53.8 132.0 %collective-permute-start.8 = (bf16[2,8,8,128]{1,3,2,0:T(8,128)(2,1)}, bf16[2,8,8,128]{1,3,2,0:T(8,128)(2,1)}, u32[]{:S(2)}, u32[]{:S(2)}) collective-permute-start(bf16[2,8,8,128]{1,3,2,0:T(8,128)(2,1)} %get-tuple-element.42), channel_id=1, source_target_pairs={{0,9},{1,10},{2,11},{3,12},{4,13},{5,14},{6,15},{7,0},{8,1},{9,2},... | collective-permute-start | bytes 98312 | tf_op jit(solution)/shard_map/ppermute | solution.py:29
  62.4 126.1 %collective-permute-start.9 = (bf16[2,8,8,128]{1,3,2,0:T(8,128)(2,1)}, bf16[2,8,8,128]{1,3,2,0:T(8,128)(2,1)S(1)}, u32[]{:S(2)}, u32[]{:S(2)}) collective-permute-start(bf16[2,8,8,128]{1,3,2,0:T(8,128)(2,1)} %get-tuple-element.44), channel_id=1, source_target_pairs={{0,10},{1,11},{2,12},{3,13},{4,14},{5,15},{6,0},{7,1},{8,2},{9,3},... | collective-permute-start | bytes 98312 | tf_op jit(solution)/shard_map/ppermute | solution.py:29
  73.6 116.5 %collective-permute-start.10 = (bf16[2,8,8,128]{1,3,2,0:T(8,128)(2,1)}, bf16[2,8,8,128]{1,3,2,0:T(8,128)(2,1)}, u32[]{:S(2)}, u32[]{:S(2)}) collective-permute-start(bf16[2,8,8,128]{1,3,2,0:T(8,128)(2,1)} %get-tuple-element.45), channel_id=1, source_target_pairs={{0,11},{1,12},{2,13},{3,14},{4,15},{5,0},{6,1},{7,2},{8,3},{9,4},{... | collective-permute-start | bytes 98312 | tf_op jit(solution)/shard_map/ppermute | solution.py:29
  112.3 79.1 %collective-permute-start.11 = (bf16[2,8,8,128]{1,3,2,0:T(8,128)(2,1)}, bf16[2,8,8,128]{1,3,2,0:T(8,128)(2,1)}, u32[]{:S(2)}, u32[]{:S(2)}) collective-permute-start(bf16[2,8,8,128]{1,3,2,0:T(8,128)(2,1)} %get-tuple-element.46), channel_id=1, source_target_pairs={{0,12},{1,13},{2,14},{3,15},{4,0},{5,1},{6,2},{7,3},{8,4},{9,5},{1... | collective-permute-start | bytes 98312 | tf_op jit(solution)/shard_map/ppermute | solution.py:29
  246.0 62.6 %collective-permute-start.40 = (bf16[8,8,128]{2,0,1:T(8,128)(2,1)}, bf16[8,8,128]{2,0,1:T(8,128)(2,1)}, u32[]{:S(2)}, u32[]{:S(2)}) collective-permute-start(bf16[8,8,128]{2,0,1:T(8,128)(2,1)} %get-tuple-element.51), channel_id=1, source_target_pairs={{0,11},{1,12},{2,13},{3,14},{4,15},{5,0},{6,1},{7,2},{8,3},{9,4},{... | collective-permute-start | bytes 49160 | tf_op jit(solution)/shard_map/ppermute | solution.py:29
  246.8 67.0 %collective-permute-start.41 = (bf16[8,8,128]{2,0,1:T(8,128)(2,1)}, bf16[8,8,128]{2,0,1:T(8,128)(2,1)}, u32[]{:S(2)}, u32[]{:S(2)}) collective-permute-start(bf16[8,8,128]{2,0,1:T(8,128)(2,1)} %get-tuple-element.50), channel_id=1, source_target_pairs={{0,12},{1,13},{2,14},{3,15},{4,0},{5,1},{6,2},{7,3},{8,4},{9,5},{1... | collective-permute-start | bytes 49160 | tf_op jit(solution)/shard_map/ppermute | solution.py:29
  248.4 70.6 %collective-permute-start.42 = (bf16[8,8,128]{2,0,1:T(8,128)(2,1)}, bf16[8,8,128]{2,0,1:T(8,128)(2,1)}, u32[]{:S(2)}, u32[]{:S(2)}) collective-permute-start(bf16[8,8,128]{2,0,1:T(8,128)(2,1)} %get-tuple-element.49), channel_id=1, source_target_pairs={{0,13},{1,14},{2,15},{3,0},{4,1},{5,2},{6,3},{7,4},{8,5},{9,6},{10... | collective-permute-start | bytes 49160 | tf_op jit(solution)/shard_map/ppermute | solution.py:29
  250.7 73.4 %collective-permute-start.43 = (bf16[8,8,128]{2,0,1:T(8,128)(2,1)}, bf16[8,8,128]{2,0,1:T(8,128)(2,1)}, u32[]{:S(2)}, u32[]{:S(2)}) collective-permute-start(bf16[8,8,128]{2,0,1:T(8,128)(2,1)} %get-tuple-element.48), channel_id=1, source_target_pairs={{0,14},{1,15},{2,0},{3,1},{4,2},{5,3},{6,4},{7,5},{8,6},{9,7},{10,... | collective-permute-start | bytes 49160 | tf_op jit(solution)/shard_map/ppermute | solution.py:29
  251.8 77.5 %collective-permute-start.44 = (bf16[8,8,128]{2,0,1:T(8,128)(2,1)}, bf16[8,8,128]{2,0,1:T(8,128)(2,1)}, u32[]{:S(2)}, u32[]{:S(2)}) collective-permute-start(bf16[8,8,128]{2,0,1:T(8,128)(2,1)} %get-tuple-element.47), channel_id=1, source_target_pairs={{0,15},{1,0},{2,1},{3,2},{4,3},{5,4},{6,5},{7,6},{8,7},{9,8},{10,9... | collective-permute-start | bytes 49160 | tf_op jit(solution)/shard_map/ppermute | solution.py:29
  351.4 53.1 %collective-permute-start.49 = (bf16[2,8,8,128]{1,3,2,0:T(8,128)(2,1)}, bf16[2,8,8,128]{1,3,2,0:T(8,128)(2,1)}, u32[]{:S(2)}, u32[]{:S(2)}) collective-permute-start(bf16[2,8,8,128]{1,3,2,0:T(8,128)(2,1)} %copy.146), channel_id=1, source_target_pairs={{0,5},{1,6},{2,7},{3,8},{4,9},{5,10},{6,11},{7,12},{8,13},{9,14},{... | collective-permute-start | bytes 98312 | tf_op jit(solution)/shard_map/ppermute | solution.py:29
  354.0 50.5 %collective-permute-start.45 = (bf16[2,8,8,128]{1,3,2,0:T(8,128)(2,1)}, bf16[2,8,8,128]{1,3,2,0:T(8,128)(2,1)}, u32[]{:S(2)}, u32[]{:S(2)}) collective-permute-start(bf16[2,8,8,128]{1,3,2,0:T(8,128)(2,1)} %copy.142), channel_id=1, source_target_pairs={{0,1},{1,2},{2,3},{3,4},{4,5},{5,6},{6,7},{7,8},{8,9},{9,10},{10,1... | collective-permute-start | bytes 98312 | tf_op jit(solution)/shard_map/ppermute | solution.py:29
  375.9 79.7 %collective-permute-start.48 = (bf16[2,8,8,128]{1,3,2,0:T(8,128)(2,1)}, bf16[2,8,8,128]{1,3,2,0:T(8,128)(2,1)}, u32[]{:S(2)}, u32[]{:S(2)}) collective-permute-start(bf16[2,8,8,128]{1,3,2,0:T(8,128)(2,1)} %copy.145), channel_id=1, source_target_pairs={{0,4},{1,5},{2,6},{3,7},{4,8},{5,9},{6,10},{7,11},{8,12},{9,13},{1... | collective-permute-start | bytes 98312 | tf_op jit(solution)/shard_map/ppermute | solution.py:29
  404.5 53.6 %collective-permute-start.50 = (bf16[2,8,8,128]{1,3,2,0:T(8,128)(2,1)}, bf16[2,8,8,128]{1,3,2,0:T(8,128)(2,1)}, u32[]{:S(2)}, u32[]{:S(2)}) collective-permute-start(bf16[2,8,8,128]{1,3,2,0:T(8,128)(2,1)} %copy.147), channel_id=1, source_target_pairs={{0,6},{1,7},{2,8},{3,9},{4,10},{5,11},{6,12},{7,13},{8,14},{9,15},... | collective-permute-start | bytes 98312 | tf_op jit(solution)/shard_map/ppermute | solution.py:29
  404.5 58.3 %collective-permute-start.51 = (bf16[2,8,8,128]{1,3,2,0:T(8,128)(2,1)}, bf16[2,8,8,128]{1,3,2,0:T(8,128)(2,1)}, u32[]{:S(2)}, u32[]{:S(2)}) collective-permute-start(bf16[2,8,8,128]{1,3,2,0:T(8,128)(2,1)} %copy.148), channel_id=1, source_target_pairs={{0,7},{1,8},{2,9},{3,10},{4,11},{5,12},{6,13},{7,14},{8,15},{9,0},... | collective-permute-start | bytes 98312 | tf_op jit(solution)/shard_map/ppermute | solution.py:29
  405.7 123.3 %collective-permute-start.52 = (bf16[2,8,8,128]{1,3,2,0:T(8,128)(2,1)}, bf16[2,8,8,128]{1,3,2,0:T(8,128)(2,1)}, u32[]{:S(2)}, u32[]{:S(2)}) collective-permute-start(bf16[2,8,8,128]{1,3,2,0:T(8,128)(2,1)} %copy.149), channel_id=1, source_target_pairs={{0,8},{1,9},{2,10},{3,11},{4,12},{5,13},{6,14},{7,15},{8,0},{9,1},... | collective-permute-start | bytes 98312 | tf_op jit(solution)/shard_map/ppermute | solution.py:29
  409.7 136.4 %collective-permute-start.53 = (bf16[2,8,8,128]{1,3,2,0:T(8,128)(2,1)}, bf16[2,8,8,128]{1,3,2,0:T(8,128)(2,1)}, u32[]{:S(2)}, u32[]{:S(2)}) collective-permute-start(bf16[2,8,8,128]{1,3,2,0:T(8,128)(2,1)} %copy.150), channel_id=1, source_target_pairs={{0,9},{1,10},{2,11},{3,12},{4,13},{5,14},{6,15},{7,0},{8,1},{9,2},... | collective-permute-start | bytes 98312 | tf_op jit(solution)/shard_map/ppermute | solution.py:29
  455.5 183.4 %collective-permute-start.55 = (bf16[2,8,8,128]{1,3,2,0:T(8,128)(2,1)}, bf16[2,8,8,128]{1,3,2,0:T(8,128)(2,1)}, u32[]{:S(2)}, u32[]{:S(2)}) collective-permute-start(bf16[2,8,8,128]{1,3,2,0:T(8,128)(2,1)} %copy.152), channel_id=1, source_target_pairs={{0,11},{1,12},{2,13},{3,14},{4,15},{5,0},{6,1},{7,2},{8,3},{9,4},{... | collective-permute-start | bytes 98312 | tf_op jit(solution)/shard_map/ppermute | solution.py:29
  458.2 187.5 %collective-permute-start.56 = (bf16[2,8,8,128]{1,3,2,0:T(8,128)(2,1)}, bf16[2,8,8,128]{1,3,2,0:T(8,128)(2,1)}, u32[]{:S(2)}, u32[]{:S(2)}) collective-permute-start(bf16[2,8,8,128]{1,3,2,0:T(8,128)(2,1)} %copy.153), channel_id=1, source_target_pairs={{0,12},{1,13},{2,14},{3,15},{4,0},{5,1},{6,2},{7,3},{8,4},{9,5},{1... | collective-permute-start | bytes 98312 | tf_op jit(solution)/shard_map/ppermute | solution.py:29
  462.8 189.5 %collective-permute-start.57 = (bf16[2,8,8,128]{1,3,2,0:T(8,128)(2,1)}, bf16[2,8,8,128]{1,3,2,0:T(8,128)(2,1)}, u32[]{:S(2)}, u32[]{:S(2)}) collective-permute-start(bf16[2,8,8,128]{1,3,2,0:T(8,128)(2,1)} %copy.154), channel_id=1, source_target_pairs={{0,13},{1,14},{2,15},{3,0},{4,1},{5,2},{6,3},{7,4},{8,5},{9,6},{10... | collective-permute-start | bytes 98312 | tf_op jit(solution)/shard_map/ppermute | solution.py:29
  529.1 130.0 %collective-permute-start.58 = (bf16[2,8,8,128]{1,3,2,0:T(8,128)(2,1)}, bf16[2,8,8,128]{1,3,2,0:T(8,128)(2,1)}, u32[]{:S(2)}, u32[]{:S(2)}) collective-permute-start(bf16[2,8,8,128]{1,3,2,0:T(8,128)(2,1)} %copy.155), channel_id=1, source_target_pairs={{0,14},{1,15},{2,0},{3,1},{4,2},{5,3},{6,4},{7,5},{8,6},{9,7},{10,... | collective-permute-start | bytes 98312 | tf_op jit(solution)/shard_map/ppermute | solution.py:29
  546.1 119.7 %collective-permute-start.59 = (bf16[2,8,8,128]{1,3,2,0:T(8,128)(2,1)}, bf16[2,8,8,128]{1,3,2,0:T(8,128)(2,1)}, u32[]{:S(2)}, u32[]{:S(2)}) collective-permute-start(bf16[2,8,8,128]{1,3,2,0:T(8,128)(2,1)} %copy.156), channel_id=1, source_target_pairs={{0,15},{1,0},{2,1},{3,2},{4,3},{5,4},{6,5},{7,6},{8,7},{9,8},{10,9... | collective-permute-start | bytes 98312 | tf_op jit(solution)/shard_map/ppermute | solution.py:29
  (57 other events, 1049.2 us)

commit v2 on v0

--- a/solution.py
+++ b/solution.py
@@ -49,20 +49,14 @@
     right_panel = (
         cell_mask * jax.nn.sigmoid(projected[2 * hidden : 3 * hidden]) * projected[3 * hidden :]
     ).astype(jnp.bfloat16)
-    panels = lax.all_to_all(
-        jnp.stack([left_panel, right_panel]), "row", split_axis=1, concat_axis=2, tiled=True
-    )
-    left_all = panels[0]
-    right_all = panels[1]
-    right_rows = lax.all_to_all(right_all, "chan", split_axis=1, concat_axis=2, tiled=True)
-    partner = right_rows
-    tri_part = jnp.einsum(
-        "gik,gjk->gij",
-        lax.all_gather(left_all, "chan", axis=2, tiled=True),
-        partner,
+    right_rows = lax.all_gather(jnp.transpose(right_panel, (1, 0, 2)), "row", axis=0, tiled=True)
+    left_all = lax.all_to_all(left_panel, "row", split_axis=0, concat_axis=1, tiled=True)
+    tri_cells = jnp.einsum(
+        "hik,jhk->hij",
+        lax.all_gather(left_panel, "chan", axis=2, tiled=True),
+        lax.all_to_all(right_rows, "chan", split_axis=0, concat_axis=2, tiled=True),
         preferred_element_type=jnp.float32,
     ).astype(jnp.bfloat16)
-    tri_cells = lax.all_to_all(tri_part, "row", split_axis=1, concat_axis=0, tiled=True)
     tri_hat, inv_tri = normalize(tri_cells.astype(jnp.float32), 0)
     scaled = (tri_hat * ln_out_gain[:, None, None] + ln_out_bias[:, None, None]).astype(
         jnp.bfloat16
@@ -78,16 +72,15 @@
     d_hat = d_hat * ln_out_gain[:, None, None]
     d_tri = norm_backward(d_hat, tri_hat, inv_tri, 0).astype(jnp.bfloat16)
     d_tri_all = lax.all_to_all(d_tri, "row", split_axis=0, concat_axis=1, tiled=True)
+    d_tri_wide = lax.all_gather(d_tri, "chan", axis=2, tiled=True)
+    d_left = jnp.einsum(
+        "hij,jhk->hik", d_tri_wide, right_rows, preferred_element_type=jnp.float32
+    ).astype(jnp.bfloat16)
     panel_piece = lax.all_gather(d_tri_all, "chan", axis=2, tiled=True)
-    partner = right_all
-    d_left = jnp.einsum("gij,gjk->gik", panel_piece, partner, preferred_element_type=jnp.float32)
-    contribution = jnp.einsum(
+    d_right = jnp.einsum(
         "gij,gik->gjk", panel_piece, left_all, preferred_element_type=jnp.float32
-    )
-    d_right = contribution
-    d_left, d_right = (d_left, d_right)
-    d_stack = jnp.stack([d_left, d_right]).astype(jnp.bfloat16)
-    d_panels = lax.all_to_all(d_stack, "row", split_axis=2, concat_axis=1, tiled=True)
+    ).astype(jnp.bfloat16)
+    d_right = lax.all_to_all(d_right, "row", split_axis=1, concat_axis=0, tiled=True)
 
     def gating(d_value, gate_proj, value_proj):
         sigmoid_val = jax.nn.sigmoid(gate_proj)
@@ -97,9 +90,9 @@
             masked_grad * sigmoid_val,
         )
 
-    gate_left, value_left = gating(d_panels[0], projected[:hidden], projected[hidden : 2 * hidden])
+    gate_left, value_left = gating(d_left, projected[:hidden], projected[hidden : 2 * hidden])
     gate_right, value_right = gating(
-        d_panels[1], projected[2 * hidden : 3 * hidden], projected[3 * hidden :]
+        d_right, projected[2 * hidden : 3 * hidden], projected[3 * hidden :]
     )
     d_proj = jnp.concatenate([gate_left, value_left, gate_right, value_right], axis=0).astype(
         jnp.bfloat16

time: 84 us -> 116 us (1.38)
  waiting for transfers between devices: 20 us -> 46.7 us
  blocking collectives: 34.4 us -> 13.1 us
  between operations: 0.34 us -> 13.7 us
  matrix products: 8.02 us -> 18.1 us
  starting transfers between devices: 7.67 us -> 11.8 us
  local copies, waits for them, and re-layouts: 10.5 us -> 7.57 us
  other arithmetic: 2.38 us -> 4.9 us
    all_gather x0 -> x1, waiting for transfers between devices: none -> 46.7 us  [shards(): lax.all_gather(jnp.transpose(right_panel, (1, 0, 2)), 'row', axis=0, tile...]
    all_to_all x1 -> x0, blocking collectives: 21.6 us -> none  [shards(): lax.all_to_all(jnp.stack([left_panel, right_panel]), 'row', split_axis=1,...]
    all_to_all x2, waiting for transfers between devices: 20 us -> 0.01 us  [the longest x1 0.01 us: shards(): lax.all_to_all(left_panel, 'row', split_axis=0, concat_axis=1, tiled=True)]
    dot_general x2, matrix products: 0.52 us -> 12.3 us  [the longest x1 6.47 us: shards(): jnp.einsum('hij,jhk->hik', d_tri_wide, right_rows, preferred_element_type...]
    all_to_all x2, starting transfers between devices: 7.67 us -> 11.8 us  [the longest x1 7.41 us: shards(): lax.all_to_all(left_panel, 'row', split_axis=0, concat_axis=1, tiled=True)]
    convert_element_type x4 -> x2, local copies, waits for them, and re-layouts: 4.2 us -> 0.27 us  [gating(): masked_grad = d_value.astype(jnp.float32) * cell_mask]
    dot_general x0 -> x1, local copies, waits for them, and re-layouts: none -> 1.81 us  [shards(): jnp.einsum('hij,jhk->hik', d_tri_wide, right_rows, preferred_element_type...]
    dot_general x1, matrix products: 2.05 us -> 0.42 us  [shards(): jnp.einsum('rmc,cd->rmd', normed_pair, w_gate, preferred_element_type=jnp...]
  transfers between devices with their start and end apart: 2 -> 3, of which waited for: 2 -> 1; matrix products, arithmetic and copies ran while one was open for 5% -> 16% of each run, Pallas kernels for 0% -> 0%
where the time goes in v2:
time: 116 us
  waiting for transfers between devices  46.7 us (40%)
  matrix products  18.1 us (16%)
  between operations  13.7 us (12%)
  blocking collectives  13.1 us (11%)
  starting transfers between devices  11.8 us (10%)
  local copies, waits for them, and re-layouts  7.57 us (7%)
  other arithmetic  4.9 us (4%)
    all_gather x1, waiting for transfers between devices, shards(): lax.all_gather(jnp.transpose(right_panel, (1, 0, 2)), 'row', axis=0, tile...  46.7 us
    all_to_all x1, blocking collectives, shards(): lax.all_to_all(d_tri, 'row', split_axis=0, concat_axis=1, tiled=True)  13.1 us
    all_to_all x1, starting transfers between devices, shards(): lax.all_to_all(left_panel, 'row', split_axis=0, concat_axis=1, tiled=True)  7.41 us
    dot_general x1, matrix products, shards(): jnp.einsum('hij,jhk->hik', d_tri_wide, right_rows, preferred_element_type...  6.47 us
    dot_general x1, matrix products, shards(): jnp.einsum('hik,jhk->hij', lax.all_gather(left_panel, 'chan', axis=2, til...  5.8 us
    all_to_all x1, starting transfers between devices, shards(): lax.all_to_all(d_right, 'row', split_axis=1, concat_axis=0, tiled=True)  4.38 us
  transfers between devices with their start and end apart: 3, of which 1 were waited for; matrix products, arithmetic and copies ran while one was open for 16% of the time, Pallas kernels for 0%

profile of v2, /device:TPU:0, one launch (start us, length us, event | category | flops | bytes accessed | tf_op | source)
XLA Modules:
  0.0 115.9 jit_solution(3226854179202416874)
XLA Ops:
  6.5 0.7 convert_element_type.62
  7.4 1.1 copy.58
  8.7 1.2 %convolution_bitcast_fusion = f32[512,8,128]{0,2,1:T(8,128)S(1)} fusion(bf16[128,512]{1,0:T(8,128)(2,1)S(1)} %copy-done, bf16[8,128,128]{1,2,0:T(8,128)(2,1)S(1)} %copy.58, f32[128]{0:T(128)} %param.14, f32[128]{0:T(128)} %param.13, f32[8,128]{1,0:T(8,128)S(1)} %add_rsqrt_fusion.1, f32[8,128]{1,0:T(8,128)S(1)} %broadcast_multiply_fusion.6), kind=kOutput, calls=%fused_computation.4 | convolution fusion | flops 135004160 | bytes 2499584 | tf_op jit(solution)/shard_map/rmc,ch->hrm/dot_general | solution.py:45
  9.9 0.3 fusion.50
  10.3 0.8 copy.60
  11.1 0.9 copy.61
  12.0 7.4 %all-to-all-start.1 = ((bf16[128,8,128]{2,1,0:T(8,128)(2,1)}), bf16[128,8,128]{2,1,0:T(8,128)(2,1)}, u32[]{:S(2)}, u32[]{:S(2)}) async-start(bf16[128,8,128]{2,1,0:T(8,128)(2,1)} %copy.61), calls=%async_computation.1 | async-start | bytes 524288 | tf_op jit(solution)/shard_map/all_to_all | solution.py:53
  19.5 0.4 fusion.7
  19.9 0.8 copy-done.1
  21.0 46.7 %all-gather.2.cloned.1.call-done = bf16[128,128,128]{2,1,0:T(8,128)(2,1)} async-done(((bf16[8,128,128]{2,1,0:T(8,128)(2,1)}), bf16[128,128,128]{2,1,0:T(8,128)(2,1)}) %all-gather.2.cloned.1.call-update) | async-done | bytes 4194320 | tf_op jit(solution)/shard_map/all_gather | solution.py:52
  67.7 5.8 %fusion.72 = (f32[8,128]{1,0:T(8,128)S(1)}, f32[128,8,128]{2,1,0:T(8,128)S(1)}) fusion(bf16[128,8,128]{2,1,0:T(8,128)(2,1)} %copy.61, bf16[128,128,128]{2,1,0:T(8,128)(2,1)} %all-gather.2.cloned.1.call-done), kind=kOutput, calls=%fused_computation.97 | convolution fusion | flops 33946624 | bytes 4984832 | tf_op jit(solution)/shard_map/hik,jhk->hij/dot_general | solution.py:54
  73.6 0.3 bitcast_reduce_fusion
  74.0 0.5 fusion.47
  74.5 13.1 %all_to_all.45 = bf16[128,8,128]{2,1,0:T(8,128)(2,1)S(1)} all-to-all(bf16[128,8,128]{2,1,0:T(8,128)(2,1)S(1)} %get-tuple-element.17), channel_id=1, replica_groups=mesh['grp'=2,'row'=16,'chan'=1] {'row'}, dimensions={0} | all-to-all | bytes 524288 | tf_op jit(solution)/shard_map/all_to_all | solution.py:74
  87.6 1.2 %convolution_convert_fusion = bf16[8,128,128]{2,1,0:T(8,128)(2,1)S(1)} fusion(bf16[8,16,8,128]{3,2,0,1:T(8,128)(2,1)} %bitcast.10, bf16[16,8,8,128]{3,2,1,0:T(8,128)(2,1)S(1)} %bitcast.55), kind=kOutput, calls=%fused_computation.17 | convolution fusion | flops 33685504 | bytes 786432 | tf_op jit(solution)/shard_map/gij,gik->gjk/dot_general | solution.py:80
  88.8 0.9 copy.71
  89.7 4.4 %all-to-all-start.2 = ((bf16[8,128,128]{2,0,1:T(8,128)(2,1)}), bf16[8,128,128]{2,0,1:T(8,128)(2,1)}, u32[]{:S(2)}, u32[]{:S(2)}) async-start(bf16[8,128,128]{2,0,1:T(8,128)(2,1)} %copy.71), calls=%async_computation.2 | async-start | bytes 524288 | tf_op jit(solution)/shard_map/all_to_all | solution.py:83
  94.1 6.5 %fusion = bf16[128,8,128]{2,1,0:T(8,128)(2,1)} fusion(bf16[128,8,128]{2,1,0:T(8,128)(2,1)S(1)} %get-tuple-element.17, bf16[128,128,128]{2,1,0:T(8,128)(2,1)} %all-gather.2.cloned.1.call-done), kind=kOutput, calls=%fused_computation | convolution fusion | flops 33554432 | bytes 4718592 | tf_op jit(solution)/shard_map/hij,jhk->hik/dot_general | solution.py:76
  100.6 1.8 %copy.66 = bf16[128,8,128]{0,2,1:T(8,128)(2,1)} copy(bf16[128,8,128]{2,1,0:T(8,128)(2,1)} %fusion) | data formatting | bytes 524288 | tf_op jit(solution)/shard_map/hij,jhk->hik/dot_general | solution.py:76
  102.4 2.2 %fusion.17 = f32[8,128,128]{1,2,0:T(8,128)} fusion(f32[8,128,128]{2,1,0:T(8,128)S(1)} %copy-done.2, bf16[8,128,128]{2,1,0:T(8,128)(2,1)} %param.11, bf16[128,8,128]{2,1,0:T(8,128)(2,1)S(1)} %get-tuple-element.18, bf16[128,128]{1,0:T(8,128)(2,1)} %param.19, bf16[128,128]{1,0:T(8,128)(2,1)} %param.16), kind=kOutput, calls=%fused_computation.18 | convolution fusion | flops 67895296 | bytes 1638400 | tf_op jit(solution)/shard_map/rmd,cd->rmc/dot_general | solution.py:101
  104.6 1.0 convert_bitcast_fusion
  105.9 1.5 %multiply_convert_fusion.3 = (bf16[128,8,128]{0,2,1:T(8,128)(2,1)S(1)}, bf16[128,8,128]{0,2,1:T(8,128)(2,1)S(1)}, bf16[128,8,128]{0,2,1:T(8,128)(2,1)S(1)}, bf16[128,8,128]{0,2,1:T(8,128)(2,1)S(1)}) fusion(f32[512,8,128]{0,2,1:T(8,128)S(1)} %convolution_bitcast_fusion, f32[8,128]{1,0:T(8,128)S(1)} %broadcast_multiply_fusion, bf16[128,8,128]{0,2,1:T(8,128)(2,1)} %copy.66, ...), kind=kLoop, calls=%fused_computation.65 | loop fusion | flops 3014656 | bytes 3936256 | tf_op jit(solution)/shard_map/convert.3
  107.5 0.5 fusion.71
  108.2 0.8 copy.77
  (43 shorter events, 1.2 us)
Async XLA Ops:
  6.5 2.1 %copy-start = (bf16[128,512]{1,0:T(8,128)(2,1)S(1)}, bf16[128,512]{1,0:T(8,128)(2,1)}, u32[]{:S(2)}) copy-start(bf16[128,512]{1,0:T(8,128)(2,1)} %param.15) | copy-start | bytes 393220
  6.5 61.1 %all-gather.2.cloned.1.call-start = ((), (), s32[]{:S(2)}) async-start(), calls=%async_computation.3 | async-start | bytes 4456448 | tf_op jit(solution)/shard_map/all_gather | solution.py:52
  9.9 9.5 %copy-start.6 = (bf16[128,128]{1,0:T(8,128)(2,1)S(1)}, bf16[128,128]{1,0:T(8,128)(2,1)}, u32[]{:S(2)}) copy-start(bf16[128,128]{1,0:T(8,128)(2,1)} %param.16) | copy-start | bytes 98308
  9.9 9.5 %copy-start.9 = (f32[128]{0:T(128)S(1)}, f32[128]{0:T(128)}, u32[]{:S(2)}) copy-start(f32[128]{0:T(128)} %param.14) | copy-start | bytes 1540
  9.9 9.5 %copy-start.10 = (f32[128]{0:T(128)S(1)}, f32[128]{0:T(128)}, u32[]{:S(2)}) copy-start(f32[128]{0:T(128)} %param.13) | copy-start | bytes 1540
  11.1 9.6 %copy-start.3 = (bf16[8,128,128]{2,1,0:T(8,128)(2,1)S(1)}, bf16[8,128,128]{2,1,0:T(8,128)(2,1)}, u32[]{:S(2)}) copy-start(bf16[8,128,128]{2,1,0:T(8,128)(2,1)} %param.11) | copy-start | bytes 786436
  11.1 9.6 %copy-start.5 = (bf16[128,128]{1,0:T(8,128)(2,1)S(1)}, bf16[128,128]{1,0:T(8,128)(2,1)}, u32[]{:S(2)}) copy-start(bf16[128,128]{1,0:T(8,128)(2,1)} %param.19) | copy-start | bytes 98308
  12.0 62.5 %all-to-all-start.1 = ((bf16[128,8,128]{2,1,0:T(8,128)(2,1)}), bf16[128,8,128]{2,1,0:T(8,128)(2,1)}, u32[]{:S(2)}, u32[]{:S(2)}) async-start(bf16[128,8,128]{2,1,0:T(8,128)(2,1)} %copy.61), calls=%async_computation.1 | async-start | bytes 524288 | tf_op jit(solution)/shard_map/all_to_all | solution.py:53
  19.9 0.8 copy-start.1
  20.9 52.7 %copy-start.7 = (f32[128]{0:T(128)S(1)}, f32[128]{0:T(128)}, u32[]{:S(2)}) copy-start(f32[128]{0:T(128)} %param.17) | copy-start | bytes 1540
  67.7 6.3 %copy-start.8 = (f32[128]{0:T(128)S(1)}, f32[128]{0:T(128)}, u32[]{:S(2)}) copy-start(f32[128]{0:T(128)} %param.18) | copy-start | bytes 1540
  89.7 14.9 %all-to-all-start.2 = ((bf16[8,128,128]{2,0,1:T(8,128)(2,1)}), bf16[8,128,128]{2,0,1:T(8,128)(2,1)}, u32[]{:S(2)}, u32[]{:S(2)}) async-start(bf16[8,128,128]{2,0,1:T(8,128)(2,1)} %copy.71), calls=%async_computation.2 | async-start | bytes 524288 | tf_op jit(solution)/shard_map/all_to_all | solution.py:83
  94.1 8.3 %copy-start.2 = (f32[8,128,128]{2,1,0:T(8,128)S(1)}, f32[8,128,128]{2,1,0:T(8,128)}, u32[]{:S(2)}) copy-start(f32[8,128,128]{2,1,0:T(8,128)} %copy-done.1) | copy-start | bytes 1572868
  105.9 1.6 %copy-start.4 = (f32[8,128,128]{1,2,0:T(8,128)S(1)}, f32[8,128,128]{1,2,0:T(8,128)}, u32[]{:S(2)}) copy-start(f32[8,128,128]{1,2,0:T(8,128)} %fusion.17) | copy-start | bytes 1572868
  105.9 1.6 %copy-start.11 = (f32[128]{0:T(128)S(1)}, f32[128]{0:T(128)}, u32[]{:S(2)}) copy-start(f32[128]{0:T(128)} %param.13) | copy-start | bytes 1540
Sparse Core Ops, SparseCore 0:
  11.3 56.3 all-gather.1

commit v3 on v0

--- a/solution.py
+++ b/solution.py
@@ -1,7 +1,302 @@
+import functools
+
 import jax
 import jax.numpy as jnp
 from jax import lax
+from jax.experimental import pallas as pl
+from jax.experimental.pallas import tpu as pltpu
 from jax.sharding import PartitionSpec as P
+
+F32 = jnp.float32
+BF16 = jnp.bfloat16
+VMEM_LIMIT = 16 * 1024 * 1024
+
+
+def dot(lhs, rhs, lhs_dim, rhs_dim):
+    return lax.dot_general(
+        lhs, rhs, (((lhs_dim,), (rhs_dim,)), ((), ())), preferred_element_type=F32
+    )
+
+
+def transposed(matrix):
+    return jnp.transpose(matrix.astype(F32)).astype(BF16)
+
+
+def sigmoid(values):
+    return 1.0 / (1.0 + jnp.exp(-values))
+
+
+def input_norm(pair_row):
+    values = pair_row.astype(F32)
+    centered = values - jnp.mean(values, axis=-1, keepdims=True)
+    variance = jnp.mean(centered * centered, axis=-1, keepdims=True)
+    inv_std = lax.rsqrt(variance + 1e-05)
+    return centered * inv_std, inv_std
+
+
+def call(kernel, name, outs, args, scratch=(), smem=(), flops=0):
+    spaces = [pltpu.SMEM if n in smem else pltpu.VMEM for n in range(len(args))]
+    moved = sum(a.size * a.dtype.itemsize for a in args) + sum(
+        o.size * jnp.dtype(o.dtype).itemsize for o in outs
+    )
+    return pl.pallas_call(
+        kernel,
+        name=name,
+        out_shape=outs,
+        in_specs=[pl.BlockSpec(memory_space=space) for space in spaces],
+        out_specs=[pl.BlockSpec(memory_space=pltpu.VMEM) for _ in outs],
+        scratch_shapes=list(scratch),
+        compiler_params=pltpu.CompilerParams(vmem_limit_bytes=VMEM_LIMIT),
+        cost_estimate=pl.CostEstimate(flops=flops, bytes_accessed=moved, transcendentals=0),
+    )(*args)
+
+
+def cell_mask_row(mask_scalars, mask_vector, rows, row):
+    own = mask_scalars[lax.axis_index("row") * rows + row].astype(F32)
+    return mask_vector[...].astype(F32) * own
+
+
+def project_kernel(pair, mask_scalars, mask_vector, gain, bias, w_proj, panels):
+    rows = pair.shape[0]
+    hidden = w_proj.shape[1] // 4
+    count, _, width = panels.shape
+    block = hidden // count
+    w_flip = transposed(w_proj[...])
+    for row in range(rows):
+        normed, _ = input_norm(pair[row])
+        zln = (normed * gain[...] + bias[...]).astype(BF16)
+        proj = dot(w_flip, zln, 1, 1)
+        mask = cell_mask_row(mask_scalars, mask_vector, rows, row)
+        left = mask * sigmoid(proj[:hidden]) * proj[hidden : 2 * hidden]
+        right = mask * sigmoid(proj[2 * hidden : 3 * hidden]) * proj[3 * hidden :]
+        both = jnp.concatenate(
+            [left.reshape(count, block, width), right.reshape(count, block, width)], axis=1
+        )
+        panels[:, row * 2 * block : (row + 1) * 2 * block, :] = both.astype(BF16)
+
+
+def prepare_kernel(
+    pair,
+    cotangent,
+    mask_scalars,
+    mask_vector,
+    gain,
+    bias,
+    w_proj,
+    w_gate,
+    out_gain,
+    w_out,
+    d_hat_centered,
+    gate_slope,
+    slopes,
+):
+    rows = pair.shape[0]
+    hidden = w_out.shape[0]
+    w_flip = transposed(w_proj[...])
+    for row in range(rows):
+        normed, _ = input_norm(pair[row])
+        zln = (normed * gain[...] + bias[...]).astype(BF16)
+        gate = sigmoid(dot(zln, w_gate[...], 1, 0))
+        cot = cotangent[row].astype(F32)
+        d_scaled = (cot * gate).astype(BF16)
+        d_hat = dot(w_out[...], d_scaled, 1, 1) * out_gain[...]
+        d_hat_centered[row] = d_hat - jnp.mean(d_hat, axis=0, keepdims=True)
+        gate_slope[row] = cot * gate * (1.0 - gate)
+        proj = dot(w_flip, zln, 1, 1)
+        mask = cell_mask_row(mask_scalars, mask_vector, rows, row)
+        for side in range(2):
+            base = 2 * side * hidden
+            sig = sigmoid(proj[base : base + hidden])
+            masked = mask * sig
+            slopes[row, base : base + hidden, :] = (
+                masked * (1.0 - sig) * proj[base + hidden : base + 2 * hidden]
+            )
+            slopes[row, base + hidden : base + 2 * hidden, :] = masked
+
+
+def tri_kernel(panels, products, matrices, wide, narrow):
+    count, depth, width = panels.shape
+    block = matrices.shape[0] // 2
+    total = matrices.shape[1]
+    wide[...] = panels[...].astype(F32).reshape(count * depth, width)
+    for h in range(block):
+        left = wide[pl.ds(h, total, stride=2 * block), :].astype(BF16)
+        right = wide[pl.ds(block + h, total, stride=2 * block), :].astype(BF16)
+        matrices[h] = left
+        matrices[block + h] = right
+        narrow[pl.ds(h, total, stride=block), :] = dot(left, right, 1, 1)
+    products[...] = narrow[...].astype(BF16).reshape(products.shape)
+
+
+def row_pair(ref, first, block):
+    count, _, width = ref.shape
+    both = ref[:, first * block : (first + 2) * block, :].astype(F32)
+    return [
+        both[:, n * block : (n + 1) * block, :].reshape(count * block, width) for n in range(2)
+    ]
+
+
+def hidden_norm(tri):
+    centered = tri - jnp.mean(tri, axis=0, keepdims=True)
+    variance = jnp.mean(centered * centered, axis=0, keepdims=True)
+    inv_std = lax.rsqrt(variance + 1e-05)
+    return centered * inv_std, inv_std
+
+
+def middle_kernel(products, d_hat_centered, d_products):
+    rows, hidden, width = d_hat_centered.shape
+    count = products.shape[0]
+    block = hidden // count
+    for first in range(0, rows, 2):
+        parts = []
+        for n, tri in enumerate(row_pair(products, first, block)):
+            tri_hat, inv_std = hidden_norm(tri)
+            d_hat = d_hat_centered[first + n]
+            cross = jnp.mean(d_hat * tri_hat, axis=0, keepdims=True)
+            d_tri = inv_std * (d_hat - tri_hat * cross)
+            parts.append(d_tri.reshape(count, block, width))
+        d_products[:, first * block : (first + 2) * block, :] = jnp.concatenate(
+            parts, axis=1
+        ).astype(BF16)
+
+
+def gate_back_kernel(products, gate_slope, out_gain, out_bias, w_out, w_gate, d_zln_gate):
+    rows = gate_slope.shape[0]
+    block = w_out.shape[0] // products.shape[0]
+    for first in range(0, rows, 2):
+        for n, tri in enumerate(row_pair(products, first, block)):
+            tri_hat, _ = hidden_norm(tri)
+            scaled = (tri_hat * out_gain[...] + out_bias[...]).astype(BF16)
+            proj_out = dot(scaled, w_out[...], 0, 0)
+            d_gate_pre = (proj_out * gate_slope[first + n]).astype(BF16)
+            d_zln_gate[first + n] = dot(d_gate_pre, w_gate[...], 1, 1)
+
+
+def products_kernel(d_products, matrices, d_panels, narrow, wide):
+    count, depth, width = d_products.shape
+    block = matrices.shape[0] // 2
+    total = matrices.shape[1]
+    narrow[...] = d_products[...].astype(F32).reshape(count * depth, width)
+    for h in range(block):
+        d_tri = narrow[pl.ds(h, total, stride=block), :].astype(BF16)
+        wide[pl.ds(h, total, stride=2 * block), :] = dot(d_tri, matrices[block + h], 1, 0)
+        wide[pl.ds(block + h, total, stride=2 * block), :] = dot(d_tri, matrices[h], 0, 0)
+    d_panels[...] = wide[...].astype(BF16).reshape(d_panels.shape)
+
+
+def finish_kernel(d_panels, slopes, d_zln_gate, pair, gain, w_proj, grad):
+    rows = pair.shape[0]
+    count, depth, width = d_panels.shape
+    block = depth // rows // 2
+    hidden = count * block
+    w_flip = transposed(w_proj[...])
+    for row in range(rows):
+        both = d_panels[:, row * 2 * block : (row + 1) * 2 * block, :].astype(F32)
+        parts = []
+        for side in range(2):
+            d_value = both[:, side * block : (side + 1) * block, :].reshape(hidden, width)
+            base = 2 * side * hidden
+            parts.append(d_value * slopes[row, base : base + hidden, :])
+            parts.append(d_value * slopes[row, base + hidden : base + 2 * hidden, :])
+        d_proj = jnp.concatenate(parts, axis=0).astype(BF16)
+        d_zln = dot(d_proj, w_flip, 0, 0) + d_zln_gate[row]
+        d_in = d_zln * gain[...]
+        normed, inv_std = input_norm(pair[row])
+        mean_grad = jnp.mean(d_in, axis=-1, keepdims=True)
+        mean_cross = jnp.mean(d_in * normed, axis=-1, keepdims=True)
+        grad[row] = (inv_std * (d_in - mean_grad - normed * mean_cross)).astype(BF16)
+
+
+def swap(values):
+    return lax.all_to_all(values, "row", split_axis=0, concat_axis=0, tiled=True)
+
+
+def kernel_shards(
+    pair,
+    cotangent,
+    residue_mask,
+    ln_in_gain,
+    ln_in_bias,
+    w_proj,
+    w_gate,
+    ln_out_gain,
+    ln_out_bias,
+    w_out,
+):
+    rows, width, channels = pair.shape
+    hidden = w_out.shape[0]
+    count = lax.axis_size("row")
+    block = hidden // count
+    total = rows * count
+    shape = jax.ShapeDtypeStruct
+    mask_vector = residue_mask.reshape(1, width)
+    gain, bias = ln_in_gain.reshape(1, channels), ln_in_bias.reshape(1, channels)
+    out_gain, out_bias = ln_out_gain.reshape(hidden, 1), ln_out_bias.reshape(hidden, 1)
+    cells = rows * width
+    (panels,) = call(
+        project_kernel,
+        "project",
+        [shape((count, rows * 2 * block, width), BF16)],
+        [pair, residue_mask, mask_vector, gain, bias, w_proj],
+        smem=(1,),
+        flops=2 * cells * channels * 4 * hidden,
+    )
+    panels = swap(panels)
+    d_hat_centered, gate_slope, slopes = call(
+        prepare_kernel,
+        "prepare",
+        [
+            shape((rows, hidden, width), F32),
+            shape((rows, width, channels), F32),
+            shape((rows, 4 * hidden, width), F32),
+        ],
+        [pair, cotangent, residue_mask, mask_vector, gain, bias, w_proj, w_gate, out_gain, w_out],
+        smem=(2,),
+        flops=2 * cells * channels * 6 * hidden,
+    )
+    wide = pltpu.VMEM((total * 2 * block, width), F32)
+    narrow = pltpu.VMEM((total * block, width), F32)
+    products, matrices = call(
+        tri_kernel,
+        "tri",
+        [shape((count, rows * block, width), BF16), shape((2 * block, total, width), BF16)],
+        [panels],
+        scratch=[wide, narrow],
+        flops=2 * block * total * width * total,
+    )
+    products = swap(products)
+    (d_products,) = call(
+        middle_kernel,
+        "middle",
+        [shape((count, rows * block, width), BF16)],
+        [products, d_hat_centered],
+        flops=20 * cells * hidden,
+    )
+    d_products = swap(d_products)
+    (d_zln_gate,) = call(
+        gate_back_kernel,
+        "gate_back",
+        [shape((rows, width, channels), F32)],
+        [products, gate_slope, out_gain, out_bias, w_out, w_gate],
+        flops=4 * cells * channels * hidden,
+    )
+    (d_panels,) = call(
+        products_kernel,
+        "products",
+        [shape((count, rows * 2 * block, width), BF16)],
+        [d_products, matrices],
+        scratch=[narrow, wide],
+        flops=4 * block * total * width * total,
+    )
+    d_panels = swap(d_panels)
+    (grad,) = call(
+        finish_kernel,
+        "finish",
+        [shape(pair.shape, BF16)],
+        [d_panels, slopes, d_zln_gate, pair, gain, w_proj],
+        flops=2 * cells * channels * 4 * hidden,
+    )
+    return grad
 
 
 def normalize(values, reduce_axis):
@@ -113,8 +408,9 @@
 
 
 def solution(mesh):
+    fits = mesh.shape["chan"] == 1 and mesh.shape["row"] <= 16
     return jax.shard_map(
-        shards,
+        kernel_shards if fits else shards,
         mesh=mesh,
         in_specs=(
             P(("grp", "row"), "chan", None),

time: 84 us -> 82.8 us (0.986)
  Pallas kernels: 0 us -> 10.9 us
  matrix products: 8.02 us -> 0 us
  other arithmetic: 2.38 us -> 0 us
  waiting for transfers between devices: 20 us -> 17.7 us
    pallas_call x0 -> x7, Pallas kernels: none -> 10.9 us  [call(): pl.pallas_call(kernel, name=name, out_shape=outs, in_specs=[pl.BlockSpec(...]
    dot_general x8 -> x0, matrix products: 8.02 us -> none  [the longest x1 2.41 us: shards(): jnp.einsum('rmd,cd->rmc', d_gate_pre, w_gate, preferred_element_type=jnp....]
    unnamed x19 -> x42, local copies, waits for them, and re-layouts: 2.48 us -> 10.4 us
    convert_element_type x7 -> x0, local copies, waits for them, and re-layouts: 6.1 us -> none  [the longest x4 4.2 us: gating(): masked_grad = d_value.astype(jnp.float32) * cell_mask]
    all_to_all x2, waiting for transfers between devices: 20 us -> 17.7 us  [swap(): lax.all_to_all(values, 'row', split_axis=0, concat_axis=0, tiled=True)]
    another operation x2 -> x0, local copies, waits for them, and re-layouts: 1.59 us -> none  [the longest x1 1.16 us: shards(): d_stack = jnp.stack([d_left, d_right]).astype(jnp.bfloat16)]
    convert_element_type x5 -> x0, other arithmetic: 1.11 us -> none  [the longest x1 0.69 us: shards(): mask_float = residue_mask.astype(jnp.float32)]
    another operation x4 -> x0, other arithmetic: 0.95 us -> none
  transfers between devices with their start and end apart: 2 -> 2, of which waited for: 2 -> 2; matrix products, arithmetic and copies ran while one was open for 5% -> 0% of each run, Pallas kernels for 0% -> 3%
where the time goes in v3:
time: 82.8 us; the launch traced here: 82.1 us
  blocking collectives  34.4 us (42%)
  waiting for transfers between devices  17.7 us (21%)
  Pallas kernels  10.9 us (13%)
  local copies, waits for them, and re-layouts  10.6 us (13%)
  starting transfers between devices  8.34 us (10%)
    all_to_all x2, blocking collectives, swap(): lax.all_to_all(values, 'row', split_axis=0, concat_axis=0, tiled=True)  34.4 us
    all_to_all x2, waiting for transfers between devices, swap(): lax.all_to_all(values, 'row', split_axis=0, concat_axis=0, tiled=True)  17.7 us
    pallas_call x7, Pallas kernels, call(): pl.pallas_call(kernel, name=name, out_shape=outs, in_specs=[pl.BlockSpec(...  10.9 us
    unnamed x42, local copies, waits for them, and re-layouts  10.4 us
    all_to_all x2, starting transfers between devices, swap(): lax.all_to_all(values, 'row', split_axis=0, concat_axis=0, tiled=True)  8.34 us
  transfers between devices with their start and end apart: 2, of which 2 were waited for; matrix products, arithmetic and copies ran while one was open for 0% of the time, Pallas kernels for 3%

profile of v3, /device:TPU:0, one launch (start us, length us, event | category | flops | bytes accessed | tf_op | source)
XLA Modules:
  0.0 82.1 jit_solution(17489695869617702414)
XLA Ops:
  0.0 1.0 %copy-done = bf16[8,128,128]{2,1,0:T(8,128)(2,1)S(1)} copy-done((bf16[8,128,128]{2,1,0:T(8,128)(2,1)S(1)}, bf16[8,128,128]{2,1,0:T(8,128)(2,1)}, u32[]{:S(2)}) %copy-start) | copy-done | bytes 262168
  1.0 0.9 %copy-done.2 = bf16[128,512]{1,0:T(8,128)(2,1)S(1)} copy-done((bf16[128,512]{1,0:T(8,128)(2,1)S(1)}, bf16[128,512]{1,0:T(8,128)(2,1)}, u32[]{:S(2)}) %copy-start.2) | copy-done | bytes 131096
  1.9 0.7 copy-done.13
  2.6 0.7 copy-done.15
  3.2 0.7 copy-done.17
  3.9 1.6 %project.1 = bf16[16,128,128]{2,1,0:T(8,128)(2,1)S(1)} custom-call(bf16[8,128,128]{2,1,0:T(8,128)(2,1)S(1)} %copy-done, s32[128]{0:T(128)S(1)} %copy-done.13, s32[1,128]{1,0:T(1,128)S(1)} %bitcast.5, f32[1,128]{1,0:T(1,128)S(1)} %bitcast.7, f32[1,128]{1,0:T(1,128)S(1)} %bitcast.10, bf16[128,512]{1,0:T(8,128)(2,1)S(1)} %copy-done.2), custom_call_target="tpu_custom_call" | custom-call | flops 134217728 | bytes 919552 | tf_op jit(solution)/shard_map/project/pallas_call | solution.py:42
  5.5 21.6 %all_to_all.20.panels = bf16[16,128,128]{2,1,0:T(8,128)(2,1)S(1)} all-to-all(bf16[16,128,128]{2,1,0:T(8,128)(2,1)S(1)} %project.1), channel_id=1, replica_groups=mesh['grp'=2,'row'=16,'chan'=1] {'row'}, dimensions={0} | all-to-all | bytes 1048576 | tf_op jit(solution)/shard_map/all_to_all | solution.py:211
  27.1 1.2 %tri.1 = (bf16[16,64,128]{2,1,0:T(8,128)(2,1)}, bf16[16,128,128]{2,1,0:T(8,128)(2,1)S(1)}) custom-call(bf16[16,128,128]{2,1,0:T(8,128)(2,1)S(1)} %all_to_all.20.panels), custom_call_target="tpu_custom_call" | custom-call | flops 33554432 | bytes 1310720 | tf_op jit(solution)/shard_map/tri/pallas_call | solution.py:42
  28.3 0.8 copy-done.6
  29.1 4.1 %all-to-all-start.1 = ((bf16[16,64,128]{2,1,0:T(8,128)(2,1)}), bf16[16,64,128]{2,1,0:T(8,128)(2,1)S(1)}, u32[]{:S(2)}, u32[]{:S(2)}) async-start(bf16[16,64,128]{2,1,0:T(8,128)(2,1)} %get-tuple-element.10), calls=%async_computation.1 | async-start | bytes 524288 | tf_op jit(solution)/shard_map/all_to_all | solution.py:211
  33.4 0.9 %copy-done.10 = bf16[8,128,128]{2,1,0:T(8,128)(2,1)S(1)} copy-done((bf16[8,128,128]{2,1,0:T(8,128)(2,1)S(1)}, bf16[8,128,128]{2,1,0:T(8,128)(2,1)}, u32[]{:S(2)}) %copy-start.10) | copy-done | bytes 262168
  34.3 2.0 %prepare.1 = (f32[8,128,128]{2,1,0:T(8,128)S(1)}, f32[8,128,128]{2,1,0:T(8,128)S(1)}, f32[8,512,128]{2,1,0:T(8,128)S(1)}) custom-call(bf16[8,128,128]{2,1,0:T(8,128)(2,1)S(1)} %copy-done.1, bf16[8,128,128]{2,1,0:T(8,128)(2,1)S(1)} %copy-done.10, s32[128]{0:T(128)S(1)} %copy-done.14, s32[1,128]{1,0:T(1,128)S(1)} %bitcast.6, f32[1,128]{1,0:T(1,128)S(1)} %bitcast.8, ...), custom_call_target="tpu_custom_call" | custom-call | flops 201326592 | bytes 3869184 | tf_op jit(solution)/shard_map/prepare/pallas_call | solution.py:42
  36.3 0.8 copy-done.4
  37.1 0.8 copy-done.8
  37.9 5.3 %all-to-all-done.1.products = bf16[16,64,128]{2,1,0:T(8,128)(2,1)S(1)} async-done(((bf16[16,64,128]{2,1,0:T(8,128)(2,1)}), bf16[16,64,128]{2,1,0:T(8,128)(2,1)S(1)}, u32[]{:S(2)}, u32[]{:S(2)}) %all-to-all-start.1) | async-done | bytes 262176 | tf_op jit(solution)/shard_map/all_to_all | solution.py:211
  43.2 1.0 %copy-done.9 = f32[8,128,128]{2,1,0:T(8,128)S(1)} copy-done((f32[8,128,128]{2,1,0:T(8,128)S(1)}, f32[8,128,128]{2,1,0:T(8,128)}, u32[]{:S(2)}) %copy-start.9) | copy-done | bytes 524312
  44.6 12.8 %all_to_all.21.d_products = bf16[16,64,128]{2,1,0:T(8,128)(2,1)S(1)} all-to-all(bf16[16,64,128]{2,1,0:T(8,128)(2,1)S(1)} %middle.1), channel_id=1, replica_groups=mesh['grp'=2,'row'=16,'chan'=1] {'row'}, dimensions={0} | all-to-all | bytes 524288 | tf_op jit(solution)/shard_map/all_to_all | solution.py:211
  57.4 1.0 %copy-done.7 = bf16[16,128,128]{2,1,0:T(8,128)(2,1)S(1)} copy-done((bf16[16,128,128]{2,1,0:T(8,128)(2,1)S(1)}, bf16[16,128,128]{2,1,0:T(8,128)(2,1)}, u32[]{:S(2)}) %copy-start.7) | copy-done | bytes 524312
  58.4 1.5 %products.1 = bf16[16,128,128]{2,1,0:T(8,128)(2,1)} custom-call(bf16[16,64,128]{2,1,0:T(8,128)(2,1)S(1)} %all_to_all.21.d_products, bf16[16,128,128]{2,1,0:T(8,128)(2,1)S(1)} %copy-done.7), custom_call_target="tpu_custom_call" | custom-call | flops 67108864 | bytes 1310720 | tf_op jit(solution)/shard_map/products/pallas_call | solution.py:42
  59.9 4.2 %all-to-all-start.3 = ((bf16[16,128,128]{2,1,0:T(8,128)(2,1)}), bf16[16,128,128]{2,1,0:T(8,128)(2,1)}, u32[]{:S(2)}, u32[]{:S(2)}) async-start(bf16[16,128,128]{2,1,0:T(8,128)(2,1)} %products.1), calls=%async_computation.3 | async-start | bytes 1048576 | tf_op jit(solution)/shard_map/all_to_all | solution.py:211
  64.3 1.0 %copy-done.5 = f32[8,128,128]{2,1,0:T(8,128)S(1)} copy-done((f32[8,128,128]{2,1,0:T(8,128)S(1)}, f32[8,128,128]{2,1,0:T(8,128)}, u32[]{:S(2)}) %copy-start.5) | copy-done | bytes 524312
  65.3 0.9 %gate_back.1.d_zln_gate = f32[8,128,128]{2,1,0:T(8,128)S(1)} custom-call(bf16[16,64,128]{2,1,0:T(8,128)(2,1)S(1)} %all-to-all-done.1.products, f32[8,128,128]{2,1,0:T(8,128)S(1)} %copy-done.5, f32[128,1]{1,0:T(8,128)S(1)} %copy.11.out_gain, f32[128,1]{1,0:T(8,128)S(1)} %copy.13.out_bias, bf16[128,128]{1,0:T(8,128)(2,1)S(1)} %copy-done.12, ...), custom_call_target="tpu_custom_call" | custom-call | flops 67108864 | bytes 1377280 | tf_op jit(solution)/shard_map/gate_back/pallas_call | solution.py:42
  66.2 12.4 %all-to-all-done.3.d_panels = bf16[16,128,128]{2,1,0:T(8,128)(2,1)} async-done(((bf16[16,128,128]{2,1,0:T(8,128)(2,1)}), bf16[16,128,128]{2,1,0:T(8,128)(2,1)}, u32[]{:S(2)}, u32[]{:S(2)}) %all-to-all-start.3) | async-done | bytes 524320 | tf_op jit(solution)/shard_map/all_to_all | solution.py:211
  78.6 3.5 %finish.1 = bf16[8,128,128]{2,1,0:T(8,128)(2,1)} custom-call(bf16[16,128,128]{2,1,0:T(8,128)(2,1)} %all-to-all-done.3.d_panels, f32[8,512,128]{2,1,0:T(8,128)S(1)} %get-tuple-element.13.slopes, f32[8,128,128]{2,1,0:T(8,128)S(1)} %gate_back.1.d_zln_gate, bf16[8,128,128]{2,1,0:T(8,128)(2,1)S(1)} %copy-done.1, f32[1,128]{1,0:T(1,128)S(1)} %bitcast.9, ...), custom_call_target="tpu_custom_call" | custom-call | flops 134217728 | bytes 3801600 | tf_op jit(solution)/shard_map/finish/pallas_call | solution.py:42
  (33 shorter events, 0.6 us)
Async XLA Ops:
  0.0 33.3 %copy-start.14 = (s32[128]{0:T(128)S(1)}, s32[128]{0:T(128)}, u32[]{:S(2)}) copy-start(s32[128]{0:T(128)} %mask_scalars.3) | copy-start | bytes 1540
  0.0 33.3 %copy-start.16 = (f32[128]{0:T(128)S(1)}, f32[128]{0:T(128)}, u32[]{:S(2)}) copy-start(f32[128]{0:T(128)} %param.13) | copy-start | bytes 1540
  0.0 33.3 %copy-start.18 = (f32[128]{0:T(128)S(1)}, f32[128]{0:T(128)}, u32[]{:S(2)}) copy-start(f32[128]{0:T(128)} %param.14) | copy-start | bytes 1540
  0.0 33.2 %copy-start.19 = (f32[128]{0:T(128)S(1)}, f32[128]{0:T(128)}, u32[]{:S(2)}) copy-start(f32[128]{0:T(128)} %param.17) | copy-start | bytes 1540
  0.0 1.0 %copy-start = (bf16[8,128,128]{2,1,0:T(8,128)(2,1)S(1)}, bf16[8,128,128]{2,1,0:T(8,128)(2,1)}, u32[]{:S(2)}) copy-start(bf16[8,128,128]{2,1,0:T(8,128)(2,1)} %pair.5) | copy-start | bytes 786436
  1.0 0.9 %copy-start.2 = (bf16[128,512]{1,0:T(8,128)(2,1)S(1)}, bf16[128,512]{1,0:T(8,128)(2,1)}, u32[]{:S(2)}) copy-start(bf16[128,512]{1,0:T(8,128)(2,1)} %w_proj.5) | copy-start | bytes 393220
  1.9 0.7 copy-start.13
  2.6 0.7 copy-start.15
  3.2 0.7 copy-start.17
  3.9 29.5 %copy-start.1 = (bf16[8,128,128]{2,1,0:T(8,128)(2,1)S(1)}, bf16[8,128,128]{2,1,0:T(8,128)(2,1)}, u32[]{:S(2)}) copy-start(bf16[8,128,128]{2,1,0:T(8,128)(2,1)} %pair.5) | copy-start | bytes 786436
  3.9 29.5 %copy-start.3 = (bf16[128,512]{1,0:T(8,128)(2,1)S(1)}, bf16[128,512]{1,0:T(8,128)(2,1)}, u32[]{:S(2)}) copy-start(bf16[128,512]{1,0:T(8,128)(2,1)} %w_proj.5) | copy-start | bytes 393220
  3.9 29.5 %copy-start.11 = (bf16[128,128]{1,0:T(8,128)(2,1)S(1)}, bf16[128,128]{1,0:T(8,128)(2,1)}, u32[]{:S(2)}) copy-start(bf16[128,128]{1,0:T(8,128)(2,1)} %w_gate.3) | copy-start | bytes 98308
  3.9 29.5 %copy-start.12 = (bf16[128,128]{1,0:T(8,128)(2,1)S(1)}, bf16[128,128]{1,0:T(8,128)(2,1)}, u32[]{:S(2)}) copy-start(bf16[128,128]{1,0:T(8,128)(2,1)} %w_out.3) | copy-start | bytes 98308
  28.3 0.8 copy-start.6
  29.1 14.2 %all-to-all-start.1 = ((bf16[16,64,128]{2,1,0:T(8,128)(2,1)}), bf16[16,64,128]{2,1,0:T(8,128)(2,1)S(1)}, u32[]{:S(2)}, u32[]{:S(2)}) async-start(bf16[16,64,128]{2,1,0:T(8,128)(2,1)} %get-tuple-element.10), calls=%async_computation.1 | async-start | bytes 524288 | tf_op jit(solution)/shard_map/all_to_all | solution.py:211
  33.4 1.0 %copy-start.10 = (bf16[8,128,128]{2,1,0:T(8,128)(2,1)S(1)}, bf16[8,128,128]{2,1,0:T(8,128)(2,1)}, u32[]{:S(2)}) copy-start(bf16[8,128,128]{2,1,0:T(8,128)(2,1)} %cotangent.1) | copy-start | bytes 786436
  36.3 0.8 copy-start.4
  37.1 0.8 copy-start.8
  37.9 26.2 %copy-start.20 = (f32[128]{0:T(128)S(1)}, f32[128]{0:T(128)}, u32[]{:S(2)}) copy-start(f32[128]{0:T(128)} %param.18) | copy-start | bytes 1540
  43.2 1.0 %copy-start.9 = (f32[8,128,128]{2,1,0:T(8,128)S(1)}, f32[8,128,128]{2,1,0:T(8,128)}, u32[]{:S(2)}) copy-start(f32[8,128,128]{2,1,0:T(8,128)} %copy-done.8) | copy-start | bytes 1572868
  57.4 1.0 %copy-start.7 = (bf16[16,128,128]{2,1,0:T(8,128)(2,1)S(1)}, bf16[16,128,128]{2,1,0:T(8,128)(2,1)}, u32[]{:S(2)}) copy-start(bf16[16,128,128]{2,1,0:T(8,128)(2,1)} %copy-done.6) | copy-start | bytes 1572868
  59.9 18.7 %all-to-all-start.3 = ((bf16[16,128,128]{2,1,0:T(8,128)(2,1)}), bf16[16,128,128]{2,1,0:T(8,128)(2,1)}, u32[]{:S(2)}, u32[]{:S(2)}) async-start(bf16[16,128,128]{2,1,0:T(8,128)(2,1)} %products.1), calls=%async_computation.3 | async-start | bytes 1048576 | tf_op jit(solution)/shard_map/all_to_all | solution.py:211
  64.3 1.0 %copy-start.5 = (f32[8,128,128]{2,1,0:T(8,128)S(1)}, f32[8,128,128]{2,1,0:T(8,128)}, u32[]{:S(2)}) copy-start(f32[8,128,128]{2,1,0:T(8,128)} %copy-done.4) | copy-start | bytes 1572868

commit v4 on v3

--- a/solution.py
+++ b/solution.py
@@ -26,49 +26,81 @@
     return 1.0 / (1.0 + jnp.exp(-values))
 
 
-def input_norm(pair_row):
-    values = pair_row.astype(F32)
-    centered = values - jnp.mean(values, axis=-1, keepdims=True)
-    variance = jnp.mean(centered * centered, axis=-1, keepdims=True)
+def column(row):
+    size = row.shape[1]
+    return jnp.transpose(jnp.broadcast_to(row, (size, size)))
+
+
+def norm_rows(values):
+    centered = values - jnp.mean(values, axis=0, keepdims=True)
+    variance = jnp.mean(centered * centered, axis=0, keepdims=True)
     inv_std = lax.rsqrt(variance + 1e-05)
     return centered * inv_std, inv_std
 
 
-def call(kernel, name, outs, args, scratch=(), smem=(), flops=0):
-    spaces = [pltpu.SMEM if n in smem else pltpu.VMEM for n in range(len(args))]
+def call(kernel, name, outs, args, fetched=(), scratch=(), flops=0, limit=VMEM_LIMIT):
     moved = sum(a.size * a.dtype.itemsize for a in args) + sum(
         o.size * jnp.dtype(o.dtype).itemsize for o in outs
     )
+    n_args, n_outs, n_fetched = len(args), len(outs), len(fetched)
+
+    def body(*refs):
+        ins = list(refs[:n_args])
+        rest = refs[n_args + n_outs :]
+        copies = []
+        for n, place in enumerate(fetched):
+            copies.append(pltpu.make_async_copy(ins[place], rest[n], rest[n_fetched].at[n]))
+            ins[place] = rest[n]
+        for copy in copies:
+            copy.start()
+        for copy in copies:
+            copy.wait()
+        kernel(*ins, *refs[n_args : n_args + n_outs], *rest[n_fetched + (n_fetched > 0) :])
+
+    buffers = [pltpu.VMEM(args[place].shape, args[place].dtype) for place in fetched]
+    if fetched:
+        buffers.append(pltpu.SemaphoreType.DMA((n_fetched,)))
     return pl.pallas_call(
-        kernel,
+        body,
         name=name,
         out_shape=outs,
-        in_specs=[pl.BlockSpec(memory_space=space) for space in spaces],
+        in_specs=[
+            pl.BlockSpec(memory_space=pltpu.HBM if n in fetched else pltpu.VMEM)
+            for n in range(n_args)
+        ],
         out_specs=[pl.BlockSpec(memory_space=pltpu.VMEM) for _ in outs],
-        scratch_shapes=list(scratch),
-        compiler_params=pltpu.CompilerParams(vmem_limit_bytes=VMEM_LIMIT),
+        scratch_shapes=buffers + list(scratch),
+        compiler_params=pltpu.CompilerParams(vmem_limit_bytes=limit),
         cost_estimate=pl.CostEstimate(flops=flops, bytes_accessed=moved, transcendentals=0),
     )(*args)
 
 
-def cell_mask_row(mask_scalars, mask_vector, rows, row):
-    own = mask_scalars[lax.axis_index("row") * rows + row].astype(F32)
-    return mask_vector[...].astype(F32) * own
-
-
-def project_kernel(pair, mask_scalars, mask_vector, gain, bias, w_proj, panels):
+def cell_masks(mask, rows):
+    columns = mask[...].astype(F32)
+    shape = (rows, columns.shape[1])
+    first = lax.axis_index("row") * rows
+    own = lax.broadcasted_iota(jnp.int32, shape, 1) == (
+        lax.broadcasted_iota(jnp.int32, shape, 0) + first
+    )
+    row_mask = jnp.sum(jnp.where(own, columns, 0.0), axis=1, keepdims=True)
+    cells = row_mask * columns
+    return [cells[row : row + 1] for row in range(rows)]
+
+
+def project_kernel(pair, mask, gain, bias, w_proj, panels):
     rows = pair.shape[0]
     hidden = w_proj.shape[1] // 4
     count, _, width = panels.shape
     block = hidden // count
     w_flip = transposed(w_proj[...])
+    gain_col, bias_col = column(gain[...]), column(bias[...])
+    masks = cell_masks(mask, rows)
     for row in range(rows):
-        normed, _ = input_norm(pair[row])
-        zln = (normed * gain[...] + bias[...]).astype(BF16)
-        proj = dot(w_flip, zln, 1, 1)
-        mask = cell_mask_row(mask_scalars, mask_vector, rows, row)
-        left = mask * sigmoid(proj[:hidden]) * proj[hidden : 2 * hidden]
-        right = mask * sigmoid(proj[2 * hidden : 3 * hidden]) * proj[3 * hidden :]
+        normed, _ = norm_rows(jnp.transpose(pair[row].astype(F32)))
+        zln = (normed * gain_col + bias_col).astype(BF16)
+        proj = dot(w_flip, zln, 1, 0)
+        left = masks[row] * sigmoid(proj[:hidden]) * proj[hidden : 2 * hidden]
+        right = masks[row] * sigmoid(proj[2 * hidden : 3 * hidden]) * proj[3 * hidden :]
         both = jnp.concatenate(
             [left.reshape(count, block, width), right.reshape(count, block, width)], axis=1
         )
@@ -76,42 +108,20 @@
 
 
 def prepare_kernel(
-    pair,
-    cotangent,
-    mask_scalars,
-    mask_vector,
-    gain,
-    bias,
-    w_proj,
-    w_gate,
-    out_gain,
-    w_out,
-    d_hat_centered,
-    gate_slope,
-    slopes,
+    pair, cotangent, gain, bias, w_gate, out_gain, w_out, d_hat_centered, gate_slope
 ):
-    rows = pair.shape[0]
-    hidden = w_out.shape[0]
-    w_flip = transposed(w_proj[...])
-    for row in range(rows):
-        normed, _ = input_norm(pair[row])
-        zln = (normed * gain[...] + bias[...]).astype(BF16)
-        gate = sigmoid(dot(zln, w_gate[...], 1, 0))
-        cot = cotangent[row].astype(F32)
+    gate_flip = transposed(w_gate[...])
+    gain_col, bias_col = column(gain[...]), column(bias[...])
+    out_gain_col = column(out_gain[...])
+    for row in range(pair.shape[0]):
+        normed, _ = norm_rows(jnp.transpose(pair[row].astype(F32)))
+        zln = (normed * gain_col + bias_col).astype(BF16)
+        gate = sigmoid(dot(gate_flip, zln, 1, 0))
+        cot = jnp.transpose(cotangent[row].astype(F32))
         d_scaled = (cot * gate).astype(BF16)
-        d_hat = dot(w_out[...], d_scaled, 1, 1) * out_gain[...]
+        d_hat = dot(w_out[...], d_scaled, 1, 0) * out_gain_col
         d_hat_centered[row] = d_hat - jnp.mean(d_hat, axis=0, keepdims=True)
         gate_slope[row] = cot * gate * (1.0 - gate)
-        proj = dot(w_flip, zln, 1, 1)
-        mask = cell_mask_row(mask_scalars, mask_vector, rows, row)
-        for side in range(2):
-            base = 2 * side * hidden
-            sig = sigmoid(proj[base : base + hidden])
-            masked = mask * sig
-            slopes[row, base : base + hidden, :] = (
-                masked * (1.0 - sig) * proj[base + hidden : base + 2 * hidden]
-            )
-            slopes[row, base + hidden : base + 2 * hidden, :] = masked
 
 
 def tri_kernel(panels, products, matrices, wide, narrow):
@@ -136,13 +146,6 @@
     ]
 
 
-def hidden_norm(tri):
-    centered = tri - jnp.mean(tri, axis=0, keepdims=True)
-    variance = jnp.mean(centered * centered, axis=0, keepdims=True)
-    inv_std = lax.rsqrt(variance + 1e-05)
-    return centered * inv_std, inv_std
-
-
 def middle_kernel(products, d_hat_centered, d_products):
     rows, hidden, width = d_hat_centered.shape
     count = products.shape[0]
@@ -150,7 +153,7 @@
     for first in range(0, rows, 2):
         parts = []
         for n, tri in enumerate(row_pair(products, first, block)):
-            tri_hat, inv_std = hidden_norm(tri)
+            tri_hat, inv_std = norm_rows(tri)
             d_hat = d_hat_centered[first + n]
             cross = jnp.mean(d_hat * tri_hat, axis=0, keepdims=True)
             d_tri = inv_std * (d_hat - tri_hat * cross)
@@ -158,18 +161,6 @@
         d_products[:, first * block : (first + 2) * block, :] = jnp.concatenate(
             parts, axis=1
         ).astype(BF16)
-
-
-def gate_back_kernel(products, gate_slope, out_gain, out_bias, w_out, w_gate, d_zln_gate):
-    rows = gate_slope.shape[0]
-    block = w_out.shape[0] // products.shape[0]
-    for first in range(0, rows, 2):
-        for n, tri in enumerate(row_pair(products, first, block)):
-            tri_hat, _ = hidden_norm(tri)
-            scaled = (tri_hat * out_gain[...] + out_bias[...]).astype(BF16)
-            proj_out = dot(scaled, w_out[...], 0, 0)
-            d_gate_pre = (proj_out * gate_slope[first + n]).astype(BF16)
-            d_zln_gate[first + n] = dot(d_gate_pre, w_gate[...], 1, 1)
 
 
 def products_kernel(d_products, matrices, d_panels, narrow, wide):
@@ -184,27 +175,71 @@
     d_panels[...] = wide[...].astype(BF16).reshape(d_panels.shape)
 
 
-def finish_kernel(d_panels, slopes, d_zln_gate, pair, gain, w_proj, grad):
+def slopes_kernel(
+    products,
+    gate_slope,
+    pair,
+    mask,
+    gain,
+    bias,
+    w_proj,
+    w_gate,
+    out_gain,
+    out_bias,
+    w_out,
+    slopes,
+    d_zln_gate,
+    normed_in,
+    inv_in,
+):
     rows = pair.shape[0]
+    hidden = w_out.shape[0]
+    block = hidden // products.shape[0]
+    w_flip = transposed(w_proj[...])
+    out_flip = transposed(w_out[...])
+    gain_col, bias_col = column(gain[...]), column(bias[...])
+    out_gain_col, out_bias_col = column(out_gain[...]), column(out_bias[...])
+    masks = cell_masks(mask, rows)
+    for row in range(rows):
+        tri_hat, _ = norm_rows(row_pair(products, row - row % 2, block)[row % 2])
+        scaled = (tri_hat * out_gain_col + out_bias_col).astype(BF16)
+        d_gate_pre = (dot(out_flip, scaled, 1, 0) * gate_slope[row]).astype(BF16)
+        d_zln_gate[row] = dot(w_gate[...], d_gate_pre, 1, 0)
+        normed, inv_std = norm_rows(jnp.transpose(pair[row].astype(F32)))
+        normed_in[row] = normed
+        inv_in[row : row + 1] = inv_std
+        zln = (normed * gain_col + bias_col).astype(BF16)
+        proj = dot(w_flip, zln, 1, 0)
+        for side in range(2):
+            base = 2 * side * hidden
+            sig = sigmoid(proj[base : base + hidden])
+            masked = masks[row] * sig
+            value = masked * (1.0 - sig) * proj[base + hidden : base + 2 * hidden]
+            slopes[row, base : base + hidden, :] = value.astype(slopes.dtype)
+            slopes[row, base + hidden : base + 2 * hidden, :] = masked.astype(slopes.dtype)
+
+
+def finish_kernel(d_panels, slopes, d_zln_gate, normed_in, inv_in, gain, w_proj, grad):
+    rows = grad.shape[0]
     count, depth, width = d_panels.shape
     block = depth // rows // 2
     hidden = count * block
-    w_flip = transposed(w_proj[...])
+    gain_col = column(gain[...])
     for row in range(rows):
         both = d_panels[:, row * 2 * block : (row + 1) * 2 * block, :].astype(F32)
         parts = []
         for side in range(2):
             d_value = both[:, side * block : (side + 1) * block, :].reshape(hidden, width)
-            base = 2 * side * hidden
-            parts.append(d_value * slopes[row, base : base + hidden, :])
-            parts.append(d_value * slopes[row, base + hidden : base + 2 * hidden, :])
-        d_proj = jnp.concatenate(parts, axis=0).astype(BF16)
-        d_zln = dot(d_proj, w_flip, 0, 0) + d_zln_gate[row]
-        d_in = d_zln * gain[...]
-        normed, inv_std = input_norm(pair[row])
-        mean_grad = jnp.mean(d_in, axis=-1, keepdims=True)
-        mean_cross = jnp.mean(d_in * normed, axis=-1, keepdims=True)
-        grad[row] = (inv_std * (d_in - mean_grad - normed * mean_cross)).astype(BF16)
+            for base in (2 * side * hidden, (2 * side + 1) * hidden):
+                slope = slopes[row, base : base + hidden, :].astype(F32)
+                parts.append((d_value * slope).astype(BF16))
+        d_zln = dot(w_proj[...], jnp.concatenate(parts, axis=0), 1, 0) + d_zln_gate[row]
+        d_in = d_zln * gain_col
+        normed = normed_in[row]
+        mean_grad = jnp.mean(d_in, axis=0, keepdims=True)
+        mean_cross = jnp.mean(d_in * normed, axis=0, keepdims=True)
+        result = inv_in[row : row + 1] * (d_in - mean_grad - normed * mean_cross)
+        grad[row] = jnp.transpose(result).astype(BF16)
 
 
 def swap(values):
@@ -229,30 +264,27 @@
     block = hidden // count
     total = rows * count
     shape = jax.ShapeDtypeStruct
-    mask_vector = residue_mask.reshape(1, width)
+    mask = residue_mask.reshape(1, width)
     gain, bias = ln_in_gain.reshape(1, channels), ln_in_bias.reshape(1, channels)
-    out_gain, out_bias = ln_out_gain.reshape(hidden, 1), ln_out_bias.reshape(hidden, 1)
+    out_gain, out_bias = ln_out_gain.reshape(1, hidden), ln_out_bias.reshape(1, hidden)
     cells = rows * width
     (panels,) = call(
         project_kernel,
         "project",
         [shape((count, rows * 2 * block, width), BF16)],
-        [pair, residue_mask, mask_vector, gain, bias, w_proj],
-        smem=(1,),
+        [pair, mask, gain, bias, w_proj],
+        fetched=range(5),
         flops=2 * cells * channels * 4 * hidden,
+        limit=64 * 1024 * 1024 - 640 * 1024,
     )
     panels = swap(panels)
-    d_hat_centered, gate_slope, slopes = call(
+    d_hat_centered, gate_slope = call(
         prepare_kernel,
         "prepare",
-        [
-            shape((rows, hidden, width), F32),
-            shape((rows, width, channels), F32),
-            shape((rows, 4 * hidden, width), F32),
-        ],
-        [pair, cotangent, residue_mask, mask_vector, gain, bias, w_proj, w_gate, out_gain, w_out],
-        smem=(2,),
-        flops=2 * cells * channels * 6 * hidden,
+        [shape((rows, hidden, width), F32), shape((rows, channels, width), F32)],
+        [pair, cotangent, gain, bias, w_gate, out_gain, w_out],
+        fetched=range(7),
+        flops=2 * cells * channels * 2 * hidden,
     )
     wide = pltpu.VMEM((total * 2 * block, width), F32)
     narrow = pltpu.VMEM((total * block, width), F32)
@@ -273,13 +305,6 @@
         flops=20 * cells * hidden,
     )
     d_products = swap(d_products)
-    (d_zln_gate,) = call(
-        gate_back_kernel,
-        "gate_back",
-        [shape((rows, width, channels), F32)],
-        [products, gate_slope, out_gain, out_bias, w_out, w_gate],
-        flops=4 * cells * channels * hidden,
-    )
     (d_panels,) = call(
         products_kernel,
         "products",
@@ -289,11 +314,37 @@
         flops=4 * block * total * width * total,
     )
     d_panels = swap(d_panels)
+    slopes, d_zln_gate, normed_in, inv_in = call(
+        slopes_kernel,
+        "slopes",
+        [
+            shape((rows, 4 * hidden, width), BF16),
+            shape((rows, channels, width), F32),
+            shape((rows, channels, width), F32),
+            shape((rows, width), F32),
+        ],
+        [
+            products,
+            gate_slope,
+            pair,
+            mask,
+            gain,
+            bias,
+            w_proj,
+            w_gate,
+            out_gain,
+            out_bias,
+            w_out,
+        ],
+        fetched=range(2, 11),
+        flops=2 * cells * channels * 6 * hidden,
+    )
     (grad,) = call(
         finish_kernel,
         "finish",
         [shape(pair.shape, BF16)],
-        [d_panels, slopes, d_zln_gate, pair, gain, w_proj],
+        [d_panels, slopes, d_zln_gate, normed_in, inv_in, gain, w_proj],
+        fetched=(5, 6),
         flops=2 * cells * channels * 4 * hidden,
     )
     return grad

time: 82.8 us -> 74.6 us (0.901)
  local copies, waits for them, and re-layouts: 10.6 us -> 3.13 us
  Pallas kernels: 10.9 us -> 9.48 us
  waiting for transfers between devices: 17.7 us -> 18.7 us
    unnamed x42 -> x24, local copies, waits for them, and re-layouts: 10.4 us -> 3.13 us
    pallas_call x7, Pallas kernels: 10.9 us -> 9.48 us  [call(): pl.pallas_call(body, name=name, out_shape=outs, in_specs=[pl.BlockSpec(me...]
    all_to_all x2, waiting for transfers between devices: 17.7 us -> 18.7 us  [swap(): lax.all_to_all(values, 'row', split_axis=0, concat_axis=0, tiled=True)]
where the time goes in v4:
time: 74.6 us; the launch traced here: 74.1 us
  blocking collectives  34.7 us (47%)
  waiting for transfers between devices  18.7 us (25%)
  Pallas kernels  9.48 us (13%)
  starting transfers between devices  7.93 us (11%)
  local copies, waits for them, and re-layouts  3.13 us (4%)
    all_to_all x2, blocking collectives, swap(): lax.all_to_all(values, 'row', split_axis=0, concat_axis=0, tiled=True)  34.7 us
    all_to_all x2, waiting for transfers between devices, swap(): lax.all_to_all(values, 'row', split_axis=0, concat_axis=0, tiled=True)  18.7 us
    pallas_call x7, Pallas kernels, call(): pl.pallas_call(body, name=name, out_shape=outs, in_specs=[pl.BlockSpec(me...  9.48 us
    all_to_all x2, starting transfers between devices, swap(): lax.all_to_all(values, 'row', split_axis=0, concat_axis=0, tiled=True)  7.93 us
    unnamed x24, local copies, waits for them, and re-layouts  3.13 us
  transfers between devices with their start and end apart: 2, of which 2 were waited for; matrix products, arithmetic and copies ran while one was open for 0% of the time, Pallas kernels for 3%

profile of v4, /device:TPU:0, one launch (start us, length us, event | category | flops | bytes accessed | tf_op | source)
XLA Modules:
  0.0 74.1 jit_solution(16760617116834635584)
XLA Ops:
  0.0 2.5 %project.1 = bf16[16,128,128]{2,1,0:T(8,128)(2,1)} custom-call(bf16[8,128,128]{2,1,0:T(8,128)(2,1)} %refs_2_.1, s32[1,128]{1,0:T(1,128)} %bitcast.12, f32[1,128]{1,0:T(1,128)} %bitcast.5, f32[1,128]{1,0:T(1,128)} %bitcast.9, bf16[128,512]{1,0:T(8,128)(2,1)} %refs_6_.5), custom_call_target="tpu_custom_call" | custom-call | flops 134217728 | bytes 919040 | tf_op jit(solution)/shard_map/project/pallas_call | solution.py:63
  2.5 21.8 %all_to_all.20.refs_0_ = bf16[16,128,128]{2,1,0:T(8,128)(2,1)S(1)} all-to-all(bf16[16,128,128]{2,1,0:T(8,128)(2,1)} %project.1), channel_id=1, replica_groups=mesh['grp'=2,'row'=16,'chan'=1] {'row'}, dimensions={0} | all-to-all | bytes 1048576 | tf_op jit(solution)/shard_map/all_to_all | solution.py:246
  24.4 1.2 %tri.1 = (bf16[16,64,128]{2,1,0:T(8,128)(2,1)}, bf16[16,128,128]{2,1,0:T(8,128)(2,1)S(1)}) custom-call(bf16[16,128,128]{2,1,0:T(8,128)(2,1)S(1)} %all_to_all.20.refs_0_), custom_call_target="tpu_custom_call" | custom-call | flops 33554432 | bytes 1310720 | tf_op jit(solution)/shard_map/tri/pallas_call | solution.py:63
  25.6 4.2 %all-to-all-start.1 = ((bf16[16,64,128]{2,1,0:T(8,128)(2,1)}), bf16[16,64,128]{2,1,0:T(8,128)(2,1)S(1)}, u32[]{:S(2)}, u32[]{:S(2)}) async-start(bf16[16,64,128]{2,1,0:T(8,128)(2,1)} %get-tuple-element.13), calls=%async_computation.1 | async-start | bytes 524288 | tf_op jit(solution)/shard_map/all_to_all | solution.py:246
  29.8 0.0 copy-start.7
  29.8 0.0 copy-start.8
  29.8 0.0 copy-start.10
  29.9 0.6 copy-done.7
  30.5 0.0 copy-done.8
  30.5 0.0 copy-done.10
  30.5 0.8 %prepare.1 = (f32[8,128,128]{2,1,0:T(8,128)S(1)}, f32[8,128,128]{2,1,0:T(8,128)S(1)}) custom-call(bf16[8,128,128]{2,1,0:T(8,128)(2,1)S(1)} %copy-done, bf16[8,128,128]{2,1,0:T(8,128)(2,1)S(1)} %copy-done.4, f32[1,128]{1,0:T(1,128)S(1)} %bitcast.6, f32[1,128]{1,0:T(1,128)S(1)} %bitcast.10, bf16[128,128]{1,0:T(8,128)(2,1)S(1)} %copy-done.5, ...), custom_call_target="tpu_custom_call" | custom-call | flops 67108864 | bytes 1639936 | tf_op jit(solution)/shard_map/prepare/pallas_call | solution.py:63
  31.3 0.8 %copy-done.2 = f32[8,128,128]{2,1,0:T(8,128)} copy-done((f32[8,128,128]{2,1,0:T(8,128)}, f32[8,128,128]{2,1,0:T(8,128)S(1)}, u32[]{:S(2)}) %copy-start.2) | copy-done | bytes 524312
  32.1 7.7 %all-to-all-done.1.refs_0_ = bf16[16,64,128]{2,1,0:T(8,128)(2,1)S(1)} async-done(((bf16[16,64,128]{2,1,0:T(8,128)(2,1)}), bf16[16,64,128]{2,1,0:T(8,128)(2,1)S(1)}, u32[]{:S(2)}, u32[]{:S(2)}) %all-to-all-start.1) | async-done | bytes 262176 | tf_op jit(solution)/shard_map/all_to_all | solution.py:246
  39.9 0.3 middle.1
  40.2 12.8 %all_to_all.21.refs_0_ = bf16[16,64,128]{2,1,0:T(8,128)(2,1)S(1)} all-to-all(bf16[16,64,128]{2,1,0:T(8,128)(2,1)S(1)} %middle.1), channel_id=1, replica_groups=mesh['grp'=2,'row'=16,'chan'=1] {'row'}, dimensions={0} | all-to-all | bytes 524288 | tf_op jit(solution)/shard_map/all_to_all | solution.py:246
  53.0 1.4 %products.1 = bf16[16,128,128]{2,1,0:T(8,128)(2,1)} custom-call(bf16[16,64,128]{2,1,0:T(8,128)(2,1)S(1)} %all_to_all.21.refs_0_, bf16[16,128,128]{2,1,0:T(8,128)(2,1)S(1)} %get-tuple-element.15.refs_1_), custom_call_target="tpu_custom_call" | custom-call | flops 67108864 | bytes 1310720 | tf_op jit(solution)/shard_map/products/pallas_call | solution.py:63
  54.4 3.7 %all-to-all-start.3 = ((bf16[16,128,128]{2,1,0:T(8,128)(2,1)}), bf16[16,128,128]{2,1,0:T(8,128)(2,1)S(1)}, u32[]{:S(2)}, u32[]{:S(2)}) async-start(bf16[16,128,128]{2,1,0:T(8,128)(2,1)} %products.1), calls=%async_computation.3 | async-start | bytes 1048576 | tf_op jit(solution)/shard_map/all_to_all | solution.py:246
  58.2 0.0 copy-start.11
  58.2 0.6 copy-done.9
  58.8 0.0 copy-done.11
  58.8 1.0 %copy-done.3 = f32[8,128,128]{2,1,0:T(8,128)S(1)} copy-done((f32[8,128,128]{2,1,0:T(8,128)S(1)}, f32[8,128,128]{2,1,0:T(8,128)}, u32[]{:S(2)}) %copy-start.3) | copy-done | bytes 524312
  59.9 1.7 %slopes.1 = (bf16[8,512,128]{2,1,0:T(8,128)(2,1)S(1)}, f32[8,128,128]{2,1,0:T(8,128)S(1)}, f32[8,128,128]{2,1,0:T(8,128)S(1)}, f32[8,128]{1,0:T(8,128)S(1)}) custom-call(bf16[16,64,128]{2,1,0:T(8,128)(2,1)S(1)} %all-to-all-done.1.refs_0_, f32[8,128,128]{2,1,0:T(8,128)S(1)} %copy-done.3, bf16[8,128,128]{2,1,0:T(8,128)(2,1)S(1)} %copy-done, ...), custom_call_target="tpu_custom_call" | custom-call | flops 201326592 | bytes 3348992 | tf_op jit(solution)/shard_map/slopes/pallas_call | solution.py:63
  61.6 11.0 %all-to-all-done.3.refs_0_ = bf16[16,128,128]{2,1,0:T(8,128)(2,1)S(1)} async-done(((bf16[16,128,128]{2,1,0:T(8,128)(2,1)}), bf16[16,128,128]{2,1,0:T(8,128)(2,1)S(1)}, u32[]{:S(2)}, u32[]{:S(2)}) %all-to-all-start.3) | async-done | bytes 524320 | tf_op jit(solution)/shard_map/all_to_all | solution.py:246
  72.6 1.5 %finish.1 = bf16[8,128,128]{2,1,0:T(8,128)(2,1)} custom-call(bf16[16,128,128]{2,1,0:T(8,128)(2,1)S(1)} %all-to-all-done.3.refs_0_, bf16[8,512,128]{2,1,0:T(8,128)(2,1)S(1)} %get-tuple-element.17.refs_1_, f32[8,128,128]{2,1,0:T(8,128)S(1)} %get-tuple-element.18.refs_2_, f32[8,128,128]{2,1,0:T(8,128)S(1)} %get-tuple-element.19.refs_3_, ...), custom_call_target="tpu_custom_call" | custom-call | flops 134217728 | bytes 3019264 | tf_op jit(solution)/shard_map/finish/pallas_call | solution.py:63
  (13 shorter events, 0.0 us)
Async XLA Ops:
  24.4 5.5 %copy-start.5 = (bf16[128,128]{1,0:T(8,128)(2,1)S(1)}, bf16[128,128]{1,0:T(8,128)(2,1)}, u32[]{:S(2)}) copy-start(bf16[128,128]{1,0:T(8,128)(2,1)} %refs_7_.1) | copy-start | bytes 98308
  24.4 5.5 %copy-start.6 = (bf16[128,128]{1,0:T(8,128)(2,1)S(1)}, bf16[128,128]{1,0:T(8,128)(2,1)}, u32[]{:S(2)}) copy-start(bf16[128,128]{1,0:T(8,128)(2,1)} %refs_10_.1) | copy-start | bytes 98308
  25.6 4.3 %copy-start = (bf16[8,128,128]{2,1,0:T(8,128)(2,1)S(1)}, bf16[8,128,128]{2,1,0:T(8,128)(2,1)}, u32[]{:S(2)}) copy-start(bf16[8,128,128]{2,1,0:T(8,128)(2,1)} %refs_2_.1) | copy-start | bytes 786436
  25.6 4.3 %copy-start.4 = (bf16[8,128,128]{2,1,0:T(8,128)(2,1)S(1)}, bf16[8,128,128]{2,1,0:T(8,128)(2,1)}, u32[]{:S(2)}) copy-start(bf16[8,128,128]{2,1,0:T(8,128)(2,1)} %refs_1_.1) | copy-start | bytes 786436
  25.6 14.3 %all-to-all-start.1 = ((bf16[16,64,128]{2,1,0:T(8,128)(2,1)}), bf16[16,64,128]{2,1,0:T(8,128)(2,1)S(1)}, u32[]{:S(2)}, u32[]{:S(2)}) async-start(bf16[16,64,128]{2,1,0:T(8,128)(2,1)} %get-tuple-element.13), calls=%async_computation.1 | async-start | bytes 524288 | tf_op jit(solution)/shard_map/all_to_all | solution.py:246
  29.8 0.7 copy-start.7
  29.8 0.7 copy-start.8
  29.8 0.7 copy-start.10
  31.3 0.8 %copy-start.2 = (f32[8,128,128]{2,1,0:T(8,128)}, f32[8,128,128]{2,1,0:T(8,128)S(1)}, u32[]{:S(2)}) copy-start(f32[8,128,128]{2,1,0:T(8,128)S(1)} %get-tuple-element.16.refs_1_) | copy-start | bytes 1572868
  54.4 3.7 %copy-start.1 = (bf16[128,512]{1,0:T(8,128)(2,1)S(1)}, bf16[128,512]{1,0:T(8,128)(2,1)}, u32[]{:S(2)}) copy-start(bf16[128,512]{1,0:T(8,128)(2,1)} %refs_6_.5) | copy-start | bytes 393220
  54.4 18.1 %all-to-all-start.3 = ((bf16[16,128,128]{2,1,0:T(8,128)(2,1)}), bf16[16,128,128]{2,1,0:T(8,128)(2,1)S(1)}, u32[]{:S(2)}, u32[]{:S(2)}) async-start(bf16[16,128,128]{2,1,0:T(8,128)(2,1)} %products.1), calls=%async_computation.3 | async-start | bytes 1048576 | tf_op jit(solution)/shard_map/all_to_all | solution.py:246
  58.1 0.7 copy-start.9
  58.2 0.7 copy-start.11
  58.8 1.0 %copy-start.3 = (f32[8,128,128]{2,1,0:T(8,128)S(1)}, f32[8,128,128]{2,1,0:T(8,128)}, u32[]{:S(2)}) copy-start(f32[8,128,128]{2,1,0:T(8,128)} %copy-done.2) | copy-start | bytes 1572868

commit v5 on v4

--- a/solution.py
+++ b/solution.py
@@ -87,11 +87,12 @@
     return [cells[row : row + 1] for row in range(rows)]
 
 
-def project_kernel(pair, mask, gain, bias, w_proj, panels):
+def project_kernel(pair, mask, gain, bias, w_proj, left_panel, right_panel):
     rows = pair.shape[0]
     hidden = w_proj.shape[1] // 4
-    count, _, width = panels.shape
-    block = hidden // count
+    count, depth, width = left_panel.shape
+    block = depth // rows
+    halves = right_panel.shape[0] // count
     w_flip = transposed(w_proj[...])
     gain_col, bias_col = column(gain[...]), column(bias[...])
     masks = cell_masks(mask, rows)
@@ -99,12 +100,13 @@
         normed, _ = norm_rows(jnp.transpose(pair[row].astype(F32)))
         zln = (normed * gain_col + bias_col).astype(BF16)
         proj = dot(w_flip, zln, 1, 0)
+        place = slice(row * block, (row + 1) * block)
         left = masks[row] * sigmoid(proj[:hidden]) * proj[hidden : 2 * hidden]
+        left_panel[:, place, :] = left.reshape(count, block, width).astype(BF16)
         right = masks[row] * sigmoid(proj[2 * hidden : 3 * hidden]) * proj[3 * hidden :]
-        both = jnp.concatenate(
-            [left.reshape(count, block, width), right.reshape(count, block, width)], axis=1
-        )
-        panels[:, row * 2 * block : (row + 1) * 2 * block, :] = both.astype(BF16)
+        right = right.reshape(count, block, width).astype(BF16)
+        for half in range(halves):
+            right_panel[half * count : (half + 1) * count, place, :] = right
 
 
 def prepare_kernel(
@@ -124,55 +126,54 @@
         gate_slope[row] = cot * gate * (1.0 - gate)
 
 
-def tri_kernel(panels, products, matrices, wide, narrow):
-    count, depth, width = panels.shape
-    block = matrices.shape[0] // 2
-    total = matrices.shape[1]
-    wide[...] = panels[...].astype(F32).reshape(count * depth, width)
+def spread(panel, wide):
+    wide[...] = panel[...].astype(F32).reshape(wide.shape)
+
+
+def tri_kernel(left_panel, right_panel, products, left_all, right_all, left_wide, right_wide):
+    block, left_rows, _ = left_all.shape
+    right_rows = right_all.shape[1]
+    spread(left_panel, left_wide)
+    spread(right_panel, right_wide)
     for h in range(block):
-        left = wide[pl.ds(h, total, stride=2 * block), :].astype(BF16)
-        right = wide[pl.ds(block + h, total, stride=2 * block), :].astype(BF16)
-        matrices[h] = left
-        matrices[block + h] = right
-        narrow[pl.ds(h, total, stride=block), :] = dot(left, right, 1, 1)
-    products[...] = narrow[...].astype(BF16).reshape(products.shape)
-
-
-def row_pair(ref, first, block):
-    count, _, width = ref.shape
-    both = ref[:, first * block : (first + 2) * block, :].astype(F32)
-    return [
-        both[:, n * block : (n + 1) * block, :].reshape(count * block, width) for n in range(2)
-    ]
+        left_all[h] = left_wide[pl.ds(h, left_rows, stride=block), :].astype(BF16)
+        right_all[h] = right_wide[pl.ds(h, right_rows, stride=block), :].astype(BF16)
+        left_wide[pl.ds(h, left_rows, stride=block), :] = dot(left_all[h], right_all[h], 1, 1)
+    products[...] = left_wide[...].astype(BF16).reshape(products.shape)
+
+
+def cell_row(ref, row, rows):
+    count, depth, width = ref.shape
+    block = depth // rows
+    return ref[:, row * block : (row + 1) * block, :].astype(F32).reshape(count * block, width)
 
 
 def middle_kernel(products, d_hat_centered, d_products):
-    rows, hidden, width = d_hat_centered.shape
-    count = products.shape[0]
-    block = hidden // count
-    for first in range(0, rows, 2):
-        parts = []
-        for n, tri in enumerate(row_pair(products, first, block)):
-            tri_hat, inv_std = norm_rows(tri)
-            d_hat = d_hat_centered[first + n]
-            cross = jnp.mean(d_hat * tri_hat, axis=0, keepdims=True)
-            d_tri = inv_std * (d_hat - tri_hat * cross)
-            parts.append(d_tri.reshape(count, block, width))
-        d_products[:, first * block : (first + 2) * block, :] = jnp.concatenate(
-            parts, axis=1
+    rows = d_hat_centered.shape[0]
+    count, depth, width = products.shape
+    block = depth // rows
+    for row in range(rows):
+        tri_hat, inv_std = norm_rows(cell_row(products, row, rows))
+        d_hat = d_hat_centered[row]
+        cross = jnp.mean(d_hat * tri_hat, axis=0, keepdims=True)
+        d_tri = inv_std * (d_hat - tri_hat * cross)
+        d_products[:, row * block : (row + 1) * block, :] = d_tri.reshape(
+            count, block, width
         ).astype(BF16)
 
 
-def products_kernel(d_products, matrices, d_panels, narrow, wide):
-    count, depth, width = d_products.shape
-    block = matrices.shape[0] // 2
-    total = matrices.shape[1]
-    narrow[...] = d_products[...].astype(F32).reshape(count * depth, width)
+def products_kernel(
+    d_products, left_all, right_all, d_left_panel, d_right_panel, left_wide, right_wide
+):
+    block, left_rows, _ = left_all.shape
+    right_rows = right_all.shape[1]
+    spread(d_products, left_wide)
     for h in range(block):
-        d_tri = narrow[pl.ds(h, total, stride=block), :].astype(BF16)
-        wide[pl.ds(h, total, stride=2 * block), :] = dot(d_tri, matrices[block + h], 1, 0)
-        wide[pl.ds(block + h, total, stride=2 * block), :] = dot(d_tri, matrices[h], 0, 0)
-    d_panels[...] = wide[...].astype(BF16).reshape(d_panels.shape)
+        d_tri = left_wide[pl.ds(h, left_rows, stride=block), :].astype(BF16)
+        left_wide[pl.ds(h, left_rows, stride=block), :] = dot(d_tri, right_all[h], 1, 0)
+        right_wide[pl.ds(h, right_rows, stride=block), :] = dot(d_tri, left_all[h], 0, 0)
+    d_left_panel[...] = left_wide[...].astype(BF16).reshape(d_left_panel.shape)
+    d_right_panel[...] = right_wide[...].astype(BF16).reshape(d_right_panel.shape)
 
 
 def slopes_kernel(
@@ -194,14 +195,13 @@
 ):
     rows = pair.shape[0]
     hidden = w_out.shape[0]
-    block = hidden // products.shape[0]
     w_flip = transposed(w_proj[...])
     out_flip = transposed(w_out[...])
     gain_col, bias_col = column(gain[...]), column(bias[...])
     out_gain_col, out_bias_col = column(out_gain[...]), column(out_bias[...])
     masks = cell_masks(mask, rows)
     for row in range(rows):
-        tri_hat, _ = norm_rows(row_pair(products, row - row % 2, block)[row % 2])
+        tri_hat, _ = norm_rows(cell_row(products, row, rows))
         scaled = (tri_hat * out_gain_col + out_bias_col).astype(BF16)
         d_gate_pre = (dot(out_flip, scaled, 1, 0) * gate_slope[row]).astype(BF16)
         d_zln_gate[row] = dot(w_gate[...], d_gate_pre, 1, 0)
@@ -219,17 +219,18 @@
             slopes[row, base + hidden : base + 2 * hidden, :] = masked.astype(slopes.dtype)
 
 
-def finish_kernel(d_panels, slopes, d_zln_gate, normed_in, inv_in, gain, w_proj, grad):
+def finish_kernel(
+    d_left_panel, d_right_panel, slopes, d_zln_gate, normed_in, inv_in, gain, w_proj, grad
+):
     rows = grad.shape[0]
-    count, depth, width = d_panels.shape
-    block = depth // rows // 2
-    hidden = count * block
+    count, depth, width = d_left_panel.shape
+    hidden = count * depth // rows
     gain_col = column(gain[...])
     for row in range(rows):
-        both = d_panels[:, row * 2 * block : (row + 1) * 2 * block, :].astype(F32)
+        d_right = cell_row(d_right_panel, row, rows)
+        d_right = sum(d_right[n : n + hidden] for n in range(0, d_right.shape[0], hidden))
         parts = []
-        for side in range(2):
-            d_value = both[:, side * block : (side + 1) * block, :].reshape(hidden, width)
+        for side, d_value in enumerate((cell_row(d_left_panel, row, rows), d_right)):
             for base in (2 * side * hidden, (2 * side + 1) * hidden):
                 slope = slopes[row, base : base + hidden, :].astype(F32)
                 parts.append((d_value * slope).astype(BF16))
@@ -242,8 +243,17 @@
         grad[row] = jnp.transpose(result).astype(BF16)
 
 
-def swap(values):
-    return lax.all_to_all(values, "row", split_axis=0, concat_axis=0, tiled=True)
+def swap(values, halves=1):
+    count = lax.axis_size("row") // halves
+    groups = [[half * count + n for n in range(count)] for half in range(halves)]
+    return lax.all_to_all(
+        values,
+        "row",
+        split_axis=0,
+        concat_axis=0,
+        tiled=True,
+        axis_index_groups=groups if halves > 1 else None,
+    )
 
 
 def kernel_shards(
@@ -260,24 +270,29 @@
 ):
     rows, width, channels = pair.shape
     hidden = w_out.shape[0]
-    count = lax.axis_size("row")
+    halves = 2
+    devices = lax.axis_size("row")
+    count = devices // halves
     block = hidden // count
-    total = rows * count
+    left_rows, right_rows = rows * count, rows * devices
     shape = jax.ShapeDtypeStruct
+    panel = shape((count, rows * block, width), BF16)
+    wide_panel = shape((devices, rows * block, width), BF16)
     mask = residue_mask.reshape(1, width)
     gain, bias = ln_in_gain.reshape(1, channels), ln_in_bias.reshape(1, channels)
     out_gain, out_bias = ln_out_gain.reshape(1, hidden), ln_out_bias.reshape(1, hidden)
     cells = rows * width
-    (panels,) = call(
+    left_panel, right_panel = call(
         project_kernel,
         "project",
-        [shape((count, rows * 2 * block, width), BF16)],
+        [panel, wide_panel],
         [pair, mask, gain, bias, w_proj],
         fetched=range(5),
         flops=2 * cells * channels * 4 * hidden,
-        limit=64 * 1024 * 1024 - 640 * 1024,
-    )
-    panels = swap(panels)
+        limit=64 * 1024 * 1024 - 896 * 1024,
+    )
+    right_panel = swap(right_panel)
+    left_panel = swap(left_panel, halves)
     d_hat_centered, gate_slope = call(
         prepare_kernel,
         "prepare",
@@ -286,34 +301,35 @@
         fetched=range(7),
         flops=2 * cells * channels * 2 * hidden,
     )
-    wide = pltpu.VMEM((total * 2 * block, width), F32)
-    narrow = pltpu.VMEM((total * block, width), F32)
-    products, matrices = call(
+    left_wide = pltpu.VMEM((left_rows * block, width), F32)
+    right_wide = pltpu.VMEM((right_rows * block, width), F32)
+    products, left_all, right_all = call(
         tri_kernel,
         "tri",
-        [shape((count, rows * block, width), BF16), shape((2 * block, total, width), BF16)],
-        [panels],
-        scratch=[wide, narrow],
-        flops=2 * block * total * width * total,
-    )
-    products = swap(products)
+        [panel, shape((block, left_rows, width), BF16), shape((block, right_rows, width), BF16)],
+        [left_panel, right_panel],
+        scratch=[left_wide, right_wide],
+        flops=2 * block * left_rows * width * right_rows,
+    )
+    products = swap(products, halves)
     (d_products,) = call(
         middle_kernel,
         "middle",
-        [shape((count, rows * block, width), BF16)],
+        [panel],
         [products, d_hat_centered],
         flops=20 * cells * hidden,
     )
-    d_products = swap(d_products)
-    (d_panels,) = call(
+    d_products = swap(d_products, halves)
+    d_left_panel, d_right_panel = call(
         products_kernel,
         "products",
-        [shape((count, rows * 2 * block, width), BF16)],
-        [d_products, matrices],
-        scratch=[narrow, wide],
-        flops=4 * block * total * width * total,
-    )
-    d_panels = swap(d_panels)
+        [panel, wide_panel],
+        [d_products, left_all, right_all],
+        scratch=[left_wide, right_wide],
+        flops=4 * block * left_rows * width * right_rows,
+    )
+    d_right_panel = swap(d_right_panel)
+    d_left_panel = swap(d_left_panel, halves)
     slopes, d_zln_gate, normed_in, inv_in = call(
         slopes_kernel,
         "slopes",
@@ -343,8 +359,8 @@
         finish_kernel,
         "finish",
         [shape(pair.shape, BF16)],
-        [d_panels, slopes, d_zln_gate, normed_in, inv_in, gain, w_proj],
-        fetched=(5, 6),
+        [d_left_panel, d_right_panel, slopes, d_zln_gate, normed_in, inv_in, gain, w_proj],
+        fetched=(6, 7),
         flops=2 * cells * channels * 4 * hidden,
     )
     return grad
@@ -459,7 +475,7 @@
 
 
 def solution(mesh):
-    fits = mesh.shape["chan"] == 1 and mesh.shape["row"] <= 16
+    fits = mesh.shape["chan"] == 1 and mesh.shape["row"] in (8, 16)
     return jax.shard_map(
         kernel_shards if fits else shards,
         mesh=mesh,

time: 74.6 us -> 86.2 us (1.16)
  blocking collectives: 34.7 us -> 47.8 us
  waiting for transfers between devices: 18.7 us -> 14.2 us
  local copies, waits for them, and re-layouts: 3.13 us -> 4.64 us
    all_to_all x2 -> x4, blocking collectives: 34.7 us -> 47.8 us  [swap(): lax.all_to_all(values, 'row', split_axis=0, concat_axis=0, tiled=True, ax...]
    all_to_all x2, waiting for transfers between devices: 18.7 us -> 14.2 us  [swap(): lax.all_to_all(values, 'row', split_axis=0, concat_axis=0, tiled=True, ax...]
    unnamed x24 -> x30, local copies, waits for them, and re-layouts: 3.13 us -> 4.64 us
where the time goes in v5:
time: 86.2 us; the launch traced here: 85.4 us
  blocking collectives  47.8 us (55%)
  waiting for transfers between devices  14.2 us (16%)
  Pallas kernels  10.3 us (12%)
  starting transfers between devices  8.25 us (10%)
  local copies, waits for them, and re-layouts  4.64 us (5%)
    all_to_all x4, blocking collectives, swap(): lax.all_to_all(values, 'row', split_axis=0, concat_axis=0, tiled=True, ax...  47.8 us
    all_to_all x2, waiting for transfers between devices, swap(): lax.all_to_all(values, 'row', split_axis=0, concat_axis=0, tiled=True, ax...  14.2 us
    pallas_call x7, Pallas kernels, call(): pl.pallas_call(body, name=name, out_shape=outs, in_specs=[pl.BlockSpec(me...  10.3 us
    all_to_all x2, starting transfers between devices, swap(): lax.all_to_all(values, 'row', split_axis=0, concat_axis=0, tiled=True, ax...  8.25 us
    unnamed x30, local copies, waits for them, and re-layouts  4.64 us
  transfers between devices with their start and end apart: 2, of which 2 were waited for; matrix products, arithmetic and copies ran while one was open for 0% of the time, Pallas kernels for 3%

profile of v5, /device:TPU:0, one launch (start us, length us, event | category | flops | bytes accessed | tf_op | source)
XLA Modules:
  0.0 85.4 jit_solution(13930477910359485685)
XLA Ops:
  0.0 2.6 %project.1 = (bf16[8,128,128]{2,1,0:T(8,128)(2,1)}, bf16[16,128,128]{2,1,0:T(8,128)(2,1)}) custom-call(bf16[8,128,128]{2,1,0:T(8,128)(2,1)} %refs_2_.1, s32[1,128]{1,0:T(1,128)} %bitcast.14, f32[1,128]{1,0:T(1,128)} %bitcast.5, f32[1,128]{1,0:T(1,128)} %bitcast.9, bf16[128,512]{1,0:T(8,128)(2,1)} %refs_7_.3), custom_call_target="tpu_custom_call" | custom-call | flops 134217728 | bytes 1181184 | tf_op jit(solution)/shard_map/project/pallas_call | solution.py:63
  2.6 11.4 %all_to_all.30.refs_0_ = bf16[8,128,128]{2,1,0:T(8,128)(2,1)S(1)} all-to-all(bf16[8,128,128]{2,1,0:T(8,128)(2,1)} %get-tuple-element.18), channel_id=1, replica_groups={{0,1,2,3,4,5,6,7},{8,9,10,11,12,13,14,15},{16,17,18,19,20,21,22,23},{24..., dimensions={0} | all-to-all | bytes 524288 | tf_op jit(solution)/shard_map/all_to_all | solution.py:249
  14.0 19.2 %all_to_all.31.refs_1_ = bf16[16,128,128]{2,1,0:T(8,128)(2,1)S(1)} all-to-all(bf16[16,128,128]{2,1,0:T(8,128)(2,1)S(1)} %copy-done.14), channel_id=1, replica_groups=mesh['grp'=2,'row'=16,'chan'=1] {'row'}, dimensions={0} | all-to-all | bytes 1048576 | tf_op jit(solution)/shard_map/all_to_all | solution.py:249
  33.2 1.7 %tri.1 = (bf16[8,128,128]{2,1,0:T(8,128)(2,1)}, bf16[16,64,128]{2,1,0:T(8,128)(2,1)S(1)}, bf16[16,128,128]{2,1,0:T(8,128)(2,1)S(1)}) custom-call(bf16[8,128,128]{2,1,0:T(8,128)(2,1)S(1)} %all_to_all.30.refs_0_, bf16[16,128,128]{2,1,0:T(8,128)(2,1)S(1)} %all_to_all.31.refs_1_), custom_call_target="tpu_custom_call" | custom-call | flops 33554432 | bytes 1835008 | tf_op jit(solution)/shard_map/tri/pallas_call | solution.py:63
  34.8 3.5 %all-to-all-start.2 = ((bf16[8,128,128]{2,1,0:T(8,128)(2,1)}), bf16[8,128,128]{2,1,0:T(8,128)(2,1)S(1)}, u32[]{:S(2)}, u32[]{:S(2)}) async-start(bf16[8,128,128]{2,1,0:T(8,128)(2,1)} %get-tuple-element.20), calls=%async_computation.2 | async-start | bytes 524288 | tf_op jit(solution)/shard_map/all_to_all | solution.py:249
  38.5 0.6 copy-done.9
  39.1 0.0 copy-done.10
  39.1 0.0 copy-done.11
  39.1 0.8 prepare.1
  39.9 4.5 %all-to-all-done.2.refs_0_ = bf16[8,128,128]{2,1,0:T(8,128)(2,1)S(1)} async-done(((bf16[8,128,128]{2,1,0:T(8,128)(2,1)}), bf16[8,128,128]{2,1,0:T(8,128)(2,1)S(1)}, u32[]{:S(2)}, u32[]{:S(2)}) %all-to-all-start.2) | async-done | bytes 262176 | tf_op jit(solution)/shard_map/all_to_all | solution.py:249
  44.4 0.3 middle.1
  44.7 8.6 %all_to_all.32.refs_0_ = bf16[8,128,128]{2,1,0:T(8,128)(2,1)S(1)} all-to-all(bf16[8,128,128]{2,1,0:T(8,128)(2,1)S(1)} %middle.1), channel_id=1, replica_groups={{0,1,2,3,4,5,6,7},{8,9,10,11,12,13,14,15},{16,17,18,19,20,21,22,23},{24..., dimensions={0} | all-to-all | bytes 524288 | tf_op jit(solution)/shard_map/all_to_all | solution.py:249
  53.3 1.8 %products.1 = (bf16[8,128,128]{2,1,0:T(8,128)(2,1)S(1)}, bf16[16,128,128]{2,1,0:T(8,128)(2,1)}) custom-call(bf16[8,128,128]{2,1,0:T(8,128)(2,1)S(1)} %all_to_all.32.refs_0_, bf16[16,64,128]{2,1,0:T(8,128)(2,1)S(1)} %get-tuple-element.22.refs_1_, bf16[16,128,128]{2,1,0:T(8,128)(2,1)S(1)} %get-tuple-element.23.refs_2_), custom_call_target="tpu_custom_call" | custom-call | flops 67108864 | bytes 1835008 | tf_op jit(solution)/shard_map/products/pallas_call | solution.py:63
  55.0 8.6 %all_to_all.33.refs_0_ = bf16[8,128,128]{2,1,0:T(8,128)(2,1)S(1)} all-to-all(bf16[8,128,128]{2,1,0:T(8,128)(2,1)S(1)} %get-tuple-element.24), channel_id=1, replica_groups={{0,1,2,3,4,5,6,7},{8,9,10,11,12,13,14,15},{16,17,18,19,20,21,22,23},{24..., dimensions={0} | all-to-all | bytes 524288 | tf_op jit(solution)/shard_map/all_to_all | solution.py:249
  63.6 4.7 %all-to-all-start.5 = ((bf16[16,128,128]{2,1,0:T(8,128)(2,1)}), bf16[16,128,128]{2,1,0:T(8,128)(2,1)S(1)}, u32[]{:S(2)}, u32[]{:S(2)}) async-start(bf16[16,128,128]{2,1,0:T(8,128)(2,1)} %get-tuple-element.25), calls=%async_computation.5 | async-start | bytes 1048576 | tf_op jit(solution)/shard_map/all_to_all | solution.py:249
  68.4 0.6 copy-done.12
  69.0 0.0 copy-done.13
  69.0 0.8 copy-done.6
  69.8 0.8 copy-done.8
  70.6 1.7 %slopes.1 = (bf16[8,512,128]{2,1,0:T(8,128)(2,1)S(1)}, f32[8,128,128]{2,1,0:T(8,128)S(1)}, f32[8,128,128]{2,1,0:T(8,128)S(1)}, f32[8,128]{1,0:T(8,128)S(1)}) custom-call(bf16[8,128,128]{2,1,0:T(8,128)(2,1)S(1)} %all-to-all-done.2.refs_0_, f32[8,128,128]{2,1,0:T(8,128)S(1)} %get-tuple-element.26.refs_1_, bf16[8,128,128]{2,1,0:T(8,128)(2,1)S(1)} %copy-done, ...), custom_call_target="tpu_custom_call" | custom-call | flops 201326592 | bytes 3348992 | tf_op jit(solution)/shard_map/slopes/pallas_call | solution.py:63
  72.3 0.8 copy-done.2
  73.0 9.8 %all-to-all-done.5.refs_1_ = bf16[16,128,128]{2,1,0:T(8,128)(2,1)S(1)} async-done(((bf16[16,128,128]{2,1,0:T(8,128)(2,1)}), bf16[16,128,128]{2,1,0:T(8,128)(2,1)S(1)}, u32[]{:S(2)}, u32[]{:S(2)}) %all-to-all-start.5) | async-done | bytes 524320 | tf_op jit(solution)/shard_map/all_to_all | solution.py:249
  82.8 1.0 %copy-done.3 = f32[8,128,128]{2,1,0:T(8,128)S(1)} copy-done((f32[8,128,128]{2,1,0:T(8,128)S(1)}, f32[8,128,128]{2,1,0:T(8,128)}, u32[]{:S(2)}) %copy-start.3) | copy-done | bytes 524312
  83.9 1.5 %finish.1 = bf16[8,128,128]{2,1,0:T(8,128)(2,1)} custom-call(bf16[8,128,128]{2,1,0:T(8,128)(2,1)S(1)} %all_to_all.33.refs_0_, bf16[16,128,128]{2,1,0:T(8,128)(2,1)S(1)} %all-to-all-done.5.refs_1_, bf16[8,512,128]{2,1,0:T(8,128)(2,1)S(1)} %get-tuple-element.27.refs_2_, f32[8,128,128]{2,1,0:T(8,128)S(1)} %get-tuple-element.28.refs_3_, ...), custom_call_target="tpu_custom_call" | custom-call | flops 134217728 | bytes 3281408 | tf_op jit(solution)/shard_map/finish/pallas_call | solution.py:63
  (21 shorter events, 0.1 us)
Async XLA Ops:
  2.6 11.4 %copy-start.14 = (bf16[16,128,128]{2,1,0:T(8,128)(2,1)S(1)}, bf16[16,128,128]{2,1,0:T(8,128)(2,1)}, u32[]{:S(2)}) copy-start(bf16[16,128,128]{2,1,0:T(8,128)(2,1)} %get-tuple-element.19) | copy-start | bytes 1572868
  33.2 5.3 %copy-start.5 = (bf16[128,128]{1,0:T(8,128)(2,1)S(1)}, bf16[128,128]{1,0:T(8,128)(2,1)}, u32[]{:S(2)}) copy-start(bf16[128,128]{1,0:T(8,128)(2,1)} %refs_7_.2) | copy-start | bytes 98308
  33.2 5.3 %copy-start.7 = (bf16[128,128]{1,0:T(8,128)(2,1)S(1)}, bf16[128,128]{1,0:T(8,128)(2,1)}, u32[]{:S(2)}) copy-start(bf16[128,128]{1,0:T(8,128)(2,1)} %refs_10_.1) | copy-start | bytes 98308
  34.8 3.6 %copy-start = (bf16[8,128,128]{2,1,0:T(8,128)(2,1)S(1)}, bf16[8,128,128]{2,1,0:T(8,128)(2,1)}, u32[]{:S(2)}) copy-start(bf16[8,128,128]{2,1,0:T(8,128)(2,1)} %refs_2_.1) | copy-start | bytes 786436
  34.8 3.6 %copy-start.4 = (bf16[8,128,128]{2,1,0:T(8,128)(2,1)S(1)}, bf16[8,128,128]{2,1,0:T(8,128)(2,1)}, u32[]{:S(2)}) copy-start(bf16[8,128,128]{2,1,0:T(8,128)(2,1)} %refs_1_.1) | copy-start | bytes 786436
  34.8 9.5 %all-to-all-start.2 = ((bf16[8,128,128]{2,1,0:T(8,128)(2,1)}), bf16[8,128,128]{2,1,0:T(8,128)(2,1)S(1)}, u32[]{:S(2)}, u32[]{:S(2)}) async-start(bf16[8,128,128]{2,1,0:T(8,128)(2,1)} %get-tuple-element.20), calls=%async_computation.2 | async-start | bytes 524288 | tf_op jit(solution)/shard_map/all_to_all | solution.py:249
  38.4 0.7 copy-start.9
  38.4 0.7 copy-start.10
  38.4 0.7 copy-start.11
  63.6 4.7 %copy-start.1 = (bf16[128,512]{1,0:T(8,128)(2,1)S(1)}, bf16[128,512]{1,0:T(8,128)(2,1)}, u32[]{:S(2)}) copy-start(bf16[128,512]{1,0:T(8,128)(2,1)} %refs_7_.3) | copy-start | bytes 393220
  63.6 19.2 %all-to-all-start.5 = ((bf16[16,128,128]{2,1,0:T(8,128)(2,1)}), bf16[16,128,128]{2,1,0:T(8,128)(2,1)S(1)}, u32[]{:S(2)}, u32[]{:S(2)}) async-start(bf16[16,128,128]{2,1,0:T(8,128)(2,1)} %get-tuple-element.25), calls=%async_computation.5 | async-start | bytes 1048576 | tf_op jit(solution)/shard_map/all_to_all | solution.py:249
  68.4 0.7 copy-start.12
  68.4 0.7 copy-start.13
  69.0 0.8 copy-start.6
  69.8 0.8 copy-start.8
  72.3 0.8 copy-start.2
  82.8 1.0 %copy-start.3 = (f32[8,128,128]{2,1,0:T(8,128)S(1)}, f32[8,128,128]{2,1,0:T(8,128)}, u32[]{:S(2)}) copy-start(f32[8,128,128]{2,1,0:T(8,128)} %copy-done.2) | copy-start | bytes 1572868

commit v6 on v5

--- a/solution.py
+++ b/solution.py
@@ -87,7 +87,12 @@
     return [cells[row : row + 1] for row in range(rows)]
 
 
-def project_kernel(pair, mask, gain, bias, w_proj, left_panel, right_panel):
+def partner(step, count):
+    return lax.rem(lax.axis_index("row"), count) ^ step
+
+
+def project_kernel(pair, mask, gain, bias, w_proj, right_panel, *refs):
+    *pieces, left_panel = refs
     rows = pair.shape[0]
     hidden = w_proj.shape[1] // 4
     count, depth, width = left_panel.shape
@@ -107,6 +112,8 @@
         right = right.reshape(count, block, width).astype(BF16)
         for half in range(halves):
             right_panel[half * count : (half + 1) * count, place, :] = right
+    for step, piece in enumerate(pieces):
+        piece[...] = left_panel[partner(step, count)]
 
 
 def prepare_kernel(
@@ -130,10 +137,14 @@
     wide[...] = panel[...].astype(F32).reshape(wide.shape)
 
 
-def tri_kernel(left_panel, right_panel, products, left_all, right_all, left_wide, right_wide):
+def tri_kernel(right_panel, *refs):
+    *pieces, products, left_all, right_all, left_wide, right_wide = refs
     block, left_rows, _ = left_all.shape
     right_rows = right_all.shape[1]
-    spread(left_panel, left_wide)
+    depth = pieces[0].shape[0]
+    for step, piece in enumerate(pieces):
+        start = pl.multiple_of(partner(step, len(pieces)) * depth, depth)
+        left_wide[pl.ds(start, depth), :] = piece[...].astype(F32)
     spread(right_panel, right_wide)
     for h in range(block):
         left_all[h] = left_wide[pl.ds(h, left_rows, stride=block), :].astype(BF16)
@@ -162,9 +173,8 @@
         ).astype(BF16)
 
 
-def products_kernel(
-    d_products, left_all, right_all, d_left_panel, d_right_panel, left_wide, right_wide
-):
+def products_kernel(d_products, left_all, right_all, d_right_panel, *refs):
+    *pieces, left_wide, right_wide = refs
     block, left_rows, _ = left_all.shape
     right_rows = right_all.shape[1]
     spread(d_products, left_wide)
@@ -172,7 +182,10 @@
         d_tri = left_wide[pl.ds(h, left_rows, stride=block), :].astype(BF16)
         left_wide[pl.ds(h, left_rows, stride=block), :] = dot(d_tri, right_all[h], 1, 0)
         right_wide[pl.ds(h, right_rows, stride=block), :] = dot(d_tri, left_all[h], 0, 0)
-    d_left_panel[...] = left_wide[...].astype(BF16).reshape(d_left_panel.shape)
+    depth = pieces[0].shape[0]
+    for step, piece in enumerate(pieces):
+        start = pl.multiple_of(partner(step, len(pieces)) * depth, depth)
+        piece[...] = left_wide[pl.ds(start, depth), :].astype(BF16)
     d_right_panel[...] = right_wide[...].astype(BF16).reshape(d_right_panel.shape)
 
 
@@ -219,9 +232,10 @@
             slopes[row, base + hidden : base + 2 * hidden, :] = masked.astype(slopes.dtype)
 
 
-def finish_kernel(
-    d_left_panel, d_right_panel, slopes, d_zln_gate, normed_in, inv_in, gain, w_proj, grad
-):
+def finish_kernel(d_right_panel, slopes, d_zln_gate, normed_in, inv_in, gain, w_proj, *refs):
+    *pieces, grad, d_left_panel = refs
+    for step, piece in enumerate(pieces):
+        d_left_panel[partner(step, len(pieces))] = piece[...]
     rows = grad.shape[0]
     count, depth, width = d_left_panel.shape
     hidden = count * depth // rows
@@ -243,17 +257,24 @@
         grad[row] = jnp.transpose(result).astype(BF16)
 
 
-def swap(values, halves=1):
-    count = lax.axis_size("row") // halves
-    groups = [[half * count + n for n in range(count)] for half in range(halves)]
+def swap(values):
+    return lax.all_to_all(values, "row", split_axis=0, concat_axis=0, tiled=True)
+
+
+def swap_half(values, count):
+    devices = range(lax.axis_size("row"))
+    groups = [[d for d in devices if d // count == half] for half in range(len(devices) // count)]
     return lax.all_to_all(
-        values,
-        "row",
-        split_axis=0,
-        concat_axis=0,
-        tiled=True,
-        axis_index_groups=groups if halves > 1 else None,
-    )
+        values, "row", split_axis=0, concat_axis=0, tiled=True, axis_index_groups=groups
+    )
+
+
+def swap_pieces(pieces):
+    devices = range(lax.axis_size("row"))
+    return [pieces[0]] + [
+        lax.ppermute(pieces[step], "row", [(d, d ^ step) for d in devices])
+        for step in range(1, len(pieces))
+    ]
 
 
 def kernel_shards(
@@ -282,17 +303,20 @@
     gain, bias = ln_in_gain.reshape(1, channels), ln_in_bias.reshape(1, channels)
     out_gain, out_bias = ln_out_gain.reshape(1, hidden), ln_out_bias.reshape(1, hidden)
     cells = rows * width
-    left_panel, right_panel = call(
+    piece = shape((rows * block, width), BF16)
+    left_panel = pltpu.VMEM(panel.shape, BF16)
+    right_panel, *pieces = call(
         project_kernel,
         "project",
-        [panel, wide_panel],
+        [wide_panel] + [piece] * count,
         [pair, mask, gain, bias, w_proj],
         fetched=range(5),
+        scratch=[left_panel],
         flops=2 * cells * channels * 4 * hidden,
         limit=64 * 1024 * 1024 - 896 * 1024,
     )
     right_panel = swap(right_panel)
-    left_panel = swap(left_panel, halves)
+    pieces = swap_pieces(pieces)
     d_hat_centered, gate_slope = call(
         prepare_kernel,
         "prepare",
@@ -307,11 +331,11 @@
         tri_kernel,
         "tri",
         [panel, shape((block, left_rows, width), BF16), shape((block, right_rows, width), BF16)],
-        [left_panel, right_panel],
+        [right_panel, *pieces],
         scratch=[left_wide, right_wide],
         flops=2 * block * left_rows * width * right_rows,
     )
-    products = swap(products, halves)
+    products = swap_half(products, count)
     (d_products,) = call(
         middle_kernel,
         "middle",
@@ -319,17 +343,17 @@
         [products, d_hat_centered],
         flops=20 * cells * hidden,
     )
-    d_products = swap(d_products, halves)
-    d_left_panel, d_right_panel = call(
+    d_products = swap_half(d_products, count)
+    d_right_panel, *d_pieces = call(
         products_kernel,
         "products",
-        [panel, wide_panel],
+        [wide_panel] + [piece] * count,
         [d_products, left_all, right_all],
         scratch=[left_wide, right_wide],
         flops=4 * block * left_rows * width * right_rows,
     )
     d_right_panel = swap(d_right_panel)
-    d_left_panel = swap(d_left_panel, halves)
+    d_pieces = swap_pieces(d_pieces)
     slopes, d_zln_gate, normed_in, inv_in = call(
         slopes_kernel,
         "slopes",
@@ -359,8 +383,9 @@
         finish_kernel,
         "finish",
         [shape(pair.shape, BF16)],
-        [d_left_panel, d_right_panel, slopes, d_zln_gate, normed_in, inv_in, gain, w_proj],
-        fetched=(6, 7),
+        [d_right_panel, slopes, d_zln_gate, normed_in, inv_in, gain, w_proj, *d_pieces],
+        fetched=(5, 6),
+        scratch=[left_panel],
         flops=2 * cells * channels * 4 * hidden,
     )
     return grad

time: 86.2 us -> 72.6 us (0.84)
  blocking collectives: 47.8 us -> 8.62 us
  starting transfers between devices: 8.25 us -> 29.2 us
  waiting for transfers between devices: 14.2 us -> 17.3 us
  local copies, waits for them, and re-layouts: 4.64 us -> 5.94 us
    all_to_all x4 -> x1, blocking collectives: 47.8 us -> 8.62 us  [swap_half(): lax.all_to_all(values, 'row', split_axis=0, concat_axis=0, tiled=True, ax...]
    ppermute x0 -> x14, starting transfers between devices: none -> 13 us  [swap_pieces(): lax.ppermute(pieces[step], 'row', [(d, d ^ step) for d in devices])]
    ppermute x0 -> x14, waiting for transfers between devices: none -> 12.3 us  [swap_pieces(): lax.ppermute(pieces[step], 'row', [(d, d ^ step) for d in devices])]
    all_to_all x2 -> x3, waiting for transfers between devices: 14.2 us -> 5.01 us  [the longest x1 4.46 us: swap_half(): lax.all_to_all(values, 'row', split_axis=0, concat_axis=0, tiled=True, ax...]
    all_to_all x2 -> x3, starting transfers between devices: 8.25 us -> 16.2 us  [the longest x2 12.7 us: swap(): lax.all_to_all(values, 'row', split_axis=0, concat_axis=0, tiled=True)]
    unnamed x30 -> x48, local copies, waits for them, and re-layouts: 4.64 us -> 5.94 us
  transfers between devices with their start and end apart: 2 -> 17, of which waited for: 2 -> 8; matrix products, arithmetic and copies ran while one was open for 0% -> 0% of each run, Pallas kernels for 3% -> 4%
where the time goes in v6:
time: 72.6 us; the launch traced here: 71.9 us
  starting transfers between devices  29.2 us (40%)
  waiting for transfers between devices  17.3 us (24%)
  Pallas kernels  10.5 us (14%)
  blocking collectives  8.62 us (12%)
  local copies, waits for them, and re-layouts  5.94 us (8%)
    ppermute x14, starting transfers between devices, swap_pieces(): lax.ppermute(pieces[step], 'row', [(d, d ^ step) for d in devices])  13 us
    all_to_all x2, starting transfers between devices, swap(): lax.all_to_all(values, 'row', split_axis=0, concat_axis=0, tiled=True)  12.7 us
    ppermute x14, waiting for transfers between devices, swap_pieces(): lax.ppermute(pieces[step], 'row', [(d, d ^ step) for d in devices])  12.3 us
    pallas_call x7, Pallas kernels, call(): pl.pallas_call(body, name=name, out_shape=outs, in_specs=[pl.BlockSpec(me...  10.5 us
    all_to_all x1, blocking collectives, swap_half(): lax.all_to_all(values, 'row', split_axis=0, concat_axis=0, tiled=True, ax...  8.62 us
    unnamed x48, local copies, waits for them, and re-layouts  5.94 us
    all_to_all x1, waiting for transfers between devices, swap_half(): lax.all_to_all(values, 'row', split_axis=0, concat_axis=0, tiled=True, ax...  4.46 us
    all_to_all x1, starting transfers between devices, swap_half(): lax.all_to_all(values, 'row', split_axis=0, concat_axis=0, tiled=True, ax...  3.54 us
  transfers between devices with their start and end apart: 17, of which 8 were waited for; matrix products, arithmetic and copies ran while one was open for 0% of the time, Pallas kernels for 4%

profile of v6, /device:TPU:0, one launch (start us, length us, event | category | flops | bytes accessed | tf_op | source)
XLA Modules:
  0.0 71.9 jit_solution(15721452376078003242)
XLA Ops:
  0.0 2.6 %project.1 = (bf16[16,128,128]{2,1,0:T(8,128)(2,1)}, bf16[128,128]{1,0:T(8,128)(2,1)}, bf16[128,128]{1,0:T(8,128)(2,1)}, bf16[128,128]{1,0:T(8,128)(2,1)}, bf16[...) custom-call(bf16[8,128,128]{2,1,0:T(8,128)(2,1)} %refs_2_.1, ...), custom_call_target="tpu_custom_call" | custom-call | flops 134217728 | bytes 1181184 | tf_op jit(solution)/shard_map/project/pallas_call | solution.py:63
  2.7 7.5 %all-to-all-start = ((bf16[16,128,128]{2,1,0:T(8,128)(2,1)}), bf16[16,128,128]{2,1,0:T(8,128)(2,1)S(1)}, u32[]{:S(2)}, u32[]{:S(2)}) async-start(bf16[16,128,128]{2,1,0:T(8,128)(2,1)} %get-tuple-element.32), calls=%async_computation | async-start | bytes 1048576 | tf_op jit(solution)/shard_map/all_to_all | solution.py:261
  10.7 1.7 %collective-permute-start.1 = (bf16[128,128]{1,0:T(8,128)(2,1)S(1)}, bf16[128,128]{1,0:T(8,128)(2,1)S(1)}, u32[]{:S(2)}, u32[]{:S(2)}) collective-permute-start(bf16[128,128]{1,0:T(8,128)(2,1)S(1)} %copy-done.22), channel_id=1, source_target_pairs={{0,2},{1,3},{2,0},{3,1},{4,6},{5,7},{6,4},{7,5},{8,10},{9,11},{10,... | collective-permute-start | bytes 98312 | tf_op jit(solution)/shard_map/ppermute | solution.py:275
  12.4 1.7 %collective-permute-start.3 = (bf16[128,128]{1,0:T(8,128)(2,1)S(1)}, bf16[128,128]{1,0:T(8,128)(2,1)S(1)}, u32[]{:S(2)}, u32[]{:S(2)}) collective-permute-start(bf16[128,128]{1,0:T(8,128)(2,1)S(1)} %copy-done.20), channel_id=1, source_target_pairs={{0,4},{1,5},{2,6},{3,7},{4,0},{5,1},{6,2},{7,3},{8,12},{9,13},{10,... | collective-permute-start | bytes 98312 | tf_op jit(solution)/shard_map/ppermute | solution.py:275
  14.2 2.6 %collective-permute-start.5 = (bf16[128,128]{1,0:T(8,128)(2,1)S(1)}, bf16[128,128]{1,0:T(8,128)(2,1)S(1)}, u32[]{:S(2)}, u32[]{:S(2)}) collective-permute-start(bf16[128,128]{1,0:T(8,128)(2,1)S(1)} %copy-done.18), channel_id=1, source_target_pairs={{0,6},{1,7},{2,4},{3,5},{4,2},{5,3},{6,0},{7,1},{8,14},{9,15},{10,... | collective-permute-start | bytes 98312 | tf_op jit(solution)/shard_map/ppermute | solution.py:275
  17.4 4.2 %collective-permute-done.3.refs_5_ = bf16[128,128]{1,0:T(8,128)(2,1)S(1)} collective-permute-done((bf16[128,128]{1,0:T(8,128)(2,1)S(1)}, bf16[128,128]{1,0:T(8,128)(2,1)S(1)}, u32[]{:S(2)}, u32[]{:S(2)}) %collective-permute-start.3) | collective-permute-done | bytes 32800 | tf_op jit(solution)/shard_map/ppermute | solution.py:275
  21.6 2.9 %collective-permute-done.5.refs_7_ = bf16[128,128]{1,0:T(8,128)(2,1)S(1)} collective-permute-done((bf16[128,128]{1,0:T(8,128)(2,1)S(1)}, bf16[128,128]{1,0:T(8,128)(2,1)S(1)}, u32[]{:S(2)}, u32[]{:S(2)}) %collective-permute-start.5) | collective-permute-done | bytes 32800 | tf_op jit(solution)/shard_map/ppermute | solution.py:275
  25.0 1.7 %tri.1 = (bf16[8,128,128]{2,1,0:T(8,128)(2,1)}, bf16[16,64,128]{2,1,0:T(8,128)(2,1)S(1)}, bf16[16,128,128]{2,1,0:T(8,128)(2,1)S(1)}) custom-call(bf16[16,128,128]{2,1,0:T(8,128)(2,1)S(1)} %all-to-all-done.refs_0_, bf16[128,128]{1,0:T(8,128)(2,1)S(1)} %copy-done.11, bf16[128,128]{1,0:T(8,128)(2,1)S(1)} %collective-permute-done.refs_2_, ...), custom_call_target="tpu_custom_call" | custom-call | flops 33554432 | bytes 1835008 | tf_op jit(solution)/shard_map/tri/pallas_call | solution.py:63
  26.7 3.5 %all-to-all-start.1 = ((bf16[8,128,128]{2,1,0:T(8,128)(2,1)}), bf16[8,128,128]{2,1,0:T(8,128)(2,1)S(1)}, u32[]{:S(2)}, u32[]{:S(2)}) async-start(bf16[8,128,128]{2,1,0:T(8,128)(2,1)} %get-tuple-element.41), calls=%async_computation.1 | async-start | bytes 524288 | tf_op jit(solution)/shard_map/all_to_all | solution.py:267
  31.0 0.8 %prepare.1 = (f32[8,128,128]{2,1,0:T(8,128)S(1)}, f32[8,128,128]{2,1,0:T(8,128)S(1)}) custom-call(bf16[8,128,128]{2,1,0:T(8,128)(2,1)S(1)} %copy-done, bf16[8,128,128]{2,1,0:T(8,128)(2,1)S(1)} %copy-done.4, f32[1,128]{1,0:T(1,128)S(1)} %bitcast.6, f32[1,128]{1,0:T(1,128)S(1)} %bitcast.10, bf16[128,128]{1,0:T(8,128)(2,1)S(1)} %copy-done.5, ...), custom_call_target="tpu_custom_call" | custom-call | flops 67108864 | bytes 1639936 | tf_op jit(solution)/shard_map/prepare/pallas_call | solution.py:63
  31.8 4.5 %all-to-all-done.1.refs_0_ = bf16[8,128,128]{2,1,0:T(8,128)(2,1)S(1)} async-done(((bf16[8,128,128]{2,1,0:T(8,128)(2,1)}), bf16[8,128,128]{2,1,0:T(8,128)(2,1)S(1)}, u32[]{:S(2)}, u32[]{:S(2)}) %all-to-all-start.1) | async-done | bytes 262176 | tf_op jit(solution)/shard_map/all_to_all | solution.py:267
  36.6 8.6 %all_to_all.20.refs_0_ = bf16[8,128,128]{2,1,0:T(8,128)(2,1)S(1)} all-to-all(bf16[8,128,128]{2,1,0:T(8,128)(2,1)S(1)} %middle.1), channel_id=1, replica_groups={{0,1,2,3,4,5,6,7},{8,9,10,11,12,13,14,15},{16,17,18,19,20,21,22,23},{24..., dimensions={0} | all-to-all | bytes 524288 | tf_op jit(solution)/shard_map/all_to_all | solution.py:267
  45.2 1.8 %products.1 = (bf16[16,128,128]{2,1,0:T(8,128)(2,1)}, bf16[128,128]{1,0:T(8,128)(2,1)S(1)}, bf16[128,128]{1,0:T(8,128)(2,1)S(1)}, bf16[128,128]{1,0:T(8,128)(2,1...) custom-call(bf16[8,128,128]{2,1,0:T(8,128)(2,1)S(1)} %all_to_all.20., ...), custom_call_target="tpu_custom_call" | custom-call | flops 67108864 | bytes 1835008 | tf_op jit(solution)/shard_map/products/pallas_call | solution.py:63
  47.0 5.2 %all-to-all-start.3 = ((bf16[16,128,128]{2,1,0:T(8,128)(2,1)}), bf16[16,128,128]{2,1,0:T(8,128)(2,1)S(1)}, u32[]{:S(2)}, u32[]{:S(2)}) async-start(bf16[16,128,128]{2,1,0:T(8,128)(2,1)} %get-tuple-element.45), calls=%async_computation.3 | async-start | bytes 1048576 | tf_op jit(solution)/shard_map/all_to_all | solution.py:261
  52.6 1.7 %collective-permute-start.8 = (bf16[128,128]{1,0:T(8,128)(2,1)S(1)}, bf16[128,128]{1,0:T(8,128)(2,1)S(1)}, u32[]{:S(2)}, u32[]{:S(2)}) collective-permute-start(bf16[128,128]{1,0:T(8,128)(2,1)S(1)} %get-tuple-element.53), channel_id=1, source_target_pairs={{0,2},{1,3},{2,0},{3,1},{4,6},{5,7},{6,4},{7,5},{8,10},{9,11},{10,... | collective-permute-start | bytes 98312 | tf_op jit(solution)/shard_map/ppermute | solution.py:275
  54.2 1.7 %collective-permute-start.10 = (bf16[128,128]{1,0:T(8,128)(2,1)}, bf16[128,128]{1,0:T(8,128)(2,1)S(1)}, u32[]{:S(2)}, u32[]{:S(2)}) collective-permute-start(bf16[128,128]{1,0:T(8,128)(2,1)} %get-tuple-element.55), channel_id=1, source_target_pairs={{0,4},{1,5},{2,6},{3,7},{4,0},{5,1},{6,2},{7,3},{8,12},{9,13},{10,... | collective-permute-start | bytes 98312 | tf_op jit(solution)/shard_map/ppermute | solution.py:275
  56.1 2.6 %collective-permute-start.12 = (bf16[128,128]{1,0:T(8,128)(2,1)}, bf16[128,128]{1,0:T(8,128)(2,1)S(1)}, u32[]{:S(2)}, u32[]{:S(2)}) collective-permute-start(bf16[128,128]{1,0:T(8,128)(2,1)} %get-tuple-element.57), channel_id=1, source_target_pairs={{0,6},{1,7},{2,4},{3,5},{4,2},{5,3},{6,0},{7,1},{8,14},{9,15},{10,... | collective-permute-start | bytes 98312 | tf_op jit(solution)/shard_map/ppermute | solution.py:275
  60.0 1.7 %slopes.1 = (bf16[8,512,128]{2,1,0:T(8,128)(2,1)S(1)}, f32[8,128,128]{2,1,0:T(8,128)S(1)}, f32[8,128,128]{2,1,0:T(8,128)S(1)}, f32[8,128]{1,0:T(8,128)S(1)}) custom-call(bf16[8,128,128]{2,1,0:T(8,128)(2,1)S(1)} %all-to-all-done.1.refs_0_, f32[8,128,128]{2,1,0:T(8,128)S(1)} %get-tuple-element.46.refs_1_, bf16[8,128,128]{2,1,0:T(8,128)(2,1)S(1)} %copy-done, ...), custom_call_target="tpu_custom_call" | custom-call | flops 201326592 | bytes 3348992 | tf_op jit(solution)/shard_map/slopes/pallas_call | solution.py:63
  61.7 0.8 %copy-done.2 = f32[8,128,128]{2,1,0:T(8,128)} copy-done((f32[8,128,128]{2,1,0:T(8,128)}, f32[8,128,128]{2,1,0:T(8,128)S(1)}, u32[]{:S(2)}) %copy-start.2) | copy-done | bytes 524312
  62.5 1.0 %collective-permute-done.10.refs_11_ = bf16[128,128]{1,0:T(8,128)(2,1)S(1)} collective-permute-done((bf16[128,128]{1,0:T(8,128)(2,1)}, bf16[128,128]{1,0:T(8,128)(2,1)S(1)}, u32[]{:S(2)}, u32[]{:S(2)}) %collective-permute-start.10) | collective-permute-done | bytes 32800 | tf_op jit(solution)/shard_map/ppermute | solution.py:275
  63.5 2.9 %collective-permute-done.12.refs_13_ = bf16[128,128]{1,0:T(8,128)(2,1)S(1)} collective-permute-done((bf16[128,128]{1,0:T(8,128)(2,1)}, bf16[128,128]{1,0:T(8,128)(2,1)S(1)}, u32[]{:S(2)}, u32[]{:S(2)}) %collective-permute-start.12) | collective-permute-done | bytes 32800 | tf_op jit(solution)/shard_map/ppermute | solution.py:275
  67.7 1.0 %copy-done.3 = f32[8,128,128]{2,1,0:T(8,128)S(1)} copy-done((f32[8,128,128]{2,1,0:T(8,128)S(1)}, f32[8,128,128]{2,1,0:T(8,128)}, u32[]{:S(2)}) %copy-start.3) | copy-done | bytes 524312
  68.7 0.8 %copy-done.8 = bf16[128,128]{1,0:T(8,128)(2,1)S(1)} copy-done((bf16[128,128]{1,0:T(8,128)(2,1)S(1)}, bf16[128,128]{1,0:T(8,128)(2,1)}, u32[]{:S(2)}) %copy-start.8) | copy-done | bytes 32792
  70.2 1.6 %finish.1 = bf16[8,128,128]{2,1,0:T(8,128)(2,1)} custom-call(bf16[16,128,128]{2,1,0:T(8,128)(2,1)S(1)} %all-to-all-done.3.refs_0_, bf16[8,512,128]{2,1,0:T(8,128)(2,1)S(1)} %get-tuple-element.47.refs_1_, f32[8,128,128]{2,1,0:T(8,128)S(1)} %get-tuple-element.48.refs_2_, f32[8,128,128]{2,1,0:T(8,128)S(1)} %copy-done.3, ...), custom_call_target="tpu_custom_call" | custom-call | flops 134217728 | bytes 3281408 | tf_op jit(solution)/shard_map/finish/pallas_call | solution.py:63
  (66 shorter events, 6.6 us)
Async XLA Ops:
  2.6 9.7 %copy-start.21 = (bf16[128,128]{1,0:T(8,128)(2,1)S(1)}, bf16[128,128]{1,0:T(8,128)(2,1)}, u32[]{:S(2)}) copy-start(bf16[128,128]{1,0:T(8,128)(2,1)} %get-tuple-element.36) | copy-start | bytes 98308
  2.6 9.8 %copy-start.20 = (bf16[128,128]{1,0:T(8,128)(2,1)S(1)}, bf16[128,128]{1,0:T(8,128)(2,1)}, u32[]{:S(2)}) copy-start(bf16[128,128]{1,0:T(8,128)(2,1)} %get-tuple-element.37) | copy-start | bytes 98308
  2.6 11.4 %copy-start.19 = (bf16[128,128]{1,0:T(8,128)(2,1)S(1)}, bf16[128,128]{1,0:T(8,128)(2,1)}, u32[]{:S(2)}) copy-start(bf16[128,128]{1,0:T(8,128)(2,1)} %get-tuple-element.38) | copy-start | bytes 98308
  2.6 11.5 %copy-start.18 = (bf16[128,128]{1,0:T(8,128)(2,1)S(1)}, bf16[128,128]{1,0:T(8,128)(2,1)}, u32[]{:S(2)}) copy-start(bf16[128,128]{1,0:T(8,128)(2,1)} %get-tuple-element.39) | copy-start | bytes 98308
  2.6 14.7 %copy-start.17 = (bf16[128,128]{1,0:T(8,128)(2,1)S(1)}, bf16[128,128]{1,0:T(8,128)(2,1)}, u32[]{:S(2)}) copy-start(bf16[128,128]{1,0:T(8,128)(2,1)} %get-tuple-element.40) | copy-start | bytes 98308
  2.7 22.4 %copy-start.11 = (bf16[128,128]{1,0:T(8,128)(2,1)S(1)}, bf16[128,128]{1,0:T(8,128)(2,1)}, u32[]{:S(2)}) copy-start(bf16[128,128]{1,0:T(8,128)(2,1)} %get-tuple-element.33.refs_1_) | copy-start | bytes 98308
  2.7 22.4 %all-to-all-start = ((bf16[16,128,128]{2,1,0:T(8,128)(2,1)}), bf16[16,128,128]{2,1,0:T(8,128)(2,1)S(1)}, u32[]{:S(2)}, u32[]{:S(2)}) async-start(bf16[16,128,128]{2,1,0:T(8,128)(2,1)} %get-tuple-element.32), calls=%async_computation | async-start | bytes 1048576 | tf_op jit(solution)/shard_map/all_to_all | solution.py:261
  10.2 4.0 %collective-permute-start = (bf16[128,128]{1,0:T(8,128)(2,1)S(1)}, bf16[128,128]{1,0:T(8,128)(2,1)S(1)}, u32[]{:S(2)}, u32[]{:S(2)}) collective-permute-start(bf16[128,128]{1,0:T(8,128)(2,1)S(1)} %copy-done.23), channel_id=1, source_target_pairs={{0,1},{1,0},{2,3},{3,2},{4,5},{5,4},{6,7},{7,6},{8,9},{9,8},{10,11... | collective-permute-start | bytes 98312 | tf_op jit(solution)/shard_map/ppermute | solution.py:275
  10.7 6.7 %collective-permute-start.1 = (bf16[128,128]{1,0:T(8,128)(2,1)S(1)}, bf16[128,128]{1,0:T(8,128)(2,1)S(1)}, u32[]{:S(2)}, u32[]{:S(2)}) collective-permute-start(bf16[128,128]{1,0:T(8,128)(2,1)S(1)} %copy-done.22), channel_id=1, source_target_pairs={{0,2},{1,3},{2,0},{3,1},{4,6},{5,7},{6,4},{7,5},{8,10},{9,11},{10,... | collective-permute-start | bytes 98312 | tf_op jit(solution)/shard_map/ppermute | solution.py:275
  12.3 5.0 %collective-permute-start.2 = (bf16[128,128]{1,0:T(8,128)(2,1)S(1)}, bf16[128,128]{1,0:T(8,128)(2,1)S(1)}, u32[]{:S(2)}, u32[]{:S(2)}) collective-permute-start(bf16[128,128]{1,0:T(8,128)(2,1)S(1)} %copy-done.21), channel_id=1, source_target_pairs={{0,3},{1,2},{2,1},{3,0},{4,7},{5,6},{6,5},{7,4},{8,11},{9,10},{10,... | collective-permute-start | bytes 98312 | tf_op jit(solution)/shard_map/ppermute | solution.py:275
  12.4 9.2 %collective-permute-start.3 = (bf16[128,128]{1,0:T(8,128)(2,1)S(1)}, bf16[128,128]{1,0:T(8,128)(2,1)S(1)}, u32[]{:S(2)}, u32[]{:S(2)}) collective-permute-start(bf16[128,128]{1,0:T(8,128)(2,1)S(1)} %copy-done.20), channel_id=1, source_target_pairs={{0,4},{1,5},{2,6},{3,7},{4,0},{5,1},{6,2},{7,3},{8,12},{9,13},{10,... | collective-permute-start | bytes 98312 | tf_op jit(solution)/shard_map/ppermute | solution.py:275
  14.1 7.5 %collective-permute-start.4 = (bf16[128,128]{1,0:T(8,128)(2,1)S(1)}, bf16[128,128]{1,0:T(8,128)(2,1)S(1)}, u32[]{:S(2)}, u32[]{:S(2)}) collective-permute-start(bf16[128,128]{1,0:T(8,128)(2,1)S(1)} %copy-done.19), channel_id=1, source_target_pairs={{0,5},{1,4},{2,7},{3,6},{4,1},{5,0},{6,3},{7,2},{8,13},{9,12},{10,... | collective-permute-start | bytes 98312 | tf_op jit(solution)/shard_map/ppermute | solution.py:275
  14.2 10.3 %collective-permute-start.5 = (bf16[128,128]{1,0:T(8,128)(2,1)S(1)}, bf16[128,128]{1,0:T(8,128)(2,1)S(1)}, u32[]{:S(2)}, u32[]{:S(2)}) collective-permute-start(bf16[128,128]{1,0:T(8,128)(2,1)S(1)} %copy-done.18), channel_id=1, source_target_pairs={{0,6},{1,7},{2,4},{3,5},{4,2},{5,3},{6,0},{7,1},{8,14},{9,15},{10,... | collective-permute-start | bytes 98312 | tf_op jit(solution)/shard_map/ppermute | solution.py:275
  17.4 7.1 %collective-permute-start.6 = (bf16[128,128]{1,0:T(8,128)(2,1)S(1)}, bf16[128,128]{1,0:T(8,128)(2,1)S(1)}, u32[]{:S(2)}, u32[]{:S(2)}) collective-permute-start(bf16[128,128]{1,0:T(8,128)(2,1)S(1)} %copy-done.17), channel_id=1, source_target_pairs={{0,7},{1,6},{2,5},{3,4},{4,3},{5,2},{6,1},{7,0},{8,15},{9,14},{10,... | collective-permute-start | bytes 98312 | tf_op jit(solution)/shard_map/ppermute | solution.py:275
  26.7 9.5 %all-to-all-start.1 = ((bf16[8,128,128]{2,1,0:T(8,128)(2,1)}), bf16[8,128,128]{2,1,0:T(8,128)(2,1)S(1)}, u32[]{:S(2)}, u32[]{:S(2)}) async-start(bf16[8,128,128]{2,1,0:T(8,128)(2,1)} %get-tuple-element.41), calls=%async_computation.1 | async-start | bytes 524288 | tf_op jit(solution)/shard_map/all_to_all | solution.py:267
  47.0 12.3 %copy-start.1 = (bf16[128,512]{1,0:T(8,128)(2,1)S(1)}, bf16[128,512]{1,0:T(8,128)(2,1)}, u32[]{:S(2)}) copy-start(bf16[128,512]{1,0:T(8,128)(2,1)} %refs_6_.5) | copy-start | bytes 393220
  47.0 20.7 %all-to-all-start.3 = ((bf16[16,128,128]{2,1,0:T(8,128)(2,1)}), bf16[16,128,128]{2,1,0:T(8,128)(2,1)S(1)}, u32[]{:S(2)}, u32[]{:S(2)}) async-start(bf16[16,128,128]{2,1,0:T(8,128)(2,1)} %get-tuple-element.45), calls=%async_computation.3 | async-start | bytes 1048576 | tf_op jit(solution)/shard_map/all_to_all | solution.py:261
  52.1 3.9 %collective-permute-start.7 = (bf16[128,128]{1,0:T(8,128)(2,1)S(1)}, bf16[128,128]{1,0:T(8,128)(2,1)S(1)}, u32[]{:S(2)}, u32[]{:S(2)}) collective-permute-start(bf16[128,128]{1,0:T(8,128)(2,1)S(1)} %get-tuple-element.52), channel_id=1, source_target_pairs={{0,1},{1,0},{2,3},{3,2},{4,5},{5,4},{6,7},{7,6},{8,9},{9,8},{10,11... | collective-permute-start | bytes 98312 | tf_op jit(solution)/shard_map/ppermute | solution.py:275
  52.6 6.8 %collective-permute-start.8 = (bf16[128,128]{1,0:T(8,128)(2,1)S(1)}, bf16[128,128]{1,0:T(8,128)(2,1)S(1)}, u32[]{:S(2)}, u32[]{:S(2)}) collective-permute-start(bf16[128,128]{1,0:T(8,128)(2,1)S(1)} %get-tuple-element.53), channel_id=1, source_target_pairs={{0,2},{1,3},{2,0},{3,1},{4,6},{5,7},{6,4},{7,5},{8,10},{9,11},{10,... | collective-permute-start | bytes 98312 | tf_op jit(solution)/shard_map/ppermute | solution.py:275
  54.2 8.3 %collective-permute-start.9 = (bf16[128,128]{1,0:T(8,128)(2,1)}, bf16[128,128]{1,0:T(8,128)(2,1)S(1)}, u32[]{:S(2)}, u32[]{:S(2)}) collective-permute-start(bf16[128,128]{1,0:T(8,128)(2,1)} %get-tuple-element.54), channel_id=1, source_target_pairs={{0,3},{1,2},{2,1},{3,0},{4,7},{5,6},{6,5},{7,4},{8,11},{9,10},{10,... | collective-permute-start | bytes 98312 | tf_op jit(solution)/shard_map/ppermute | solution.py:275
  54.2 9.3 %collective-permute-start.10 = (bf16[128,128]{1,0:T(8,128)(2,1)}, bf16[128,128]{1,0:T(8,128)(2,1)S(1)}, u32[]{:S(2)}, u32[]{:S(2)}) collective-permute-start(bf16[128,128]{1,0:T(8,128)(2,1)} %get-tuple-element.55), channel_id=1, source_target_pairs={{0,4},{1,5},{2,6},{3,7},{4,0},{5,1},{6,2},{7,3},{8,12},{9,13},{10,... | collective-permute-start | bytes 98312 | tf_op jit(solution)/shard_map/ppermute | solution.py:275
  55.9 7.6 %collective-permute-start.11 = (bf16[128,128]{1,0:T(8,128)(2,1)}, bf16[128,128]{1,0:T(8,128)(2,1)S(1)}, u32[]{:S(2)}, u32[]{:S(2)}) collective-permute-start(bf16[128,128]{1,0:T(8,128)(2,1)} %get-tuple-element.56), channel_id=1, source_target_pairs={{0,5},{1,4},{2,7},{3,6},{4,1},{5,0},{6,3},{7,2},{8,13},{9,12},{10,... | collective-permute-start | bytes 98312 | tf_op jit(solution)/shard_map/ppermute | solution.py:275
  56.1 10.4 %collective-permute-start.12 = (bf16[128,128]{1,0:T(8,128)(2,1)}, bf16[128,128]{1,0:T(8,128)(2,1)S(1)}, u32[]{:S(2)}, u32[]{:S(2)}) collective-permute-start(bf16[128,128]{1,0:T(8,128)(2,1)} %get-tuple-element.57), channel_id=1, source_target_pairs={{0,6},{1,7},{2,4},{3,5},{4,2},{5,3},{6,0},{7,1},{8,14},{9,15},{10,... | collective-permute-start | bytes 98312 | tf_op jit(solution)/shard_map/ppermute | solution.py:275
  59.3 7.7 %collective-permute-start.13 = (bf16[128,128]{1,0:T(8,128)(2,1)}, bf16[128,128]{1,0:T(8,128)(2,1)S(1)}, u32[]{:S(2)}, u32[]{:S(2)}) collective-permute-start(bf16[128,128]{1,0:T(8,128)(2,1)} %get-tuple-element.58), channel_id=1, source_target_pairs={{0,7},{1,6},{2,5},{3,4},{4,3},{5,2},{6,1},{7,0},{8,15},{9,14},{10,... | collective-permute-start | bytes 98312 | tf_op jit(solution)/shard_map/ppermute | solution.py:275
  (17 other events, 41.4 us)

commit v7 on v6

--- a/solution.py
+++ b/solution.py
@@ -38,7 +38,9 @@
     return centered * inv_std, inv_std
 
 
-def call(kernel, name, outs, args, fetched=(), scratch=(), flops=0, limit=VMEM_LIMIT):
+def call(
+    kernel, name, outs, args, fetched=(), unread=(), scratch=(), flops=0, limit=VMEM_LIMIT
+):
     moved = sum(a.size * a.dtype.itemsize for a in args) + sum(
         o.size * jnp.dtype(o.dtype).itemsize for o in outs
     )
@@ -65,7 +67,9 @@
         name=name,
         out_shape=outs,
         in_specs=[
-            pl.BlockSpec(memory_space=pltpu.HBM if n in fetched else pltpu.VMEM)
+            pl.BlockSpec(
+                memory_space=pltpu.HBM if n in fetched else pl.ANY if n in unread else pltpu.VMEM
+            )
             for n in range(n_args)
         ],
         out_specs=[pl.BlockSpec(memory_space=pltpu.VMEM) for _ in outs],
@@ -91,27 +95,40 @@
     return lax.rem(lax.axis_index("row"), count) ^ step
 
 
-def project_kernel(pair, mask, gain, bias, w_proj, right_panel, *refs):
-    *pieces, left_panel = refs
+def gated_rows(pair, mask, gain, bias, w_proj, side):
     rows = pair.shape[0]
     hidden = w_proj.shape[1] // 4
-    count, depth, width = left_panel.shape
-    block = depth // rows
-    halves = right_panel.shape[0] // count
-    w_flip = transposed(w_proj[...])
+    w_flip = transposed(w_proj[:, 2 * side * hidden : 2 * (side + 1) * hidden])
     gain_col, bias_col = column(gain[...]), column(bias[...])
     masks = cell_masks(mask, rows)
     for row in range(rows):
         normed, _ = norm_rows(jnp.transpose(pair[row].astype(F32)))
         zln = (normed * gain_col + bias_col).astype(BF16)
         proj = dot(w_flip, zln, 1, 0)
-        place = slice(row * block, (row + 1) * block)
-        left = masks[row] * sigmoid(proj[:hidden]) * proj[hidden : 2 * hidden]
-        left_panel[:, place, :] = left.reshape(count, block, width).astype(BF16)
-        right = masks[row] * sigmoid(proj[2 * hidden : 3 * hidden]) * proj[3 * hidden :]
+        yield row, masks[row] * sigmoid(proj[:hidden]) * proj[hidden:]
+
+
+def project_right_kernel(pair, mask, gain, bias, w_proj, right_panel):
+    rows = pair.shape[0]
+    devices, depth, width = right_panel.shape
+    block = depth // rows
+    hidden = w_proj.shape[1] // 4
+    count = hidden // block
+    for row, right in gated_rows(pair, mask, gain, bias, w_proj, 1):
         right = right.reshape(count, block, width).astype(BF16)
-        for half in range(halves):
-            right_panel[half * count : (half + 1) * count, place, :] = right
+        for start in range(0, devices, count):
+            right_panel[start : start + count, row * block : (row + 1) * block, :] = right
+
+
+def project_left_kernel(pair, mask, gain, bias, w_proj, after, *refs):
+    del after
+    *pieces, left_panel = refs
+    rows = pair.shape[0]
+    count, depth, width = left_panel.shape
+    block = depth // rows
+    for row, left in gated_rows(pair, mask, gain, bias, w_proj, 0):
+        left = left.reshape(count, block, width).astype(BF16)
+        left_panel[:, row * block : (row + 1) * block, :] = left
     for step, piece in enumerate(pieces):
         piece[...] = left_panel[partner(step, count)]
 
@@ -137,19 +154,26 @@
     wide[...] = panel[...].astype(F32).reshape(wide.shape)
 
 
-def tri_kernel(right_panel, *refs):
-    *pieces, products, left_all, right_all, left_wide, right_wide = refs
+def sort_left_kernel(*refs):
+    *pieces, left_all, left_wide = refs
     block, left_rows, _ = left_all.shape
-    right_rows = right_all.shape[1]
     depth = pieces[0].shape[0]
     for step, piece in enumerate(pieces):
         start = pl.multiple_of(partner(step, len(pieces)) * depth, depth)
         left_wide[pl.ds(start, depth), :] = piece[...].astype(F32)
+    for h in range(block):
+        left_all[h] = left_wide[pl.ds(h, left_rows, stride=block), :].astype(BF16)
+
+
+def tri_kernel(right_panel, left_all, after, products, right_all, left_wide, right_wide):
+    del after
+    block, left_rows, _ = left_all.shape
+    right_rows = right_all.shape[1]
     spread(right_panel, right_wide)
     for h in range(block):
-        left_all[h] = left_wide[pl.ds(h, left_rows, stride=block), :].astype(BF16)
-        right_all[h] = right_wide[pl.ds(h, right_rows, stride=block), :].astype(BF16)
-        left_wide[pl.ds(h, left_rows, stride=block), :] = dot(left_all[h], right_all[h], 1, 1)
+        right = right_wide[pl.ds(h, right_rows, stride=block), :].astype(BF16)
+        right_all[h] = right
+        left_wide[pl.ds(h, left_rows, stride=block), :] = dot(left_all[h], right, 1, 1)
     products[...] = left_wide[...].astype(BF16).reshape(products.shape)
 
 
@@ -173,20 +197,26 @@
         ).astype(BF16)
 
 
-def products_kernel(d_products, left_all, right_all, d_right_panel, *refs):
-    *pieces, left_wide, right_wide = refs
+def d_right_kernel(d_products, left_all, d_right_panel, d_tri_all, left_wide, right_wide):
     block, left_rows, _ = left_all.shape
-    right_rows = right_all.shape[1]
+    right_rows = right_wide.shape[0] // block
     spread(d_products, left_wide)
     for h in range(block):
         d_tri = left_wide[pl.ds(h, left_rows, stride=block), :].astype(BF16)
-        left_wide[pl.ds(h, left_rows, stride=block), :] = dot(d_tri, right_all[h], 1, 0)
+        d_tri_all[h] = d_tri
         right_wide[pl.ds(h, right_rows, stride=block), :] = dot(d_tri, left_all[h], 0, 0)
+    d_right_panel[...] = right_wide[...].astype(BF16).reshape(d_right_panel.shape)
+
+
+def d_left_kernel(d_tri_all, right_all, *refs):
+    *pieces, left_wide = refs
+    block, left_rows, _ = d_tri_all.shape
+    for h in range(block):
+        left_wide[pl.ds(h, left_rows, stride=block), :] = dot(d_tri_all[h], right_all[h], 1, 0)
     depth = pieces[0].shape[0]
     for step, piece in enumerate(pieces):
         start = pl.multiple_of(partner(step, len(pieces)) * depth, depth)
         piece[...] = left_wide[pl.ds(start, depth), :].astype(BF16)
-    d_right_panel[...] = right_wide[...].astype(BF16).reshape(d_right_panel.shape)
 
 
 def slopes_kernel(
@@ -197,12 +227,11 @@
     gain,
     bias,
     w_proj,
-    w_gate,
     out_gain,
     out_bias,
     w_out,
     slopes,
-    d_zln_gate,
+    d_gate_pre,
     normed_in,
     inv_in,
 ):
@@ -216,10 +245,9 @@
     for row in range(rows):
         tri_hat, _ = norm_rows(cell_row(products, row, rows))
         scaled = (tri_hat * out_gain_col + out_bias_col).astype(BF16)
-        d_gate_pre = (dot(out_flip, scaled, 1, 0) * gate_slope[row]).astype(BF16)
-        d_zln_gate[row] = dot(w_gate[...], d_gate_pre, 1, 0)
+        d_gate_pre[row] = (dot(out_flip, scaled, 1, 0) * gate_slope[row]).astype(BF16)
         normed, inv_std = norm_rows(jnp.transpose(pair[row].astype(F32)))
-        normed_in[row] = normed
+        normed_in[row] = normed.astype(normed_in.dtype)
         inv_in[row : row + 1] = inv_std
         zln = (normed * gain_col + bias_col).astype(BF16)
         proj = dot(w_flip, zln, 1, 0)
@@ -232,7 +260,9 @@
             slopes[row, base + hidden : base + 2 * hidden, :] = masked.astype(slopes.dtype)
 
 
-def finish_kernel(d_right_panel, slopes, d_zln_gate, normed_in, inv_in, gain, w_proj, *refs):
+def finish_kernel(
+    d_right_panel, slopes, d_gate_pre, normed_in, inv_in, gain, w_proj, w_gate, *refs
+):
     *pieces, grad, d_left_panel = refs
     for step, piece in enumerate(pieces):
         d_left_panel[partner(step, len(pieces))] = piece[...]
@@ -240,6 +270,7 @@
     count, depth, width = d_left_panel.shape
     hidden = count * depth // rows
     gain_col = column(gain[...])
+    weights = jnp.concatenate([w_proj[...], w_gate[...]], axis=1)
     for row in range(rows):
         d_right = cell_row(d_right_panel, row, rows)
         d_right = sum(d_right[n : n + hidden] for n in range(0, d_right.shape[0], hidden))
@@ -248,9 +279,9 @@
             for base in (2 * side * hidden, (2 * side + 1) * hidden):
                 slope = slopes[row, base : base + hidden, :].astype(F32)
                 parts.append((d_value * slope).astype(BF16))
-        d_zln = dot(w_proj[...], jnp.concatenate(parts, axis=0), 1, 0) + d_zln_gate[row]
-        d_in = d_zln * gain_col
-        normed = normed_in[row]
+        parts.append(d_gate_pre[row])
+        d_in = dot(weights, jnp.concatenate(parts, axis=0), 1, 0) * gain_col
+        normed = normed_in[row].astype(F32)
         mean_grad = jnp.mean(d_in, axis=0, keepdims=True)
         mean_cross = jnp.mean(d_in * normed, axis=0, keepdims=True)
         result = inv_in[row : row + 1] * (d_in - mean_grad - normed * mean_cross)
@@ -305,18 +336,36 @@
     cells = rows * width
     piece = shape((rows * block, width), BF16)
     left_panel = pltpu.VMEM(panel.shape, BF16)
-    right_panel, *pieces = call(
-        project_kernel,
-        "project",
-        [wide_panel] + [piece] * count,
+    left_wide = pltpu.VMEM((left_rows * block, width), F32)
+    right_wide = pltpu.VMEM((right_rows * block, width), F32)
+    (own_right,) = call(
+        project_right_kernel,
+        "project_right",
+        [wide_panel],
         [pair, mask, gain, bias, w_proj],
         fetched=range(5),
+        flops=2 * cells * channels * 2 * hidden,
+        limit=64 * 1024 * 1024 - 640 * 1024,
+    )
+    right_panel = swap(own_right)
+    pieces = call(
+        project_left_kernel,
+        "project_left",
+        [piece] * count,
+        [pair, mask, gain, bias, w_proj, own_right],
+        fetched=range(5),
+        unread=(5,),
         scratch=[left_panel],
-        flops=2 * cells * channels * 4 * hidden,
-        limit=64 * 1024 * 1024 - 896 * 1024,
-    )
-    right_panel = swap(right_panel)
+        flops=2 * cells * channels * 2 * hidden,
+    )
     pieces = swap_pieces(pieces)
+    (left_all,) = call(
+        sort_left_kernel,
+        "sort_left",
+        [shape((block, left_rows, width), BF16)],
+        pieces,
+        scratch=[left_wide],
+    )
     d_hat_centered, gate_slope = call(
         prepare_kernel,
         "prepare",
@@ -325,13 +374,12 @@
         fetched=range(7),
         flops=2 * cells * channels * 2 * hidden,
     )
-    left_wide = pltpu.VMEM((left_rows * block, width), F32)
-    right_wide = pltpu.VMEM((right_rows * block, width), F32)
-    products, left_all, right_all = call(
+    products, right_all = call(
         tri_kernel,
         "tri",
-        [panel, shape((block, left_rows, width), BF16), shape((block, right_rows, width), BF16)],
-        [right_panel, *pieces],
+        [panel, shape((block, right_rows, width), BF16)],
+        [right_panel, left_all, d_hat_centered],
+        unread=(2,),
         scratch=[left_wide, right_wide],
         flops=2 * block * left_rows * width * right_rows,
     )
@@ -344,23 +392,31 @@
         flops=20 * cells * hidden,
     )
     d_products = swap_half(d_products, count)
-    d_right_panel, *d_pieces = call(
-        products_kernel,
-        "products",
-        [wide_panel] + [piece] * count,
-        [d_products, left_all, right_all],
+    d_right_panel, d_tri_all = call(
+        d_right_kernel,
+        "d_right",
+        [wide_panel, shape((block, left_rows, width), BF16)],
+        [d_products, left_all],
         scratch=[left_wide, right_wide],
-        flops=4 * block * left_rows * width * right_rows,
+        flops=2 * block * left_rows * width * right_rows,
     )
     d_right_panel = swap(d_right_panel)
+    d_pieces = call(
+        d_left_kernel,
+        "d_left",
+        [piece] * count,
+        [d_tri_all, right_all],
+        scratch=[left_wide],
+        flops=2 * block * left_rows * width * right_rows,
+    )
     d_pieces = swap_pieces(d_pieces)
-    slopes, d_zln_gate, normed_in, inv_in = call(
+    slopes, d_gate_pre, normed_in, inv_in = call(
         slopes_kernel,
         "slopes",
         [
             shape((rows, 4 * hidden, width), BF16),
-            shape((rows, channels, width), F32),
-            shape((rows, channels, width), F32),
+            shape((rows, channels, width), BF16),
+            shape((rows, channels, width), BF16),
             shape((rows, width), F32),
         ],
         [
@@ -371,20 +427,19 @@
             gain,
             bias,
             w_proj,
-            w_gate,
             out_gain,
             out_bias,
             w_out,
         ],
-        fetched=range(2, 11),
+        fetched=range(2, 10),
         flops=2 * cells * channels * 6 * hidden,
     )
     (grad,) = call(
         finish_kernel,
         "finish",
         [shape(pair.shape, BF16)],
-        [d_right_panel, slopes, d_zln_gate, normed_in, inv_in, gain, w_proj, *d_pieces],
-        fetched=(5, 6),
+        [d_right_panel, slopes, d_gate_pre, normed_in, inv_in, gain, w_proj, w_gate, *d_pieces],
+        fetched=(5, 6, 7),
         scratch=[left_panel],
         flops=2 * cells * channels * 4 * hidden,
     )

time: 72.6 us -> 68.7 us (0.946)
  blocking collectives: 8.62 us -> 17.2 us
  waiting for transfers between devices: 17.3 us -> 11.1 us
  starting transfers between devices: 29.2 us -> 25.8 us
  local copies, waits for them, and re-layouts: 5.94 us -> 4.08 us
  Pallas kernels: 10.5 us -> 9.75 us
    all_to_all x1 -> x2, blocking collectives: 8.62 us -> 17.2 us  [swap_half(): lax.all_to_all(values, 'row', split_axis=0, concat_axis=0, tiled=True, ax...]
    all_to_all x1 -> x0, waiting for transfers between devices: 4.46 us -> none  [swap_half(): lax.all_to_all(values, 'row', split_axis=0, concat_axis=0, tiled=True, ax...]
    all_to_all x1 -> x0, starting transfers between devices: 3.54 us -> none  [swap_half(): lax.all_to_all(values, 'row', split_axis=0, concat_axis=0, tiled=True, ax...]
    unnamed x48 -> x36, local copies, waits for them, and re-layouts: 5.94 us -> 4.08 us
    ppermute x14, waiting for transfers between devices: 12.3 us -> 10.8 us  [swap_pieces(): lax.ppermute(pieces[step], 'row', [(d, d ^ step) for d in devices])]
    pallas_call x7 -> x10, Pallas kernels: 10.5 us -> 9.75 us  [call(): pl.pallas_call(body, name=name, out_shape=outs, in_specs=[pl.BlockSpec(me...]
  transfers between devices with their start and end apart: 17 -> 16, of which waited for: 8 -> 6; matrix products, arithmetic and copies ran while one was open for 0% -> 0% of each run, Pallas kernels for 4% -> 5%
where the time goes in v7:
time: 68.7 us; the launch traced here: 68.1 us
  starting transfers between devices  25.8 us (38%)
  blocking collectives  17.2 us (25%)
  waiting for transfers between devices  11.1 us (16%)
  Pallas kernels  9.75 us (14%)
  local copies, waits for them, and re-layouts  4.08 us (6%)
    all_to_all x2, blocking collectives, swap_half(): lax.all_to_all(values, 'row', split_axis=0, concat_axis=0, tiled=True, ax...  17.2 us
    ppermute x14, starting transfers between devices, swap_pieces(): lax.ppermute(pieces[step], 'row', [(d, d ^ step) for d in devices])  13.1 us
    all_to_all x2, starting transfers between devices, swap(): lax.all_to_all(values, 'row', split_axis=0, concat_axis=0, tiled=True)  12.6 us
    ppermute x14, waiting for transfers between devices, swap_pieces(): lax.ppermute(pieces[step], 'row', [(d, d ^ step) for d in devices])  10.8 us
    pallas_call x10, Pallas kernels, call(): pl.pallas_call(body, name=name, out_shape=outs, in_specs=[pl.BlockSpec(me...  9.75 us
    unnamed x36, local copies, waits for them, and re-layouts  4.08 us
  transfers between devices with their start and end apart: 16, of which 6 were waited for; matrix products, arithmetic and copies ran while one was open for 0% of the time, Pallas kernels for 5%

profile of v7, /device:TPU:0, one launch (start us, length us, event | category | flops | bytes accessed | tf_op | source)
XLA Modules:
  0.0 68.1 jit_solution(12072241201507791188)
XLA Ops:
  0.0 2.4 %project_right.1.refs_5_ = bf16[16,128,128]{2,1,0:T(8,128)(2,1)} custom-call(bf16[8,128,128]{2,1,0:T(8,128)(2,1)} %refs_2_.1, s32[1,128]{1,0:T(1,128)} %bitcast.14, f32[1,128]{1,0:T(1,128)} %bitcast.5, f32[1,128]{1,0:T(1,128)} %bitcast.10, bf16[128,512]{1,0:T(8,128)(2,1)} %refs_6_.5), custom_call_target="tpu_custom_call" | custom-call | flops 67108864 | bytes 919040 | tf_op jit(solution)/shard_map/project_right/pallas_call | solution.py:65
  2.5 7.5 %all-to-all-start = ((bf16[16,128,128]{2,1,0:T(8,128)(2,1)}), bf16[16,128,128]{2,1,0:T(8,128)(2,1)S(1)}, u32[]{:S(2)}, u32[]{:S(2)}) async-start(bf16[16,128,128]{2,1,0:T(8,128)(2,1)} %project_right.1.refs_5_), calls=%async_computation | async-start | bytes 1048576 | tf_op jit(solution)/shard_map/all_to_all | solution.py:292
  10.1 0.8 %project_left.1 = (bf16[128,128]{1,0:T(8,128)(2,1)S(1)}, bf16[128,128]{1,0:T(8,128)(2,1)S(1)}, bf16[128,128]{1,0:T(8,128)(2,1)S(1)}, bf16[128,128]{1,0:T(8,128)(...) custom-call(bf16[8,128,128]{2,1,0:T(8,128)(2,1)S(1)} %copy-done.1, ...), custom_call_target="tpu_custom_call" | custom-call | flops 67108864 | bytes 1181184 | tf_op jit(solution)/shard_map/project_left/pallas_call | solution.py:65
  11.3 1.7 %collective-permute-start.1 = (bf16[128,128]{1,0:T(8,128)(2,1)S(1)}, bf16[128,128]{1,0:T(8,128)(2,1)S(1)}, u32[]{:S(2)}, u32[]{:S(2)}) collective-permute-start(bf16[128,128]{1,0:T(8,128)(2,1)S(1)} %get-tuple-element.33), channel_id=1, source_target_pairs={{0,2},{1,3},{2,0},{3,1},{4,6},{5,7},{6,4},{7,5},{8,10},{9,11},{10,... | collective-permute-start | bytes 98312 | tf_op jit(solution)/shard_map/ppermute | solution.py:306
  13.0 1.7 %collective-permute-start.3 = (bf16[128,128]{1,0:T(8,128)(2,1)S(1)}, bf16[128,128]{1,0:T(8,128)(2,1)S(1)}, u32[]{:S(2)}, u32[]{:S(2)}) collective-permute-start(bf16[128,128]{1,0:T(8,128)(2,1)S(1)} %get-tuple-element.35), channel_id=1, source_target_pairs={{0,4},{1,5},{2,6},{3,7},{4,0},{5,1},{6,2},{7,3},{8,12},{9,13},{10,... | collective-permute-start | bytes 98312 | tf_op jit(solution)/shard_map/ppermute | solution.py:306
  14.8 2.6 %collective-permute-start.5 = (bf16[128,128]{1,0:T(8,128)(2,1)S(1)}, bf16[128,128]{1,0:T(8,128)(2,1)S(1)}, u32[]{:S(2)}, u32[]{:S(2)}) collective-permute-start(bf16[128,128]{1,0:T(8,128)(2,1)S(1)} %get-tuple-element.37), channel_id=1, source_target_pairs={{0,6},{1,7},{2,4},{3,5},{4,2},{5,3},{6,0},{7,1},{8,14},{9,15},{10,... | collective-permute-start | bytes 98312 | tf_op jit(solution)/shard_map/ppermute | solution.py:306
  18.1 0.8 %prepare.1 = (f32[8,128,128]{2,1,0:T(8,128)S(1)}, f32[8,128,128]{2,1,0:T(8,128)S(1)}) custom-call(bf16[8,128,128]{2,1,0:T(8,128)(2,1)S(1)} %copy-done.1, bf16[8,128,128]{2,1,0:T(8,128)(2,1)S(1)} %copy-done.3, f32[1,128]{1,0:T(1,128)S(1)} %bitcast.7, f32[1,128]{1,0:T(1,128)S(1)} %bitcast.12, bf16[128,128]{1,0:T(8,128)(2,1)S(1)} %copy-done.4, ...), custom_call_target="tpu_custom_call" | custom-call | flops 67108864 | bytes 1639936 | tf_op jit(solution)/shard_map/prepare/pallas_call | solution.py:65
  18.9 2.4 %collective-permute-done.3.refs_4_ = bf16[128,128]{1,0:T(8,128)(2,1)S(1)} collective-permute-done((bf16[128,128]{1,0:T(8,128)(2,1)S(1)}, bf16[128,128]{1,0:T(8,128)(2,1)S(1)}, u32[]{:S(2)}, u32[]{:S(2)}) %collective-permute-start.3) | collective-permute-done | bytes 32800 | tf_op jit(solution)/shard_map/ppermute | solution.py:306
  21.3 2.9 %collective-permute-done.5.refs_6_ = bf16[128,128]{1,0:T(8,128)(2,1)S(1)} collective-permute-done((bf16[128,128]{1,0:T(8,128)(2,1)S(1)}, bf16[128,128]{1,0:T(8,128)(2,1)S(1)}, u32[]{:S(2)}, u32[]{:S(2)}) %collective-permute-start.5) | collective-permute-done | bytes 32800 | tf_op jit(solution)/shard_map/ppermute | solution.py:306
  24.8 0.6 tri.1
  25.4 8.6 %all_to_all.20.refs_0_ = bf16[8,128,128]{2,1,0:T(8,128)(2,1)S(1)} all-to-all(bf16[8,128,128]{2,1,0:T(8,128)(2,1)S(1)} %get-tuple-element.40), channel_id=1, replica_groups={{0,1,2,3,4,5,6,7},{8,9,10,11,12,13,14,15},{16,17,18,19,20,21,22,23},{24..., dimensions={0} | all-to-all | bytes 524288 | tf_op jit(solution)/shard_map/all_to_all | solution.py:298
  34.3 8.6 %all_to_all.21.refs_0_ = bf16[8,128,128]{2,1,0:T(8,128)(2,1)S(1)} all-to-all(bf16[8,128,128]{2,1,0:T(8,128)(2,1)S(1)} %middle.1), channel_id=1, replica_groups={{0,1,2,3,4,5,6,7},{8,9,10,11,12,13,14,15},{16,17,18,19,20,21,22,23},{24..., dimensions={0} | all-to-all | bytes 524288 | tf_op jit(solution)/shard_map/all_to_all | solution.py:298
  42.9 1.5 %d_right.1 = (bf16[16,128,128]{2,1,0:T(8,128)(2,1)}, bf16[16,64,128]{2,1,0:T(8,128)(2,1)S(1)}) custom-call(bf16[8,128,128]{2,1,0:T(8,128)(2,1)S(1)} %all_to_all.21.refs_0_, bf16[16,64,128]{2,1,0:T(8,128)(2,1)S(1)} %sort_left.1.refs_1_), custom_call_target="tpu_custom_call" | custom-call | flops 33554432 | bytes 1310720 | tf_op jit(solution)/shard_map/d_right/pallas_call | solution.py:65
  44.4 5.1 %all-to-all-start.3 = ((bf16[16,128,128]{2,1,0:T(8,128)(2,1)}), bf16[16,128,128]{2,1,0:T(8,128)(2,1)S(1)}, u32[]{:S(2)}, u32[]{:S(2)}) async-start(bf16[16,128,128]{2,1,0:T(8,128)(2,1)} %get-tuple-element.41), calls=%async_computation.3 | async-start | bytes 1048576 | tf_op jit(solution)/shard_map/all_to_all | solution.py:292
  50.3 1.7 %collective-permute-start.8 = (bf16[128,128]{1,0:T(8,128)(2,1)S(1)}, bf16[128,128]{1,0:T(8,128)(2,1)S(1)}, u32[]{:S(2)}, u32[]{:S(2)}) collective-permute-start(bf16[128,128]{1,0:T(8,128)(2,1)S(1)} %get-tuple-element.51), channel_id=1, source_target_pairs={{0,2},{1,3},{2,0},{3,1},{4,6},{5,7},{6,4},{7,5},{8,10},{9,11},{10,... | collective-permute-start | bytes 98312 | tf_op jit(solution)/shard_map/ppermute | solution.py:306
  52.0 1.7 %collective-permute-start.10 = (bf16[128,128]{1,0:T(8,128)(2,1)S(1)}, bf16[128,128]{1,0:T(8,128)(2,1)S(1)}, u32[]{:S(2)}, u32[]{:S(2)}) collective-permute-start(bf16[128,128]{1,0:T(8,128)(2,1)S(1)} %get-tuple-element.53), channel_id=1, source_target_pairs={{0,4},{1,5},{2,6},{3,7},{4,0},{5,1},{6,2},{7,3},{8,12},{9,13},{10,... | collective-permute-start | bytes 98312 | tf_op jit(solution)/shard_map/ppermute | solution.py:306
  53.8 2.6 %collective-permute-start.12 = (bf16[128,128]{1,0:T(8,128)(2,1)S(1)}, bf16[128,128]{1,0:T(8,128)(2,1)S(1)}, u32[]{:S(2)}, u32[]{:S(2)}) collective-permute-start(bf16[128,128]{1,0:T(8,128)(2,1)S(1)} %get-tuple-element.55), channel_id=1, source_target_pairs={{0,6},{1,7},{2,4},{3,5},{4,2},{5,3},{6,0},{7,1},{8,14},{9,15},{10,... | collective-permute-start | bytes 98312 | tf_op jit(solution)/shard_map/ppermute | solution.py:306
  56.7 0.6 copy-done.16
  57.3 1.3 %slopes.1 = (bf16[8,512,128]{2,1,0:T(8,128)(2,1)S(1)}, bf16[8,128,128]{2,1,0:T(8,128)(2,1)S(1)}, bf16[8,128,128]{2,1,0:T(8,128)(2,1)S(1)}, f32[8,128]{1,0:T(8,128)S(1)}) custom-call(bf16[8,128,128]{2,1,0:T(8,128)(2,1)S(1)} %all_to_all.20.refs_0_, f32[8,128,128]{2,1,0:T(8,128)S(1)} %get-tuple-element.42.refs_1_, bf16[8,128,128]{2,1,0:T(8,128)(2,1)S(1)} %copy-done.1, ...), custom_call_target="tpu_custom_call" | custom-call | flops 201326592 | bytes 2791936 | tf_op jit(solution)/shard_map/slopes/pallas_call | solution.py:65
  58.6 2.3 %collective-permute-done.10.refs_12_ = bf16[128,128]{1,0:T(8,128)(2,1)S(1)} collective-permute-done((bf16[128,128]{1,0:T(8,128)(2,1)S(1)}, bf16[128,128]{1,0:T(8,128)(2,1)S(1)}, u32[]{:S(2)}, u32[]{:S(2)}) %collective-permute-start.10) | collective-permute-done | bytes 32800 | tf_op jit(solution)/shard_map/ppermute | solution.py:306
  60.9 2.9 %collective-permute-done.12.refs_14_ = bf16[128,128]{1,0:T(8,128)(2,1)S(1)} collective-permute-done((bf16[128,128]{1,0:T(8,128)(2,1)S(1)}, bf16[128,128]{1,0:T(8,128)(2,1)S(1)}, u32[]{:S(2)}, u32[]{:S(2)}) %collective-permute-start.12) | collective-permute-done | bytes 32800 | tf_op jit(solution)/shard_map/ppermute | solution.py:306
  65.0 0.8 %copy-done.9 = bf16[128,128]{1,0:T(8,128)(2,1)S(1)} copy-done((bf16[128,128]{1,0:T(8,128)(2,1)S(1)}, bf16[128,128]{1,0:T(8,128)(2,1)}, u32[]{:S(2)}) %copy-start.9) | copy-done | bytes 32792
  65.8 0.8 %copy-done.11 = bf16[128,128]{1,0:T(8,128)(2,1)S(1)} copy-done((bf16[128,128]{1,0:T(8,128)(2,1)S(1)}, bf16[128,128]{1,0:T(8,128)(2,1)}, u32[]{:S(2)}) %copy-start.11) | copy-done | bytes 32792
  66.5 1.6 %finish.1 = bf16[8,128,128]{2,1,0:T(8,128)(2,1)} custom-call(bf16[16,128,128]{2,1,0:T(8,128)(2,1)S(1)} %all-to-all-done.3.refs_0_, bf16[8,512,128]{2,1,0:T(8,128)(2,1)S(1)} %get-tuple-element.43.refs_1_, bf16[8,128,128]{2,1,0:T(8,128)(2,1)S(1)} %get-tuple-element.44.refs_2_, bf16[8,128,128]{2,1,0:T(8,128)(2,1)S(1)} %get-tuple-element.45.refs_3_, ...), custom_call_target="tpu_custom_call" | custom-call | flops 134217728 | bytes 2789888 | tf_op jit(solution)/shard_map/finish/pallas_call | solution.py:65
  (56 shorter events, 4.6 us)
Async XLA Ops:
  2.4 7.6 %copy-start = (bf16[16,128,128]{2,1,0:T(8,128)(2,1)S(1)}, bf16[16,128,128]{2,1,0:T(8,128)(2,1)}, u32[]{:S(2)}) copy-start(bf16[16,128,128]{2,1,0:T(8,128)(2,1)} %project_right.1.refs_5_) | copy-start | bytes 1572868
  2.4 7.6 %copy-start.1 = (bf16[8,128,128]{2,1,0:T(8,128)(2,1)S(1)}, bf16[8,128,128]{2,1,0:T(8,128)(2,1)}, u32[]{:S(2)}) copy-start(bf16[8,128,128]{2,1,0:T(8,128)(2,1)} %refs_2_.1) | copy-start | bytes 786436
  2.4 7.6 %copy-start.2 = (bf16[128,512]{1,0:T(8,128)(2,1)S(1)}, bf16[128,512]{1,0:T(8,128)(2,1)}, u32[]{:S(2)}) copy-start(bf16[128,512]{1,0:T(8,128)(2,1)} %refs_6_.5) | copy-start | bytes 393220
  2.4 7.6 %copy-start.12 = (f32[128]{0:T(128)S(1)}, f32[128]{0:T(128)}, u32[]{:S(2)}) copy-start(f32[128]{0:T(128)} %param.13) | copy-start | bytes 1540
  2.4 7.6 %copy-start.13 = (f32[128]{0:T(128)S(1)}, f32[128]{0:T(128)}, u32[]{:S(2)}) copy-start(f32[128]{0:T(128)} %param.14) | copy-start | bytes 1540
  2.4 7.6 %copy-start.14 = (s32[128]{0:T(128)S(1)}, s32[128]{0:T(128)}, u32[]{:S(2)}) copy-start(s32[128]{0:T(128)} %param.12) | copy-start | bytes 1540
  2.5 22.3 %all-to-all-start = ((bf16[16,128,128]{2,1,0:T(8,128)(2,1)}), bf16[16,128,128]{2,1,0:T(8,128)(2,1)S(1)}, u32[]{:S(2)}, u32[]{:S(2)}) async-start(bf16[16,128,128]{2,1,0:T(8,128)(2,1)} %project_right.1.refs_5_), calls=%async_computation | async-start | bytes 1048576 | tf_op jit(solution)/shard_map/all_to_all | solution.py:292
  10.0 7.4 %copy-start.3 = (bf16[8,128,128]{2,1,0:T(8,128)(2,1)S(1)}, bf16[8,128,128]{2,1,0:T(8,128)(2,1)}, u32[]{:S(2)}) copy-start(bf16[8,128,128]{2,1,0:T(8,128)(2,1)} %refs_1_.1) | copy-start | bytes 786436
  10.9 4.0 %collective-permute-start = (bf16[128,128]{1,0:T(8,128)(2,1)S(1)}, bf16[128,128]{1,0:T(8,128)(2,1)S(1)}, u32[]{:S(2)}, u32[]{:S(2)}) collective-permute-start(bf16[128,128]{1,0:T(8,128)(2,1)S(1)} %get-tuple-element.32), channel_id=1, source_target_pairs={{0,1},{1,0},{2,3},{3,2},{4,5},{5,4},{6,7},{7,6},{8,9},{9,8},{10,11... | collective-permute-start | bytes 98312 | tf_op jit(solution)/shard_map/ppermute | solution.py:306
  11.3 6.1 %collective-permute-start.1 = (bf16[128,128]{1,0:T(8,128)(2,1)S(1)}, bf16[128,128]{1,0:T(8,128)(2,1)S(1)}, u32[]{:S(2)}, u32[]{:S(2)}) collective-permute-start(bf16[128,128]{1,0:T(8,128)(2,1)S(1)} %get-tuple-element.33), channel_id=1, source_target_pairs={{0,2},{1,3},{2,0},{3,1},{4,6},{5,7},{6,4},{7,5},{8,10},{9,11},{10,... | collective-permute-start | bytes 98312 | tf_op jit(solution)/shard_map/ppermute | solution.py:306
  13.0 5.9 %collective-permute-start.2 = (bf16[128,128]{1,0:T(8,128)(2,1)S(1)}, bf16[128,128]{1,0:T(8,128)(2,1)S(1)}, u32[]{:S(2)}, u32[]{:S(2)}) collective-permute-start(bf16[128,128]{1,0:T(8,128)(2,1)S(1)} %get-tuple-element.34), channel_id=1, source_target_pairs={{0,3},{1,2},{2,1},{3,0},{4,7},{5,6},{6,5},{7,4},{8,11},{9,10},{10,... | collective-permute-start | bytes 98312 | tf_op jit(solution)/shard_map/ppermute | solution.py:306
  13.0 8.3 %collective-permute-start.3 = (bf16[128,128]{1,0:T(8,128)(2,1)S(1)}, bf16[128,128]{1,0:T(8,128)(2,1)S(1)}, u32[]{:S(2)}, u32[]{:S(2)}) collective-permute-start(bf16[128,128]{1,0:T(8,128)(2,1)S(1)} %get-tuple-element.35), channel_id=1, source_target_pairs={{0,4},{1,5},{2,6},{3,7},{4,0},{5,1},{6,2},{7,3},{8,12},{9,13},{10,... | collective-permute-start | bytes 98312 | tf_op jit(solution)/shard_map/ppermute | solution.py:306
  14.7 6.6 %collective-permute-start.4 = (bf16[128,128]{1,0:T(8,128)(2,1)S(1)}, bf16[128,128]{1,0:T(8,128)(2,1)S(1)}, u32[]{:S(2)}, u32[]{:S(2)}) collective-permute-start(bf16[128,128]{1,0:T(8,128)(2,1)S(1)} %get-tuple-element.36), channel_id=1, source_target_pairs={{0,5},{1,4},{2,7},{3,6},{4,1},{5,0},{6,3},{7,2},{8,13},{9,12},{10,... | collective-permute-start | bytes 98312 | tf_op jit(solution)/shard_map/ppermute | solution.py:306
  14.8 9.4 %collective-permute-start.5 = (bf16[128,128]{1,0:T(8,128)(2,1)S(1)}, bf16[128,128]{1,0:T(8,128)(2,1)S(1)}, u32[]{:S(2)}, u32[]{:S(2)}) collective-permute-start(bf16[128,128]{1,0:T(8,128)(2,1)S(1)} %get-tuple-element.37), channel_id=1, source_target_pairs={{0,6},{1,7},{2,4},{3,5},{4,2},{5,3},{6,0},{7,1},{8,14},{9,15},{10,... | collective-permute-start | bytes 98312 | tf_op jit(solution)/shard_map/ppermute | solution.py:306
  17.4 6.8 %collective-permute-start.6 = (bf16[128,128]{1,0:T(8,128)(2,1)S(1)}, bf16[128,128]{1,0:T(8,128)(2,1)S(1)}, u32[]{:S(2)}, u32[]{:S(2)}) collective-permute-start(bf16[128,128]{1,0:T(8,128)(2,1)S(1)} %get-tuple-element.38), channel_id=1, source_target_pairs={{0,7},{1,6},{2,5},{3,4},{4,3},{5,2},{6,1},{7,0},{8,15},{9,14},{10,... | collective-permute-start | bytes 98312 | tf_op jit(solution)/shard_map/ppermute | solution.py:306
  44.4 20.7 %all-to-all-start.3 = ((bf16[16,128,128]{2,1,0:T(8,128)(2,1)}), bf16[16,128,128]{2,1,0:T(8,128)(2,1)S(1)}, u32[]{:S(2)}, u32[]{:S(2)}) async-start(bf16[16,128,128]{2,1,0:T(8,128)(2,1)} %get-tuple-element.41), calls=%async_computation.3 | async-start | bytes 1048576 | tf_op jit(solution)/shard_map/all_to_all | solution.py:292
  49.9 4.0 %collective-permute-start.7 = (bf16[128,128]{1,0:T(8,128)(2,1)S(1)}, bf16[128,128]{1,0:T(8,128)(2,1)S(1)}, u32[]{:S(2)}, u32[]{:S(2)}) collective-permute-start(bf16[128,128]{1,0:T(8,128)(2,1)S(1)} %get-tuple-element.50), channel_id=1, source_target_pairs={{0,1},{1,0},{2,3},{3,2},{4,5},{5,4},{6,7},{7,6},{8,9},{9,8},{10,11... | collective-permute-start | bytes 98312 | tf_op jit(solution)/shard_map/ppermute | solution.py:306
  50.3 6.3 %collective-permute-start.8 = (bf16[128,128]{1,0:T(8,128)(2,1)S(1)}, bf16[128,128]{1,0:T(8,128)(2,1)S(1)}, u32[]{:S(2)}, u32[]{:S(2)}) collective-permute-start(bf16[128,128]{1,0:T(8,128)(2,1)S(1)} %get-tuple-element.51), channel_id=1, source_target_pairs={{0,2},{1,3},{2,0},{3,1},{4,6},{5,7},{6,4},{7,5},{8,10},{9,11},{10,... | collective-permute-start | bytes 98312 | tf_op jit(solution)/shard_map/ppermute | solution.py:306
  52.0 6.6 %collective-permute-start.9 = (bf16[128,128]{1,0:T(8,128)(2,1)S(1)}, bf16[128,128]{1,0:T(8,128)(2,1)S(1)}, u32[]{:S(2)}, u32[]{:S(2)}) collective-permute-start(bf16[128,128]{1,0:T(8,128)(2,1)S(1)} %get-tuple-element.52), channel_id=1, source_target_pairs={{0,3},{1,2},{2,1},{3,0},{4,7},{5,6},{6,5},{7,4},{8,11},{9,10},{10,... | collective-permute-start | bytes 98312 | tf_op jit(solution)/shard_map/ppermute | solution.py:306
  52.0 8.9 %collective-permute-start.10 = (bf16[128,128]{1,0:T(8,128)(2,1)S(1)}, bf16[128,128]{1,0:T(8,128)(2,1)S(1)}, u32[]{:S(2)}, u32[]{:S(2)}) collective-permute-start(bf16[128,128]{1,0:T(8,128)(2,1)S(1)} %get-tuple-element.53), channel_id=1, source_target_pairs={{0,4},{1,5},{2,6},{3,7},{4,0},{5,1},{6,2},{7,3},{8,12},{9,13},{10,... | collective-permute-start | bytes 98312 | tf_op jit(solution)/shard_map/ppermute | solution.py:306
  53.7 7.2 %collective-permute-start.11 = (bf16[128,128]{1,0:T(8,128)(2,1)S(1)}, bf16[128,128]{1,0:T(8,128)(2,1)S(1)}, u32[]{:S(2)}, u32[]{:S(2)}) collective-permute-start(bf16[128,128]{1,0:T(8,128)(2,1)S(1)} %get-tuple-element.54), channel_id=1, source_target_pairs={{0,5},{1,4},{2,7},{3,6},{4,1},{5,0},{6,3},{7,2},{8,13},{9,12},{10,... | collective-permute-start | bytes 98312 | tf_op jit(solution)/shard_map/ppermute | solution.py:306
  53.8 10.0 %collective-permute-start.12 = (bf16[128,128]{1,0:T(8,128)(2,1)S(1)}, bf16[128,128]{1,0:T(8,128)(2,1)S(1)}, u32[]{:S(2)}, u32[]{:S(2)}) collective-permute-start(bf16[128,128]{1,0:T(8,128)(2,1)S(1)} %get-tuple-element.55), channel_id=1, source_target_pairs={{0,6},{1,7},{2,4},{3,5},{4,2},{5,3},{6,0},{7,1},{8,14},{9,15},{10,... | collective-permute-start | bytes 98312 | tf_op jit(solution)/shard_map/ppermute | solution.py:306
  56.7 7.7 %collective-permute-start.13 = (bf16[128,128]{1,0:T(8,128)(2,1)S(1)}, bf16[128,128]{1,0:T(8,128)(2,1)S(1)}, u32[]{:S(2)}, u32[]{:S(2)}) collective-permute-start(bf16[128,128]{1,0:T(8,128)(2,1)S(1)} %get-tuple-element.56), channel_id=1, source_target_pairs={{0,7},{1,6},{2,5},{3,4},{4,3},{5,2},{6,1},{7,0},{8,15},{9,14},{10,... | collective-permute-start | bytes 98312 | tf_op jit(solution)/shard_map/ppermute | solution.py:306
  57.3 7.7 %copy-start.5 = (bf16[128,128]{1,0:T(8,128)(2,1)S(1)}, bf16[128,128]{1,0:T(8,128)(2,1)}, u32[]{:S(2)}) copy-start(bf16[128,128]{1,0:T(8,128)(2,1)} %refs_7_.1) | copy-start | bytes 98308
  (10 other events, 26.7 us)

commit v8 on v7

--- a/solution.py
+++ b/solution.py
@@ -39,7 +39,7 @@
 
 
 def call(
-    kernel, name, outs, args, fetched=(), unread=(), scratch=(), flops=0, limit=VMEM_LIMIT
+    kernel, name, outs, args, fetched=(), unread=(), sent=(), scratch=(), flops=0, limit=VMEM_LIMIT
 ):
     moved = sum(a.size * a.dtype.itemsize for a in args) + sum(
         o.size * jnp.dtype(o.dtype).itemsize for o in outs
@@ -72,7 +72,9 @@
             )
             for n in range(n_args)
         ],
-        out_specs=[pl.BlockSpec(memory_space=pltpu.VMEM) for _ in outs],
+        out_specs=[
+            pl.BlockSpec(memory_space=pltpu.HBM if n in sent else pltpu.VMEM) for n in range(n_outs)
+        ],
         scratch_shapes=buffers + list(scratch),
         compiler_params=pltpu.CompilerParams(vmem_limit_bytes=limit),
         cost_estimate=pl.CostEstimate(flops=flops, bytes_accessed=moved, transcendentals=0),
@@ -96,28 +98,40 @@
 
 
 def gated_rows(pair, mask, gain, bias, w_proj, side):
-    rows = pair.shape[0]
+    rows, width, _ = pair.shape
     hidden = w_proj.shape[1] // 4
     w_flip = transposed(w_proj[:, 2 * side * hidden : 2 * (side + 1) * hidden])
     gain_col, bias_col = column(gain[...]), column(bias[...])
     masks = cell_masks(mask, rows)
-    for row in range(rows):
-        normed, _ = norm_rows(jnp.transpose(pair[row].astype(F32)))
-        zln = (normed * gain_col + bias_col).astype(BF16)
-        proj = dot(w_flip, zln, 1, 0)
-        yield row, masks[row] * sigmoid(proj[:hidden]) * proj[hidden:]
-
-
-def project_right_kernel(pair, mask, gain, bias, w_proj, right_panel):
+    for first in range(0, rows, 2):
+        zlns = []
+        for row in (first, first + 1):
+            normed, _ = norm_rows(jnp.transpose(pair[row].astype(F32)))
+            zlns.append((normed * gain_col + bias_col).astype(BF16))
+        proj = dot(w_flip, jnp.concatenate(zlns, axis=1), 1, 0)
+        gated = sigmoid(proj[:hidden]) * proj[hidden:]
+        yield first, masks[first] * gated[:, :width]
+        yield first + 1, masks[first + 1] * gated[:, width:]
+
+
+def project_right_kernel(pair, mask, gain, bias, w_proj, right_panel, own_panel, sems):
     rows = pair.shape[0]
-    devices, depth, width = right_panel.shape
+    count, depth, width = own_panel.shape
     block = depth // rows
-    hidden = w_proj.shape[1] // 4
-    count = hidden // block
+    copies = []
     for row, right in gated_rows(pair, mask, gain, bias, w_proj, 1):
-        right = right.reshape(count, block, width).astype(BF16)
-        for start in range(0, devices, count):
-            right_panel[start : start + count, row * block : (row + 1) * block, :] = right
+        place = pl.ds(row * block, block)
+        own_panel[:, place, :] = right.reshape(count, block, width).astype(BF16)
+        for half in range(right_panel.shape[0] // count):
+            copy = pltpu.make_async_copy(
+                own_panel.at[:, place, :],
+                right_panel.at[pl.ds(half * count, count), place, :],
+                sems.at[row, half],
+            )
+            copy.start()
+            copies.append(copy)
+    for copy in copies:
+        copy.wait()
 
 
 def project_left_kernel(pair, mask, gain, bias, w_proj, after, *refs):
@@ -197,15 +211,26 @@
         ).astype(BF16)
 
 
-def d_right_kernel(d_products, left_all, d_right_panel, d_tri_all, left_wide, right_wide):
+def d_right_kernel(
+    d_products, left_all, d_right_panel, d_tri_all, left_wide, right_wide, panel, sems
+):
     block, left_rows, _ = left_all.shape
-    right_rows = right_wide.shape[0] // block
+    devices, depth, _ = panel.shape
     spread(d_products, left_wide)
     for h in range(block):
         d_tri = left_wide[pl.ds(h, left_rows, stride=block), :].astype(BF16)
         d_tri_all[h] = d_tri
-        right_wide[pl.ds(h, right_rows, stride=block), :] = dot(d_tri, left_all[h], 0, 0)
-    d_right_panel[...] = right_wide[...].astype(BF16).reshape(d_right_panel.shape)
+        right_wide[pl.ds(h, devices * depth // block, stride=block), :] = dot(
+            d_tri, left_all[h], 0, 0
+        )
+    copies = []
+    for device in range(devices):
+        panel[device] = right_wide[device * depth : (device + 1) * depth, :].astype(BF16)
+        copy = pltpu.make_async_copy(panel.at[device], d_right_panel.at[device], sems.at[device])
+        copy.start()
+        copies.append(copy)
+    for copy in copies:
+        copy.wait()
 
 
 def d_left_kernel(d_tri_all, right_all, *refs):
@@ -260,32 +285,57 @@
             slopes[row, base + hidden : base + 2 * hidden, :] = masked.astype(slopes.dtype)
 
 
-def finish_kernel(
-    d_right_panel, slopes, d_gate_pre, normed_in, inv_in, gain, w_proj, w_gate, *refs
-):
-    *pieces, grad, d_left_panel = refs
+def sort_d_left_kernel(*refs):
+    *pieces, d_left_panel = refs
     for step, piece in enumerate(pieces):
         d_left_panel[partner(step, len(pieces))] = piece[...]
+
+
+def finish_kernel(
+    d_right_panel,
+    d_left_panel,
+    slopes,
+    d_gate_pre,
+    normed_in,
+    inv_in,
+    gain,
+    w_proj,
+    w_gate,
+    grad,
+    own_grad,
+    sems,
+):
     rows = grad.shape[0]
     count, depth, width = d_left_panel.shape
     hidden = count * depth // rows
     gain_col = column(gain[...])
     weights = jnp.concatenate([w_proj[...], w_gate[...]], axis=1)
-    for row in range(rows):
-        d_right = cell_row(d_right_panel, row, rows)
-        d_right = sum(d_right[n : n + hidden] for n in range(0, d_right.shape[0], hidden))
-        parts = []
-        for side, d_value in enumerate((cell_row(d_left_panel, row, rows), d_right)):
-            for base in (2 * side * hidden, (2 * side + 1) * hidden):
-                slope = slopes[row, base : base + hidden, :].astype(F32)
-                parts.append((d_value * slope).astype(BF16))
-        parts.append(d_gate_pre[row])
-        d_in = dot(weights, jnp.concatenate(parts, axis=0), 1, 0) * gain_col
-        normed = normed_in[row].astype(F32)
-        mean_grad = jnp.mean(d_in, axis=0, keepdims=True)
-        mean_cross = jnp.mean(d_in * normed, axis=0, keepdims=True)
-        result = inv_in[row : row + 1] * (d_in - mean_grad - normed * mean_cross)
-        grad[row] = jnp.transpose(result).astype(BF16)
+    copies = []
+    for first in range(0, rows, 2):
+        stacks = []
+        for row in (first, first + 1):
+            d_right = cell_row(d_right_panel, row, rows)
+            d_right = sum(d_right[n : n + hidden] for n in range(0, d_right.shape[0], hidden))
+            parts = []
+            for side, d_value in enumerate((cell_row(d_left_panel, row, rows), d_right)):
+                for base in (2 * side * hidden, (2 * side + 1) * hidden):
+                    slope = slopes[row, base : base + hidden, :].astype(F32)
+                    parts.append((d_value * slope).astype(BF16))
+            parts.append(d_gate_pre[row])
+            stacks.append(jnp.concatenate(parts, axis=0))
+        d_zln = dot(weights, jnp.concatenate(stacks, axis=1), 1, 0)
+        for n, row in enumerate((first, first + 1)):
+            d_in = d_zln[:, n * width : (n + 1) * width] * gain_col
+            normed = normed_in[row].astype(F32)
+            mean_grad = jnp.mean(d_in, axis=0, keepdims=True)
+            mean_cross = jnp.mean(d_in * normed, axis=0, keepdims=True)
+            result = inv_in[row : row + 1] * (d_in - mean_grad - normed * mean_cross)
+            own_grad[row] = jnp.transpose(result).astype(BF16)
+            copy = pltpu.make_async_copy(own_grad.at[row], grad.at[row], sems.at[row])
+            copy.start()
+            copies.append(copy)
+    for copy in copies:
+        copy.wait()
 
 
 def swap(values):
@@ -344,6 +394,8 @@
         [wide_panel],
         [pair, mask, gain, bias, w_proj],
         fetched=range(5),
+        sent=(0,),
+        scratch=[left_panel, pltpu.SemaphoreType.DMA((rows, halves))],
         flops=2 * cells * channels * 2 * hidden,
         limit=64 * 1024 * 1024 - 640 * 1024,
     )
@@ -397,7 +449,13 @@
         "d_right",
         [wide_panel, shape((block, left_rows, width), BF16)],
         [d_products, left_all],
-        scratch=[left_wide, right_wide],
+        sent=(0,),
+        scratch=[
+            left_wide,
+            right_wide,
+            pltpu.VMEM(wide_panel.shape, BF16),
+            pltpu.SemaphoreType.DMA((devices,)),
+        ],
         flops=2 * block * left_rows * width * right_rows,
     )
     d_right_panel = swap(d_right_panel)
@@ -410,6 +468,7 @@
         flops=2 * block * left_rows * width * right_rows,
     )
     d_pieces = swap_pieces(d_pieces)
+    (d_left_panel,) = call(sort_d_left_kernel, "sort_d_left", [panel], d_pieces)
     slopes, d_gate_pre, normed_in, inv_in = call(
         slopes_kernel,
         "slopes",
@@ -438,9 +497,20 @@
         finish_kernel,
         "finish",
         [shape(pair.shape, BF16)],
-        [d_right_panel, slopes, d_gate_pre, normed_in, inv_in, gain, w_proj, w_gate, *d_pieces],
-        fetched=(5, 6, 7),
-        scratch=[left_panel],
+        [
+            d_right_panel,
+            d_left_panel,
+            slopes,
+            d_gate_pre,
+            normed_in,
+            inv_in,
+            gain,
+            w_proj,
+            w_gate,
+        ],
+        fetched=(6, 7, 8),
+        sent=(0,),
+        scratch=[pltpu.VMEM(pair.shape, BF16), pltpu.SemaphoreType.DMA((rows,))],
         flops=2 * cells * channels * 4 * hidden,
     )
     return grad

time: 68.7 us -> 67.2 us (0.978)
  local copies, waits for them, and re-layouts: 4.08 us -> 1.54 us
    unnamed x36 -> x28, local copies, waits for them, and re-layouts: 4.08 us -> 1.54 us
    pallas_call x10 -> x11, Pallas kernels: 9.75 us -> 10 us  [call(): pl.pallas_call(body, name=name, out_shape=outs, in_specs=[pl.BlockSpec(me...]
  transfers between devices with their start and end apart: 16 -> 16, of which waited for: 6 -> 7; matrix products, arithmetic and copies ran while one was open for 0% -> 0% of each run, Pallas kernels for 5% -> 5%
where the time goes in v8:
time: 67.2 us; the launch traced here: 66.4 us
  starting transfers between devices  25.8 us (38%)
  blocking collectives  17.2 us (26%)
  waiting for transfers between devices  11.6 us (17%)
  Pallas kernels  10 us (15%)
  local copies, waits for them, and re-layouts  1.54 us (2%)
    all_to_all x2, blocking collectives, swap_half(): lax.all_to_all(values, 'row', split_axis=0, concat_axis=0, tiled=True, ax...  17.2 us
    ppermute x14, starting transfers between devices, swap_pieces(): lax.ppermute(pieces[step], 'row', [(d, d ^ step) for d in devices])  13.1 us
    all_to_all x2, starting transfers between devices, swap(): lax.all_to_all(values, 'row', split_axis=0, concat_axis=0, tiled=True)  12.6 us
    ppermute x14, waiting for transfers between devices, swap_pieces(): lax.ppermute(pieces[step], 'row', [(d, d ^ step) for d in devices])  10.8 us
    pallas_call x11, Pallas kernels, call(): pl.pallas_call(body, name=name, out_shape=outs, in_specs=[pl.BlockSpec(me...  10 us
    unnamed x28, local copies, waits for them, and re-layouts  1.54 us
  transfers between devices with their start and end apart: 16, of which 7 were waited for; matrix products, arithmetic and copies ran while one was open for 0% of the time, Pallas kernels for 5%

profile of v8, /device:TPU:0, one launch (start us, length us, event | category | flops | bytes accessed | tf_op | source)
XLA Modules:
  0.0 66.4 jit_solution(10241109723143121559)
XLA Ops:
  0.0 2.5 %project_right.1.refs_5_ = bf16[16,128,128]{2,1,0:T(8,128)(2,1)} custom-call(bf16[8,128,128]{2,1,0:T(8,128)(2,1)} %refs_2_.1, s32[1,128]{1,0:T(1,128)} %bitcast.14, f32[1,128]{1,0:T(1,128)} %bitcast.5, f32[1,128]{1,0:T(1,128)} %bitcast.10, bf16[128,512]{1,0:T(8,128)(2,1)} %refs_7_.1), custom_call_target="tpu_custom_call" | custom-call | flops 67108864 | bytes 919040 | tf_op jit(solution)/shard_map/project_right/pallas_call | solution.py:65
  2.5 7.5 %all-to-all-start = ((bf16[16,128,128]{2,1,0:T(8,128)(2,1)}), bf16[16,128,128]{2,1,0:T(8,128)(2,1)S(1)}, u32[]{:S(2)}, u32[]{:S(2)}) async-start(bf16[16,128,128]{2,1,0:T(8,128)(2,1)} %project_right.1.refs_5_), calls=%async_computation | async-start | bytes 1048576 | tf_op jit(solution)/shard_map/all_to_all | solution.py:342
  10.2 0.8 %project_left.1 = (bf16[128,128]{1,0:T(8,128)(2,1)S(1)}, bf16[128,128]{1,0:T(8,128)(2,1)S(1)}, bf16[128,128]{1,0:T(8,128)(2,1)S(1)}, bf16[128,128]{1,0:T(8,128)(...) custom-call(bf16[8,128,128]{2,1,0:T(8,128)(2,1)S(1)} %copy-done.1, ...), custom_call_target="tpu_custom_call" | custom-call | flops 67108864 | bytes 1181184 | tf_op jit(solution)/shard_map/project_left/pallas_call | solution.py:65
  11.4 1.7 %collective-permute-start.1 = (bf16[128,128]{1,0:T(8,128)(2,1)S(1)}, bf16[128,128]{1,0:T(8,128)(2,1)S(1)}, u32[]{:S(2)}, u32[]{:S(2)}) collective-permute-start(bf16[128,128]{1,0:T(8,128)(2,1)S(1)} %get-tuple-element.33), channel_id=1, source_target_pairs={{0,2},{1,3},{2,0},{3,1},{4,6},{5,7},{6,4},{7,5},{8,10},{9,11},{10,... | collective-permute-start | bytes 98312 | tf_op jit(solution)/shard_map/ppermute | solution.py:356
  13.1 1.7 %collective-permute-start.3 = (bf16[128,128]{1,0:T(8,128)(2,1)S(1)}, bf16[128,128]{1,0:T(8,128)(2,1)S(1)}, u32[]{:S(2)}, u32[]{:S(2)}) collective-permute-start(bf16[128,128]{1,0:T(8,128)(2,1)S(1)} %get-tuple-element.35), channel_id=1, source_target_pairs={{0,4},{1,5},{2,6},{3,7},{4,0},{5,1},{6,2},{7,3},{8,12},{9,13},{10,... | collective-permute-start | bytes 98312 | tf_op jit(solution)/shard_map/ppermute | solution.py:356
  14.9 2.6 %collective-permute-start.5 = (bf16[128,128]{1,0:T(8,128)(2,1)S(1)}, bf16[128,128]{1,0:T(8,128)(2,1)S(1)}, u32[]{:S(2)}, u32[]{:S(2)}) collective-permute-start(bf16[128,128]{1,0:T(8,128)(2,1)S(1)} %get-tuple-element.37), channel_id=1, source_target_pairs={{0,6},{1,7},{2,4},{3,5},{4,2},{5,3},{6,0},{7,1},{8,14},{9,15},{10,... | collective-permute-start | bytes 98312 | tf_op jit(solution)/shard_map/ppermute | solution.py:356
  17.6 0.6 copy-done.11
  18.2 0.8 %prepare.1 = (f32[8,128,128]{2,1,0:T(8,128)S(1)}, f32[8,128,128]{2,1,0:T(8,128)S(1)}) custom-call(bf16[8,128,128]{2,1,0:T(8,128)(2,1)S(1)} %copy-done.1, bf16[8,128,128]{2,1,0:T(8,128)(2,1)S(1)} %copy-done.3, f32[1,128]{1,0:T(1,128)S(1)} %bitcast.7, f32[1,128]{1,0:T(1,128)S(1)} %bitcast.12, bf16[128,128]{1,0:T(8,128)(2,1)S(1)} %copy-done.4, ...), custom_call_target="tpu_custom_call" | custom-call | flops 67108864 | bytes 1639936 | tf_op jit(solution)/shard_map/prepare/pallas_call | solution.py:65
  19.0 2.4 %collective-permute-done.3.refs_4_ = bf16[128,128]{1,0:T(8,128)(2,1)S(1)} collective-permute-done((bf16[128,128]{1,0:T(8,128)(2,1)S(1)}, bf16[128,128]{1,0:T(8,128)(2,1)S(1)}, u32[]{:S(2)}, u32[]{:S(2)}) %collective-permute-start.3) | collective-permute-done | bytes 32800 | tf_op jit(solution)/shard_map/ppermute | solution.py:356
  21.4 2.9 %collective-permute-done.5.refs_6_ = bf16[128,128]{1,0:T(8,128)(2,1)S(1)} collective-permute-done((bf16[128,128]{1,0:T(8,128)(2,1)S(1)}, bf16[128,128]{1,0:T(8,128)(2,1)S(1)}, u32[]{:S(2)}, u32[]{:S(2)}) %collective-permute-start.5) | collective-permute-done | bytes 32800 | tf_op jit(solution)/shard_map/ppermute | solution.py:356
  24.9 0.6 tri.1
  25.5 8.6 %all_to_all.20.refs_0_ = bf16[8,128,128]{2,1,0:T(8,128)(2,1)S(1)} all-to-all(bf16[8,128,128]{2,1,0:T(8,128)(2,1)S(1)} %get-tuple-element.40), channel_id=1, replica_groups={{0,1,2,3,4,5,6,7},{8,9,10,11,12,13,14,15},{16,17,18,19,20,21,22,23},{24..., dimensions={0} | all-to-all | bytes 524288 | tf_op jit(solution)/shard_map/all_to_all | solution.py:348
  34.4 8.6 %all_to_all.21.refs_0_ = bf16[8,128,128]{2,1,0:T(8,128)(2,1)S(1)} all-to-all(bf16[8,128,128]{2,1,0:T(8,128)(2,1)S(1)} %middle.1), channel_id=1, replica_groups={{0,1,2,3,4,5,6,7},{8,9,10,11,12,13,14,15},{16,17,18,19,20,21,22,23},{24..., dimensions={0} | all-to-all | bytes 524288 | tf_op jit(solution)/shard_map/all_to_all | solution.py:348
  43.0 1.5 %d_right.1 = (bf16[16,128,128]{2,1,0:T(8,128)(2,1)}, bf16[16,64,128]{2,1,0:T(8,128)(2,1)S(1)}) custom-call(bf16[8,128,128]{2,1,0:T(8,128)(2,1)S(1)} %all_to_all.21.refs_0_, bf16[16,64,128]{2,1,0:T(8,128)(2,1)S(1)} %sort_left.1.refs_1_), custom_call_target="tpu_custom_call" | custom-call | flops 33554432 | bytes 1310720 | tf_op jit(solution)/shard_map/d_right/pallas_call | solution.py:65
  44.6 5.1 %all-to-all-start.3 = ((bf16[16,128,128]{2,1,0:T(8,128)(2,1)}), bf16[16,128,128]{2,1,0:T(8,128)(2,1)S(1)}, u32[]{:S(2)}, u32[]{:S(2)}) async-start(bf16[16,128,128]{2,1,0:T(8,128)(2,1)} %get-tuple-element.41), calls=%async_computation.3 | async-start | bytes 1048576 | tf_op jit(solution)/shard_map/all_to_all | solution.py:342
  50.5 1.7 %collective-permute-start.8 = (bf16[128,128]{1,0:T(8,128)(2,1)S(1)}, bf16[128,128]{1,0:T(8,128)(2,1)S(1)}, u32[]{:S(2)}, u32[]{:S(2)}) collective-permute-start(bf16[128,128]{1,0:T(8,128)(2,1)S(1)} %get-tuple-element.46), channel_id=1, source_target_pairs={{0,2},{1,3},{2,0},{3,1},{4,6},{5,7},{6,4},{7,5},{8,10},{9,11},{10,... | collective-permute-start | bytes 98312 | tf_op jit(solution)/shard_map/ppermute | solution.py:356
  52.2 1.7 %collective-permute-start.10 = (bf16[128,128]{1,0:T(8,128)(2,1)S(1)}, bf16[128,128]{1,0:T(8,128)(2,1)S(1)}, u32[]{:S(2)}, u32[]{:S(2)}) collective-permute-start(bf16[128,128]{1,0:T(8,128)(2,1)S(1)} %get-tuple-element.48), channel_id=1, source_target_pairs={{0,4},{1,5},{2,6},{3,7},{4,0},{5,1},{6,2},{7,3},{8,12},{9,13},{10,... | collective-permute-start | bytes 98312 | tf_op jit(solution)/shard_map/ppermute | solution.py:356
  54.0 2.6 %collective-permute-start.12 = (bf16[128,128]{1,0:T(8,128)(2,1)S(1)}, bf16[128,128]{1,0:T(8,128)(2,1)S(1)}, u32[]{:S(2)}, u32[]{:S(2)}) collective-permute-start(bf16[128,128]{1,0:T(8,128)(2,1)S(1)} %get-tuple-element.50), channel_id=1, source_target_pairs={{0,6},{1,7},{2,4},{3,5},{4,2},{5,3},{6,0},{7,1},{8,14},{9,15},{10,... | collective-permute-start | bytes 98312 | tf_op jit(solution)/shard_map/ppermute | solution.py:356
  56.9 0.6 copy-done.12
  57.6 1.2 %slopes.1 = (bf16[8,512,128]{2,1,0:T(8,128)(2,1)S(1)}, bf16[8,128,128]{2,1,0:T(8,128)(2,1)S(1)}, bf16[8,128,128]{2,1,0:T(8,128)(2,1)S(1)}, f32[8,128]{1,0:T(8,128)S(1)}) custom-call(bf16[8,128,128]{2,1,0:T(8,128)(2,1)S(1)} %all_to_all.20.refs_0_, f32[8,128,128]{2,1,0:T(8,128)S(1)} %get-tuple-element.52.refs_1_, bf16[8,128,128]{2,1,0:T(8,128)(2,1)S(1)} %copy-done.1, ...), custom_call_target="tpu_custom_call" | custom-call | flops 201326592 | bytes 2791936 | tf_op jit(solution)/shard_map/slopes/pallas_call | solution.py:65
  58.8 2.3 %collective-permute-done.10.refs_4_ = bf16[128,128]{1,0:T(8,128)(2,1)S(1)} collective-permute-done((bf16[128,128]{1,0:T(8,128)(2,1)S(1)}, bf16[128,128]{1,0:T(8,128)(2,1)S(1)}, u32[]{:S(2)}, u32[]{:S(2)}) %collective-permute-start.10) | collective-permute-done | bytes 32800 | tf_op jit(solution)/shard_map/ppermute | solution.py:356
  61.1 2.9 %collective-permute-done.12.refs_6_ = bf16[128,128]{1,0:T(8,128)(2,1)S(1)} collective-permute-done((bf16[128,128]{1,0:T(8,128)(2,1)S(1)}, bf16[128,128]{1,0:T(8,128)(2,1)S(1)}, u32[]{:S(2)}, u32[]{:S(2)}) %collective-permute-start.12) | collective-permute-done | bytes 32800 | tf_op jit(solution)/shard_map/ppermute | solution.py:356
  64.0 0.5 all-to-all-done.3.refs_0_
  64.8 1.6 %finish.1 = bf16[8,128,128]{2,1,0:T(8,128)(2,1)} custom-call(bf16[16,128,128]{2,1,0:T(8,128)(2,1)S(1)} %all-to-all-done.3.refs_0_, bf16[8,128,128]{2,1,0:T(8,128)(2,1)S(1)} %sort_d_left.1.refs_1_, bf16[8,512,128]{2,1,0:T(8,128)(2,1)S(1)} %get-tuple-element.53.refs_2_, bf16[8,128,128]{2,1,0:T(8,128)(2,1)S(1)} %get-tuple-element.54.refs_3_, ...), custom_call_target="tpu_custom_call" | custom-call | flops 134217728 | bytes 2789888 | tf_op jit(solution)/shard_map/finish/pallas_call | solution.py:65
  (49 shorter events, 3.0 us)
Async XLA Ops:
  2.5 7.6 %copy-start = (bf16[16,128,128]{2,1,0:T(8,128)(2,1)S(1)}, bf16[16,128,128]{2,1,0:T(8,128)(2,1)}, u32[]{:S(2)}) copy-start(bf16[16,128,128]{2,1,0:T(8,128)(2,1)} %project_right.1.refs_5_) | copy-start | bytes 1572868
  2.5 7.6 %copy-start.1 = (bf16[8,128,128]{2,1,0:T(8,128)(2,1)S(1)}, bf16[8,128,128]{2,1,0:T(8,128)(2,1)}, u32[]{:S(2)}) copy-start(bf16[8,128,128]{2,1,0:T(8,128)(2,1)} %refs_2_.1) | copy-start | bytes 786436
  2.5 7.6 %copy-start.2 = (bf16[128,512]{1,0:T(8,128)(2,1)S(1)}, bf16[128,512]{1,0:T(8,128)(2,1)}, u32[]{:S(2)}) copy-start(bf16[128,512]{1,0:T(8,128)(2,1)} %refs_7_.1) | copy-start | bytes 393220
  2.5 7.6 %copy-start.8 = (f32[128]{0:T(128)S(1)}, f32[128]{0:T(128)}, u32[]{:S(2)}) copy-start(f32[128]{0:T(128)} %param.13) | copy-start | bytes 1540
  2.5 7.6 %copy-start.9 = (f32[128]{0:T(128)S(1)}, f32[128]{0:T(128)}, u32[]{:S(2)}) copy-start(f32[128]{0:T(128)} %param.14) | copy-start | bytes 1540
  2.5 7.6 %copy-start.10 = (s32[128]{0:T(128)S(1)}, s32[128]{0:T(128)}, u32[]{:S(2)}) copy-start(s32[128]{0:T(128)} %param.12) | copy-start | bytes 1540
  2.5 22.4 %all-to-all-start = ((bf16[16,128,128]{2,1,0:T(8,128)(2,1)}), bf16[16,128,128]{2,1,0:T(8,128)(2,1)S(1)}, u32[]{:S(2)}, u32[]{:S(2)}) async-start(bf16[16,128,128]{2,1,0:T(8,128)(2,1)} %project_right.1.refs_5_), calls=%async_computation | async-start | bytes 1048576 | tf_op jit(solution)/shard_map/all_to_all | solution.py:342
  10.1 7.5 %copy-start.3 = (bf16[8,128,128]{2,1,0:T(8,128)(2,1)S(1)}, bf16[8,128,128]{2,1,0:T(8,128)(2,1)}, u32[]{:S(2)}) copy-start(bf16[8,128,128]{2,1,0:T(8,128)(2,1)} %refs_1_.1) | copy-start | bytes 786436
  10.1 7.4 %copy-start.4 = (bf16[128,128]{1,0:T(8,128)(2,1)S(1)}, bf16[128,128]{1,0:T(8,128)(2,1)}, u32[]{:S(2)}) copy-start(bf16[128,128]{1,0:T(8,128)(2,1)} %refs_8_.1) | copy-start | bytes 98308
  11.0 4.0 %collective-permute-start = (bf16[128,128]{1,0:T(8,128)(2,1)S(1)}, bf16[128,128]{1,0:T(8,128)(2,1)S(1)}, u32[]{:S(2)}, u32[]{:S(2)}) collective-permute-start(bf16[128,128]{1,0:T(8,128)(2,1)S(1)} %get-tuple-element.32), channel_id=1, source_target_pairs={{0,1},{1,0},{2,3},{3,2},{4,5},{5,4},{6,7},{7,6},{8,9},{9,8},{10,11... | collective-permute-start | bytes 98312 | tf_op jit(solution)/shard_map/ppermute | solution.py:356
  11.4 6.1 %collective-permute-start.1 = (bf16[128,128]{1,0:T(8,128)(2,1)S(1)}, bf16[128,128]{1,0:T(8,128)(2,1)S(1)}, u32[]{:S(2)}, u32[]{:S(2)}) collective-permute-start(bf16[128,128]{1,0:T(8,128)(2,1)S(1)} %get-tuple-element.33), channel_id=1, source_target_pairs={{0,2},{1,3},{2,0},{3,1},{4,6},{5,7},{6,4},{7,5},{8,10},{9,11},{10,... | collective-permute-start | bytes 98312 | tf_op jit(solution)/shard_map/ppermute | solution.py:356
  13.1 5.9 %collective-permute-start.2 = (bf16[128,128]{1,0:T(8,128)(2,1)S(1)}, bf16[128,128]{1,0:T(8,128)(2,1)S(1)}, u32[]{:S(2)}, u32[]{:S(2)}) collective-permute-start(bf16[128,128]{1,0:T(8,128)(2,1)S(1)} %get-tuple-element.34), channel_id=1, source_target_pairs={{0,3},{1,2},{2,1},{3,0},{4,7},{5,6},{6,5},{7,4},{8,11},{9,10},{10,... | collective-permute-start | bytes 98312 | tf_op jit(solution)/shard_map/ppermute | solution.py:356
  13.1 8.3 %collective-permute-start.3 = (bf16[128,128]{1,0:T(8,128)(2,1)S(1)}, bf16[128,128]{1,0:T(8,128)(2,1)S(1)}, u32[]{:S(2)}, u32[]{:S(2)}) collective-permute-start(bf16[128,128]{1,0:T(8,128)(2,1)S(1)} %get-tuple-element.35), channel_id=1, source_target_pairs={{0,4},{1,5},{2,6},{3,7},{4,0},{5,1},{6,2},{7,3},{8,12},{9,13},{10,... | collective-permute-start | bytes 98312 | tf_op jit(solution)/shard_map/ppermute | solution.py:356
  14.8 6.6 %collective-permute-start.4 = (bf16[128,128]{1,0:T(8,128)(2,1)S(1)}, bf16[128,128]{1,0:T(8,128)(2,1)S(1)}, u32[]{:S(2)}, u32[]{:S(2)}) collective-permute-start(bf16[128,128]{1,0:T(8,128)(2,1)S(1)} %get-tuple-element.36), channel_id=1, source_target_pairs={{0,5},{1,4},{2,7},{3,6},{4,1},{5,0},{6,3},{7,2},{8,13},{9,12},{10,... | collective-permute-start | bytes 98312 | tf_op jit(solution)/shard_map/ppermute | solution.py:356
  14.9 9.4 %collective-permute-start.5 = (bf16[128,128]{1,0:T(8,128)(2,1)S(1)}, bf16[128,128]{1,0:T(8,128)(2,1)S(1)}, u32[]{:S(2)}, u32[]{:S(2)}) collective-permute-start(bf16[128,128]{1,0:T(8,128)(2,1)S(1)} %get-tuple-element.37), channel_id=1, source_target_pairs={{0,6},{1,7},{2,4},{3,5},{4,2},{5,3},{6,0},{7,1},{8,14},{9,15},{10,... | collective-permute-start | bytes 98312 | tf_op jit(solution)/shard_map/ppermute | solution.py:356
  17.5 6.8 %collective-permute-start.6 = (bf16[128,128]{1,0:T(8,128)(2,1)S(1)}, bf16[128,128]{1,0:T(8,128)(2,1)S(1)}, u32[]{:S(2)}, u32[]{:S(2)}) collective-permute-start(bf16[128,128]{1,0:T(8,128)(2,1)S(1)} %get-tuple-element.38), channel_id=1, source_target_pairs={{0,7},{1,6},{2,5},{3,4},{4,3},{5,2},{6,1},{7,0},{8,15},{9,14},{10,... | collective-permute-start | bytes 98312 | tf_op jit(solution)/shard_map/ppermute | solution.py:356
  44.6 20.0 %all-to-all-start.3 = ((bf16[16,128,128]{2,1,0:T(8,128)(2,1)}), bf16[16,128,128]{2,1,0:T(8,128)(2,1)S(1)}, u32[]{:S(2)}, u32[]{:S(2)}) async-start(bf16[16,128,128]{2,1,0:T(8,128)(2,1)} %get-tuple-element.41), calls=%async_computation.3 | async-start | bytes 1048576 | tf_op jit(solution)/shard_map/all_to_all | solution.py:342
  50.1 4.0 %collective-permute-start.7 = (bf16[128,128]{1,0:T(8,128)(2,1)S(1)}, bf16[128,128]{1,0:T(8,128)(2,1)S(1)}, u32[]{:S(2)}, u32[]{:S(2)}) collective-permute-start(bf16[128,128]{1,0:T(8,128)(2,1)S(1)} %get-tuple-element.45), channel_id=1, source_target_pairs={{0,1},{1,0},{2,3},{3,2},{4,5},{5,4},{6,7},{7,6},{8,9},{9,8},{10,11... | collective-permute-start | bytes 98312 | tf_op jit(solution)/shard_map/ppermute | solution.py:356
  50.5 6.3 %collective-permute-start.8 = (bf16[128,128]{1,0:T(8,128)(2,1)S(1)}, bf16[128,128]{1,0:T(8,128)(2,1)S(1)}, u32[]{:S(2)}, u32[]{:S(2)}) collective-permute-start(bf16[128,128]{1,0:T(8,128)(2,1)S(1)} %get-tuple-element.46), channel_id=1, source_target_pairs={{0,2},{1,3},{2,0},{3,1},{4,6},{5,7},{6,4},{7,5},{8,10},{9,11},{10,... | collective-permute-start | bytes 98312 | tf_op jit(solution)/shard_map/ppermute | solution.py:356
  52.2 6.6 %collective-permute-start.9 = (bf16[128,128]{1,0:T(8,128)(2,1)S(1)}, bf16[128,128]{1,0:T(8,128)(2,1)S(1)}, u32[]{:S(2)}, u32[]{:S(2)}) collective-permute-start(bf16[128,128]{1,0:T(8,128)(2,1)S(1)} %get-tuple-element.47), channel_id=1, source_target_pairs={{0,3},{1,2},{2,1},{3,0},{4,7},{5,6},{6,5},{7,4},{8,11},{9,10},{10,... | collective-permute-start | bytes 98312 | tf_op jit(solution)/shard_map/ppermute | solution.py:356
  52.2 8.9 %collective-permute-start.10 = (bf16[128,128]{1,0:T(8,128)(2,1)S(1)}, bf16[128,128]{1,0:T(8,128)(2,1)S(1)}, u32[]{:S(2)}, u32[]{:S(2)}) collective-permute-start(bf16[128,128]{1,0:T(8,128)(2,1)S(1)} %get-tuple-element.48), channel_id=1, source_target_pairs={{0,4},{1,5},{2,6},{3,7},{4,0},{5,1},{6,2},{7,3},{8,12},{9,13},{10,... | collective-permute-start | bytes 98312 | tf_op jit(solution)/shard_map/ppermute | solution.py:356
  53.9 7.2 %collective-permute-start.11 = (bf16[128,128]{1,0:T(8,128)(2,1)S(1)}, bf16[128,128]{1,0:T(8,128)(2,1)S(1)}, u32[]{:S(2)}, u32[]{:S(2)}) collective-permute-start(bf16[128,128]{1,0:T(8,128)(2,1)S(1)} %get-tuple-element.49), channel_id=1, source_target_pairs={{0,5},{1,4},{2,7},{3,6},{4,1},{5,0},{6,3},{7,2},{8,13},{9,12},{10,... | collective-permute-start | bytes 98312 | tf_op jit(solution)/shard_map/ppermute | solution.py:356
  54.0 10.0 %collective-permute-start.12 = (bf16[128,128]{1,0:T(8,128)(2,1)S(1)}, bf16[128,128]{1,0:T(8,128)(2,1)S(1)}, u32[]{:S(2)}, u32[]{:S(2)}) collective-permute-start(bf16[128,128]{1,0:T(8,128)(2,1)S(1)} %get-tuple-element.50), channel_id=1, source_target_pairs={{0,6},{1,7},{2,4},{3,5},{4,2},{5,3},{6,0},{7,1},{8,14},{9,15},{10,... | collective-permute-start | bytes 98312 | tf_op jit(solution)/shard_map/ppermute | solution.py:356
  56.9 7.1 %collective-permute-start.13 = (bf16[128,128]{1,0:T(8,128)(2,1)S(1)}, bf16[128,128]{1,0:T(8,128)(2,1)S(1)}, u32[]{:S(2)}, u32[]{:S(2)}) collective-permute-start(bf16[128,128]{1,0:T(8,128)(2,1)S(1)} %get-tuple-element.51), channel_id=1, source_target_pairs={{0,7},{1,6},{2,5},{3,4},{4,3},{5,2},{6,1},{7,0},{8,15},{9,14},{10,... | collective-permute-start | bytes 98312 | tf_op jit(solution)/shard_map/ppermute | solution.py:356
  (6 other events, 17.4 us)

commit v9 on v7

--- a/solution.py
+++ b/solution.py
@@ -227,6 +227,7 @@
     gain,
     bias,
     w_proj,
+    w_gate,
     out_gain,
     out_bias,
     w_out,
@@ -234,12 +235,16 @@
     d_gate_pre,
     normed_in,
     inv_in,
+    in_gain,
+    weights,
 ):
     rows = pair.shape[0]
     hidden = w_out.shape[0]
     w_flip = transposed(w_proj[...])
     out_flip = transposed(w_out[...])
     gain_col, bias_col = column(gain[...]), column(bias[...])
+    in_gain[...] = gain_col
+    weights[...] = jnp.concatenate([w_proj[...], w_gate[...]], axis=1)
     out_gain_col, out_bias_col = column(out_gain[...]), column(out_bias[...])
     masks = cell_masks(mask, rows)
     for row in range(rows):
@@ -260,17 +265,18 @@
             slopes[row, base + hidden : base + 2 * hidden, :] = masked.astype(slopes.dtype)
 
 
-def finish_kernel(
-    d_right_panel, slopes, d_gate_pre, normed_in, inv_in, gain, w_proj, w_gate, *refs
-):
-    *pieces, grad, d_left_panel = refs
+def sort_d_left_kernel(*refs):
+    *pieces, d_left_panel = refs
     for step, piece in enumerate(pieces):
         d_left_panel[partner(step, len(pieces))] = piece[...]
+
+
+def finish_kernel(
+    d_right_panel, d_left_panel, slopes, d_gate_pre, normed_in, inv_in, gain_col, weights, grad
+):
     rows = grad.shape[0]
     count, depth, width = d_left_panel.shape
     hidden = count * depth // rows
-    gain_col = column(gain[...])
-    weights = jnp.concatenate([w_proj[...], w_gate[...]], axis=1)
     for row in range(rows):
         d_right = cell_row(d_right_panel, row, rows)
         d_right = sum(d_right[n : n + hidden] for n in range(0, d_right.shape[0], hidden))
@@ -280,7 +286,7 @@
                 slope = slopes[row, base : base + hidden, :].astype(F32)
                 parts.append((d_value * slope).astype(BF16))
         parts.append(d_gate_pre[row])
-        d_in = dot(weights, jnp.concatenate(parts, axis=0), 1, 0) * gain_col
+        d_in = dot(weights[...], jnp.concatenate(parts, axis=0), 1, 0) * gain_col[...]
         normed = normed_in[row].astype(F32)
         mean_grad = jnp.mean(d_in, axis=0, keepdims=True)
         mean_cross = jnp.mean(d_in * normed, axis=0, keepdims=True)
@@ -410,7 +416,8 @@
         flops=2 * block * left_rows * width * right_rows,
     )
     d_pieces = swap_pieces(d_pieces)
-    slopes, d_gate_pre, normed_in, inv_in = call(
+    (d_left_panel,) = call(sort_d_left_kernel, "sort_d_left", [panel], d_pieces)
+    slopes, d_gate_pre, normed_in, inv_in, gain_col, weights = call(
         slopes_kernel,
         "slopes",
         [
@@ -418,6 +425,8 @@
             shape((rows, channels, width), BF16),
             shape((rows, channels, width), BF16),
             shape((rows, width), F32),
+            shape((channels, channels), F32),
+            shape((channels, 4 * hidden + channels), BF16),
         ],
         [
             products,
@@ -427,20 +436,28 @@
             gain,
             bias,
             w_proj,
+            w_gate,
             out_gain,
             out_bias,
             w_out,
         ],
-        fetched=range(2, 10),
+        fetched=range(2, 11),
         flops=2 * cells * channels * 6 * hidden,
     )
     (grad,) = call(
         finish_kernel,
         "finish",
         [shape(pair.shape, BF16)],
-        [d_right_panel, slopes, d_gate_pre, normed_in, inv_in, gain, w_proj, w_gate, *d_pieces],
-        fetched=(5, 6, 7),
-        scratch=[left_panel],
+        [
+            d_right_panel,
+            d_left_panel,
+            slopes,
+            d_gate_pre,
+            normed_in,
+            inv_in,
+            gain_col,
+            weights,
+        ],
         flops=2 * cells * channels * 4 * hidden,
     )
     return grad

time: 68.7 us -> 66.9 us (0.974)
  local copies, waits for them, and re-layouts: 4.08 us -> 2.98 us
  waiting for transfers between devices: 11.1 us -> 10.3 us
    ppermute x14, waiting for transfers between devices: 10.8 us -> 9.43 us  [swap_pieces(): lax.ppermute(pieces[step], 'row', [(d, d ^ step) for d in devices])]
    unnamed x36, local copies, waits for them, and re-layouts: 4.08 us -> 2.98 us
    pallas_call x10 -> x11, Pallas kernels: 9.75 us -> 9.65 us  [call(): pl.pallas_call(body, name=name, out_shape=outs, in_specs=[pl.BlockSpec(me...]
  transfers between devices with their start and end apart: 16 -> 16, of which waited for: 6 -> 7; matrix products, arithmetic and copies ran while one was open for 0% -> 0% of each run, Pallas kernels for 5% -> 5%
where the time goes in v9:
time: 66.9 us; the launch traced here: 66.1 us
  starting transfers between devices  25.8 us (39%)
  blocking collectives  17.2 us (26%)
  waiting for transfers between devices  10.3 us (15%)
  Pallas kernels  9.65 us (14%)
  local copies, waits for them, and re-layouts  2.98 us (4%)
    all_to_all x2, blocking collectives, swap_half(): lax.all_to_all(values, 'row', split_axis=0, concat_axis=0, tiled=True, ax...  17.2 us
    ppermute x14, starting transfers between devices, swap_pieces(): lax.ppermute(pieces[step], 'row', [(d, d ^ step) for d in devices])  13.1 us
    all_to_all x2, starting transfers between devices, swap(): lax.all_to_all(values, 'row', split_axis=0, concat_axis=0, tiled=True)  12.6 us
    pallas_call x11, Pallas kernels, call(): pl.pallas_call(body, name=name, out_shape=outs, in_specs=[pl.BlockSpec(me...  9.65 us
    ppermute x14, waiting for transfers between devices, swap_pieces(): lax.ppermute(pieces[step], 'row', [(d, d ^ step) for d in devices])  9.43 us
    unnamed x36, local copies, waits for them, and re-layouts  2.98 us
  transfers between devices with their start and end apart: 16, of which 7 were waited for; matrix products, arithmetic and copies ran while one was open for 0% of the time, Pallas kernels for 5%

profile of v9, /device:TPU:0, one launch (start us, length us, event | category | flops | bytes accessed | tf_op | source)
XLA Modules:
  0.0 66.1 jit_solution(10494666645496877382)
XLA Ops:
  0.0 2.4 %project_right.1.refs_5_ = bf16[16,128,128]{2,1,0:T(8,128)(2,1)} custom-call(bf16[8,128,128]{2,1,0:T(8,128)(2,1)} %refs_2_.1, s32[1,128]{1,0:T(1,128)} %bitcast.13, f32[1,128]{1,0:T(1,128)} %bitcast.5, f32[1,128]{1,0:T(1,128)} %bitcast.9, bf16[128,512]{1,0:T(8,128)(2,1)} %refs_6_.3), custom_call_target="tpu_custom_call" | custom-call | flops 67108864 | bytes 919040 | tf_op jit(solution)/shard_map/project_right/pallas_call | solution.py:65
  2.5 7.5 %all-to-all-start = ((bf16[16,128,128]{2,1,0:T(8,128)(2,1)}), bf16[16,128,128]{2,1,0:T(8,128)(2,1)S(1)}, u32[]{:S(2)}, u32[]{:S(2)}) async-start(bf16[16,128,128]{2,1,0:T(8,128)(2,1)} %project_right.1.refs_5_), calls=%async_computation | async-start | bytes 1048576 | tf_op jit(solution)/shard_map/all_to_all | solution.py:298
  10.1 0.8 %project_left.1 = (bf16[128,128]{1,0:T(8,128)(2,1)S(1)}, bf16[128,128]{1,0:T(8,128)(2,1)S(1)}, bf16[128,128]{1,0:T(8,128)(2,1)S(1)}, bf16[128,128]{1,0:T(8,128)(...) custom-call(bf16[8,128,128]{2,1,0:T(8,128)(2,1)S(1)} %copy-done.1, ...), custom_call_target="tpu_custom_call" | custom-call | flops 67108864 | bytes 1181184 | tf_op jit(solution)/shard_map/project_left/pallas_call | solution.py:65
  11.3 1.7 %collective-permute-start.1 = (bf16[128,128]{1,0:T(8,128)(2,1)S(1)}, bf16[128,128]{1,0:T(8,128)(2,1)S(1)}, u32[]{:S(2)}, u32[]{:S(2)}) collective-permute-start(bf16[128,128]{1,0:T(8,128)(2,1)S(1)} %get-tuple-element.35), channel_id=1, source_target_pairs={{0,2},{1,3},{2,0},{3,1},{4,6},{5,7},{6,4},{7,5},{8,10},{9,11},{10,... | collective-permute-start | bytes 98312 | tf_op jit(solution)/shard_map/ppermute | solution.py:312
  13.0 1.7 %collective-permute-start.3 = (bf16[128,128]{1,0:T(8,128)(2,1)S(1)}, bf16[128,128]{1,0:T(8,128)(2,1)S(1)}, u32[]{:S(2)}, u32[]{:S(2)}) collective-permute-start(bf16[128,128]{1,0:T(8,128)(2,1)S(1)} %get-tuple-element.37), channel_id=1, source_target_pairs={{0,4},{1,5},{2,6},{3,7},{4,0},{5,1},{6,2},{7,3},{8,12},{9,13},{10,... | collective-permute-start | bytes 98312 | tf_op jit(solution)/shard_map/ppermute | solution.py:312
  14.8 2.6 %collective-permute-start.5 = (bf16[128,128]{1,0:T(8,128)(2,1)S(1)}, bf16[128,128]{1,0:T(8,128)(2,1)S(1)}, u32[]{:S(2)}, u32[]{:S(2)}) collective-permute-start(bf16[128,128]{1,0:T(8,128)(2,1)S(1)} %get-tuple-element.39), channel_id=1, source_target_pairs={{0,6},{1,7},{2,4},{3,5},{4,2},{5,3},{6,0},{7,1},{8,14},{9,15},{10,... | collective-permute-start | bytes 98312 | tf_op jit(solution)/shard_map/ppermute | solution.py:312
  18.1 0.8 %prepare.1 = (f32[8,128,128]{2,1,0:T(8,128)S(1)}, f32[8,128,128]{2,1,0:T(8,128)S(1)}) custom-call(bf16[8,128,128]{2,1,0:T(8,128)(2,1)S(1)} %copy-done.1, bf16[8,128,128]{2,1,0:T(8,128)(2,1)S(1)} %copy-done.3, f32[1,128]{1,0:T(1,128)S(1)} %bitcast.7, f32[1,128]{1,0:T(1,128)S(1)} %bitcast.11, bf16[128,128]{1,0:T(8,128)(2,1)S(1)} %copy-done.6, ...), custom_call_target="tpu_custom_call" | custom-call | flops 67108864 | bytes 1639936 | tf_op jit(solution)/shard_map/prepare/pallas_call | solution.py:65
  18.9 2.4 %collective-permute-done.3.refs_4_ = bf16[128,128]{1,0:T(8,128)(2,1)S(1)} collective-permute-done((bf16[128,128]{1,0:T(8,128)(2,1)S(1)}, bf16[128,128]{1,0:T(8,128)(2,1)S(1)}, u32[]{:S(2)}, u32[]{:S(2)}) %collective-permute-start.3) | collective-permute-done | bytes 32800 | tf_op jit(solution)/shard_map/ppermute | solution.py:312
  21.3 2.9 %collective-permute-done.5.refs_6_ = bf16[128,128]{1,0:T(8,128)(2,1)S(1)} collective-permute-done((bf16[128,128]{1,0:T(8,128)(2,1)S(1)}, bf16[128,128]{1,0:T(8,128)(2,1)S(1)}, u32[]{:S(2)}, u32[]{:S(2)}) %collective-permute-start.5) | collective-permute-done | bytes 32800 | tf_op jit(solution)/shard_map/ppermute | solution.py:312
  24.8 0.6 tri.1
  25.4 8.6 %all_to_all.20.refs_0_ = bf16[8,128,128]{2,1,0:T(8,128)(2,1)S(1)} all-to-all(bf16[8,128,128]{2,1,0:T(8,128)(2,1)S(1)} %get-tuple-element.42), channel_id=1, replica_groups={{0,1,2,3,4,5,6,7},{8,9,10,11,12,13,14,15},{16,17,18,19,20,21,22,23},{24..., dimensions={0} | all-to-all | bytes 524288 | tf_op jit(solution)/shard_map/all_to_all | solution.py:304
  34.3 8.6 %all_to_all.21.refs_0_ = bf16[8,128,128]{2,1,0:T(8,128)(2,1)S(1)} all-to-all(bf16[8,128,128]{2,1,0:T(8,128)(2,1)S(1)} %middle.1), channel_id=1, replica_groups={{0,1,2,3,4,5,6,7},{8,9,10,11,12,13,14,15},{16,17,18,19,20,21,22,23},{24..., dimensions={0} | all-to-all | bytes 524288 | tf_op jit(solution)/shard_map/all_to_all | solution.py:304
  42.9 1.5 %d_right.1 = (bf16[16,128,128]{2,1,0:T(8,128)(2,1)}, bf16[16,64,128]{2,1,0:T(8,128)(2,1)S(1)}) custom-call(bf16[8,128,128]{2,1,0:T(8,128)(2,1)S(1)} %all_to_all.21.refs_0_, bf16[16,64,128]{2,1,0:T(8,128)(2,1)S(1)} %sort_left.1.refs_1_), custom_call_target="tpu_custom_call" | custom-call | flops 33554432 | bytes 1310720 | tf_op jit(solution)/shard_map/d_right/pallas_call | solution.py:65
  44.4 5.1 %all-to-all-start.3 = ((bf16[16,128,128]{2,1,0:T(8,128)(2,1)}), bf16[16,128,128]{2,1,0:T(8,128)(2,1)S(1)}, u32[]{:S(2)}, u32[]{:S(2)}) async-start(bf16[16,128,128]{2,1,0:T(8,128)(2,1)} %get-tuple-element.43), calls=%async_computation.3 | async-start | bytes 1048576 | tf_op jit(solution)/shard_map/all_to_all | solution.py:298
  50.3 1.7 %collective-permute-start.8 = (bf16[128,128]{1,0:T(8,128)(2,1)S(1)}, bf16[128,128]{1,0:T(8,128)(2,1)S(1)}, u32[]{:S(2)}, u32[]{:S(2)}) collective-permute-start(bf16[128,128]{1,0:T(8,128)(2,1)S(1)} %get-tuple-element.48), channel_id=1, source_target_pairs={{0,2},{1,3},{2,0},{3,1},{4,6},{5,7},{6,4},{7,5},{8,10},{9,11},{10,... | collective-permute-start | bytes 98312 | tf_op jit(solution)/shard_map/ppermute | solution.py:312
  52.0 1.7 %collective-permute-start.10 = (bf16[128,128]{1,0:T(8,128)(2,1)S(1)}, bf16[128,128]{1,0:T(8,128)(2,1)S(1)}, u32[]{:S(2)}, u32[]{:S(2)}) collective-permute-start(bf16[128,128]{1,0:T(8,128)(2,1)S(1)} %get-tuple-element.50), channel_id=1, source_target_pairs={{0,4},{1,5},{2,6},{3,7},{4,0},{5,1},{6,2},{7,3},{8,12},{9,13},{10,... | collective-permute-start | bytes 98312 | tf_op jit(solution)/shard_map/ppermute | solution.py:312
  53.8 2.6 %collective-permute-start.12 = (bf16[128,128]{1,0:T(8,128)(2,1)S(1)}, bf16[128,128]{1,0:T(8,128)(2,1)S(1)}, u32[]{:S(2)}, u32[]{:S(2)}) collective-permute-start(bf16[128,128]{1,0:T(8,128)(2,1)S(1)} %get-tuple-element.52), channel_id=1, source_target_pairs={{0,6},{1,7},{2,4},{3,5},{4,2},{5,3},{6,0},{7,1},{8,14},{9,15},{10,... | collective-permute-start | bytes 98312 | tf_op jit(solution)/shard_map/ppermute | solution.py:312
  56.7 0.6 copy-done.16
  57.3 1.3 %slopes.1 = (bf16[8,512,128]{2,1,0:T(8,128)(2,1)S(1)}, bf16[8,128,128]{2,1,0:T(8,128)(2,1)S(1)}, bf16[8,128,128]{2,1,0:T(8,128)(2,1)S(1)}, f32[8,128]{1,0:T(8,12...) custom-call(bf16[8,128,128]{2,1,0:T(8,128)(2,1)S(1)} %all_to_all.20.refs_0_, ...), custom_call_target="tpu_custom_call" | custom-call | flops 201326592 | bytes 3054080 | tf_op jit(solution)/shard_map/slopes/pallas_call | solution.py:65
  58.7 0.7 copy-done.4
  59.3 0.6 copy-done.10
  60.0 0.9 %collective-permute-done.10.refs_4_ = bf16[128,128]{1,0:T(8,128)(2,1)S(1)} collective-permute-done((bf16[128,128]{1,0:T(8,128)(2,1)S(1)}, bf16[128,128]{1,0:T(8,128)(2,1)S(1)}, u32[]{:S(2)}, u32[]{:S(2)}) %collective-permute-start.10) | collective-permute-done | bytes 32800 | tf_op jit(solution)/shard_map/ppermute | solution.py:312
  60.9 2.9 %collective-permute-done.12.refs_6_ = bf16[128,128]{1,0:T(8,128)(2,1)S(1)} collective-permute-done((bf16[128,128]{1,0:T(8,128)(2,1)S(1)}, bf16[128,128]{1,0:T(8,128)(2,1)S(1)}, u32[]{:S(2)}, u32[]{:S(2)}) %collective-permute-start.12) | collective-permute-done | bytes 32800 | tf_op jit(solution)/shard_map/ppermute | solution.py:312
  64.7 1.4 %finish.1 = bf16[8,128,128]{2,1,0:T(8,128)(2,1)} custom-call(bf16[16,128,128]{2,1,0:T(8,128)(2,1)S(1)} %all-to-all-done.3.refs_0_, bf16[8,128,128]{2,1,0:T(8,128)(2,1)S(1)} %sort_d_left.1.refs_1_, bf16[8,512,128]{2,1,0:T(8,128)(2,1)S(1)} %get-tuple-element.55.refs_2_, bf16[8,128,128]{2,1,0:T(8,128)(2,1)S(1)} %get-tuple-element.56.refs_3_, ...), custom_call_target="tpu_custom_call" | custom-call | flops 134217728 | bytes 2854912 | tf_op jit(solution)/shard_map/finish/pallas_call | solution.py:65
  (57 shorter events, 4.3 us)
Async XLA Ops:
  2.4 7.6 %copy-start = (bf16[16,128,128]{2,1,0:T(8,128)(2,1)S(1)}, bf16[16,128,128]{2,1,0:T(8,128)(2,1)}, u32[]{:S(2)}) copy-start(bf16[16,128,128]{2,1,0:T(8,128)(2,1)} %project_right.1.refs_5_) | copy-start | bytes 1572868
  2.4 7.6 %copy-start.1 = (bf16[8,128,128]{2,1,0:T(8,128)(2,1)S(1)}, bf16[8,128,128]{2,1,0:T(8,128)(2,1)}, u32[]{:S(2)}) copy-start(bf16[8,128,128]{2,1,0:T(8,128)(2,1)} %refs_2_.1) | copy-start | bytes 786436
  2.4 7.6 %copy-start.2 = (bf16[128,512]{1,0:T(8,128)(2,1)S(1)}, bf16[128,512]{1,0:T(8,128)(2,1)}, u32[]{:S(2)}) copy-start(bf16[128,512]{1,0:T(8,128)(2,1)} %refs_6_.3) | copy-start | bytes 393220
  2.4 7.6 %copy-start.12 = (f32[128]{0:T(128)S(1)}, f32[128]{0:T(128)}, u32[]{:S(2)}) copy-start(f32[128]{0:T(128)} %param.13) | copy-start | bytes 1540
  2.4 7.6 %copy-start.13 = (f32[128]{0:T(128)S(1)}, f32[128]{0:T(128)}, u32[]{:S(2)}) copy-start(f32[128]{0:T(128)} %param.14) | copy-start | bytes 1540
  2.4 7.6 %copy-start.14 = (s32[128]{0:T(128)S(1)}, s32[128]{0:T(128)}, u32[]{:S(2)}) copy-start(s32[128]{0:T(128)} %param.12) | copy-start | bytes 1540
  2.5 22.3 %all-to-all-start = ((bf16[16,128,128]{2,1,0:T(8,128)(2,1)}), bf16[16,128,128]{2,1,0:T(8,128)(2,1)S(1)}, u32[]{:S(2)}, u32[]{:S(2)}) async-start(bf16[16,128,128]{2,1,0:T(8,128)(2,1)} %project_right.1.refs_5_), calls=%async_computation | async-start | bytes 1048576 | tf_op jit(solution)/shard_map/all_to_all | solution.py:298
  10.0 7.4 %copy-start.3 = (bf16[8,128,128]{2,1,0:T(8,128)(2,1)S(1)}, bf16[8,128,128]{2,1,0:T(8,128)(2,1)}, u32[]{:S(2)}) copy-start(bf16[8,128,128]{2,1,0:T(8,128)(2,1)} %refs_1_.1) | copy-start | bytes 786436
  10.0 7.4 %copy-start.6 = (bf16[128,128]{1,0:T(8,128)(2,1)S(1)}, bf16[128,128]{1,0:T(8,128)(2,1)}, u32[]{:S(2)}) copy-start(bf16[128,128]{1,0:T(8,128)(2,1)} %refs_7_.1) | copy-start | bytes 98308
  10.9 4.0 %collective-permute-start = (bf16[128,128]{1,0:T(8,128)(2,1)S(1)}, bf16[128,128]{1,0:T(8,128)(2,1)S(1)}, u32[]{:S(2)}, u32[]{:S(2)}) collective-permute-start(bf16[128,128]{1,0:T(8,128)(2,1)S(1)} %get-tuple-element.34), channel_id=1, source_target_pairs={{0,1},{1,0},{2,3},{3,2},{4,5},{5,4},{6,7},{7,6},{8,9},{9,8},{10,11... | collective-permute-start | bytes 98312 | tf_op jit(solution)/shard_map/ppermute | solution.py:312
  11.3 6.1 %collective-permute-start.1 = (bf16[128,128]{1,0:T(8,128)(2,1)S(1)}, bf16[128,128]{1,0:T(8,128)(2,1)S(1)}, u32[]{:S(2)}, u32[]{:S(2)}) collective-permute-start(bf16[128,128]{1,0:T(8,128)(2,1)S(1)} %get-tuple-element.35), channel_id=1, source_target_pairs={{0,2},{1,3},{2,0},{3,1},{4,6},{5,7},{6,4},{7,5},{8,10},{9,11},{10,... | collective-permute-start | bytes 98312 | tf_op jit(solution)/shard_map/ppermute | solution.py:312
  13.0 5.9 %collective-permute-start.2 = (bf16[128,128]{1,0:T(8,128)(2,1)S(1)}, bf16[128,128]{1,0:T(8,128)(2,1)S(1)}, u32[]{:S(2)}, u32[]{:S(2)}) collective-permute-start(bf16[128,128]{1,0:T(8,128)(2,1)S(1)} %get-tuple-element.36), channel_id=1, source_target_pairs={{0,3},{1,2},{2,1},{3,0},{4,7},{5,6},{6,5},{7,4},{8,11},{9,10},{10,... | collective-permute-start | bytes 98312 | tf_op jit(solution)/shard_map/ppermute | solution.py:312
  13.0 8.3 %collective-permute-start.3 = (bf16[128,128]{1,0:T(8,128)(2,1)S(1)}, bf16[128,128]{1,0:T(8,128)(2,1)S(1)}, u32[]{:S(2)}, u32[]{:S(2)}) collective-permute-start(bf16[128,128]{1,0:T(8,128)(2,1)S(1)} %get-tuple-element.37), channel_id=1, source_target_pairs={{0,4},{1,5},{2,6},{3,7},{4,0},{5,1},{6,2},{7,3},{8,12},{9,13},{10,... | collective-permute-start | bytes 98312 | tf_op jit(solution)/shard_map/ppermute | solution.py:312
  14.7 6.6 %collective-permute-start.4 = (bf16[128,128]{1,0:T(8,128)(2,1)S(1)}, bf16[128,128]{1,0:T(8,128)(2,1)S(1)}, u32[]{:S(2)}, u32[]{:S(2)}) collective-permute-start(bf16[128,128]{1,0:T(8,128)(2,1)S(1)} %get-tuple-element.38), channel_id=1, source_target_pairs={{0,5},{1,4},{2,7},{3,6},{4,1},{5,0},{6,3},{7,2},{8,13},{9,12},{10,... | collective-permute-start | bytes 98312 | tf_op jit(solution)/shard_map/ppermute | solution.py:312
  14.8 9.4 %collective-permute-start.5 = (bf16[128,128]{1,0:T(8,128)(2,1)S(1)}, bf16[128,128]{1,0:T(8,128)(2,1)S(1)}, u32[]{:S(2)}, u32[]{:S(2)}) collective-permute-start(bf16[128,128]{1,0:T(8,128)(2,1)S(1)} %get-tuple-element.39), channel_id=1, source_target_pairs={{0,6},{1,7},{2,4},{3,5},{4,2},{5,3},{6,0},{7,1},{8,14},{9,15},{10,... | collective-permute-start | bytes 98312 | tf_op jit(solution)/shard_map/ppermute | solution.py:312
  17.4 6.8 %collective-permute-start.6 = (bf16[128,128]{1,0:T(8,128)(2,1)S(1)}, bf16[128,128]{1,0:T(8,128)(2,1)S(1)}, u32[]{:S(2)}, u32[]{:S(2)}) collective-permute-start(bf16[128,128]{1,0:T(8,128)(2,1)S(1)} %get-tuple-element.40), channel_id=1, source_target_pairs={{0,7},{1,6},{2,5},{3,4},{4,3},{5,2},{6,1},{7,0},{8,15},{9,14},{10,... | collective-permute-start | bytes 98312 | tf_op jit(solution)/shard_map/ppermute | solution.py:312
  44.4 20.0 %all-to-all-start.3 = ((bf16[16,128,128]{2,1,0:T(8,128)(2,1)}), bf16[16,128,128]{2,1,0:T(8,128)(2,1)S(1)}, u32[]{:S(2)}, u32[]{:S(2)}) async-start(bf16[16,128,128]{2,1,0:T(8,128)(2,1)} %get-tuple-element.43), calls=%async_computation.3 | async-start | bytes 1048576 | tf_op jit(solution)/shard_map/all_to_all | solution.py:298
  49.9 4.0 %collective-permute-start.7 = (bf16[128,128]{1,0:T(8,128)(2,1)S(1)}, bf16[128,128]{1,0:T(8,128)(2,1)S(1)}, u32[]{:S(2)}, u32[]{:S(2)}) collective-permute-start(bf16[128,128]{1,0:T(8,128)(2,1)S(1)} %get-tuple-element.47), channel_id=1, source_target_pairs={{0,1},{1,0},{2,3},{3,2},{4,5},{5,4},{6,7},{7,6},{8,9},{9,8},{10,11... | collective-permute-start | bytes 98312 | tf_op jit(solution)/shard_map/ppermute | solution.py:312
  50.3 6.3 %collective-permute-start.8 = (bf16[128,128]{1,0:T(8,128)(2,1)S(1)}, bf16[128,128]{1,0:T(8,128)(2,1)S(1)}, u32[]{:S(2)}, u32[]{:S(2)}) collective-permute-start(bf16[128,128]{1,0:T(8,128)(2,1)S(1)} %get-tuple-element.48), channel_id=1, source_target_pairs={{0,2},{1,3},{2,0},{3,1},{4,6},{5,7},{6,4},{7,5},{8,10},{9,11},{10,... | collective-permute-start | bytes 98312 | tf_op jit(solution)/shard_map/ppermute | solution.py:312
  52.0 7.9 %collective-permute-start.9 = (bf16[128,128]{1,0:T(8,128)(2,1)S(1)}, bf16[128,128]{1,0:T(8,128)(2,1)S(1)}, u32[]{:S(2)}, u32[]{:S(2)}) collective-permute-start(bf16[128,128]{1,0:T(8,128)(2,1)S(1)} %get-tuple-element.49), channel_id=1, source_target_pairs={{0,3},{1,2},{2,1},{3,0},{4,7},{5,6},{6,5},{7,4},{8,11},{9,10},{10,... | collective-permute-start | bytes 98312 | tf_op jit(solution)/shard_map/ppermute | solution.py:312
  52.0 8.9 %collective-permute-start.10 = (bf16[128,128]{1,0:T(8,128)(2,1)S(1)}, bf16[128,128]{1,0:T(8,128)(2,1)S(1)}, u32[]{:S(2)}, u32[]{:S(2)}) collective-permute-start(bf16[128,128]{1,0:T(8,128)(2,1)S(1)} %get-tuple-element.50), channel_id=1, source_target_pairs={{0,4},{1,5},{2,6},{3,7},{4,0},{5,1},{6,2},{7,3},{8,12},{9,13},{10,... | collective-permute-start | bytes 98312 | tf_op jit(solution)/shard_map/ppermute | solution.py:312
  53.7 7.2 %collective-permute-start.11 = (bf16[128,128]{1,0:T(8,128)(2,1)S(1)}, bf16[128,128]{1,0:T(8,128)(2,1)S(1)}, u32[]{:S(2)}, u32[]{:S(2)}) collective-permute-start(bf16[128,128]{1,0:T(8,128)(2,1)S(1)} %get-tuple-element.51), channel_id=1, source_target_pairs={{0,5},{1,4},{2,7},{3,6},{4,1},{5,0},{6,3},{7,2},{8,13},{9,12},{10,... | collective-permute-start | bytes 98312 | tf_op jit(solution)/shard_map/ppermute | solution.py:312
  53.8 9.9 %collective-permute-start.12 = (bf16[128,128]{1,0:T(8,128)(2,1)S(1)}, bf16[128,128]{1,0:T(8,128)(2,1)S(1)}, u32[]{:S(2)}, u32[]{:S(2)}) collective-permute-start(bf16[128,128]{1,0:T(8,128)(2,1)S(1)} %get-tuple-element.52), channel_id=1, source_target_pairs={{0,6},{1,7},{2,4},{3,5},{4,2},{5,3},{6,0},{7,1},{8,14},{9,15},{10,... | collective-permute-start | bytes 98312 | tf_op jit(solution)/shard_map/ppermute | solution.py:312
  56.7 7.1 %collective-permute-start.13 = (bf16[128,128]{1,0:T(8,128)(2,1)S(1)}, bf16[128,128]{1,0:T(8,128)(2,1)S(1)}, u32[]{:S(2)}, u32[]{:S(2)}) collective-permute-start(bf16[128,128]{1,0:T(8,128)(2,1)S(1)} %get-tuple-element.53), channel_id=1, source_target_pairs={{0,7},{1,6},{2,5},{3,4},{4,3},{5,2},{6,1},{7,0},{8,15},{9,14},{10,... | collective-permute-start | bytes 98312 | tf_op jit(solution)/shard_map/ppermute | solution.py:312
  (10 other events, 26.9 us)

commit v10 on v9

--- a/solution.py
+++ b/solution.py
@@ -91,6 +91,10 @@
     return [cells[row : row + 1] for row in range(rows)]
 
 
+def wide_order(devices, count):
+    return [half * count + place for place in range(count) for half in range(devices // count)]
+
+
 def partner(step, count):
     return lax.rem(lax.axis_index("row"), count) ^ step
 
@@ -112,12 +116,12 @@
     rows = pair.shape[0]
     devices, depth, width = right_panel.shape
     block = depth // rows
-    hidden = w_proj.shape[1] // 4
-    count = hidden // block
+    count = w_proj.shape[1] // 4 // block
     for row, right in gated_rows(pair, mask, gain, bias, w_proj, 1):
         right = right.reshape(count, block, width).astype(BF16)
-        for start in range(0, devices, count):
-            right_panel[start : start + count, row * block : (row + 1) * block, :] = right
+        for rank in range(devices):
+            place = wide_order(devices, count)[rank] % count
+            right_panel[rank, row * block : (row + 1) * block, :] = right[place]
 
 
 def project_left_kernel(pair, mask, gain, bias, w_proj, after, *refs):
@@ -154,6 +158,12 @@
     wide[...] = panel[...].astype(F32).reshape(wide.shape)
 
 
+def wide_places(panel, count):
+    devices, depth, _ = panel.shape
+    for rank, device in enumerate(wide_order(devices, count)):
+        yield rank, slice(device * depth, (device + 1) * depth)
+
+
 def sort_left_kernel(*refs):
     *pieces, left_all, left_wide = refs
     block, left_rows, _ = left_all.shape
@@ -169,7 +179,8 @@
     del after
     block, left_rows, _ = left_all.shape
     right_rows = right_all.shape[1]
-    spread(right_panel, right_wide)
+    for rank, place in wide_places(right_panel, products.shape[0]):
+        right_wide[place, :] = right_panel[rank].astype(F32)
     for h in range(block):
         right = right_wide[pl.ds(h, right_rows, stride=block), :].astype(BF16)
         right_all[h] = right
@@ -205,7 +216,8 @@
         d_tri = left_wide[pl.ds(h, left_rows, stride=block), :].astype(BF16)
         d_tri_all[h] = d_tri
         right_wide[pl.ds(h, right_rows, stride=block), :] = dot(d_tri, left_all[h], 0, 0)
-    d_right_panel[...] = right_wide[...].astype(BF16).reshape(d_right_panel.shape)
+    for rank, place in wide_places(d_right_panel, d_products.shape[0]):
+        d_right_panel[rank] = right_wide[place, :].astype(BF16)
 
 
 def d_left_kernel(d_tri_all, right_all, *refs):
@@ -279,9 +291,9 @@
     hidden = count * depth // rows
     for row in range(rows):
         d_right = cell_row(d_right_panel, row, rows)
-        d_right = sum(d_right[n : n + hidden] for n in range(0, d_right.shape[0], hidden))
+        d_right = jnp.sum(d_right.reshape(count, -1, depth // rows, width), axis=1)
         parts = []
-        for side, d_value in enumerate((cell_row(d_left_panel, row, rows), d_right)):
+        for side, d_value in enumerate((cell_row(d_left_panel, row, rows), d_right.reshape(hidden, width))):
             for base in (2 * side * hidden, (2 * side + 1) * hidden):
                 slope = slopes[row, base : base + hidden, :].astype(F32)
                 parts.append((d_value * slope).astype(BF16))
@@ -294,8 +306,11 @@
         grad[row] = jnp.transpose(result).astype(BF16)
 
 
-def swap(values):
-    return lax.all_to_all(values, "row", split_axis=0, concat_axis=0, tiled=True)
+def swap(values, count):
+    groups = [wide_order(lax.axis_size("row"), count)]
+    return lax.all_to_all(
+        values, "row", split_axis=0, concat_axis=0, tiled=True, axis_index_groups=groups
+    )
 
 
 def swap_half(values, count):
@@ -353,7 +368,7 @@
         flops=2 * cells * channels * 2 * hidden,
         limit=64 * 1024 * 1024 - 640 * 1024,
     )
-    right_panel = swap(own_right)
+    right_panel = swap(own_right, count)
     pieces = call(
         project_left_kernel,
         "project_left",
@@ -406,7 +421,7 @@
         scratch=[left_wide, right_wide],
         flops=2 * block * left_rows * width * right_rows,
     )
-    d_right_panel = swap(d_right_panel)
+    d_right_panel = swap(d_right_panel, count)
     d_pieces = call(
         d_left_kernel,
         "d_left",

time: 66.9 us -> 66.5 us (level)
  local copies, waits for them, and re-layouts: 2.98 us -> 2.23 us
    ppermute x14, waiting for transfers between devices: 9.43 us -> 6.12 us  [swap_pieces(): lax.ppermute(pieces[step], 'row', [(d, d ^ step) for d in devices])]
    all_to_all x2, waiting for transfers between devices: 0.86 us -> 4.16 us  [swap(): lax.all_to_all(values, 'row', split_axis=0, concat_axis=0, tiled=True, ax...]
    ppermute x14, starting transfers between devices: 13.1 us -> 14.5 us  [swap_pieces(): lax.ppermute(pieces[step], 'row', [(d, d ^ step) for d in devices])]
    unnamed x36, local copies, waits for them, and re-layouts: 2.98 us -> 2.23 us
  transfers between devices with their start and end apart: 16 -> 16, of which waited for: 7 -> 9; matrix products, arithmetic and copies ran while one was open for 0% -> 0% of each run, Pallas kernels for 5% -> 5%
where the time goes in v10:
time: 66.5 us; the launch traced here: 66 us
  starting transfers between devices  26.4 us (40%)
  blocking collectives  17.2 us (26%)
  waiting for transfers between devices  10.3 us (15%)
  Pallas kernels  9.65 us (15%)
  local copies, waits for them, and re-layouts  2.23 us (3%)
    all_to_all x2, blocking collectives, swap_half(): lax.all_to_all(values, 'row', split_axis=0, concat_axis=0, tiled=True, ax...  17.2 us
    ppermute x14, starting transfers between devices, swap_pieces(): lax.ppermute(pieces[step], 'row', [(d, d ^ step) for d in devices])  14.5 us
    all_to_all x2, starting transfers between devices, swap(): lax.all_to_all(values, 'row', split_axis=0, concat_axis=0, tiled=True, ax...  12 us
    pallas_call x11, Pallas kernels, call(): pl.pallas_call(body, name=name, out_shape=outs, in_specs=[pl.BlockSpec(me...  9.65 us
    ppermute x14, waiting for transfers between devices, swap_pieces(): lax.ppermute(pieces[step], 'row', [(d, d ^ step) for d in devices])  6.12 us
    all_to_all x2, waiting for transfers between devices, swap(): lax.all_to_all(values, 'row', split_axis=0, concat_axis=0, tiled=True, ax...  4.16 us
    unnamed x36, local copies, waits for them, and re-layouts  2.23 us
  transfers between devices with their start and end apart: 16, of which 9 were waited for; matrix products, arithmetic and copies ran while one was open for 0% of the time, Pallas kernels for 5%

profile of v10, /device:TPU:0, one launch (start us, length us, event | category | flops | bytes accessed | tf_op | source)
XLA Modules:
  0.0 66.0 jit_solution(946642406527332625)
XLA Ops:
  0.0 2.4 %project_right.1.refs_5_ = bf16[16,128,128]{2,1,0:T(8,128)(2,1)} custom-call(bf16[8,128,128]{2,1,0:T(8,128)(2,1)} %refs_2_.1, s32[1,128]{1,0:T(1,128)} %bitcast.13, f32[1,128]{1,0:T(1,128)} %bitcast.5, f32[1,128]{1,0:T(1,128)} %bitcast.9, bf16[128,512]{1,0:T(8,128)(2,1)} %refs_6_.3), custom_call_target="tpu_custom_call" | custom-call | flops 67108864 | bytes 919040 | tf_op jit(solution)/shard_map/project_right/pallas_call | solution.py:65
  2.5 7.5 %all-to-all-start = ((bf16[16,128,128]{2,1,0:T(8,128)(2,1)}), bf16[16,128,128]{2,1,0:T(8,128)(2,1)S(1)}, u32[]{:S(2)}, u32[]{:S(2)}) async-start(bf16[16,128,128]{2,1,0:T(8,128)(2,1)} %project_right.1.refs_5_), calls=%async_computation | async-start | bytes 1048576 | tf_op jit(solution)/shard_map/all_to_all | solution.py:311
  10.1 0.8 %project_left.1 = (bf16[128,128]{1,0:T(8,128)(2,1)S(1)}, bf16[128,128]{1,0:T(8,128)(2,1)S(1)}, bf16[128,128]{1,0:T(8,128)(2,1)S(1)}, bf16[128,128]{1,0:T(8,128)(...) custom-call(bf16[8,128,128]{2,1,0:T(8,128)(2,1)S(1)} %copy-done.1, ...), custom_call_target="tpu_custom_call" | custom-call | flops 67108864 | bytes 1181184 | tf_op jit(solution)/shard_map/project_left/pallas_call | solution.py:65
  11.3 1.7 %collective-permute-start.1 = (bf16[128,128]{1,0:T(8,128)(2,1)S(1)}, bf16[128,128]{1,0:T(8,128)(2,1)S(1)}, u32[]{:S(2)}, u32[]{:S(2)}) collective-permute-start(bf16[128,128]{1,0:T(8,128)(2,1)S(1)} %get-tuple-element.35), channel_id=1, source_target_pairs={{0,2},{1,3},{2,0},{3,1},{4,6},{5,7},{6,4},{7,5},{8,10},{9,11},{10,... | collective-permute-start | bytes 98312 | tf_op jit(solution)/shard_map/ppermute | solution.py:327
  13.0 1.7 %collective-permute-start.3 = (bf16[128,128]{1,0:T(8,128)(2,1)S(1)}, bf16[128,128]{1,0:T(8,128)(2,1)S(1)}, u32[]{:S(2)}, u32[]{:S(2)}) collective-permute-start(bf16[128,128]{1,0:T(8,128)(2,1)S(1)} %get-tuple-element.37), channel_id=1, source_target_pairs={{0,4},{1,5},{2,6},{3,7},{4,0},{5,1},{6,2},{7,3},{8,12},{9,13},{10,... | collective-permute-start | bytes 98312 | tf_op jit(solution)/shard_map/ppermute | solution.py:327
  14.8 2.6 %collective-permute-start.5 = (bf16[128,128]{1,0:T(8,128)(2,1)S(1)}, bf16[128,128]{1,0:T(8,128)(2,1)S(1)}, u32[]{:S(2)}, u32[]{:S(2)}) collective-permute-start(bf16[128,128]{1,0:T(8,128)(2,1)S(1)} %get-tuple-element.39), channel_id=1, source_target_pairs={{0,6},{1,7},{2,4},{3,5},{4,2},{5,3},{6,0},{7,1},{8,14},{9,15},{10,... | collective-permute-start | bytes 98312 | tf_op jit(solution)/shard_map/ppermute | solution.py:327
  18.1 0.8 %prepare.1 = (f32[8,128,128]{2,1,0:T(8,128)S(1)}, f32[8,128,128]{2,1,0:T(8,128)S(1)}) custom-call(bf16[8,128,128]{2,1,0:T(8,128)(2,1)S(1)} %copy-done.1, bf16[8,128,128]{2,1,0:T(8,128)(2,1)S(1)} %copy-done.3, f32[1,128]{1,0:T(1,128)S(1)} %bitcast.7, f32[1,128]{1,0:T(1,128)S(1)} %bitcast.11, bf16[128,128]{1,0:T(8,128)(2,1)S(1)} %copy-done.6, ...), custom_call_target="tpu_custom_call" | custom-call | flops 67108864 | bytes 1639936 | tf_op jit(solution)/shard_map/prepare/pallas_call | solution.py:65
  18.9 1.5 %collective-permute-done.3.refs_4_ = bf16[128,128]{1,0:T(8,128)(2,1)S(1)} collective-permute-done((bf16[128,128]{1,0:T(8,128)(2,1)S(1)}, bf16[128,128]{1,0:T(8,128)(2,1)S(1)}, u32[]{:S(2)}, u32[]{:S(2)}) %collective-permute-start.3) | collective-permute-done | bytes 32800 | tf_op jit(solution)/shard_map/ppermute | solution.py:327
  20.4 0.7 %collective-permute-done.4.refs_5_ = bf16[128,128]{1,0:T(8,128)(2,1)S(1)} collective-permute-done((bf16[128,128]{1,0:T(8,128)(2,1)S(1)}, bf16[128,128]{1,0:T(8,128)(2,1)S(1)}, u32[]{:S(2)}, u32[]{:S(2)}) %collective-permute-start.4) | collective-permute-done | bytes 32800 | tf_op jit(solution)/shard_map/ppermute | solution.py:327
  21.1 1.8 %collective-permute-done.5.refs_6_ = bf16[128,128]{1,0:T(8,128)(2,1)S(1)} collective-permute-done((bf16[128,128]{1,0:T(8,128)(2,1)S(1)}, bf16[128,128]{1,0:T(8,128)(2,1)S(1)}, u32[]{:S(2)}, u32[]{:S(2)}) %collective-permute-start.5) | collective-permute-done | bytes 32800 | tf_op jit(solution)/shard_map/ppermute | solution.py:327
  23.3 2.0 %all-to-all-done.refs_0_ = bf16[16,128,128]{2,1,0:T(8,128)(2,1)S(1)} async-done(((bf16[16,128,128]{2,1,0:T(8,128)(2,1)}), bf16[16,128,128]{2,1,0:T(8,128)(2,1)S(1)}, u32[]{:S(2)}, u32[]{:S(2)}) %all-to-all-start) | async-done | bytes 524320 | tf_op jit(solution)/shard_map/all_to_all | solution.py:311
  25.9 8.5 %all_to_all.20.refs_0_ = bf16[8,128,128]{2,1,0:T(8,128)(2,1)S(1)} all-to-all(bf16[8,128,128]{2,1,0:T(8,128)(2,1)S(1)} %get-tuple-element.42), channel_id=1, replica_groups={{0,1,2,3,4,5,6,7},{8,9,10,11,12,13,14,15},{16,17,18,19,20,21,22,23},{24..., dimensions={0} | all-to-all | bytes 524288 | tf_op jit(solution)/shard_map/all_to_all | solution.py:319
  34.8 8.6 %all_to_all.21.refs_0_ = bf16[8,128,128]{2,1,0:T(8,128)(2,1)S(1)} all-to-all(bf16[8,128,128]{2,1,0:T(8,128)(2,1)S(1)} %middle.1), channel_id=1, replica_groups={{0,1,2,3,4,5,6,7},{8,9,10,11,12,13,14,15},{16,17,18,19,20,21,22,23},{24..., dimensions={0} | all-to-all | bytes 524288 | tf_op jit(solution)/shard_map/all_to_all | solution.py:319
  43.4 1.5 %d_right.1 = (bf16[16,128,128]{2,1,0:T(8,128)(2,1)}, bf16[16,64,128]{2,1,0:T(8,128)(2,1)S(1)}) custom-call(bf16[8,128,128]{2,1,0:T(8,128)(2,1)S(1)} %all_to_all.21.refs_0_, bf16[16,64,128]{2,1,0:T(8,128)(2,1)S(1)} %sort_left.1.refs_1_), custom_call_target="tpu_custom_call" | custom-call | flops 33554432 | bytes 1310720 | tf_op jit(solution)/shard_map/d_right/pallas_call | solution.py:65
  44.8 4.5 %all-to-all-start.3 = ((bf16[16,128,128]{2,1,0:T(8,128)(2,1)}), bf16[16,128,128]{2,1,0:T(8,128)(2,1)S(1)}, u32[]{:S(2)}, u32[]{:S(2)}) async-start(bf16[16,128,128]{2,1,0:T(8,128)(2,1)} %get-tuple-element.43), calls=%async_computation.3 | async-start | bytes 1048576 | tf_op jit(solution)/shard_map/all_to_all | solution.py:311
  50.1 1.7 %collective-permute-start.8 = (bf16[128,128]{1,0:T(8,128)(2,1)S(1)}, bf16[128,128]{1,0:T(8,128)(2,1)S(1)}, u32[]{:S(2)}, u32[]{:S(2)}) collective-permute-start(bf16[128,128]{1,0:T(8,128)(2,1)S(1)} %get-tuple-element.48), channel_id=1, source_target_pairs={{0,2},{1,3},{2,0},{3,1},{4,6},{5,7},{6,4},{7,5},{8,10},{9,11},{10,... | collective-permute-start | bytes 98312 | tf_op jit(solution)/shard_map/ppermute | solution.py:327
  51.8 1.7 %collective-permute-start.10 = (bf16[128,128]{1,0:T(8,128)(2,1)S(1)}, bf16[128,128]{1,0:T(8,128)(2,1)S(1)}, u32[]{:S(2)}, u32[]{:S(2)}) collective-permute-start(bf16[128,128]{1,0:T(8,128)(2,1)S(1)} %get-tuple-element.50), channel_id=1, source_target_pairs={{0,4},{1,5},{2,6},{3,7},{4,0},{5,1},{6,2},{7,3},{8,12},{9,13},{10,... | collective-permute-start | bytes 98312 | tf_op jit(solution)/shard_map/ppermute | solution.py:327
  53.6 2.6 %collective-permute-start.12 = (bf16[128,128]{1,0:T(8,128)(2,1)S(1)}, bf16[128,128]{1,0:T(8,128)(2,1)S(1)}, u32[]{:S(2)}, u32[]{:S(2)}) collective-permute-start(bf16[128,128]{1,0:T(8,128)(2,1)S(1)} %get-tuple-element.52), channel_id=1, source_target_pairs={{0,6},{1,7},{2,4},{3,5},{4,2},{5,3},{6,0},{7,1},{8,14},{9,15},{10,... | collective-permute-start | bytes 98312 | tf_op jit(solution)/shard_map/ppermute | solution.py:327
  56.3 0.9 %collective-permute-start.13 = (bf16[128,128]{1,0:T(8,128)(2,1)S(1)}, bf16[128,128]{1,0:T(8,128)(2,1)S(1)}, u32[]{:S(2)}, u32[]{:S(2)}) collective-permute-start(bf16[128,128]{1,0:T(8,128)(2,1)S(1)} %get-tuple-element.53), channel_id=1, source_target_pairs={{0,7},{1,6},{2,5},{3,4},{4,3},{5,2},{6,1},{7,0},{8,15},{9,14},{10,... | collective-permute-start | bytes 98312 | tf_op jit(solution)/shard_map/ppermute | solution.py:327
  57.9 1.3 %slopes.1 = (bf16[8,512,128]{2,1,0:T(8,128)(2,1)S(1)}, bf16[8,128,128]{2,1,0:T(8,128)(2,1)S(1)}, bf16[8,128,128]{2,1,0:T(8,128)(2,1)S(1)}, f32[8,128]{1,0:T(8,12...) custom-call(bf16[8,128,128]{2,1,0:T(8,128)(2,1)S(1)} %all_to_all.20.refs_0_, ...), custom_call_target="tpu_custom_call" | custom-call | flops 201326592 | bytes 3054080 | tf_op jit(solution)/shard_map/slopes/pallas_call | solution.py:65
  59.2 0.7 copy-done.4
  60.5 1.7 %collective-permute-done.12.refs_6_ = bf16[128,128]{1,0:T(8,128)(2,1)S(1)} collective-permute-done((bf16[128,128]{1,0:T(8,128)(2,1)S(1)}, bf16[128,128]{1,0:T(8,128)(2,1)S(1)}, u32[]{:S(2)}, u32[]{:S(2)}) %collective-permute-start.12) | collective-permute-done | bytes 32800 | tf_op jit(solution)/shard_map/ppermute | solution.py:327
  62.4 2.2 %all-to-all-done.3.refs_0_ = bf16[16,128,128]{2,1,0:T(8,128)(2,1)S(1)} async-done(((bf16[16,128,128]{2,1,0:T(8,128)(2,1)}), bf16[16,128,128]{2,1,0:T(8,128)(2,1)S(1)}, u32[]{:S(2)}, u32[]{:S(2)}) %all-to-all-start.3) | async-done | bytes 524320 | tf_op jit(solution)/shard_map/all_to_all | solution.py:311
  64.6 1.4 %finish.1 = bf16[8,128,128]{2,1,0:T(8,128)(2,1)} custom-call(bf16[16,128,128]{2,1,0:T(8,128)(2,1)S(1)} %all-to-all-done.3.refs_0_, bf16[8,128,128]{2,1,0:T(8,128)(2,1)S(1)} %sort_d_left.1.refs_1_, bf16[8,512,128]{2,1,0:T(8,128)(2,1)S(1)} %get-tuple-element.55.refs_2_, bf16[8,128,128]{2,1,0:T(8,128)(2,1)S(1)} %get-tuple-element.56.refs_3_, ...), custom_call_target="tpu_custom_call" | custom-call | flops 134217728 | bytes 2854912 | tf_op jit(solution)/shard_map/finish/pallas_call | solution.py:65
  (57 shorter events, 5.0 us)
Async XLA Ops:
  2.4 7.6 %copy-start = (bf16[16,128,128]{2,1,0:T(8,128)(2,1)S(1)}, bf16[16,128,128]{2,1,0:T(8,128)(2,1)}, u32[]{:S(2)}) copy-start(bf16[16,128,128]{2,1,0:T(8,128)(2,1)} %project_right.1.refs_5_) | copy-start | bytes 1572868
  2.4 7.6 %copy-start.1 = (bf16[8,128,128]{2,1,0:T(8,128)(2,1)S(1)}, bf16[8,128,128]{2,1,0:T(8,128)(2,1)}, u32[]{:S(2)}) copy-start(bf16[8,128,128]{2,1,0:T(8,128)(2,1)} %refs_2_.1) | copy-start | bytes 786436
  2.4 7.6 %copy-start.2 = (bf16[128,512]{1,0:T(8,128)(2,1)S(1)}, bf16[128,512]{1,0:T(8,128)(2,1)}, u32[]{:S(2)}) copy-start(bf16[128,512]{1,0:T(8,128)(2,1)} %refs_6_.3) | copy-start | bytes 393220
  2.5 22.8 %all-to-all-start = ((bf16[16,128,128]{2,1,0:T(8,128)(2,1)}), bf16[16,128,128]{2,1,0:T(8,128)(2,1)S(1)}, u32[]{:S(2)}, u32[]{:S(2)}) async-start(bf16[16,128,128]{2,1,0:T(8,128)(2,1)} %project_right.1.refs_5_), calls=%async_computation | async-start | bytes 1048576 | tf_op jit(solution)/shard_map/all_to_all | solution.py:311
  10.0 7.8 %copy-start.3 = (bf16[8,128,128]{2,1,0:T(8,128)(2,1)S(1)}, bf16[8,128,128]{2,1,0:T(8,128)(2,1)}, u32[]{:S(2)}) copy-start(bf16[8,128,128]{2,1,0:T(8,128)(2,1)} %refs_1_.1) | copy-start | bytes 786436
  10.0 7.8 %copy-start.6 = (bf16[128,128]{1,0:T(8,128)(2,1)S(1)}, bf16[128,128]{1,0:T(8,128)(2,1)}, u32[]{:S(2)}) copy-start(bf16[128,128]{1,0:T(8,128)(2,1)} %refs_7_.1) | copy-start | bytes 98308
  10.0 7.8 %copy-start.8 = (bf16[128,128]{1,0:T(8,128)(2,1)S(1)}, bf16[128,128]{1,0:T(8,128)(2,1)}, u32[]{:S(2)}) copy-start(bf16[128,128]{1,0:T(8,128)(2,1)} %refs_10_.1) | copy-start | bytes 98308
  10.9 4.0 %collective-permute-start = (bf16[128,128]{1,0:T(8,128)(2,1)S(1)}, bf16[128,128]{1,0:T(8,128)(2,1)S(1)}, u32[]{:S(2)}, u32[]{:S(2)}) collective-permute-start(bf16[128,128]{1,0:T(8,128)(2,1)S(1)} %get-tuple-element.34), channel_id=1, source_target_pairs={{0,1},{1,0},{2,3},{3,2},{4,5},{5,4},{6,7},{7,6},{8,9},{9,8},{10,11... | collective-permute-start | bytes 98312 | tf_op jit(solution)/shard_map/ppermute | solution.py:327
  11.3 6.1 %collective-permute-start.1 = (bf16[128,128]{1,0:T(8,128)(2,1)S(1)}, bf16[128,128]{1,0:T(8,128)(2,1)S(1)}, u32[]{:S(2)}, u32[]{:S(2)}) collective-permute-start(bf16[128,128]{1,0:T(8,128)(2,1)S(1)} %get-tuple-element.35), channel_id=1, source_target_pairs={{0,2},{1,3},{2,0},{3,1},{4,6},{5,7},{6,4},{7,5},{8,10},{9,11},{10,... | collective-permute-start | bytes 98312 | tf_op jit(solution)/shard_map/ppermute | solution.py:327
  13.0 5.9 %collective-permute-start.2 = (bf16[128,128]{1,0:T(8,128)(2,1)S(1)}, bf16[128,128]{1,0:T(8,128)(2,1)S(1)}, u32[]{:S(2)}, u32[]{:S(2)}) collective-permute-start(bf16[128,128]{1,0:T(8,128)(2,1)S(1)} %get-tuple-element.36), channel_id=1, source_target_pairs={{0,3},{1,2},{2,1},{3,0},{4,7},{5,6},{6,5},{7,4},{8,11},{9,10},{10,... | collective-permute-start | bytes 98312 | tf_op jit(solution)/shard_map/ppermute | solution.py:327
  13.0 7.4 %collective-permute-start.3 = (bf16[128,128]{1,0:T(8,128)(2,1)S(1)}, bf16[128,128]{1,0:T(8,128)(2,1)S(1)}, u32[]{:S(2)}, u32[]{:S(2)}) collective-permute-start(bf16[128,128]{1,0:T(8,128)(2,1)S(1)} %get-tuple-element.37), channel_id=1, source_target_pairs={{0,4},{1,5},{2,6},{3,7},{4,0},{5,1},{6,2},{7,3},{8,12},{9,13},{10,... | collective-permute-start | bytes 98312 | tf_op jit(solution)/shard_map/ppermute | solution.py:327
  14.7 6.4 %collective-permute-start.4 = (bf16[128,128]{1,0:T(8,128)(2,1)S(1)}, bf16[128,128]{1,0:T(8,128)(2,1)S(1)}, u32[]{:S(2)}, u32[]{:S(2)}) collective-permute-start(bf16[128,128]{1,0:T(8,128)(2,1)S(1)} %get-tuple-element.38), channel_id=1, source_target_pairs={{0,5},{1,4},{2,7},{3,6},{4,1},{5,0},{6,3},{7,2},{8,13},{9,12},{10,... | collective-permute-start | bytes 98312 | tf_op jit(solution)/shard_map/ppermute | solution.py:327
  14.8 8.1 %collective-permute-start.5 = (bf16[128,128]{1,0:T(8,128)(2,1)S(1)}, bf16[128,128]{1,0:T(8,128)(2,1)S(1)}, u32[]{:S(2)}, u32[]{:S(2)}) collective-permute-start(bf16[128,128]{1,0:T(8,128)(2,1)S(1)} %get-tuple-element.39), channel_id=1, source_target_pairs={{0,6},{1,7},{2,4},{3,5},{4,2},{5,3},{6,0},{7,1},{8,14},{9,15},{10,... | collective-permute-start | bytes 98312 | tf_op jit(solution)/shard_map/ppermute | solution.py:327
  17.4 5.7 %collective-permute-start.6 = (bf16[128,128]{1,0:T(8,128)(2,1)S(1)}, bf16[128,128]{1,0:T(8,128)(2,1)S(1)}, u32[]{:S(2)}, u32[]{:S(2)}) collective-permute-start(bf16[128,128]{1,0:T(8,128)(2,1)S(1)} %get-tuple-element.40), channel_id=1, source_target_pairs={{0,7},{1,6},{2,5},{3,4},{4,3},{5,2},{6,1},{7,0},{8,15},{9,14},{10,... | collective-permute-start | bytes 98312 | tf_op jit(solution)/shard_map/ppermute | solution.py:327
  44.8 19.8 %all-to-all-start.3 = ((bf16[16,128,128]{2,1,0:T(8,128)(2,1)}), bf16[16,128,128]{2,1,0:T(8,128)(2,1)S(1)}, u32[]{:S(2)}, u32[]{:S(2)}) async-start(bf16[16,128,128]{2,1,0:T(8,128)(2,1)} %get-tuple-element.43), calls=%async_computation.3 | async-start | bytes 1048576 | tf_op jit(solution)/shard_map/all_to_all | solution.py:311
  49.3 7.9 %copy-start.7 = (bf16[128,128]{1,0:T(8,128)(2,1)S(1)}, bf16[128,128]{1,0:T(8,128)(2,1)}, u32[]{:S(2)}) copy-start(bf16[128,128]{1,0:T(8,128)(2,1)} %refs_7_.1) | copy-start | bytes 98308
  49.3 7.9 %copy-start.9 = (bf16[128,128]{1,0:T(8,128)(2,1)S(1)}, bf16[128,128]{1,0:T(8,128)(2,1)}, u32[]{:S(2)}) copy-start(bf16[128,128]{1,0:T(8,128)(2,1)} %refs_10_.1) | copy-start | bytes 98308
  49.7 4.0 %collective-permute-start.7 = (bf16[128,128]{1,0:T(8,128)(2,1)S(1)}, bf16[128,128]{1,0:T(8,128)(2,1)S(1)}, u32[]{:S(2)}, u32[]{:S(2)}) collective-permute-start(bf16[128,128]{1,0:T(8,128)(2,1)S(1)} %get-tuple-element.47), channel_id=1, source_target_pairs={{0,1},{1,0},{2,3},{3,2},{4,5},{5,4},{6,7},{7,6},{8,9},{9,8},{10,11... | collective-permute-start | bytes 98312 | tf_op jit(solution)/shard_map/ppermute | solution.py:327
  50.1 6.1 %collective-permute-start.8 = (bf16[128,128]{1,0:T(8,128)(2,1)S(1)}, bf16[128,128]{1,0:T(8,128)(2,1)S(1)}, u32[]{:S(2)}, u32[]{:S(2)}) collective-permute-start(bf16[128,128]{1,0:T(8,128)(2,1)S(1)} %get-tuple-element.48), channel_id=1, source_target_pairs={{0,2},{1,3},{2,0},{3,1},{4,6},{5,7},{6,4},{7,5},{8,10},{9,11},{10,... | collective-permute-start | bytes 98312 | tf_op jit(solution)/shard_map/ppermute | solution.py:327
  51.8 8.7 %collective-permute-start.9 = (bf16[128,128]{1,0:T(8,128)(2,1)S(1)}, bf16[128,128]{1,0:T(8,128)(2,1)S(1)}, u32[]{:S(2)}, u32[]{:S(2)}) collective-permute-start(bf16[128,128]{1,0:T(8,128)(2,1)S(1)} %get-tuple-element.49), channel_id=1, source_target_pairs={{0,3},{1,2},{2,1},{3,0},{4,7},{5,6},{6,5},{7,4},{8,11},{9,10},{10,... | collective-permute-start | bytes 98312 | tf_op jit(solution)/shard_map/ppermute | solution.py:327
  51.8 8.7 %collective-permute-start.10 = (bf16[128,128]{1,0:T(8,128)(2,1)S(1)}, bf16[128,128]{1,0:T(8,128)(2,1)S(1)}, u32[]{:S(2)}, u32[]{:S(2)}) collective-permute-start(bf16[128,128]{1,0:T(8,128)(2,1)S(1)} %get-tuple-element.50), channel_id=1, source_target_pairs={{0,4},{1,5},{2,6},{3,7},{4,0},{5,1},{6,2},{7,3},{8,12},{9,13},{10,... | collective-permute-start | bytes 98312 | tf_op jit(solution)/shard_map/ppermute | solution.py:327
  53.5 7.0 %collective-permute-start.11 = (bf16[128,128]{1,0:T(8,128)(2,1)S(1)}, bf16[128,128]{1,0:T(8,128)(2,1)S(1)}, u32[]{:S(2)}, u32[]{:S(2)}) collective-permute-start(bf16[128,128]{1,0:T(8,128)(2,1)S(1)} %get-tuple-element.51), channel_id=1, source_target_pairs={{0,5},{1,4},{2,7},{3,6},{4,1},{5,0},{6,3},{7,2},{8,13},{9,12},{10,... | collective-permute-start | bytes 98312 | tf_op jit(solution)/shard_map/ppermute | solution.py:327
  53.6 8.6 %collective-permute-start.12 = (bf16[128,128]{1,0:T(8,128)(2,1)S(1)}, bf16[128,128]{1,0:T(8,128)(2,1)S(1)}, u32[]{:S(2)}, u32[]{:S(2)}) collective-permute-start(bf16[128,128]{1,0:T(8,128)(2,1)S(1)} %get-tuple-element.52), channel_id=1, source_target_pairs={{0,6},{1,7},{2,4},{3,5},{4,2},{5,3},{6,0},{7,1},{8,14},{9,15},{10,... | collective-permute-start | bytes 98312 | tf_op jit(solution)/shard_map/ppermute | solution.py:327
  56.3 6.1 %collective-permute-start.13 = (bf16[128,128]{1,0:T(8,128)(2,1)S(1)}, bf16[128,128]{1,0:T(8,128)(2,1)S(1)}, u32[]{:S(2)}, u32[]{:S(2)}) collective-permute-start(bf16[128,128]{1,0:T(8,128)(2,1)S(1)} %get-tuple-element.53), channel_id=1, source_target_pairs={{0,7},{1,6},{2,5},{3,4},{4,3},{5,2},{6,1},{7,0},{8,15},{9,14},{10,... | collective-permute-start | bytes 98312 | tf_op jit(solution)/shard_map/ppermute | solution.py:327
  (10 other events, 30.5 us)

commit v11 on v10

--- a/solution.py
+++ b/solution.py
@@ -92,7 +92,8 @@
 
 
 def wide_order(devices, count):
-    return [half * count + place for place in range(count) for half in range(devices // count)]
+    inner = [(place + count // 2) % count for place in range(count)]
+    return [device for place in range(count) for device in (inner[place], count + place)]
 
 
 def partner(step, count):
@@ -283,6 +284,13 @@
         d_left_panel[partner(step, len(pieces))] = piece[...]
 
 
+def both_halves(blocks, count):
+    order = wide_order(2 * count, count)
+    return jnp.stack(
+        [blocks[order.index(place)] + blocks[order.index(count + place)] for place in range(count)]
+    )
+
+
 def finish_kernel(
     d_right_panel, d_left_panel, slopes, d_gate_pre, normed_in, inv_in, gain_col, weights, grad
 ):
@@ -291,7 +299,7 @@
     hidden = count * depth // rows
     for row in range(rows):
         d_right = cell_row(d_right_panel, row, rows)
-        d_right = jnp.sum(d_right.reshape(count, -1, depth // rows, width), axis=1)
+        d_right = both_halves(d_right.reshape(2 * count, depth // rows, width), count)
         parts = []
         for side, d_value in enumerate((cell_row(d_left_panel, row, rows), d_right.reshape(hidden, width))):
             for base in (2 * side * hidden, (2 * side + 1) * hidden):

time: 66.5 us -> 65.6 us (0.986)
  starting transfers between devices: 26.4 us -> 23.3 us
  local copies, waits for them, and re-layouts: 2.23 us -> 3.5 us
  waiting for transfers between devices: 10.3 us -> 11.1 us
    ppermute x14, waiting for transfers between devices: 6.12 us -> 11.1 us  [swap_pieces(): lax.ppermute(pieces[step], 'row', [(d, d ^ step) for d in devices])]
    all_to_all x2, waiting for transfers between devices: 4.16 us -> 0.01 us  [swap(): lax.all_to_all(values, 'row', split_axis=0, concat_axis=0, tiled=True, ax...]
    ppermute x14, starting transfers between devices: 14.5 us -> 10.4 us  [swap_pieces(): lax.ppermute(pieces[step], 'row', [(d, d ^ step) for d in devices])]
    unnamed x36, local copies, waits for them, and re-layouts: 2.23 us -> 3.5 us
    all_to_all x2, starting transfers between devices: 12 us -> 12.9 us  [swap(): lax.all_to_all(values, 'row', split_axis=0, concat_axis=0, tiled=True, ax...]
  transfers between devices with their start and end apart: 16 -> 16, of which waited for: 9 -> 8; matrix products, arithmetic and copies ran while one was open for 0% -> 0% of each run, Pallas kernels for 5% -> 5%
where the time goes in v11:
time: 65.6 us; the launch traced here: 65.2 us
  starting transfers between devices  23.3 us (36%)
  blocking collectives  17.4 us (27%)
  waiting for transfers between devices  11.1 us (17%)
  Pallas kernels  9.66 us (15%)
  local copies, waits for them, and re-layouts  3.5 us (5%)
    all_to_all x2, blocking collectives, swap_half(): lax.all_to_all(values, 'row', split_axis=0, concat_axis=0, tiled=True, ax...  17.4 us
    all_to_all x2, starting transfers between devices, swap(): lax.all_to_all(values, 'row', split_axis=0, concat_axis=0, tiled=True, ax...  12.9 us
    ppermute x14, waiting for transfers between devices, swap_pieces(): lax.ppermute(pieces[step], 'row', [(d, d ^ step) for d in devices])  11.1 us
    ppermute x14, starting transfers between devices, swap_pieces(): lax.ppermute(pieces[step], 'row', [(d, d ^ step) for d in devices])  10.4 us
    pallas_call x11, Pallas kernels, call(): pl.pallas_call(body, name=name, out_shape=outs, in_specs=[pl.BlockSpec(me...  9.66 us
    unnamed x36, local copies, waits for them, and re-layouts  3.5 us
  transfers between devices with their start and end apart: 16, of which 8 were waited for; matrix products, arithmetic and copies ran while one was open for 0% of the time, Pallas kernels for 5%

profile of v11, /device:TPU:0, one launch (start us, length us, event | category | flops | bytes accessed | tf_op | source)
XLA Modules:
  0.0 65.2 jit_solution(7344825876729534252)
XLA Ops:
  0.0 2.4 %project_right.1.refs_5_ = bf16[16,128,128]{2,1,0:T(8,128)(2,1)} custom-call(bf16[8,128,128]{2,1,0:T(8,128)(2,1)} %refs_2_.1, s32[1,128]{1,0:T(1,128)} %bitcast.13, f32[1,128]{1,0:T(1,128)} %bitcast.5, f32[1,128]{1,0:T(1,128)} %bitcast.9, bf16[128,512]{1,0:T(8,128)(2,1)} %refs_6_.3), custom_call_target="tpu_custom_call" | custom-call | flops 67108864 | bytes 919040 | tf_op jit(solution)/shard_map/project_right/pallas_call | solution.py:65
  2.5 8.0 %all-to-all-start = ((bf16[16,128,128]{2,1,0:T(8,128)(2,1)}), bf16[16,128,128]{2,1,0:T(8,128)(2,1)S(1)}, u32[]{:S(2)}, u32[]{:S(2)}) async-start(bf16[16,128,128]{2,1,0:T(8,128)(2,1)} %project_right.1.refs_5_), calls=%async_computation | async-start | bytes 1048576 | tf_op jit(solution)/shard_map/all_to_all | solution.py:319
  10.5 0.8 %project_left.1 = (bf16[128,128]{1,0:T(8,128)(2,1)S(1)}, bf16[128,128]{1,0:T(8,128)(2,1)S(1)}, bf16[128,128]{1,0:T(8,128)(2,1)S(1)}, bf16[128,128]{1,0:T(8,128)(...) custom-call(bf16[8,128,128]{2,1,0:T(8,128)(2,1)S(1)} %copy-done.1, ...), custom_call_target="tpu_custom_call" | custom-call | flops 67108864 | bytes 1181184 | tf_op jit(solution)/shard_map/project_left/pallas_call | solution.py:65
  11.5 1.5 %collective-permute-start.1 = (bf16[128,128]{1,0:T(8,128)(2,1)S(1)}, bf16[128,128]{1,0:T(8,128)(2,1)S(1)}, u32[]{:S(2)}, u32[]{:S(2)}) collective-permute-start(bf16[128,128]{1,0:T(8,128)(2,1)S(1)} %get-tuple-element.35), channel_id=1, source_target_pairs={{0,2},{1,3},{2,0},{3,1},{4,6},{5,7},{6,4},{7,5},{8,10},{9,11},{10,... | collective-permute-start | bytes 98312 | tf_op jit(solution)/shard_map/ppermute | solution.py:335
  13.6 1.5 %collective-permute-start.4 = (bf16[128,128]{1,0:T(8,128)(2,1)S(1)}, bf16[128,128]{1,0:T(8,128)(2,1)S(1)}, u32[]{:S(2)}, u32[]{:S(2)}) collective-permute-start(bf16[128,128]{1,0:T(8,128)(2,1)S(1)} %get-tuple-element.38), channel_id=1, source_target_pairs={{0,5},{1,4},{2,7},{3,6},{4,1},{5,0},{6,3},{7,2},{8,13},{9,12},{10,... | collective-permute-start | bytes 98312 | tf_op jit(solution)/shard_map/ppermute | solution.py:335
  15.0 1.5 %collective-permute-start.5 = (bf16[128,128]{1,0:T(8,128)(2,1)S(1)}, bf16[128,128]{1,0:T(8,128)(2,1)S(1)}, u32[]{:S(2)}, u32[]{:S(2)}) collective-permute-start(bf16[128,128]{1,0:T(8,128)(2,1)S(1)} %get-tuple-element.39), channel_id=1, source_target_pairs={{0,6},{1,7},{2,4},{3,5},{4,2},{5,3},{6,0},{7,1},{8,14},{9,15},{10,... | collective-permute-start | bytes 98312 | tf_op jit(solution)/shard_map/ppermute | solution.py:335
  16.5 1.7 %collective-permute-done.1.refs_2_ = bf16[128,128]{1,0:T(8,128)(2,1)S(1)} collective-permute-done((bf16[128,128]{1,0:T(8,128)(2,1)S(1)}, bf16[128,128]{1,0:T(8,128)(2,1)S(1)}, u32[]{:S(2)}, u32[]{:S(2)}) %collective-permute-start.1) | collective-permute-done | bytes 32800 | tf_op jit(solution)/shard_map/ppermute | solution.py:335
  18.8 0.8 %prepare.1 = (f32[8,128,128]{2,1,0:T(8,128)S(1)}, f32[8,128,128]{2,1,0:T(8,128)S(1)}) custom-call(bf16[8,128,128]{2,1,0:T(8,128)(2,1)S(1)} %copy-done.1, bf16[8,128,128]{2,1,0:T(8,128)(2,1)S(1)} %copy-done.3, f32[1,128]{1,0:T(1,128)S(1)} %bitcast.7, f32[1,128]{1,0:T(1,128)S(1)} %bitcast.11, bf16[128,128]{1,0:T(8,128)(2,1)S(1)} %copy-done.6, ...), custom_call_target="tpu_custom_call" | custom-call | flops 67108864 | bytes 1639936 | tf_op jit(solution)/shard_map/prepare/pallas_call | solution.py:65
  19.7 1.1 %collective-permute-done.3.refs_4_ = bf16[128,128]{1,0:T(8,128)(2,1)S(1)} collective-permute-done((bf16[128,128]{1,0:T(8,128)(2,1)S(1)}, bf16[128,128]{1,0:T(8,128)(2,1)S(1)}, u32[]{:S(2)}, u32[]{:S(2)}) %collective-permute-start.3) | collective-permute-done | bytes 32800 | tf_op jit(solution)/shard_map/ppermute | solution.py:335
  20.8 0.7 %collective-permute-done.4.refs_5_ = bf16[128,128]{1,0:T(8,128)(2,1)S(1)} collective-permute-done((bf16[128,128]{1,0:T(8,128)(2,1)S(1)}, bf16[128,128]{1,0:T(8,128)(2,1)S(1)}, u32[]{:S(2)}, u32[]{:S(2)}) %collective-permute-start.4) | collective-permute-done | bytes 32800 | tf_op jit(solution)/shard_map/ppermute | solution.py:335
  21.5 2.2 %collective-permute-done.5.refs_6_ = bf16[128,128]{1,0:T(8,128)(2,1)S(1)} collective-permute-done((bf16[128,128]{1,0:T(8,128)(2,1)S(1)}, bf16[128,128]{1,0:T(8,128)(2,1)S(1)}, u32[]{:S(2)}, u32[]{:S(2)}) %collective-permute-start.5) | collective-permute-done | bytes 32800 | tf_op jit(solution)/shard_map/ppermute | solution.py:335
  25.1 8.7 %all_to_all.20.refs_0_ = bf16[8,128,128]{2,1,0:T(8,128)(2,1)S(1)} all-to-all(bf16[8,128,128]{2,1,0:T(8,128)(2,1)S(1)} %get-tuple-element.42), channel_id=1, replica_groups={{0,1,2,3,4,5,6,7},{8,9,10,11,12,13,14,15},{16,17,18,19,20,21,22,23},{24..., dimensions={0} | all-to-all | bytes 524288 | tf_op jit(solution)/shard_map/all_to_all | solution.py:327
  34.1 8.6 %all_to_all.21.refs_0_ = bf16[8,128,128]{2,1,0:T(8,128)(2,1)S(1)} all-to-all(bf16[8,128,128]{2,1,0:T(8,128)(2,1)S(1)} %middle.1), channel_id=1, replica_groups={{0,1,2,3,4,5,6,7},{8,9,10,11,12,13,14,15},{16,17,18,19,20,21,22,23},{24..., dimensions={0} | all-to-all | bytes 524288 | tf_op jit(solution)/shard_map/all_to_all | solution.py:327
  42.7 1.5 %d_right.1 = (bf16[16,128,128]{2,1,0:T(8,128)(2,1)}, bf16[16,64,128]{2,1,0:T(8,128)(2,1)S(1)}) custom-call(bf16[8,128,128]{2,1,0:T(8,128)(2,1)S(1)} %all_to_all.21.refs_0_, bf16[16,64,128]{2,1,0:T(8,128)(2,1)S(1)} %sort_left.1.refs_1_), custom_call_target="tpu_custom_call" | custom-call | flops 33554432 | bytes 1310720 | tf_op jit(solution)/shard_map/d_right/pallas_call | solution.py:65
  44.2 4.9 %all-to-all-start.3 = ((bf16[16,128,128]{2,1,0:T(8,128)(2,1)}), bf16[16,128,128]{2,1,0:T(8,128)(2,1)S(1)}, u32[]{:S(2)}, u32[]{:S(2)}) async-start(bf16[16,128,128]{2,1,0:T(8,128)(2,1)} %get-tuple-element.43), calls=%async_computation.3 | async-start | bytes 1048576 | tf_op jit(solution)/shard_map/all_to_all | solution.py:319
  49.7 1.5 %collective-permute-start.8 = (bf16[128,128]{1,0:T(8,128)(2,1)S(1)}, bf16[128,128]{1,0:T(8,128)(2,1)S(1)}, u32[]{:S(2)}, u32[]{:S(2)}) collective-permute-start(bf16[128,128]{1,0:T(8,128)(2,1)S(1)} %get-tuple-element.48), channel_id=1, source_target_pairs={{0,2},{1,3},{2,0},{3,1},{4,6},{5,7},{6,4},{7,5},{8,10},{9,11},{10,... | collective-permute-start | bytes 98312 | tf_op jit(solution)/shard_map/ppermute | solution.py:335
  51.7 1.5 %collective-permute-start.11 = (bf16[128,128]{1,0:T(8,128)(2,1)S(1)}, bf16[128,128]{1,0:T(8,128)(2,1)S(1)}, u32[]{:S(2)}, u32[]{:S(2)}) collective-permute-start(bf16[128,128]{1,0:T(8,128)(2,1)S(1)} %get-tuple-element.51), channel_id=1, source_target_pairs={{0,5},{1,4},{2,7},{3,6},{4,1},{5,0},{6,3},{7,2},{8,13},{9,12},{10,... | collective-permute-start | bytes 98312 | tf_op jit(solution)/shard_map/ppermute | solution.py:335
  53.2 1.5 %collective-permute-start.12 = (bf16[128,128]{1,0:T(8,128)(2,1)S(1)}, bf16[128,128]{1,0:T(8,128)(2,1)S(1)}, u32[]{:S(2)}, u32[]{:S(2)}) collective-permute-start(bf16[128,128]{1,0:T(8,128)(2,1)S(1)} %get-tuple-element.52), channel_id=1, source_target_pairs={{0,6},{1,7},{2,4},{3,5},{4,2},{5,3},{6,0},{7,1},{8,14},{9,15},{10,... | collective-permute-start | bytes 98312 | tf_op jit(solution)/shard_map/ppermute | solution.py:335
  54.7 2.2 %collective-permute-done.8.refs_2_ = bf16[128,128]{1,0:T(8,128)(2,1)S(1)} collective-permute-done((bf16[128,128]{1,0:T(8,128)(2,1)S(1)}, bf16[128,128]{1,0:T(8,128)(2,1)S(1)}, u32[]{:S(2)}, u32[]{:S(2)}) %collective-permute-start.8) | collective-permute-done | bytes 32800 | tf_op jit(solution)/shard_map/ppermute | solution.py:335
  57.5 1.3 %slopes.1 = (bf16[8,512,128]{2,1,0:T(8,128)(2,1)S(1)}, bf16[8,128,128]{2,1,0:T(8,128)(2,1)S(1)}, bf16[8,128,128]{2,1,0:T(8,128)(2,1)S(1)}, f32[8,128]{1,0:T(8,12...) custom-call(bf16[8,128,128]{2,1,0:T(8,128)(2,1)S(1)} %all_to_all.20.refs_0_, ...), custom_call_target="tpu_custom_call" | custom-call | flops 201326592 | bytes 3054080 | tf_op jit(solution)/shard_map/slopes/pallas_call | solution.py:65
  58.9 0.7 %copy-done.4 = bf16[128,640]{1,0:T(8,128)(2,1)} copy-done((bf16[128,640]{1,0:T(8,128)(2,1)}, bf16[128,640]{1,0:T(8,128)(2,1)S(1)}, u32[]{:S(2)}) %copy-start.4) | copy-done | bytes 163864
  60.2 2.1 %collective-permute-done.12.refs_6_ = bf16[128,128]{1,0:T(8,128)(2,1)S(1)} collective-permute-done((bf16[128,128]{1,0:T(8,128)(2,1)S(1)}, bf16[128,128]{1,0:T(8,128)(2,1)S(1)}, u32[]{:S(2)}, u32[]{:S(2)}) %collective-permute-start.12) | collective-permute-done | bytes 32800 | tf_op jit(solution)/shard_map/ppermute | solution.py:335
  62.9 0.9 %copy-done.5 = bf16[128,640]{1,0:T(8,128)(2,1)S(1)} copy-done((bf16[128,640]{1,0:T(8,128)(2,1)S(1)}, bf16[128,640]{1,0:T(8,128)(2,1)}, u32[]{:S(2)}) %copy-start.5) | copy-done | bytes 163864
  63.8 1.4 %finish.1 = bf16[8,128,128]{2,1,0:T(8,128)(2,1)} custom-call(bf16[16,128,128]{2,1,0:T(8,128)(2,1)S(1)} %all-to-all-done.3.refs_0_, bf16[8,128,128]{2,1,0:T(8,128)(2,1)S(1)} %sort_d_left.1.refs_1_, bf16[8,512,128]{2,1,0:T(8,128)(2,1)S(1)} %get-tuple-element.55.refs_2_, bf16[8,128,128]{2,1,0:T(8,128)(2,1)S(1)} %get-tuple-element.56.refs_3_, ...), custom_call_target="tpu_custom_call" | custom-call | flops 134217728 | bytes 2854912 | tf_op jit(solution)/shard_map/finish/pallas_call | solution.py:65
  (57 shorter events, 6.2 us)
Async XLA Ops:
  2.4 8.0 %copy-start = (bf16[16,128,128]{2,1,0:T(8,128)(2,1)S(1)}, bf16[16,128,128]{2,1,0:T(8,128)(2,1)}, u32[]{:S(2)}) copy-start(bf16[16,128,128]{2,1,0:T(8,128)(2,1)} %project_right.1.refs_5_) | copy-start | bytes 1572868
  2.4 8.0 %copy-start.1 = (bf16[8,128,128]{2,1,0:T(8,128)(2,1)S(1)}, bf16[8,128,128]{2,1,0:T(8,128)(2,1)}, u32[]{:S(2)}) copy-start(bf16[8,128,128]{2,1,0:T(8,128)(2,1)} %refs_2_.1) | copy-start | bytes 786436
  2.4 8.0 %copy-start.2 = (bf16[128,512]{1,0:T(8,128)(2,1)S(1)}, bf16[128,512]{1,0:T(8,128)(2,1)}, u32[]{:S(2)}) copy-start(bf16[128,512]{1,0:T(8,128)(2,1)} %refs_6_.3) | copy-start | bytes 393220
  2.4 8.0 %copy-start.12 = (f32[128]{0:T(128)S(1)}, f32[128]{0:T(128)}, u32[]{:S(2)}) copy-start(f32[128]{0:T(128)} %param.13) | copy-start | bytes 1540
  2.4 8.0 %copy-start.13 = (f32[128]{0:T(128)S(1)}, f32[128]{0:T(128)}, u32[]{:S(2)}) copy-start(f32[128]{0:T(128)} %param.14) | copy-start | bytes 1540
  2.4 8.0 %copy-start.14 = (s32[128]{0:T(128)S(1)}, s32[128]{0:T(128)}, u32[]{:S(2)}) copy-start(s32[128]{0:T(128)} %param.12) | copy-start | bytes 1540
  2.5 21.9 %all-to-all-start = ((bf16[16,128,128]{2,1,0:T(8,128)(2,1)}), bf16[16,128,128]{2,1,0:T(8,128)(2,1)S(1)}, u32[]{:S(2)}, u32[]{:S(2)}) async-start(bf16[16,128,128]{2,1,0:T(8,128)(2,1)} %project_right.1.refs_5_), calls=%async_computation | async-start | bytes 1048576 | tf_op jit(solution)/shard_map/all_to_all | solution.py:319
  11.3 3.7 %collective-permute-start = (bf16[128,128]{1,0:T(8,128)(2,1)S(1)}, bf16[128,128]{1,0:T(8,128)(2,1)S(1)}, u32[]{:S(2)}, u32[]{:S(2)}) collective-permute-start(bf16[128,128]{1,0:T(8,128)(2,1)S(1)} %get-tuple-element.34), channel_id=1, source_target_pairs={{0,1},{1,0},{2,3},{3,2},{4,5},{5,4},{6,7},{7,6},{8,9},{9,8},{10,11... | collective-permute-start | bytes 98312 | tf_op jit(solution)/shard_map/ppermute | solution.py:335
  11.5 6.7 %collective-permute-start.1 = (bf16[128,128]{1,0:T(8,128)(2,1)S(1)}, bf16[128,128]{1,0:T(8,128)(2,1)S(1)}, u32[]{:S(2)}, u32[]{:S(2)}) collective-permute-start(bf16[128,128]{1,0:T(8,128)(2,1)S(1)} %get-tuple-element.35), channel_id=1, source_target_pairs={{0,2},{1,3},{2,0},{3,1},{4,6},{5,7},{6,4},{7,5},{8,10},{9,11},{10,... | collective-permute-start | bytes 98312 | tf_op jit(solution)/shard_map/ppermute | solution.py:335
  13.0 6.7 %collective-permute-start.2 = (bf16[128,128]{1,0:T(8,128)(2,1)S(1)}, bf16[128,128]{1,0:T(8,128)(2,1)S(1)}, u32[]{:S(2)}, u32[]{:S(2)}) collective-permute-start(bf16[128,128]{1,0:T(8,128)(2,1)S(1)} %get-tuple-element.36), channel_id=1, source_target_pairs={{0,3},{1,2},{2,1},{3,0},{4,7},{5,6},{6,5},{7,4},{8,11},{9,10},{10,... | collective-permute-start | bytes 98312 | tf_op jit(solution)/shard_map/ppermute | solution.py:335
  13.2 7.5 %collective-permute-start.3 = (bf16[128,128]{1,0:T(8,128)(2,1)S(1)}, bf16[128,128]{1,0:T(8,128)(2,1)S(1)}, u32[]{:S(2)}, u32[]{:S(2)}) collective-permute-start(bf16[128,128]{1,0:T(8,128)(2,1)S(1)} %get-tuple-element.37), channel_id=1, source_target_pairs={{0,4},{1,5},{2,6},{3,7},{4,0},{5,1},{6,2},{7,3},{8,12},{9,13},{10,... | collective-permute-start | bytes 98312 | tf_op jit(solution)/shard_map/ppermute | solution.py:335
  13.6 7.9 %collective-permute-start.4 = (bf16[128,128]{1,0:T(8,128)(2,1)S(1)}, bf16[128,128]{1,0:T(8,128)(2,1)S(1)}, u32[]{:S(2)}, u32[]{:S(2)}) collective-permute-start(bf16[128,128]{1,0:T(8,128)(2,1)S(1)} %get-tuple-element.38), channel_id=1, source_target_pairs={{0,5},{1,4},{2,7},{3,6},{4,1},{5,0},{6,3},{7,2},{8,13},{9,12},{10,... | collective-permute-start | bytes 98312 | tf_op jit(solution)/shard_map/ppermute | solution.py:335
  15.0 8.6 %collective-permute-start.5 = (bf16[128,128]{1,0:T(8,128)(2,1)S(1)}, bf16[128,128]{1,0:T(8,128)(2,1)S(1)}, u32[]{:S(2)}, u32[]{:S(2)}) collective-permute-start(bf16[128,128]{1,0:T(8,128)(2,1)S(1)} %get-tuple-element.39), channel_id=1, source_target_pairs={{0,6},{1,7},{2,4},{3,5},{4,2},{5,3},{6,0},{7,1},{8,14},{9,15},{10,... | collective-permute-start | bytes 98312 | tf_op jit(solution)/shard_map/ppermute | solution.py:335
  18.2 6.0 %collective-permute-start.6 = (bf16[128,128]{1,0:T(8,128)(2,1)S(1)}, bf16[128,128]{1,0:T(8,128)(2,1)S(1)}, u32[]{:S(2)}, u32[]{:S(2)}) collective-permute-start(bf16[128,128]{1,0:T(8,128)(2,1)S(1)} %get-tuple-element.40), channel_id=1, source_target_pairs={{0,7},{1,6},{2,5},{3,4},{4,3},{5,2},{6,1},{7,0},{8,15},{9,14},{10,... | collective-permute-start | bytes 98312 | tf_op jit(solution)/shard_map/ppermute | solution.py:335
  44.2 18.7 %all-to-all-start.3 = ((bf16[16,128,128]{2,1,0:T(8,128)(2,1)}), bf16[16,128,128]{2,1,0:T(8,128)(2,1)S(1)}, u32[]{:S(2)}, u32[]{:S(2)}) async-start(bf16[16,128,128]{2,1,0:T(8,128)(2,1)} %get-tuple-element.43), calls=%async_computation.3 | async-start | bytes 1048576 | tf_op jit(solution)/shard_map/all_to_all | solution.py:319
  49.1 7.8 %copy-start.7 = (bf16[128,128]{1,0:T(8,128)(2,1)S(1)}, bf16[128,128]{1,0:T(8,128)(2,1)}, u32[]{:S(2)}) copy-start(bf16[128,128]{1,0:T(8,128)(2,1)} %refs_7_.1) | copy-start | bytes 98308
  49.1 7.8 %copy-start.9 = (bf16[128,128]{1,0:T(8,128)(2,1)S(1)}, bf16[128,128]{1,0:T(8,128)(2,1)}, u32[]{:S(2)}) copy-start(bf16[128,128]{1,0:T(8,128)(2,1)} %refs_10_.1) | copy-start | bytes 98308
  49.5 3.7 %collective-permute-start.7 = (bf16[128,128]{1,0:T(8,128)(2,1)S(1)}, bf16[128,128]{1,0:T(8,128)(2,1)S(1)}, u32[]{:S(2)}, u32[]{:S(2)}) collective-permute-start(bf16[128,128]{1,0:T(8,128)(2,1)S(1)} %get-tuple-element.47), channel_id=1, source_target_pairs={{0,1},{1,0},{2,3},{3,2},{4,5},{5,4},{6,7},{7,6},{8,9},{9,8},{10,11... | collective-permute-start | bytes 98312 | tf_op jit(solution)/shard_map/ppermute | solution.py:335
  49.7 7.2 %collective-permute-start.8 = (bf16[128,128]{1,0:T(8,128)(2,1)S(1)}, bf16[128,128]{1,0:T(8,128)(2,1)S(1)}, u32[]{:S(2)}, u32[]{:S(2)}) collective-permute-start(bf16[128,128]{1,0:T(8,128)(2,1)S(1)} %get-tuple-element.48), channel_id=1, source_target_pairs={{0,2},{1,3},{2,0},{3,1},{4,6},{5,7},{6,4},{7,5},{8,10},{9,11},{10,... | collective-permute-start | bytes 98312 | tf_op jit(solution)/shard_map/ppermute | solution.py:335
  51.2 9.0 %collective-permute-start.9 = (bf16[128,128]{1,0:T(8,128)(2,1)S(1)}, bf16[128,128]{1,0:T(8,128)(2,1)S(1)}, u32[]{:S(2)}, u32[]{:S(2)}) collective-permute-start(bf16[128,128]{1,0:T(8,128)(2,1)S(1)} %get-tuple-element.49), channel_id=1, source_target_pairs={{0,3},{1,2},{2,1},{3,0},{4,7},{5,6},{6,5},{7,4},{8,11},{9,10},{10,... | collective-permute-start | bytes 98312 | tf_op jit(solution)/shard_map/ppermute | solution.py:335
  51.4 8.8 %collective-permute-start.10 = (bf16[128,128]{1,0:T(8,128)(2,1)S(1)}, bf16[128,128]{1,0:T(8,128)(2,1)S(1)}, u32[]{:S(2)}, u32[]{:S(2)}) collective-permute-start(bf16[128,128]{1,0:T(8,128)(2,1)S(1)} %get-tuple-element.50), channel_id=1, source_target_pairs={{0,4},{1,5},{2,6},{3,7},{4,0},{5,1},{6,2},{7,3},{8,12},{9,13},{10,... | collective-permute-start | bytes 98312 | tf_op jit(solution)/shard_map/ppermute | solution.py:335
  51.7 8.4 %collective-permute-start.11 = (bf16[128,128]{1,0:T(8,128)(2,1)S(1)}, bf16[128,128]{1,0:T(8,128)(2,1)S(1)}, u32[]{:S(2)}, u32[]{:S(2)}) collective-permute-start(bf16[128,128]{1,0:T(8,128)(2,1)S(1)} %get-tuple-element.51), channel_id=1, source_target_pairs={{0,5},{1,4},{2,7},{3,6},{4,1},{5,0},{6,3},{7,2},{8,13},{9,12},{10,... | collective-permute-start | bytes 98312 | tf_op jit(solution)/shard_map/ppermute | solution.py:335
  53.2 9.1 %collective-permute-start.12 = (bf16[128,128]{1,0:T(8,128)(2,1)S(1)}, bf16[128,128]{1,0:T(8,128)(2,1)S(1)}, u32[]{:S(2)}, u32[]{:S(2)}) collective-permute-start(bf16[128,128]{1,0:T(8,128)(2,1)S(1)} %get-tuple-element.52), channel_id=1, source_target_pairs={{0,6},{1,7},{2,4},{3,5},{4,2},{5,3},{6,0},{7,1},{8,14},{9,15},{10,... | collective-permute-start | bytes 98312 | tf_op jit(solution)/shard_map/ppermute | solution.py:335
  56.9 6.0 %collective-permute-start.13 = (bf16[128,128]{1,0:T(8,128)(2,1)S(1)}, bf16[128,128]{1,0:T(8,128)(2,1)S(1)}, u32[]{:S(2)}, u32[]{:S(2)}) collective-permute-start(bf16[128,128]{1,0:T(8,128)(2,1)S(1)} %get-tuple-element.53), channel_id=1, source_target_pairs={{0,7},{1,6},{2,5},{3,4},{4,3},{5,2},{6,1},{7,0},{8,15},{9,14},{10,... | collective-permute-start | bytes 98312 | tf_op jit(solution)/shard_map/ppermute | solution.py:335
  (10 other events, 28.2 us)

commit v12 on v11

--- a/solution.py
+++ b/solution.py
@@ -232,38 +232,28 @@
         piece[...] = left_wide[pl.ds(start, depth), :].astype(BF16)
 
 
-def slopes_kernel(
-    products,
-    gate_slope,
-    pair,
-    mask,
-    gain,
-    bias,
-    w_proj,
-    w_gate,
-    out_gain,
-    out_bias,
-    w_out,
-    slopes,
-    d_gate_pre,
-    normed_in,
-    inv_in,
-    in_gain,
-    weights,
-):
-    rows = pair.shape[0]
-    hidden = w_out.shape[0]
-    w_flip = transposed(w_proj[...])
+def gate_back_kernel(products, gate_slope, out_gain, out_bias, w_out, d_gate_pre):
+    rows = gate_slope.shape[0]
     out_flip = transposed(w_out[...])
-    gain_col, bias_col = column(gain[...]), column(bias[...])
-    in_gain[...] = gain_col
-    weights[...] = jnp.concatenate([w_proj[...], w_gate[...]], axis=1)
     out_gain_col, out_bias_col = column(out_gain[...]), column(out_bias[...])
-    masks = cell_masks(mask, rows)
     for row in range(rows):
         tri_hat, _ = norm_rows(cell_row(products, row, rows))
         scaled = (tri_hat * out_gain_col + out_bias_col).astype(BF16)
         d_gate_pre[row] = (dot(out_flip, scaled, 1, 0) * gate_slope[row]).astype(BF16)
+
+
+def slopes_kernel(
+    pair, mask, gain, bias, w_proj, w_gate, after, slopes, normed_in, inv_in, in_gain, weights
+):
+    del after
+    rows = pair.shape[0]
+    hidden = w_proj.shape[1] // 4
+    w_flip = transposed(w_proj[...])
+    gain_col, bias_col = column(gain[...]), column(bias[...])
+    in_gain[...] = gain_col
+    weights[...] = jnp.concatenate([w_proj[...], w_gate[...]], axis=1)
+    masks = cell_masks(mask, rows)
+    for row in range(rows):
         normed, inv_std = norm_rows(jnp.transpose(pair[row].astype(F32)))
         normed_in[row] = normed.astype(normed_in.dtype)
         inv_in[row : row + 1] = inv_std
@@ -331,10 +321,11 @@
 
 def swap_pieces(pieces):
     devices = range(lax.axis_size("row"))
-    return [pieces[0]] + [
+    swapped = [
         lax.ppermute(pieces[step], "row", [(d, d ^ step) for d in devices])
-        for step in range(1, len(pieces))
+        for step in range(len(pieces) - 1, 0, -1)
     ]
+    return [pieces[0]] + swapped[::-1]
 
 
 def kernel_shards(
@@ -440,32 +431,28 @@
     )
     d_pieces = swap_pieces(d_pieces)
     (d_left_panel,) = call(sort_d_left_kernel, "sort_d_left", [panel], d_pieces)
-    slopes, d_gate_pre, normed_in, inv_in, gain_col, weights = call(
+    (d_gate_pre,) = call(
+        gate_back_kernel,
+        "gate_back",
+        [shape((rows, channels, width), BF16)],
+        [products, gate_slope, out_gain, out_bias, w_out],
+        fetched=range(2, 5),
+        flops=2 * cells * channels * hidden,
+    )
+    slopes, normed_in, inv_in, gain_col, weights = call(
         slopes_kernel,
         "slopes",
         [
             shape((rows, 4 * hidden, width), BF16),
             shape((rows, channels, width), BF16),
-            shape((rows, channels, width), BF16),
             shape((rows, width), F32),
             shape((channels, channels), F32),
             shape((channels, 4 * hidden + channels), BF16),
         ],
-        [
-            products,
-            gate_slope,
-            pair,
-            mask,
-            gain,
-            bias,
-            w_proj,
-            w_gate,
-            out_gain,
-            out_bias,
-            w_out,
-        ],
-        fetched=range(2, 11),
-        flops=2 * cells * channels * 6 * hidden,
+        [pair, mask, gain, bias, w_proj, w_gate, d_gate_pre],
+        fetched=range(6),
+        unread=(6,),
+        flops=2 * cells * channels * 4 * hidden,
     )
     (grad,) = call(
         finish_kernel,

time: 65.6 us -> 64.8 us (0.988)
  local copies, waits for them, and re-layouts: 3.5 us -> 1.34 us
  waiting for transfers between devices: 11.1 us -> 12.3 us
    unnamed x36 -> x22, local copies, waits for them, and re-layouts: 3.5 us -> 1.34 us
    ppermute x14, waiting for transfers between devices: 11.1 us -> 12.3 us  [swap_pieces(): lax.ppermute(pieces[step], 'row', [(d, d ^ step) for d in devices])]
    pallas_call x11 -> x12, Pallas kernels: 9.66 us -> 9.83 us  [call(): pl.pallas_call(body, name=name, out_shape=outs, in_specs=[pl.BlockSpec(me...]
  transfers between devices with their start and end apart: 16 -> 16, of which waited for: 8 -> 10; matrix products, arithmetic and copies ran while one was open for 0% -> 0% of each run, Pallas kernels for 5% -> 6%
where the time goes in v12:
time: 64.8 us; the launch traced here: 64.4 us
  starting transfers between devices  23.3 us (36%)
  blocking collectives  17.4 us (27%)
  waiting for transfers between devices  12.3 us (19%)
  Pallas kernels  9.83 us (15%)
  local copies, waits for them, and re-layouts  1.34 us (2%)
    all_to_all x2, blocking collectives, swap_half(): lax.all_to_all(values, 'row', split_axis=0, concat_axis=0, tiled=True, ax...  17.4 us
    all_to_all x2, starting transfers between devices, swap(): lax.all_to_all(values, 'row', split_axis=0, concat_axis=0, tiled=True, ax...  12.9 us
    ppermute x14, waiting for transfers between devices, swap_pieces(): lax.ppermute(pieces[step], 'row', [(d, d ^ step) for d in devices])  12.3 us
    ppermute x14, starting transfers between devices, swap_pieces(): lax.ppermute(pieces[step], 'row', [(d, d ^ step) for d in devices])  10.4 us
    pallas_call x12, Pallas kernels, call(): pl.pallas_call(body, name=name, out_shape=outs, in_specs=[pl.BlockSpec(me...  9.83 us
    unnamed x22, local copies, waits for them, and re-layouts  1.34 us
  transfers between devices with their start and end apart: 16, of which 10 were waited for; matrix products, arithmetic and copies ran while one was open for 0% of the time, Pallas kernels for 6%

profile of v12, /device:TPU:0, one launch (start us, length us, event | category | flops | bytes accessed | tf_op | source)
XLA Modules:
  0.0 64.4 jit_solution(14684950149714798531)
XLA Ops:
  0.0 2.4 %project_right.1.refs_5_ = bf16[16,128,128]{2,1,0:T(8,128)(2,1)} custom-call(bf16[8,128,128]{2,1,0:T(8,128)(2,1)} %refs_0_.7, s32[1,128]{1,0:T(1,128)} %bitcast.13, f32[1,128]{1,0:T(1,128)} %bitcast.5, f32[1,128]{1,0:T(1,128)} %bitcast.9, bf16[128,512]{1,0:T(8,128)(2,1)} %refs_4_.9), custom_call_target="tpu_custom_call" | custom-call | flops 67108864 | bytes 919040 | tf_op jit(solution)/shard_map/project_right/pallas_call | solution.py:65
  2.5 8.0 %all-to-all-start = ((bf16[16,128,128]{2,1,0:T(8,128)(2,1)}), bf16[16,128,128]{2,1,0:T(8,128)(2,1)S(1)}, u32[]{:S(2)}, u32[]{:S(2)}) async-start(bf16[16,128,128]{2,1,0:T(8,128)(2,1)} %project_right.1.refs_5_), calls=%async_computation | async-start | bytes 1048576 | tf_op jit(solution)/shard_map/all_to_all | solution.py:309
  10.5 0.8 %project_left.1 = (bf16[128,128]{1,0:T(8,128)(2,1)S(1)}, bf16[128,128]{1,0:T(8,128)(2,1)S(1)}, bf16[128,128]{1,0:T(8,128)(2,1)S(1)}, bf16[128,128]{1,0:T(8,128)(...) custom-call(bf16[8,128,128]{2,1,0:T(8,128)(2,1)S(1)} %copy-done.1, ...), custom_call_target="tpu_custom_call" | custom-call | flops 67108864 | bytes 1181184 | tf_op jit(solution)/shard_map/project_left/pallas_call | solution.py:65
  11.5 1.5 %collective-permute-start.1 = (bf16[128,128]{1,0:T(8,128)(2,1)S(1)}, bf16[128,128]{1,0:T(8,128)(2,1)S(1)}, u32[]{:S(2)}, u32[]{:S(2)}) collective-permute-start(bf16[128,128]{1,0:T(8,128)(2,1)S(1)} %get-tuple-element.34), channel_id=1, source_target_pairs={{0,2},{1,3},{2,0},{3,1},{4,6},{5,7},{6,4},{7,5},{8,10},{9,11},{10,... | collective-permute-start | bytes 98312 | tf_op jit(solution)/shard_map/ppermute | solution.py:325
  13.6 1.5 %collective-permute-start.4 = (bf16[128,128]{1,0:T(8,128)(2,1)S(1)}, bf16[128,128]{1,0:T(8,128)(2,1)S(1)}, u32[]{:S(2)}, u32[]{:S(2)}) collective-permute-start(bf16[128,128]{1,0:T(8,128)(2,1)S(1)} %get-tuple-element.37), channel_id=1, source_target_pairs={{0,5},{1,4},{2,7},{3,6},{4,1},{5,0},{6,3},{7,2},{8,13},{9,12},{10,... | collective-permute-start | bytes 98312 | tf_op jit(solution)/shard_map/ppermute | solution.py:325
  15.1 1.5 %collective-permute-start.5 = (bf16[128,128]{1,0:T(8,128)(2,1)S(1)}, bf16[128,128]{1,0:T(8,128)(2,1)S(1)}, u32[]{:S(2)}, u32[]{:S(2)}) collective-permute-start(bf16[128,128]{1,0:T(8,128)(2,1)S(1)} %get-tuple-element.38), channel_id=1, source_target_pairs={{0,6},{1,7},{2,4},{3,5},{4,2},{5,3},{6,0},{7,1},{8,14},{9,15},{10,... | collective-permute-start | bytes 98312 | tf_op jit(solution)/shard_map/ppermute | solution.py:325
  16.5 1.7 %collective-permute-done.1.refs_2_ = bf16[128,128]{1,0:T(8,128)(2,1)S(1)} collective-permute-done((bf16[128,128]{1,0:T(8,128)(2,1)S(1)}, bf16[128,128]{1,0:T(8,128)(2,1)S(1)}, u32[]{:S(2)}, u32[]{:S(2)}) %collective-permute-start.1) | collective-permute-done | bytes 32800 | tf_op jit(solution)/shard_map/ppermute | solution.py:325
  18.9 0.8 %prepare.1 = (f32[8,128,128]{2,1,0:T(8,128)S(1)}, f32[8,128,128]{2,1,0:T(8,128)S(1)}) custom-call(bf16[8,128,128]{2,1,0:T(8,128)(2,1)S(1)} %copy-done.1, bf16[8,128,128]{2,1,0:T(8,128)(2,1)S(1)} %copy-done.3, f32[1,128]{1,0:T(1,128)S(1)} %bitcast.7, f32[1,128]{1,0:T(1,128)S(1)} %bitcast.11, bf16[128,128]{1,0:T(8,128)(2,1)S(1)} %copy-done.5, ...), custom_call_target="tpu_custom_call" | custom-call | flops 67108864 | bytes 1639936 | tf_op jit(solution)/shard_map/prepare/pallas_call | solution.py:65
  19.7 1.1 %collective-permute-done.3.refs_4_ = bf16[128,128]{1,0:T(8,128)(2,1)S(1)} collective-permute-done((bf16[128,128]{1,0:T(8,128)(2,1)S(1)}, bf16[128,128]{1,0:T(8,128)(2,1)S(1)}, u32[]{:S(2)}, u32[]{:S(2)}) %collective-permute-start.3) | collective-permute-done | bytes 32800 | tf_op jit(solution)/shard_map/ppermute | solution.py:325
  20.8 0.7 %collective-permute-done.4.refs_5_ = bf16[128,128]{1,0:T(8,128)(2,1)S(1)} collective-permute-done((bf16[128,128]{1,0:T(8,128)(2,1)S(1)}, bf16[128,128]{1,0:T(8,128)(2,1)S(1)}, u32[]{:S(2)}, u32[]{:S(2)}) %collective-permute-start.4) | collective-permute-done | bytes 32800 | tf_op jit(solution)/shard_map/ppermute | solution.py:325
  21.5 2.2 %collective-permute-done.5.refs_6_ = bf16[128,128]{1,0:T(8,128)(2,1)S(1)} collective-permute-done((bf16[128,128]{1,0:T(8,128)(2,1)S(1)}, bf16[128,128]{1,0:T(8,128)(2,1)S(1)}, u32[]{:S(2)}, u32[]{:S(2)}) %collective-permute-start.5) | collective-permute-done | bytes 32800 | tf_op jit(solution)/shard_map/ppermute | solution.py:325
  25.1 8.7 %all_to_all.20.refs_0_ = bf16[8,128,128]{2,1,0:T(8,128)(2,1)S(1)} all-to-all(bf16[8,128,128]{2,1,0:T(8,128)(2,1)S(1)} %get-tuple-element.41), channel_id=1, replica_groups={{0,1,2,3,4,5,6,7},{8,9,10,11,12,13,14,15},{16,17,18,19,20,21,22,23},{24..., dimensions={0} | all-to-all | bytes 524288 | tf_op jit(solution)/shard_map/all_to_all | solution.py:317
  34.1 8.6 %all_to_all.21.refs_0_ = bf16[8,128,128]{2,1,0:T(8,128)(2,1)S(1)} all-to-all(bf16[8,128,128]{2,1,0:T(8,128)(2,1)S(1)} %middle.1), channel_id=1, replica_groups={{0,1,2,3,4,5,6,7},{8,9,10,11,12,13,14,15},{16,17,18,19,20,21,22,23},{24..., dimensions={0} | all-to-all | bytes 524288 | tf_op jit(solution)/shard_map/all_to_all | solution.py:317
  42.7 1.5 %d_right.1 = (bf16[16,128,128]{2,1,0:T(8,128)(2,1)}, bf16[16,64,128]{2,1,0:T(8,128)(2,1)S(1)}) custom-call(bf16[8,128,128]{2,1,0:T(8,128)(2,1)S(1)} %all_to_all.21.refs_0_, bf16[16,64,128]{2,1,0:T(8,128)(2,1)S(1)} %sort_left.1.refs_1_), custom_call_target="tpu_custom_call" | custom-call | flops 33554432 | bytes 1310720 | tf_op jit(solution)/shard_map/d_right/pallas_call | solution.py:65
  44.2 4.9 %all-to-all-start.3 = ((bf16[16,128,128]{2,1,0:T(8,128)(2,1)}), bf16[16,128,128]{2,1,0:T(8,128)(2,1)S(1)}, u32[]{:S(2)}, u32[]{:S(2)}) async-start(bf16[16,128,128]{2,1,0:T(8,128)(2,1)} %get-tuple-element.42), calls=%async_computation.3 | async-start | bytes 1048576 | tf_op jit(solution)/shard_map/all_to_all | solution.py:309
  49.7 1.5 %collective-permute-start.8 = (bf16[128,128]{1,0:T(8,128)(2,1)S(1)}, bf16[128,128]{1,0:T(8,128)(2,1)S(1)}, u32[]{:S(2)}, u32[]{:S(2)}) collective-permute-start(bf16[128,128]{1,0:T(8,128)(2,1)S(1)} %get-tuple-element.47), channel_id=1, source_target_pairs={{0,2},{1,3},{2,0},{3,1},{4,6},{5,7},{6,4},{7,5},{8,10},{9,11},{10,... | collective-permute-start | bytes 98312 | tf_op jit(solution)/shard_map/ppermute | solution.py:325
  51.7 1.5 %collective-permute-start.11 = (bf16[128,128]{1,0:T(8,128)(2,1)S(1)}, bf16[128,128]{1,0:T(8,128)(2,1)S(1)}, u32[]{:S(2)}, u32[]{:S(2)}) collective-permute-start(bf16[128,128]{1,0:T(8,128)(2,1)S(1)} %get-tuple-element.50), channel_id=1, source_target_pairs={{0,5},{1,4},{2,7},{3,6},{4,1},{5,0},{6,3},{7,2},{8,13},{9,12},{10,... | collective-permute-start | bytes 98312 | tf_op jit(solution)/shard_map/ppermute | solution.py:325
  53.2 1.5 %collective-permute-start.12 = (bf16[128,128]{1,0:T(8,128)(2,1)S(1)}, bf16[128,128]{1,0:T(8,128)(2,1)S(1)}, u32[]{:S(2)}, u32[]{:S(2)}) collective-permute-start(bf16[128,128]{1,0:T(8,128)(2,1)S(1)} %get-tuple-element.51), channel_id=1, source_target_pairs={{0,6},{1,7},{2,4},{3,5},{4,2},{5,3},{6,0},{7,1},{8,14},{9,15},{10,... | collective-permute-start | bytes 98312 | tf_op jit(solution)/shard_map/ppermute | solution.py:325
  54.7 2.2 %collective-permute-done.8.refs_2_ = bf16[128,128]{1,0:T(8,128)(2,1)S(1)} collective-permute-done((bf16[128,128]{1,0:T(8,128)(2,1)S(1)}, bf16[128,128]{1,0:T(8,128)(2,1)S(1)}, u32[]{:S(2)}, u32[]{:S(2)}) %collective-permute-start.8) | collective-permute-done | bytes 32800 | tf_op jit(solution)/shard_map/ppermute | solution.py:325
  56.9 0.7 %copy-done.10 = f32[128]{0:T(128)S(1)} copy-done((f32[128]{0:T(128)S(1)}, f32[128]{0:T(128)}, u32[]{:S(2)}) %copy-start.10) | copy-done | bytes 536
  58.0 1.0 %slopes.1 = (bf16[8,512,128]{2,1,0:T(8,128)(2,1)S(1)}, bf16[8,128,128]{2,1,0:T(8,128)(2,1)S(1)}, f32[8,128]{1,0:T(8,128)S(1)}, f32[128,128]{1,0:T(8,128)S(1)}, bf16[128,640]{1,0:T(8,128)(2,1)S(1)}) custom-call(bf16[8,128,128]{2,1,0:T(8,128)(2,1)S(1)} %copy-done.1, s32[1,128]{1,0:T(1,128)S(1)} %bitcast.15, f32[1,128]{1,0:T(1,128)S(1)} %bitcast.8, ...), custom_call_target="tpu_custom_call" | custom-call | flops 134217728 | bytes 2233856 | tf_op jit(solution)/shard_map/slopes/pallas_call | solution.py:65
  59.5 0.7 %collective-permute-done.11.refs_5_ = bf16[128,128]{1,0:T(8,128)(2,1)S(1)} collective-permute-done((bf16[128,128]{1,0:T(8,128)(2,1)S(1)}, bf16[128,128]{1,0:T(8,128)(2,1)S(1)}, u32[]{:S(2)}, u32[]{:S(2)}) %collective-permute-start.11) | collective-permute-done | bytes 32800 | tf_op jit(solution)/shard_map/ppermute | solution.py:325
  60.2 2.2 %collective-permute-done.12.refs_6_ = bf16[128,128]{1,0:T(8,128)(2,1)S(1)} collective-permute-done((bf16[128,128]{1,0:T(8,128)(2,1)S(1)}, bf16[128,128]{1,0:T(8,128)(2,1)S(1)}, u32[]{:S(2)}, u32[]{:S(2)}) %collective-permute-start.12) | collective-permute-done | bytes 32800 | tf_op jit(solution)/shard_map/ppermute | solution.py:325
  62.9 1.4 %finish.1 = bf16[8,128,128]{2,1,0:T(8,128)(2,1)} custom-call(bf16[16,128,128]{2,1,0:T(8,128)(2,1)S(1)} %all-to-all-done.3.refs_0_, bf16[8,128,128]{2,1,0:T(8,128)(2,1)S(1)} %sort_d_left.1.refs_1_, bf16[8,512,128]{2,1,0:T(8,128)(2,1)S(1)} %get-tuple-element.54.refs_2_, bf16[8,128,128]{2,1,0:T(8,128)(2,1)S(1)} %gate_back.1.refs_6_.refs_3_, ...), custom_call_target="tpu_custom_call" | custom-call | flops 134217728 | bytes 2854912 | tf_op jit(solution)/shard_map/finish/pallas_call | solution.py:65
  (44 shorter events, 5.7 us)
Async XLA Ops:
  2.4 8.0 %copy-start = (bf16[16,128,128]{2,1,0:T(8,128)(2,1)S(1)}, bf16[16,128,128]{2,1,0:T(8,128)(2,1)}, u32[]{:S(2)}) copy-start(bf16[16,128,128]{2,1,0:T(8,128)(2,1)} %project_right.1.refs_5_) | copy-start | bytes 1572868
  2.4 8.0 %copy-start.1 = (bf16[8,128,128]{2,1,0:T(8,128)(2,1)S(1)}, bf16[8,128,128]{2,1,0:T(8,128)(2,1)}, u32[]{:S(2)}) copy-start(bf16[8,128,128]{2,1,0:T(8,128)(2,1)} %refs_0_.7) | copy-start | bytes 786436
  2.4 8.0 %copy-start.2 = (bf16[128,512]{1,0:T(8,128)(2,1)S(1)}, bf16[128,512]{1,0:T(8,128)(2,1)}, u32[]{:S(2)}) copy-start(bf16[128,512]{1,0:T(8,128)(2,1)} %refs_4_.9) | copy-start | bytes 393220
  2.4 8.0 %copy-start.6 = (f32[128]{0:T(128)S(1)}, f32[128]{0:T(128)}, u32[]{:S(2)}) copy-start(f32[128]{0:T(128)} %param.13) | copy-start | bytes 1540
  2.4 8.0 %copy-start.7 = (f32[128]{0:T(128)S(1)}, f32[128]{0:T(128)}, u32[]{:S(2)}) copy-start(f32[128]{0:T(128)} %param.14) | copy-start | bytes 1540
  2.5 8.0 %copy-start.8 = (s32[128]{0:T(128)S(1)}, s32[128]{0:T(128)}, u32[]{:S(2)}) copy-start(s32[128]{0:T(128)} %param.12) | copy-start | bytes 1540
  2.5 21.9 %all-to-all-start = ((bf16[16,128,128]{2,1,0:T(8,128)(2,1)}), bf16[16,128,128]{2,1,0:T(8,128)(2,1)S(1)}, u32[]{:S(2)}, u32[]{:S(2)}) async-start(bf16[16,128,128]{2,1,0:T(8,128)(2,1)} %project_right.1.refs_5_), calls=%async_computation | async-start | bytes 1048576 | tf_op jit(solution)/shard_map/all_to_all | solution.py:309
  10.5 7.7 %copy-start.3 = (bf16[8,128,128]{2,1,0:T(8,128)(2,1)S(1)}, bf16[8,128,128]{2,1,0:T(8,128)(2,1)}, u32[]{:S(2)}) copy-start(bf16[8,128,128]{2,1,0:T(8,128)(2,1)} %refs_1_.1) | copy-start | bytes 786436
  10.5 7.7 %copy-start.4 = (bf16[128,128]{1,0:T(8,128)(2,1)S(1)}, bf16[128,128]{1,0:T(8,128)(2,1)}, u32[]{:S(2)}) copy-start(bf16[128,128]{1,0:T(8,128)(2,1)} %refs_4_.8) | copy-start | bytes 98308
  11.3 3.7 %collective-permute-start = (bf16[128,128]{1,0:T(8,128)(2,1)S(1)}, bf16[128,128]{1,0:T(8,128)(2,1)S(1)}, u32[]{:S(2)}, u32[]{:S(2)}) collective-permute-start(bf16[128,128]{1,0:T(8,128)(2,1)S(1)} %get-tuple-element.33), channel_id=1, source_target_pairs={{0,1},{1,0},{2,3},{3,2},{4,5},{5,4},{6,7},{7,6},{8,9},{9,8},{10,11... | collective-permute-start | bytes 98312 | tf_op jit(solution)/shard_map/ppermute | solution.py:325
  11.5 6.7 %collective-permute-start.1 = (bf16[128,128]{1,0:T(8,128)(2,1)S(1)}, bf16[128,128]{1,0:T(8,128)(2,1)S(1)}, u32[]{:S(2)}, u32[]{:S(2)}) collective-permute-start(bf16[128,128]{1,0:T(8,128)(2,1)S(1)} %get-tuple-element.34), channel_id=1, source_target_pairs={{0,2},{1,3},{2,0},{3,1},{4,6},{5,7},{6,4},{7,5},{8,10},{9,11},{10,... | collective-permute-start | bytes 98312 | tf_op jit(solution)/shard_map/ppermute | solution.py:325
  13.0 6.7 %collective-permute-start.2 = (bf16[128,128]{1,0:T(8,128)(2,1)S(1)}, bf16[128,128]{1,0:T(8,128)(2,1)S(1)}, u32[]{:S(2)}, u32[]{:S(2)}) collective-permute-start(bf16[128,128]{1,0:T(8,128)(2,1)S(1)} %get-tuple-element.35), channel_id=1, source_target_pairs={{0,3},{1,2},{2,1},{3,0},{4,7},{5,6},{6,5},{7,4},{8,11},{9,10},{10,... | collective-permute-start | bytes 98312 | tf_op jit(solution)/shard_map/ppermute | solution.py:325
  13.3 7.5 %collective-permute-start.3 = (bf16[128,128]{1,0:T(8,128)(2,1)S(1)}, bf16[128,128]{1,0:T(8,128)(2,1)S(1)}, u32[]{:S(2)}, u32[]{:S(2)}) collective-permute-start(bf16[128,128]{1,0:T(8,128)(2,1)S(1)} %get-tuple-element.36), channel_id=1, source_target_pairs={{0,4},{1,5},{2,6},{3,7},{4,0},{5,1},{6,2},{7,3},{8,12},{9,13},{10,... | collective-permute-start | bytes 98312 | tf_op jit(solution)/shard_map/ppermute | solution.py:325
  13.6 7.9 %collective-permute-start.4 = (bf16[128,128]{1,0:T(8,128)(2,1)S(1)}, bf16[128,128]{1,0:T(8,128)(2,1)S(1)}, u32[]{:S(2)}, u32[]{:S(2)}) collective-permute-start(bf16[128,128]{1,0:T(8,128)(2,1)S(1)} %get-tuple-element.37), channel_id=1, source_target_pairs={{0,5},{1,4},{2,7},{3,6},{4,1},{5,0},{6,3},{7,2},{8,13},{9,12},{10,... | collective-permute-start | bytes 98312 | tf_op jit(solution)/shard_map/ppermute | solution.py:325
  15.1 8.6 %collective-permute-start.5 = (bf16[128,128]{1,0:T(8,128)(2,1)S(1)}, bf16[128,128]{1,0:T(8,128)(2,1)S(1)}, u32[]{:S(2)}, u32[]{:S(2)}) collective-permute-start(bf16[128,128]{1,0:T(8,128)(2,1)S(1)} %get-tuple-element.38), channel_id=1, source_target_pairs={{0,6},{1,7},{2,4},{3,5},{4,2},{5,3},{6,0},{7,1},{8,14},{9,15},{10,... | collective-permute-start | bytes 98312 | tf_op jit(solution)/shard_map/ppermute | solution.py:325
  18.2 6.0 %collective-permute-start.6 = (bf16[128,128]{1,0:T(8,128)(2,1)S(1)}, bf16[128,128]{1,0:T(8,128)(2,1)S(1)}, u32[]{:S(2)}, u32[]{:S(2)}) collective-permute-start(bf16[128,128]{1,0:T(8,128)(2,1)S(1)} %get-tuple-element.39), channel_id=1, source_target_pairs={{0,7},{1,6},{2,5},{3,4},{4,3},{5,2},{6,1},{7,0},{8,15},{9,14},{10,... | collective-permute-start | bytes 98312 | tf_op jit(solution)/shard_map/ppermute | solution.py:325
  44.2 18.7 %all-to-all-start.3 = ((bf16[16,128,128]{2,1,0:T(8,128)(2,1)}), bf16[16,128,128]{2,1,0:T(8,128)(2,1)S(1)}, u32[]{:S(2)}, u32[]{:S(2)}) async-start(bf16[16,128,128]{2,1,0:T(8,128)(2,1)} %get-tuple-element.42), calls=%async_computation.3 | async-start | bytes 1048576 | tf_op jit(solution)/shard_map/all_to_all | solution.py:309
  49.5 3.7 %collective-permute-start.7 = (bf16[128,128]{1,0:T(8,128)(2,1)S(1)}, bf16[128,128]{1,0:T(8,128)(2,1)S(1)}, u32[]{:S(2)}, u32[]{:S(2)}) collective-permute-start(bf16[128,128]{1,0:T(8,128)(2,1)S(1)} %get-tuple-element.46), channel_id=1, source_target_pairs={{0,1},{1,0},{2,3},{3,2},{4,5},{5,4},{6,7},{7,6},{8,9},{9,8},{10,11... | collective-permute-start | bytes 98312 | tf_op jit(solution)/shard_map/ppermute | solution.py:325
  49.7 7.2 %collective-permute-start.8 = (bf16[128,128]{1,0:T(8,128)(2,1)S(1)}, bf16[128,128]{1,0:T(8,128)(2,1)S(1)}, u32[]{:S(2)}, u32[]{:S(2)}) collective-permute-start(bf16[128,128]{1,0:T(8,128)(2,1)S(1)} %get-tuple-element.47), channel_id=1, source_target_pairs={{0,2},{1,3},{2,0},{3,1},{4,6},{5,7},{6,4},{7,5},{8,10},{9,11},{10,... | collective-permute-start | bytes 98312 | tf_op jit(solution)/shard_map/ppermute | solution.py:325
  51.2 7.9 %collective-permute-start.9 = (bf16[128,128]{1,0:T(8,128)(2,1)S(1)}, bf16[128,128]{1,0:T(8,128)(2,1)S(1)}, u32[]{:S(2)}, u32[]{:S(2)}) collective-permute-start(bf16[128,128]{1,0:T(8,128)(2,1)S(1)} %get-tuple-element.48), channel_id=1, source_target_pairs={{0,3},{1,2},{2,1},{3,0},{4,7},{5,6},{6,5},{7,4},{8,11},{9,10},{10,... | collective-permute-start | bytes 98312 | tf_op jit(solution)/shard_map/ppermute | solution.py:325
  51.4 8.1 %collective-permute-start.10 = (bf16[128,128]{1,0:T(8,128)(2,1)S(1)}, bf16[128,128]{1,0:T(8,128)(2,1)S(1)}, u32[]{:S(2)}, u32[]{:S(2)}) collective-permute-start(bf16[128,128]{1,0:T(8,128)(2,1)S(1)} %get-tuple-element.49), channel_id=1, source_target_pairs={{0,4},{1,5},{2,6},{3,7},{4,0},{5,1},{6,2},{7,3},{8,12},{9,13},{10,... | collective-permute-start | bytes 98312 | tf_op jit(solution)/shard_map/ppermute | solution.py:325
  51.7 8.4 %collective-permute-start.11 = (bf16[128,128]{1,0:T(8,128)(2,1)S(1)}, bf16[128,128]{1,0:T(8,128)(2,1)S(1)}, u32[]{:S(2)}, u32[]{:S(2)}) collective-permute-start(bf16[128,128]{1,0:T(8,128)(2,1)S(1)} %get-tuple-element.50), channel_id=1, source_target_pairs={{0,5},{1,4},{2,7},{3,6},{4,1},{5,0},{6,3},{7,2},{8,13},{9,12},{10,... | collective-permute-start | bytes 98312 | tf_op jit(solution)/shard_map/ppermute | solution.py:325
  53.2 9.1 %collective-permute-start.12 = (bf16[128,128]{1,0:T(8,128)(2,1)S(1)}, bf16[128,128]{1,0:T(8,128)(2,1)S(1)}, u32[]{:S(2)}, u32[]{:S(2)}) collective-permute-start(bf16[128,128]{1,0:T(8,128)(2,1)S(1)} %get-tuple-element.51), channel_id=1, source_target_pairs={{0,6},{1,7},{2,4},{3,5},{4,2},{5,3},{6,0},{7,1},{8,14},{9,15},{10,... | collective-permute-start | bytes 98312 | tf_op jit(solution)/shard_map/ppermute | solution.py:325
  56.9 6.0 %collective-permute-start.13 = (bf16[128,128]{1,0:T(8,128)(2,1)S(1)}, bf16[128,128]{1,0:T(8,128)(2,1)S(1)}, u32[]{:S(2)}, u32[]{:S(2)}) collective-permute-start(bf16[128,128]{1,0:T(8,128)(2,1)S(1)} %get-tuple-element.52), channel_id=1, source_target_pairs={{0,7},{1,6},{2,5},{3,4},{4,3},{5,2},{6,1},{7,0},{8,15},{9,14},{10,... | collective-permute-start | bytes 98312 | tf_op jit(solution)/shard_map/ppermute | solution.py:325
  (3 other events, 9.0 us)

commit v13 on v12

--- a/solution.py
+++ b/solution.py
@@ -96,8 +96,12 @@
     return [device for place in range(count) for device in (inner[place], count + place)]
 
 
+def distance(step, count):
+    return (count - step) % count
+
+
 def partner(step, count):
-    return lax.rem(lax.axis_index("row"), count) ^ step
+    return lax.rem(lax.axis_index("row"), count) ^ distance(step, count)
 
 
 def gated_rows(pair, mask, gain, bias, w_proj, side):
@@ -321,11 +325,11 @@
 
 def swap_pieces(pieces):
     devices = range(lax.axis_size("row"))
-    swapped = [
-        lax.ppermute(pieces[step], "row", [(d, d ^ step) for d in devices])
-        for step in range(len(pieces) - 1, 0, -1)
+    count = len(pieces)
+    return [pieces[0]] + [
+        lax.ppermute(pieces[step], "row", [(d, d ^ distance(step, count)) for d in devices])
+        for step in range(1, count)
     ]
-    return [pieces[0]] + swapped[::-1]
 
 
 def kernel_shards(

time: 64.8 us -> 67.3 us (1.039)
  starting transfers between devices: 23.3 us -> 27.4 us
  waiting for transfers between devices: 12.3 us -> 9.22 us
  blocking collectives: 17.4 us -> 18.5 us
    ppermute x14, starting transfers between devices: 10.4 us -> 14.4 us  [swap_pieces(): lax.ppermute(pieces[step], 'row', [(d, d ^ distance(step, count)) for d i...]
    ppermute x14, waiting for transfers between devices: 12.3 us -> 9.21 us  [swap_pieces(): lax.ppermute(pieces[step], 'row', [(d, d ^ distance(step, count)) for d i...]
    all_to_all x2, blocking collectives: 17.4 us -> 18.5 us  [swap_half(): lax.all_to_all(values, 'row', split_axis=0, concat_axis=0, tiled=True, ax...]
  transfers between devices with their start and end apart: 16 -> 16, of which waited for: 10 -> 4; matrix products, arithmetic and copies ran while one was open for 0% -> 0% of each run, Pallas kernels for 6% -> 5%
where the time goes in v13:
time: 67.3 us; the launch traced here: 66.5 us
  starting transfers between devices  27.4 us (41%)
  blocking collectives  18.5 us (27%)
  Pallas kernels  9.82 us (15%)
  waiting for transfers between devices  9.22 us (14%)
  local copies, waits for them, and re-layouts  1.33 us (2%)
    all_to_all x2, blocking collectives, swap_half(): lax.all_to_all(values, 'row', split_axis=0, concat_axis=0, tiled=True, ax...  18.5 us
    ppermute x14, starting transfers between devices, swap_pieces(): lax.ppermute(pieces[step], 'row', [(d, d ^ distance(step, count)) for d i...  14.4 us
    all_to_all x2, starting transfers between devices, swap(): lax.all_to_all(values, 'row', split_axis=0, concat_axis=0, tiled=True, ax...  13 us
    pallas_call x12, Pallas kernels, call(): pl.pallas_call(body, name=name, out_shape=outs, in_specs=[pl.BlockSpec(me...  9.82 us
    ppermute x14, waiting for transfers between devices, swap_pieces(): lax.ppermute(pieces[step], 'row', [(d, d ^ distance(step, count)) for d i...  9.21 us
  transfers between devices with their start and end apart: 16, of which 4 were waited for; matrix products, arithmetic and copies ran while one was open for 0% of the time, Pallas kernels for 5%

profile of v13, /device:TPU:0, one launch (start us, length us, event | category | flops | bytes accessed | tf_op | source)
XLA Modules:
  0.0 66.5 jit_solution(16452876252633461228)
XLA Ops:
  0.0 2.4 %project_right.1.refs_5_ = bf16[16,128,128]{2,1,0:T(8,128)(2,1)} custom-call(bf16[8,128,128]{2,1,0:T(8,128)(2,1)} %refs_0_.7, s32[1,128]{1,0:T(1,128)} %bitcast.13, f32[1,128]{1,0:T(1,128)} %bitcast.5, f32[1,128]{1,0:T(1,128)} %bitcast.9, bf16[128,512]{1,0:T(8,128)(2,1)} %refs_4_.9), custom_call_target="tpu_custom_call" | custom-call | flops 67108864 | bytes 919040 | tf_op jit(solution)/shard_map/project_right/pallas_call | solution.py:65
  2.5 8.0 %all-to-all-start = ((bf16[16,128,128]{2,1,0:T(8,128)(2,1)}), bf16[16,128,128]{2,1,0:T(8,128)(2,1)S(1)}, u32[]{:S(2)}, u32[]{:S(2)}) async-start(bf16[16,128,128]{2,1,0:T(8,128)(2,1)} %project_right.1.refs_5_), calls=%async_computation | async-start | bytes 1048576 | tf_op jit(solution)/shard_map/all_to_all | solution.py:313
  10.5 0.8 %project_left.1 = (bf16[128,128]{1,0:T(8,128)(2,1)S(1)}, bf16[128,128]{1,0:T(8,128)(2,1)S(1)}, bf16[128,128]{1,0:T(8,128)(2,1)S(1)}, bf16[128,128]{1,0:T(8,128)(...) custom-call(bf16[8,128,128]{2,1,0:T(8,128)(2,1)S(1)} %copy-done.1, ...), custom_call_target="tpu_custom_call" | custom-call | flops 67108864 | bytes 1181184 | tf_op jit(solution)/shard_map/project_left/pallas_call | solution.py:65
  11.3 1.3 %collective-permute-start = (bf16[128,128]{1,0:T(8,128)(2,1)S(1)}, bf16[128,128]{1,0:T(8,128)(2,1)S(1)}, u32[]{:S(2)}, u32[]{:S(2)}) collective-permute-start(bf16[128,128]{1,0:T(8,128)(2,1)S(1)} %get-tuple-element.33), channel_id=1, source_target_pairs={{0,7},{1,6},{2,5},{3,4},{4,3},{5,2},{6,1},{7,0},{8,15},{9,14},{10,... | collective-permute-start | bytes 98312 | tf_op jit(solution)/shard_map/ppermute | solution.py:330
  12.6 1.5 %collective-permute-start.1 = (bf16[128,128]{1,0:T(8,128)(2,1)S(1)}, bf16[128,128]{1,0:T(8,128)(2,1)S(1)}, u32[]{:S(2)}, u32[]{:S(2)}) collective-permute-start(bf16[128,128]{1,0:T(8,128)(2,1)S(1)} %get-tuple-element.34), channel_id=1, source_target_pairs={{0,6},{1,7},{2,4},{3,5},{4,2},{5,3},{6,0},{7,1},{8,14},{9,15},{10,... | collective-permute-start | bytes 98312 | tf_op jit(solution)/shard_map/ppermute | solution.py:330
  14.1 1.7 %collective-permute-start.3 = (bf16[128,128]{1,0:T(8,128)(2,1)S(1)}, bf16[128,128]{1,0:T(8,128)(2,1)S(1)}, u32[]{:S(2)}, u32[]{:S(2)}) collective-permute-start(bf16[128,128]{1,0:T(8,128)(2,1)S(1)} %get-tuple-element.36), channel_id=1, source_target_pairs={{0,4},{1,5},{2,6},{3,7},{4,0},{5,1},{6,2},{7,3},{8,12},{9,13},{10,... | collective-permute-start | bytes 98312 | tf_op jit(solution)/shard_map/ppermute | solution.py:330
  15.8 1.2 %collective-permute-start.4 = (bf16[128,128]{1,0:T(8,128)(2,1)S(1)}, bf16[128,128]{1,0:T(8,128)(2,1)S(1)}, u32[]{:S(2)}, u32[]{:S(2)}) collective-permute-start(bf16[128,128]{1,0:T(8,128)(2,1)S(1)} %get-tuple-element.37), channel_id=1, source_target_pairs={{0,3},{1,2},{2,1},{3,0},{4,7},{5,6},{6,5},{7,4},{8,11},{9,10},{10,... | collective-permute-start | bytes 98312 | tf_op jit(solution)/shard_map/ppermute | solution.py:330
  17.0 3.8 %collective-permute-done.refs_1_ = bf16[128,128]{1,0:T(8,128)(2,1)S(1)} collective-permute-done((bf16[128,128]{1,0:T(8,128)(2,1)S(1)}, bf16[128,128]{1,0:T(8,128)(2,1)S(1)}, u32[]{:S(2)}, u32[]{:S(2)}) %collective-permute-start) | collective-permute-done | bytes 32800 | tf_op jit(solution)/shard_map/ppermute | solution.py:330
  20.8 1.5 %collective-permute-start.5 = (bf16[128,128]{1,0:T(8,128)(2,1)S(1)}, bf16[128,128]{1,0:T(8,128)(2,1)S(1)}, u32[]{:S(2)}, u32[]{:S(2)}) collective-permute-start(bf16[128,128]{1,0:T(8,128)(2,1)S(1)} %get-tuple-element.38), channel_id=1, source_target_pairs={{0,2},{1,3},{2,0},{3,1},{4,6},{5,7},{6,4},{7,5},{8,10},{9,11},{10,... | collective-permute-start | bytes 98312 | tf_op jit(solution)/shard_map/ppermute | solution.py:330
  23.0 0.8 %prepare.1 = (f32[8,128,128]{2,1,0:T(8,128)S(1)}, f32[8,128,128]{2,1,0:T(8,128)S(1)}) custom-call(bf16[8,128,128]{2,1,0:T(8,128)(2,1)S(1)} %copy-done.1, bf16[8,128,128]{2,1,0:T(8,128)(2,1)S(1)} %copy-done.3, f32[1,128]{1,0:T(1,128)S(1)} %bitcast.7, f32[1,128]{1,0:T(1,128)S(1)} %bitcast.11, bf16[128,128]{1,0:T(8,128)(2,1)S(1)} %copy-done.5, ...), custom_call_target="tpu_custom_call" | custom-call | flops 67108864 | bytes 1639936 | tf_op jit(solution)/shard_map/prepare/pallas_call | solution.py:65
  23.8 0.9 %collective-permute-done.5.refs_6_ = bf16[128,128]{1,0:T(8,128)(2,1)S(1)} collective-permute-done((bf16[128,128]{1,0:T(8,128)(2,1)S(1)}, bf16[128,128]{1,0:T(8,128)(2,1)S(1)}, u32[]{:S(2)}, u32[]{:S(2)}) %collective-permute-start.5) | collective-permute-done | bytes 32800 | tf_op jit(solution)/shard_map/ppermute | solution.py:330
  25.6 9.9 %all_to_all.20.refs_0_ = bf16[8,128,128]{2,1,0:T(8,128)(2,1)S(1)} all-to-all(bf16[8,128,128]{2,1,0:T(8,128)(2,1)S(1)} %get-tuple-element.41), channel_id=1, replica_groups={{0,1,2,3,4,5,6,7},{8,9,10,11,12,13,14,15},{16,17,18,19,20,21,22,23},{24..., dimensions={0} | all-to-all | bytes 524288 | tf_op jit(solution)/shard_map/all_to_all | solution.py:321
  35.7 8.6 %all_to_all.21.refs_0_ = bf16[8,128,128]{2,1,0:T(8,128)(2,1)S(1)} all-to-all(bf16[8,128,128]{2,1,0:T(8,128)(2,1)S(1)} %middle.1), channel_id=1, replica_groups={{0,1,2,3,4,5,6,7},{8,9,10,11,12,13,14,15},{16,17,18,19,20,21,22,23},{24..., dimensions={0} | all-to-all | bytes 524288 | tf_op jit(solution)/shard_map/all_to_all | solution.py:321
  44.3 1.5 %d_right.1 = (bf16[16,128,128]{2,1,0:T(8,128)(2,1)}, bf16[16,64,128]{2,1,0:T(8,128)(2,1)S(1)}) custom-call(bf16[8,128,128]{2,1,0:T(8,128)(2,1)S(1)} %all_to_all.21.refs_0_, bf16[16,64,128]{2,1,0:T(8,128)(2,1)S(1)} %sort_left.1.refs_1_), custom_call_target="tpu_custom_call" | custom-call | flops 33554432 | bytes 1310720 | tf_op jit(solution)/shard_map/d_right/pallas_call | solution.py:65
  45.8 5.0 %all-to-all-start.3 = ((bf16[16,128,128]{2,1,0:T(8,128)(2,1)}), bf16[16,128,128]{2,1,0:T(8,128)(2,1)S(1)}, u32[]{:S(2)}, u32[]{:S(2)}) async-start(bf16[16,128,128]{2,1,0:T(8,128)(2,1)} %get-tuple-element.42), calls=%async_computation.3 | async-start | bytes 1048576 | tf_op jit(solution)/shard_map/all_to_all | solution.py:313
  51.2 1.3 %collective-permute-start.7 = (bf16[128,128]{1,0:T(8,128)(2,1)S(1)}, bf16[128,128]{1,0:T(8,128)(2,1)S(1)}, u32[]{:S(2)}, u32[]{:S(2)}) collective-permute-start(bf16[128,128]{1,0:T(8,128)(2,1)S(1)} %get-tuple-element.46), channel_id=1, source_target_pairs={{0,7},{1,6},{2,5},{3,4},{4,3},{5,2},{6,1},{7,0},{8,15},{9,14},{10,... | collective-permute-start | bytes 98312 | tf_op jit(solution)/shard_map/ppermute | solution.py:330
  52.5 1.5 %collective-permute-start.8 = (bf16[128,128]{1,0:T(8,128)(2,1)S(1)}, bf16[128,128]{1,0:T(8,128)(2,1)S(1)}, u32[]{:S(2)}, u32[]{:S(2)}) collective-permute-start(bf16[128,128]{1,0:T(8,128)(2,1)S(1)} %get-tuple-element.47), channel_id=1, source_target_pairs={{0,6},{1,7},{2,4},{3,5},{4,2},{5,3},{6,0},{7,1},{8,14},{9,15},{10,... | collective-permute-start | bytes 98312 | tf_op jit(solution)/shard_map/ppermute | solution.py:330
  53.9 1.7 %collective-permute-start.10 = (bf16[128,128]{1,0:T(8,128)(2,1)S(1)}, bf16[128,128]{1,0:T(8,128)(2,1)S(1)}, u32[]{:S(2)}, u32[]{:S(2)}) collective-permute-start(bf16[128,128]{1,0:T(8,128)(2,1)S(1)} %get-tuple-element.49), channel_id=1, source_target_pairs={{0,4},{1,5},{2,6},{3,7},{4,0},{5,1},{6,2},{7,3},{8,12},{9,13},{10,... | collective-permute-start | bytes 98312 | tf_op jit(solution)/shard_map/ppermute | solution.py:330
  55.6 1.2 %collective-permute-start.11 = (bf16[128,128]{1,0:T(8,128)(2,1)S(1)}, bf16[128,128]{1,0:T(8,128)(2,1)S(1)}, u32[]{:S(2)}, u32[]{:S(2)}) collective-permute-start(bf16[128,128]{1,0:T(8,128)(2,1)S(1)} %get-tuple-element.50), channel_id=1, source_target_pairs={{0,3},{1,2},{2,1},{3,0},{4,7},{5,6},{6,5},{7,4},{8,11},{9,10},{10,... | collective-permute-start | bytes 98312 | tf_op jit(solution)/shard_map/ppermute | solution.py:330
  56.9 4.3 %collective-permute-done.7.refs_1_ = bf16[128,128]{1,0:T(8,128)(2,1)S(1)} collective-permute-done((bf16[128,128]{1,0:T(8,128)(2,1)S(1)}, bf16[128,128]{1,0:T(8,128)(2,1)S(1)}, u32[]{:S(2)}, u32[]{:S(2)}) %collective-permute-start.7) | collective-permute-done | bytes 32800 | tf_op jit(solution)/shard_map/ppermute | solution.py:330
  61.2 1.5 %collective-permute-start.12 = (bf16[128,128]{1,0:T(8,128)(2,1)S(1)}, bf16[128,128]{1,0:T(8,128)(2,1)S(1)}, u32[]{:S(2)}, u32[]{:S(2)}) collective-permute-start(bf16[128,128]{1,0:T(8,128)(2,1)S(1)} %get-tuple-element.51), channel_id=1, source_target_pairs={{0,2},{1,3},{2,0},{3,1},{4,6},{5,7},{6,4},{7,5},{8,10},{9,11},{10,... | collective-permute-start | bytes 98312 | tf_op jit(solution)/shard_map/ppermute | solution.py:330
  62.7 0.7 copy-done.10
  63.8 1.0 %slopes.1 = (bf16[8,512,128]{2,1,0:T(8,128)(2,1)S(1)}, bf16[8,128,128]{2,1,0:T(8,128)(2,1)S(1)}, f32[8,128]{1,0:T(8,128)S(1)}, f32[128,128]{1,0:T(8,128)S(1)}, bf16[128,640]{1,0:T(8,128)(2,1)S(1)}) custom-call(bf16[8,128,128]{2,1,0:T(8,128)(2,1)S(1)} %copy-done.1, s32[1,128]{1,0:T(1,128)S(1)} %bitcast.15, f32[1,128]{1,0:T(1,128)S(1)} %bitcast.8, ...), custom_call_target="tpu_custom_call" | custom-call | flops 134217728 | bytes 2233856 | tf_op jit(solution)/shard_map/slopes/pallas_call | solution.py:65
  65.1 1.4 %finish.1 = bf16[8,128,128]{2,1,0:T(8,128)(2,1)} custom-call(bf16[16,128,128]{2,1,0:T(8,128)(2,1)S(1)} %all-to-all-done.3.refs_0_, bf16[8,128,128]{2,1,0:T(8,128)(2,1)S(1)} %sort_d_left.1.refs_1_, bf16[8,512,128]{2,1,0:T(8,128)(2,1)S(1)} %get-tuple-element.54.refs_2_, bf16[8,128,128]{2,1,0:T(8,128)(2,1)S(1)} %gate_back.1.refs_6_.refs_3_, ...), custom_call_target="tpu_custom_call" | custom-call | flops 134217728 | bytes 2854912 | tf_op jit(solution)/shard_map/finish/pallas_call | solution.py:65
  (44 shorter events, 2.9 us)
Async XLA Ops:
  2.4 8.0 %copy-start = (bf16[16,128,128]{2,1,0:T(8,128)(2,1)S(1)}, bf16[16,128,128]{2,1,0:T(8,128)(2,1)}, u32[]{:S(2)}) copy-start(bf16[16,128,128]{2,1,0:T(8,128)(2,1)} %project_right.1.refs_5_) | copy-start | bytes 1572868
  2.4 8.0 %copy-start.1 = (bf16[8,128,128]{2,1,0:T(8,128)(2,1)S(1)}, bf16[8,128,128]{2,1,0:T(8,128)(2,1)}, u32[]{:S(2)}) copy-start(bf16[8,128,128]{2,1,0:T(8,128)(2,1)} %refs_0_.7) | copy-start | bytes 786436
  2.4 8.0 %copy-start.2 = (bf16[128,512]{1,0:T(8,128)(2,1)S(1)}, bf16[128,512]{1,0:T(8,128)(2,1)}, u32[]{:S(2)}) copy-start(bf16[128,512]{1,0:T(8,128)(2,1)} %refs_4_.9) | copy-start | bytes 393220
  2.4 8.0 %copy-start.6 = (f32[128]{0:T(128)S(1)}, f32[128]{0:T(128)}, u32[]{:S(2)}) copy-start(f32[128]{0:T(128)} %param.13) | copy-start | bytes 1540
  2.4 8.0 %copy-start.7 = (f32[128]{0:T(128)S(1)}, f32[128]{0:T(128)}, u32[]{:S(2)}) copy-start(f32[128]{0:T(128)} %param.14) | copy-start | bytes 1540
  2.5 22.4 %all-to-all-start = ((bf16[16,128,128]{2,1,0:T(8,128)(2,1)}), bf16[16,128,128]{2,1,0:T(8,128)(2,1)S(1)}, u32[]{:S(2)}, u32[]{:S(2)}) async-start(bf16[16,128,128]{2,1,0:T(8,128)(2,1)} %project_right.1.refs_5_), calls=%async_computation | async-start | bytes 1048576 | tf_op jit(solution)/shard_map/all_to_all | solution.py:313
  10.5 11.8 %copy-start.3 = (bf16[8,128,128]{2,1,0:T(8,128)(2,1)S(1)}, bf16[8,128,128]{2,1,0:T(8,128)(2,1)}, u32[]{:S(2)}) copy-start(bf16[8,128,128]{2,1,0:T(8,128)(2,1)} %refs_1_.1) | copy-start | bytes 786436
  10.5 11.8 %copy-start.4 = (bf16[128,128]{1,0:T(8,128)(2,1)S(1)}, bf16[128,128]{1,0:T(8,128)(2,1)}, u32[]{:S(2)}) copy-start(bf16[128,128]{1,0:T(8,128)(2,1)} %refs_4_.8) | copy-start | bytes 98308
  10.5 11.8 %copy-start.5 = (bf16[128,128]{1,0:T(8,128)(2,1)S(1)}, bf16[128,128]{1,0:T(8,128)(2,1)}, u32[]{:S(2)}) copy-start(bf16[128,128]{1,0:T(8,128)(2,1)} %refs_5_.1) | copy-start | bytes 98308
  11.3 9.5 %collective-permute-start = (bf16[128,128]{1,0:T(8,128)(2,1)S(1)}, bf16[128,128]{1,0:T(8,128)(2,1)S(1)}, u32[]{:S(2)}, u32[]{:S(2)}) collective-permute-start(bf16[128,128]{1,0:T(8,128)(2,1)S(1)} %get-tuple-element.33), channel_id=1, source_target_pairs={{0,7},{1,6},{2,5},{3,4},{4,3},{5,2},{6,1},{7,0},{8,15},{9,14},{10,... | collective-permute-start | bytes 98312 | tf_op jit(solution)/shard_map/ppermute | solution.py:330
  12.6 9.7 %collective-permute-start.1 = (bf16[128,128]{1,0:T(8,128)(2,1)S(1)}, bf16[128,128]{1,0:T(8,128)(2,1)S(1)}, u32[]{:S(2)}, u32[]{:S(2)}) collective-permute-start(bf16[128,128]{1,0:T(8,128)(2,1)S(1)} %get-tuple-element.34), channel_id=1, source_target_pairs={{0,6},{1,7},{2,4},{3,5},{4,2},{5,3},{6,0},{7,1},{8,14},{9,15},{10,... | collective-permute-start | bytes 98312 | tf_op jit(solution)/shard_map/ppermute | solution.py:330
  14.1 9.7 %collective-permute-start.2 = (bf16[128,128]{1,0:T(8,128)(2,1)S(1)}, bf16[128,128]{1,0:T(8,128)(2,1)S(1)}, u32[]{:S(2)}, u32[]{:S(2)}) collective-permute-start(bf16[128,128]{1,0:T(8,128)(2,1)S(1)} %get-tuple-element.35), channel_id=1, source_target_pairs={{0,5},{1,4},{2,7},{3,6},{4,1},{5,0},{6,3},{7,2},{8,13},{9,12},{10,... | collective-permute-start | bytes 98312 | tf_op jit(solution)/shard_map/ppermute | solution.py:330
  14.1 9.7 %collective-permute-start.3 = (bf16[128,128]{1,0:T(8,128)(2,1)S(1)}, bf16[128,128]{1,0:T(8,128)(2,1)S(1)}, u32[]{:S(2)}, u32[]{:S(2)}) collective-permute-start(bf16[128,128]{1,0:T(8,128)(2,1)S(1)} %get-tuple-element.36), channel_id=1, source_target_pairs={{0,4},{1,5},{2,6},{3,7},{4,0},{5,1},{6,2},{7,3},{8,12},{9,13},{10,... | collective-permute-start | bytes 98312 | tf_op jit(solution)/shard_map/ppermute | solution.py:330
  15.8 8.0 %collective-permute-start.4 = (bf16[128,128]{1,0:T(8,128)(2,1)S(1)}, bf16[128,128]{1,0:T(8,128)(2,1)S(1)}, u32[]{:S(2)}, u32[]{:S(2)}) collective-permute-start(bf16[128,128]{1,0:T(8,128)(2,1)S(1)} %get-tuple-element.37), channel_id=1, source_target_pairs={{0,3},{1,2},{2,1},{3,0},{4,7},{5,6},{6,5},{7,4},{8,11},{9,10},{10,... | collective-permute-start | bytes 98312 | tf_op jit(solution)/shard_map/ppermute | solution.py:330
  20.8 3.9 %collective-permute-start.5 = (bf16[128,128]{1,0:T(8,128)(2,1)S(1)}, bf16[128,128]{1,0:T(8,128)(2,1)S(1)}, u32[]{:S(2)}, u32[]{:S(2)}) collective-permute-start(bf16[128,128]{1,0:T(8,128)(2,1)S(1)} %get-tuple-element.38), channel_id=1, source_target_pairs={{0,2},{1,3},{2,0},{3,1},{4,6},{5,7},{6,4},{7,5},{8,10},{9,11},{10,... | collective-permute-start | bytes 98312 | tf_op jit(solution)/shard_map/ppermute | solution.py:330
  22.3 2.4 %collective-permute-start.6 = (bf16[128,128]{1,0:T(8,128)(2,1)S(1)}, bf16[128,128]{1,0:T(8,128)(2,1)S(1)}, u32[]{:S(2)}, u32[]{:S(2)}) collective-permute-start(bf16[128,128]{1,0:T(8,128)(2,1)S(1)} %get-tuple-element.39), channel_id=1, source_target_pairs={{0,1},{1,0},{2,3},{3,2},{4,5},{5,4},{6,7},{7,6},{8,9},{9,8},{10,11... | collective-permute-start | bytes 98312 | tf_op jit(solution)/shard_map/ppermute | solution.py:330
  45.8 19.3 %all-to-all-start.3 = ((bf16[16,128,128]{2,1,0:T(8,128)(2,1)}), bf16[16,128,128]{2,1,0:T(8,128)(2,1)S(1)}, u32[]{:S(2)}, u32[]{:S(2)}) async-start(bf16[16,128,128]{2,1,0:T(8,128)(2,1)} %get-tuple-element.42), calls=%async_computation.3 | async-start | bytes 1048576 | tf_op jit(solution)/shard_map/all_to_all | solution.py:313
  51.2 10.0 %collective-permute-start.7 = (bf16[128,128]{1,0:T(8,128)(2,1)S(1)}, bf16[128,128]{1,0:T(8,128)(2,1)S(1)}, u32[]{:S(2)}, u32[]{:S(2)}) collective-permute-start(bf16[128,128]{1,0:T(8,128)(2,1)S(1)} %get-tuple-element.46), channel_id=1, source_target_pairs={{0,7},{1,6},{2,5},{3,4},{4,3},{5,2},{6,1},{7,0},{8,15},{9,14},{10,... | collective-permute-start | bytes 98312 | tf_op jit(solution)/shard_map/ppermute | solution.py:330
  52.5 10.2 %collective-permute-start.8 = (bf16[128,128]{1,0:T(8,128)(2,1)S(1)}, bf16[128,128]{1,0:T(8,128)(2,1)S(1)}, u32[]{:S(2)}, u32[]{:S(2)}) collective-permute-start(bf16[128,128]{1,0:T(8,128)(2,1)S(1)} %get-tuple-element.47), channel_id=1, source_target_pairs={{0,6},{1,7},{2,4},{3,5},{4,2},{5,3},{6,0},{7,1},{8,14},{9,15},{10,... | collective-permute-start | bytes 98312 | tf_op jit(solution)/shard_map/ppermute | solution.py:330
  53.9 10.9 %collective-permute-start.9 = (bf16[128,128]{1,0:T(8,128)(2,1)S(1)}, bf16[128,128]{1,0:T(8,128)(2,1)S(1)}, u32[]{:S(2)}, u32[]{:S(2)}) collective-permute-start(bf16[128,128]{1,0:T(8,128)(2,1)S(1)} %get-tuple-element.48), channel_id=1, source_target_pairs={{0,5},{1,4},{2,7},{3,6},{4,1},{5,0},{6,3},{7,2},{8,13},{9,12},{10,... | collective-permute-start | bytes 98312 | tf_op jit(solution)/shard_map/ppermute | solution.py:330
  53.9 10.9 %collective-permute-start.10 = (bf16[128,128]{1,0:T(8,128)(2,1)S(1)}, bf16[128,128]{1,0:T(8,128)(2,1)S(1)}, u32[]{:S(2)}, u32[]{:S(2)}) collective-permute-start(bf16[128,128]{1,0:T(8,128)(2,1)S(1)} %get-tuple-element.49), channel_id=1, source_target_pairs={{0,4},{1,5},{2,6},{3,7},{4,0},{5,1},{6,2},{7,3},{8,12},{9,13},{10,... | collective-permute-start | bytes 98312 | tf_op jit(solution)/shard_map/ppermute | solution.py:330
  55.6 9.2 %collective-permute-start.11 = (bf16[128,128]{1,0:T(8,128)(2,1)S(1)}, bf16[128,128]{1,0:T(8,128)(2,1)S(1)}, u32[]{:S(2)}, u32[]{:S(2)}) collective-permute-start(bf16[128,128]{1,0:T(8,128)(2,1)S(1)} %get-tuple-element.50), channel_id=1, source_target_pairs={{0,3},{1,2},{2,1},{3,0},{4,7},{5,6},{6,5},{7,4},{8,11},{9,10},{10,... | collective-permute-start | bytes 98312 | tf_op jit(solution)/shard_map/ppermute | solution.py:330
  61.2 3.9 %collective-permute-start.12 = (bf16[128,128]{1,0:T(8,128)(2,1)S(1)}, bf16[128,128]{1,0:T(8,128)(2,1)S(1)}, u32[]{:S(2)}, u32[]{:S(2)}) collective-permute-start(bf16[128,128]{1,0:T(8,128)(2,1)S(1)} %get-tuple-element.51), channel_id=1, source_target_pairs={{0,2},{1,3},{2,0},{3,1},{4,6},{5,7},{6,4},{7,5},{8,10},{9,11},{10,... | collective-permute-start | bytes 98312 | tf_op jit(solution)/shard_map/ppermute | solution.py:330
  62.7 2.4 %collective-permute-start.13 = (bf16[128,128]{1,0:T(8,128)(2,1)S(1)}, bf16[128,128]{1,0:T(8,128)(2,1)S(1)}, u32[]{:S(2)}, u32[]{:S(2)}) collective-permute-start(bf16[128,128]{1,0:T(8,128)(2,1)S(1)} %get-tuple-element.52), channel_id=1, source_target_pairs={{0,1},{1,0},{2,3},{3,2},{4,5},{5,4},{6,7},{7,6},{8,9},{9,8},{10,11... | collective-permute-start | bytes 98312 | tf_op jit(solution)/shard_map/ppermute | solution.py:330
  (3 other events, 9.3 us)

commit v14 on v13

--- a/solution.py
+++ b/solution.py
@@ -97,7 +97,8 @@
 
 
 def distance(step, count):
-    return (count - step) % count
+    far = sorted(range(3, count), key=lambda apart: -(apart // 2))
+    return [*range(min(3, count)), *far][step]
 
 
 def partner(step, count):

time: 67.3 us -> 63.1 us (0.938)
  starting transfers between devices: 27.4 us -> 25 us
  waiting for transfers between devices: 9.22 us -> 7.63 us
    ppermute x14, waiting for transfers between devices: 9.21 us -> 6.9 us  [swap_pieces(): lax.ppermute(pieces[step], 'row', [(d, d ^ distance(step, count)) for d i...]
    ppermute x14, starting transfers between devices: 14.4 us -> 12.2 us  [swap_pieces(): lax.ppermute(pieces[step], 'row', [(d, d ^ distance(step, count)) for d i...]
    all_to_all x2, waiting for transfers between devices: 0.01 us -> 0.73 us  [swap(): lax.all_to_all(values, 'row', split_axis=0, concat_axis=0, tiled=True, ax...]
  transfers between devices with their start and end apart: 16 -> 16, of which waited for: 4 -> 12; matrix products, arithmetic and copies ran while one was open for 0% -> 0% of each run, Pallas kernels for 5% -> 6%
where the time goes in v14:
time: 63.1 us; the launch traced here: 62.7 us
  starting transfers between devices  25 us (40%)
  blocking collectives  18.6 us (29%)
  Pallas kernels  9.81 us (16%)
  waiting for transfers between devices  7.63 us (12%)
  local copies, waits for them, and re-layouts  1.34 us (2%)
    all_to_all x2, blocking collectives, swap_half(): lax.all_to_all(values, 'row', split_axis=0, concat_axis=0, tiled=True, ax...  18.6 us
    all_to_all x2, starting transfers between devices, swap(): lax.all_to_all(values, 'row', split_axis=0, concat_axis=0, tiled=True, ax...  12.8 us
    ppermute x14, starting transfers between devices, swap_pieces(): lax.ppermute(pieces[step], 'row', [(d, d ^ distance(step, count)) for d i...  12.2 us
    pallas_call x12, Pallas kernels, call(): pl.pallas_call(body, name=name, out_shape=outs, in_specs=[pl.BlockSpec(me...  9.81 us
    ppermute x14, waiting for transfers between devices, swap_pieces(): lax.ppermute(pieces[step], 'row', [(d, d ^ distance(step, count)) for d i...  6.9 us
    unnamed x22, local copies, waits for them, and re-layouts  1.34 us
  transfers between devices with their start and end apart: 16, of which 12 were waited for; matrix products, arithmetic and copies ran while one was open for 0% of the time, Pallas kernels for 6%

profile of v14, /device:TPU:0, one launch (start us, length us, event | category | flops | bytes accessed | tf_op | source)
XLA Modules:
  0.0 62.7 jit_solution(4431418504298863840)
XLA Ops:
  0.0 2.4 %project_right.1.refs_5_ = bf16[16,128,128]{2,1,0:T(8,128)(2,1)} custom-call(bf16[8,128,128]{2,1,0:T(8,128)(2,1)} %refs_0_.7, s32[1,128]{1,0:T(1,128)} %bitcast.13, f32[1,128]{1,0:T(1,128)} %bitcast.5, f32[1,128]{1,0:T(1,128)} %bitcast.9, bf16[128,512]{1,0:T(8,128)(2,1)} %refs_4_.9), custom_call_target="tpu_custom_call" | custom-call | flops 67108864 | bytes 919040 | tf_op jit(solution)/shard_map/project_right/pallas_call | solution.py:65
  2.5 8.0 %all-to-all-start = ((bf16[16,128,128]{2,1,0:T(8,128)(2,1)}), bf16[16,128,128]{2,1,0:T(8,128)(2,1)S(1)}, u32[]{:S(2)}, u32[]{:S(2)}) async-start(bf16[16,128,128]{2,1,0:T(8,128)(2,1)} %project_right.1.refs_5_), calls=%async_computation | async-start | bytes 1048576 | tf_op jit(solution)/shard_map/all_to_all | solution.py:314
  10.5 0.8 %project_left.1 = (bf16[128,128]{1,0:T(8,128)(2,1)S(1)}, bf16[128,128]{1,0:T(8,128)(2,1)S(1)}, bf16[128,128]{1,0:T(8,128)(2,1)S(1)}, bf16[128,128]{1,0:T(8,128)(...) custom-call(bf16[8,128,128]{2,1,0:T(8,128)(2,1)S(1)} %copy-done.1, ...), custom_call_target="tpu_custom_call" | custom-call | flops 67108864 | bytes 1181184 | tf_op jit(solution)/shard_map/project_left/pallas_call | solution.py:65
  11.5 1.5 %collective-permute-start.1 = (bf16[128,128]{1,0:T(8,128)(2,1)S(1)}, bf16[128,128]{1,0:T(8,128)(2,1)S(1)}, u32[]{:S(2)}, u32[]{:S(2)}) collective-permute-start(bf16[128,128]{1,0:T(8,128)(2,1)S(1)} %get-tuple-element.34), channel_id=1, source_target_pairs={{0,2},{1,3},{2,0},{3,1},{4,6},{5,7},{6,4},{7,5},{8,10},{9,11},{10,... | collective-permute-start | bytes 98312 | tf_op jit(solution)/shard_map/ppermute | solution.py:331
  13.4 2.0 %collective-permute-start.3 = (bf16[128,128]{1,0:T(8,128)(2,1)S(1)}, bf16[128,128]{1,0:T(8,128)(2,1)S(1)}, u32[]{:S(2)}, u32[]{:S(2)}) collective-permute-start(bf16[128,128]{1,0:T(8,128)(2,1)S(1)} %get-tuple-element.36), channel_id=1, source_target_pairs={{0,7},{1,6},{2,5},{3,4},{4,3},{5,2},{6,1},{7,0},{8,15},{9,14},{10,... | collective-permute-start | bytes 98312 | tf_op jit(solution)/shard_map/ppermute | solution.py:331
  15.9 1.5 %collective-permute-start.5 = (bf16[128,128]{1,0:T(8,128)(2,1)S(1)}, bf16[128,128]{1,0:T(8,128)(2,1)S(1)}, u32[]{:S(2)}, u32[]{:S(2)}) collective-permute-start(bf16[128,128]{1,0:T(8,128)(2,1)S(1)} %get-tuple-element.38), channel_id=1, source_target_pairs={{0,5},{1,4},{2,7},{3,6},{4,1},{5,0},{6,3},{7,2},{8,13},{9,12},{10,... | collective-permute-start | bytes 98312 | tf_op jit(solution)/shard_map/ppermute | solution.py:331
  17.4 0.7 %collective-permute-done.1.refs_2_ = bf16[128,128]{1,0:T(8,128)(2,1)S(1)} collective-permute-done((bf16[128,128]{1,0:T(8,128)(2,1)S(1)}, bf16[128,128]{1,0:T(8,128)(2,1)S(1)}, u32[]{:S(2)}, u32[]{:S(2)}) %collective-permute-start.1) | collective-permute-done | bytes 32800 | tf_op jit(solution)/shard_map/ppermute | solution.py:331
  18.1 0.6 copy-done.9
  18.8 0.8 %prepare.1 = (f32[8,128,128]{2,1,0:T(8,128)S(1)}, f32[8,128,128]{2,1,0:T(8,128)S(1)}) custom-call(bf16[8,128,128]{2,1,0:T(8,128)(2,1)S(1)} %copy-done.1, bf16[8,128,128]{2,1,0:T(8,128)(2,1)S(1)} %copy-done.3, f32[1,128]{1,0:T(1,128)S(1)} %bitcast.7, f32[1,128]{1,0:T(1,128)S(1)} %bitcast.11, bf16[128,128]{1,0:T(8,128)(2,1)S(1)} %copy-done.5, ...), custom_call_target="tpu_custom_call" | custom-call | flops 67108864 | bytes 1639936 | tf_op jit(solution)/shard_map/prepare/pallas_call | solution.py:65
  19.6 1.2 %collective-permute-done.2.refs_3_ = bf16[128,128]{1,0:T(8,128)(2,1)S(1)} collective-permute-done((bf16[128,128]{1,0:T(8,128)(2,1)S(1)}, bf16[128,128]{1,0:T(8,128)(2,1)S(1)}, u32[]{:S(2)}, u32[]{:S(2)}) %collective-permute-start.2) | collective-permute-done | bytes 32800 | tf_op jit(solution)/shard_map/ppermute | solution.py:331
  20.8 0.7 %collective-permute-done.3.refs_4_ = bf16[128,128]{1,0:T(8,128)(2,1)S(1)} collective-permute-done((bf16[128,128]{1,0:T(8,128)(2,1)S(1)}, bf16[128,128]{1,0:T(8,128)(2,1)S(1)}, u32[]{:S(2)}, u32[]{:S(2)}) %collective-permute-start.3) | collective-permute-done | bytes 32800 | tf_op jit(solution)/shard_map/ppermute | solution.py:331
  22.9 0.6 %tri.1 = (bf16[8,128,128]{2,1,0:T(8,128)(2,1)S(1)}, bf16[16,128,128]{2,1,0:T(8,128)(2,1)S(1)}) custom-call(bf16[16,128,128]{2,1,0:T(8,128)(2,1)S(1)} %all-to-all-done.refs_0_, bf16[16,64,128]{2,1,0:T(8,128)(2,1)S(1)} %sort_left.1.refs_1_, f32[8,128,128]{2,1,0:T(8,128)S(1)} %get-tuple-element.40.refs_2_.refs_1_), custom_call_target="tpu_custom_call" | custom-call | flops 33554432 | bytes 2097152 | tf_op jit(solution)/shard_map/tri/pallas_call | solution.py:65
  23.6 10.0 %all_to_all.20.refs_0_ = bf16[8,128,128]{2,1,0:T(8,128)(2,1)S(1)} all-to-all(bf16[8,128,128]{2,1,0:T(8,128)(2,1)S(1)} %get-tuple-element.41), channel_id=1, replica_groups={{0,1,2,3,4,5,6,7},{8,9,10,11,12,13,14,15},{16,17,18,19,20,21,22,23},{24..., dimensions={0} | all-to-all | bytes 524288 | tf_op jit(solution)/shard_map/all_to_all | solution.py:322
  33.9 8.6 %all_to_all.21.refs_0_ = bf16[8,128,128]{2,1,0:T(8,128)(2,1)S(1)} all-to-all(bf16[8,128,128]{2,1,0:T(8,128)(2,1)S(1)} %middle.1), channel_id=1, replica_groups={{0,1,2,3,4,5,6,7},{8,9,10,11,12,13,14,15},{16,17,18,19,20,21,22,23},{24..., dimensions={0} | all-to-all | bytes 524288 | tf_op jit(solution)/shard_map/all_to_all | solution.py:322
  42.5 1.5 %d_right.1 = (bf16[16,128,128]{2,1,0:T(8,128)(2,1)}, bf16[16,64,128]{2,1,0:T(8,128)(2,1)S(1)}) custom-call(bf16[8,128,128]{2,1,0:T(8,128)(2,1)S(1)} %all_to_all.21.refs_0_, bf16[16,64,128]{2,1,0:T(8,128)(2,1)S(1)} %sort_left.1.refs_1_), custom_call_target="tpu_custom_call" | custom-call | flops 33554432 | bytes 1310720 | tf_op jit(solution)/shard_map/d_right/pallas_call | solution.py:65
  44.0 4.9 %all-to-all-start.3 = ((bf16[16,128,128]{2,1,0:T(8,128)(2,1)}), bf16[16,128,128]{2,1,0:T(8,128)(2,1)S(1)}, u32[]{:S(2)}, u32[]{:S(2)}) async-start(bf16[16,128,128]{2,1,0:T(8,128)(2,1)} %get-tuple-element.42), calls=%async_computation.3 | async-start | bytes 1048576 | tf_op jit(solution)/shard_map/all_to_all | solution.py:314
  49.4 1.5 %collective-permute-start.8 = (bf16[128,128]{1,0:T(8,128)(2,1)S(1)}, bf16[128,128]{1,0:T(8,128)(2,1)S(1)}, u32[]{:S(2)}, u32[]{:S(2)}) collective-permute-start(bf16[128,128]{1,0:T(8,128)(2,1)S(1)} %get-tuple-element.47), channel_id=1, source_target_pairs={{0,2},{1,3},{2,0},{3,1},{4,6},{5,7},{6,4},{7,5},{8,10},{9,11},{10,... | collective-permute-start | bytes 98312 | tf_op jit(solution)/shard_map/ppermute | solution.py:331
  51.2 2.0 %collective-permute-start.10 = (bf16[128,128]{1,0:T(8,128)(2,1)S(1)}, bf16[128,128]{1,0:T(8,128)(2,1)S(1)}, u32[]{:S(2)}, u32[]{:S(2)}) collective-permute-start(bf16[128,128]{1,0:T(8,128)(2,1)S(1)} %get-tuple-element.49), channel_id=1, source_target_pairs={{0,7},{1,6},{2,5},{3,4},{4,3},{5,2},{6,1},{7,0},{8,15},{9,14},{10,... | collective-permute-start | bytes 98312 | tf_op jit(solution)/shard_map/ppermute | solution.py:331
  53.7 1.6 %collective-permute-start.12 = (bf16[128,128]{1,0:T(8,128)(2,1)S(1)}, bf16[128,128]{1,0:T(8,128)(2,1)S(1)}, u32[]{:S(2)}, u32[]{:S(2)}) collective-permute-start(bf16[128,128]{1,0:T(8,128)(2,1)S(1)} %get-tuple-element.51), channel_id=1, source_target_pairs={{0,5},{1,4},{2,7},{3,6},{4,1},{5,0},{6,3},{7,2},{8,13},{9,12},{10,... | collective-permute-start | bytes 98312 | tf_op jit(solution)/shard_map/ppermute | solution.py:331
  55.3 1.2 %collective-permute-done.8.refs_2_ = bf16[128,128]{1,0:T(8,128)(2,1)S(1)} collective-permute-done((bf16[128,128]{1,0:T(8,128)(2,1)S(1)}, bf16[128,128]{1,0:T(8,128)(2,1)S(1)}, u32[]{:S(2)}, u32[]{:S(2)}) %collective-permute-start.8) | collective-permute-done | bytes 32800 | tf_op jit(solution)/shard_map/ppermute | solution.py:331
  56.5 0.7 %copy-done.10 = f32[128]{0:T(128)S(1)} copy-done((f32[128]{0:T(128)S(1)}, f32[128]{0:T(128)}, u32[]{:S(2)}) %copy-start.10) | copy-done | bytes 536
  57.6 1.0 %slopes.1 = (bf16[8,512,128]{2,1,0:T(8,128)(2,1)S(1)}, bf16[8,128,128]{2,1,0:T(8,128)(2,1)S(1)}, f32[8,128]{1,0:T(8,128)S(1)}, f32[128,128]{1,0:T(8,128)S(1)}, bf16[128,640]{1,0:T(8,128)(2,1)S(1)}) custom-call(bf16[8,128,128]{2,1,0:T(8,128)(2,1)S(1)} %copy-done.1, s32[1,128]{1,0:T(1,128)S(1)} %bitcast.15, f32[1,128]{1,0:T(1,128)S(1)} %bitcast.8, ...), custom_call_target="tpu_custom_call" | custom-call | flops 134217728 | bytes 2233856 | tf_op jit(solution)/shard_map/slopes/pallas_call | solution.py:65
  59.2 0.7 %collective-permute-done.10.refs_4_ = bf16[128,128]{1,0:T(8,128)(2,1)S(1)} collective-permute-done((bf16[128,128]{1,0:T(8,128)(2,1)S(1)}, bf16[128,128]{1,0:T(8,128)(2,1)S(1)}, u32[]{:S(2)}, u32[]{:S(2)}) %collective-permute-start.10) | collective-permute-done | bytes 32800 | tf_op jit(solution)/shard_map/ppermute | solution.py:331
  61.3 1.4 %finish.1 = bf16[8,128,128]{2,1,0:T(8,128)(2,1)} custom-call(bf16[16,128,128]{2,1,0:T(8,128)(2,1)S(1)} %all-to-all-done.3.refs_0_, bf16[8,128,128]{2,1,0:T(8,128)(2,1)S(1)} %sort_d_left.1.refs_1_, bf16[8,512,128]{2,1,0:T(8,128)(2,1)S(1)} %get-tuple-element.54.refs_2_, bf16[8,128,128]{2,1,0:T(8,128)(2,1)S(1)} %gate_back.1.refs_6_.refs_3_, ...), custom_call_target="tpu_custom_call" | custom-call | flops 134217728 | bytes 2854912 | tf_op jit(solution)/shard_map/finish/pallas_call | solution.py:65
  (44 shorter events, 6.6 us)
Async XLA Ops:
  2.4 8.0 %copy-start = (bf16[16,128,128]{2,1,0:T(8,128)(2,1)S(1)}, bf16[16,128,128]{2,1,0:T(8,128)(2,1)}, u32[]{:S(2)}) copy-start(bf16[16,128,128]{2,1,0:T(8,128)(2,1)} %project_right.1.refs_5_) | copy-start | bytes 1572868
  2.4 8.0 %copy-start.1 = (bf16[8,128,128]{2,1,0:T(8,128)(2,1)S(1)}, bf16[8,128,128]{2,1,0:T(8,128)(2,1)}, u32[]{:S(2)}) copy-start(bf16[8,128,128]{2,1,0:T(8,128)(2,1)} %refs_0_.7) | copy-start | bytes 786436
  2.4 8.0 %copy-start.2 = (bf16[128,512]{1,0:T(8,128)(2,1)S(1)}, bf16[128,512]{1,0:T(8,128)(2,1)}, u32[]{:S(2)}) copy-start(bf16[128,512]{1,0:T(8,128)(2,1)} %refs_4_.9) | copy-start | bytes 393220
  2.4 8.0 %copy-start.6 = (f32[128]{0:T(128)S(1)}, f32[128]{0:T(128)}, u32[]{:S(2)}) copy-start(f32[128]{0:T(128)} %param.13) | copy-start | bytes 1540
  2.4 8.0 %copy-start.7 = (f32[128]{0:T(128)S(1)}, f32[128]{0:T(128)}, u32[]{:S(2)}) copy-start(f32[128]{0:T(128)} %param.14) | copy-start | bytes 1540
  2.5 8.0 %copy-start.8 = (s32[128]{0:T(128)S(1)}, s32[128]{0:T(128)}, u32[]{:S(2)}) copy-start(s32[128]{0:T(128)} %param.12) | copy-start | bytes 1540
  2.5 20.4 %all-to-all-start = ((bf16[16,128,128]{2,1,0:T(8,128)(2,1)}), bf16[16,128,128]{2,1,0:T(8,128)(2,1)S(1)}, u32[]{:S(2)}, u32[]{:S(2)}) async-start(bf16[16,128,128]{2,1,0:T(8,128)(2,1)} %project_right.1.refs_5_), calls=%async_computation | async-start | bytes 1048576 | tf_op jit(solution)/shard_map/all_to_all | solution.py:314
  10.5 7.6 %copy-start.3 = (bf16[8,128,128]{2,1,0:T(8,128)(2,1)S(1)}, bf16[8,128,128]{2,1,0:T(8,128)(2,1)}, u32[]{:S(2)}) copy-start(bf16[8,128,128]{2,1,0:T(8,128)(2,1)} %refs_1_.1) | copy-start | bytes 786436
  10.5 7.6 %copy-start.4 = (bf16[128,128]{1,0:T(8,128)(2,1)S(1)}, bf16[128,128]{1,0:T(8,128)(2,1)}, u32[]{:S(2)}) copy-start(bf16[128,128]{1,0:T(8,128)(2,1)} %refs_4_.8) | copy-start | bytes 98308
  11.3 4.6 %collective-permute-start = (bf16[128,128]{1,0:T(8,128)(2,1)S(1)}, bf16[128,128]{1,0:T(8,128)(2,1)S(1)}, u32[]{:S(2)}, u32[]{:S(2)}) collective-permute-start(bf16[128,128]{1,0:T(8,128)(2,1)S(1)} %get-tuple-element.33), channel_id=1, source_target_pairs={{0,1},{1,0},{2,3},{3,2},{4,5},{5,4},{6,7},{7,6},{8,9},{9,8},{10,11... | collective-permute-start | bytes 98312 | tf_op jit(solution)/shard_map/ppermute | solution.py:331
  11.5 6.6 %collective-permute-start.1 = (bf16[128,128]{1,0:T(8,128)(2,1)S(1)}, bf16[128,128]{1,0:T(8,128)(2,1)S(1)}, u32[]{:S(2)}, u32[]{:S(2)}) collective-permute-start(bf16[128,128]{1,0:T(8,128)(2,1)S(1)} %get-tuple-element.34), channel_id=1, source_target_pairs={{0,2},{1,3},{2,0},{3,1},{4,6},{5,7},{6,4},{7,5},{8,10},{9,11},{10,... | collective-permute-start | bytes 98312 | tf_op jit(solution)/shard_map/ppermute | solution.py:331
  13.0 7.8 %collective-permute-start.2 = (bf16[128,128]{1,0:T(8,128)(2,1)S(1)}, bf16[128,128]{1,0:T(8,128)(2,1)S(1)}, u32[]{:S(2)}, u32[]{:S(2)}) collective-permute-start(bf16[128,128]{1,0:T(8,128)(2,1)S(1)} %get-tuple-element.35), channel_id=1, source_target_pairs={{0,6},{1,7},{2,4},{3,5},{4,2},{5,3},{6,0},{7,1},{8,14},{9,15},{10,... | collective-permute-start | bytes 98312 | tf_op jit(solution)/shard_map/ppermute | solution.py:331
  13.4 8.1 %collective-permute-start.3 = (bf16[128,128]{1,0:T(8,128)(2,1)S(1)}, bf16[128,128]{1,0:T(8,128)(2,1)S(1)}, u32[]{:S(2)}, u32[]{:S(2)}) collective-permute-start(bf16[128,128]{1,0:T(8,128)(2,1)S(1)} %get-tuple-element.36), channel_id=1, source_target_pairs={{0,7},{1,6},{2,5},{3,4},{4,3},{5,2},{6,1},{7,0},{8,15},{9,14},{10,... | collective-permute-start | bytes 98312 | tf_op jit(solution)/shard_map/ppermute | solution.py:331
  15.3 6.7 %collective-permute-start.4 = (bf16[128,128]{1,0:T(8,128)(2,1)S(1)}, bf16[128,128]{1,0:T(8,128)(2,1)S(1)}, u32[]{:S(2)}, u32[]{:S(2)}) collective-permute-start(bf16[128,128]{1,0:T(8,128)(2,1)S(1)} %get-tuple-element.37), channel_id=1, source_target_pairs={{0,4},{1,5},{2,6},{3,7},{4,0},{5,1},{6,2},{7,3},{8,12},{9,13},{10,... | collective-permute-start | bytes 98312 | tf_op jit(solution)/shard_map/ppermute | solution.py:331
  15.9 6.5 %collective-permute-start.5 = (bf16[128,128]{1,0:T(8,128)(2,1)S(1)}, bf16[128,128]{1,0:T(8,128)(2,1)S(1)}, u32[]{:S(2)}, u32[]{:S(2)}) collective-permute-start(bf16[128,128]{1,0:T(8,128)(2,1)S(1)} %get-tuple-element.38), channel_id=1, source_target_pairs={{0,5},{1,4},{2,7},{3,6},{4,1},{5,0},{6,3},{7,2},{8,13},{9,12},{10,... | collective-permute-start | bytes 98312 | tf_op jit(solution)/shard_map/ppermute | solution.py:331
  18.1 4.3 %collective-permute-start.6 = (bf16[128,128]{1,0:T(8,128)(2,1)S(1)}, bf16[128,128]{1,0:T(8,128)(2,1)S(1)}, u32[]{:S(2)}, u32[]{:S(2)}) collective-permute-start(bf16[128,128]{1,0:T(8,128)(2,1)S(1)} %get-tuple-element.39), channel_id=1, source_target_pairs={{0,3},{1,2},{2,1},{3,0},{4,7},{5,6},{6,5},{7,4},{8,11},{9,10},{10,... | collective-permute-start | bytes 98312 | tf_op jit(solution)/shard_map/ppermute | solution.py:331
  44.0 17.3 %all-to-all-start.3 = ((bf16[16,128,128]{2,1,0:T(8,128)(2,1)}), bf16[16,128,128]{2,1,0:T(8,128)(2,1)S(1)}, u32[]{:S(2)}, u32[]{:S(2)}) async-start(bf16[16,128,128]{2,1,0:T(8,128)(2,1)} %get-tuple-element.42), calls=%async_computation.3 | async-start | bytes 1048576 | tf_op jit(solution)/shard_map/all_to_all | solution.py:314
  49.2 4.5 %collective-permute-start.7 = (bf16[128,128]{1,0:T(8,128)(2,1)S(1)}, bf16[128,128]{1,0:T(8,128)(2,1)S(1)}, u32[]{:S(2)}, u32[]{:S(2)}) collective-permute-start(bf16[128,128]{1,0:T(8,128)(2,1)S(1)} %get-tuple-element.46), channel_id=1, source_target_pairs={{0,1},{1,0},{2,3},{3,2},{4,5},{5,4},{6,7},{7,6},{8,9},{9,8},{10,11... | collective-permute-start | bytes 98312 | tf_op jit(solution)/shard_map/ppermute | solution.py:331
  49.4 7.1 %collective-permute-start.8 = (bf16[128,128]{1,0:T(8,128)(2,1)S(1)}, bf16[128,128]{1,0:T(8,128)(2,1)S(1)}, u32[]{:S(2)}, u32[]{:S(2)}) collective-permute-start(bf16[128,128]{1,0:T(8,128)(2,1)S(1)} %get-tuple-element.47), channel_id=1, source_target_pairs={{0,2},{1,3},{2,0},{3,1},{4,6},{5,7},{6,4},{7,5},{8,10},{9,11},{10,... | collective-permute-start | bytes 98312 | tf_op jit(solution)/shard_map/ppermute | solution.py:331
  50.9 8.3 %collective-permute-start.9 = (bf16[128,128]{1,0:T(8,128)(2,1)S(1)}, bf16[128,128]{1,0:T(8,128)(2,1)S(1)}, u32[]{:S(2)}, u32[]{:S(2)}) collective-permute-start(bf16[128,128]{1,0:T(8,128)(2,1)S(1)} %get-tuple-element.48), channel_id=1, source_target_pairs={{0,6},{1,7},{2,4},{3,5},{4,2},{5,3},{6,0},{7,1},{8,14},{9,15},{10,... | collective-permute-start | bytes 98312 | tf_op jit(solution)/shard_map/ppermute | solution.py:331
  51.2 8.7 %collective-permute-start.10 = (bf16[128,128]{1,0:T(8,128)(2,1)S(1)}, bf16[128,128]{1,0:T(8,128)(2,1)S(1)}, u32[]{:S(2)}, u32[]{:S(2)}) collective-permute-start(bf16[128,128]{1,0:T(8,128)(2,1)S(1)} %get-tuple-element.49), channel_id=1, source_target_pairs={{0,7},{1,6},{2,5},{3,4},{4,3},{5,2},{6,1},{7,0},{8,15},{9,14},{10,... | collective-permute-start | bytes 98312 | tf_op jit(solution)/shard_map/ppermute | solution.py:331
  53.2 7.2 %collective-permute-start.11 = (bf16[128,128]{1,0:T(8,128)(2,1)S(1)}, bf16[128,128]{1,0:T(8,128)(2,1)S(1)}, u32[]{:S(2)}, u32[]{:S(2)}) collective-permute-start(bf16[128,128]{1,0:T(8,128)(2,1)S(1)} %get-tuple-element.50), channel_id=1, source_target_pairs={{0,4},{1,5},{2,6},{3,7},{4,0},{5,1},{6,2},{7,3},{8,12},{9,13},{10,... | collective-permute-start | bytes 98312 | tf_op jit(solution)/shard_map/ppermute | solution.py:331
  53.7 7.1 %collective-permute-start.12 = (bf16[128,128]{1,0:T(8,128)(2,1)S(1)}, bf16[128,128]{1,0:T(8,128)(2,1)S(1)}, u32[]{:S(2)}, u32[]{:S(2)}) collective-permute-start(bf16[128,128]{1,0:T(8,128)(2,1)S(1)} %get-tuple-element.51), channel_id=1, source_target_pairs={{0,5},{1,4},{2,7},{3,6},{4,1},{5,0},{6,3},{7,2},{8,13},{9,12},{10,... | collective-permute-start | bytes 98312 | tf_op jit(solution)/shard_map/ppermute | solution.py:331
  56.5 4.3 %collective-permute-start.13 = (bf16[128,128]{1,0:T(8,128)(2,1)S(1)}, bf16[128,128]{1,0:T(8,128)(2,1)S(1)}, u32[]{:S(2)}, u32[]{:S(2)}) collective-permute-start(bf16[128,128]{1,0:T(8,128)(2,1)S(1)} %get-tuple-element.52), channel_id=1, source_target_pairs={{0,3},{1,2},{2,1},{3,0},{4,7},{5,6},{6,5},{7,4},{8,11},{9,10},{10,... | collective-permute-start | bytes 98312 | tf_op jit(solution)/shard_map/ppermute | solution.py:331
  (3 other events, 8.9 us)

commit v15 on v14

--- a/solution.py
+++ b/solution.py
@@ -92,8 +92,10 @@
 
 
 def wide_order(devices, count):
-    inner = [(place + count // 2) % count for place in range(count)]
-    return [device for place in range(count) for device in (inner[place], count + place)]
+    order = []
+    for place in range(count):
+        order += [count + (place ^ 2), place ^ (count // 2)]
+    return order
 
 
 def distance(step, count):

time: 63.1 us -> 63.9 us (1.013)
  waiting for transfers between devices: 7.63 us -> 9.91 us
  blocking collectives: 18.6 us -> 17.3 us
    ppermute x14, waiting for transfers between devices: 6.9 us -> 9.91 us  [swap_pieces(): lax.ppermute(pieces[step], 'row', [(d, d ^ distance(step, count)) for d i...]
    ppermute x14, starting transfers between devices: 12.2 us -> 10.4 us  [swap_pieces(): lax.ppermute(pieces[step], 'row', [(d, d ^ distance(step, count)) for d i...]
    all_to_all x2, starting transfers between devices: 12.8 us -> 14.4 us  [swap(): lax.all_to_all(values, 'row', split_axis=0, concat_axis=0, tiled=True, ax...]
    all_to_all x2, blocking collectives: 18.6 us -> 17.3 us  [swap_half(): lax.all_to_all(values, 'row', split_axis=0, concat_axis=0, tiled=True, ax...]
    all_to_all x2, waiting for transfers between devices: 0.73 us -> 0.01 us  [swap(): lax.all_to_all(values, 'row', split_axis=0, concat_axis=0, tiled=True, ax...]
  transfers between devices with their start and end apart: 16 -> 16, of which waited for: 12 -> 8; matrix products, arithmetic and copies ran while one was open for 0% -> 0% of each run, Pallas kernels for 6% -> 6%
where the time goes in v15:
time: 63.9 us; the launch traced here: 63.5 us
  starting transfers between devices  24.8 us (39%)
  blocking collectives  17.3 us (27%)
  waiting for transfers between devices  9.91 us (16%)
  Pallas kernels  9.82 us (15%)
  local copies, waits for them, and re-layouts  1.34 us (2%)
    all_to_all x2, blocking collectives, swap_half(): lax.all_to_all(values, 'row', split_axis=0, concat_axis=0, tiled=True, ax...  17.3 us
    all_to_all x2, starting transfers between devices, swap(): lax.all_to_all(values, 'row', split_axis=0, concat_axis=0, tiled=True, ax...  14.4 us
    ppermute x14, starting transfers between devices, swap_pieces(): lax.ppermute(pieces[step], 'row', [(d, d ^ distance(step, count)) for d i...  10.4 us
    ppermute x14, waiting for transfers between devices, swap_pieces(): lax.ppermute(pieces[step], 'row', [(d, d ^ distance(step, count)) for d i...  9.91 us
    pallas_call x12, Pallas kernels, call(): pl.pallas_call(body, name=name, out_shape=outs, in_specs=[pl.BlockSpec(me...  9.82 us
    unnamed x22, local copies, waits for them, and re-layouts  1.34 us
  transfers between devices with their start and end apart: 16, of which 8 were waited for; matrix products, arithmetic and copies ran while one was open for 0% of the time, Pallas kernels for 6%

profile of v15, /device:TPU:0, one launch (start us, length us, event | category | flops | bytes accessed | tf_op | source)
XLA Modules:
  0.0 63.5 jit_solution(3243427524272139147)
XLA Ops:
  0.0 2.4 %project_right.1.refs_5_ = bf16[16,128,128]{2,1,0:T(8,128)(2,1)} custom-call(bf16[8,128,128]{2,1,0:T(8,128)(2,1)} %refs_0_.7, s32[1,128]{1,0:T(1,128)} %bitcast.13, f32[1,128]{1,0:T(1,128)} %bitcast.5, f32[1,128]{1,0:T(1,128)} %bitcast.9, bf16[128,512]{1,0:T(8,128)(2,1)} %refs_4_.9), custom_call_target="tpu_custom_call" | custom-call | flops 67108864 | bytes 919040 | tf_op jit(solution)/shard_map/project_right/pallas_call | solution.py:65
  2.5 8.5 %all-to-all-start = ((bf16[16,128,128]{2,1,0:T(8,128)(2,1)}), bf16[16,128,128]{2,1,0:T(8,128)(2,1)S(1)}, u32[]{:S(2)}, u32[]{:S(2)}) async-start(bf16[16,128,128]{2,1,0:T(8,128)(2,1)} %project_right.1.refs_5_), calls=%async_computation | async-start | bytes 1048576 | tf_op jit(solution)/shard_map/all_to_all | solution.py:316
  11.1 0.8 %project_left.1 = (bf16[128,128]{1,0:T(8,128)(2,1)S(1)}, bf16[128,128]{1,0:T(8,128)(2,1)S(1)}, bf16[128,128]{1,0:T(8,128)(2,1)S(1)}, bf16[128,128]{1,0:T(8,128)(...) custom-call(bf16[8,128,128]{2,1,0:T(8,128)(2,1)S(1)} %copy-done.1, ...), custom_call_target="tpu_custom_call" | custom-call | flops 67108864 | bytes 1181184 | tf_op jit(solution)/shard_map/project_left/pallas_call | solution.py:65
  12.7 1.4 %collective-permute-start.2 = (bf16[128,128]{1,0:T(8,128)(2,1)S(1)}, bf16[128,128]{1,0:T(8,128)(2,1)S(1)}, u32[]{:S(2)}, u32[]{:S(2)}) collective-permute-start(bf16[128,128]{1,0:T(8,128)(2,1)S(1)} %get-tuple-element.35), channel_id=1, source_target_pairs={{0,6},{1,7},{2,4},{3,5},{4,2},{5,3},{6,0},{7,1},{8,14},{9,15},{10,... | collective-permute-start | bytes 98312 | tf_op jit(solution)/shard_map/ppermute | solution.py:333
  14.1 0.9 %collective-permute-start.3 = (bf16[128,128]{1,0:T(8,128)(2,1)S(1)}, bf16[128,128]{1,0:T(8,128)(2,1)S(1)}, u32[]{:S(2)}, u32[]{:S(2)}) collective-permute-start(bf16[128,128]{1,0:T(8,128)(2,1)S(1)} %get-tuple-element.36), channel_id=1, source_target_pairs={{0,7},{1,6},{2,5},{3,4},{4,3},{5,2},{6,1},{7,0},{8,15},{9,14},{10,... | collective-permute-start | bytes 98312 | tf_op jit(solution)/shard_map/ppermute | solution.py:333
  15.6 1.5 %collective-permute-start.5 = (bf16[128,128]{1,0:T(8,128)(2,1)S(1)}, bf16[128,128]{1,0:T(8,128)(2,1)S(1)}, u32[]{:S(2)}, u32[]{:S(2)}) collective-permute-start(bf16[128,128]{1,0:T(8,128)(2,1)S(1)} %get-tuple-element.38), channel_id=1, source_target_pairs={{0,5},{1,4},{2,7},{3,6},{4,1},{5,0},{6,3},{7,2},{8,13},{9,12},{10,... | collective-permute-start | bytes 98312 | tf_op jit(solution)/shard_map/ppermute | solution.py:333
  17.1 1.3 %collective-permute-done.1.refs_2_ = bf16[128,128]{1,0:T(8,128)(2,1)S(1)} collective-permute-done((bf16[128,128]{1,0:T(8,128)(2,1)S(1)}, bf16[128,128]{1,0:T(8,128)(2,1)S(1)}, u32[]{:S(2)}, u32[]{:S(2)}) %collective-permute-start.1) | collective-permute-done | bytes 32800 | tf_op jit(solution)/shard_map/ppermute | solution.py:333
  19.1 0.8 %prepare.1 = (f32[8,128,128]{2,1,0:T(8,128)S(1)}, f32[8,128,128]{2,1,0:T(8,128)S(1)}) custom-call(bf16[8,128,128]{2,1,0:T(8,128)(2,1)S(1)} %copy-done.1, bf16[8,128,128]{2,1,0:T(8,128)(2,1)S(1)} %copy-done.3, f32[1,128]{1,0:T(1,128)S(1)} %bitcast.7, f32[1,128]{1,0:T(1,128)S(1)} %bitcast.11, bf16[128,128]{1,0:T(8,128)(2,1)S(1)} %copy-done.5, ...), custom_call_target="tpu_custom_call" | custom-call | flops 67108864 | bytes 1639936 | tf_op jit(solution)/shard_map/prepare/pallas_call | solution.py:65
  19.9 1.5 %collective-permute-done.2.refs_3_ = bf16[128,128]{1,0:T(8,128)(2,1)S(1)} collective-permute-done((bf16[128,128]{1,0:T(8,128)(2,1)S(1)}, bf16[128,128]{1,0:T(8,128)(2,1)S(1)}, u32[]{:S(2)}, u32[]{:S(2)}) %collective-permute-start.2) | collective-permute-done | bytes 32800 | tf_op jit(solution)/shard_map/ppermute | solution.py:333
  21.3 0.7 %collective-permute-done.3.refs_4_ = bf16[128,128]{1,0:T(8,128)(2,1)S(1)} collective-permute-done((bf16[128,128]{1,0:T(8,128)(2,1)S(1)}, bf16[128,128]{1,0:T(8,128)(2,1)S(1)}, u32[]{:S(2)}, u32[]{:S(2)}) %collective-permute-start.3) | collective-permute-done | bytes 32800 | tf_op jit(solution)/shard_map/ppermute | solution.py:333
  22.0 1.5 %collective-permute-done.4.refs_5_ = bf16[128,128]{1,0:T(8,128)(2,1)S(1)} collective-permute-done((bf16[128,128]{1,0:T(8,128)(2,1)S(1)}, bf16[128,128]{1,0:T(8,128)(2,1)S(1)}, u32[]{:S(2)}, u32[]{:S(2)}) %collective-permute-start.4) | collective-permute-done | bytes 32800 | tf_op jit(solution)/shard_map/ppermute | solution.py:333
  24.5 8.7 %all_to_all.20.refs_0_ = bf16[8,128,128]{2,1,0:T(8,128)(2,1)S(1)} all-to-all(bf16[8,128,128]{2,1,0:T(8,128)(2,1)S(1)} %get-tuple-element.41), channel_id=1, replica_groups={{0,1,2,3,4,5,6,7},{8,9,10,11,12,13,14,15},{16,17,18,19,20,21,22,23},{24..., dimensions={0} | all-to-all | bytes 524288 | tf_op jit(solution)/shard_map/all_to_all | solution.py:324
  33.5 8.6 %all_to_all.21.refs_0_ = bf16[8,128,128]{2,1,0:T(8,128)(2,1)S(1)} all-to-all(bf16[8,128,128]{2,1,0:T(8,128)(2,1)S(1)} %middle.1), channel_id=1, replica_groups={{0,1,2,3,4,5,6,7},{8,9,10,11,12,13,14,15},{16,17,18,19,20,21,22,23},{24..., dimensions={0} | all-to-all | bytes 524288 | tf_op jit(solution)/shard_map/all_to_all | solution.py:324
  42.1 1.5 %d_right.1 = (bf16[16,128,128]{2,1,0:T(8,128)(2,1)}, bf16[16,64,128]{2,1,0:T(8,128)(2,1)S(1)}) custom-call(bf16[8,128,128]{2,1,0:T(8,128)(2,1)S(1)} %all_to_all.21.refs_0_, bf16[16,64,128]{2,1,0:T(8,128)(2,1)S(1)} %sort_left.1.refs_1_), custom_call_target="tpu_custom_call" | custom-call | flops 33554432 | bytes 1310720 | tf_op jit(solution)/shard_map/d_right/pallas_call | solution.py:65
  43.5 5.9 %all-to-all-start.3 = ((bf16[16,128,128]{2,1,0:T(8,128)(2,1)}), bf16[16,128,128]{2,1,0:T(8,128)(2,1)S(1)}, u32[]{:S(2)}, u32[]{:S(2)}) async-start(bf16[16,128,128]{2,1,0:T(8,128)(2,1)} %get-tuple-element.42), calls=%async_computation.3 | async-start | bytes 1048576 | tf_op jit(solution)/shard_map/all_to_all | solution.py:316
  50.6 1.4 %collective-permute-start.9 = (bf16[128,128]{1,0:T(8,128)(2,1)S(1)}, bf16[128,128]{1,0:T(8,128)(2,1)S(1)}, u32[]{:S(2)}, u32[]{:S(2)}) collective-permute-start(bf16[128,128]{1,0:T(8,128)(2,1)S(1)} %get-tuple-element.48), channel_id=1, source_target_pairs={{0,6},{1,7},{2,4},{3,5},{4,2},{5,3},{6,0},{7,1},{8,14},{9,15},{10,... | collective-permute-start | bytes 98312 | tf_op jit(solution)/shard_map/ppermute | solution.py:333
  52.0 0.9 %collective-permute-start.10 = (bf16[128,128]{1,0:T(8,128)(2,1)S(1)}, bf16[128,128]{1,0:T(8,128)(2,1)S(1)}, u32[]{:S(2)}, u32[]{:S(2)}) collective-permute-start(bf16[128,128]{1,0:T(8,128)(2,1)S(1)} %get-tuple-element.49), channel_id=1, source_target_pairs={{0,7},{1,6},{2,5},{3,4},{4,3},{5,2},{6,1},{7,0},{8,15},{9,14},{10,... | collective-permute-start | bytes 98312 | tf_op jit(solution)/shard_map/ppermute | solution.py:333
  53.5 1.5 %collective-permute-start.12 = (bf16[128,128]{1,0:T(8,128)(2,1)S(1)}, bf16[128,128]{1,0:T(8,128)(2,1)S(1)}, u32[]{:S(2)}, u32[]{:S(2)}) collective-permute-start(bf16[128,128]{1,0:T(8,128)(2,1)S(1)} %get-tuple-element.51), channel_id=1, source_target_pairs={{0,5},{1,4},{2,7},{3,6},{4,1},{5,0},{6,3},{7,2},{8,13},{9,12},{10,... | collective-permute-start | bytes 98312 | tf_op jit(solution)/shard_map/ppermute | solution.py:333
  55.0 1.9 %collective-permute-done.8.refs_2_ = bf16[128,128]{1,0:T(8,128)(2,1)S(1)} collective-permute-done((bf16[128,128]{1,0:T(8,128)(2,1)S(1)}, bf16[128,128]{1,0:T(8,128)(2,1)S(1)}, u32[]{:S(2)}, u32[]{:S(2)}) %collective-permute-start.8) | collective-permute-done | bytes 32800 | tf_op jit(solution)/shard_map/ppermute | solution.py:333
  58.0 1.0 %slopes.1 = (bf16[8,512,128]{2,1,0:T(8,128)(2,1)S(1)}, bf16[8,128,128]{2,1,0:T(8,128)(2,1)S(1)}, f32[8,128]{1,0:T(8,128)S(1)}, f32[128,128]{1,0:T(8,128)S(1)}, bf16[128,640]{1,0:T(8,128)(2,1)S(1)}) custom-call(bf16[8,128,128]{2,1,0:T(8,128)(2,1)S(1)} %copy-done.1, s32[1,128]{1,0:T(1,128)S(1)} %bitcast.15, f32[1,128]{1,0:T(1,128)S(1)} %bitcast.8, ...), custom_call_target="tpu_custom_call" | custom-call | flops 134217728 | bytes 2233856 | tf_op jit(solution)/shard_map/slopes/pallas_call | solution.py:65
  59.0 0.8 %collective-permute-done.9.refs_3_ = bf16[128,128]{1,0:T(8,128)(2,1)S(1)} collective-permute-done((bf16[128,128]{1,0:T(8,128)(2,1)S(1)}, bf16[128,128]{1,0:T(8,128)(2,1)S(1)}, u32[]{:S(2)}, u32[]{:S(2)}) %collective-permute-start.9) | collective-permute-done | bytes 32800 | tf_op jit(solution)/shard_map/ppermute | solution.py:333
  59.8 0.7 %collective-permute-done.10.refs_4_ = bf16[128,128]{1,0:T(8,128)(2,1)S(1)} collective-permute-done((bf16[128,128]{1,0:T(8,128)(2,1)S(1)}, bf16[128,128]{1,0:T(8,128)(2,1)S(1)}, u32[]{:S(2)}, u32[]{:S(2)}) %collective-permute-start.10) | collective-permute-done | bytes 32800 | tf_op jit(solution)/shard_map/ppermute | solution.py:333
  60.5 1.5 %collective-permute-done.11.refs_5_ = bf16[128,128]{1,0:T(8,128)(2,1)S(1)} collective-permute-done((bf16[128,128]{1,0:T(8,128)(2,1)S(1)}, bf16[128,128]{1,0:T(8,128)(2,1)S(1)}, u32[]{:S(2)}, u32[]{:S(2)}) %collective-permute-start.11) | collective-permute-done | bytes 32800 | tf_op jit(solution)/shard_map/ppermute | solution.py:333
  62.1 1.4 %finish.1 = bf16[8,128,128]{2,1,0:T(8,128)(2,1)} custom-call(bf16[16,128,128]{2,1,0:T(8,128)(2,1)S(1)} %all-to-all-done.3.refs_0_, bf16[8,128,128]{2,1,0:T(8,128)(2,1)S(1)} %sort_d_left.1.refs_1_, bf16[8,512,128]{2,1,0:T(8,128)(2,1)S(1)} %get-tuple-element.54.refs_2_, bf16[8,128,128]{2,1,0:T(8,128)(2,1)S(1)} %gate_back.1.refs_6_.refs_3_, ...), custom_call_target="tpu_custom_call" | custom-call | flops 134217728 | bytes 2854912 | tf_op jit(solution)/shard_map/finish/pallas_call | solution.py:65
  (44 shorter events, 6.1 us)
Async XLA Ops:
  2.4 8.6 %copy-start = (bf16[16,128,128]{2,1,0:T(8,128)(2,1)S(1)}, bf16[16,128,128]{2,1,0:T(8,128)(2,1)}, u32[]{:S(2)}) copy-start(bf16[16,128,128]{2,1,0:T(8,128)(2,1)} %project_right.1.refs_5_) | copy-start | bytes 1572868
  2.4 8.6 %copy-start.1 = (bf16[8,128,128]{2,1,0:T(8,128)(2,1)S(1)}, bf16[8,128,128]{2,1,0:T(8,128)(2,1)}, u32[]{:S(2)}) copy-start(bf16[8,128,128]{2,1,0:T(8,128)(2,1)} %refs_0_.7) | copy-start | bytes 786436
  2.4 8.6 %copy-start.2 = (bf16[128,512]{1,0:T(8,128)(2,1)S(1)}, bf16[128,512]{1,0:T(8,128)(2,1)}, u32[]{:S(2)}) copy-start(bf16[128,512]{1,0:T(8,128)(2,1)} %refs_4_.9) | copy-start | bytes 393220
  2.4 8.6 %copy-start.6 = (f32[128]{0:T(128)S(1)}, f32[128]{0:T(128)}, u32[]{:S(2)}) copy-start(f32[128]{0:T(128)} %param.13) | copy-start | bytes 1540
  2.4 8.6 %copy-start.7 = (f32[128]{0:T(128)S(1)}, f32[128]{0:T(128)}, u32[]{:S(2)}) copy-start(f32[128]{0:T(128)} %param.14) | copy-start | bytes 1540
  2.5 8.6 %copy-start.8 = (s32[128]{0:T(128)S(1)}, s32[128]{0:T(128)}, u32[]{:S(2)}) copy-start(s32[128]{0:T(128)} %param.12) | copy-start | bytes 1540
  2.5 21.3 %all-to-all-start = ((bf16[16,128,128]{2,1,0:T(8,128)(2,1)}), bf16[16,128,128]{2,1,0:T(8,128)(2,1)S(1)}, u32[]{:S(2)}, u32[]{:S(2)}) async-start(bf16[16,128,128]{2,1,0:T(8,128)(2,1)} %project_right.1.refs_5_), calls=%async_computation | async-start | bytes 1048576 | tf_op jit(solution)/shard_map/all_to_all | solution.py:316
  11.0 7.4 %copy-start.3 = (bf16[8,128,128]{2,1,0:T(8,128)(2,1)S(1)}, bf16[8,128,128]{2,1,0:T(8,128)(2,1)}, u32[]{:S(2)}) copy-start(bf16[8,128,128]{2,1,0:T(8,128)(2,1)} %refs_1_.1) | copy-start | bytes 786436
  11.1 7.3 %copy-start.4 = (bf16[128,128]{1,0:T(8,128)(2,1)S(1)}, bf16[128,128]{1,0:T(8,128)(2,1)}, u32[]{:S(2)}) copy-start(bf16[128,128]{1,0:T(8,128)(2,1)} %refs_4_.8) | copy-start | bytes 98308
  11.9 3.7 %collective-permute-start = (bf16[128,128]{1,0:T(8,128)(2,1)S(1)}, bf16[128,128]{1,0:T(8,128)(2,1)S(1)}, u32[]{:S(2)}, u32[]{:S(2)}) collective-permute-start(bf16[128,128]{1,0:T(8,128)(2,1)S(1)} %get-tuple-element.33), channel_id=1, source_target_pairs={{0,1},{1,0},{2,3},{3,2},{4,5},{5,4},{6,7},{7,6},{8,9},{9,8},{10,11... | collective-permute-start | bytes 98312 | tf_op jit(solution)/shard_map/ppermute | solution.py:333
  12.1 6.3 %collective-permute-start.1 = (bf16[128,128]{1,0:T(8,128)(2,1)S(1)}, bf16[128,128]{1,0:T(8,128)(2,1)S(1)}, u32[]{:S(2)}, u32[]{:S(2)}) collective-permute-start(bf16[128,128]{1,0:T(8,128)(2,1)S(1)} %get-tuple-element.34), channel_id=1, source_target_pairs={{0,2},{1,3},{2,0},{3,1},{4,6},{5,7},{6,4},{7,5},{8,10},{9,11},{10,... | collective-permute-start | bytes 98312 | tf_op jit(solution)/shard_map/ppermute | solution.py:333
  12.7 8.6 %collective-permute-start.2 = (bf16[128,128]{1,0:T(8,128)(2,1)S(1)}, bf16[128,128]{1,0:T(8,128)(2,1)S(1)}, u32[]{:S(2)}, u32[]{:S(2)}) collective-permute-start(bf16[128,128]{1,0:T(8,128)(2,1)S(1)} %get-tuple-element.35), channel_id=1, source_target_pairs={{0,6},{1,7},{2,4},{3,5},{4,2},{5,3},{6,0},{7,1},{8,14},{9,15},{10,... | collective-permute-start | bytes 98312 | tf_op jit(solution)/shard_map/ppermute | solution.py:333
  14.1 8.0 %collective-permute-start.3 = (bf16[128,128]{1,0:T(8,128)(2,1)S(1)}, bf16[128,128]{1,0:T(8,128)(2,1)S(1)}, u32[]{:S(2)}, u32[]{:S(2)}) collective-permute-start(bf16[128,128]{1,0:T(8,128)(2,1)S(1)} %get-tuple-element.36), channel_id=1, source_target_pairs={{0,7},{1,6},{2,5},{3,4},{4,3},{5,2},{6,1},{7,0},{8,15},{9,14},{10,... | collective-permute-start | bytes 98312 | tf_op jit(solution)/shard_map/ppermute | solution.py:333
  15.0 8.6 %collective-permute-start.4 = (bf16[128,128]{1,0:T(8,128)(2,1)S(1)}, bf16[128,128]{1,0:T(8,128)(2,1)S(1)}, u32[]{:S(2)}, u32[]{:S(2)}) collective-permute-start(bf16[128,128]{1,0:T(8,128)(2,1)S(1)} %get-tuple-element.37), channel_id=1, source_target_pairs={{0,4},{1,5},{2,6},{3,7},{4,0},{5,1},{6,2},{7,3},{8,12},{9,13},{10,... | collective-permute-start | bytes 98312 | tf_op jit(solution)/shard_map/ppermute | solution.py:333
  15.6 8.0 %collective-permute-start.5 = (bf16[128,128]{1,0:T(8,128)(2,1)S(1)}, bf16[128,128]{1,0:T(8,128)(2,1)S(1)}, u32[]{:S(2)}, u32[]{:S(2)}) collective-permute-start(bf16[128,128]{1,0:T(8,128)(2,1)S(1)} %get-tuple-element.38), channel_id=1, source_target_pairs={{0,5},{1,4},{2,7},{3,6},{4,1},{5,0},{6,3},{7,2},{8,13},{9,12},{10,... | collective-permute-start | bytes 98312 | tf_op jit(solution)/shard_map/ppermute | solution.py:333
  18.4 5.2 %collective-permute-start.6 = (bf16[128,128]{1,0:T(8,128)(2,1)S(1)}, bf16[128,128]{1,0:T(8,128)(2,1)S(1)}, u32[]{:S(2)}, u32[]{:S(2)}) collective-permute-start(bf16[128,128]{1,0:T(8,128)(2,1)S(1)} %get-tuple-element.39), channel_id=1, source_target_pairs={{0,3},{1,2},{2,1},{3,0},{4,7},{5,6},{6,5},{7,4},{8,11},{9,10},{10,... | collective-permute-start | bytes 98312 | tf_op jit(solution)/shard_map/ppermute | solution.py:333
  43.5 18.5 %all-to-all-start.3 = ((bf16[16,128,128]{2,1,0:T(8,128)(2,1)}), bf16[16,128,128]{2,1,0:T(8,128)(2,1)S(1)}, u32[]{:S(2)}, u32[]{:S(2)}) async-start(bf16[16,128,128]{2,1,0:T(8,128)(2,1)} %get-tuple-element.42), calls=%async_computation.3 | async-start | bytes 1048576 | tf_op jit(solution)/shard_map/all_to_all | solution.py:316
  49.8 3.7 %collective-permute-start.7 = (bf16[128,128]{1,0:T(8,128)(2,1)S(1)}, bf16[128,128]{1,0:T(8,128)(2,1)S(1)}, u32[]{:S(2)}, u32[]{:S(2)}) collective-permute-start(bf16[128,128]{1,0:T(8,128)(2,1)S(1)} %get-tuple-element.46), channel_id=1, source_target_pairs={{0,1},{1,0},{2,3},{3,2},{4,5},{5,4},{6,7},{7,6},{8,9},{9,8},{10,11... | collective-permute-start | bytes 98312 | tf_op jit(solution)/shard_map/ppermute | solution.py:333
  50.0 6.9 %collective-permute-start.8 = (bf16[128,128]{1,0:T(8,128)(2,1)S(1)}, bf16[128,128]{1,0:T(8,128)(2,1)S(1)}, u32[]{:S(2)}, u32[]{:S(2)}) collective-permute-start(bf16[128,128]{1,0:T(8,128)(2,1)S(1)} %get-tuple-element.47), channel_id=1, source_target_pairs={{0,2},{1,3},{2,0},{3,1},{4,6},{5,7},{6,4},{7,5},{8,10},{9,11},{10,... | collective-permute-start | bytes 98312 | tf_op jit(solution)/shard_map/ppermute | solution.py:333
  50.6 9.2 %collective-permute-start.9 = (bf16[128,128]{1,0:T(8,128)(2,1)S(1)}, bf16[128,128]{1,0:T(8,128)(2,1)S(1)}, u32[]{:S(2)}, u32[]{:S(2)}) collective-permute-start(bf16[128,128]{1,0:T(8,128)(2,1)S(1)} %get-tuple-element.48), channel_id=1, source_target_pairs={{0,6},{1,7},{2,4},{3,5},{4,2},{5,3},{6,0},{7,1},{8,14},{9,15},{10,... | collective-permute-start | bytes 98312 | tf_op jit(solution)/shard_map/ppermute | solution.py:333
  52.0 8.5 %collective-permute-start.10 = (bf16[128,128]{1,0:T(8,128)(2,1)S(1)}, bf16[128,128]{1,0:T(8,128)(2,1)S(1)}, u32[]{:S(2)}, u32[]{:S(2)}) collective-permute-start(bf16[128,128]{1,0:T(8,128)(2,1)S(1)} %get-tuple-element.49), channel_id=1, source_target_pairs={{0,7},{1,6},{2,5},{3,4},{4,3},{5,2},{6,1},{7,0},{8,15},{9,14},{10,... | collective-permute-start | bytes 98312 | tf_op jit(solution)/shard_map/ppermute | solution.py:333
  52.9 9.1 %collective-permute-start.11 = (bf16[128,128]{1,0:T(8,128)(2,1)S(1)}, bf16[128,128]{1,0:T(8,128)(2,1)S(1)}, u32[]{:S(2)}, u32[]{:S(2)}) collective-permute-start(bf16[128,128]{1,0:T(8,128)(2,1)S(1)} %get-tuple-element.50), channel_id=1, source_target_pairs={{0,4},{1,5},{2,6},{3,7},{4,0},{5,1},{6,2},{7,3},{8,12},{9,13},{10,... | collective-permute-start | bytes 98312 | tf_op jit(solution)/shard_map/ppermute | solution.py:333
  53.5 8.5 %collective-permute-start.12 = (bf16[128,128]{1,0:T(8,128)(2,1)S(1)}, bf16[128,128]{1,0:T(8,128)(2,1)S(1)}, u32[]{:S(2)}, u32[]{:S(2)}) collective-permute-start(bf16[128,128]{1,0:T(8,128)(2,1)S(1)} %get-tuple-element.51), channel_id=1, source_target_pairs={{0,5},{1,4},{2,7},{3,6},{4,1},{5,0},{6,3},{7,2},{8,13},{9,12},{10,... | collective-permute-start | bytes 98312 | tf_op jit(solution)/shard_map/ppermute | solution.py:333
  56.9 5.2 %collective-permute-start.13 = (bf16[128,128]{1,0:T(8,128)(2,1)S(1)}, bf16[128,128]{1,0:T(8,128)(2,1)S(1)}, u32[]{:S(2)}, u32[]{:S(2)}) collective-permute-start(bf16[128,128]{1,0:T(8,128)(2,1)S(1)} %get-tuple-element.52), channel_id=1, source_target_pairs={{0,3},{1,2},{2,1},{3,0},{4,7},{5,6},{6,5},{7,4},{8,11},{9,10},{10,... | collective-permute-start | bytes 98312 | tf_op jit(solution)/shard_map/ppermute | solution.py:333
  (3 other events, 8.7 us)

commit v16 on v15

--- a/solution.py
+++ b/solution.py
@@ -91,10 +91,13 @@
     return [cells[row : row + 1] for row in range(rows)]
 
 
-def wide_order(devices, count):
+def wide_order(devices, count, back):
     order = []
     for place in range(count):
-        order += [count + (place ^ 2), place ^ (count // 2)]
+        if back:
+            order += [place ^ (count // 2), count + place]
+        else:
+            order += [count + (place ^ 2), place ^ (count // 2)]
     return order
 
 
@@ -128,7 +131,7 @@
     for row, right in gated_rows(pair, mask, gain, bias, w_proj, 1):
         right = right.reshape(count, block, width).astype(BF16)
         for rank in range(devices):
-            place = wide_order(devices, count)[rank] % count
+            place = wide_order(devices, count, False)[rank] % count
             right_panel[rank, row * block : (row + 1) * block, :] = right[place]
 
 
@@ -166,9 +169,9 @@
     wide[...] = panel[...].astype(F32).reshape(wide.shape)
 
 
-def wide_places(panel, count):
+def wide_places(panel, count, back):
     devices, depth, _ = panel.shape
-    for rank, device in enumerate(wide_order(devices, count)):
+    for rank, device in enumerate(wide_order(devices, count, back)):
         yield rank, slice(device * depth, (device + 1) * depth)
 
 
@@ -187,7 +190,7 @@
     del after
     block, left_rows, _ = left_all.shape
     right_rows = right_all.shape[1]
-    for rank, place in wide_places(right_panel, products.shape[0]):
+    for rank, place in wide_places(right_panel, products.shape[0], False):
         right_wide[place, :] = right_panel[rank].astype(F32)
     for h in range(block):
         right = right_wide[pl.ds(h, right_rows, stride=block), :].astype(BF16)
@@ -224,7 +227,7 @@
         d_tri = left_wide[pl.ds(h, left_rows, stride=block), :].astype(BF16)
         d_tri_all[h] = d_tri
         right_wide[pl.ds(h, right_rows, stride=block), :] = dot(d_tri, left_all[h], 0, 0)
-    for rank, place in wide_places(d_right_panel, d_products.shape[0]):
+    for rank, place in wide_places(d_right_panel, d_products.shape[0], True):
         d_right_panel[rank] = right_wide[place, :].astype(BF16)
 
 
@@ -282,7 +285,7 @@
 
 
 def both_halves(blocks, count):
-    order = wide_order(2 * count, count)
+    order = wide_order(2 * count, count, True)
     return jnp.stack(
         [blocks[order.index(place)] + blocks[order.index(count + place)] for place in range(count)]
     )
@@ -311,8 +314,8 @@
         grad[row] = jnp.transpose(result).astype(BF16)
 
 
-def swap(values, count):
-    groups = [wide_order(lax.axis_size("row"), count)]
+def swap(values, count, back):
+    groups = [wide_order(lax.axis_size("row"), count, back)]
     return lax.all_to_all(
         values, "row", split_axis=0, concat_axis=0, tiled=True, axis_index_groups=groups
     )
@@ -374,7 +377,7 @@
         flops=2 * cells * channels * 2 * hidden,
         limit=64 * 1024 * 1024 - 640 * 1024,
     )
-    right_panel = swap(own_right, count)
+    right_panel = swap(own_right, count, False)
     pieces = call(
         project_left_kernel,
         "project_left",
@@ -427,7 +430,7 @@
         scratch=[left_wide, right_wide],
         flops=2 * block * left_rows * width * right_rows,
     )
-    d_right_panel = swap(d_right_panel, count)
+    d_right_panel = swap(d_right_panel, count, True)
     d_pieces = call(
         d_left_kernel,
         "d_left",

time: 63.9 us -> 62.7 us (0.981)
  waiting for transfers between devices: 9.91 us -> 8.85 us
    ppermute x14, waiting for transfers between devices: 9.91 us -> 8.39 us  [swap_pieces(): lax.ppermute(pieces[step], 'row', [(d, d ^ distance(step, count)) for d i...]
    all_to_all x2, starting transfers between devices: 14.4 us -> 13.4 us  [swap(): lax.all_to_all(values, 'row', split_axis=0, concat_axis=0, tiled=True, ax...]
    ppermute x14, starting transfers between devices: 10.4 us -> 11.3 us  [swap_pieces(): lax.ppermute(pieces[step], 'row', [(d, d ^ distance(step, count)) for d i...]
  transfers between devices with their start and end apart: 16 -> 16, of which waited for: 8 -> 10; matrix products, arithmetic and copies ran while one was open for 0% -> 0% of each run, Pallas kernels for 6% -> 6%
where the time goes in v16:
time: 62.7 us; the launch traced here: 62.3 us
  starting transfers between devices  24.7 us (39%)
  blocking collectives  17.3 us (28%)
  Pallas kernels  9.82 us (16%)
  waiting for transfers between devices  8.85 us (14%)
  local copies, waits for them, and re-layouts  1.34 us (2%)
    all_to_all x2, blocking collectives, swap_half(): lax.all_to_all(values, 'row', split_axis=0, concat_axis=0, tiled=True, ax...  17.3 us
    all_to_all x2, starting transfers between devices, swap(): lax.all_to_all(values, 'row', split_axis=0, concat_axis=0, tiled=True, ax...  13.4 us
    ppermute x14, starting transfers between devices, swap_pieces(): lax.ppermute(pieces[step], 'row', [(d, d ^ distance(step, count)) for d i...  11.3 us
    pallas_call x12, Pallas kernels, call(): pl.pallas_call(body, name=name, out_shape=outs, in_specs=[pl.BlockSpec(me...  9.82 us
    ppermute x14, waiting for transfers between devices, swap_pieces(): lax.ppermute(pieces[step], 'row', [(d, d ^ distance(step, count)) for d i...  8.39 us
    unnamed x22, local copies, waits for them, and re-layouts  1.34 us
  transfers between devices with their start and end apart: 16, of which 10 were waited for; matrix products, arithmetic and copies ran while one was open for 0% of the time, Pallas kernels for 6%

profile of v16, /device:TPU:0, one launch (start us, length us, event | category | flops | bytes accessed | tf_op | source)
XLA Modules:
  0.0 62.3 jit_solution(11361310024780539006)
XLA Ops:
  0.0 2.4 %project_right.1.refs_5_ = bf16[16,128,128]{2,1,0:T(8,128)(2,1)} custom-call(bf16[8,128,128]{2,1,0:T(8,128)(2,1)} %refs_0_.7, s32[1,128]{1,0:T(1,128)} %bitcast.13, f32[1,128]{1,0:T(1,128)} %bitcast.5, f32[1,128]{1,0:T(1,128)} %bitcast.9, bf16[128,512]{1,0:T(8,128)(2,1)} %refs_4_.9), custom_call_target="tpu_custom_call" | custom-call | flops 67108864 | bytes 919040 | tf_op jit(solution)/shard_map/project_right/pallas_call | solution.py:65
  2.5 8.5 %all-to-all-start = ((bf16[16,128,128]{2,1,0:T(8,128)(2,1)}), bf16[16,128,128]{2,1,0:T(8,128)(2,1)S(1)}, u32[]{:S(2)}, u32[]{:S(2)}) async-start(bf16[16,128,128]{2,1,0:T(8,128)(2,1)} %project_right.1.refs_5_), calls=%async_computation | async-start | bytes 1048576 | tf_op jit(solution)/shard_map/all_to_all | solution.py:319
  11.1 0.8 %project_left.1 = (bf16[128,128]{1,0:T(8,128)(2,1)S(1)}, bf16[128,128]{1,0:T(8,128)(2,1)S(1)}, bf16[128,128]{1,0:T(8,128)(2,1)S(1)}, bf16[128,128]{1,0:T(8,128)(...) custom-call(bf16[8,128,128]{2,1,0:T(8,128)(2,1)S(1)} %copy-done.1, ...), custom_call_target="tpu_custom_call" | custom-call | flops 67108864 | bytes 1181184 | tf_op jit(solution)/shard_map/project_left/pallas_call | solution.py:65
  12.7 1.4 %collective-permute-start.2 = (bf16[128,128]{1,0:T(8,128)(2,1)S(1)}, bf16[128,128]{1,0:T(8,128)(2,1)S(1)}, u32[]{:S(2)}, u32[]{:S(2)}) collective-permute-start(bf16[128,128]{1,0:T(8,128)(2,1)S(1)} %get-tuple-element.35), channel_id=1, source_target_pairs={{0,6},{1,7},{2,4},{3,5},{4,2},{5,3},{6,0},{7,1},{8,14},{9,15},{10,... | collective-permute-start | bytes 98312 | tf_op jit(solution)/shard_map/ppermute | solution.py:336
  14.1 0.9 %collective-permute-start.3 = (bf16[128,128]{1,0:T(8,128)(2,1)S(1)}, bf16[128,128]{1,0:T(8,128)(2,1)S(1)}, u32[]{:S(2)}, u32[]{:S(2)}) collective-permute-start(bf16[128,128]{1,0:T(8,128)(2,1)S(1)} %get-tuple-element.36), channel_id=1, source_target_pairs={{0,7},{1,6},{2,5},{3,4},{4,3},{5,2},{6,1},{7,0},{8,15},{9,14},{10,... | collective-permute-start | bytes 98312 | tf_op jit(solution)/shard_map/ppermute | solution.py:336
  15.6 1.5 %collective-permute-start.5 = (bf16[128,128]{1,0:T(8,128)(2,1)S(1)}, bf16[128,128]{1,0:T(8,128)(2,1)S(1)}, u32[]{:S(2)}, u32[]{:S(2)}) collective-permute-start(bf16[128,128]{1,0:T(8,128)(2,1)S(1)} %get-tuple-element.38), channel_id=1, source_target_pairs={{0,5},{1,4},{2,7},{3,6},{4,1},{5,0},{6,3},{7,2},{8,13},{9,12},{10,... | collective-permute-start | bytes 98312 | tf_op jit(solution)/shard_map/ppermute | solution.py:336
  17.1 1.3 %collective-permute-done.1.refs_2_ = bf16[128,128]{1,0:T(8,128)(2,1)S(1)} collective-permute-done((bf16[128,128]{1,0:T(8,128)(2,1)S(1)}, bf16[128,128]{1,0:T(8,128)(2,1)S(1)}, u32[]{:S(2)}, u32[]{:S(2)}) %collective-permute-start.1) | collective-permute-done | bytes 32800 | tf_op jit(solution)/shard_map/ppermute | solution.py:336
  19.1 0.8 %prepare.1 = (f32[8,128,128]{2,1,0:T(8,128)S(1)}, f32[8,128,128]{2,1,0:T(8,128)S(1)}) custom-call(bf16[8,128,128]{2,1,0:T(8,128)(2,1)S(1)} %copy-done.1, bf16[8,128,128]{2,1,0:T(8,128)(2,1)S(1)} %copy-done.3, f32[1,128]{1,0:T(1,128)S(1)} %bitcast.7, f32[1,128]{1,0:T(1,128)S(1)} %bitcast.11, bf16[128,128]{1,0:T(8,128)(2,1)S(1)} %copy-done.5, ...), custom_call_target="tpu_custom_call" | custom-call | flops 67108864 | bytes 1639936 | tf_op jit(solution)/shard_map/prepare/pallas_call | solution.py:65
  19.9 1.5 %collective-permute-done.2.refs_3_ = bf16[128,128]{1,0:T(8,128)(2,1)S(1)} collective-permute-done((bf16[128,128]{1,0:T(8,128)(2,1)S(1)}, bf16[128,128]{1,0:T(8,128)(2,1)S(1)}, u32[]{:S(2)}, u32[]{:S(2)}) %collective-permute-start.2) | collective-permute-done | bytes 32800 | tf_op jit(solution)/shard_map/ppermute | solution.py:336
  21.3 0.7 %collective-permute-done.3.refs_4_ = bf16[128,128]{1,0:T(8,128)(2,1)S(1)} collective-permute-done((bf16[128,128]{1,0:T(8,128)(2,1)S(1)}, bf16[128,128]{1,0:T(8,128)(2,1)S(1)}, u32[]{:S(2)}, u32[]{:S(2)}) %collective-permute-start.3) | collective-permute-done | bytes 32800 | tf_op jit(solution)/shard_map/ppermute | solution.py:336
  22.0 1.5 %collective-permute-done.4.refs_5_ = bf16[128,128]{1,0:T(8,128)(2,1)S(1)} collective-permute-done((bf16[128,128]{1,0:T(8,128)(2,1)S(1)}, bf16[128,128]{1,0:T(8,128)(2,1)S(1)}, u32[]{:S(2)}, u32[]{:S(2)}) %collective-permute-start.4) | collective-permute-done | bytes 32800 | tf_op jit(solution)/shard_map/ppermute | solution.py:336
  23.8 0.6 %tri.1 = (bf16[8,128,128]{2,1,0:T(8,128)(2,1)S(1)}, bf16[16,128,128]{2,1,0:T(8,128)(2,1)S(1)}) custom-call(bf16[16,128,128]{2,1,0:T(8,128)(2,1)S(1)} %all-to-all-done.refs_0_, bf16[16,64,128]{2,1,0:T(8,128)(2,1)S(1)} %sort_left.1.refs_1_, f32[8,128,128]{2,1,0:T(8,128)S(1)} %get-tuple-element.40.refs_2_.refs_1_), custom_call_target="tpu_custom_call" | custom-call | flops 33554432 | bytes 2097152 | tf_op jit(solution)/shard_map/tri/pallas_call | solution.py:65
  24.5 8.7 %all_to_all.20.refs_0_ = bf16[8,128,128]{2,1,0:T(8,128)(2,1)S(1)} all-to-all(bf16[8,128,128]{2,1,0:T(8,128)(2,1)S(1)} %get-tuple-element.41), channel_id=1, replica_groups={{0,1,2,3,4,5,6,7},{8,9,10,11,12,13,14,15},{16,17,18,19,20,21,22,23},{24..., dimensions={0} | all-to-all | bytes 524288 | tf_op jit(solution)/shard_map/all_to_all | solution.py:327
  33.5 8.6 %all_to_all.21.refs_0_ = bf16[8,128,128]{2,1,0:T(8,128)(2,1)S(1)} all-to-all(bf16[8,128,128]{2,1,0:T(8,128)(2,1)S(1)} %middle.1), channel_id=1, replica_groups={{0,1,2,3,4,5,6,7},{8,9,10,11,12,13,14,15},{16,17,18,19,20,21,22,23},{24..., dimensions={0} | all-to-all | bytes 524288 | tf_op jit(solution)/shard_map/all_to_all | solution.py:327
  42.1 1.5 %d_right.1 = (bf16[16,128,128]{2,1,0:T(8,128)(2,1)}, bf16[16,64,128]{2,1,0:T(8,128)(2,1)S(1)}) custom-call(bf16[8,128,128]{2,1,0:T(8,128)(2,1)S(1)} %all_to_all.21.refs_0_, bf16[16,64,128]{2,1,0:T(8,128)(2,1)S(1)} %sort_left.1.refs_1_), custom_call_target="tpu_custom_call" | custom-call | flops 33554432 | bytes 1310720 | tf_op jit(solution)/shard_map/d_right/pallas_call | solution.py:65
  43.5 4.9 %all-to-all-start.3 = ((bf16[16,128,128]{2,1,0:T(8,128)(2,1)}), bf16[16,128,128]{2,1,0:T(8,128)(2,1)S(1)}, u32[]{:S(2)}, u32[]{:S(2)}) async-start(bf16[16,128,128]{2,1,0:T(8,128)(2,1)} %get-tuple-element.42), calls=%async_computation.3 | async-start | bytes 1048576 | tf_op jit(solution)/shard_map/all_to_all | solution.py:319
  49.0 1.5 %collective-permute-start.8 = (bf16[128,128]{1,0:T(8,128)(2,1)S(1)}, bf16[128,128]{1,0:T(8,128)(2,1)S(1)}, u32[]{:S(2)}, u32[]{:S(2)}) collective-permute-start(bf16[128,128]{1,0:T(8,128)(2,1)S(1)} %get-tuple-element.47), channel_id=1, source_target_pairs={{0,2},{1,3},{2,0},{3,1},{4,6},{5,7},{6,4},{7,5},{8,10},{9,11},{10,... | collective-permute-start | bytes 98312 | tf_op jit(solution)/shard_map/ppermute | solution.py:336
  50.8 2.0 %collective-permute-start.10 = (bf16[128,128]{1,0:T(8,128)(2,1)S(1)}, bf16[128,128]{1,0:T(8,128)(2,1)S(1)}, u32[]{:S(2)}, u32[]{:S(2)}) collective-permute-start(bf16[128,128]{1,0:T(8,128)(2,1)S(1)} %get-tuple-element.49), channel_id=1, source_target_pairs={{0,7},{1,6},{2,5},{3,4},{4,3},{5,2},{6,1},{7,0},{8,15},{9,14},{10,... | collective-permute-start | bytes 98312 | tf_op jit(solution)/shard_map/ppermute | solution.py:336
  53.3 1.6 %collective-permute-start.12 = (bf16[128,128]{1,0:T(8,128)(2,1)S(1)}, bf16[128,128]{1,0:T(8,128)(2,1)S(1)}, u32[]{:S(2)}, u32[]{:S(2)}) collective-permute-start(bf16[128,128]{1,0:T(8,128)(2,1)S(1)} %get-tuple-element.51), channel_id=1, source_target_pairs={{0,5},{1,4},{2,7},{3,6},{4,1},{5,0},{6,3},{7,2},{8,13},{9,12},{10,... | collective-permute-start | bytes 98312 | tf_op jit(solution)/shard_map/ppermute | solution.py:336
  54.9 1.2 %collective-permute-done.8.refs_2_ = bf16[128,128]{1,0:T(8,128)(2,1)S(1)} collective-permute-done((bf16[128,128]{1,0:T(8,128)(2,1)S(1)}, bf16[128,128]{1,0:T(8,128)(2,1)S(1)}, u32[]{:S(2)}, u32[]{:S(2)}) %collective-permute-start.8) | collective-permute-done | bytes 32800 | tf_op jit(solution)/shard_map/ppermute | solution.py:336
  56.1 0.7 %copy-done.10 = f32[128]{0:T(128)S(1)} copy-done((f32[128]{0:T(128)S(1)}, f32[128]{0:T(128)}, u32[]{:S(2)}) %copy-start.10) | copy-done | bytes 536
  57.2 1.0 %slopes.1 = (bf16[8,512,128]{2,1,0:T(8,128)(2,1)S(1)}, bf16[8,128,128]{2,1,0:T(8,128)(2,1)S(1)}, f32[8,128]{1,0:T(8,128)S(1)}, f32[128,128]{1,0:T(8,128)S(1)}, bf16[128,640]{1,0:T(8,128)(2,1)S(1)}) custom-call(bf16[8,128,128]{2,1,0:T(8,128)(2,1)S(1)} %copy-done.1, s32[1,128]{1,0:T(1,128)S(1)} %bitcast.15, f32[1,128]{1,0:T(1,128)S(1)} %bitcast.8, ...), custom_call_target="tpu_custom_call" | custom-call | flops 134217728 | bytes 2233856 | tf_op jit(solution)/shard_map/slopes/pallas_call | solution.py:65
  58.8 0.7 %collective-permute-done.10.refs_4_ = bf16[128,128]{1,0:T(8,128)(2,1)S(1)} collective-permute-done((bf16[128,128]{1,0:T(8,128)(2,1)S(1)}, bf16[128,128]{1,0:T(8,128)(2,1)S(1)}, u32[]{:S(2)}, u32[]{:S(2)}) %collective-permute-start.10) | collective-permute-done | bytes 32800 | tf_op jit(solution)/shard_map/ppermute | solution.py:336
  60.9 1.4 %finish.1 = bf16[8,128,128]{2,1,0:T(8,128)(2,1)} custom-call(bf16[16,128,128]{2,1,0:T(8,128)(2,1)S(1)} %all-to-all-done.3.refs_0_, bf16[8,128,128]{2,1,0:T(8,128)(2,1)S(1)} %sort_d_left.1.refs_1_, bf16[8,512,128]{2,1,0:T(8,128)(2,1)S(1)} %get-tuple-element.54.refs_2_, bf16[8,128,128]{2,1,0:T(8,128)(2,1)S(1)} %gate_back.1.refs_6_.refs_3_, ...), custom_call_target="tpu_custom_call" | custom-call | flops 134217728 | bytes 2854912 | tf_op jit(solution)/shard_map/finish/pallas_call | solution.py:65
  (44 shorter events, 6.3 us)
Async XLA Ops:
  2.4 8.6 %copy-start = (bf16[16,128,128]{2,1,0:T(8,128)(2,1)S(1)}, bf16[16,128,128]{2,1,0:T(8,128)(2,1)}, u32[]{:S(2)}) copy-start(bf16[16,128,128]{2,1,0:T(8,128)(2,1)} %project_right.1.refs_5_) | copy-start | bytes 1572868
  2.4 8.6 %copy-start.1 = (bf16[8,128,128]{2,1,0:T(8,128)(2,1)S(1)}, bf16[8,128,128]{2,1,0:T(8,128)(2,1)}, u32[]{:S(2)}) copy-start(bf16[8,128,128]{2,1,0:T(8,128)(2,1)} %refs_0_.7) | copy-start | bytes 786436
  2.4 8.6 %copy-start.2 = (bf16[128,512]{1,0:T(8,128)(2,1)S(1)}, bf16[128,512]{1,0:T(8,128)(2,1)}, u32[]{:S(2)}) copy-start(bf16[128,512]{1,0:T(8,128)(2,1)} %refs_4_.9) | copy-start | bytes 393220
  2.4 8.6 %copy-start.6 = (f32[128]{0:T(128)S(1)}, f32[128]{0:T(128)}, u32[]{:S(2)}) copy-start(f32[128]{0:T(128)} %param.13) | copy-start | bytes 1540
  2.4 8.6 %copy-start.7 = (f32[128]{0:T(128)S(1)}, f32[128]{0:T(128)}, u32[]{:S(2)}) copy-start(f32[128]{0:T(128)} %param.14) | copy-start | bytes 1540
  2.5 8.6 %copy-start.8 = (s32[128]{0:T(128)S(1)}, s32[128]{0:T(128)}, u32[]{:S(2)}) copy-start(s32[128]{0:T(128)} %param.12) | copy-start | bytes 1540
  2.5 21.3 %all-to-all-start = ((bf16[16,128,128]{2,1,0:T(8,128)(2,1)}), bf16[16,128,128]{2,1,0:T(8,128)(2,1)S(1)}, u32[]{:S(2)}, u32[]{:S(2)}) async-start(bf16[16,128,128]{2,1,0:T(8,128)(2,1)} %project_right.1.refs_5_), calls=%async_computation | async-start | bytes 1048576 | tf_op jit(solution)/shard_map/all_to_all | solution.py:319
  11.0 7.4 %copy-start.3 = (bf16[8,128,128]{2,1,0:T(8,128)(2,1)S(1)}, bf16[8,128,128]{2,1,0:T(8,128)(2,1)}, u32[]{:S(2)}) copy-start(bf16[8,128,128]{2,1,0:T(8,128)(2,1)} %refs_1_.1) | copy-start | bytes 786436
  11.1 7.3 %copy-start.4 = (bf16[128,128]{1,0:T(8,128)(2,1)S(1)}, bf16[128,128]{1,0:T(8,128)(2,1)}, u32[]{:S(2)}) copy-start(bf16[128,128]{1,0:T(8,128)(2,1)} %refs_4_.8) | copy-start | bytes 98308
  11.9 3.7 %collective-permute-start = (bf16[128,128]{1,0:T(8,128)(2,1)S(1)}, bf16[128,128]{1,0:T(8,128)(2,1)S(1)}, u32[]{:S(2)}, u32[]{:S(2)}) collective-permute-start(bf16[128,128]{1,0:T(8,128)(2,1)S(1)} %get-tuple-element.33), channel_id=1, source_target_pairs={{0,1},{1,0},{2,3},{3,2},{4,5},{5,4},{6,7},{7,6},{8,9},{9,8},{10,11... | collective-permute-start | bytes 98312 | tf_op jit(solution)/shard_map/ppermute | solution.py:336
  12.1 6.3 %collective-permute-start.1 = (bf16[128,128]{1,0:T(8,128)(2,1)S(1)}, bf16[128,128]{1,0:T(8,128)(2,1)S(1)}, u32[]{:S(2)}, u32[]{:S(2)}) collective-permute-start(bf16[128,128]{1,0:T(8,128)(2,1)S(1)} %get-tuple-element.34), channel_id=1, source_target_pairs={{0,2},{1,3},{2,0},{3,1},{4,6},{5,7},{6,4},{7,5},{8,10},{9,11},{10,... | collective-permute-start | bytes 98312 | tf_op jit(solution)/shard_map/ppermute | solution.py:336
  12.7 8.6 %collective-permute-start.2 = (bf16[128,128]{1,0:T(8,128)(2,1)S(1)}, bf16[128,128]{1,0:T(8,128)(2,1)S(1)}, u32[]{:S(2)}, u32[]{:S(2)}) collective-permute-start(bf16[128,128]{1,0:T(8,128)(2,1)S(1)} %get-tuple-element.35), channel_id=1, source_target_pairs={{0,6},{1,7},{2,4},{3,5},{4,2},{5,3},{6,0},{7,1},{8,14},{9,15},{10,... | collective-permute-start | bytes 98312 | tf_op jit(solution)/shard_map/ppermute | solution.py:336
  14.1 8.0 %collective-permute-start.3 = (bf16[128,128]{1,0:T(8,128)(2,1)S(1)}, bf16[128,128]{1,0:T(8,128)(2,1)S(1)}, u32[]{:S(2)}, u32[]{:S(2)}) collective-permute-start(bf16[128,128]{1,0:T(8,128)(2,1)S(1)} %get-tuple-element.36), channel_id=1, source_target_pairs={{0,7},{1,6},{2,5},{3,4},{4,3},{5,2},{6,1},{7,0},{8,15},{9,14},{10,... | collective-permute-start | bytes 98312 | tf_op jit(solution)/shard_map/ppermute | solution.py:336
  15.0 8.6 %collective-permute-start.4 = (bf16[128,128]{1,0:T(8,128)(2,1)S(1)}, bf16[128,128]{1,0:T(8,128)(2,1)S(1)}, u32[]{:S(2)}, u32[]{:S(2)}) collective-permute-start(bf16[128,128]{1,0:T(8,128)(2,1)S(1)} %get-tuple-element.37), channel_id=1, source_target_pairs={{0,4},{1,5},{2,6},{3,7},{4,0},{5,1},{6,2},{7,3},{8,12},{9,13},{10,... | collective-permute-start | bytes 98312 | tf_op jit(solution)/shard_map/ppermute | solution.py:336
  15.6 8.0 %collective-permute-start.5 = (bf16[128,128]{1,0:T(8,128)(2,1)S(1)}, bf16[128,128]{1,0:T(8,128)(2,1)S(1)}, u32[]{:S(2)}, u32[]{:S(2)}) collective-permute-start(bf16[128,128]{1,0:T(8,128)(2,1)S(1)} %get-tuple-element.38), channel_id=1, source_target_pairs={{0,5},{1,4},{2,7},{3,6},{4,1},{5,0},{6,3},{7,2},{8,13},{9,12},{10,... | collective-permute-start | bytes 98312 | tf_op jit(solution)/shard_map/ppermute | solution.py:336
  18.4 5.2 %collective-permute-start.6 = (bf16[128,128]{1,0:T(8,128)(2,1)S(1)}, bf16[128,128]{1,0:T(8,128)(2,1)S(1)}, u32[]{:S(2)}, u32[]{:S(2)}) collective-permute-start(bf16[128,128]{1,0:T(8,128)(2,1)S(1)} %get-tuple-element.39), channel_id=1, source_target_pairs={{0,3},{1,2},{2,1},{3,0},{4,7},{5,6},{6,5},{7,4},{8,11},{9,10},{10,... | collective-permute-start | bytes 98312 | tf_op jit(solution)/shard_map/ppermute | solution.py:336
  43.5 17.3 %all-to-all-start.3 = ((bf16[16,128,128]{2,1,0:T(8,128)(2,1)}), bf16[16,128,128]{2,1,0:T(8,128)(2,1)S(1)}, u32[]{:S(2)}, u32[]{:S(2)}) async-start(bf16[16,128,128]{2,1,0:T(8,128)(2,1)} %get-tuple-element.42), calls=%async_computation.3 | async-start | bytes 1048576 | tf_op jit(solution)/shard_map/all_to_all | solution.py:319
  48.8 4.5 %collective-permute-start.7 = (bf16[128,128]{1,0:T(8,128)(2,1)S(1)}, bf16[128,128]{1,0:T(8,128)(2,1)S(1)}, u32[]{:S(2)}, u32[]{:S(2)}) collective-permute-start(bf16[128,128]{1,0:T(8,128)(2,1)S(1)} %get-tuple-element.46), channel_id=1, source_target_pairs={{0,1},{1,0},{2,3},{3,2},{4,5},{5,4},{6,7},{7,6},{8,9},{9,8},{10,11... | collective-permute-start | bytes 98312 | tf_op jit(solution)/shard_map/ppermute | solution.py:336
  49.0 7.1 %collective-permute-start.8 = (bf16[128,128]{1,0:T(8,128)(2,1)S(1)}, bf16[128,128]{1,0:T(8,128)(2,1)S(1)}, u32[]{:S(2)}, u32[]{:S(2)}) collective-permute-start(bf16[128,128]{1,0:T(8,128)(2,1)S(1)} %get-tuple-element.47), channel_id=1, source_target_pairs={{0,2},{1,3},{2,0},{3,1},{4,6},{5,7},{6,4},{7,5},{8,10},{9,11},{10,... | collective-permute-start | bytes 98312 | tf_op jit(solution)/shard_map/ppermute | solution.py:336
  50.5 8.3 %collective-permute-start.9 = (bf16[128,128]{1,0:T(8,128)(2,1)S(1)}, bf16[128,128]{1,0:T(8,128)(2,1)S(1)}, u32[]{:S(2)}, u32[]{:S(2)}) collective-permute-start(bf16[128,128]{1,0:T(8,128)(2,1)S(1)} %get-tuple-element.48), channel_id=1, source_target_pairs={{0,6},{1,7},{2,4},{3,5},{4,2},{5,3},{6,0},{7,1},{8,14},{9,15},{10,... | collective-permute-start | bytes 98312 | tf_op jit(solution)/shard_map/ppermute | solution.py:336
  50.8 8.7 %collective-permute-start.10 = (bf16[128,128]{1,0:T(8,128)(2,1)S(1)}, bf16[128,128]{1,0:T(8,128)(2,1)S(1)}, u32[]{:S(2)}, u32[]{:S(2)}) collective-permute-start(bf16[128,128]{1,0:T(8,128)(2,1)S(1)} %get-tuple-element.49), channel_id=1, source_target_pairs={{0,7},{1,6},{2,5},{3,4},{4,3},{5,2},{6,1},{7,0},{8,15},{9,14},{10,... | collective-permute-start | bytes 98312 | tf_op jit(solution)/shard_map/ppermute | solution.py:336
  52.8 7.2 %collective-permute-start.11 = (bf16[128,128]{1,0:T(8,128)(2,1)S(1)}, bf16[128,128]{1,0:T(8,128)(2,1)S(1)}, u32[]{:S(2)}, u32[]{:S(2)}) collective-permute-start(bf16[128,128]{1,0:T(8,128)(2,1)S(1)} %get-tuple-element.50), channel_id=1, source_target_pairs={{0,4},{1,5},{2,6},{3,7},{4,0},{5,1},{6,2},{7,3},{8,12},{9,13},{10,... | collective-permute-start | bytes 98312 | tf_op jit(solution)/shard_map/ppermute | solution.py:336
  53.3 7.1 %collective-permute-start.12 = (bf16[128,128]{1,0:T(8,128)(2,1)S(1)}, bf16[128,128]{1,0:T(8,128)(2,1)S(1)}, u32[]{:S(2)}, u32[]{:S(2)}) collective-permute-start(bf16[128,128]{1,0:T(8,128)(2,1)S(1)} %get-tuple-element.51), channel_id=1, source_target_pairs={{0,5},{1,4},{2,7},{3,6},{4,1},{5,0},{6,3},{7,2},{8,13},{9,12},{10,... | collective-permute-start | bytes 98312 | tf_op jit(solution)/shard_map/ppermute | solution.py:336
  56.1 4.3 %collective-permute-start.13 = (bf16[128,128]{1,0:T(8,128)(2,1)S(1)}, bf16[128,128]{1,0:T(8,128)(2,1)S(1)}, u32[]{:S(2)}, u32[]{:S(2)}) collective-permute-start(bf16[128,128]{1,0:T(8,128)(2,1)S(1)} %get-tuple-element.52), channel_id=1, source_target_pairs={{0,3},{1,2},{2,1},{3,0},{4,7},{5,6},{6,5},{7,4},{8,11},{9,10},{10,... | collective-permute-start | bytes 98312 | tf_op jit(solution)/shard_map/ppermute | solution.py:336
  (3 other events, 8.7 us)

commit v17 on v16

--- a/solution.py
+++ b/solution.py
@@ -101,13 +101,33 @@
     return order
 
 
-def distance(step, count):
-    far = sorted(range(3, count), key=lambda apart: -(apart // 2))
-    return [*range(min(3, count)), *far][step]
-
-
-def partner(step, count):
-    return lax.rem(lax.axis_index("row"), count) ^ distance(step, count)
+def distances(count, beside):
+    far = sorted(range(2, count), key=lambda apart: -(apart // 2))
+    if beside:
+        return [0, 1, 2] + [apart for apart in far if apart != 2]
+    return [0] + far + [1]
+
+
+def partners(count, beside):
+    place = lax.rem(lax.axis_index("row"), count)
+    return [place ^ apart for apart in distances(count, beside)]
+
+
+def gather(pieces, panel, beside):
+    for place, piece in zip(partners(len(pieces), beside), pieces):
+        panel[place] = piece[...]
+
+
+def spread(pieces, wide, beside):
+    depth = pieces[0].shape[0]
+    for place, piece in zip(partners(len(pieces), beside), pieces):
+        wide[pl.ds(pl.multiple_of(place * depth, depth), depth), :] = piece[...].astype(F32)
+
+
+def hand_out(wide, pieces, beside):
+    depth = pieces[0].shape[0]
+    for place, piece in zip(partners(len(pieces), beside), pieces):
+        piece[...] = wide[pl.ds(pl.multiple_of(place * depth, depth), depth), :].astype(BF16)
 
 
 def gated_rows(pair, mask, gain, bias, w_proj, side):
@@ -144,8 +164,8 @@
     for row, left in gated_rows(pair, mask, gain, bias, w_proj, 0):
         left = left.reshape(count, block, width).astype(BF16)
         left_panel[:, row * block : (row + 1) * block, :] = left
-    for step, piece in enumerate(pieces):
-        piece[...] = left_panel[partner(step, count)]
+    for place, piece in zip(partners(count, True), pieces):
+        piece[...] = left_panel[place]
 
 
 def prepare_kernel(
@@ -165,10 +185,6 @@
         gate_slope[row] = cot * gate * (1.0 - gate)
 
 
-def spread(panel, wide):
-    wide[...] = panel[...].astype(F32).reshape(wide.shape)
-
-
 def wide_places(panel, count, back):
     devices, depth, _ = panel.shape
     for rank, device in enumerate(wide_order(devices, count, back)):
@@ -178,25 +194,23 @@
 def sort_left_kernel(*refs):
     *pieces, left_all, left_wide = refs
     block, left_rows, _ = left_all.shape
-    depth = pieces[0].shape[0]
-    for step, piece in enumerate(pieces):
-        start = pl.multiple_of(partner(step, len(pieces)) * depth, depth)
-        left_wide[pl.ds(start, depth), :] = piece[...].astype(F32)
+    spread(pieces, left_wide, True)
     for h in range(block):
         left_all[h] = left_wide[pl.ds(h, left_rows, stride=block), :].astype(BF16)
 
 
-def tri_kernel(right_panel, left_all, after, products, right_all, left_wide, right_wide):
+def tri_kernel(right_panel, left_all, after, *refs):
     del after
+    right_all, *pieces, left_wide, right_wide = refs
     block, left_rows, _ = left_all.shape
     right_rows = right_all.shape[1]
-    for rank, place in wide_places(right_panel, products.shape[0], False):
+    for rank, place in wide_places(right_panel, len(pieces), False):
         right_wide[place, :] = right_panel[rank].astype(F32)
     for h in range(block):
         right = right_wide[pl.ds(h, right_rows, stride=block), :].astype(BF16)
         right_all[h] = right
         left_wide[pl.ds(h, left_rows, stride=block), :] = dot(left_all[h], right, 1, 1)
-    products[...] = left_wide[...].astype(BF16).reshape(products.shape)
+    hand_out(left_wide, pieces, False)
 
 
 def cell_row(ref, row, rows):
@@ -205,29 +219,36 @@
     return ref[:, row * block : (row + 1) * block, :].astype(F32).reshape(count * block, width)
 
 
-def middle_kernel(products, d_hat_centered, d_products):
+def middle_kernel(d_hat_centered, *refs):
+    count = (len(refs) - 2) // 2
+    products, pieces = refs[:count], refs[count : 2 * count]
+    panel, d_panel = refs[2 * count :]
     rows = d_hat_centered.shape[0]
-    count, depth, width = products.shape
+    _, depth, width = panel.shape
     block = depth // rows
+    gather(products, panel, False)
     for row in range(rows):
-        tri_hat, inv_std = norm_rows(cell_row(products, row, rows))
+        tri_hat, inv_std = norm_rows(cell_row(panel, row, rows))
         d_hat = d_hat_centered[row]
         cross = jnp.mean(d_hat * tri_hat, axis=0, keepdims=True)
         d_tri = inv_std * (d_hat - tri_hat * cross)
-        d_products[:, row * block : (row + 1) * block, :] = d_tri.reshape(
+        d_panel[:, row * block : (row + 1) * block, :] = d_tri.reshape(
             count, block, width
         ).astype(BF16)
-
-
-def d_right_kernel(d_products, left_all, d_right_panel, d_tri_all, left_wide, right_wide):
+    for place, piece in zip(partners(count, False), pieces):
+        piece[...] = d_panel[place]
+
+
+def d_right_kernel(left_all, *refs):
+    *d_products, d_right_panel, d_tri_all, left_wide, right_wide = refs
     block, left_rows, _ = left_all.shape
     right_rows = right_wide.shape[0] // block
-    spread(d_products, left_wide)
+    spread(d_products, left_wide, False)
     for h in range(block):
         d_tri = left_wide[pl.ds(h, left_rows, stride=block), :].astype(BF16)
         d_tri_all[h] = d_tri
         right_wide[pl.ds(h, right_rows, stride=block), :] = dot(d_tri, left_all[h], 0, 0)
-    for rank, place in wide_places(d_right_panel, d_products.shape[0], True):
+    for rank, place in wide_places(d_right_panel, len(d_products), True):
         d_right_panel[rank] = right_wide[place, :].astype(BF16)
 
 
@@ -236,18 +257,17 @@
     block, left_rows, _ = d_tri_all.shape
     for h in range(block):
         left_wide[pl.ds(h, left_rows, stride=block), :] = dot(d_tri_all[h], right_all[h], 1, 0)
-    depth = pieces[0].shape[0]
-    for step, piece in enumerate(pieces):
-        start = pl.multiple_of(partner(step, len(pieces)) * depth, depth)
-        piece[...] = left_wide[pl.ds(start, depth), :].astype(BF16)
-
-
-def gate_back_kernel(products, gate_slope, out_gain, out_bias, w_out, d_gate_pre):
+    hand_out(left_wide, pieces, True)
+
+
+def gate_back_kernel(gate_slope, out_gain, out_bias, w_out, *refs):
+    *products, d_gate_pre, panel = refs
     rows = gate_slope.shape[0]
+    gather(products, panel, False)
     out_flip = transposed(w_out[...])
     out_gain_col, out_bias_col = column(out_gain[...]), column(out_bias[...])
     for row in range(rows):
-        tri_hat, _ = norm_rows(cell_row(products, row, rows))
+        tri_hat, _ = norm_rows(cell_row(panel, row, rows))
         scaled = (tri_hat * out_gain_col + out_bias_col).astype(BF16)
         d_gate_pre[row] = (dot(out_flip, scaled, 1, 0) * gate_slope[row]).astype(BF16)
 
@@ -280,8 +300,7 @@
 
 def sort_d_left_kernel(*refs):
     *pieces, d_left_panel = refs
-    for step, piece in enumerate(pieces):
-        d_left_panel[partner(step, len(pieces))] = piece[...]
+    gather(pieces, d_left_panel, True)
 
 
 def both_halves(blocks, count):
@@ -321,20 +340,12 @@
     )
 
 
-def swap_half(values, count):
+def swap_pieces(pieces, beside):
     devices = range(lax.axis_size("row"))
-    groups = [[d for d in devices if d // count == half] for half in range(len(devices) // count)]
-    return lax.all_to_all(
-        values, "row", split_axis=0, concat_axis=0, tiled=True, axis_index_groups=groups
-    )
-
-
-def swap_pieces(pieces):
-    devices = range(lax.axis_size("row"))
-    count = len(pieces)
+    apart = distances(len(pieces), beside)
     return [pieces[0]] + [
-        lax.ppermute(pieces[step], "row", [(d, d ^ distance(step, count)) for d in devices])
-        for step in range(1, count)
+        lax.ppermute(pieces[step], "row", [(d, d ^ apart[step]) for d in devices])
+        for step in range(1, len(pieces))
     ]
 
 
@@ -388,7 +399,7 @@
         scratch=[left_panel],
         flops=2 * cells * channels * 2 * hidden,
     )
-    pieces = swap_pieces(pieces)
+    pieces = swap_pieces(pieces, True)
     (left_all,) = call(
         sort_left_kernel,
         "sort_left",
@@ -404,29 +415,30 @@
         fetched=range(7),
         flops=2 * cells * channels * 2 * hidden,
     )
-    products, right_all = call(
+    right_all, *products = call(
         tri_kernel,
         "tri",
-        [panel, shape((block, right_rows, width), BF16)],
+        [shape((block, right_rows, width), BF16)] + [piece] * count,
         [right_panel, left_all, d_hat_centered],
         unread=(2,),
         scratch=[left_wide, right_wide],
         flops=2 * block * left_rows * width * right_rows,
     )
-    products = swap_half(products, count)
-    (d_products,) = call(
+    products = swap_pieces(products, False)
+    d_products = call(
         middle_kernel,
         "middle",
-        [panel],
-        [products, d_hat_centered],
+        [piece] * count,
+        [d_hat_centered, *products],
+        scratch=[left_panel, left_panel],
         flops=20 * cells * hidden,
     )
-    d_products = swap_half(d_products, count)
+    d_products = swap_pieces(d_products, False)
     d_right_panel, d_tri_all = call(
         d_right_kernel,
         "d_right",
         [wide_panel, shape((block, left_rows, width), BF16)],
-        [d_products, left_all],
+        [left_all, *d_products],
         scratch=[left_wide, right_wide],
         flops=2 * block * left_rows * width * right_rows,
     )
@@ -439,14 +451,15 @@
         scratch=[left_wide],
         flops=2 * block * left_rows * width * right_rows,
     )
-    d_pieces = swap_pieces(d_pieces)
+    d_pieces = swap_pieces(d_pieces, True)
     (d_left_panel,) = call(sort_d_left_kernel, "sort_d_left", [panel], d_pieces)
     (d_gate_pre,) = call(
         gate_back_kernel,
         "gate_back",
         [shape((rows, channels, width), BF16)],
-        [products, gate_slope, out_gain, out_bias, w_out],
-        fetched=range(2, 5),
+        [gate_slope, out_gain, out_bias, w_out, *products],
+        fetched=range(1, 4),
+        scratch=[left_panel],
         flops=2 * cells * channels * hidden,
     )
     slopes, normed_in, inv_in, gain_col, weights = call(

time: 62.7 us -> 63.7 us (1.016)
  blocking collectives: 17.3 us -> 0 us
  starting transfers between devices: 24.7 us -> 37.3 us
  waiting for transfers between devices: 8.85 us -> 14.5 us
    all_to_all x2 -> x0, blocking collectives: 17.3 us -> none  [swap_half(): lax.all_to_all(values, 'row', split_axis=0, concat_axis=0, tiled=True, ax...]
    ppermute x14 -> x28, starting transfers between devices: 11.3 us -> 23.9 us  [swap_pieces(): lax.ppermute(pieces[step], 'row', [(d, d ^ apart[step]) for d in devices])]
    ppermute x14 -> x28, waiting for transfers between devices: 8.39 us -> 14 us  [swap_pieces(): lax.ppermute(pieces[step], 'row', [(d, d ^ apart[step]) for d in devices])]
  transfers between devices with their start and end apart: 16 -> 30, of which waited for: 10 -> 18; matrix products, arithmetic and copies ran while one was open for 0% -> 0% of each run, Pallas kernels for 6% -> 6%
where the time goes in v17:
time: 63.7 us; the launch traced here: 63.3 us
  starting transfers between devices  37.3 us (59%)
  waiting for transfers between devices  14.5 us (23%)
  Pallas kernels  9.93 us (16%)
  local copies, waits for them, and re-layouts  1.34 us (2%)
    ppermute x28, starting transfers between devices, swap_pieces(): lax.ppermute(pieces[step], 'row', [(d, d ^ apart[step]) for d in devices])  23.9 us
    ppermute x28, waiting for transfers between devices, swap_pieces(): lax.ppermute(pieces[step], 'row', [(d, d ^ apart[step]) for d in devices])  14 us
    all_to_all x2, starting transfers between devices, swap(): lax.all_to_all(values, 'row', split_axis=0, concat_axis=0, tiled=True, ax...  13.4 us
    pallas_call x12, Pallas kernels, call(): pl.pallas_call(body, name=name, out_shape=outs, in_specs=[pl.BlockSpec(me...  9.93 us
    unnamed x22, local copies, waits for them, and re-layouts  1.34 us
  transfers between devices with their start and end apart: 30, of which 18 were waited for; matrix products, arithmetic and copies ran while one was open for 0% of the time, Pallas kernels for 6%

profile of v17, /device:TPU:0, one launch (start us, length us, event | category | flops | bytes accessed | tf_op | source)
XLA Modules:
  0.0 63.3 jit_solution(3311534461889335468)
XLA Ops:
  0.0 2.4 %project_right.1.refs_5_ = bf16[16,128,128]{2,1,0:T(8,128)(2,1)} custom-call(bf16[8,128,128]{2,1,0:T(8,128)(2,1)} %refs_0_.7, s32[1,128]{1,0:T(1,128)} %bitcast.13, f32[1,128]{1,0:T(1,128)} %bitcast.5, f32[1,128]{1,0:T(1,128)} %bitcast.9, bf16[128,512]{1,0:T(8,128)(2,1)} %refs_4_.7), custom_call_target="tpu_custom_call" | custom-call | flops 67108864 | bytes 919040 | tf_op jit(solution)/shard_map/project_right/pallas_call | solution.py:65
  2.5 8.5 %all-to-all-start = ((bf16[16,128,128]{2,1,0:T(8,128)(2,1)}), bf16[16,128,128]{2,1,0:T(8,128)(2,1)S(1)}, u32[]{:S(2)}, u32[]{:S(2)}) async-start(bf16[16,128,128]{2,1,0:T(8,128)(2,1)} %project_right.1.refs_5_), calls=%async_computation | async-start | bytes 1048576 | tf_op jit(solution)/shard_map/all_to_all | solution.py:338
  12.7 1.4 %collective-permute-start.2 = (bf16[128,128]{1,0:T(8,128)(2,1)S(1)}, bf16[128,128]{1,0:T(8,128)(2,1)S(1)}, u32[]{:S(2)}, u32[]{:S(2)}) collective-permute-start(bf16[128,128]{1,0:T(8,128)(2,1)S(1)} %get-tuple-element.50), channel_id=1, source_target_pairs={{0,6},{1,7},{2,4},{3,5},{4,2},{5,3},{6,0},{7,1},{8,14},{9,15},{10,... | collective-permute-start | bytes 98312 | tf_op jit(solution)/shard_map/ppermute | solution.py:347
  15.6 1.5 %collective-permute-start.5 = (bf16[128,128]{1,0:T(8,128)(2,1)S(1)}, bf16[128,128]{1,0:T(8,128)(2,1)S(1)}, u32[]{:S(2)}, u32[]{:S(2)}) collective-permute-start(bf16[128,128]{1,0:T(8,128)(2,1)S(1)} %get-tuple-element.53), channel_id=1, source_target_pairs={{0,5},{1,4},{2,7},{3,6},{4,1},{5,0},{6,3},{7,2},{8,13},{9,12},{10,... | collective-permute-start | bytes 98312 | tf_op jit(solution)/shard_map/ppermute | solution.py:347
  17.1 1.3 %collective-permute-done.1.refs_2_ = bf16[128,128]{1,0:T(8,128)(2,1)S(1)} collective-permute-done((bf16[128,128]{1,0:T(8,128)(2,1)S(1)}, bf16[128,128]{1,0:T(8,128)(2,1)S(1)}, u32[]{:S(2)}, u32[]{:S(2)}) %collective-permute-start.1) | collective-permute-done | bytes 32800 | tf_op jit(solution)/shard_map/ppermute | solution.py:347
  19.9 1.5 %collective-permute-done.2.refs_3_ = bf16[128,128]{1,0:T(8,128)(2,1)S(1)} collective-permute-done((bf16[128,128]{1,0:T(8,128)(2,1)S(1)}, bf16[128,128]{1,0:T(8,128)(2,1)S(1)}, u32[]{:S(2)}, u32[]{:S(2)}) %collective-permute-start.2) | collective-permute-done | bytes 32800 | tf_op jit(solution)/shard_map/ppermute | solution.py:347
  22.1 1.5 %collective-permute-done.4.refs_5_ = bf16[128,128]{1,0:T(8,128)(2,1)S(1)} collective-permute-done((bf16[128,128]{1,0:T(8,128)(2,1)S(1)}, bf16[128,128]{1,0:T(8,128)(2,1)S(1)}, u32[]{:S(2)}, u32[]{:S(2)}) %collective-permute-start.4) | collective-permute-done | bytes 32800 | tf_op jit(solution)/shard_map/ppermute | solution.py:347
  24.5 1.7 %collective-permute-start.7 = (bf16[128,128]{1,0:T(8,128)(2,1)S(1)}, bf16[128,128]{1,0:T(8,128)(2,1)S(1)}, u32[]{:S(2)}, u32[]{:S(2)}) collective-permute-start(bf16[128,128]{1,0:T(8,128)(2,1)S(1)} %get-tuple-element.57), channel_id=1, source_target_pairs={{0,6},{1,7},{2,4},{3,5},{4,2},{5,3},{6,0},{7,1},{8,14},{9,15},{10,... | collective-permute-start | bytes 98312 | tf_op jit(solution)/shard_map/ppermute | solution.py:347
  26.9 1.5 %collective-permute-start.9 = (bf16[128,128]{1,0:T(8,128)(2,1)S(1)}, bf16[128,128]{1,0:T(8,128)(2,1)S(1)}, u32[]{:S(2)}, u32[]{:S(2)}) collective-permute-start(bf16[128,128]{1,0:T(8,128)(2,1)S(1)} %get-tuple-element.59), channel_id=1, source_target_pairs={{0,4},{1,5},{2,6},{3,7},{4,0},{5,1},{6,2},{7,3},{8,12},{9,13},{10,... | collective-permute-start | bytes 98312 | tf_op jit(solution)/shard_map/ppermute | solution.py:347
  29.4 1.1 %collective-permute-start.12 = (bf16[128,128]{1,0:T(8,128)(2,1)S(1)}, bf16[128,128]{1,0:T(8,128)(2,1)S(1)}, u32[]{:S(2)}, u32[]{:S(2)}) collective-permute-start(bf16[128,128]{1,0:T(8,128)(2,1)S(1)} %get-tuple-element.62), channel_id=1, source_target_pairs={{0,3},{1,2},{2,1},{3,0},{4,7},{5,6},{6,5},{7,4},{8,11},{9,10},{10,... | collective-permute-start | bytes 98312 | tf_op jit(solution)/shard_map/ppermute | solution.py:347
  31.8 1.2 %collective-permute-done.11.refs_6_.refs_9_ = bf16[128,128]{1,0:T(8,128)(2,1)S(1)} collective-permute-done((bf16[128,128]{1,0:T(8,128)(2,1)S(1)}, bf16[128,128]{1,0:T(8,128)(2,1)S(1)}, u32[]{:S(2)}, u32[]{:S(2)}) %collective-permute-start.11) | collective-permute-done | bytes 32800 | tf_op jit(solution)/shard_map/ppermute | solution.py:347
  33.4 2.5 %collective-permute-start.14 = (bf16[128,128]{1,0:T(8,128)(2,1)S(1)}, bf16[128,128]{1,0:T(8,128)(2,1)S(1)}, u32[]{:S(2)}, u32[]{:S(2)}) collective-permute-start(bf16[128,128]{1,0:T(8,128)(2,1)S(1)} %get-tuple-element.65), channel_id=1, source_target_pairs={{0,6},{1,7},{2,4},{3,5},{4,2},{5,3},{6,0},{7,1},{8,14},{9,15},{10,... | collective-permute-start | bytes 98312 | tf_op jit(solution)/shard_map/ppermute | solution.py:347
  35.9 1.6 %collective-permute-start.16 = (bf16[128,128]{1,0:T(8,128)(2,1)S(1)}, bf16[128,128]{1,0:T(8,128)(2,1)S(1)}, u32[]{:S(2)}, u32[]{:S(2)}) collective-permute-start(bf16[128,128]{1,0:T(8,128)(2,1)S(1)} %get-tuple-element.67), channel_id=1, source_target_pairs={{0,4},{1,5},{2,6},{3,7},{4,0},{5,1},{6,2},{7,3},{8,12},{9,13},{10,... | collective-permute-start | bytes 98312 | tf_op jit(solution)/shard_map/ppermute | solution.py:347
  37.9 1.5 %collective-permute-start.18 = (bf16[128,128]{1,0:T(8,128)(2,1)S(1)}, bf16[128,128]{1,0:T(8,128)(2,1)S(1)}, u32[]{:S(2)}, u32[]{:S(2)}) collective-permute-start(bf16[128,128]{1,0:T(8,128)(2,1)S(1)} %get-tuple-element.69), channel_id=1, source_target_pairs={{0,2},{1,3},{2,0},{3,1},{4,6},{5,7},{6,4},{7,5},{8,10},{9,11},{10,... | collective-permute-start | bytes 98312 | tf_op jit(solution)/shard_map/ppermute | solution.py:347
  39.4 1.1 %collective-permute-done.15.refs_3_ = bf16[128,128]{1,0:T(8,128)(2,1)S(1)} collective-permute-done((bf16[128,128]{1,0:T(8,128)(2,1)S(1)}, bf16[128,128]{1,0:T(8,128)(2,1)S(1)}, u32[]{:S(2)}, u32[]{:S(2)}) %collective-permute-start.15) | collective-permute-done | bytes 32800 | tf_op jit(solution)/shard_map/ppermute | solution.py:347
  41.8 1.2 %collective-permute-done.19.refs_7_ = bf16[128,128]{1,0:T(8,128)(2,1)S(1)} collective-permute-done((bf16[128,128]{1,0:T(8,128)(2,1)S(1)}, bf16[128,128]{1,0:T(8,128)(2,1)S(1)}, u32[]{:S(2)}, u32[]{:S(2)}) %collective-permute-start.19) | collective-permute-done | bytes 32800 | tf_op jit(solution)/shard_map/ppermute | solution.py:347
  43.0 1.5 %d_right.1 = (bf16[16,128,128]{2,1,0:T(8,128)(2,1)}, bf16[16,64,128]{2,1,0:T(8,128)(2,1)S(1)}) custom-call(bf16[16,64,128]{2,1,0:T(8,128)(2,1)S(1)} %sort_left.1.refs_1_.refs_0_, bf16[128,128]{1,0:T(8,128)(2,1)S(1)} %get-tuple-element.64.refs_1_, bf16[128,128]{1,0:T(8,128)(2,1)S(1)} %collective-permute-done.14.refs_2_, ...), custom_call_target="tpu_custom_call" | custom-call | flops 33554432 | bytes 1310720 | tf_op jit(solution)/shard_map/d_right/pallas_call | solution.py:65
  44.6 4.9 %all-to-all-start.1 = ((bf16[16,128,128]{2,1,0:T(8,128)(2,1)}), bf16[16,128,128]{2,1,0:T(8,128)(2,1)S(1)}, u32[]{:S(2)}, u32[]{:S(2)}) async-start(bf16[16,128,128]{2,1,0:T(8,128)(2,1)} %get-tuple-element.72), calls=%async_computation.1 | async-start | bytes 1048576 | tf_op jit(solution)/shard_map/all_to_all | solution.py:338
  50.0 1.5 %collective-permute-start.22 = (bf16[128,128]{1,0:T(8,128)(2,1)S(1)}, bf16[128,128]{1,0:T(8,128)(2,1)S(1)}, u32[]{:S(2)}, u32[]{:S(2)}) collective-permute-start(bf16[128,128]{1,0:T(8,128)(2,1)S(1)} %get-tuple-element.77), channel_id=1, source_target_pairs={{0,2},{1,3},{2,0},{3,1},{4,6},{5,7},{6,4},{7,5},{8,10},{9,11},{10,... | collective-permute-start | bytes 98312 | tf_op jit(solution)/shard_map/ppermute | solution.py:347
  51.8 2.0 %collective-permute-start.24 = (bf16[128,128]{1,0:T(8,128)(2,1)S(1)}, bf16[128,128]{1,0:T(8,128)(2,1)S(1)}, u32[]{:S(2)}, u32[]{:S(2)}) collective-permute-start(bf16[128,128]{1,0:T(8,128)(2,1)S(1)} %get-tuple-element.79), channel_id=1, source_target_pairs={{0,7},{1,6},{2,5},{3,4},{4,3},{5,2},{6,1},{7,0},{8,15},{9,14},{10,... | collective-permute-start | bytes 98312 | tf_op jit(solution)/shard_map/ppermute | solution.py:347
  54.4 1.6 %collective-permute-start.26 = (bf16[128,128]{1,0:T(8,128)(2,1)S(1)}, bf16[128,128]{1,0:T(8,128)(2,1)S(1)}, u32[]{:S(2)}, u32[]{:S(2)}) collective-permute-start(bf16[128,128]{1,0:T(8,128)(2,1)S(1)} %get-tuple-element.81), channel_id=1, source_target_pairs={{0,5},{1,4},{2,7},{3,6},{4,1},{5,0},{6,3},{7,2},{8,13},{9,12},{10,... | collective-permute-start | bytes 98312 | tf_op jit(solution)/shard_map/ppermute | solution.py:347
  55.9 1.2 %collective-permute-done.22.refs_2_ = bf16[128,128]{1,0:T(8,128)(2,1)S(1)} collective-permute-done((bf16[128,128]{1,0:T(8,128)(2,1)S(1)}, bf16[128,128]{1,0:T(8,128)(2,1)S(1)}, u32[]{:S(2)}, u32[]{:S(2)}) %collective-permute-start.22) | collective-permute-done | bytes 32800 | tf_op jit(solution)/shard_map/ppermute | solution.py:347
  58.2 1.0 %slopes.1 = (bf16[8,512,128]{2,1,0:T(8,128)(2,1)S(1)}, bf16[8,128,128]{2,1,0:T(8,128)(2,1)S(1)}, f32[8,128]{1,0:T(8,128)S(1)}, f32[128,128]{1,0:T(8,128)S(1)}, bf16[128,640]{1,0:T(8,128)(2,1)S(1)}) custom-call(bf16[8,128,128]{2,1,0:T(8,128)(2,1)S(1)} %copy-done.1, s32[1,128]{1,0:T(1,128)S(1)} %bitcast.15, f32[1,128]{1,0:T(1,128)S(1)} %bitcast.8, ...), custom_call_target="tpu_custom_call" | custom-call | flops 134217728 | bytes 2233856 | tf_op jit(solution)/shard_map/slopes/pallas_call | solution.py:65
  61.9 1.4 %finish.1 = bf16[8,128,128]{2,1,0:T(8,128)(2,1)} custom-call(bf16[16,128,128]{2,1,0:T(8,128)(2,1)S(1)} %all-to-all-done.1.refs_0_, bf16[8,128,128]{2,1,0:T(8,128)(2,1)S(1)} %sort_d_left.1.refs_1_, bf16[8,512,128]{2,1,0:T(8,128)(2,1)S(1)} %get-tuple-element.84.refs_2_, bf16[8,128,128]{2,1,0:T(8,128)(2,1)S(1)} %gate_back.1.refs_6_.refs_3_, ...), custom_call_target="tpu_custom_call" | custom-call | flops 134217728 | bytes 2854912 | tf_op jit(solution)/shard_map/finish/pallas_call | solution.py:65
  (70 shorter events, 16.4 us)
Async XLA Ops:
  2.5 21.3 %all-to-all-start = ((bf16[16,128,128]{2,1,0:T(8,128)(2,1)}), bf16[16,128,128]{2,1,0:T(8,128)(2,1)S(1)}, u32[]{:S(2)}, u32[]{:S(2)}) async-start(bf16[16,128,128]{2,1,0:T(8,128)(2,1)} %project_right.1.refs_5_), calls=%async_computation | async-start | bytes 1048576 | tf_op jit(solution)/shard_map/all_to_all | solution.py:338
  11.9 3.7 %collective-permute-start = (bf16[128,128]{1,0:T(8,128)(2,1)S(1)}, bf16[128,128]{1,0:T(8,128)(2,1)S(1)}, u32[]{:S(2)}, u32[]{:S(2)}) collective-permute-start(bf16[128,128]{1,0:T(8,128)(2,1)S(1)} %get-tuple-element.48), channel_id=1, source_target_pairs={{0,1},{1,0},{2,3},{3,2},{4,5},{5,4},{6,7},{7,6},{8,9},{9,8},{10,11... | collective-permute-start | bytes 98312 | tf_op jit(solution)/shard_map/ppermute | solution.py:347
  12.1 6.3 %collective-permute-start.1 = (bf16[128,128]{1,0:T(8,128)(2,1)S(1)}, bf16[128,128]{1,0:T(8,128)(2,1)S(1)}, u32[]{:S(2)}, u32[]{:S(2)}) collective-permute-start(bf16[128,128]{1,0:T(8,128)(2,1)S(1)} %get-tuple-element.49), channel_id=1, source_target_pairs={{0,2},{1,3},{2,0},{3,1},{4,6},{5,7},{6,4},{7,5},{8,10},{9,11},{10,... | collective-permute-start | bytes 98312 | tf_op jit(solution)/shard_map/ppermute | solution.py:347
  12.7 8.6 %collective-permute-start.2 = (bf16[128,128]{1,0:T(8,128)(2,1)S(1)}, bf16[128,128]{1,0:T(8,128)(2,1)S(1)}, u32[]{:S(2)}, u32[]{:S(2)}) collective-permute-start(bf16[128,128]{1,0:T(8,128)(2,1)S(1)} %get-tuple-element.50), channel_id=1, source_target_pairs={{0,6},{1,7},{2,4},{3,5},{4,2},{5,3},{6,0},{7,1},{8,14},{9,15},{10,... | collective-permute-start | bytes 98312 | tf_op jit(solution)/shard_map/ppermute | solution.py:347
  14.1 8.0 %collective-permute-start.3 = (bf16[128,128]{1,0:T(8,128)(2,1)S(1)}, bf16[128,128]{1,0:T(8,128)(2,1)S(1)}, u32[]{:S(2)}, u32[]{:S(2)}) collective-permute-start(bf16[128,128]{1,0:T(8,128)(2,1)S(1)} %get-tuple-element.51), channel_id=1, source_target_pairs={{0,7},{1,6},{2,5},{3,4},{4,3},{5,2},{6,1},{7,0},{8,15},{9,14},{10,... | collective-permute-start | bytes 98312 | tf_op jit(solution)/shard_map/ppermute | solution.py:347
  15.0 8.6 %collective-permute-start.4 = (bf16[128,128]{1,0:T(8,128)(2,1)S(1)}, bf16[128,128]{1,0:T(8,128)(2,1)S(1)}, u32[]{:S(2)}, u32[]{:S(2)}) collective-permute-start(bf16[128,128]{1,0:T(8,128)(2,1)S(1)} %get-tuple-element.52), channel_id=1, source_target_pairs={{0,4},{1,5},{2,6},{3,7},{4,0},{5,1},{6,2},{7,3},{8,12},{9,13},{10,... | collective-permute-start | bytes 98312 | tf_op jit(solution)/shard_map/ppermute | solution.py:347
  15.6 8.0 %collective-permute-start.5 = (bf16[128,128]{1,0:T(8,128)(2,1)S(1)}, bf16[128,128]{1,0:T(8,128)(2,1)S(1)}, u32[]{:S(2)}, u32[]{:S(2)}) collective-permute-start(bf16[128,128]{1,0:T(8,128)(2,1)S(1)} %get-tuple-element.53), channel_id=1, source_target_pairs={{0,5},{1,4},{2,7},{3,6},{4,1},{5,0},{6,3},{7,2},{8,13},{9,12},{10,... | collective-permute-start | bytes 98312 | tf_op jit(solution)/shard_map/ppermute | solution.py:347
  18.4 5.2 %collective-permute-start.6 = (bf16[128,128]{1,0:T(8,128)(2,1)S(1)}, bf16[128,128]{1,0:T(8,128)(2,1)S(1)}, u32[]{:S(2)}, u32[]{:S(2)}) collective-permute-start(bf16[128,128]{1,0:T(8,128)(2,1)S(1)} %get-tuple-element.54), channel_id=1, source_target_pairs={{0,3},{1,2},{2,1},{3,0},{4,7},{5,6},{6,5},{7,4},{8,11},{9,10},{10,... | collective-permute-start | bytes 98312 | tf_op jit(solution)/shard_map/ppermute | solution.py:347
  24.5 4.9 %collective-permute-start.7 = (bf16[128,128]{1,0:T(8,128)(2,1)S(1)}, bf16[128,128]{1,0:T(8,128)(2,1)S(1)}, u32[]{:S(2)}, u32[]{:S(2)}) collective-permute-start(bf16[128,128]{1,0:T(8,128)(2,1)S(1)} %get-tuple-element.57), channel_id=1, source_target_pairs={{0,6},{1,7},{2,4},{3,5},{4,2},{5,3},{6,0},{7,1},{8,14},{9,15},{10,... | collective-permute-start | bytes 98312 | tf_op jit(solution)/shard_map/ppermute | solution.py:347
  26.1 4.5 %collective-permute-start.8 = (bf16[128,128]{1,0:T(8,128)(2,1)S(1)}, bf16[128,128]{1,0:T(8,128)(2,1)S(1)}, u32[]{:S(2)}, u32[]{:S(2)}) collective-permute-start(bf16[128,128]{1,0:T(8,128)(2,1)S(1)} %get-tuple-element.58), channel_id=1, source_target_pairs={{0,7},{1,6},{2,5},{3,4},{4,3},{5,2},{6,1},{7,0},{8,15},{9,14},{10,... | collective-permute-start | bytes 98312 | tf_op jit(solution)/shard_map/ppermute | solution.py:347
  26.9 4.4 %collective-permute-start.9 = (bf16[128,128]{1,0:T(8,128)(2,1)S(1)}, bf16[128,128]{1,0:T(8,128)(2,1)S(1)}, u32[]{:S(2)}, u32[]{:S(2)}) collective-permute-start(bf16[128,128]{1,0:T(8,128)(2,1)S(1)} %get-tuple-element.59), channel_id=1, source_target_pairs={{0,4},{1,5},{2,6},{3,7},{4,0},{5,1},{6,2},{7,3},{8,12},{9,13},{10,... | collective-permute-start | bytes 98312 | tf_op jit(solution)/shard_map/ppermute | solution.py:347
  28.9 4.1 %collective-permute-start.11 = (bf16[128,128]{1,0:T(8,128)(2,1)S(1)}, bf16[128,128]{1,0:T(8,128)(2,1)S(1)}, u32[]{:S(2)}, u32[]{:S(2)}) collective-permute-start(bf16[128,128]{1,0:T(8,128)(2,1)S(1)} %get-tuple-element.61), channel_id=1, source_target_pairs={{0,2},{1,3},{2,0},{3,1},{4,6},{5,7},{6,4},{7,5},{8,10},{9,11},{10,... | collective-permute-start | bytes 98312 | tf_op jit(solution)/shard_map/ppermute | solution.py:347
  33.4 6.0 %collective-permute-start.14 = (bf16[128,128]{1,0:T(8,128)(2,1)S(1)}, bf16[128,128]{1,0:T(8,128)(2,1)S(1)}, u32[]{:S(2)}, u32[]{:S(2)}) collective-permute-start(bf16[128,128]{1,0:T(8,128)(2,1)S(1)} %get-tuple-element.65), channel_id=1, source_target_pairs={{0,6},{1,7},{2,4},{3,5},{4,2},{5,3},{6,0},{7,1},{8,14},{9,15},{10,... | collective-permute-start | bytes 98312 | tf_op jit(solution)/shard_map/ppermute | solution.py:347
  35.9 4.6 %collective-permute-start.15 = (bf16[128,128]{1,0:T(8,128)(2,1)S(1)}, bf16[128,128]{1,0:T(8,128)(2,1)S(1)}, u32[]{:S(2)}, u32[]{:S(2)}) collective-permute-start(bf16[128,128]{1,0:T(8,128)(2,1)S(1)} %get-tuple-element.66), channel_id=1, source_target_pairs={{0,7},{1,6},{2,5},{3,4},{4,3},{5,2},{6,1},{7,0},{8,15},{9,14},{10,... | collective-permute-start | bytes 98312 | tf_op jit(solution)/shard_map/ppermute | solution.py:347
  35.9 4.7 %collective-permute-start.16 = (bf16[128,128]{1,0:T(8,128)(2,1)S(1)}, bf16[128,128]{1,0:T(8,128)(2,1)S(1)}, u32[]{:S(2)}, u32[]{:S(2)}) collective-permute-start(bf16[128,128]{1,0:T(8,128)(2,1)S(1)} %get-tuple-element.67), channel_id=1, source_target_pairs={{0,4},{1,5},{2,6},{3,7},{4,0},{5,1},{6,2},{7,3},{8,12},{9,13},{10,... | collective-permute-start | bytes 98312 | tf_op jit(solution)/shard_map/ppermute | solution.py:347
  37.9 3.9 %collective-permute-start.18 = (bf16[128,128]{1,0:T(8,128)(2,1)S(1)}, bf16[128,128]{1,0:T(8,128)(2,1)S(1)}, u32[]{:S(2)}, u32[]{:S(2)}) collective-permute-start(bf16[128,128]{1,0:T(8,128)(2,1)S(1)} %get-tuple-element.69), channel_id=1, source_target_pairs={{0,2},{1,3},{2,0},{3,1},{4,6},{5,7},{6,4},{7,5},{8,10},{9,11},{10,... | collective-permute-start | bytes 98312 | tf_op jit(solution)/shard_map/ppermute | solution.py:347
  44.6 17.4 %all-to-all-start.1 = ((bf16[16,128,128]{2,1,0:T(8,128)(2,1)}), bf16[16,128,128]{2,1,0:T(8,128)(2,1)S(1)}, u32[]{:S(2)}, u32[]{:S(2)}) async-start(bf16[16,128,128]{2,1,0:T(8,128)(2,1)} %get-tuple-element.72), calls=%async_computation.1 | async-start | bytes 1048576 | tf_op jit(solution)/shard_map/all_to_all | solution.py:338
  49.8 4.5 %collective-permute-start.21 = (bf16[128,128]{1,0:T(8,128)(2,1)S(1)}, bf16[128,128]{1,0:T(8,128)(2,1)S(1)}, u32[]{:S(2)}, u32[]{:S(2)}) collective-permute-start(bf16[128,128]{1,0:T(8,128)(2,1)S(1)} %get-tuple-element.76), channel_id=1, source_target_pairs={{0,1},{1,0},{2,3},{3,2},{4,5},{5,4},{6,7},{7,6},{8,9},{9,8},{10,11... | collective-permute-start | bytes 98312 | tf_op jit(solution)/shard_map/ppermute | solution.py:347
  50.0 7.1 %collective-permute-start.22 = (bf16[128,128]{1,0:T(8,128)(2,1)S(1)}, bf16[128,128]{1,0:T(8,128)(2,1)S(1)}, u32[]{:S(2)}, u32[]{:S(2)}) collective-permute-start(bf16[128,128]{1,0:T(8,128)(2,1)S(1)} %get-tuple-element.77), channel_id=1, source_target_pairs={{0,2},{1,3},{2,0},{3,1},{4,6},{5,7},{6,4},{7,5},{8,10},{9,11},{10,... | collective-permute-start | bytes 98312 | tf_op jit(solution)/shard_map/ppermute | solution.py:347
  51.5 8.3 %collective-permute-start.23 = (bf16[128,128]{1,0:T(8,128)(2,1)S(1)}, bf16[128,128]{1,0:T(8,128)(2,1)S(1)}, u32[]{:S(2)}, u32[]{:S(2)}) collective-permute-start(bf16[128,128]{1,0:T(8,128)(2,1)S(1)} %get-tuple-element.78), channel_id=1, source_target_pairs={{0,6},{1,7},{2,4},{3,5},{4,2},{5,3},{6,0},{7,1},{8,14},{9,15},{10,... | collective-permute-start | bytes 98312 | tf_op jit(solution)/shard_map/ppermute | solution.py:347
  51.8 8.7 %collective-permute-start.24 = (bf16[128,128]{1,0:T(8,128)(2,1)S(1)}, bf16[128,128]{1,0:T(8,128)(2,1)S(1)}, u32[]{:S(2)}, u32[]{:S(2)}) collective-permute-start(bf16[128,128]{1,0:T(8,128)(2,1)S(1)} %get-tuple-element.79), channel_id=1, source_target_pairs={{0,7},{1,6},{2,5},{3,4},{4,3},{5,2},{6,1},{7,0},{8,15},{9,14},{10,... | collective-permute-start | bytes 98312 | tf_op jit(solution)/shard_map/ppermute | solution.py:347
  53.9 7.2 %collective-permute-start.25 = (bf16[128,128]{1,0:T(8,128)(2,1)S(1)}, bf16[128,128]{1,0:T(8,128)(2,1)S(1)}, u32[]{:S(2)}, u32[]{:S(2)}) collective-permute-start(bf16[128,128]{1,0:T(8,128)(2,1)S(1)} %get-tuple-element.80), channel_id=1, source_target_pairs={{0,4},{1,5},{2,6},{3,7},{4,0},{5,1},{6,2},{7,3},{8,12},{9,13},{10,... | collective-permute-start | bytes 98312 | tf_op jit(solution)/shard_map/ppermute | solution.py:347
  54.4 7.1 %collective-permute-start.26 = (bf16[128,128]{1,0:T(8,128)(2,1)S(1)}, bf16[128,128]{1,0:T(8,128)(2,1)S(1)}, u32[]{:S(2)}, u32[]{:S(2)}) collective-permute-start(bf16[128,128]{1,0:T(8,128)(2,1)S(1)} %get-tuple-element.81), channel_id=1, source_target_pairs={{0,5},{1,4},{2,7},{3,6},{4,1},{5,0},{6,3},{7,2},{8,13},{9,12},{10,... | collective-permute-start | bytes 98312 | tf_op jit(solution)/shard_map/ppermute | solution.py:347
  57.1 4.3 %collective-permute-start.27 = (bf16[128,128]{1,0:T(8,128)(2,1)S(1)}, bf16[128,128]{1,0:T(8,128)(2,1)S(1)}, u32[]{:S(2)}, u32[]{:S(2)}) collective-permute-start(bf16[128,128]{1,0:T(8,128)(2,1)S(1)} %get-tuple-element.82), channel_id=1, source_target_pairs={{0,3},{1,2},{2,1},{3,0},{4,7},{5,6},{6,5},{7,4},{8,11},{9,10},{10,... | collective-permute-start | bytes 98312 | tf_op jit(solution)/shard_map/ppermute | solution.py:347
  (17 other events, 93.9 us)

commit v18 on v16

--- a/solution.py
+++ b/solution.py
@@ -23,7 +23,7 @@
 
 
 def sigmoid(values):
-    return 1.0 / (1.0 + jnp.exp(-values))
+    return 0.5 + 0.5 * jnp.tanh(0.5 * values)
 
 
 def column(row):
@@ -39,7 +39,7 @@
 
 
 def call(
-    kernel, name, outs, args, fetched=(), unread=(), scratch=(), flops=0, limit=VMEM_LIMIT
+    kernel, name, outs, args, fetched=(), columns={}, unread=(), scratch=(), flops=0, limit=VMEM_LIMIT
 ):
     moved = sum(a.size * a.dtype.itemsize for a in args) + sum(
         o.size * jnp.dtype(o.dtype).itemsize for o in outs
@@ -51,7 +51,8 @@
         rest = refs[n_args + n_outs :]
         copies = []
         for n, place in enumerate(fetched):
-            copies.append(pltpu.make_async_copy(ins[place], rest[n], rest[n_fetched].at[n]))
+            source = ins[place].at[:, columns[place]] if place in columns else ins[place]
+            copies.append(pltpu.make_async_copy(source, rest[n], rest[n_fetched].at[n]))
             ins[place] = rest[n]
         for copy in copies:
             copy.start()
@@ -59,7 +60,13 @@
             copy.wait()
         kernel(*ins, *refs[n_args : n_args + n_outs], *rest[n_fetched + (n_fetched > 0) :])
 
-    buffers = [pltpu.VMEM(args[place].shape, args[place].dtype) for place in fetched]
+    buffers = [
+        pltpu.VMEM(
+            (*args[place].shape[:-1], columns[place].size) if place in columns else args[place].shape,
+            args[place].dtype,
+        )
+        for place in fetched
+    ]
     if fetched:
         buffers.append(pltpu.SemaphoreType.DMA((n_fetched,)))
     return pl.pallas_call(
@@ -110,10 +117,10 @@
     return lax.rem(lax.axis_index("row"), count) ^ distance(step, count)
 
 
-def gated_rows(pair, mask, gain, bias, w_proj, side):
+def gated_rows(pair, mask, gain, bias, w_side):
     rows = pair.shape[0]
-    hidden = w_proj.shape[1] // 4
-    w_flip = transposed(w_proj[:, 2 * side * hidden : 2 * (side + 1) * hidden])
+    hidden = w_side.shape[1] // 2
+    w_flip = transposed(w_side[...])
     gain_col, bias_col = column(gain[...]), column(bias[...])
     masks = cell_masks(mask, rows)
     for row in range(rows):
@@ -123,25 +130,25 @@
         yield row, masks[row] * sigmoid(proj[:hidden]) * proj[hidden:]
 
 
-def project_right_kernel(pair, mask, gain, bias, w_proj, right_panel):
+def project_right_kernel(pair, mask, gain, bias, w_side, right_panel):
     rows = pair.shape[0]
     devices, depth, width = right_panel.shape
     block = depth // rows
-    count = w_proj.shape[1] // 4 // block
-    for row, right in gated_rows(pair, mask, gain, bias, w_proj, 1):
+    count = w_side.shape[1] // 2 // block
+    for row, right in gated_rows(pair, mask, gain, bias, w_side):
         right = right.reshape(count, block, width).astype(BF16)
         for rank in range(devices):
             place = wide_order(devices, count, False)[rank] % count
             right_panel[rank, row * block : (row + 1) * block, :] = right[place]
 
 
-def project_left_kernel(pair, mask, gain, bias, w_proj, after, *refs):
+def project_left_kernel(pair, mask, gain, bias, w_side, after, *refs):
     del after
     *pieces, left_panel = refs
     rows = pair.shape[0]
     count, depth, width = left_panel.shape
     block = depth // rows
-    for row, left in gated_rows(pair, mask, gain, bias, w_proj, 0):
+    for row, left in gated_rows(pair, mask, gain, bias, w_side):
         left = left.reshape(count, block, width).astype(BF16)
         left_panel[:, row * block : (row + 1) * block, :] = left
     for step, piece in enumerate(pieces):
@@ -374,6 +381,7 @@
         [wide_panel],
         [pair, mask, gain, bias, w_proj],
         fetched=range(5),
+        columns={4: pl.ds(2 * hidden, 2 * hidden)},
         flops=2 * cells * channels * 2 * hidden,
         limit=64 * 1024 * 1024 - 640 * 1024,
     )
@@ -384,6 +392,7 @@
         [piece] * count,
         [pair, mask, gain, bias, w_proj, own_right],
         fetched=range(5),
+        columns={4: pl.ds(0, 2 * hidden)},
         unread=(5,),
         scratch=[left_panel],
         flops=2 * cells * channels * 2 * hidden,

time: 62.7 us -> 62.6 us (level)
  transfers between devices with their start and end apart: 16 -> 16, of which waited for: 10 -> 10; matrix products, arithmetic and copies ran while one was open for 0% -> 0% of each run, Pallas kernels for 6% -> 5%
where the time goes in v18:
time: 62.6 us; the launch traced here: 62.2 us
  starting transfers between devices  24.7 us (39%)
  blocking collectives  17.3 us (28%)
  Pallas kernels  9.52 us (15%)
  waiting for transfers between devices  9.08 us (15%)
  local copies, waits for them, and re-layouts  1.34 us (2%)
    all_to_all x2, blocking collectives, swap_half(): lax.all_to_all(values, 'row', split_axis=0, concat_axis=0, tiled=True, ax...  17.3 us
    all_to_all x2, starting transfers between devices, swap(): lax.all_to_all(values, 'row', split_axis=0, concat_axis=0, tiled=True, ax...  13.4 us
    ppermute x14, starting transfers between devices, swap_pieces(): lax.ppermute(pieces[step], 'row', [(d, d ^ distance(step, count)) for d i...  11.3 us
    pallas_call x12, Pallas kernels, call(): pl.pallas_call(body, name=name, out_shape=outs, in_specs=[pl.BlockSpec(me...  9.52 us
    ppermute x14, waiting for transfers between devices, swap_pieces(): lax.ppermute(pieces[step], 'row', [(d, d ^ distance(step, count)) for d i...  8.62 us
    unnamed x22, local copies, waits for them, and re-layouts  1.34 us
  transfers between devices with their start and end apart: 16, of which 10 were waited for; matrix products, arithmetic and copies ran while one was open for 0% of the time, Pallas kernels for 5%

profile of v18, /device:TPU:0, one launch (start us, length us, event | category | flops | bytes accessed | tf_op | source)
XLA Modules:
  0.0 62.2 jit_solution(61395449319276696)
XLA Ops:
  0.0 2.3 %project_right.1.refs_5_ = bf16[16,128,128]{2,1,0:T(8,128)(2,1)} custom-call(bf16[8,128,128]{2,1,0:T(8,128)(2,1)} %refs_0_.7, s32[1,128]{1,0:T(1,128)} %bitcast.13, f32[1,128]{1,0:T(1,128)} %bitcast.5, f32[1,128]{1,0:T(1,128)} %bitcast.9, bf16[128,512]{1,0:T(8,128)(2,1)} %refs_4_.9), custom_call_target="tpu_custom_call" | custom-call | flops 67108864 | bytes 919040 | tf_op jit(solution)/shard_map/project_right/pallas_call | solution.py:72
  2.4 8.5 %all-to-all-start = ((bf16[16,128,128]{2,1,0:T(8,128)(2,1)}), bf16[16,128,128]{2,1,0:T(8,128)(2,1)S(1)}, u32[]{:S(2)}, u32[]{:S(2)}) async-start(bf16[16,128,128]{2,1,0:T(8,128)(2,1)} %project_right.1.refs_5_), calls=%async_computation | async-start | bytes 1048576 | tf_op jit(solution)/shard_map/all_to_all | solution.py:326
  12.4 1.4 %collective-permute-start.2 = (bf16[128,128]{1,0:T(8,128)(2,1)S(1)}, bf16[128,128]{1,0:T(8,128)(2,1)S(1)}, u32[]{:S(2)}, u32[]{:S(2)}) collective-permute-start(bf16[128,128]{1,0:T(8,128)(2,1)S(1)} %get-tuple-element.35), channel_id=1, source_target_pairs={{0,6},{1,7},{2,4},{3,5},{4,2},{5,3},{6,0},{7,1},{8,14},{9,15},{10,... | collective-permute-start | bytes 98312 | tf_op jit(solution)/shard_map/ppermute | solution.py:343
  13.8 0.9 %collective-permute-start.3 = (bf16[128,128]{1,0:T(8,128)(2,1)S(1)}, bf16[128,128]{1,0:T(8,128)(2,1)S(1)}, u32[]{:S(2)}, u32[]{:S(2)}) collective-permute-start(bf16[128,128]{1,0:T(8,128)(2,1)S(1)} %get-tuple-element.36), channel_id=1, source_target_pairs={{0,7},{1,6},{2,5},{3,4},{4,3},{5,2},{6,1},{7,0},{8,15},{9,14},{10,... | collective-permute-start | bytes 98312 | tf_op jit(solution)/shard_map/ppermute | solution.py:343
  15.3 1.5 %collective-permute-start.5 = (bf16[128,128]{1,0:T(8,128)(2,1)S(1)}, bf16[128,128]{1,0:T(8,128)(2,1)S(1)}, u32[]{:S(2)}, u32[]{:S(2)}) collective-permute-start(bf16[128,128]{1,0:T(8,128)(2,1)S(1)} %get-tuple-element.38), channel_id=1, source_target_pairs={{0,5},{1,4},{2,7},{3,6},{4,1},{5,0},{6,3},{7,2},{8,13},{9,12},{10,... | collective-permute-start | bytes 98312 | tf_op jit(solution)/shard_map/ppermute | solution.py:343
  16.8 1.5 %collective-permute-done.1.refs_2_ = bf16[128,128]{1,0:T(8,128)(2,1)S(1)} collective-permute-done((bf16[128,128]{1,0:T(8,128)(2,1)S(1)}, bf16[128,128]{1,0:T(8,128)(2,1)S(1)}, u32[]{:S(2)}, u32[]{:S(2)}) %collective-permute-start.1) | collective-permute-done | bytes 32800 | tf_op jit(solution)/shard_map/ppermute | solution.py:343
  18.3 0.6 %copy-done.9 = f32[128]{0:T(128)S(1)} copy-done((f32[128]{0:T(128)S(1)}, f32[128]{0:T(128)}, u32[]{:S(2)}) %copy-start.9) | copy-done | bytes 536
  19.0 0.8 %prepare.1 = (f32[8,128,128]{2,1,0:T(8,128)S(1)}, f32[8,128,128]{2,1,0:T(8,128)S(1)}) custom-call(bf16[8,128,128]{2,1,0:T(8,128)(2,1)S(1)} %copy-done.1, bf16[8,128,128]{2,1,0:T(8,128)(2,1)S(1)} %copy-done.3, f32[1,128]{1,0:T(1,128)S(1)} %bitcast.7, f32[1,128]{1,0:T(1,128)S(1)} %bitcast.11, bf16[128,128]{1,0:T(8,128)(2,1)S(1)} %copy-done.5, ...), custom_call_target="tpu_custom_call" | custom-call | flops 67108864 | bytes 1639936 | tf_op jit(solution)/shard_map/prepare/pallas_call | solution.py:72
  19.8 1.5 %collective-permute-done.2.refs_3_ = bf16[128,128]{1,0:T(8,128)(2,1)S(1)} collective-permute-done((bf16[128,128]{1,0:T(8,128)(2,1)S(1)}, bf16[128,128]{1,0:T(8,128)(2,1)S(1)}, u32[]{:S(2)}, u32[]{:S(2)}) %collective-permute-start.2) | collective-permute-done | bytes 32800 | tf_op jit(solution)/shard_map/ppermute | solution.py:343
  21.3 0.7 %collective-permute-done.3.refs_4_ = bf16[128,128]{1,0:T(8,128)(2,1)S(1)} collective-permute-done((bf16[128,128]{1,0:T(8,128)(2,1)S(1)}, bf16[128,128]{1,0:T(8,128)(2,1)S(1)}, u32[]{:S(2)}, u32[]{:S(2)}) %collective-permute-start.3) | collective-permute-done | bytes 32800 | tf_op jit(solution)/shard_map/ppermute | solution.py:343
  22.0 1.5 %collective-permute-done.4.refs_5_ = bf16[128,128]{1,0:T(8,128)(2,1)S(1)} collective-permute-done((bf16[128,128]{1,0:T(8,128)(2,1)S(1)}, bf16[128,128]{1,0:T(8,128)(2,1)S(1)}, u32[]{:S(2)}, u32[]{:S(2)}) %collective-permute-start.4) | collective-permute-done | bytes 32800 | tf_op jit(solution)/shard_map/ppermute | solution.py:343
  23.7 0.6 %tri.1 = (bf16[8,128,128]{2,1,0:T(8,128)(2,1)S(1)}, bf16[16,128,128]{2,1,0:T(8,128)(2,1)S(1)}) custom-call(bf16[16,128,128]{2,1,0:T(8,128)(2,1)S(1)} %all-to-all-done.refs_0_, bf16[16,64,128]{2,1,0:T(8,128)(2,1)S(1)} %sort_left.1.refs_1_, f32[8,128,128]{2,1,0:T(8,128)S(1)} %get-tuple-element.40.refs_2_.refs_1_), custom_call_target="tpu_custom_call" | custom-call | flops 33554432 | bytes 2097152 | tf_op jit(solution)/shard_map/tri/pallas_call | solution.py:72
  24.4 8.7 %all_to_all.20.refs_0_ = bf16[8,128,128]{2,1,0:T(8,128)(2,1)S(1)} all-to-all(bf16[8,128,128]{2,1,0:T(8,128)(2,1)S(1)} %get-tuple-element.41), channel_id=1, replica_groups={{0,1,2,3,4,5,6,7},{8,9,10,11,12,13,14,15},{16,17,18,19,20,21,22,23},{24..., dimensions={0} | all-to-all | bytes 524288 | tf_op jit(solution)/shard_map/all_to_all | solution.py:334
  33.4 8.6 %all_to_all.21.refs_0_ = bf16[8,128,128]{2,1,0:T(8,128)(2,1)S(1)} all-to-all(bf16[8,128,128]{2,1,0:T(8,128)(2,1)S(1)} %middle.1), channel_id=1, replica_groups={{0,1,2,3,4,5,6,7},{8,9,10,11,12,13,14,15},{16,17,18,19,20,21,22,23},{24..., dimensions={0} | all-to-all | bytes 524288 | tf_op jit(solution)/shard_map/all_to_all | solution.py:334
  42.0 1.5 %d_right.1 = (bf16[16,128,128]{2,1,0:T(8,128)(2,1)}, bf16[16,64,128]{2,1,0:T(8,128)(2,1)S(1)}) custom-call(bf16[8,128,128]{2,1,0:T(8,128)(2,1)S(1)} %all_to_all.21.refs_0_, bf16[16,64,128]{2,1,0:T(8,128)(2,1)S(1)} %sort_left.1.refs_1_), custom_call_target="tpu_custom_call" | custom-call | flops 33554432 | bytes 1310720 | tf_op jit(solution)/shard_map/d_right/pallas_call | solution.py:72
  43.5 4.9 %all-to-all-start.3 = ((bf16[16,128,128]{2,1,0:T(8,128)(2,1)}), bf16[16,128,128]{2,1,0:T(8,128)(2,1)S(1)}, u32[]{:S(2)}, u32[]{:S(2)}) async-start(bf16[16,128,128]{2,1,0:T(8,128)(2,1)} %get-tuple-element.42), calls=%async_computation.3 | async-start | bytes 1048576 | tf_op jit(solution)/shard_map/all_to_all | solution.py:326
  48.9 1.5 %collective-permute-start.8 = (bf16[128,128]{1,0:T(8,128)(2,1)S(1)}, bf16[128,128]{1,0:T(8,128)(2,1)S(1)}, u32[]{:S(2)}, u32[]{:S(2)}) collective-permute-start(bf16[128,128]{1,0:T(8,128)(2,1)S(1)} %get-tuple-element.47), channel_id=1, source_target_pairs={{0,2},{1,3},{2,0},{3,1},{4,6},{5,7},{6,4},{7,5},{8,10},{9,11},{10,... | collective-permute-start | bytes 98312 | tf_op jit(solution)/shard_map/ppermute | solution.py:343
  50.7 2.0 %collective-permute-start.10 = (bf16[128,128]{1,0:T(8,128)(2,1)S(1)}, bf16[128,128]{1,0:T(8,128)(2,1)S(1)}, u32[]{:S(2)}, u32[]{:S(2)}) collective-permute-start(bf16[128,128]{1,0:T(8,128)(2,1)S(1)} %get-tuple-element.49), channel_id=1, source_target_pairs={{0,7},{1,6},{2,5},{3,4},{4,3},{5,2},{6,1},{7,0},{8,15},{9,14},{10,... | collective-permute-start | bytes 98312 | tf_op jit(solution)/shard_map/ppermute | solution.py:343
  53.2 1.6 %collective-permute-start.12 = (bf16[128,128]{1,0:T(8,128)(2,1)S(1)}, bf16[128,128]{1,0:T(8,128)(2,1)S(1)}, u32[]{:S(2)}, u32[]{:S(2)}) collective-permute-start(bf16[128,128]{1,0:T(8,128)(2,1)S(1)} %get-tuple-element.51), channel_id=1, source_target_pairs={{0,5},{1,4},{2,7},{3,6},{4,1},{5,0},{6,3},{7,2},{8,13},{9,12},{10,... | collective-permute-start | bytes 98312 | tf_op jit(solution)/shard_map/ppermute | solution.py:343
  54.8 1.2 %collective-permute-done.8.refs_2_ = bf16[128,128]{1,0:T(8,128)(2,1)S(1)} collective-permute-done((bf16[128,128]{1,0:T(8,128)(2,1)S(1)}, bf16[128,128]{1,0:T(8,128)(2,1)S(1)}, u32[]{:S(2)}, u32[]{:S(2)}) %collective-permute-start.8) | collective-permute-done | bytes 32800 | tf_op jit(solution)/shard_map/ppermute | solution.py:343
  56.0 0.7 %copy-done.10 = f32[128]{0:T(128)S(1)} copy-done((f32[128]{0:T(128)S(1)}, f32[128]{0:T(128)}, u32[]{:S(2)}) %copy-start.10) | copy-done | bytes 536
  57.1 1.0 %slopes.1 = (bf16[8,512,128]{2,1,0:T(8,128)(2,1)S(1)}, bf16[8,128,128]{2,1,0:T(8,128)(2,1)S(1)}, f32[8,128]{1,0:T(8,128)S(1)}, f32[128,128]{1,0:T(8,128)S(1)}, bf16[128,640]{1,0:T(8,128)(2,1)S(1)}) custom-call(bf16[8,128,128]{2,1,0:T(8,128)(2,1)S(1)} %copy-done.1, s32[1,128]{1,0:T(1,128)S(1)} %bitcast.15, f32[1,128]{1,0:T(1,128)S(1)} %bitcast.8, ...), custom_call_target="tpu_custom_call" | custom-call | flops 134217728 | bytes 2233856 | tf_op jit(solution)/shard_map/slopes/pallas_call | solution.py:72
  58.7 0.7 %collective-permute-done.10.refs_4_ = bf16[128,128]{1,0:T(8,128)(2,1)S(1)} collective-permute-done((bf16[128,128]{1,0:T(8,128)(2,1)S(1)}, bf16[128,128]{1,0:T(8,128)(2,1)S(1)}, u32[]{:S(2)}, u32[]{:S(2)}) %collective-permute-start.10) | collective-permute-done | bytes 32800 | tf_op jit(solution)/shard_map/ppermute | solution.py:343
  60.8 1.4 %finish.1 = bf16[8,128,128]{2,1,0:T(8,128)(2,1)} custom-call(bf16[16,128,128]{2,1,0:T(8,128)(2,1)S(1)} %all-to-all-done.3.refs_0_, bf16[8,128,128]{2,1,0:T(8,128)(2,1)S(1)} %sort_d_left.1.refs_1_, bf16[8,512,128]{2,1,0:T(8,128)(2,1)S(1)} %get-tuple-element.54.refs_2_, bf16[8,128,128]{2,1,0:T(8,128)(2,1)S(1)} %gate_back.1.refs_6_.refs_3_, ...), custom_call_target="tpu_custom_call" | custom-call | flops 134217728 | bytes 2854912 | tf_op jit(solution)/shard_map/finish/pallas_call | solution.py:72
  (44 shorter events, 6.4 us)
Async XLA Ops:
  2.3 8.6 %copy-start = (bf16[16,128,128]{2,1,0:T(8,128)(2,1)S(1)}, bf16[16,128,128]{2,1,0:T(8,128)(2,1)}, u32[]{:S(2)}) copy-start(bf16[16,128,128]{2,1,0:T(8,128)(2,1)} %project_right.1.refs_5_) | copy-start | bytes 1572868
  2.3 8.6 %copy-start.1 = (bf16[8,128,128]{2,1,0:T(8,128)(2,1)S(1)}, bf16[8,128,128]{2,1,0:T(8,128)(2,1)}, u32[]{:S(2)}) copy-start(bf16[8,128,128]{2,1,0:T(8,128)(2,1)} %refs_0_.7) | copy-start | bytes 786436
  2.3 8.6 %copy-start.2 = (bf16[128,512]{1,0:T(8,128)(2,1)S(1)}, bf16[128,512]{1,0:T(8,128)(2,1)}, u32[]{:S(2)}) copy-start(bf16[128,512]{1,0:T(8,128)(2,1)} %refs_4_.9) | copy-start | bytes 393220
  2.3 8.6 %copy-start.6 = (f32[128]{0:T(128)S(1)}, f32[128]{0:T(128)}, u32[]{:S(2)}) copy-start(f32[128]{0:T(128)} %param.13) | copy-start | bytes 1540
  2.4 8.6 %copy-start.7 = (f32[128]{0:T(128)S(1)}, f32[128]{0:T(128)}, u32[]{:S(2)}) copy-start(f32[128]{0:T(128)} %param.14) | copy-start | bytes 1540
  2.4 8.6 %copy-start.8 = (s32[128]{0:T(128)S(1)}, s32[128]{0:T(128)}, u32[]{:S(2)}) copy-start(s32[128]{0:T(128)} %param.12) | copy-start | bytes 1540
  2.4 21.3 %all-to-all-start = ((bf16[16,128,128]{2,1,0:T(8,128)(2,1)}), bf16[16,128,128]{2,1,0:T(8,128)(2,1)S(1)}, u32[]{:S(2)}, u32[]{:S(2)}) async-start(bf16[16,128,128]{2,1,0:T(8,128)(2,1)} %project_right.1.refs_5_), calls=%async_computation | async-start | bytes 1048576 | tf_op jit(solution)/shard_map/all_to_all | solution.py:326
  11.0 7.4 %copy-start.3 = (bf16[8,128,128]{2,1,0:T(8,128)(2,1)S(1)}, bf16[8,128,128]{2,1,0:T(8,128)(2,1)}, u32[]{:S(2)}) copy-start(bf16[8,128,128]{2,1,0:T(8,128)(2,1)} %refs_1_.1) | copy-start | bytes 786436
  11.0 7.3 %copy-start.4 = (bf16[128,128]{1,0:T(8,128)(2,1)S(1)}, bf16[128,128]{1,0:T(8,128)(2,1)}, u32[]{:S(2)}) copy-start(bf16[128,128]{1,0:T(8,128)(2,1)} %refs_4_.8) | copy-start | bytes 98308
  11.6 3.7 %collective-permute-start = (bf16[128,128]{1,0:T(8,128)(2,1)S(1)}, bf16[128,128]{1,0:T(8,128)(2,1)S(1)}, u32[]{:S(2)}, u32[]{:S(2)}) collective-permute-start(bf16[128,128]{1,0:T(8,128)(2,1)S(1)} %get-tuple-element.33), channel_id=1, source_target_pairs={{0,1},{1,0},{2,3},{3,2},{4,5},{5,4},{6,7},{7,6},{8,9},{9,8},{10,11... | collective-permute-start | bytes 98312 | tf_op jit(solution)/shard_map/ppermute | solution.py:343
  11.8 6.5 %collective-permute-start.1 = (bf16[128,128]{1,0:T(8,128)(2,1)S(1)}, bf16[128,128]{1,0:T(8,128)(2,1)S(1)}, u32[]{:S(2)}, u32[]{:S(2)}) collective-permute-start(bf16[128,128]{1,0:T(8,128)(2,1)S(1)} %get-tuple-element.34), channel_id=1, source_target_pairs={{0,2},{1,3},{2,0},{3,1},{4,6},{5,7},{6,4},{7,5},{8,10},{9,11},{10,... | collective-permute-start | bytes 98312 | tf_op jit(solution)/shard_map/ppermute | solution.py:343
  12.4 8.8 %collective-permute-start.2 = (bf16[128,128]{1,0:T(8,128)(2,1)S(1)}, bf16[128,128]{1,0:T(8,128)(2,1)S(1)}, u32[]{:S(2)}, u32[]{:S(2)}) collective-permute-start(bf16[128,128]{1,0:T(8,128)(2,1)S(1)} %get-tuple-element.35), channel_id=1, source_target_pairs={{0,6},{1,7},{2,4},{3,5},{4,2},{5,3},{6,0},{7,1},{8,14},{9,15},{10,... | collective-permute-start | bytes 98312 | tf_op jit(solution)/shard_map/ppermute | solution.py:343
  13.8 8.1 %collective-permute-start.3 = (bf16[128,128]{1,0:T(8,128)(2,1)S(1)}, bf16[128,128]{1,0:T(8,128)(2,1)S(1)}, u32[]{:S(2)}, u32[]{:S(2)}) collective-permute-start(bf16[128,128]{1,0:T(8,128)(2,1)S(1)} %get-tuple-element.36), channel_id=1, source_target_pairs={{0,7},{1,6},{2,5},{3,4},{4,3},{5,2},{6,1},{7,0},{8,15},{9,14},{10,... | collective-permute-start | bytes 98312 | tf_op jit(solution)/shard_map/ppermute | solution.py:343
  14.8 8.8 %collective-permute-start.4 = (bf16[128,128]{1,0:T(8,128)(2,1)S(1)}, bf16[128,128]{1,0:T(8,128)(2,1)S(1)}, u32[]{:S(2)}, u32[]{:S(2)}) collective-permute-start(bf16[128,128]{1,0:T(8,128)(2,1)S(1)} %get-tuple-element.37), channel_id=1, source_target_pairs={{0,4},{1,5},{2,6},{3,7},{4,0},{5,1},{6,2},{7,3},{8,12},{9,13},{10,... | collective-permute-start | bytes 98312 | tf_op jit(solution)/shard_map/ppermute | solution.py:343
  15.3 8.2 %collective-permute-start.5 = (bf16[128,128]{1,0:T(8,128)(2,1)S(1)}, bf16[128,128]{1,0:T(8,128)(2,1)S(1)}, u32[]{:S(2)}, u32[]{:S(2)}) collective-permute-start(bf16[128,128]{1,0:T(8,128)(2,1)S(1)} %get-tuple-element.38), channel_id=1, source_target_pairs={{0,5},{1,4},{2,7},{3,6},{4,1},{5,0},{6,3},{7,2},{8,13},{9,12},{10,... | collective-permute-start | bytes 98312 | tf_op jit(solution)/shard_map/ppermute | solution.py:343
  18.3 5.2 %collective-permute-start.6 = (bf16[128,128]{1,0:T(8,128)(2,1)S(1)}, bf16[128,128]{1,0:T(8,128)(2,1)S(1)}, u32[]{:S(2)}, u32[]{:S(2)}) collective-permute-start(bf16[128,128]{1,0:T(8,128)(2,1)S(1)} %get-tuple-element.39), channel_id=1, source_target_pairs={{0,3},{1,2},{2,1},{3,0},{4,7},{5,6},{6,5},{7,4},{8,11},{9,10},{10,... | collective-permute-start | bytes 98312 | tf_op jit(solution)/shard_map/ppermute | solution.py:343
  43.5 17.3 %all-to-all-start.3 = ((bf16[16,128,128]{2,1,0:T(8,128)(2,1)}), bf16[16,128,128]{2,1,0:T(8,128)(2,1)S(1)}, u32[]{:S(2)}, u32[]{:S(2)}) async-start(bf16[16,128,128]{2,1,0:T(8,128)(2,1)} %get-tuple-element.42), calls=%async_computation.3 | async-start | bytes 1048576 | tf_op jit(solution)/shard_map/all_to_all | solution.py:326
  48.7 4.5 %collective-permute-start.7 = (bf16[128,128]{1,0:T(8,128)(2,1)S(1)}, bf16[128,128]{1,0:T(8,128)(2,1)S(1)}, u32[]{:S(2)}, u32[]{:S(2)}) collective-permute-start(bf16[128,128]{1,0:T(8,128)(2,1)S(1)} %get-tuple-element.46), channel_id=1, source_target_pairs={{0,1},{1,0},{2,3},{3,2},{4,5},{5,4},{6,7},{7,6},{8,9},{9,8},{10,11... | collective-permute-start | bytes 98312 | tf_op jit(solution)/shard_map/ppermute | solution.py:343
  48.9 7.1 %collective-permute-start.8 = (bf16[128,128]{1,0:T(8,128)(2,1)S(1)}, bf16[128,128]{1,0:T(8,128)(2,1)S(1)}, u32[]{:S(2)}, u32[]{:S(2)}) collective-permute-start(bf16[128,128]{1,0:T(8,128)(2,1)S(1)} %get-tuple-element.47), channel_id=1, source_target_pairs={{0,2},{1,3},{2,0},{3,1},{4,6},{5,7},{6,4},{7,5},{8,10},{9,11},{10,... | collective-permute-start | bytes 98312 | tf_op jit(solution)/shard_map/ppermute | solution.py:343
  50.4 8.3 %collective-permute-start.9 = (bf16[128,128]{1,0:T(8,128)(2,1)S(1)}, bf16[128,128]{1,0:T(8,128)(2,1)S(1)}, u32[]{:S(2)}, u32[]{:S(2)}) collective-permute-start(bf16[128,128]{1,0:T(8,128)(2,1)S(1)} %get-tuple-element.48), channel_id=1, source_target_pairs={{0,6},{1,7},{2,4},{3,5},{4,2},{5,3},{6,0},{7,1},{8,14},{9,15},{10,... | collective-permute-start | bytes 98312 | tf_op jit(solution)/shard_map/ppermute | solution.py:343
  50.7 8.7 %collective-permute-start.10 = (bf16[128,128]{1,0:T(8,128)(2,1)S(1)}, bf16[128,128]{1,0:T(8,128)(2,1)S(1)}, u32[]{:S(2)}, u32[]{:S(2)}) collective-permute-start(bf16[128,128]{1,0:T(8,128)(2,1)S(1)} %get-tuple-element.49), channel_id=1, source_target_pairs={{0,7},{1,6},{2,5},{3,4},{4,3},{5,2},{6,1},{7,0},{8,15},{9,14},{10,... | collective-permute-start | bytes 98312 | tf_op jit(solution)/shard_map/ppermute | solution.py:343
  52.7 7.2 %collective-permute-start.11 = (bf16[128,128]{1,0:T(8,128)(2,1)S(1)}, bf16[128,128]{1,0:T(8,128)(2,1)S(1)}, u32[]{:S(2)}, u32[]{:S(2)}) collective-permute-start(bf16[128,128]{1,0:T(8,128)(2,1)S(1)} %get-tuple-element.50), channel_id=1, source_target_pairs={{0,4},{1,5},{2,6},{3,7},{4,0},{5,1},{6,2},{7,3},{8,12},{9,13},{10,... | collective-permute-start | bytes 98312 | tf_op jit(solution)/shard_map/ppermute | solution.py:343
  53.2 7.1 %collective-permute-start.12 = (bf16[128,128]{1,0:T(8,128)(2,1)S(1)}, bf16[128,128]{1,0:T(8,128)(2,1)S(1)}, u32[]{:S(2)}, u32[]{:S(2)}) collective-permute-start(bf16[128,128]{1,0:T(8,128)(2,1)S(1)} %get-tuple-element.51), channel_id=1, source_target_pairs={{0,5},{1,4},{2,7},{3,6},{4,1},{5,0},{6,3},{7,2},{8,13},{9,12},{10,... | collective-permute-start | bytes 98312 | tf_op jit(solution)/shard_map/ppermute | solution.py:343
  56.0 4.3 %collective-permute-start.13 = (bf16[128,128]{1,0:T(8,128)(2,1)S(1)}, bf16[128,128]{1,0:T(8,128)(2,1)S(1)}, u32[]{:S(2)}, u32[]{:S(2)}) collective-permute-start(bf16[128,128]{1,0:T(8,128)(2,1)S(1)} %get-tuple-element.52), channel_id=1, source_target_pairs={{0,3},{1,2},{2,1},{3,0},{4,7},{5,6},{6,5},{7,4},{8,11},{9,10},{10,... | collective-permute-start | bytes 98312 | tf_op jit(solution)/shard_map/ppermute | solution.py:343
  (3 other events, 8.7 us)

commit v19 on v16

--- a/solution.py
+++ b/solution.py
@@ -101,6 +101,10 @@
     return order
 
 
+def half_order(count):
+    return [*range(0, count, 2), *range(1, count, 2)]
+
+
 def distance(step, count):
     far = sorted(range(3, count), key=lambda apart: -(apart // 2))
     return [*range(min(3, count)), *far][step]
@@ -165,8 +169,10 @@
         gate_slope[row] = cot * gate * (1.0 - gate)
 
 
-def spread(panel, wide):
-    wide[...] = panel[...].astype(F32).reshape(wide.shape)
+def half_places(panel):
+    count, depth, _ = panel.shape
+    for rank, place in enumerate(half_order(count)):
+        yield rank, slice(place * depth, (place + 1) * depth)
 
 
 def wide_places(panel, count, back):
@@ -196,33 +202,39 @@
         right = right_wide[pl.ds(h, right_rows, stride=block), :].astype(BF16)
         right_all[h] = right
         left_wide[pl.ds(h, left_rows, stride=block), :] = dot(left_all[h], right, 1, 1)
-    products[...] = left_wide[...].astype(BF16).reshape(products.shape)
-
-
-def cell_row(ref, row, rows):
+    for rank, place in half_places(products):
+        products[rank] = left_wide[place, :].astype(BF16)
+
+
+def cell_row(ref, row, rows, order=None):
     count, depth, width = ref.shape
     block = depth // rows
-    return ref[:, row * block : (row + 1) * block, :].astype(F32).reshape(count * block, width)
+    part = ref[:, row * block : (row + 1) * block, :].astype(F32)
+    if order:
+        part = jnp.stack([part[order.index(place)] for place in range(count)])
+    return part.reshape(count * block, width)
 
 
 def middle_kernel(products, d_hat_centered, d_products):
     rows = d_hat_centered.shape[0]
     count, depth, width = products.shape
     block = depth // rows
+    order = half_order(count)
     for row in range(rows):
-        tri_hat, inv_std = norm_rows(cell_row(products, row, rows))
+        tri_hat, inv_std = norm_rows(cell_row(products, row, rows, order))
         d_hat = d_hat_centered[row]
         cross = jnp.mean(d_hat * tri_hat, axis=0, keepdims=True)
         d_tri = inv_std * (d_hat - tri_hat * cross)
-        d_products[:, row * block : (row + 1) * block, :] = d_tri.reshape(
-            count, block, width
-        ).astype(BF16)
+        d_tri = d_tri.reshape(count, block, width).astype(BF16)
+        for rank, place in enumerate(order):
+            d_products[rank, row * block : (row + 1) * block, :] = d_tri[place]
 
 
 def d_right_kernel(d_products, left_all, d_right_panel, d_tri_all, left_wide, right_wide):
     block, left_rows, _ = left_all.shape
     right_rows = right_wide.shape[0] // block
-    spread(d_products, left_wide)
+    for rank, place in half_places(d_products):
+        left_wide[place, :] = d_products[rank].astype(F32)
     for h in range(block):
         d_tri = left_wide[pl.ds(h, left_rows, stride=block), :].astype(BF16)
         d_tri_all[h] = d_tri
@@ -247,7 +259,7 @@
     out_flip = transposed(w_out[...])
     out_gain_col, out_bias_col = column(out_gain[...]), column(out_bias[...])
     for row in range(rows):
-        tri_hat, _ = norm_rows(cell_row(products, row, rows))
+        tri_hat, _ = norm_rows(cell_row(products, row, rows, half_order(products.shape[0])))
         scaled = (tri_hat * out_gain_col + out_bias_col).astype(BF16)
         d_gate_pre[row] = (dot(out_flip, scaled, 1, 0) * gate_slope[row]).astype(BF16)
 
@@ -323,7 +335,8 @@
 
 def swap_half(values, count):
     devices = range(lax.axis_size("row"))
-    groups = [[d for d in devices if d // count == half] for half in range(len(devices) // count)]
+    order = half_order(count)
+    groups = [[start + place for place in order] for start in range(0, len(devices), count)]
     return lax.all_to_all(
         values, "row", split_axis=0, concat_axis=0, tiled=True, axis_index_groups=groups
     )

time: 62.7 us -> 63.1 us (level)
  blocking collectives: 17.3 us -> 18.2 us
    all_to_all x2, blocking collectives: 17.3 us -> 18.2 us  [swap_half(): lax.all_to_all(values, 'row', split_axis=0, concat_axis=0, tiled=True, ax...]
where the time goes in v19:
time: 63.1 us; the launch traced here: 62.6 us
  starting transfers between devices  24.2 us (38%)
  blocking collectives  18.2 us (29%)
  Pallas kernels  9.82 us (16%)
  waiting for transfers between devices  8.85 us (14%)
  local copies, waits for them, and re-layouts  1.34 us (2%)
    all_to_all x2, blocking collectives, swap_half(): lax.all_to_all(values, 'row', split_axis=0, concat_axis=0, tiled=True, ax...  18.2 us
    all_to_all x2, starting transfers between devices, swap(): lax.all_to_all(values, 'row', split_axis=0, concat_axis=0, tiled=True, ax...  12.8 us
    ppermute x14, starting transfers between devices, swap_pieces(): lax.ppermute(pieces[step], 'row', [(d, d ^ distance(step, count)) for d i...  11.3 us
    pallas_call x12, Pallas kernels, call(): pl.pallas_call(body, name=name, out_shape=outs, in_specs=[pl.BlockSpec(me...  9.82 us
    ppermute x14, waiting for transfers between devices, swap_pieces(): lax.ppermute(pieces[step], 'row', [(d, d ^ distance(step, count)) for d i...  8.39 us
    unnamed x22, local copies, waits for them, and re-layouts  1.34 us
  transfers between devices with their start and end apart: 16, of which 10 were waited for; matrix products, arithmetic and copies ran while one was open for 0% of the time, Pallas kernels for 6%

profile of v19, /device:TPU:0, one launch (start us, length us, event | category | flops | bytes accessed | tf_op | source)
XLA Modules:
  0.0 62.6 jit_solution(13211538872833624731)
XLA Ops:
  0.0 2.4 %project_right.1.refs_5_ = bf16[16,128,128]{2,1,0:T(8,128)(2,1)} custom-call(bf16[8,128,128]{2,1,0:T(8,128)(2,1)} %refs_0_.7, s32[1,128]{1,0:T(1,128)} %bitcast.13, f32[1,128]{1,0:T(1,128)} %bitcast.5, f32[1,128]{1,0:T(1,128)} %bitcast.9, bf16[128,512]{1,0:T(8,128)(2,1)} %refs_4_.9), custom_call_target="tpu_custom_call" | custom-call | flops 67108864 | bytes 919040 | tf_op jit(solution)/shard_map/project_right/pallas_call | solution.py:65
  2.5 8.5 %all-to-all-start = ((bf16[16,128,128]{2,1,0:T(8,128)(2,1)}), bf16[16,128,128]{2,1,0:T(8,128)(2,1)S(1)}, u32[]{:S(2)}, u32[]{:S(2)}) async-start(bf16[16,128,128]{2,1,0:T(8,128)(2,1)} %project_right.1.refs_5_), calls=%async_computation | async-start | bytes 1048576 | tf_op jit(solution)/shard_map/all_to_all | solution.py:331
  11.1 0.8 %project_left.1 = (bf16[128,128]{1,0:T(8,128)(2,1)S(1)}, bf16[128,128]{1,0:T(8,128)(2,1)S(1)}, bf16[128,128]{1,0:T(8,128)(2,1)S(1)}, bf16[128,128]{1,0:T(8,128)(...) custom-call(bf16[8,128,128]{2,1,0:T(8,128)(2,1)S(1)} %copy-done.1, ...), custom_call_target="tpu_custom_call" | custom-call | flops 67108864 | bytes 1181184 | tf_op jit(solution)/shard_map/project_left/pallas_call | solution.py:65
  12.7 1.4 %collective-permute-start.2 = (bf16[128,128]{1,0:T(8,128)(2,1)S(1)}, bf16[128,128]{1,0:T(8,128)(2,1)S(1)}, u32[]{:S(2)}, u32[]{:S(2)}) collective-permute-start(bf16[128,128]{1,0:T(8,128)(2,1)S(1)} %get-tuple-element.35), channel_id=1, source_target_pairs={{0,6},{1,7},{2,4},{3,5},{4,2},{5,3},{6,0},{7,1},{8,14},{9,15},{10,... | collective-permute-start | bytes 98312 | tf_op jit(solution)/shard_map/ppermute | solution.py:349
  14.1 0.9 %collective-permute-start.3 = (bf16[128,128]{1,0:T(8,128)(2,1)S(1)}, bf16[128,128]{1,0:T(8,128)(2,1)S(1)}, u32[]{:S(2)}, u32[]{:S(2)}) collective-permute-start(bf16[128,128]{1,0:T(8,128)(2,1)S(1)} %get-tuple-element.36), channel_id=1, source_target_pairs={{0,7},{1,6},{2,5},{3,4},{4,3},{5,2},{6,1},{7,0},{8,15},{9,14},{10,... | collective-permute-start | bytes 98312 | tf_op jit(solution)/shard_map/ppermute | solution.py:349
  15.6 1.5 %collective-permute-start.5 = (bf16[128,128]{1,0:T(8,128)(2,1)S(1)}, bf16[128,128]{1,0:T(8,128)(2,1)S(1)}, u32[]{:S(2)}, u32[]{:S(2)}) collective-permute-start(bf16[128,128]{1,0:T(8,128)(2,1)S(1)} %get-tuple-element.38), channel_id=1, source_target_pairs={{0,5},{1,4},{2,7},{3,6},{4,1},{5,0},{6,3},{7,2},{8,13},{9,12},{10,... | collective-permute-start | bytes 98312 | tf_op jit(solution)/shard_map/ppermute | solution.py:349
  17.1 1.3 %collective-permute-done.1.refs_2_ = bf16[128,128]{1,0:T(8,128)(2,1)S(1)} collective-permute-done((bf16[128,128]{1,0:T(8,128)(2,1)S(1)}, bf16[128,128]{1,0:T(8,128)(2,1)S(1)}, u32[]{:S(2)}, u32[]{:S(2)}) %collective-permute-start.1) | collective-permute-done | bytes 32800 | tf_op jit(solution)/shard_map/ppermute | solution.py:349
  19.1 0.8 %prepare.1 = (f32[8,128,128]{2,1,0:T(8,128)S(1)}, f32[8,128,128]{2,1,0:T(8,128)S(1)}) custom-call(bf16[8,128,128]{2,1,0:T(8,128)(2,1)S(1)} %copy-done.1, bf16[8,128,128]{2,1,0:T(8,128)(2,1)S(1)} %copy-done.3, f32[1,128]{1,0:T(1,128)S(1)} %bitcast.7, f32[1,128]{1,0:T(1,128)S(1)} %bitcast.11, bf16[128,128]{1,0:T(8,128)(2,1)S(1)} %copy-done.5, ...), custom_call_target="tpu_custom_call" | custom-call | flops 67108864 | bytes 1639936 | tf_op jit(solution)/shard_map/prepare/pallas_call | solution.py:65
  19.9 1.5 %collective-permute-done.2.refs_3_ = bf16[128,128]{1,0:T(8,128)(2,1)S(1)} collective-permute-done((bf16[128,128]{1,0:T(8,128)(2,1)S(1)}, bf16[128,128]{1,0:T(8,128)(2,1)S(1)}, u32[]{:S(2)}, u32[]{:S(2)}) %collective-permute-start.2) | collective-permute-done | bytes 32800 | tf_op jit(solution)/shard_map/ppermute | solution.py:349
  21.3 0.7 %collective-permute-done.3.refs_4_ = bf16[128,128]{1,0:T(8,128)(2,1)S(1)} collective-permute-done((bf16[128,128]{1,0:T(8,128)(2,1)S(1)}, bf16[128,128]{1,0:T(8,128)(2,1)S(1)}, u32[]{:S(2)}, u32[]{:S(2)}) %collective-permute-start.3) | collective-permute-done | bytes 32800 | tf_op jit(solution)/shard_map/ppermute | solution.py:349
  22.0 1.5 %collective-permute-done.4.refs_5_ = bf16[128,128]{1,0:T(8,128)(2,1)S(1)} collective-permute-done((bf16[128,128]{1,0:T(8,128)(2,1)S(1)}, bf16[128,128]{1,0:T(8,128)(2,1)S(1)}, u32[]{:S(2)}, u32[]{:S(2)}) %collective-permute-start.4) | collective-permute-done | bytes 32800 | tf_op jit(solution)/shard_map/ppermute | solution.py:349
  23.8 0.6 %tri.1 = (bf16[8,128,128]{2,1,0:T(8,128)(2,1)S(1)}, bf16[16,128,128]{2,1,0:T(8,128)(2,1)S(1)}) custom-call(bf16[16,128,128]{2,1,0:T(8,128)(2,1)S(1)} %all-to-all-done.refs_0_, bf16[16,64,128]{2,1,0:T(8,128)(2,1)S(1)} %sort_left.1.refs_1_, f32[8,128,128]{2,1,0:T(8,128)S(1)} %get-tuple-element.40.refs_2_.refs_1_), custom_call_target="tpu_custom_call" | custom-call | flops 33554432 | bytes 2097152 | tf_op jit(solution)/shard_map/tri/pallas_call | solution.py:65
  24.5 9.2 %all_to_all.20.refs_0_ = bf16[8,128,128]{2,1,0:T(8,128)(2,1)S(1)} all-to-all(bf16[8,128,128]{2,1,0:T(8,128)(2,1)S(1)} %get-tuple-element.41), channel_id=1, replica_groups={{0,2,4,6,1,3,5,7},{8,10,12,14,9,11,13,15},{16,18,20,22,17,19,21,23},{24..., dimensions={0} | all-to-all | bytes 524288 | tf_op jit(solution)/shard_map/all_to_all | solution.py:340
  34.0 9.0 %all_to_all.21.refs_0_ = bf16[8,128,128]{2,1,0:T(8,128)(2,1)S(1)} all-to-all(bf16[8,128,128]{2,1,0:T(8,128)(2,1)S(1)} %middle.1), channel_id=1, replica_groups={{0,2,4,6,1,3,5,7},{8,10,12,14,9,11,13,15},{16,18,20,22,17,19,21,23},{24..., dimensions={0} | all-to-all | bytes 524288 | tf_op jit(solution)/shard_map/all_to_all | solution.py:340
  43.0 1.5 %d_right.1 = (bf16[16,128,128]{2,1,0:T(8,128)(2,1)}, bf16[16,64,128]{2,1,0:T(8,128)(2,1)S(1)}) custom-call(bf16[8,128,128]{2,1,0:T(8,128)(2,1)S(1)} %all_to_all.21.refs_0_, bf16[16,64,128]{2,1,0:T(8,128)(2,1)S(1)} %sort_left.1.refs_1_), custom_call_target="tpu_custom_call" | custom-call | flops 33554432 | bytes 1310720 | tf_op jit(solution)/shard_map/d_right/pallas_call | solution.py:65
  44.5 4.3 %all-to-all-start.3 = ((bf16[16,128,128]{2,1,0:T(8,128)(2,1)}), bf16[16,128,128]{2,1,0:T(8,128)(2,1)S(1)}, u32[]{:S(2)}, u32[]{:S(2)}) async-start(bf16[16,128,128]{2,1,0:T(8,128)(2,1)} %get-tuple-element.42), calls=%async_computation.3 | async-start | bytes 1048576 | tf_op jit(solution)/shard_map/all_to_all | solution.py:331
  49.3 1.5 %collective-permute-start.8 = (bf16[128,128]{1,0:T(8,128)(2,1)S(1)}, bf16[128,128]{1,0:T(8,128)(2,1)S(1)}, u32[]{:S(2)}, u32[]{:S(2)}) collective-permute-start(bf16[128,128]{1,0:T(8,128)(2,1)S(1)} %get-tuple-element.47), channel_id=1, source_target_pairs={{0,2},{1,3},{2,0},{3,1},{4,6},{5,7},{6,4},{7,5},{8,10},{9,11},{10,... | collective-permute-start | bytes 98312 | tf_op jit(solution)/shard_map/ppermute | solution.py:349
  51.1 2.0 %collective-permute-start.10 = (bf16[128,128]{1,0:T(8,128)(2,1)S(1)}, bf16[128,128]{1,0:T(8,128)(2,1)S(1)}, u32[]{:S(2)}, u32[]{:S(2)}) collective-permute-start(bf16[128,128]{1,0:T(8,128)(2,1)S(1)} %get-tuple-element.49), channel_id=1, source_target_pairs={{0,7},{1,6},{2,5},{3,4},{4,3},{5,2},{6,1},{7,0},{8,15},{9,14},{10,... | collective-permute-start | bytes 98312 | tf_op jit(solution)/shard_map/ppermute | solution.py:349
  53.7 1.6 %collective-permute-start.12 = (bf16[128,128]{1,0:T(8,128)(2,1)S(1)}, bf16[128,128]{1,0:T(8,128)(2,1)S(1)}, u32[]{:S(2)}, u32[]{:S(2)}) collective-permute-start(bf16[128,128]{1,0:T(8,128)(2,1)S(1)} %get-tuple-element.51), channel_id=1, source_target_pairs={{0,5},{1,4},{2,7},{3,6},{4,1},{5,0},{6,3},{7,2},{8,13},{9,12},{10,... | collective-permute-start | bytes 98312 | tf_op jit(solution)/shard_map/ppermute | solution.py:349
  55.2 1.2 %collective-permute-done.8.refs_2_ = bf16[128,128]{1,0:T(8,128)(2,1)S(1)} collective-permute-done((bf16[128,128]{1,0:T(8,128)(2,1)S(1)}, bf16[128,128]{1,0:T(8,128)(2,1)S(1)}, u32[]{:S(2)}, u32[]{:S(2)}) %collective-permute-start.8) | collective-permute-done | bytes 32800 | tf_op jit(solution)/shard_map/ppermute | solution.py:349
  56.4 0.7 %copy-done.10 = f32[128]{0:T(128)S(1)} copy-done((f32[128]{0:T(128)S(1)}, f32[128]{0:T(128)}, u32[]{:S(2)}) %copy-start.10) | copy-done | bytes 536
  57.5 1.0 %slopes.1 = (bf16[8,512,128]{2,1,0:T(8,128)(2,1)S(1)}, bf16[8,128,128]{2,1,0:T(8,128)(2,1)S(1)}, f32[8,128]{1,0:T(8,128)S(1)}, f32[128,128]{1,0:T(8,128)S(1)}, bf16[128,640]{1,0:T(8,128)(2,1)S(1)}) custom-call(bf16[8,128,128]{2,1,0:T(8,128)(2,1)S(1)} %copy-done.1, s32[1,128]{1,0:T(1,128)S(1)} %bitcast.15, f32[1,128]{1,0:T(1,128)S(1)} %bitcast.8, ...), custom_call_target="tpu_custom_call" | custom-call | flops 134217728 | bytes 2233856 | tf_op jit(solution)/shard_map/slopes/pallas_call | solution.py:65
  59.1 0.7 %collective-permute-done.10.refs_4_ = bf16[128,128]{1,0:T(8,128)(2,1)S(1)} collective-permute-done((bf16[128,128]{1,0:T(8,128)(2,1)S(1)}, bf16[128,128]{1,0:T(8,128)(2,1)S(1)}, u32[]{:S(2)}, u32[]{:S(2)}) %collective-permute-start.10) | collective-permute-done | bytes 32800 | tf_op jit(solution)/shard_map/ppermute | solution.py:349
  61.2 1.4 %finish.1 = bf16[8,128,128]{2,1,0:T(8,128)(2,1)} custom-call(bf16[16,128,128]{2,1,0:T(8,128)(2,1)S(1)} %all-to-all-done.3.refs_0_, bf16[8,128,128]{2,1,0:T(8,128)(2,1)S(1)} %sort_d_left.1.refs_1_, bf16[8,512,128]{2,1,0:T(8,128)(2,1)S(1)} %get-tuple-element.54.refs_2_, bf16[8,128,128]{2,1,0:T(8,128)(2,1)S(1)} %gate_back.1.refs_6_.refs_3_, ...), custom_call_target="tpu_custom_call" | custom-call | flops 134217728 | bytes 2854912 | tf_op jit(solution)/shard_map/finish/pallas_call | solution.py:65
  (44 shorter events, 6.3 us)
Async XLA Ops:
  2.4 8.6 %copy-start = (bf16[16,128,128]{2,1,0:T(8,128)(2,1)S(1)}, bf16[16,128,128]{2,1,0:T(8,128)(2,1)}, u32[]{:S(2)}) copy-start(bf16[16,128,128]{2,1,0:T(8,128)(2,1)} %project_right.1.refs_5_) | copy-start | bytes 1572868
  2.4 8.6 %copy-start.1 = (bf16[8,128,128]{2,1,0:T(8,128)(2,1)S(1)}, bf16[8,128,128]{2,1,0:T(8,128)(2,1)}, u32[]{:S(2)}) copy-start(bf16[8,128,128]{2,1,0:T(8,128)(2,1)} %refs_0_.7) | copy-start | bytes 786436
  2.4 8.6 %copy-start.2 = (bf16[128,512]{1,0:T(8,128)(2,1)S(1)}, bf16[128,512]{1,0:T(8,128)(2,1)}, u32[]{:S(2)}) copy-start(bf16[128,512]{1,0:T(8,128)(2,1)} %refs_4_.9) | copy-start | bytes 393220
  2.4 8.6 %copy-start.6 = (f32[128]{0:T(128)S(1)}, f32[128]{0:T(128)}, u32[]{:S(2)}) copy-start(f32[128]{0:T(128)} %param.13) | copy-start | bytes 1540
  2.4 8.6 %copy-start.7 = (f32[128]{0:T(128)S(1)}, f32[128]{0:T(128)}, u32[]{:S(2)}) copy-start(f32[128]{0:T(128)} %param.14) | copy-start | bytes 1540
  2.5 8.6 %copy-start.8 = (s32[128]{0:T(128)S(1)}, s32[128]{0:T(128)}, u32[]{:S(2)}) copy-start(s32[128]{0:T(128)} %param.12) | copy-start | bytes 1540
  2.5 21.3 %all-to-all-start = ((bf16[16,128,128]{2,1,0:T(8,128)(2,1)}), bf16[16,128,128]{2,1,0:T(8,128)(2,1)S(1)}, u32[]{:S(2)}, u32[]{:S(2)}) async-start(bf16[16,128,128]{2,1,0:T(8,128)(2,1)} %project_right.1.refs_5_), calls=%async_computation | async-start | bytes 1048576 | tf_op jit(solution)/shard_map/all_to_all | solution.py:331
  11.0 7.4 %copy-start.3 = (bf16[8,128,128]{2,1,0:T(8,128)(2,1)S(1)}, bf16[8,128,128]{2,1,0:T(8,128)(2,1)}, u32[]{:S(2)}) copy-start(bf16[8,128,128]{2,1,0:T(8,128)(2,1)} %refs_1_.1) | copy-start | bytes 786436
  11.1 7.3 %copy-start.4 = (bf16[128,128]{1,0:T(8,128)(2,1)S(1)}, bf16[128,128]{1,0:T(8,128)(2,1)}, u32[]{:S(2)}) copy-start(bf16[128,128]{1,0:T(8,128)(2,1)} %refs_4_.8) | copy-start | bytes 98308
  11.9 3.7 %collective-permute-start = (bf16[128,128]{1,0:T(8,128)(2,1)S(1)}, bf16[128,128]{1,0:T(8,128)(2,1)S(1)}, u32[]{:S(2)}, u32[]{:S(2)}) collective-permute-start(bf16[128,128]{1,0:T(8,128)(2,1)S(1)} %get-tuple-element.33), channel_id=1, source_target_pairs={{0,1},{1,0},{2,3},{3,2},{4,5},{5,4},{6,7},{7,6},{8,9},{9,8},{10,11... | collective-permute-start | bytes 98312 | tf_op jit(solution)/shard_map/ppermute | solution.py:349
  12.1 6.3 %collective-permute-start.1 = (bf16[128,128]{1,0:T(8,128)(2,1)S(1)}, bf16[128,128]{1,0:T(8,128)(2,1)S(1)}, u32[]{:S(2)}, u32[]{:S(2)}) collective-permute-start(bf16[128,128]{1,0:T(8,128)(2,1)S(1)} %get-tuple-element.34), channel_id=1, source_target_pairs={{0,2},{1,3},{2,0},{3,1},{4,6},{5,7},{6,4},{7,5},{8,10},{9,11},{10,... | collective-permute-start | bytes 98312 | tf_op jit(solution)/shard_map/ppermute | solution.py:349
  12.7 8.6 %collective-permute-start.2 = (bf16[128,128]{1,0:T(8,128)(2,1)S(1)}, bf16[128,128]{1,0:T(8,128)(2,1)S(1)}, u32[]{:S(2)}, u32[]{:S(2)}) collective-permute-start(bf16[128,128]{1,0:T(8,128)(2,1)S(1)} %get-tuple-element.35), channel_id=1, source_target_pairs={{0,6},{1,7},{2,4},{3,5},{4,2},{5,3},{6,0},{7,1},{8,14},{9,15},{10,... | collective-permute-start | bytes 98312 | tf_op jit(solution)/shard_map/ppermute | solution.py:349
  14.1 8.0 %collective-permute-start.3 = (bf16[128,128]{1,0:T(8,128)(2,1)S(1)}, bf16[128,128]{1,0:T(8,128)(2,1)S(1)}, u32[]{:S(2)}, u32[]{:S(2)}) collective-permute-start(bf16[128,128]{1,0:T(8,128)(2,1)S(1)} %get-tuple-element.36), channel_id=1, source_target_pairs={{0,7},{1,6},{2,5},{3,4},{4,3},{5,2},{6,1},{7,0},{8,15},{9,14},{10,... | collective-permute-start | bytes 98312 | tf_op jit(solution)/shard_map/ppermute | solution.py:349
  15.0 8.6 %collective-permute-start.4 = (bf16[128,128]{1,0:T(8,128)(2,1)S(1)}, bf16[128,128]{1,0:T(8,128)(2,1)S(1)}, u32[]{:S(2)}, u32[]{:S(2)}) collective-permute-start(bf16[128,128]{1,0:T(8,128)(2,1)S(1)} %get-tuple-element.37), channel_id=1, source_target_pairs={{0,4},{1,5},{2,6},{3,7},{4,0},{5,1},{6,2},{7,3},{8,12},{9,13},{10,... | collective-permute-start | bytes 98312 | tf_op jit(solution)/shard_map/ppermute | solution.py:349
  15.6 8.0 %collective-permute-start.5 = (bf16[128,128]{1,0:T(8,128)(2,1)S(1)}, bf16[128,128]{1,0:T(8,128)(2,1)S(1)}, u32[]{:S(2)}, u32[]{:S(2)}) collective-permute-start(bf16[128,128]{1,0:T(8,128)(2,1)S(1)} %get-tuple-element.38), channel_id=1, source_target_pairs={{0,5},{1,4},{2,7},{3,6},{4,1},{5,0},{6,3},{7,2},{8,13},{9,12},{10,... | collective-permute-start | bytes 98312 | tf_op jit(solution)/shard_map/ppermute | solution.py:349
  18.4 5.2 %collective-permute-start.6 = (bf16[128,128]{1,0:T(8,128)(2,1)S(1)}, bf16[128,128]{1,0:T(8,128)(2,1)S(1)}, u32[]{:S(2)}, u32[]{:S(2)}) collective-permute-start(bf16[128,128]{1,0:T(8,128)(2,1)S(1)} %get-tuple-element.39), channel_id=1, source_target_pairs={{0,3},{1,2},{2,1},{3,0},{4,7},{5,6},{6,5},{7,4},{8,11},{9,10},{10,... | collective-permute-start | bytes 98312 | tf_op jit(solution)/shard_map/ppermute | solution.py:349
  44.5 16.8 %all-to-all-start.3 = ((bf16[16,128,128]{2,1,0:T(8,128)(2,1)}), bf16[16,128,128]{2,1,0:T(8,128)(2,1)S(1)}, u32[]{:S(2)}, u32[]{:S(2)}) async-start(bf16[16,128,128]{2,1,0:T(8,128)(2,1)} %get-tuple-element.42), calls=%async_computation.3 | async-start | bytes 1048576 | tf_op jit(solution)/shard_map/all_to_all | solution.py:331
  49.1 4.5 %collective-permute-start.7 = (bf16[128,128]{1,0:T(8,128)(2,1)S(1)}, bf16[128,128]{1,0:T(8,128)(2,1)S(1)}, u32[]{:S(2)}, u32[]{:S(2)}) collective-permute-start(bf16[128,128]{1,0:T(8,128)(2,1)S(1)} %get-tuple-element.46), channel_id=1, source_target_pairs={{0,1},{1,0},{2,3},{3,2},{4,5},{5,4},{6,7},{7,6},{8,9},{9,8},{10,11... | collective-permute-start | bytes 98312 | tf_op jit(solution)/shard_map/ppermute | solution.py:349
  49.3 7.1 %collective-permute-start.8 = (bf16[128,128]{1,0:T(8,128)(2,1)S(1)}, bf16[128,128]{1,0:T(8,128)(2,1)S(1)}, u32[]{:S(2)}, u32[]{:S(2)}) collective-permute-start(bf16[128,128]{1,0:T(8,128)(2,1)S(1)} %get-tuple-element.47), channel_id=1, source_target_pairs={{0,2},{1,3},{2,0},{3,1},{4,6},{5,7},{6,4},{7,5},{8,10},{9,11},{10,... | collective-permute-start | bytes 98312 | tf_op jit(solution)/shard_map/ppermute | solution.py:349
  50.8 8.3 %collective-permute-start.9 = (bf16[128,128]{1,0:T(8,128)(2,1)S(1)}, bf16[128,128]{1,0:T(8,128)(2,1)S(1)}, u32[]{:S(2)}, u32[]{:S(2)}) collective-permute-start(bf16[128,128]{1,0:T(8,128)(2,1)S(1)} %get-tuple-element.48), channel_id=1, source_target_pairs={{0,6},{1,7},{2,4},{3,5},{4,2},{5,3},{6,0},{7,1},{8,14},{9,15},{10,... | collective-permute-start | bytes 98312 | tf_op jit(solution)/shard_map/ppermute | solution.py:349
  51.1 8.7 %collective-permute-start.10 = (bf16[128,128]{1,0:T(8,128)(2,1)S(1)}, bf16[128,128]{1,0:T(8,128)(2,1)S(1)}, u32[]{:S(2)}, u32[]{:S(2)}) collective-permute-start(bf16[128,128]{1,0:T(8,128)(2,1)S(1)} %get-tuple-element.49), channel_id=1, source_target_pairs={{0,7},{1,6},{2,5},{3,4},{4,3},{5,2},{6,1},{7,0},{8,15},{9,14},{10,... | collective-permute-start | bytes 98312 | tf_op jit(solution)/shard_map/ppermute | solution.py:349
  53.2 7.2 %collective-permute-start.11 = (bf16[128,128]{1,0:T(8,128)(2,1)S(1)}, bf16[128,128]{1,0:T(8,128)(2,1)S(1)}, u32[]{:S(2)}, u32[]{:S(2)}) collective-permute-start(bf16[128,128]{1,0:T(8,128)(2,1)S(1)} %get-tuple-element.50), channel_id=1, source_target_pairs={{0,4},{1,5},{2,6},{3,7},{4,0},{5,1},{6,2},{7,3},{8,12},{9,13},{10,... | collective-permute-start | bytes 98312 | tf_op jit(solution)/shard_map/ppermute | solution.py:349
  53.7 7.1 %collective-permute-start.12 = (bf16[128,128]{1,0:T(8,128)(2,1)S(1)}, bf16[128,128]{1,0:T(8,128)(2,1)S(1)}, u32[]{:S(2)}, u32[]{:S(2)}) collective-permute-start(bf16[128,128]{1,0:T(8,128)(2,1)S(1)} %get-tuple-element.51), channel_id=1, source_target_pairs={{0,5},{1,4},{2,7},{3,6},{4,1},{5,0},{6,3},{7,2},{8,13},{9,12},{10,... | collective-permute-start | bytes 98312 | tf_op jit(solution)/shard_map/ppermute | solution.py:349
  56.4 4.3 %collective-permute-start.13 = (bf16[128,128]{1,0:T(8,128)(2,1)S(1)}, bf16[128,128]{1,0:T(8,128)(2,1)S(1)}, u32[]{:S(2)}, u32[]{:S(2)}) collective-permute-start(bf16[128,128]{1,0:T(8,128)(2,1)S(1)} %get-tuple-element.52), channel_id=1, source_target_pairs={{0,3},{1,2},{2,1},{3,0},{4,7},{5,6},{6,5},{7,4},{8,11},{9,10},{10,... | collective-permute-start | bytes 98312 | tf_op jit(solution)/shard_map/ppermute | solution.py:349
  (3 other events, 8.7 us)

commit v20 on v19

--- a/solution.py
+++ b/solution.py
@@ -102,7 +102,7 @@
 
 
 def half_order(count):
-    return [*range(0, count, 2), *range(1, count, 2)]
+    return [place + plane for place in range(count // 2) for plane in (0, count // 2)]
 
 
 def distance(step, count):

time: 63.1 us -> 63 us (level)
  no operation moved by 1% of the time
where the time goes in v20:
time: 63 us; the launch traced here: 62.5 us
  starting transfers between devices  24.3 us (39%)
  blocking collectives  18 us (29%)
  Pallas kernels  9.82 us (16%)
  waiting for transfers between devices  8.85 us (14%)
  local copies, waits for them, and re-layouts  1.34 us (2%)
    all_to_all x2, blocking collectives, swap_half(): lax.all_to_all(values, 'row', split_axis=0, concat_axis=0, tiled=True, ax...  18 us
    all_to_all x2, starting transfers between devices, swap(): lax.all_to_all(values, 'row', split_axis=0, concat_axis=0, tiled=True, ax...  13 us
    ppermute x14, starting transfers between devices, swap_pieces(): lax.ppermute(pieces[step], 'row', [(d, d ^ distance(step, count)) for d i...  11.3 us
    pallas_call x12, Pallas kernels, call(): pl.pallas_call(body, name=name, out_shape=outs, in_specs=[pl.BlockSpec(me...  9.82 us
    ppermute x14, waiting for transfers between devices, swap_pieces(): lax.ppermute(pieces[step], 'row', [(d, d ^ distance(step, count)) for d i...  8.39 us
    unnamed x22, local copies, waits for them, and re-layouts  1.34 us
  transfers between devices with their start and end apart: 16, of which 10 were waited for; matrix products, arithmetic and copies ran while one was open for 0% of the time, Pallas kernels for 6%

profile of v20, /device:TPU:0, one launch (start us, length us, event | category | flops | bytes accessed | tf_op | source)
XLA Modules:
  0.0 62.5 jit_solution(10290000708731261623)
XLA Ops:
  0.0 2.4 %project_right.1.refs_5_ = bf16[16,128,128]{2,1,0:T(8,128)(2,1)} custom-call(bf16[8,128,128]{2,1,0:T(8,128)(2,1)} %refs_0_.7, s32[1,128]{1,0:T(1,128)} %bitcast.13, f32[1,128]{1,0:T(1,128)} %bitcast.5, f32[1,128]{1,0:T(1,128)} %bitcast.9, bf16[128,512]{1,0:T(8,128)(2,1)} %refs_4_.9), custom_call_target="tpu_custom_call" | custom-call | flops 67108864 | bytes 919040 | tf_op jit(solution)/shard_map/project_right/pallas_call | solution.py:65
  2.5 8.5 %all-to-all-start = ((bf16[16,128,128]{2,1,0:T(8,128)(2,1)}), bf16[16,128,128]{2,1,0:T(8,128)(2,1)S(1)}, u32[]{:S(2)}, u32[]{:S(2)}) async-start(bf16[16,128,128]{2,1,0:T(8,128)(2,1)} %project_right.1.refs_5_), calls=%async_computation | async-start | bytes 1048576 | tf_op jit(solution)/shard_map/all_to_all | solution.py:331
  11.1 0.8 %project_left.1 = (bf16[128,128]{1,0:T(8,128)(2,1)S(1)}, bf16[128,128]{1,0:T(8,128)(2,1)S(1)}, bf16[128,128]{1,0:T(8,128)(2,1)S(1)}, bf16[128,128]{1,0:T(8,128)(...) custom-call(bf16[8,128,128]{2,1,0:T(8,128)(2,1)S(1)} %copy-done.1, ...), custom_call_target="tpu_custom_call" | custom-call | flops 67108864 | bytes 1181184 | tf_op jit(solution)/shard_map/project_left/pallas_call | solution.py:65
  12.7 1.4 %collective-permute-start.2 = (bf16[128,128]{1,0:T(8,128)(2,1)S(1)}, bf16[128,128]{1,0:T(8,128)(2,1)S(1)}, u32[]{:S(2)}, u32[]{:S(2)}) collective-permute-start(bf16[128,128]{1,0:T(8,128)(2,1)S(1)} %get-tuple-element.35), channel_id=1, source_target_pairs={{0,6},{1,7},{2,4},{3,5},{4,2},{5,3},{6,0},{7,1},{8,14},{9,15},{10,... | collective-permute-start | bytes 98312 | tf_op jit(solution)/shard_map/ppermute | solution.py:349
  14.1 0.9 %collective-permute-start.3 = (bf16[128,128]{1,0:T(8,128)(2,1)S(1)}, bf16[128,128]{1,0:T(8,128)(2,1)S(1)}, u32[]{:S(2)}, u32[]{:S(2)}) collective-permute-start(bf16[128,128]{1,0:T(8,128)(2,1)S(1)} %get-tuple-element.36), channel_id=1, source_target_pairs={{0,7},{1,6},{2,5},{3,4},{4,3},{5,2},{6,1},{7,0},{8,15},{9,14},{10,... | collective-permute-start | bytes 98312 | tf_op jit(solution)/shard_map/ppermute | solution.py:349
  15.6 1.5 %collective-permute-start.5 = (bf16[128,128]{1,0:T(8,128)(2,1)S(1)}, bf16[128,128]{1,0:T(8,128)(2,1)S(1)}, u32[]{:S(2)}, u32[]{:S(2)}) collective-permute-start(bf16[128,128]{1,0:T(8,128)(2,1)S(1)} %get-tuple-element.38), channel_id=1, source_target_pairs={{0,5},{1,4},{2,7},{3,6},{4,1},{5,0},{6,3},{7,2},{8,13},{9,12},{10,... | collective-permute-start | bytes 98312 | tf_op jit(solution)/shard_map/ppermute | solution.py:349
  17.1 1.3 %collective-permute-done.1.refs_2_ = bf16[128,128]{1,0:T(8,128)(2,1)S(1)} collective-permute-done((bf16[128,128]{1,0:T(8,128)(2,1)S(1)}, bf16[128,128]{1,0:T(8,128)(2,1)S(1)}, u32[]{:S(2)}, u32[]{:S(2)}) %collective-permute-start.1) | collective-permute-done | bytes 32800 | tf_op jit(solution)/shard_map/ppermute | solution.py:349
  19.1 0.8 %prepare.1 = (f32[8,128,128]{2,1,0:T(8,128)S(1)}, f32[8,128,128]{2,1,0:T(8,128)S(1)}) custom-call(bf16[8,128,128]{2,1,0:T(8,128)(2,1)S(1)} %copy-done.1, bf16[8,128,128]{2,1,0:T(8,128)(2,1)S(1)} %copy-done.3, f32[1,128]{1,0:T(1,128)S(1)} %bitcast.7, f32[1,128]{1,0:T(1,128)S(1)} %bitcast.11, bf16[128,128]{1,0:T(8,128)(2,1)S(1)} %copy-done.5, ...), custom_call_target="tpu_custom_call" | custom-call | flops 67108864 | bytes 1639936 | tf_op jit(solution)/shard_map/prepare/pallas_call | solution.py:65
  19.9 1.5 %collective-permute-done.2.refs_3_ = bf16[128,128]{1,0:T(8,128)(2,1)S(1)} collective-permute-done((bf16[128,128]{1,0:T(8,128)(2,1)S(1)}, bf16[128,128]{1,0:T(8,128)(2,1)S(1)}, u32[]{:S(2)}, u32[]{:S(2)}) %collective-permute-start.2) | collective-permute-done | bytes 32800 | tf_op jit(solution)/shard_map/ppermute | solution.py:349
  21.3 0.7 %collective-permute-done.3.refs_4_ = bf16[128,128]{1,0:T(8,128)(2,1)S(1)} collective-permute-done((bf16[128,128]{1,0:T(8,128)(2,1)S(1)}, bf16[128,128]{1,0:T(8,128)(2,1)S(1)}, u32[]{:S(2)}, u32[]{:S(2)}) %collective-permute-start.3) | collective-permute-done | bytes 32800 | tf_op jit(solution)/shard_map/ppermute | solution.py:349
  22.0 1.5 %collective-permute-done.4.refs_5_ = bf16[128,128]{1,0:T(8,128)(2,1)S(1)} collective-permute-done((bf16[128,128]{1,0:T(8,128)(2,1)S(1)}, bf16[128,128]{1,0:T(8,128)(2,1)S(1)}, u32[]{:S(2)}, u32[]{:S(2)}) %collective-permute-start.4) | collective-permute-done | bytes 32800 | tf_op jit(solution)/shard_map/ppermute | solution.py:349
  23.8 0.6 %tri.1 = (bf16[8,128,128]{2,1,0:T(8,128)(2,1)S(1)}, bf16[16,128,128]{2,1,0:T(8,128)(2,1)S(1)}) custom-call(bf16[16,128,128]{2,1,0:T(8,128)(2,1)S(1)} %all-to-all-done.refs_0_, bf16[16,64,128]{2,1,0:T(8,128)(2,1)S(1)} %sort_left.1.refs_1_, f32[8,128,128]{2,1,0:T(8,128)S(1)} %get-tuple-element.40.refs_2_.refs_1_), custom_call_target="tpu_custom_call" | custom-call | flops 33554432 | bytes 2097152 | tf_op jit(solution)/shard_map/tri/pallas_call | solution.py:65
  24.5 9.1 %all_to_all.20.refs_0_ = bf16[8,128,128]{2,1,0:T(8,128)(2,1)S(1)} all-to-all(bf16[8,128,128]{2,1,0:T(8,128)(2,1)S(1)} %get-tuple-element.41), channel_id=1, replica_groups={{0,4,1,5,2,6,3,7},{8,12,9,13,10,14,11,15},{16,20,17,21,18,22,19,23},{24..., dimensions={0} | all-to-all | bytes 524288 | tf_op jit(solution)/shard_map/all_to_all | solution.py:340
  33.9 8.9 %all_to_all.21.refs_0_ = bf16[8,128,128]{2,1,0:T(8,128)(2,1)S(1)} all-to-all(bf16[8,128,128]{2,1,0:T(8,128)(2,1)S(1)} %middle.1), channel_id=1, replica_groups={{0,4,1,5,2,6,3,7},{8,12,9,13,10,14,11,15},{16,20,17,21,18,22,19,23},{24..., dimensions={0} | all-to-all | bytes 524288 | tf_op jit(solution)/shard_map/all_to_all | solution.py:340
  42.7 1.5 %d_right.1 = (bf16[16,128,128]{2,1,0:T(8,128)(2,1)}, bf16[16,64,128]{2,1,0:T(8,128)(2,1)S(1)}) custom-call(bf16[8,128,128]{2,1,0:T(8,128)(2,1)S(1)} %all_to_all.21.refs_0_, bf16[16,64,128]{2,1,0:T(8,128)(2,1)S(1)} %sort_left.1.refs_1_), custom_call_target="tpu_custom_call" | custom-call | flops 33554432 | bytes 1310720 | tf_op jit(solution)/shard_map/d_right/pallas_call | solution.py:65
  44.2 4.5 %all-to-all-start.3 = ((bf16[16,128,128]{2,1,0:T(8,128)(2,1)}), bf16[16,128,128]{2,1,0:T(8,128)(2,1)S(1)}, u32[]{:S(2)}, u32[]{:S(2)}) async-start(bf16[16,128,128]{2,1,0:T(8,128)(2,1)} %get-tuple-element.42), calls=%async_computation.3 | async-start | bytes 1048576 | tf_op jit(solution)/shard_map/all_to_all | solution.py:331
  49.2 1.5 %collective-permute-start.8 = (bf16[128,128]{1,0:T(8,128)(2,1)S(1)}, bf16[128,128]{1,0:T(8,128)(2,1)S(1)}, u32[]{:S(2)}, u32[]{:S(2)}) collective-permute-start(bf16[128,128]{1,0:T(8,128)(2,1)S(1)} %get-tuple-element.47), channel_id=1, source_target_pairs={{0,2},{1,3},{2,0},{3,1},{4,6},{5,7},{6,4},{7,5},{8,10},{9,11},{10,... | collective-permute-start | bytes 98312 | tf_op jit(solution)/shard_map/ppermute | solution.py:349
  51.0 2.0 %collective-permute-start.10 = (bf16[128,128]{1,0:T(8,128)(2,1)S(1)}, bf16[128,128]{1,0:T(8,128)(2,1)S(1)}, u32[]{:S(2)}, u32[]{:S(2)}) collective-permute-start(bf16[128,128]{1,0:T(8,128)(2,1)S(1)} %get-tuple-element.49), channel_id=1, source_target_pairs={{0,7},{1,6},{2,5},{3,4},{4,3},{5,2},{6,1},{7,0},{8,15},{9,14},{10,... | collective-permute-start | bytes 98312 | tf_op jit(solution)/shard_map/ppermute | solution.py:349
  53.5 1.6 %collective-permute-start.12 = (bf16[128,128]{1,0:T(8,128)(2,1)S(1)}, bf16[128,128]{1,0:T(8,128)(2,1)S(1)}, u32[]{:S(2)}, u32[]{:S(2)}) collective-permute-start(bf16[128,128]{1,0:T(8,128)(2,1)S(1)} %get-tuple-element.51), channel_id=1, source_target_pairs={{0,5},{1,4},{2,7},{3,6},{4,1},{5,0},{6,3},{7,2},{8,13},{9,12},{10,... | collective-permute-start | bytes 98312 | tf_op jit(solution)/shard_map/ppermute | solution.py:349
  55.1 1.2 %collective-permute-done.8.refs_2_ = bf16[128,128]{1,0:T(8,128)(2,1)S(1)} collective-permute-done((bf16[128,128]{1,0:T(8,128)(2,1)S(1)}, bf16[128,128]{1,0:T(8,128)(2,1)S(1)}, u32[]{:S(2)}, u32[]{:S(2)}) %collective-permute-start.8) | collective-permute-done | bytes 32800 | tf_op jit(solution)/shard_map/ppermute | solution.py:349
  56.3 0.7 %copy-done.10 = f32[128]{0:T(128)S(1)} copy-done((f32[128]{0:T(128)S(1)}, f32[128]{0:T(128)}, u32[]{:S(2)}) %copy-start.10) | copy-done | bytes 536
  57.4 1.0 %slopes.1 = (bf16[8,512,128]{2,1,0:T(8,128)(2,1)S(1)}, bf16[8,128,128]{2,1,0:T(8,128)(2,1)S(1)}, f32[8,128]{1,0:T(8,128)S(1)}, f32[128,128]{1,0:T(8,128)S(1)}, bf16[128,640]{1,0:T(8,128)(2,1)S(1)}) custom-call(bf16[8,128,128]{2,1,0:T(8,128)(2,1)S(1)} %copy-done.1, s32[1,128]{1,0:T(1,128)S(1)} %bitcast.15, f32[1,128]{1,0:T(1,128)S(1)} %bitcast.8, ...), custom_call_target="tpu_custom_call" | custom-call | flops 134217728 | bytes 2233856 | tf_op jit(solution)/shard_map/slopes/pallas_call | solution.py:65
  59.0 0.7 %collective-permute-done.10.refs_4_ = bf16[128,128]{1,0:T(8,128)(2,1)S(1)} collective-permute-done((bf16[128,128]{1,0:T(8,128)(2,1)S(1)}, bf16[128,128]{1,0:T(8,128)(2,1)S(1)}, u32[]{:S(2)}, u32[]{:S(2)}) %collective-permute-start.10) | collective-permute-done | bytes 32800 | tf_op jit(solution)/shard_map/ppermute | solution.py:349
  61.1 1.4 %finish.1 = bf16[8,128,128]{2,1,0:T(8,128)(2,1)} custom-call(bf16[16,128,128]{2,1,0:T(8,128)(2,1)S(1)} %all-to-all-done.3.refs_0_, bf16[8,128,128]{2,1,0:T(8,128)(2,1)S(1)} %sort_d_left.1.refs_1_, bf16[8,512,128]{2,1,0:T(8,128)(2,1)S(1)} %get-tuple-element.54.refs_2_, bf16[8,128,128]{2,1,0:T(8,128)(2,1)S(1)} %gate_back.1.refs_6_.refs_3_, ...), custom_call_target="tpu_custom_call" | custom-call | flops 134217728 | bytes 2854912 | tf_op jit(solution)/shard_map/finish/pallas_call | solution.py:65
  (44 shorter events, 6.3 us)
Async XLA Ops:
  2.4 8.6 %copy-start = (bf16[16,128,128]{2,1,0:T(8,128)(2,1)S(1)}, bf16[16,128,128]{2,1,0:T(8,128)(2,1)}, u32[]{:S(2)}) copy-start(bf16[16,128,128]{2,1,0:T(8,128)(2,1)} %project_right.1.refs_5_) | copy-start | bytes 1572868
  2.4 8.6 %copy-start.1 = (bf16[8,128,128]{2,1,0:T(8,128)(2,1)S(1)}, bf16[8,128,128]{2,1,0:T(8,128)(2,1)}, u32[]{:S(2)}) copy-start(bf16[8,128,128]{2,1,0:T(8,128)(2,1)} %refs_0_.7) | copy-start | bytes 786436
  2.4 8.6 %copy-start.2 = (bf16[128,512]{1,0:T(8,128)(2,1)S(1)}, bf16[128,512]{1,0:T(8,128)(2,1)}, u32[]{:S(2)}) copy-start(bf16[128,512]{1,0:T(8,128)(2,1)} %refs_4_.9) | copy-start | bytes 393220
  2.4 8.6 %copy-start.6 = (f32[128]{0:T(128)S(1)}, f32[128]{0:T(128)}, u32[]{:S(2)}) copy-start(f32[128]{0:T(128)} %param.13) | copy-start | bytes 1540
  2.4 8.6 %copy-start.7 = (f32[128]{0:T(128)S(1)}, f32[128]{0:T(128)}, u32[]{:S(2)}) copy-start(f32[128]{0:T(128)} %param.14) | copy-start | bytes 1540
  2.5 8.6 %copy-start.8 = (s32[128]{0:T(128)S(1)}, s32[128]{0:T(128)}, u32[]{:S(2)}) copy-start(s32[128]{0:T(128)} %param.12) | copy-start | bytes 1540
  2.5 21.3 %all-to-all-start = ((bf16[16,128,128]{2,1,0:T(8,128)(2,1)}), bf16[16,128,128]{2,1,0:T(8,128)(2,1)S(1)}, u32[]{:S(2)}, u32[]{:S(2)}) async-start(bf16[16,128,128]{2,1,0:T(8,128)(2,1)} %project_right.1.refs_5_), calls=%async_computation | async-start | bytes 1048576 | tf_op jit(solution)/shard_map/all_to_all | solution.py:331
  11.0 7.4 %copy-start.3 = (bf16[8,128,128]{2,1,0:T(8,128)(2,1)S(1)}, bf16[8,128,128]{2,1,0:T(8,128)(2,1)}, u32[]{:S(2)}) copy-start(bf16[8,128,128]{2,1,0:T(8,128)(2,1)} %refs_1_.1) | copy-start | bytes 786436
  11.1 7.3 %copy-start.4 = (bf16[128,128]{1,0:T(8,128)(2,1)S(1)}, bf16[128,128]{1,0:T(8,128)(2,1)}, u32[]{:S(2)}) copy-start(bf16[128,128]{1,0:T(8,128)(2,1)} %refs_4_.8) | copy-start | bytes 98308
  11.9 3.7 %collective-permute-start = (bf16[128,128]{1,0:T(8,128)(2,1)S(1)}, bf16[128,128]{1,0:T(8,128)(2,1)S(1)}, u32[]{:S(2)}, u32[]{:S(2)}) collective-permute-start(bf16[128,128]{1,0:T(8,128)(2,1)S(1)} %get-tuple-element.33), channel_id=1, source_target_pairs={{0,1},{1,0},{2,3},{3,2},{4,5},{5,4},{6,7},{7,6},{8,9},{9,8},{10,11... | collective-permute-start | bytes 98312 | tf_op jit(solution)/shard_map/ppermute | solution.py:349
  12.1 6.3 %collective-permute-start.1 = (bf16[128,128]{1,0:T(8,128)(2,1)S(1)}, bf16[128,128]{1,0:T(8,128)(2,1)S(1)}, u32[]{:S(2)}, u32[]{:S(2)}) collective-permute-start(bf16[128,128]{1,0:T(8,128)(2,1)S(1)} %get-tuple-element.34), channel_id=1, source_target_pairs={{0,2},{1,3},{2,0},{3,1},{4,6},{5,7},{6,4},{7,5},{8,10},{9,11},{10,... | collective-permute-start | bytes 98312 | tf_op jit(solution)/shard_map/ppermute | solution.py:349
  12.7 8.6 %collective-permute-start.2 = (bf16[128,128]{1,0:T(8,128)(2,1)S(1)}, bf16[128,128]{1,0:T(8,128)(2,1)S(1)}, u32[]{:S(2)}, u32[]{:S(2)}) collective-permute-start(bf16[128,128]{1,0:T(8,128)(2,1)S(1)} %get-tuple-element.35), channel_id=1, source_target_pairs={{0,6},{1,7},{2,4},{3,5},{4,2},{5,3},{6,0},{7,1},{8,14},{9,15},{10,... | collective-permute-start | bytes 98312 | tf_op jit(solution)/shard_map/ppermute | solution.py:349
  14.1 8.0 %collective-permute-start.3 = (bf16[128,128]{1,0:T(8,128)(2,1)S(1)}, bf16[128,128]{1,0:T(8,128)(2,1)S(1)}, u32[]{:S(2)}, u32[]{:S(2)}) collective-permute-start(bf16[128,128]{1,0:T(8,128)(2,1)S(1)} %get-tuple-element.36), channel_id=1, source_target_pairs={{0,7},{1,6},{2,5},{3,4},{4,3},{5,2},{6,1},{7,0},{8,15},{9,14},{10,... | collective-permute-start | bytes 98312 | tf_op jit(solution)/shard_map/ppermute | solution.py:349
  15.0 8.6 %collective-permute-start.4 = (bf16[128,128]{1,0:T(8,128)(2,1)S(1)}, bf16[128,128]{1,0:T(8,128)(2,1)S(1)}, u32[]{:S(2)}, u32[]{:S(2)}) collective-permute-start(bf16[128,128]{1,0:T(8,128)(2,1)S(1)} %get-tuple-element.37), channel_id=1, source_target_pairs={{0,4},{1,5},{2,6},{3,7},{4,0},{5,1},{6,2},{7,3},{8,12},{9,13},{10,... | collective-permute-start | bytes 98312 | tf_op jit(solution)/shard_map/ppermute | solution.py:349
  15.6 8.0 %collective-permute-start.5 = (bf16[128,128]{1,0:T(8,128)(2,1)S(1)}, bf16[128,128]{1,0:T(8,128)(2,1)S(1)}, u32[]{:S(2)}, u32[]{:S(2)}) collective-permute-start(bf16[128,128]{1,0:T(8,128)(2,1)S(1)} %get-tuple-element.38), channel_id=1, source_target_pairs={{0,5},{1,4},{2,7},{3,6},{4,1},{5,0},{6,3},{7,2},{8,13},{9,12},{10,... | collective-permute-start | bytes 98312 | tf_op jit(solution)/shard_map/ppermute | solution.py:349
  18.4 5.2 %collective-permute-start.6 = (bf16[128,128]{1,0:T(8,128)(2,1)S(1)}, bf16[128,128]{1,0:T(8,128)(2,1)S(1)}, u32[]{:S(2)}, u32[]{:S(2)}) collective-permute-start(bf16[128,128]{1,0:T(8,128)(2,1)S(1)} %get-tuple-element.39), channel_id=1, source_target_pairs={{0,3},{1,2},{2,1},{3,0},{4,7},{5,6},{6,5},{7,4},{8,11},{9,10},{10,... | collective-permute-start | bytes 98312 | tf_op jit(solution)/shard_map/ppermute | solution.py:349
  44.2 16.9 %all-to-all-start.3 = ((bf16[16,128,128]{2,1,0:T(8,128)(2,1)}), bf16[16,128,128]{2,1,0:T(8,128)(2,1)S(1)}, u32[]{:S(2)}, u32[]{:S(2)}) async-start(bf16[16,128,128]{2,1,0:T(8,128)(2,1)} %get-tuple-element.42), calls=%async_computation.3 | async-start | bytes 1048576 | tf_op jit(solution)/shard_map/all_to_all | solution.py:331
  49.0 4.5 %collective-permute-start.7 = (bf16[128,128]{1,0:T(8,128)(2,1)S(1)}, bf16[128,128]{1,0:T(8,128)(2,1)S(1)}, u32[]{:S(2)}, u32[]{:S(2)}) collective-permute-start(bf16[128,128]{1,0:T(8,128)(2,1)S(1)} %get-tuple-element.46), channel_id=1, source_target_pairs={{0,1},{1,0},{2,3},{3,2},{4,5},{5,4},{6,7},{7,6},{8,9},{9,8},{10,11... | collective-permute-start | bytes 98312 | tf_op jit(solution)/shard_map/ppermute | solution.py:349
  49.2 7.1 %collective-permute-start.8 = (bf16[128,128]{1,0:T(8,128)(2,1)S(1)}, bf16[128,128]{1,0:T(8,128)(2,1)S(1)}, u32[]{:S(2)}, u32[]{:S(2)}) collective-permute-start(bf16[128,128]{1,0:T(8,128)(2,1)S(1)} %get-tuple-element.47), channel_id=1, source_target_pairs={{0,2},{1,3},{2,0},{3,1},{4,6},{5,7},{6,4},{7,5},{8,10},{9,11},{10,... | collective-permute-start | bytes 98312 | tf_op jit(solution)/shard_map/ppermute | solution.py:349
  50.7 8.3 %collective-permute-start.9 = (bf16[128,128]{1,0:T(8,128)(2,1)S(1)}, bf16[128,128]{1,0:T(8,128)(2,1)S(1)}, u32[]{:S(2)}, u32[]{:S(2)}) collective-permute-start(bf16[128,128]{1,0:T(8,128)(2,1)S(1)} %get-tuple-element.48), channel_id=1, source_target_pairs={{0,6},{1,7},{2,4},{3,5},{4,2},{5,3},{6,0},{7,1},{8,14},{9,15},{10,... | collective-permute-start | bytes 98312 | tf_op jit(solution)/shard_map/ppermute | solution.py:349
  51.0 8.7 %collective-permute-start.10 = (bf16[128,128]{1,0:T(8,128)(2,1)S(1)}, bf16[128,128]{1,0:T(8,128)(2,1)S(1)}, u32[]{:S(2)}, u32[]{:S(2)}) collective-permute-start(bf16[128,128]{1,0:T(8,128)(2,1)S(1)} %get-tuple-element.49), channel_id=1, source_target_pairs={{0,7},{1,6},{2,5},{3,4},{4,3},{5,2},{6,1},{7,0},{8,15},{9,14},{10,... | collective-permute-start | bytes 98312 | tf_op jit(solution)/shard_map/ppermute | solution.py:349
  53.0 7.2 %collective-permute-start.11 = (bf16[128,128]{1,0:T(8,128)(2,1)S(1)}, bf16[128,128]{1,0:T(8,128)(2,1)S(1)}, u32[]{:S(2)}, u32[]{:S(2)}) collective-permute-start(bf16[128,128]{1,0:T(8,128)(2,1)S(1)} %get-tuple-element.50), channel_id=1, source_target_pairs={{0,4},{1,5},{2,6},{3,7},{4,0},{5,1},{6,2},{7,3},{8,12},{9,13},{10,... | collective-permute-start | bytes 98312 | tf_op jit(solution)/shard_map/ppermute | solution.py:349
  53.5 7.1 %collective-permute-start.12 = (bf16[128,128]{1,0:T(8,128)(2,1)S(1)}, bf16[128,128]{1,0:T(8,128)(2,1)S(1)}, u32[]{:S(2)}, u32[]{:S(2)}) collective-permute-start(bf16[128,128]{1,0:T(8,128)(2,1)S(1)} %get-tuple-element.51), channel_id=1, source_target_pairs={{0,5},{1,4},{2,7},{3,6},{4,1},{5,0},{6,3},{7,2},{8,13},{9,12},{10,... | collective-permute-start | bytes 98312 | tf_op jit(solution)/shard_map/ppermute | solution.py:349
  56.3 4.3 %collective-permute-start.13 = (bf16[128,128]{1,0:T(8,128)(2,1)S(1)}, bf16[128,128]{1,0:T(8,128)(2,1)S(1)}, u32[]{:S(2)}, u32[]{:S(2)}) collective-permute-start(bf16[128,128]{1,0:T(8,128)(2,1)S(1)} %get-tuple-element.52), channel_id=1, source_target_pairs={{0,3},{1,2},{2,1},{3,0},{4,7},{5,6},{6,5},{7,4},{8,11},{9,10},{10,... | collective-permute-start | bytes 98312 | tf_op jit(solution)/shard_map/ppermute | solution.py:349
  (3 other events, 8.7 us)

commit v21 on v16

--- a/solution.py
+++ b/solution.py
@@ -92,13 +92,8 @@
 
 
 def wide_order(devices, count, back):
-    order = []
-    for place in range(count):
-        if back:
-            order += [place ^ (count // 2), count + place]
-        else:
-            order += [count + (place ^ 2), place ^ (count // 2)]
-    return order
+    first = count // 2 if back else count
+    return [(first + n) % devices for n in range(devices)]
 
 
 def distance(step, count):

time: 62.7 us -> 64.1 us (1.022)
  blocking collectives: 17.3 us -> 18.1 us
    ppermute x14, starting transfers between devices: 11.3 us -> 12.4 us  [swap_pieces(): lax.ppermute(pieces[step], 'row', [(d, d ^ distance(step, count)) for d i...]
    all_to_all x2, waiting for transfers between devices: 0.45 us -> 1.35 us  [swap(): lax.all_to_all(values, 'row', split_axis=0, concat_axis=0, tiled=True, ax...]
    all_to_all x2, blocking collectives: 17.3 us -> 18.1 us  [swap_half(): lax.all_to_all(values, 'row', split_axis=0, concat_axis=0, tiled=True, ax...]
where the time goes in v21:
time: 64.1 us; the launch traced here: 63.6 us
  starting transfers between devices  25.3 us (39%)
  blocking collectives  18.1 us (28%)
  Pallas kernels  9.82 us (15%)
  waiting for transfers between devices  9.11 us (14%)
  local copies, waits for them, and re-layouts  1.12 us (2%)
    all_to_all x2, blocking collectives, swap_half(): lax.all_to_all(values, 'row', split_axis=0, concat_axis=0, tiled=True, ax...  18.1 us
    all_to_all x2, starting transfers between devices, swap(): lax.all_to_all(values, 'row', split_axis=0, concat_axis=0, tiled=True, ax...  12.9 us
    ppermute x14, starting transfers between devices, swap_pieces(): lax.ppermute(pieces[step], 'row', [(d, d ^ distance(step, count)) for d i...  12.4 us
    pallas_call x12, Pallas kernels, call(): pl.pallas_call(body, name=name, out_shape=outs, in_specs=[pl.BlockSpec(me...  9.82 us
    ppermute x14, waiting for transfers between devices, swap_pieces(): lax.ppermute(pieces[step], 'row', [(d, d ^ distance(step, count)) for d i...  7.76 us
    all_to_all x2, waiting for transfers between devices, swap(): lax.all_to_all(values, 'row', split_axis=0, concat_axis=0, tiled=True, ax...  1.35 us
  transfers between devices with their start and end apart: 16, of which 10 were waited for; matrix products, arithmetic and copies ran while one was open for 0% of the time, Pallas kernels for 6%

profile of v21, /device:TPU:0, one launch (start us, length us, event | category | flops | bytes accessed | tf_op | source)
XLA Modules:
  0.0 63.6 jit_solution(518559972897370594)
XLA Ops:
  0.0 2.4 %project_right.1.refs_5_ = bf16[16,128,128]{2,1,0:T(8,128)(2,1)} custom-call(bf16[8,128,128]{2,1,0:T(8,128)(2,1)} %refs_0_.7, s32[1,128]{1,0:T(1,128)} %bitcast.13, f32[1,128]{1,0:T(1,128)} %bitcast.5, f32[1,128]{1,0:T(1,128)} %bitcast.9, bf16[128,512]{1,0:T(8,128)(2,1)} %refs_4_.9), custom_call_target="tpu_custom_call" | custom-call | flops 67108864 | bytes 919040 | tf_op jit(solution)/shard_map/project_right/pallas_call | solution.py:65
  2.5 8.0 %all-to-all-start = ((bf16[16,128,128]{2,1,0:T(8,128)(2,1)}), bf16[16,128,128]{2,1,0:T(8,128)(2,1)S(1)}, u32[]{:S(2)}, u32[]{:S(2)}) async-start(bf16[16,128,128]{2,1,0:T(8,128)(2,1)} %project_right.1.refs_5_), calls=%async_computation | async-start | bytes 1048576 | tf_op jit(solution)/shard_map/all_to_all | solution.py:314
  10.5 0.8 %project_left.1 = (bf16[128,128]{1,0:T(8,128)(2,1)S(1)}, bf16[128,128]{1,0:T(8,128)(2,1)S(1)}, bf16[128,128]{1,0:T(8,128)(2,1)S(1)}, bf16[128,128]{1,0:T(8,128)(...) custom-call(bf16[8,128,128]{2,1,0:T(8,128)(2,1)S(1)} %copy-done.1, ...), custom_call_target="tpu_custom_call" | custom-call | flops 67108864 | bytes 1181184 | tf_op jit(solution)/shard_map/project_left/pallas_call | solution.py:65
  11.5 1.5 %collective-permute-start.1 = (bf16[128,128]{1,0:T(8,128)(2,1)S(1)}, bf16[128,128]{1,0:T(8,128)(2,1)S(1)}, u32[]{:S(2)}, u32[]{:S(2)}) collective-permute-start(bf16[128,128]{1,0:T(8,128)(2,1)S(1)} %get-tuple-element.34), channel_id=1, source_target_pairs={{0,2},{1,3},{2,0},{3,1},{4,6},{5,7},{6,4},{7,5},{8,10},{9,11},{10,... | collective-permute-start | bytes 98312 | tf_op jit(solution)/shard_map/ppermute | solution.py:331
  13.6 1.8 %collective-permute-start.3 = (bf16[128,128]{1,0:T(8,128)(2,1)S(1)}, bf16[128,128]{1,0:T(8,128)(2,1)S(1)}, u32[]{:S(2)}, u32[]{:S(2)}) collective-permute-start(bf16[128,128]{1,0:T(8,128)(2,1)S(1)} %get-tuple-element.36), channel_id=1, source_target_pairs={{0,7},{1,6},{2,5},{3,4},{4,3},{5,2},{6,1},{7,0},{8,15},{9,14},{10,... | collective-permute-start | bytes 98312 | tf_op jit(solution)/shard_map/ppermute | solution.py:331
  15.9 1.5 %collective-permute-start.5 = (bf16[128,128]{1,0:T(8,128)(2,1)S(1)}, bf16[128,128]{1,0:T(8,128)(2,1)S(1)}, u32[]{:S(2)}, u32[]{:S(2)}) collective-permute-start(bf16[128,128]{1,0:T(8,128)(2,1)S(1)} %get-tuple-element.38), channel_id=1, source_target_pairs={{0,5},{1,4},{2,7},{3,6},{4,1},{5,0},{6,3},{7,2},{8,13},{9,12},{10,... | collective-permute-start | bytes 98312 | tf_op jit(solution)/shard_map/ppermute | solution.py:331
  18.1 0.8 %prepare.1 = (f32[8,128,128]{2,1,0:T(8,128)S(1)}, f32[8,128,128]{2,1,0:T(8,128)S(1)}) custom-call(bf16[8,128,128]{2,1,0:T(8,128)(2,1)S(1)} %copy-done.1, bf16[8,128,128]{2,1,0:T(8,128)(2,1)S(1)} %copy-done.3, f32[1,128]{1,0:T(1,128)S(1)} %bitcast.7, f32[1,128]{1,0:T(1,128)S(1)} %bitcast.11, bf16[128,128]{1,0:T(8,128)(2,1)S(1)} %copy-done.5, ...), custom_call_target="tpu_custom_call" | custom-call | flops 67108864 | bytes 1639936 | tf_op jit(solution)/shard_map/prepare/pallas_call | solution.py:65
  18.9 2.0 %collective-permute-done.2.refs_3_ = bf16[128,128]{1,0:T(8,128)(2,1)S(1)} collective-permute-done((bf16[128,128]{1,0:T(8,128)(2,1)S(1)}, bf16[128,128]{1,0:T(8,128)(2,1)S(1)}, u32[]{:S(2)}, u32[]{:S(2)}) %collective-permute-start.2) | collective-permute-done | bytes 32800 | tf_op jit(solution)/shard_map/ppermute | solution.py:331
  20.9 0.7 %collective-permute-done.3.refs_4_ = bf16[128,128]{1,0:T(8,128)(2,1)S(1)} collective-permute-done((bf16[128,128]{1,0:T(8,128)(2,1)S(1)}, bf16[128,128]{1,0:T(8,128)(2,1)S(1)}, u32[]{:S(2)}, u32[]{:S(2)}) %collective-permute-start.3) | collective-permute-done | bytes 32800 | tf_op jit(solution)/shard_map/ppermute | solution.py:331
  21.6 1.0 %collective-permute-done.4.refs_5_ = bf16[128,128]{1,0:T(8,128)(2,1)S(1)} collective-permute-done((bf16[128,128]{1,0:T(8,128)(2,1)S(1)}, bf16[128,128]{1,0:T(8,128)(2,1)S(1)}, u32[]{:S(2)}, u32[]{:S(2)}) %collective-permute-start.4) | collective-permute-done | bytes 32800 | tf_op jit(solution)/shard_map/ppermute | solution.py:331
  23.4 0.6 %tri.1 = (bf16[8,128,128]{2,1,0:T(8,128)(2,1)S(1)}, bf16[16,128,128]{2,1,0:T(8,128)(2,1)S(1)}) custom-call(bf16[16,128,128]{2,1,0:T(8,128)(2,1)S(1)} %all-to-all-done.refs_0_, bf16[16,64,128]{2,1,0:T(8,128)(2,1)S(1)} %sort_left.1.refs_1_, f32[8,128,128]{2,1,0:T(8,128)S(1)} %get-tuple-element.40.refs_2_.refs_1_), custom_call_target="tpu_custom_call" | custom-call | flops 33554432 | bytes 2097152 | tf_op jit(solution)/shard_map/tri/pallas_call | solution.py:65
  24.1 9.4 %all_to_all.20.refs_0_ = bf16[8,128,128]{2,1,0:T(8,128)(2,1)S(1)} all-to-all(bf16[8,128,128]{2,1,0:T(8,128)(2,1)S(1)} %get-tuple-element.41), channel_id=1, replica_groups={{0,1,2,3,4,5,6,7},{8,9,10,11,12,13,14,15},{16,17,18,19,20,21,22,23},{24..., dimensions={0} | all-to-all | bytes 524288 | tf_op jit(solution)/shard_map/all_to_all | solution.py:322
  33.8 8.6 %all_to_all.21.refs_0_ = bf16[8,128,128]{2,1,0:T(8,128)(2,1)S(1)} all-to-all(bf16[8,128,128]{2,1,0:T(8,128)(2,1)S(1)} %middle.1), channel_id=1, replica_groups={{0,1,2,3,4,5,6,7},{8,9,10,11,12,13,14,15},{16,17,18,19,20,21,22,23},{24..., dimensions={0} | all-to-all | bytes 524288 | tf_op jit(solution)/shard_map/all_to_all | solution.py:322
  42.4 1.5 %d_right.1 = (bf16[16,128,128]{2,1,0:T(8,128)(2,1)}, bf16[16,64,128]{2,1,0:T(8,128)(2,1)S(1)}) custom-call(bf16[8,128,128]{2,1,0:T(8,128)(2,1)S(1)} %all_to_all.21.refs_0_, bf16[16,64,128]{2,1,0:T(8,128)(2,1)S(1)} %sort_left.1.refs_1_), custom_call_target="tpu_custom_call" | custom-call | flops 33554432 | bytes 1310720 | tf_op jit(solution)/shard_map/d_right/pallas_call | solution.py:65
  43.9 4.9 %all-to-all-start.3 = ((bf16[16,128,128]{2,1,0:T(8,128)(2,1)}), bf16[16,128,128]{2,1,0:T(8,128)(2,1)S(1)}, u32[]{:S(2)}, u32[]{:S(2)}) async-start(bf16[16,128,128]{2,1,0:T(8,128)(2,1)} %get-tuple-element.42), calls=%async_computation.3 | async-start | bytes 1048576 | tf_op jit(solution)/shard_map/all_to_all | solution.py:314
  49.3 1.5 %collective-permute-start.8 = (bf16[128,128]{1,0:T(8,128)(2,1)S(1)}, bf16[128,128]{1,0:T(8,128)(2,1)S(1)}, u32[]{:S(2)}, u32[]{:S(2)}) collective-permute-start(bf16[128,128]{1,0:T(8,128)(2,1)S(1)} %get-tuple-element.47), channel_id=1, source_target_pairs={{0,2},{1,3},{2,0},{3,1},{4,6},{5,7},{6,4},{7,5},{8,10},{9,11},{10,... | collective-permute-start | bytes 98312 | tf_op jit(solution)/shard_map/ppermute | solution.py:331
  51.1 2.1 %collective-permute-start.10 = (bf16[128,128]{1,0:T(8,128)(2,1)S(1)}, bf16[128,128]{1,0:T(8,128)(2,1)S(1)}, u32[]{:S(2)}, u32[]{:S(2)}) collective-permute-start(bf16[128,128]{1,0:T(8,128)(2,1)S(1)} %get-tuple-element.49), channel_id=1, source_target_pairs={{0,7},{1,6},{2,5},{3,4},{4,3},{5,2},{6,1},{7,0},{8,15},{9,14},{10,... | collective-permute-start | bytes 98312 | tf_op jit(solution)/shard_map/ppermute | solution.py:331
  53.6 1.6 %collective-permute-start.12 = (bf16[128,128]{1,0:T(8,128)(2,1)S(1)}, bf16[128,128]{1,0:T(8,128)(2,1)S(1)}, u32[]{:S(2)}, u32[]{:S(2)}) collective-permute-start(bf16[128,128]{1,0:T(8,128)(2,1)S(1)} %get-tuple-element.51), channel_id=1, source_target_pairs={{0,5},{1,4},{2,7},{3,6},{4,1},{5,0},{6,3},{7,2},{8,13},{9,12},{10,... | collective-permute-start | bytes 98312 | tf_op jit(solution)/shard_map/ppermute | solution.py:331
  55.4 0.7 %copy-done.10 = f32[128]{0:T(128)S(1)} copy-done((f32[128]{0:T(128)S(1)}, f32[128]{0:T(128)}, u32[]{:S(2)}) %copy-start.10) | copy-done | bytes 536
  56.5 1.0 %slopes.1 = (bf16[8,512,128]{2,1,0:T(8,128)(2,1)S(1)}, bf16[8,128,128]{2,1,0:T(8,128)(2,1)S(1)}, f32[8,128]{1,0:T(8,128)S(1)}, f32[128,128]{1,0:T(8,128)S(1)}, bf16[128,640]{1,0:T(8,128)(2,1)S(1)}) custom-call(bf16[8,128,128]{2,1,0:T(8,128)(2,1)S(1)} %copy-done.1, s32[1,128]{1,0:T(1,128)S(1)} %bitcast.15, f32[1,128]{1,0:T(1,128)S(1)} %bitcast.8, ...), custom_call_target="tpu_custom_call" | custom-call | flops 134217728 | bytes 2233856 | tf_op jit(solution)/shard_map/slopes/pallas_call | solution.py:65
  57.6 1.6 %collective-permute-done.9.refs_3_ = bf16[128,128]{1,0:T(8,128)(2,1)S(1)} collective-permute-done((bf16[128,128]{1,0:T(8,128)(2,1)S(1)}, bf16[128,128]{1,0:T(8,128)(2,1)S(1)}, u32[]{:S(2)}, u32[]{:S(2)}) %collective-permute-start.9) | collective-permute-done | bytes 32800 | tf_op jit(solution)/shard_map/ppermute | solution.py:331
  59.2 0.7 %collective-permute-done.10.refs_4_ = bf16[128,128]{1,0:T(8,128)(2,1)S(1)} collective-permute-done((bf16[128,128]{1,0:T(8,128)(2,1)S(1)}, bf16[128,128]{1,0:T(8,128)(2,1)S(1)}, u32[]{:S(2)}, u32[]{:S(2)}) %collective-permute-start.10) | collective-permute-done | bytes 32800 | tf_op jit(solution)/shard_map/ppermute | solution.py:331
  60.9 1.3 %all-to-all-done.3.refs_0_ = bf16[16,128,128]{2,1,0:T(8,128)(2,1)S(1)} async-done(((bf16[16,128,128]{2,1,0:T(8,128)(2,1)}), bf16[16,128,128]{2,1,0:T(8,128)(2,1)S(1)}, u32[]{:S(2)}, u32[]{:S(2)}) %all-to-all-start.3) | async-done | bytes 524320 | tf_op jit(solution)/shard_map/all_to_all | solution.py:314
  62.2 1.4 %finish.1 = bf16[8,128,128]{2,1,0:T(8,128)(2,1)} custom-call(bf16[16,128,128]{2,1,0:T(8,128)(2,1)S(1)} %all-to-all-done.3.refs_0_, bf16[8,128,128]{2,1,0:T(8,128)(2,1)S(1)} %sort_d_left.1.refs_1_, bf16[8,512,128]{2,1,0:T(8,128)(2,1)S(1)} %get-tuple-element.54.refs_2_, bf16[8,128,128]{2,1,0:T(8,128)(2,1)S(1)} %gate_back.1.refs_6_.refs_3_, ...), custom_call_target="tpu_custom_call" | custom-call | flops 134217728 | bytes 2854912 | tf_op jit(solution)/shard_map/finish/pallas_call | solution.py:65
  (44 shorter events, 6.1 us)
Async XLA Ops:
  2.4 8.0 %copy-start = (bf16[16,128,128]{2,1,0:T(8,128)(2,1)S(1)}, bf16[16,128,128]{2,1,0:T(8,128)(2,1)}, u32[]{:S(2)}) copy-start(bf16[16,128,128]{2,1,0:T(8,128)(2,1)} %project_right.1.refs_5_) | copy-start | bytes 1572868
  2.4 8.0 %copy-start.1 = (bf16[8,128,128]{2,1,0:T(8,128)(2,1)S(1)}, bf16[8,128,128]{2,1,0:T(8,128)(2,1)}, u32[]{:S(2)}) copy-start(bf16[8,128,128]{2,1,0:T(8,128)(2,1)} %refs_0_.7) | copy-start | bytes 786436
  2.4 8.0 %copy-start.2 = (bf16[128,512]{1,0:T(8,128)(2,1)S(1)}, bf16[128,512]{1,0:T(8,128)(2,1)}, u32[]{:S(2)}) copy-start(bf16[128,512]{1,0:T(8,128)(2,1)} %refs_4_.9) | copy-start | bytes 393220
  2.4 8.0 %copy-start.6 = (f32[128]{0:T(128)S(1)}, f32[128]{0:T(128)}, u32[]{:S(2)}) copy-start(f32[128]{0:T(128)} %param.13) | copy-start | bytes 1540
  2.4 8.0 %copy-start.7 = (f32[128]{0:T(128)S(1)}, f32[128]{0:T(128)}, u32[]{:S(2)}) copy-start(f32[128]{0:T(128)} %param.14) | copy-start | bytes 1540
  2.5 8.0 %copy-start.8 = (s32[128]{0:T(128)S(1)}, s32[128]{0:T(128)}, u32[]{:S(2)}) copy-start(s32[128]{0:T(128)} %param.12) | copy-start | bytes 1540
  2.5 20.9 %all-to-all-start = ((bf16[16,128,128]{2,1,0:T(8,128)(2,1)}), bf16[16,128,128]{2,1,0:T(8,128)(2,1)S(1)}, u32[]{:S(2)}, u32[]{:S(2)}) async-start(bf16[16,128,128]{2,1,0:T(8,128)(2,1)} %project_right.1.refs_5_), calls=%async_computation | async-start | bytes 1048576 | tf_op jit(solution)/shard_map/all_to_all | solution.py:314
  10.5 7.2 %copy-start.3 = (bf16[8,128,128]{2,1,0:T(8,128)(2,1)S(1)}, bf16[8,128,128]{2,1,0:T(8,128)(2,1)}, u32[]{:S(2)}) copy-start(bf16[8,128,128]{2,1,0:T(8,128)(2,1)} %refs_1_.1) | copy-start | bytes 786436
  10.5 7.2 %copy-start.4 = (bf16[128,128]{1,0:T(8,128)(2,1)S(1)}, bf16[128,128]{1,0:T(8,128)(2,1)}, u32[]{:S(2)}) copy-start(bf16[128,128]{1,0:T(8,128)(2,1)} %refs_4_.8) | copy-start | bytes 98308
  11.3 4.6 %collective-permute-start = (bf16[128,128]{1,0:T(8,128)(2,1)S(1)}, bf16[128,128]{1,0:T(8,128)(2,1)S(1)}, u32[]{:S(2)}, u32[]{:S(2)}) collective-permute-start(bf16[128,128]{1,0:T(8,128)(2,1)S(1)} %get-tuple-element.33), channel_id=1, source_target_pairs={{0,1},{1,0},{2,3},{3,2},{4,5},{5,4},{6,7},{7,6},{8,9},{9,8},{10,11... | collective-permute-start | bytes 98312 | tf_op jit(solution)/shard_map/ppermute | solution.py:331
  11.5 5.9 %collective-permute-start.1 = (bf16[128,128]{1,0:T(8,128)(2,1)S(1)}, bf16[128,128]{1,0:T(8,128)(2,1)S(1)}, u32[]{:S(2)}, u32[]{:S(2)}) collective-permute-start(bf16[128,128]{1,0:T(8,128)(2,1)S(1)} %get-tuple-element.34), channel_id=1, source_target_pairs={{0,2},{1,3},{2,0},{3,1},{4,6},{5,7},{6,4},{7,5},{8,10},{9,11},{10,... | collective-permute-start | bytes 98312 | tf_op jit(solution)/shard_map/ppermute | solution.py:331
  13.0 7.9 %collective-permute-start.2 = (bf16[128,128]{1,0:T(8,128)(2,1)S(1)}, bf16[128,128]{1,0:T(8,128)(2,1)S(1)}, u32[]{:S(2)}, u32[]{:S(2)}) collective-permute-start(bf16[128,128]{1,0:T(8,128)(2,1)S(1)} %get-tuple-element.35), channel_id=1, source_target_pairs={{0,6},{1,7},{2,4},{3,5},{4,2},{5,3},{6,0},{7,1},{8,14},{9,15},{10,... | collective-permute-start | bytes 98312 | tf_op jit(solution)/shard_map/ppermute | solution.py:331
  13.6 8.0 %collective-permute-start.3 = (bf16[128,128]{1,0:T(8,128)(2,1)S(1)}, bf16[128,128]{1,0:T(8,128)(2,1)S(1)}, u32[]{:S(2)}, u32[]{:S(2)}) collective-permute-start(bf16[128,128]{1,0:T(8,128)(2,1)S(1)} %get-tuple-element.36), channel_id=1, source_target_pairs={{0,7},{1,6},{2,5},{3,4},{4,3},{5,2},{6,1},{7,0},{8,15},{9,14},{10,... | collective-permute-start | bytes 98312 | tf_op jit(solution)/shard_map/ppermute | solution.py:331
  15.3 7.2 %collective-permute-start.4 = (bf16[128,128]{1,0:T(8,128)(2,1)S(1)}, bf16[128,128]{1,0:T(8,128)(2,1)S(1)}, u32[]{:S(2)}, u32[]{:S(2)}) collective-permute-start(bf16[128,128]{1,0:T(8,128)(2,1)S(1)} %get-tuple-element.37), channel_id=1, source_target_pairs={{0,4},{1,5},{2,6},{3,7},{4,0},{5,1},{6,2},{7,3},{8,12},{9,13},{10,... | collective-permute-start | bytes 98312 | tf_op jit(solution)/shard_map/ppermute | solution.py:331
  15.9 7.3 %collective-permute-start.5 = (bf16[128,128]{1,0:T(8,128)(2,1)S(1)}, bf16[128,128]{1,0:T(8,128)(2,1)S(1)}, u32[]{:S(2)}, u32[]{:S(2)}) collective-permute-start(bf16[128,128]{1,0:T(8,128)(2,1)S(1)} %get-tuple-element.38), channel_id=1, source_target_pairs={{0,5},{1,4},{2,7},{3,6},{4,1},{5,0},{6,3},{7,2},{8,13},{9,12},{10,... | collective-permute-start | bytes 98312 | tf_op jit(solution)/shard_map/ppermute | solution.py:331
  17.4 5.8 %collective-permute-start.6 = (bf16[128,128]{1,0:T(8,128)(2,1)S(1)}, bf16[128,128]{1,0:T(8,128)(2,1)S(1)}, u32[]{:S(2)}, u32[]{:S(2)}) collective-permute-start(bf16[128,128]{1,0:T(8,128)(2,1)S(1)} %get-tuple-element.39), channel_id=1, source_target_pairs={{0,3},{1,2},{2,1},{3,0},{4,7},{5,6},{6,5},{7,4},{8,11},{9,10},{10,... | collective-permute-start | bytes 98312 | tf_op jit(solution)/shard_map/ppermute | solution.py:331
  43.9 18.3 %all-to-all-start.3 = ((bf16[16,128,128]{2,1,0:T(8,128)(2,1)}), bf16[16,128,128]{2,1,0:T(8,128)(2,1)S(1)}, u32[]{:S(2)}, u32[]{:S(2)}) async-start(bf16[16,128,128]{2,1,0:T(8,128)(2,1)} %get-tuple-element.42), calls=%async_computation.3 | async-start | bytes 1048576 | tf_op jit(solution)/shard_map/all_to_all | solution.py:314
  49.1 4.5 %collective-permute-start.7 = (bf16[128,128]{1,0:T(8,128)(2,1)S(1)}, bf16[128,128]{1,0:T(8,128)(2,1)S(1)}, u32[]{:S(2)}, u32[]{:S(2)}) collective-permute-start(bf16[128,128]{1,0:T(8,128)(2,1)S(1)} %get-tuple-element.46), channel_id=1, source_target_pairs={{0,1},{1,0},{2,3},{3,2},{4,5},{5,4},{6,7},{7,6},{8,9},{9,8},{10,11... | collective-permute-start | bytes 98312 | tf_op jit(solution)/shard_map/ppermute | solution.py:331
  49.3 6.1 %collective-permute-start.8 = (bf16[128,128]{1,0:T(8,128)(2,1)S(1)}, bf16[128,128]{1,0:T(8,128)(2,1)S(1)}, u32[]{:S(2)}, u32[]{:S(2)}) collective-permute-start(bf16[128,128]{1,0:T(8,128)(2,1)S(1)} %get-tuple-element.47), channel_id=1, source_target_pairs={{0,2},{1,3},{2,0},{3,1},{4,6},{5,7},{6,4},{7,5},{8,10},{9,11},{10,... | collective-permute-start | bytes 98312 | tf_op jit(solution)/shard_map/ppermute | solution.py:331
  50.8 8.4 %collective-permute-start.9 = (bf16[128,128]{1,0:T(8,128)(2,1)S(1)}, bf16[128,128]{1,0:T(8,128)(2,1)S(1)}, u32[]{:S(2)}, u32[]{:S(2)}) collective-permute-start(bf16[128,128]{1,0:T(8,128)(2,1)S(1)} %get-tuple-element.48), channel_id=1, source_target_pairs={{0,6},{1,7},{2,4},{3,5},{4,2},{5,3},{6,0},{7,1},{8,14},{9,15},{10,... | collective-permute-start | bytes 98312 | tf_op jit(solution)/shard_map/ppermute | solution.py:331
  51.1 8.8 %collective-permute-start.10 = (bf16[128,128]{1,0:T(8,128)(2,1)S(1)}, bf16[128,128]{1,0:T(8,128)(2,1)S(1)}, u32[]{:S(2)}, u32[]{:S(2)}) collective-permute-start(bf16[128,128]{1,0:T(8,128)(2,1)S(1)} %get-tuple-element.49), channel_id=1, source_target_pairs={{0,7},{1,6},{2,5},{3,4},{4,3},{5,2},{6,1},{7,0},{8,15},{9,14},{10,... | collective-permute-start | bytes 98312 | tf_op jit(solution)/shard_map/ppermute | solution.py:331
  53.1 7.4 %collective-permute-start.11 = (bf16[128,128]{1,0:T(8,128)(2,1)S(1)}, bf16[128,128]{1,0:T(8,128)(2,1)S(1)}, u32[]{:S(2)}, u32[]{:S(2)}) collective-permute-start(bf16[128,128]{1,0:T(8,128)(2,1)S(1)} %get-tuple-element.50), channel_id=1, source_target_pairs={{0,4},{1,5},{2,6},{3,7},{4,0},{5,1},{6,2},{7,3},{8,12},{9,13},{10,... | collective-permute-start | bytes 98312 | tf_op jit(solution)/shard_map/ppermute | solution.py:331
  53.6 7.2 %collective-permute-start.12 = (bf16[128,128]{1,0:T(8,128)(2,1)S(1)}, bf16[128,128]{1,0:T(8,128)(2,1)S(1)}, u32[]{:S(2)}, u32[]{:S(2)}) collective-permute-start(bf16[128,128]{1,0:T(8,128)(2,1)S(1)} %get-tuple-element.51), channel_id=1, source_target_pairs={{0,5},{1,4},{2,7},{3,6},{4,1},{5,0},{6,3},{7,2},{8,13},{9,12},{10,... | collective-permute-start | bytes 98312 | tf_op jit(solution)/shard_map/ppermute | solution.py:331
  55.4 5.4 %collective-permute-start.13 = (bf16[128,128]{1,0:T(8,128)(2,1)S(1)}, bf16[128,128]{1,0:T(8,128)(2,1)S(1)}, u32[]{:S(2)}, u32[]{:S(2)}) collective-permute-start(bf16[128,128]{1,0:T(8,128)(2,1)S(1)} %get-tuple-element.52), channel_id=1, source_target_pairs={{0,3},{1,2},{2,1},{3,0},{4,7},{5,6},{6,5},{7,4},{8,11},{9,10},{10,... | collective-permute-start | bytes 98312 | tf_op jit(solution)/shard_map/ppermute | solution.py:331
  (3 other events, 8.5 us)

commit v22 on v17

--- a/solution.py
+++ b/solution.py
@@ -79,26 +79,60 @@
     )(*args)
 
 
+HALVES = 2
+PLANES = 2
+
+
+def reorder(columns):
+    size = columns.shape[0] // (HALVES * PLANES)
+    parts = [columns[n * size : (n + 1) * size] for n in (0, 2, 1, 3)]
+    return jnp.concatenate(parts, axis=0)
+
+
+def on_lanes(cells):
+    return jnp.transpose(reorder(cells.astype(F32)))
+
+
+def lane_of(shape):
+    return lax.broadcasted_iota(jnp.int32, shape, len(shape) - 1)
+
+
+def own_plane(per_plane):
+    return lax.rem(lax.div(lax.axis_index("row"), per_plane), PLANES)
+
+
 def cell_masks(mask, rows):
     columns = mask[...].astype(F32)
-    shape = (rows, columns.shape[1])
+    width = columns.shape[1]
+    shape = (rows, width)
     first = lax.axis_index("row") * rows
-    own = lax.broadcasted_iota(jnp.int32, shape, 1) == (
-        lax.broadcasted_iota(jnp.int32, shape, 0) + first
-    )
+    lane = lane_of(shape)
+    own = lane == lax.broadcasted_iota(jnp.int32, shape, 0) + first
     row_mask = jnp.sum(jnp.where(own, columns, 0.0), axis=1, keepdims=True)
     cells = row_mask * columns
+    size = width // (HALVES * PLANES)
+    later, earlier = pltpu.roll(cells, width - size, 1), pltpu.roll(cells, size, 1)
+    segment = lax.div(lane, size)
+    cells = jnp.where(segment == 1, later, jnp.where(segment == 2, earlier, cells))
     return [cells[row : row + 1] for row in range(rows)]
 
 
-def wide_order(devices, count, back):
-    order = []
-    for place in range(count):
-        if back:
-            order += [place ^ (count // 2), count + place]
-        else:
-            order += [count + (place ^ 2), place ^ (count // 2)]
-    return order
+def pack(first, second, plane):
+    half = first.shape[1] // 2
+    lane = lane_of(first.shape)
+    zero = lane * 0 + plane == 0
+    first = jnp.where(zero, pltpu.roll(first, half, 1), first)
+    second = jnp.where(zero, second, pltpu.roll(second, half, 1))
+    return jnp.where(lane < half, first, second)
+
+
+def unpack(own, packed, is_first, plane):
+    half = own.shape[1] // 2
+    lane = lane_of(own.shape)
+    zero = lane * 0 + plane == 0
+    moved = pltpu.roll(packed, half, 1)
+    other = jnp.where(zero, moved, packed) if is_first else jnp.where(zero, packed, moved)
+    return jnp.where(lax.div(lane, half) == plane, own, other)
 
 
 def distances(count, beside):
@@ -137,7 +171,7 @@
     gain_col, bias_col = column(gain[...]), column(bias[...])
     masks = cell_masks(mask, rows)
     for row in range(rows):
-        normed, _ = norm_rows(jnp.transpose(pair[row].astype(F32)))
+        normed, _ = norm_rows(on_lanes(pair[row]))
         zln = (normed * gain_col + bias_col).astype(BF16)
         proj = dot(w_flip, zln, 1, 0)
         yield row, masks[row] * sigmoid(proj[:hidden]) * proj[hidden:]
@@ -147,48 +181,60 @@
     rows = pair.shape[0]
     devices, depth, width = right_panel.shape
     block = depth // rows
-    count = w_proj.shape[1] // 4 // block
     for row, right in gated_rows(pair, mask, gain, bias, w_proj, 1):
-        right = right.reshape(count, block, width).astype(BF16)
-        for rank in range(devices):
-            place = wide_order(devices, count, False)[rank] % count
-            right_panel[rank, row * block : (row + 1) * block, :] = right[place]
+        right = right.reshape(devices // HALVES, block, width).astype(BF16)
+        for half in range(HALVES):
+            start = half * (devices // HALVES)
+            right_panel[
+                start : start + devices // HALVES, row * block : (row + 1) * block, :
+            ] = right
 
 
 def project_left_kernel(pair, mask, gain, bias, w_proj, after, *refs):
     del after
     *pieces, left_panel = refs
     rows = pair.shape[0]
-    count, depth, width = left_panel.shape
+    per_plane, depth, width = left_panel.shape
     block = depth // rows
     for row, left in gated_rows(pair, mask, gain, bias, w_proj, 0):
-        left = left.reshape(count, block, width).astype(BF16)
+        left = left.reshape(per_plane, block, width).astype(BF16)
         left_panel[:, row * block : (row + 1) * block, :] = left
-    for place, piece in zip(partners(count, True), pieces):
-        piece[...] = left_panel[place]
+    for place, piece in zip(partners(len(pieces), True), pieces):
+        piece[...] = left_panel[lax.rem(place, per_plane)]
+
+
+def pack_rows(cells, packed, per_plane):
+    rows, channels, _ = cells.shape
+    plane = own_plane(per_plane)
+    for row in range(rows // 2):
+        both = pack(cells[row], cells[row + rows // 2], plane)
+        packed[row * channels : (row + 1) * channels, :] = both.astype(BF16)
+
+
+def unpack_row(own, packed, row, rows, per_plane):
+    channels = own.shape[0]
+    place = row % (rows // 2) * channels
+    other = packed[place : place + channels, :].astype(F32)
+    return unpack(own, other, row < rows // 2, own_plane(per_plane))
 
 
 def prepare_kernel(
-    pair, cotangent, gain, bias, w_gate, out_gain, w_out, d_hat_centered, gate_slope
+    pair, cotangent, gain, bias, w_gate, out_gain, w_out, after, d_hat_centered, gate_slope, d_hat_sent
 ):
+    del after
     gate_flip = transposed(w_gate[...])
     gain_col, bias_col = column(gain[...]), column(bias[...])
     out_gain_col = column(out_gain[...])
     for row in range(pair.shape[0]):
-        normed, _ = norm_rows(jnp.transpose(pair[row].astype(F32)))
+        normed, _ = norm_rows(on_lanes(pair[row]))
         zln = (normed * gain_col + bias_col).astype(BF16)
         gate = sigmoid(dot(gate_flip, zln, 1, 0))
-        cot = jnp.transpose(cotangent[row].astype(F32))
+        cot = on_lanes(cotangent[row])
         d_scaled = (cot * gate).astype(BF16)
         d_hat = dot(w_out[...], d_scaled, 1, 0) * out_gain_col
         d_hat_centered[row] = d_hat - jnp.mean(d_hat, axis=0, keepdims=True)
         gate_slope[row] = cot * gate * (1.0 - gate)
-
-
-def wide_places(panel, count, back):
-    devices, depth, _ = panel.shape
-    for rank, device in enumerate(wide_order(devices, count, back)):
-        yield rank, slice(device * depth, (device + 1) * depth)
+    pack_rows(d_hat_centered, d_hat_sent, pair.shape[1] // (HALVES * PLANES) // pair.shape[0])
 
 
 def sort_left_kernel(*refs):
@@ -199,18 +245,23 @@
         left_all[h] = left_wide[pl.ds(h, left_rows, stride=block), :].astype(BF16)
 
 
-def tri_kernel(right_panel, left_all, after, *refs):
+def twice(matrix):
+    return jnp.concatenate([matrix, matrix], axis=0)
+
+
+def tri_kernel(right_panel, left_all, after, right_all, *refs):
     del after
-    right_all, *pieces, left_wide, right_wide = refs
-    block, left_rows, _ = left_all.shape
-    right_rows = right_all.shape[1]
-    for rank, place in wide_places(right_panel, len(pieces), False):
-        right_wide[place, :] = right_panel[rank].astype(F32)
+    *pieces, right_wide, tri_wide = refs
+    block, right_rows, width = right_all.shape
+    cells = left_all.shape[1] // PLANES
+    low = lane_of((cells, width)) < width // 2
+    right_wide[...] = right_panel[...].astype(F32).reshape(right_wide.shape)
     for h in range(block):
         right = right_wide[pl.ds(h, right_rows, stride=block), :].astype(BF16)
         right_all[h] = right
-        left_wide[pl.ds(h, left_rows, stride=block), :] = dot(left_all[h], right, 1, 1)
-    hand_out(left_wide, pieces, False)
+        tri = dot(left_all[h], twice(right), 1, 1)
+        tri_wide[pl.ds(h, cells, stride=block), :] = jnp.where(low, tri[:cells], tri[cells:])
+    hand_out(tri_wide, pieces, False)
 
 
 def cell_row(ref, row, rows):
@@ -219,55 +270,74 @@
     return ref[:, row * block : (row + 1) * block, :].astype(F32).reshape(count * block, width)
 
 
-def middle_kernel(d_hat_centered, *refs):
-    count = (len(refs) - 2) // 2
-    products, pieces = refs[:count], refs[count : 2 * count]
-    panel, d_panel = refs[2 * count :]
+def middle_kernel(d_hat_centered, d_hat_other, *refs):
+    per_plane = (len(refs) - 2) // 2
+    products, pieces = refs[:per_plane], refs[per_plane : 2 * per_plane]
+    panel, d_panel = refs[2 * per_plane :]
     rows = d_hat_centered.shape[0]
     _, depth, width = panel.shape
     block = depth // rows
     gather(products, panel, False)
     for row in range(rows):
         tri_hat, inv_std = norm_rows(cell_row(panel, row, rows))
-        d_hat = d_hat_centered[row]
+        d_hat = unpack_row(d_hat_centered[row], d_hat_other, row, rows, per_plane)
         cross = jnp.mean(d_hat * tri_hat, axis=0, keepdims=True)
         d_tri = inv_std * (d_hat - tri_hat * cross)
         d_panel[:, row * block : (row + 1) * block, :] = d_tri.reshape(
-            count, block, width
+            per_plane, block, width
         ).astype(BF16)
-    for place, piece in zip(partners(count, False), pieces):
+    for place, piece in zip(partners(per_plane, False), pieces):
         piece[...] = d_panel[place]
 
 
 def d_right_kernel(left_all, *refs):
-    *d_products, d_right_panel, d_tri_all, left_wide, right_wide = refs
-    block, left_rows, _ = left_all.shape
+    *d_products, d_right_panel, d_tri_all, tri_wide, right_wide = refs
+    block, _, width = left_all.shape
+    cells = d_tri_all.shape[1] // PLANES
     right_rows = right_wide.shape[0] // block
-    spread(d_products, left_wide, False)
+    low = lane_of((cells, width)) < width // 2
+    spread(d_products, tri_wide, False)
     for h in range(block):
-        d_tri = left_wide[pl.ds(h, left_rows, stride=block), :].astype(BF16)
+        d_tri = tri_wide[pl.ds(h, cells, stride=block), :]
+        parts = [jnp.where(low, d_tri, 0.0), jnp.where(low, 0.0, d_tri)]
+        d_tri = jnp.concatenate(parts, axis=0).astype(BF16)
         d_tri_all[h] = d_tri
-        right_wide[pl.ds(h, right_rows, stride=block), :] = dot(d_tri, left_all[h], 0, 0)
-    for rank, place in wide_places(d_right_panel, len(d_products), True):
-        d_right_panel[rank] = right_wide[place, :].astype(BF16)
+        d_right = dot(d_tri, left_all[h], 0, 0)
+        right_wide[pl.ds(h, right_rows, stride=block), :] = (
+            d_right[:right_rows] + d_right[right_rows:]
+        )
+    d_right_panel[...] = right_wide[...].astype(BF16).reshape(d_right_panel.shape)
 
 
 def d_left_kernel(d_tri_all, right_all, *refs):
     *pieces, left_wide = refs
     block, left_rows, _ = d_tri_all.shape
     for h in range(block):
-        left_wide[pl.ds(h, left_rows, stride=block), :] = dot(d_tri_all[h], right_all[h], 1, 0)
+        left_wide[pl.ds(h, left_rows, stride=block), :] = dot(
+            d_tri_all[h], twice(right_all[h]), 1, 0
+        )
     hand_out(left_wide, pieces, True)
 
 
-def gate_back_kernel(gate_slope, out_gain, out_bias, w_out, *refs):
+def pack_tri_kernel(after, *refs):
+    del after
+    *products, tri_sent, panel, cells = refs
+    rows = cells.shape[0]
+    gather(products, panel, False)
+    for row in range(rows):
+        cells[row] = cell_row(panel, row, rows)
+    pack_rows(cells, tri_sent, len(products))
+
+
+def gate_back_kernel(gate_slope, out_gain, out_bias, w_out, tri_other, *refs):
     *products, d_gate_pre, panel = refs
     rows = gate_slope.shape[0]
     gather(products, panel, False)
     out_flip = transposed(w_out[...])
     out_gain_col, out_bias_col = column(out_gain[...]), column(out_bias[...])
     for row in range(rows):
-        tri_hat, _ = norm_rows(cell_row(panel, row, rows))
+        own = cell_row(panel, row, rows)
+        tri_hat, _ = norm_rows(unpack_row(own, tri_other, row, rows, len(products)))
         scaled = (tri_hat * out_gain_col + out_bias_col).astype(BF16)
         d_gate_pre[row] = (dot(out_flip, scaled, 1, 0) * gate_slope[row]).astype(BF16)
 
@@ -284,7 +354,7 @@
     weights[...] = jnp.concatenate([w_proj[...], w_gate[...]], axis=1)
     masks = cell_masks(mask, rows)
     for row in range(rows):
-        normed, inv_std = norm_rows(jnp.transpose(pair[row].astype(F32)))
+        normed, inv_std = norm_rows(on_lanes(pair[row]))
         normed_in[row] = normed.astype(normed_in.dtype)
         inv_in[row : row + 1] = inv_std
         zln = (normed * gain_col + bias_col).astype(BF16)
@@ -303,24 +373,16 @@
     gather(pieces, d_left_panel, True)
 
 
-def both_halves(blocks, count):
-    order = wide_order(2 * count, count, True)
-    return jnp.stack(
-        [blocks[order.index(place)] + blocks[order.index(count + place)] for place in range(count)]
-    )
-
-
 def finish_kernel(
     d_right_panel, d_left_panel, slopes, d_gate_pre, normed_in, inv_in, gain_col, weights, grad
 ):
     rows = grad.shape[0]
-    count, depth, width = d_left_panel.shape
-    hidden = count * depth // rows
+    hidden = slopes.shape[1] // 4
     for row in range(rows):
-        d_right = cell_row(d_right_panel, row, rows)
-        d_right = both_halves(d_right.reshape(2 * count, depth // rows, width), count)
         parts = []
-        for side, d_value in enumerate((cell_row(d_left_panel, row, rows), d_right.reshape(hidden, width))):
+        for side, panel in enumerate((d_left_panel, d_right_panel)):
+            d_value = cell_row(panel, row, rows)
+            d_value = d_value[:hidden] + d_value[hidden:]
             for base in (2 * side * hidden, (2 * side + 1) * hidden):
                 slope = slopes[row, base : base + hidden, :].astype(F32)
                 parts.append((d_value * slope).astype(BF16))
@@ -330,22 +392,28 @@
         mean_grad = jnp.mean(d_in, axis=0, keepdims=True)
         mean_cross = jnp.mean(d_in * normed, axis=0, keepdims=True)
         result = inv_in[row : row + 1] * (d_in - mean_grad - normed * mean_cross)
-        grad[row] = jnp.transpose(result).astype(BF16)
-
-
-def swap(values, count, back):
-    groups = [wide_order(lax.axis_size("row"), count, back)]
+        grad[row] = reorder(jnp.transpose(result)).astype(BF16)
+
+
+def swap(values, per_plane):
+    groups = [
+        [(half * PLANES + plane) * per_plane + n for half in range(HALVES) for n in range(per_plane)]
+        for plane in range(PLANES)
+    ]
     return lax.all_to_all(
         values, "row", split_axis=0, concat_axis=0, tiled=True, axis_index_groups=groups
     )
 
 
+def swap_with(values, apart):
+    devices = range(lax.axis_size("row"))
+    return lax.ppermute(values, "row", [(d, d ^ apart) for d in devices])
+
+
 def swap_pieces(pieces, beside):
-    devices = range(lax.axis_size("row"))
     apart = distances(len(pieces), beside)
     return [pieces[0]] + [
-        lax.ppermute(pieces[step], "row", [(d, d ^ apart[step]) for d in devices])
-        for step in range(1, len(pieces))
+        swap_with(pieces[step], apart[step]) for step in range(1, len(pieces))
     ]
 
 
@@ -363,22 +431,22 @@
 ):
     rows, width, channels = pair.shape
     hidden = w_out.shape[0]
-    halves = 2
-    devices = lax.axis_size("row")
-    count = devices // halves
-    block = hidden // count
-    left_rows, right_rows = rows * count, rows * devices
+    per_plane = lax.axis_size("row") // (HALVES * PLANES)
+    count = per_plane * PLANES
+    block = hidden // per_plane
+    left_rows, right_rows = rows * count, rows * per_plane * HALVES
     shape = jax.ShapeDtypeStruct
-    panel = shape((count, rows * block, width), BF16)
-    wide_panel = shape((devices, rows * block, width), BF16)
+    piece = shape((rows * block, width), BF16)
+    wide_panel = shape((per_plane * HALVES, rows * block, width), BF16)
+    swapped = shape((rows // 2 * hidden, width), BF16)
     mask = residue_mask.reshape(1, width)
     gain, bias = ln_in_gain.reshape(1, channels), ln_in_bias.reshape(1, channels)
     out_gain, out_bias = ln_out_gain.reshape(1, hidden), ln_out_bias.reshape(1, hidden)
     cells = rows * width
-    piece = shape((rows * block, width), BF16)
-    left_panel = pltpu.VMEM(panel.shape, BF16)
+    plane_panel = pltpu.VMEM((per_plane, rows * block, width), BF16)
     left_wide = pltpu.VMEM((left_rows * block, width), F32)
     right_wide = pltpu.VMEM((right_rows * block, width), F32)
+    tri_wide = pltpu.VMEM((rows * per_plane * block, width), F32)
     (own_right,) = call(
         project_right_kernel,
         "project_right",
@@ -388,7 +456,7 @@
         flops=2 * cells * channels * 2 * hidden,
         limit=64 * 1024 * 1024 - 640 * 1024,
     )
-    right_panel = swap(own_right, count, False)
+    right_panel = swap(own_right, per_plane)
     pieces = call(
         project_left_kernel,
         "project_left",
@@ -396,7 +464,7 @@
         [pair, mask, gain, bias, w_proj, own_right],
         fetched=range(5),
         unread=(5,),
-        scratch=[left_panel],
+        scratch=[plane_panel],
         flops=2 * cells * channels * 2 * hidden,
     )
     pieces = swap_pieces(pieces, True)
@@ -407,42 +475,44 @@
         pieces,
         scratch=[left_wide],
     )
-    d_hat_centered, gate_slope = call(
+    d_hat_centered, gate_slope, d_hat_sent = call(
         prepare_kernel,
         "prepare",
-        [shape((rows, hidden, width), F32), shape((rows, channels, width), F32)],
-        [pair, cotangent, gain, bias, w_gate, out_gain, w_out],
+        [shape((rows, hidden, width), F32), shape((rows, channels, width), F32), swapped],
+        [pair, cotangent, gain, bias, w_gate, out_gain, w_out, own_right],
         fetched=range(7),
+        unread=(7,),
         flops=2 * cells * channels * 2 * hidden,
     )
+    d_hat_other = swap_with(d_hat_sent, per_plane)
     right_all, *products = call(
         tri_kernel,
         "tri",
-        [shape((block, right_rows, width), BF16)] + [piece] * count,
-        [right_panel, left_all, d_hat_centered],
+        [shape((block, right_rows, width), BF16)] + [piece] * per_plane,
+        [right_panel, left_all, d_hat_other],
         unread=(2,),
-        scratch=[left_wide, right_wide],
+        scratch=[right_wide, tri_wide],
         flops=2 * block * left_rows * width * right_rows,
     )
     products = swap_pieces(products, False)
     d_products = call(
         middle_kernel,
         "middle",
-        [piece] * count,
-        [d_hat_centered, *products],
-        scratch=[left_panel, left_panel],
+        [piece] * per_plane,
+        [d_hat_centered, d_hat_other, *products],
+        scratch=[plane_panel, plane_panel],
         flops=20 * cells * hidden,
     )
     d_products = swap_pieces(d_products, False)
-    d_right_panel, d_tri_all = call(
+    own_d_right, d_tri_all = call(
         d_right_kernel,
         "d_right",
         [wide_panel, shape((block, left_rows, width), BF16)],
         [left_all, *d_products],
-        scratch=[left_wide, right_wide],
+        scratch=[tri_wide, right_wide],
         flops=2 * block * left_rows * width * right_rows,
     )
-    d_right_panel = swap(d_right_panel, count, True)
+    d_right_panel = swap(own_d_right, per_plane)
     d_pieces = call(
         d_left_kernel,
         "d_left",
@@ -452,14 +522,24 @@
         flops=2 * block * left_rows * width * right_rows,
     )
     d_pieces = swap_pieces(d_pieces, True)
-    (d_left_panel,) = call(sort_d_left_kernel, "sort_d_left", [panel], d_pieces)
+    d_left_panel = shape((count, rows * block, width), BF16)
+    (d_left_panel,) = call(sort_d_left_kernel, "sort_d_left", [d_left_panel], d_pieces)
+    (tri_sent,) = call(
+        pack_tri_kernel,
+        "pack_tri",
+        [swapped],
+        [own_d_right, *products],
+        unread=(0,),
+        scratch=[plane_panel, pltpu.VMEM((rows, hidden, width), F32)],
+    )
+    tri_other = swap_with(tri_sent, per_plane)
     (d_gate_pre,) = call(
         gate_back_kernel,
         "gate_back",
         [shape((rows, channels, width), BF16)],
-        [gate_slope, out_gain, out_bias, w_out, *products],
+        [gate_slope, out_gain, out_bias, w_out, tri_other, *products],
         fetched=range(1, 4),
-        scratch=[left_panel],
+        scratch=[plane_panel],
         flops=2 * cells * channels * hidden,
     )
     slopes, normed_in, inv_in, gain_col, weights = call(
@@ -605,7 +685,7 @@
 
 
 def solution(mesh):
-    fits = mesh.shape["chan"] == 1 and mesh.shape["row"] in (8, 16)
+    fits = mesh.shape["chan"] == 1 and mesh.shape["row"] == 16
     return jax.shard_map(
         kernel_shards if fits else shards,
         mesh=mesh,

time: 63.7 us -> 70.3 us (1.10)
  waiting for transfers between devices: 14.5 us -> 19.7 us
  Pallas kernels: 9.93 us -> 12.6 us
  starting transfers between devices: 37.3 us -> 36.1 us
    ppermute x28 -> x22, waiting for transfers between devices: 14 us -> 19.7 us  [swap_with(): return lax.ppermute(values, 'row', [(d, d ^ apart) for d in devices])]
    all_to_all x2, starting transfers between devices: 13.4 us -> 10.4 us  [swap(): lax.all_to_all(values, 'row', split_axis=0, concat_axis=0, tiled=True, ax...]
    pallas_call x12 -> x13, Pallas kernels: 9.93 us -> 12.6 us  [call(): pl.pallas_call(body, name=name, out_shape=outs, in_specs=[pl.BlockSpec(me...]
    ppermute x28 -> x22, starting transfers between devices: 23.9 us -> 25.6 us  [swap_with(): return lax.ppermute(values, 'row', [(d, d ^ apart) for d in devices])]
  transfers between devices with their start and end apart: 30 -> 24, of which waited for: 18 -> 10; matrix products, arithmetic and copies ran while one was open for 0% -> 0% of each run, Pallas kernels for 6% -> 7%
where the time goes in v22:
time: 70.3 us; the launch traced here: 69.3 us
  starting transfers between devices  36.1 us (51%)
  waiting for transfers between devices  19.7 us (28%)
  Pallas kernels  12.6 us (18%)
  local copies, waits for them, and re-layouts  0.72 us (1%)
    ppermute x22, starting transfers between devices, swap_with(): return lax.ppermute(values, 'row', [(d, d ^ apart) for d in devices])  25.6 us
    ppermute x22, waiting for transfers between devices, swap_with(): return lax.ppermute(values, 'row', [(d, d ^ apart) for d in devices])  19.7 us
    pallas_call x13, Pallas kernels, call(): pl.pallas_call(body, name=name, out_shape=outs, in_specs=[pl.BlockSpec(me...  12.6 us
    all_to_all x2, starting transfers between devices, swap(): lax.all_to_all(values, 'row', split_axis=0, concat_axis=0, tiled=True, ax...  10.4 us
  transfers between devices with their start and end apart: 24, of which 10 were waited for; matrix products, arithmetic and copies ran while one was open for 0% of the time, Pallas kernels for 7%

profile of v22, /device:TPU:0, one launch (start us, length us, event | category | flops | bytes accessed | tf_op | source)
XLA Modules:
  0.0 69.3 jit_solution(16602720212839276301)
XLA Ops:
  0.0 2.4 %project_right.1.refs_5_.refs_7_ = bf16[8,256,128]{2,1,0:T(8,128)(2,1)} custom-call(bf16[8,128,128]{2,1,0:T(8,128)(2,1)} %refs_0_.7, s32[1,128]{1,0:T(1,128)} %bitcast.13, f32[1,128]{1,0:T(1,128)} %bitcast.5, f32[1,128]{1,0:T(1,128)} %bitcast.9, bf16[128,512]{1,0:T(8,128)(2,1)} %refs_4_.7), custom_call_target="tpu_custom_call" | custom-call | flops 67108864 | bytes 919040 | tf_op jit(solution)/shard_map/project_right/pallas_call | solution.py:65
  2.5 6.4 %all-to-all-start = ((bf16[8,256,128]{2,1,0:T(8,128)(2,1)}), bf16[8,256,128]{2,1,0:T(8,128)(2,1)S(1)}, u32[]{:S(2)}, u32[]{:S(2)}) async-start(bf16[8,256,128]{2,1,0:T(8,128)(2,1)} %project_right.1.refs_5_.refs_7_), calls=%async_computation | async-start | bytes 1048576 | tf_op jit(solution)/shard_map/all_to_all | solution.py:403
  10.3 1.7 %collective-permute-start.1 = (bf16[256,128]{1,0:T(8,128)(2,1)S(1)}, bf16[256,128]{1,0:T(8,128)(2,1)S(1)}, u32[]{:S(2)}, u32[]{:S(2)}) collective-permute-start(bf16[256,128]{1,0:T(8,128)(2,1)S(1)} %get-tuple-element.42), channel_id=1, source_target_pairs={{0,2},{1,3},{2,0},{3,1},{4,6},{5,7},{6,4},{7,5},{8,10},{9,11},{10,... | collective-permute-start | bytes 196616 | tf_op jit(solution)/shard_map/ppermute | solution.py:410
  12.0 1.4 %collective-permute-start.2 = (bf16[256,128]{1,0:T(8,128)(2,1)S(1)}, bf16[256,128]{1,0:T(8,128)(2,1)S(1)}, u32[]{:S(2)}, u32[]{:S(2)}) collective-permute-start(bf16[256,128]{1,0:T(8,128)(2,1)S(1)} %get-tuple-element.43), channel_id=1, source_target_pairs={{0,6},{1,7},{2,4},{3,5},{4,2},{5,3},{6,0},{7,1},{8,14},{9,15},{10,... | collective-permute-start | bytes 196616 | tf_op jit(solution)/shard_map/ppermute | solution.py:410
  15.2 1.4 %collective-permute-start.3 = (bf16[256,128]{1,0:T(8,128)(2,1)S(1)}, bf16[256,128]{1,0:T(8,128)(2,1)S(1)}, u32[]{:S(2)}, u32[]{:S(2)}) collective-permute-start(bf16[256,128]{1,0:T(8,128)(2,1)S(1)} %get-tuple-element.44), channel_id=1, source_target_pairs={{0,7},{1,6},{2,5},{3,4},{4,3},{5,2},{6,1},{7,0},{8,15},{9,14},{10,... | collective-permute-start | bytes 196616 | tf_op jit(solution)/shard_map/ppermute | solution.py:410
  18.1 3.2 %collective-permute-start.5 = (bf16[256,128]{1,0:T(8,128)(2,1)S(1)}, bf16[256,128]{1,0:T(8,128)(2,1)S(1)}, u32[]{:S(2)}, u32[]{:S(2)}) collective-permute-start(bf16[256,128]{1,0:T(8,128)(2,1)S(1)} %get-tuple-element.46), channel_id=1, source_target_pairs={{0,5},{1,4},{2,7},{3,6},{4,1},{5,0},{6,3},{7,2},{8,13},{9,12},{10,... | collective-permute-start | bytes 196616 | tf_op jit(solution)/shard_map/ppermute | solution.py:410
  22.2 3.2 %collective-permute-done.3.refs_4_ = bf16[256,128]{1,0:T(8,128)(2,1)S(1)} collective-permute-done((bf16[256,128]{1,0:T(8,128)(2,1)S(1)}, bf16[256,128]{1,0:T(8,128)(2,1)S(1)}, u32[]{:S(2)}, u32[]{:S(2)}) %collective-permute-start.3) | collective-permute-done | bytes 65568 | tf_op jit(solution)/shard_map/ppermute | solution.py:410
  25.3 2.0 %collective-permute-done.4.refs_5_ = bf16[256,128]{1,0:T(8,128)(2,1)S(1)} collective-permute-done((bf16[256,128]{1,0:T(8,128)(2,1)S(1)}, bf16[256,128]{1,0:T(8,128)(2,1)S(1)}, u32[]{:S(2)}, u32[]{:S(2)}) %collective-permute-start.4) | collective-permute-done | bytes 65568 | tf_op jit(solution)/shard_map/ppermute | solution.py:410
  28.3 1.2 %tri.1 = (bf16[32,64,128]{2,1,0:T(8,128)(2,1)S(1)}, bf16[256,128]{1,0:T(8,128)(2,1)S(1)}, bf16[256,128]{1,0:T(8,128)(2,1)S(1)}, bf16[256,128]{1,0:T(8,128)(2,1)S(1)}, bf16[256,128]{1,0:T(8,128)(2,1)S(1)}) custom-call(bf16[8,256,128]{2,1,0:T(8,128)(2,1)S(1)} %all-to-all-done.refs_0_, bf16[32,64,128]{2,1,0:T(8,128)(2,1)S(1)} %sort_left.1.refs_1_.refs_0_, ...), custom_call_target="tpu_custom_call" | custom-call | flops 33554432 | bytes 1966080 | tf_op jit(solution)/shard_map/tri/pallas_call | solution.py:65
  29.5 1.7 %collective-permute-start.8 = (bf16[256,128]{1,0:T(8,128)(2,1)S(1)}, bf16[256,128]{1,0:T(8,128)(2,1)S(1)}, u32[]{:S(2)}, u32[]{:S(2)}) collective-permute-start(bf16[256,128]{1,0:T(8,128)(2,1)S(1)} %get-tuple-element.51), channel_id=1, source_target_pairs={{0,2},{1,3},{2,0},{3,1},{4,6},{5,7},{6,4},{7,5},{8,10},{9,11},{10,... | collective-permute-start | bytes 196616 | tf_op jit(solution)/shard_map/ppermute | solution.py:410
  31.7 2.3 %collective-permute-done.8.refs_3_.refs_2_.refs_6_ = bf16[256,128]{1,0:T(8,128)(2,1)S(1)} collective-permute-done((bf16[256,128]{1,0:T(8,128)(2,1)S(1)}, bf16[256,128]{1,0:T(8,128)(2,1)S(1)}, u32[]{:S(2)}, u32[]{:S(2)}) %collective-permute-start.8) | collective-permute-done | bytes 65568 | tf_op jit(solution)/shard_map/ppermute | solution.py:410
  34.0 1.3 %collective-permute-done.9.refs_4_.refs_3_.refs_7_ = bf16[256,128]{1,0:T(8,128)(2,1)S(1)} collective-permute-done((bf16[256,128]{1,0:T(8,128)(2,1)S(1)}, bf16[256,128]{1,0:T(8,128)(2,1)S(1)}, u32[]{:S(2)}, u32[]{:S(2)}) %collective-permute-start.9) | collective-permute-done | bytes 65568 | tf_op jit(solution)/shard_map/ppermute | solution.py:410
  35.6 1.6 %collective-permute-start.11 = (bf16[256,128]{1,0:T(8,128)(2,1)S(1)}, bf16[256,128]{1,0:T(8,128)(2,1)S(1)}, u32[]{:S(2)}, u32[]{:S(2)}) collective-permute-start(bf16[256,128]{1,0:T(8,128)(2,1)S(1)} %get-tuple-element.55), channel_id=1, source_target_pairs={{0,2},{1,3},{2,0},{3,1},{4,6},{5,7},{6,4},{7,5},{8,10},{9,11},{10,... | collective-permute-start | bytes 196616 | tf_op jit(solution)/shard_map/ppermute | solution.py:410
  37.8 2.1 %collective-permute-done.11.refs_2_ = bf16[256,128]{1,0:T(8,128)(2,1)S(1)} collective-permute-done((bf16[256,128]{1,0:T(8,128)(2,1)S(1)}, bf16[256,128]{1,0:T(8,128)(2,1)S(1)}, u32[]{:S(2)}, u32[]{:S(2)}) %collective-permute-start.11) | collective-permute-done | bytes 65568 | tf_op jit(solution)/shard_map/ppermute | solution.py:410
  40.0 1.5 %collective-permute-done.12.refs_3_ = bf16[256,128]{1,0:T(8,128)(2,1)S(1)} collective-permute-done((bf16[256,128]{1,0:T(8,128)(2,1)S(1)}, bf16[256,128]{1,0:T(8,128)(2,1)S(1)}, u32[]{:S(2)}, u32[]{:S(2)}) %collective-permute-start.12) | collective-permute-done | bytes 65568 | tf_op jit(solution)/shard_map/ppermute | solution.py:410
  41.5 2.1 %d_right.1 = (bf16[8,256,128]{2,1,0:T(8,128)(2,1)}, bf16[32,64,128]{2,1,0:T(8,128)(2,1)S(1)}) custom-call(bf16[32,64,128]{2,1,0:T(8,128)(2,1)S(1)} %sort_left.1.refs_1_.refs_0_, bf16[256,128]{1,0:T(8,128)(2,1)S(1)} %get-tuple-element.54.refs_1_, bf16[256,128]{1,0:T(8,128)(2,1)S(1)} %collective-permute-done.11.refs_2_, ...), custom_call_target="tpu_custom_call" | custom-call | flops 33554432 | bytes 1835008 | tf_op jit(solution)/shard_map/d_right/pallas_call | solution.py:65
  43.6 4.0 %all-to-all-start.1 = ((bf16[8,256,128]{2,1,0:T(8,128)(2,1)}), bf16[8,256,128]{2,1,0:T(8,128)(2,1)S(1)}, u32[]{:S(2)}, u32[]{:S(2)}) async-start(bf16[8,256,128]{2,1,0:T(8,128)(2,1)} %get-tuple-element.58.refs_0_), calls=%async_computation.1 | async-start | bytes 1048576 | tf_op jit(solution)/shard_map/all_to_all | solution.py:403
  49.2 1.7 %collective-permute-start.15 = (bf16[256,128]{1,0:T(8,128)(2,1)S(1)}, bf16[256,128]{1,0:T(8,128)(2,1)S(1)}, u32[]{:S(2)}, u32[]{:S(2)}) collective-permute-start(bf16[256,128]{1,0:T(8,128)(2,1)S(1)} %get-tuple-element.63), channel_id=1, source_target_pairs={{0,2},{1,3},{2,0},{3,1},{4,6},{5,7},{6,4},{7,5},{8,10},{9,11},{10,... | collective-permute-start | bytes 196616 | tf_op jit(solution)/shard_map/ppermute | solution.py:410
  50.8 1.8 %collective-permute-start.16 = (bf16[256,128]{1,0:T(8,128)(2,1)S(1)}, bf16[256,128]{1,0:T(8,128)(2,1)S(1)}, u32[]{:S(2)}, u32[]{:S(2)}) collective-permute-start(bf16[256,128]{1,0:T(8,128)(2,1)S(1)} %get-tuple-element.64), channel_id=1, source_target_pairs={{0,6},{1,7},{2,4},{3,5},{4,2},{5,3},{6,0},{7,1},{8,14},{9,15},{10,... | collective-permute-start | bytes 196616 | tf_op jit(solution)/shard_map/ppermute | solution.py:410
  53.1 2.0 %collective-permute-start.17 = (bf16[256,128]{1,0:T(8,128)(2,1)S(1)}, bf16[256,128]{1,0:T(8,128)(2,1)S(1)}, u32[]{:S(2)}, u32[]{:S(2)}) collective-permute-start(bf16[256,128]{1,0:T(8,128)(2,1)S(1)} %get-tuple-element.65), channel_id=1, source_target_pairs={{0,7},{1,6},{2,5},{3,4},{4,3},{5,2},{6,1},{7,0},{8,15},{9,14},{10,... | collective-permute-start | bytes 196616 | tf_op jit(solution)/shard_map/ppermute | solution.py:410
  55.5 1.9 %collective-permute-done.15.refs_2_ = bf16[256,128]{1,0:T(8,128)(2,1)S(1)} collective-permute-done((bf16[256,128]{1,0:T(8,128)(2,1)S(1)}, bf16[256,128]{1,0:T(8,128)(2,1)S(1)}, u32[]{:S(2)}, u32[]{:S(2)}) %collective-permute-start.15) | collective-permute-done | bytes 65568 | tf_op jit(solution)/shard_map/ppermute | solution.py:410
  57.4 3.2 %collective-permute-start.19 = (bf16[256,128]{1,0:T(8,128)(2,1)S(1)}, bf16[256,128]{1,0:T(8,128)(2,1)S(1)}, u32[]{:S(2)}, u32[]{:S(2)}) collective-permute-start(bf16[256,128]{1,0:T(8,128)(2,1)S(1)} %get-tuple-element.67), channel_id=1, source_target_pairs={{0,5},{1,4},{2,7},{3,6},{4,1},{5,0},{6,3},{7,2},{8,13},{9,12},{10,... | collective-permute-start | bytes 196616 | tf_op jit(solution)/shard_map/ppermute | solution.py:410
  61.4 4.1 %collective-permute-done.18.refs_5_ = bf16[256,128]{1,0:T(8,128)(2,1)S(1)} collective-permute-done((bf16[256,128]{1,0:T(8,128)(2,1)S(1)}, bf16[256,128]{1,0:T(8,128)(2,1)S(1)}, u32[]{:S(2)}, u32[]{:S(2)}) %collective-permute-start.18) | collective-permute-done | bytes 65568 | tf_op jit(solution)/shard_map/ppermute | solution.py:410
  67.9 1.4 %finish.1 = bf16[8,128,128]{2,1,0:T(8,128)(2,1)} custom-call(bf16[8,256,128]{2,1,0:T(8,128)(2,1)S(1)} %all-to-all-done.1.refs_0_, bf16[8,256,128]{2,1,0:T(8,128)(2,1)S(1)} %sort_d_left.1.refs_1_, bf16[8,512,128]{2,1,0:T(8,128)(2,1)S(1)} %get-tuple-element.70.refs_2_, bf16[8,128,128]{2,1,0:T(8,128)(2,1)S(1)} %gate_back.1.refs_6_.refs_3_, ...), custom_call_target="tpu_custom_call" | custom-call | flops 134217728 | bytes 3117056 | tf_op jit(solution)/shard_map/finish/pallas_call | solution.py:65
  (63 shorter events, 13.4 us)
Async XLA Ops:
  2.5 25.8 %all-to-all-start = ((bf16[8,256,128]{2,1,0:T(8,128)(2,1)}), bf16[8,256,128]{2,1,0:T(8,128)(2,1)S(1)}, u32[]{:S(2)}, u32[]{:S(2)}) async-start(bf16[8,256,128]{2,1,0:T(8,128)(2,1)} %project_right.1.refs_5_.refs_7_), calls=%async_computation | async-start | bytes 1048576 | tf_op jit(solution)/shard_map/all_to_all | solution.py:403
  9.7 6.9 %collective-permute-start = (bf16[256,128]{1,0:T(8,128)(2,1)S(1)}, bf16[256,128]{1,0:T(8,128)(2,1)S(1)}, u32[]{:S(2)}, u32[]{:S(2)}) collective-permute-start(bf16[256,128]{1,0:T(8,128)(2,1)S(1)} %get-tuple-element.41), channel_id=1, source_target_pairs={{0,1},{1,0},{2,3},{3,2},{4,5},{5,4},{6,7},{7,6},{8,9},{9,8},{10,11... | collective-permute-start | bytes 196616 | tf_op jit(solution)/shard_map/ppermute | solution.py:410
  10.3 7.8 %collective-permute-start.1 = (bf16[256,128]{1,0:T(8,128)(2,1)S(1)}, bf16[256,128]{1,0:T(8,128)(2,1)S(1)}, u32[]{:S(2)}, u32[]{:S(2)}) collective-permute-start(bf16[256,128]{1,0:T(8,128)(2,1)S(1)} %get-tuple-element.42), channel_id=1, source_target_pairs={{0,2},{1,3},{2,0},{3,1},{4,6},{5,7},{6,4},{7,5},{8,10},{9,11},{10,... | collective-permute-start | bytes 196616 | tf_op jit(solution)/shard_map/ppermute | solution.py:410
  12.0 9.4 %collective-permute-start.2 = (bf16[256,128]{1,0:T(8,128)(2,1)S(1)}, bf16[256,128]{1,0:T(8,128)(2,1)S(1)}, u32[]{:S(2)}, u32[]{:S(2)}) collective-permute-start(bf16[256,128]{1,0:T(8,128)(2,1)S(1)} %get-tuple-element.43), channel_id=1, source_target_pairs={{0,6},{1,7},{2,4},{3,5},{4,2},{5,3},{6,0},{7,1},{8,14},{9,15},{10,... | collective-permute-start | bytes 196616 | tf_op jit(solution)/shard_map/ppermute | solution.py:410
  14.3 14.0 %collective-permute-start.7 = (bf16[512,128]{1,0:T(8,128)(2,1)S(1)}, bf16[512,128]{1,0:T(8,128)(2,1)S(1)}, u32[]{:S(2)}, u32[]{:S(2)}) collective-permute-start(bf16[512,128]{1,0:T(8,128)(2,1)S(1)} %get-tuple-element.49), channel_id=1, source_target_pairs={{0,4},{1,5},{2,6},{3,7},{4,0},{5,1},{6,2},{7,3},{8,12},{9,13},{10,... | collective-permute-start | bytes 393224 | tf_op jit(solution)/shard_map/ppermute | solution.py:410
  15.2 10.2 %collective-permute-start.3 = (bf16[256,128]{1,0:T(8,128)(2,1)S(1)}, bf16[256,128]{1,0:T(8,128)(2,1)S(1)}, u32[]{:S(2)}, u32[]{:S(2)}) collective-permute-start(bf16[256,128]{1,0:T(8,128)(2,1)S(1)} %get-tuple-element.44), channel_id=1, source_target_pairs={{0,7},{1,6},{2,5},{3,4},{4,3},{5,2},{6,1},{7,0},{8,15},{9,14},{10,... | collective-permute-start | bytes 196616 | tf_op jit(solution)/shard_map/ppermute | solution.py:410
  16.6 10.8 %collective-permute-start.4 = (bf16[256,128]{1,0:T(8,128)(2,1)S(1)}, bf16[256,128]{1,0:T(8,128)(2,1)S(1)}, u32[]{:S(2)}, u32[]{:S(2)}) collective-permute-start(bf16[256,128]{1,0:T(8,128)(2,1)S(1)} %get-tuple-element.45), channel_id=1, source_target_pairs={{0,4},{1,5},{2,6},{3,7},{4,0},{5,1},{6,2},{7,3},{8,12},{9,13},{10,... | collective-permute-start | bytes 196616 | tf_op jit(solution)/shard_map/ppermute | solution.py:410
  18.1 9.5 %collective-permute-start.5 = (bf16[256,128]{1,0:T(8,128)(2,1)S(1)}, bf16[256,128]{1,0:T(8,128)(2,1)S(1)}, u32[]{:S(2)}, u32[]{:S(2)}) collective-permute-start(bf16[256,128]{1,0:T(8,128)(2,1)S(1)} %get-tuple-element.46), channel_id=1, source_target_pairs={{0,5},{1,4},{2,7},{3,6},{4,1},{5,0},{6,3},{7,2},{8,13},{9,12},{10,... | collective-permute-start | bytes 196616 | tf_op jit(solution)/shard_map/ppermute | solution.py:410
  21.3 6.3 %collective-permute-start.6 = (bf16[256,128]{1,0:T(8,128)(2,1)S(1)}, bf16[256,128]{1,0:T(8,128)(2,1)S(1)}, u32[]{:S(2)}, u32[]{:S(2)}) collective-permute-start(bf16[256,128]{1,0:T(8,128)(2,1)S(1)} %get-tuple-element.47), channel_id=1, source_target_pairs={{0,3},{1,2},{2,1},{3,0},{4,7},{5,6},{6,5},{7,4},{8,11},{9,10},{10,... | collective-permute-start | bytes 196616 | tf_op jit(solution)/shard_map/ppermute | solution.py:410
  29.5 4.5 %collective-permute-start.8 = (bf16[256,128]{1,0:T(8,128)(2,1)S(1)}, bf16[256,128]{1,0:T(8,128)(2,1)S(1)}, u32[]{:S(2)}, u32[]{:S(2)}) collective-permute-start(bf16[256,128]{1,0:T(8,128)(2,1)S(1)} %get-tuple-element.51), channel_id=1, source_target_pairs={{0,2},{1,3},{2,0},{3,1},{4,6},{5,7},{6,4},{7,5},{8,10},{9,11},{10,... | collective-permute-start | bytes 196616 | tf_op jit(solution)/shard_map/ppermute | solution.py:410
  31.2 4.1 %collective-permute-start.9 = (bf16[256,128]{1,0:T(8,128)(2,1)S(1)}, bf16[256,128]{1,0:T(8,128)(2,1)S(1)}, u32[]{:S(2)}, u32[]{:S(2)}) collective-permute-start(bf16[256,128]{1,0:T(8,128)(2,1)S(1)} %get-tuple-element.52), channel_id=1, source_target_pairs={{0,3},{1,2},{2,1},{3,0},{4,7},{5,6},{6,5},{7,4},{8,11},{9,10},{10,... | collective-permute-start | bytes 196616 | tf_op jit(solution)/shard_map/ppermute | solution.py:410
  31.4 3.9 %collective-permute-start.10 = (bf16[256,128]{1,0:T(8,128)(2,1)S(1)}, bf16[256,128]{1,0:T(8,128)(2,1)S(1)}, u32[]{:S(2)}, u32[]{:S(2)}) collective-permute-start(bf16[256,128]{1,0:T(8,128)(2,1)S(1)} %get-tuple-element.53), channel_id=1, source_target_pairs={{0,1},{1,0},{2,3},{3,2},{4,5},{5,4},{6,7},{7,6},{8,9},{9,8},{10,11... | collective-permute-start | bytes 196616 | tf_op jit(solution)/shard_map/ppermute | solution.py:410
  35.6 4.3 %collective-permute-start.11 = (bf16[256,128]{1,0:T(8,128)(2,1)S(1)}, bf16[256,128]{1,0:T(8,128)(2,1)S(1)}, u32[]{:S(2)}, u32[]{:S(2)}) collective-permute-start(bf16[256,128]{1,0:T(8,128)(2,1)S(1)} %get-tuple-element.55), channel_id=1, source_target_pairs={{0,2},{1,3},{2,0},{3,1},{4,6},{5,7},{6,4},{7,5},{8,10},{9,11},{10,... | collective-permute-start | bytes 196616 | tf_op jit(solution)/shard_map/ppermute | solution.py:410
  37.2 4.3 %collective-permute-start.12 = (bf16[256,128]{1,0:T(8,128)(2,1)S(1)}, bf16[256,128]{1,0:T(8,128)(2,1)S(1)}, u32[]{:S(2)}, u32[]{:S(2)}) collective-permute-start(bf16[256,128]{1,0:T(8,128)(2,1)S(1)} %get-tuple-element.56), channel_id=1, source_target_pairs={{0,3},{1,2},{2,1},{3,0},{4,7},{5,6},{6,5},{7,4},{8,11},{9,10},{10,... | collective-permute-start | bytes 196616 | tf_op jit(solution)/shard_map/ppermute | solution.py:410
  37.2 4.3 %collective-permute-start.13 = (bf16[256,128]{1,0:T(8,128)(2,1)S(1)}, bf16[256,128]{1,0:T(8,128)(2,1)S(1)}, u32[]{:S(2)}, u32[]{:S(2)}) collective-permute-start(bf16[256,128]{1,0:T(8,128)(2,1)S(1)} %get-tuple-element.57), channel_id=1, source_target_pairs={{0,1},{1,0},{2,3},{3,2},{4,5},{5,4},{6,7},{7,6},{8,9},{9,8},{10,11... | collective-permute-start | bytes 196616 | tf_op jit(solution)/shard_map/ppermute | solution.py:410
  43.6 24.3 %all-to-all-start.1 = ((bf16[8,256,128]{2,1,0:T(8,128)(2,1)}), bf16[8,256,128]{2,1,0:T(8,128)(2,1)S(1)}, u32[]{:S(2)}, u32[]{:S(2)}) async-start(bf16[8,256,128]{2,1,0:T(8,128)(2,1)} %get-tuple-element.58.refs_0_), calls=%async_computation.1 | async-start | bytes 1048576 | tf_op jit(solution)/shard_map/all_to_all | solution.py:403
  48.6 6.6 %collective-permute-start.14 = (bf16[256,128]{1,0:T(8,128)(2,1)S(1)}, bf16[256,128]{1,0:T(8,128)(2,1)S(1)}, u32[]{:S(2)}, u32[]{:S(2)}) collective-permute-start(bf16[256,128]{1,0:T(8,128)(2,1)S(1)} %get-tuple-element.62), channel_id=1, source_target_pairs={{0,1},{1,0},{2,3},{3,2},{4,5},{5,4},{6,7},{7,6},{8,9},{9,8},{10,11... | collective-permute-start | bytes 196616 | tf_op jit(solution)/shard_map/ppermute | solution.py:410
  49.2 8.2 %collective-permute-start.15 = (bf16[256,128]{1,0:T(8,128)(2,1)S(1)}, bf16[256,128]{1,0:T(8,128)(2,1)S(1)}, u32[]{:S(2)}, u32[]{:S(2)}) collective-permute-start(bf16[256,128]{1,0:T(8,128)(2,1)S(1)} %get-tuple-element.63), channel_id=1, source_target_pairs={{0,2},{1,3},{2,0},{3,1},{4,6},{5,7},{6,4},{7,5},{8,10},{9,11},{10,... | collective-permute-start | bytes 196616 | tf_op jit(solution)/shard_map/ppermute | solution.py:410
  50.8 9.8 %collective-permute-start.16 = (bf16[256,128]{1,0:T(8,128)(2,1)S(1)}, bf16[256,128]{1,0:T(8,128)(2,1)S(1)}, u32[]{:S(2)}, u32[]{:S(2)}) collective-permute-start(bf16[256,128]{1,0:T(8,128)(2,1)S(1)} %get-tuple-element.64), channel_id=1, source_target_pairs={{0,6},{1,7},{2,4},{3,5},{4,2},{5,3},{6,0},{7,1},{8,14},{9,15},{10,... | collective-permute-start | bytes 196616 | tf_op jit(solution)/shard_map/ppermute | solution.py:410
  52.9 12.8 %collective-permute-start.21 = (bf16[512,128]{1,0:T(8,128)(2,1)S(1)}, bf16[512,128]{1,0:T(8,128)(2,1)S(1)}, u32[]{:S(2)}, u32[]{:S(2)}) collective-permute-start(bf16[512,128]{1,0:T(8,128)(2,1)S(1)} %pack_tri.1), channel_id=1, source_target_pairs={{0,4},{1,5},{2,6},{3,7},{4,0},{5,1},{6,2},{7,3},{8,12},{9,13},{10,... | collective-permute-start | bytes 393224 | tf_op jit(solution)/shard_map/ppermute | solution.py:410
  53.1 8.3 %collective-permute-start.17 = (bf16[256,128]{1,0:T(8,128)(2,1)S(1)}, bf16[256,128]{1,0:T(8,128)(2,1)S(1)}, u32[]{:S(2)}, u32[]{:S(2)}) collective-permute-start(bf16[256,128]{1,0:T(8,128)(2,1)S(1)} %get-tuple-element.65), channel_id=1, source_target_pairs={{0,7},{1,6},{2,5},{3,4},{4,3},{5,2},{6,1},{7,0},{8,15},{9,14},{10,... | collective-permute-start | bytes 196616 | tf_op jit(solution)/shard_map/ppermute | solution.py:410
  55.2 10.4 %collective-permute-start.18 = (bf16[256,128]{1,0:T(8,128)(2,1)S(1)}, bf16[256,128]{1,0:T(8,128)(2,1)S(1)}, u32[]{:S(2)}, u32[]{:S(2)}) collective-permute-start(bf16[256,128]{1,0:T(8,128)(2,1)S(1)} %get-tuple-element.66), channel_id=1, source_target_pairs={{0,4},{1,5},{2,6},{3,7},{4,0},{5,1},{6,2},{7,3},{8,12},{9,13},{10,... | collective-permute-start | bytes 196616 | tf_op jit(solution)/shard_map/ppermute | solution.py:410
  57.4 8.2 %collective-permute-start.19 = (bf16[256,128]{1,0:T(8,128)(2,1)S(1)}, bf16[256,128]{1,0:T(8,128)(2,1)S(1)}, u32[]{:S(2)}, u32[]{:S(2)}) collective-permute-start(bf16[256,128]{1,0:T(8,128)(2,1)S(1)} %get-tuple-element.67), channel_id=1, source_target_pairs={{0,5},{1,4},{2,7},{3,6},{4,1},{5,0},{6,3},{7,2},{8,13},{9,12},{10,... | collective-permute-start | bytes 196616 | tf_op jit(solution)/shard_map/ppermute | solution.py:410
  60.6 5.0 %collective-permute-start.20 = (bf16[256,128]{1,0:T(8,128)(2,1)S(1)}, bf16[256,128]{1,0:T(8,128)(2,1)S(1)}, u32[]{:S(2)}, u32[]{:S(2)}) collective-permute-start(bf16[256,128]{1,0:T(8,128)(2,1)S(1)} %get-tuple-element.68), channel_id=1, source_target_pairs={{0,3},{1,2},{2,1},{3,0},{4,7},{5,6},{6,5},{7,4},{8,11},{9,10},{10,... | collective-permute-start | bytes 196616 | tf_op jit(solution)/shard_map/ppermute | solution.py:410
  (13 other events, 72.2 us)

commit v23 on v16

--- a/solution.py
+++ b/solution.py
@@ -95,7 +95,8 @@
     order = []
     for place in range(count):
         if back:
-            order += [place ^ (count // 2), count + place]
+            inner = place ^ (count // 2)
+            order += [inner if place < count // 2 else inner ^ 2, count + place]
         else:
             order += [count + (place ^ 2), place ^ (count // 2)]
     return order

time: 62.7 us -> 63.7 us (1.016)
  starting transfers between devices: 24.7 us -> 25.7 us
    ppermute x14, starting transfers between devices: 11.3 us -> 12.2 us  [swap_pieces(): lax.ppermute(pieces[step], 'row', [(d, d ^ distance(step, count)) for d i...]
    all_to_all x2, waiting for transfers between devices: 0.45 us -> 1.36 us  [swap(): lax.all_to_all(values, 'row', split_axis=0, concat_axis=0, tiled=True, ax...]
    ppermute x14, waiting for transfers between devices: 8.39 us -> 7.51 us  [swap_pieces(): lax.ppermute(pieces[step], 'row', [(d, d ^ distance(step, count)) for d i...]
  transfers between devices with their start and end apart: 16 -> 16, of which waited for: 10 -> 9; matrix products, arithmetic and copies ran while one was open for 0% -> 0% of each run, Pallas kernels for 6% -> 6%
where the time goes in v23:
time: 63.7 us; the launch traced here: 63.3 us
  starting transfers between devices  25.7 us (40%)
  blocking collectives  17.3 us (27%)
  Pallas kernels  9.82 us (15%)
  waiting for transfers between devices  8.87 us (14%)
  local copies, waits for them, and re-layouts  1.34 us (2%)
    all_to_all x2, blocking collectives, swap_half(): lax.all_to_all(values, 'row', split_axis=0, concat_axis=0, tiled=True, ax...  17.3 us
    all_to_all x2, starting transfers between devices, swap(): lax.all_to_all(values, 'row', split_axis=0, concat_axis=0, tiled=True, ax...  13.4 us
    ppermute x14, starting transfers between devices, swap_pieces(): lax.ppermute(pieces[step], 'row', [(d, d ^ distance(step, count)) for d i...  12.2 us
    pallas_call x12, Pallas kernels, call(): pl.pallas_call(body, name=name, out_shape=outs, in_specs=[pl.BlockSpec(me...  9.82 us
    ppermute x14, waiting for transfers between devices, swap_pieces(): lax.ppermute(pieces[step], 'row', [(d, d ^ distance(step, count)) for d i...  7.51 us
    all_to_all x2, waiting for transfers between devices, swap(): lax.all_to_all(values, 'row', split_axis=0, concat_axis=0, tiled=True, ax...  1.36 us
    unnamed x22, local copies, waits for them, and re-layouts  1.34 us
  transfers between devices with their start and end apart: 16, of which 9 were waited for; matrix products, arithmetic and copies ran while one was open for 0% of the time, Pallas kernels for 6%

profile of v23, /device:TPU:0, one launch (start us, length us, event | category | flops | bytes accessed | tf_op | source)
XLA Modules:
  0.0 63.3 jit_solution(8799724879238157467)
XLA Ops:
  0.0 2.4 %project_right.1.refs_5_ = bf16[16,128,128]{2,1,0:T(8,128)(2,1)} custom-call(bf16[8,128,128]{2,1,0:T(8,128)(2,1)} %refs_0_.7, s32[1,128]{1,0:T(1,128)} %bitcast.13, f32[1,128]{1,0:T(1,128)} %bitcast.5, f32[1,128]{1,0:T(1,128)} %bitcast.9, bf16[128,512]{1,0:T(8,128)(2,1)} %refs_4_.9), custom_call_target="tpu_custom_call" | custom-call | flops 67108864 | bytes 919040 | tf_op jit(solution)/shard_map/project_right/pallas_call | solution.py:65
  2.5 8.5 %all-to-all-start = ((bf16[16,128,128]{2,1,0:T(8,128)(2,1)}), bf16[16,128,128]{2,1,0:T(8,128)(2,1)S(1)}, u32[]{:S(2)}, u32[]{:S(2)}) async-start(bf16[16,128,128]{2,1,0:T(8,128)(2,1)} %project_right.1.refs_5_), calls=%async_computation | async-start | bytes 1048576 | tf_op jit(solution)/shard_map/all_to_all | solution.py:320
  11.1 0.8 %project_left.1 = (bf16[128,128]{1,0:T(8,128)(2,1)S(1)}, bf16[128,128]{1,0:T(8,128)(2,1)S(1)}, bf16[128,128]{1,0:T(8,128)(2,1)S(1)}, bf16[128,128]{1,0:T(8,128)(...) custom-call(bf16[8,128,128]{2,1,0:T(8,128)(2,1)S(1)} %copy-done.1, ...), custom_call_target="tpu_custom_call" | custom-call | flops 67108864 | bytes 1181184 | tf_op jit(solution)/shard_map/project_left/pallas_call | solution.py:65
  12.7 1.4 %collective-permute-start.2 = (bf16[128,128]{1,0:T(8,128)(2,1)S(1)}, bf16[128,128]{1,0:T(8,128)(2,1)S(1)}, u32[]{:S(2)}, u32[]{:S(2)}) collective-permute-start(bf16[128,128]{1,0:T(8,128)(2,1)S(1)} %get-tuple-element.35), channel_id=1, source_target_pairs={{0,6},{1,7},{2,4},{3,5},{4,2},{5,3},{6,0},{7,1},{8,14},{9,15},{10,... | collective-permute-start | bytes 98312 | tf_op jit(solution)/shard_map/ppermute | solution.py:337
  14.1 0.9 %collective-permute-start.3 = (bf16[128,128]{1,0:T(8,128)(2,1)S(1)}, bf16[128,128]{1,0:T(8,128)(2,1)S(1)}, u32[]{:S(2)}, u32[]{:S(2)}) collective-permute-start(bf16[128,128]{1,0:T(8,128)(2,1)S(1)} %get-tuple-element.36), channel_id=1, source_target_pairs={{0,7},{1,6},{2,5},{3,4},{4,3},{5,2},{6,1},{7,0},{8,15},{9,14},{10,... | collective-permute-start | bytes 98312 | tf_op jit(solution)/shard_map/ppermute | solution.py:337
  15.6 1.5 %collective-permute-start.5 = (bf16[128,128]{1,0:T(8,128)(2,1)S(1)}, bf16[128,128]{1,0:T(8,128)(2,1)S(1)}, u32[]{:S(2)}, u32[]{:S(2)}) collective-permute-start(bf16[128,128]{1,0:T(8,128)(2,1)S(1)} %get-tuple-element.38), channel_id=1, source_target_pairs={{0,5},{1,4},{2,7},{3,6},{4,1},{5,0},{6,3},{7,2},{8,13},{9,12},{10,... | collective-permute-start | bytes 98312 | tf_op jit(solution)/shard_map/ppermute | solution.py:337
  17.1 1.3 %collective-permute-done.1.refs_2_ = bf16[128,128]{1,0:T(8,128)(2,1)S(1)} collective-permute-done((bf16[128,128]{1,0:T(8,128)(2,1)S(1)}, bf16[128,128]{1,0:T(8,128)(2,1)S(1)}, u32[]{:S(2)}, u32[]{:S(2)}) %collective-permute-start.1) | collective-permute-done | bytes 32800 | tf_op jit(solution)/shard_map/ppermute | solution.py:337
  19.1 0.8 %prepare.1 = (f32[8,128,128]{2,1,0:T(8,128)S(1)}, f32[8,128,128]{2,1,0:T(8,128)S(1)}) custom-call(bf16[8,128,128]{2,1,0:T(8,128)(2,1)S(1)} %copy-done.1, bf16[8,128,128]{2,1,0:T(8,128)(2,1)S(1)} %copy-done.3, f32[1,128]{1,0:T(1,128)S(1)} %bitcast.7, f32[1,128]{1,0:T(1,128)S(1)} %bitcast.11, bf16[128,128]{1,0:T(8,128)(2,1)S(1)} %copy-done.5, ...), custom_call_target="tpu_custom_call" | custom-call | flops 67108864 | bytes 1639936 | tf_op jit(solution)/shard_map/prepare/pallas_call | solution.py:65
  19.9 1.5 %collective-permute-done.2.refs_3_ = bf16[128,128]{1,0:T(8,128)(2,1)S(1)} collective-permute-done((bf16[128,128]{1,0:T(8,128)(2,1)S(1)}, bf16[128,128]{1,0:T(8,128)(2,1)S(1)}, u32[]{:S(2)}, u32[]{:S(2)}) %collective-permute-start.2) | collective-permute-done | bytes 32800 | tf_op jit(solution)/shard_map/ppermute | solution.py:337
  21.3 0.7 %collective-permute-done.3.refs_4_ = bf16[128,128]{1,0:T(8,128)(2,1)S(1)} collective-permute-done((bf16[128,128]{1,0:T(8,128)(2,1)S(1)}, bf16[128,128]{1,0:T(8,128)(2,1)S(1)}, u32[]{:S(2)}, u32[]{:S(2)}) %collective-permute-start.3) | collective-permute-done | bytes 32800 | tf_op jit(solution)/shard_map/ppermute | solution.py:337
  22.0 1.5 %collective-permute-done.4.refs_5_ = bf16[128,128]{1,0:T(8,128)(2,1)S(1)} collective-permute-done((bf16[128,128]{1,0:T(8,128)(2,1)S(1)}, bf16[128,128]{1,0:T(8,128)(2,1)S(1)}, u32[]{:S(2)}, u32[]{:S(2)}) %collective-permute-start.4) | collective-permute-done | bytes 32800 | tf_op jit(solution)/shard_map/ppermute | solution.py:337
  24.5 8.7 %all_to_all.20.refs_0_ = bf16[8,128,128]{2,1,0:T(8,128)(2,1)S(1)} all-to-all(bf16[8,128,128]{2,1,0:T(8,128)(2,1)S(1)} %get-tuple-element.41), channel_id=1, replica_groups={{0,1,2,3,4,5,6,7},{8,9,10,11,12,13,14,15},{16,17,18,19,20,21,22,23},{24..., dimensions={0} | all-to-all | bytes 524288 | tf_op jit(solution)/shard_map/all_to_all | solution.py:328
  33.5 8.6 %all_to_all.21.refs_0_ = bf16[8,128,128]{2,1,0:T(8,128)(2,1)S(1)} all-to-all(bf16[8,128,128]{2,1,0:T(8,128)(2,1)S(1)} %middle.1), channel_id=1, replica_groups={{0,1,2,3,4,5,6,7},{8,9,10,11,12,13,14,15},{16,17,18,19,20,21,22,23},{24..., dimensions={0} | all-to-all | bytes 524288 | tf_op jit(solution)/shard_map/all_to_all | solution.py:328
  42.1 1.5 %d_right.1 = (bf16[16,128,128]{2,1,0:T(8,128)(2,1)}, bf16[16,64,128]{2,1,0:T(8,128)(2,1)S(1)}) custom-call(bf16[8,128,128]{2,1,0:T(8,128)(2,1)S(1)} %all_to_all.21.refs_0_, bf16[16,64,128]{2,1,0:T(8,128)(2,1)S(1)} %sort_left.1.refs_1_), custom_call_target="tpu_custom_call" | custom-call | flops 33554432 | bytes 1310720 | tf_op jit(solution)/shard_map/d_right/pallas_call | solution.py:65
  43.5 4.9 %all-to-all-start.3 = ((bf16[16,128,128]{2,1,0:T(8,128)(2,1)}), bf16[16,128,128]{2,1,0:T(8,128)(2,1)S(1)}, u32[]{:S(2)}, u32[]{:S(2)}) async-start(bf16[16,128,128]{2,1,0:T(8,128)(2,1)} %get-tuple-element.42), calls=%async_computation.3 | async-start | bytes 1048576 | tf_op jit(solution)/shard_map/all_to_all | solution.py:320
  49.0 1.4 %collective-permute-start.8 = (bf16[128,128]{1,0:T(8,128)(2,1)S(1)}, bf16[128,128]{1,0:T(8,128)(2,1)S(1)}, u32[]{:S(2)}, u32[]{:S(2)}) collective-permute-start(bf16[128,128]{1,0:T(8,128)(2,1)S(1)} %get-tuple-element.47), channel_id=1, source_target_pairs={{0,2},{1,3},{2,0},{3,1},{4,6},{5,7},{6,4},{7,5},{8,10},{9,11},{10,... | collective-permute-start | bytes 98312 | tf_op jit(solution)/shard_map/ppermute | solution.py:337
  50.8 2.0 %collective-permute-start.10 = (bf16[128,128]{1,0:T(8,128)(2,1)S(1)}, bf16[128,128]{1,0:T(8,128)(2,1)S(1)}, u32[]{:S(2)}, u32[]{:S(2)}) collective-permute-start(bf16[128,128]{1,0:T(8,128)(2,1)S(1)} %get-tuple-element.49), channel_id=1, source_target_pairs={{0,7},{1,6},{2,5},{3,4},{4,3},{5,2},{6,1},{7,0},{8,15},{9,14},{10,... | collective-permute-start | bytes 98312 | tf_op jit(solution)/shard_map/ppermute | solution.py:337
  53.3 1.5 %collective-permute-start.12 = (bf16[128,128]{1,0:T(8,128)(2,1)S(1)}, bf16[128,128]{1,0:T(8,128)(2,1)S(1)}, u32[]{:S(2)}, u32[]{:S(2)}) collective-permute-start(bf16[128,128]{1,0:T(8,128)(2,1)S(1)} %get-tuple-element.51), channel_id=1, source_target_pairs={{0,5},{1,4},{2,7},{3,6},{4,1},{5,0},{6,3},{7,2},{8,13},{9,12},{10,... | collective-permute-start | bytes 98312 | tf_op jit(solution)/shard_map/ppermute | solution.py:337
  54.8 1.0 %collective-permute-start.13 = (bf16[128,128]{1,0:T(8,128)(2,1)S(1)}, bf16[128,128]{1,0:T(8,128)(2,1)S(1)}, u32[]{:S(2)}, u32[]{:S(2)}) collective-permute-start(bf16[128,128]{1,0:T(8,128)(2,1)S(1)} %get-tuple-element.52), channel_id=1, source_target_pairs={{0,3},{1,2},{2,1},{3,0},{4,7},{5,6},{6,5},{7,4},{8,11},{9,10},{10,... | collective-permute-start | bytes 98312 | tf_op jit(solution)/shard_map/ppermute | solution.py:337
  56.9 1.0 %slopes.1 = (bf16[8,512,128]{2,1,0:T(8,128)(2,1)S(1)}, bf16[8,128,128]{2,1,0:T(8,128)(2,1)S(1)}, f32[8,128]{1,0:T(8,128)S(1)}, f32[128,128]{1,0:T(8,128)S(1)}, bf16[128,640]{1,0:T(8,128)(2,1)S(1)}) custom-call(bf16[8,128,128]{2,1,0:T(8,128)(2,1)S(1)} %copy-done.1, s32[1,128]{1,0:T(1,128)S(1)} %bitcast.15, f32[1,128]{1,0:T(1,128)S(1)} %bitcast.8, ...), custom_call_target="tpu_custom_call" | custom-call | flops 134217728 | bytes 2233856 | tf_op jit(solution)/shard_map/slopes/pallas_call | solution.py:65
  58.0 0.9 %collective-permute-done.9.refs_3_ = bf16[128,128]{1,0:T(8,128)(2,1)S(1)} collective-permute-done((bf16[128,128]{1,0:T(8,128)(2,1)S(1)}, bf16[128,128]{1,0:T(8,128)(2,1)S(1)}, u32[]{:S(2)}, u32[]{:S(2)}) %collective-permute-start.9) | collective-permute-done | bytes 32800 | tf_op jit(solution)/shard_map/ppermute | solution.py:337
  58.8 0.7 %collective-permute-done.10.refs_4_ = bf16[128,128]{1,0:T(8,128)(2,1)S(1)} collective-permute-done((bf16[128,128]{1,0:T(8,128)(2,1)S(1)}, bf16[128,128]{1,0:T(8,128)(2,1)S(1)}, u32[]{:S(2)}, u32[]{:S(2)}) %collective-permute-start.10) | collective-permute-done | bytes 32800 | tf_op jit(solution)/shard_map/ppermute | solution.py:337
  60.5 1.4 %all-to-all-done.3.refs_0_ = bf16[16,128,128]{2,1,0:T(8,128)(2,1)S(1)} async-done(((bf16[16,128,128]{2,1,0:T(8,128)(2,1)}), bf16[16,128,128]{2,1,0:T(8,128)(2,1)S(1)}, u32[]{:S(2)}, u32[]{:S(2)}) %all-to-all-start.3) | async-done | bytes 524320 | tf_op jit(solution)/shard_map/all_to_all | solution.py:320
  61.9 1.4 %finish.1 = bf16[8,128,128]{2,1,0:T(8,128)(2,1)} custom-call(bf16[16,128,128]{2,1,0:T(8,128)(2,1)S(1)} %all-to-all-done.3.refs_0_, bf16[8,128,128]{2,1,0:T(8,128)(2,1)S(1)} %sort_d_left.1.refs_1_, bf16[8,512,128]{2,1,0:T(8,128)(2,1)S(1)} %get-tuple-element.54.refs_2_, bf16[8,128,128]{2,1,0:T(8,128)(2,1)S(1)} %gate_back.1.refs_6_.refs_3_, ...), custom_call_target="tpu_custom_call" | custom-call | flops 134217728 | bytes 2854912 | tf_op jit(solution)/shard_map/finish/pallas_call | solution.py:65
  (44 shorter events, 6.7 us)
Async XLA Ops:
  2.4 8.6 %copy-start = (bf16[16,128,128]{2,1,0:T(8,128)(2,1)S(1)}, bf16[16,128,128]{2,1,0:T(8,128)(2,1)}, u32[]{:S(2)}) copy-start(bf16[16,128,128]{2,1,0:T(8,128)(2,1)} %project_right.1.refs_5_) | copy-start | bytes 1572868
  2.4 8.6 %copy-start.1 = (bf16[8,128,128]{2,1,0:T(8,128)(2,1)S(1)}, bf16[8,128,128]{2,1,0:T(8,128)(2,1)}, u32[]{:S(2)}) copy-start(bf16[8,128,128]{2,1,0:T(8,128)(2,1)} %refs_0_.7) | copy-start | bytes 786436
  2.4 8.6 %copy-start.2 = (bf16[128,512]{1,0:T(8,128)(2,1)S(1)}, bf16[128,512]{1,0:T(8,128)(2,1)}, u32[]{:S(2)}) copy-start(bf16[128,512]{1,0:T(8,128)(2,1)} %refs_4_.9) | copy-start | bytes 393220
  2.4 8.6 %copy-start.6 = (f32[128]{0:T(128)S(1)}, f32[128]{0:T(128)}, u32[]{:S(2)}) copy-start(f32[128]{0:T(128)} %param.13) | copy-start | bytes 1540
  2.4 8.6 %copy-start.7 = (f32[128]{0:T(128)S(1)}, f32[128]{0:T(128)}, u32[]{:S(2)}) copy-start(f32[128]{0:T(128)} %param.14) | copy-start | bytes 1540
  2.5 8.6 %copy-start.8 = (s32[128]{0:T(128)S(1)}, s32[128]{0:T(128)}, u32[]{:S(2)}) copy-start(s32[128]{0:T(128)} %param.12) | copy-start | bytes 1540
  2.5 21.3 %all-to-all-start = ((bf16[16,128,128]{2,1,0:T(8,128)(2,1)}), bf16[16,128,128]{2,1,0:T(8,128)(2,1)S(1)}, u32[]{:S(2)}, u32[]{:S(2)}) async-start(bf16[16,128,128]{2,1,0:T(8,128)(2,1)} %project_right.1.refs_5_), calls=%async_computation | async-start | bytes 1048576 | tf_op jit(solution)/shard_map/all_to_all | solution.py:320
  11.0 7.4 %copy-start.3 = (bf16[8,128,128]{2,1,0:T(8,128)(2,1)S(1)}, bf16[8,128,128]{2,1,0:T(8,128)(2,1)}, u32[]{:S(2)}) copy-start(bf16[8,128,128]{2,1,0:T(8,128)(2,1)} %refs_1_.1) | copy-start | bytes 786436
  11.1 7.3 %copy-start.4 = (bf16[128,128]{1,0:T(8,128)(2,1)S(1)}, bf16[128,128]{1,0:T(8,128)(2,1)}, u32[]{:S(2)}) copy-start(bf16[128,128]{1,0:T(8,128)(2,1)} %refs_4_.8) | copy-start | bytes 98308
  11.9 3.7 %collective-permute-start = (bf16[128,128]{1,0:T(8,128)(2,1)S(1)}, bf16[128,128]{1,0:T(8,128)(2,1)S(1)}, u32[]{:S(2)}, u32[]{:S(2)}) collective-permute-start(bf16[128,128]{1,0:T(8,128)(2,1)S(1)} %get-tuple-element.33), channel_id=1, source_target_pairs={{0,1},{1,0},{2,3},{3,2},{4,5},{5,4},{6,7},{7,6},{8,9},{9,8},{10,11... | collective-permute-start | bytes 98312 | tf_op jit(solution)/shard_map/ppermute | solution.py:337
  12.1 6.3 %collective-permute-start.1 = (bf16[128,128]{1,0:T(8,128)(2,1)S(1)}, bf16[128,128]{1,0:T(8,128)(2,1)S(1)}, u32[]{:S(2)}, u32[]{:S(2)}) collective-permute-start(bf16[128,128]{1,0:T(8,128)(2,1)S(1)} %get-tuple-element.34), channel_id=1, source_target_pairs={{0,2},{1,3},{2,0},{3,1},{4,6},{5,7},{6,4},{7,5},{8,10},{9,11},{10,... | collective-permute-start | bytes 98312 | tf_op jit(solution)/shard_map/ppermute | solution.py:337
  12.7 8.6 %collective-permute-start.2 = (bf16[128,128]{1,0:T(8,128)(2,1)S(1)}, bf16[128,128]{1,0:T(8,128)(2,1)S(1)}, u32[]{:S(2)}, u32[]{:S(2)}) collective-permute-start(bf16[128,128]{1,0:T(8,128)(2,1)S(1)} %get-tuple-element.35), channel_id=1, source_target_pairs={{0,6},{1,7},{2,4},{3,5},{4,2},{5,3},{6,0},{7,1},{8,14},{9,15},{10,... | collective-permute-start | bytes 98312 | tf_op jit(solution)/shard_map/ppermute | solution.py:337
  14.1 8.0 %collective-permute-start.3 = (bf16[128,128]{1,0:T(8,128)(2,1)S(1)}, bf16[128,128]{1,0:T(8,128)(2,1)S(1)}, u32[]{:S(2)}, u32[]{:S(2)}) collective-permute-start(bf16[128,128]{1,0:T(8,128)(2,1)S(1)} %get-tuple-element.36), channel_id=1, source_target_pairs={{0,7},{1,6},{2,5},{3,4},{4,3},{5,2},{6,1},{7,0},{8,15},{9,14},{10,... | collective-permute-start | bytes 98312 | tf_op jit(solution)/shard_map/ppermute | solution.py:337
  15.0 8.6 %collective-permute-start.4 = (bf16[128,128]{1,0:T(8,128)(2,1)S(1)}, bf16[128,128]{1,0:T(8,128)(2,1)S(1)}, u32[]{:S(2)}, u32[]{:S(2)}) collective-permute-start(bf16[128,128]{1,0:T(8,128)(2,1)S(1)} %get-tuple-element.37), channel_id=1, source_target_pairs={{0,4},{1,5},{2,6},{3,7},{4,0},{5,1},{6,2},{7,3},{8,12},{9,13},{10,... | collective-permute-start | bytes 98312 | tf_op jit(solution)/shard_map/ppermute | solution.py:337
  15.6 8.0 %collective-permute-start.5 = (bf16[128,128]{1,0:T(8,128)(2,1)S(1)}, bf16[128,128]{1,0:T(8,128)(2,1)S(1)}, u32[]{:S(2)}, u32[]{:S(2)}) collective-permute-start(bf16[128,128]{1,0:T(8,128)(2,1)S(1)} %get-tuple-element.38), channel_id=1, source_target_pairs={{0,5},{1,4},{2,7},{3,6},{4,1},{5,0},{6,3},{7,2},{8,13},{9,12},{10,... | collective-permute-start | bytes 98312 | tf_op jit(solution)/shard_map/ppermute | solution.py:337
  18.4 5.2 %collective-permute-start.6 = (bf16[128,128]{1,0:T(8,128)(2,1)S(1)}, bf16[128,128]{1,0:T(8,128)(2,1)S(1)}, u32[]{:S(2)}, u32[]{:S(2)}) collective-permute-start(bf16[128,128]{1,0:T(8,128)(2,1)S(1)} %get-tuple-element.39), channel_id=1, source_target_pairs={{0,3},{1,2},{2,1},{3,0},{4,7},{5,6},{6,5},{7,4},{8,11},{9,10},{10,... | collective-permute-start | bytes 98312 | tf_op jit(solution)/shard_map/ppermute | solution.py:337
  43.5 18.3 %all-to-all-start.3 = ((bf16[16,128,128]{2,1,0:T(8,128)(2,1)}), bf16[16,128,128]{2,1,0:T(8,128)(2,1)S(1)}, u32[]{:S(2)}, u32[]{:S(2)}) async-start(bf16[16,128,128]{2,1,0:T(8,128)(2,1)} %get-tuple-element.42), calls=%async_computation.3 | async-start | bytes 1048576 | tf_op jit(solution)/shard_map/all_to_all | solution.py:320
  48.8 4.5 %collective-permute-start.7 = (bf16[128,128]{1,0:T(8,128)(2,1)S(1)}, bf16[128,128]{1,0:T(8,128)(2,1)S(1)}, u32[]{:S(2)}, u32[]{:S(2)}) collective-permute-start(bf16[128,128]{1,0:T(8,128)(2,1)S(1)} %get-tuple-element.46), channel_id=1, source_target_pairs={{0,1},{1,0},{2,3},{3,2},{4,5},{5,4},{6,7},{7,6},{8,9},{9,8},{10,11... | collective-permute-start | bytes 98312 | tf_op jit(solution)/shard_map/ppermute | solution.py:337
  49.0 5.8 %collective-permute-start.8 = (bf16[128,128]{1,0:T(8,128)(2,1)S(1)}, bf16[128,128]{1,0:T(8,128)(2,1)S(1)}, u32[]{:S(2)}, u32[]{:S(2)}) collective-permute-start(bf16[128,128]{1,0:T(8,128)(2,1)S(1)} %get-tuple-element.47), channel_id=1, source_target_pairs={{0,2},{1,3},{2,0},{3,1},{4,6},{5,7},{6,4},{7,5},{8,10},{9,11},{10,... | collective-permute-start | bytes 98312 | tf_op jit(solution)/shard_map/ppermute | solution.py:337
  50.4 8.4 %collective-permute-start.9 = (bf16[128,128]{1,0:T(8,128)(2,1)S(1)}, bf16[128,128]{1,0:T(8,128)(2,1)S(1)}, u32[]{:S(2)}, u32[]{:S(2)}) collective-permute-start(bf16[128,128]{1,0:T(8,128)(2,1)S(1)} %get-tuple-element.48), channel_id=1, source_target_pairs={{0,6},{1,7},{2,4},{3,5},{4,2},{5,3},{6,0},{7,1},{8,14},{9,15},{10,... | collective-permute-start | bytes 98312 | tf_op jit(solution)/shard_map/ppermute | solution.py:337
  50.8 8.8 %collective-permute-start.10 = (bf16[128,128]{1,0:T(8,128)(2,1)S(1)}, bf16[128,128]{1,0:T(8,128)(2,1)S(1)}, u32[]{:S(2)}, u32[]{:S(2)}) collective-permute-start(bf16[128,128]{1,0:T(8,128)(2,1)S(1)} %get-tuple-element.49), channel_id=1, source_target_pairs={{0,7},{1,6},{2,5},{3,4},{4,3},{5,2},{6,1},{7,0},{8,15},{9,14},{10,... | collective-permute-start | bytes 98312 | tf_op jit(solution)/shard_map/ppermute | solution.py:337
  52.8 7.3 %collective-permute-start.11 = (bf16[128,128]{1,0:T(8,128)(2,1)S(1)}, bf16[128,128]{1,0:T(8,128)(2,1)S(1)}, u32[]{:S(2)}, u32[]{:S(2)}) collective-permute-start(bf16[128,128]{1,0:T(8,128)(2,1)S(1)} %get-tuple-element.50), channel_id=1, source_target_pairs={{0,4},{1,5},{2,6},{3,7},{4,0},{5,1},{6,2},{7,3},{8,12},{9,13},{10,... | collective-permute-start | bytes 98312 | tf_op jit(solution)/shard_map/ppermute | solution.py:337
  53.3 7.2 %collective-permute-start.12 = (bf16[128,128]{1,0:T(8,128)(2,1)S(1)}, bf16[128,128]{1,0:T(8,128)(2,1)S(1)}, u32[]{:S(2)}, u32[]{:S(2)}) collective-permute-start(bf16[128,128]{1,0:T(8,128)(2,1)S(1)} %get-tuple-element.51), channel_id=1, source_target_pairs={{0,5},{1,4},{2,7},{3,6},{4,1},{5,0},{6,3},{7,2},{8,13},{9,12},{10,... | collective-permute-start | bytes 98312 | tf_op jit(solution)/shard_map/ppermute | solution.py:337
  54.8 5.6 %collective-permute-start.13 = (bf16[128,128]{1,0:T(8,128)(2,1)S(1)}, bf16[128,128]{1,0:T(8,128)(2,1)S(1)}, u32[]{:S(2)}, u32[]{:S(2)}) collective-permute-start(bf16[128,128]{1,0:T(8,128)(2,1)S(1)} %get-tuple-element.52), channel_id=1, source_target_pairs={{0,3},{1,2},{2,1},{3,0},{4,7},{5,6},{6,5},{7,4},{8,11},{9,10},{10,... | collective-permute-start | bytes 98312 | tf_op jit(solution)/shard_map/ppermute | solution.py:337
  (3 other events, 8.7 us)

commit v24 on v16

--- a/solution.py
+++ b/solution.py
@@ -102,7 +102,7 @@
 
 
 def distance(step, count):
-    far = sorted(range(3, count), key=lambda apart: -(apart // 2))
+    far = sorted(range(3, count), key=lambda apart: apart < count // 2)
     return [*range(min(3, count)), *far][step]
 
 

time: 62.7 us -> 64.6 us (1.030)
  blocking collectives: 17.3 us -> 18.5 us
  waiting for transfers between devices: 8.85 us -> 9.6 us
    ppermute x14, waiting for transfers between devices: 8.39 us -> 9.59 us  [swap_pieces(): lax.ppermute(pieces[step], 'row', [(d, d ^ distance(step, count)) for d i...]
    all_to_all x2, blocking collectives: 17.3 us -> 18.5 us  [swap_half(): lax.all_to_all(values, 'row', split_axis=0, concat_axis=0, tiled=True, ax...]
  transfers between devices with their start and end apart: 16 -> 16, of which waited for: 10 -> 9; matrix products, arithmetic and copies ran while one was open for 0% -> 0% of each run, Pallas kernels for 6% -> 6%
where the time goes in v24:
time: 64.6 us; the launch traced here: 64.2 us
  starting transfers between devices  24.7 us (38%)
  blocking collectives  18.5 us (29%)
  Pallas kernels  9.82 us (15%)
  waiting for transfers between devices  9.6 us (15%)
  local copies, waits for them, and re-layouts  1.34 us (2%)
    all_to_all x2, blocking collectives, swap_half(): lax.all_to_all(values, 'row', split_axis=0, concat_axis=0, tiled=True, ax...  18.5 us
    all_to_all x2, starting transfers between devices, swap(): lax.all_to_all(values, 'row', split_axis=0, concat_axis=0, tiled=True, ax...  13.4 us
    ppermute x14, starting transfers between devices, swap_pieces(): lax.ppermute(pieces[step], 'row', [(d, d ^ distance(step, count)) for d i...  11.3 us
    pallas_call x12, Pallas kernels, call(): pl.pallas_call(body, name=name, out_shape=outs, in_specs=[pl.BlockSpec(me...  9.82 us
    ppermute x14, waiting for transfers between devices, swap_pieces(): lax.ppermute(pieces[step], 'row', [(d, d ^ distance(step, count)) for d i...  9.59 us
    unnamed x22, local copies, waits for them, and re-layouts  1.34 us
  transfers between devices with their start and end apart: 16, of which 9 were waited for; matrix products, arithmetic and copies ran while one was open for 0% of the time, Pallas kernels for 6%

profile of v24, /device:TPU:0, one launch (start us, length us, event | category | flops | bytes accessed | tf_op | source)
XLA Modules:
  0.0 64.2 jit_solution(16143066671447136536)
XLA Ops:
  0.0 2.4 %project_right.1.refs_5_ = bf16[16,128,128]{2,1,0:T(8,128)(2,1)} custom-call(bf16[8,128,128]{2,1,0:T(8,128)(2,1)} %refs_0_.7, s32[1,128]{1,0:T(1,128)} %bitcast.13, f32[1,128]{1,0:T(1,128)} %bitcast.5, f32[1,128]{1,0:T(1,128)} %bitcast.9, bf16[128,512]{1,0:T(8,128)(2,1)} %refs_4_.9), custom_call_target="tpu_custom_call" | custom-call | flops 67108864 | bytes 919040 | tf_op jit(solution)/shard_map/project_right/pallas_call | solution.py:65
  2.5 8.5 %all-to-all-start = ((bf16[16,128,128]{2,1,0:T(8,128)(2,1)}), bf16[16,128,128]{2,1,0:T(8,128)(2,1)S(1)}, u32[]{:S(2)}, u32[]{:S(2)}) async-start(bf16[16,128,128]{2,1,0:T(8,128)(2,1)} %project_right.1.refs_5_), calls=%async_computation | async-start | bytes 1048576 | tf_op jit(solution)/shard_map/all_to_all | solution.py:319
  11.1 0.8 %project_left.1 = (bf16[128,128]{1,0:T(8,128)(2,1)S(1)}, bf16[128,128]{1,0:T(8,128)(2,1)S(1)}, bf16[128,128]{1,0:T(8,128)(2,1)S(1)}, bf16[128,128]{1,0:T(8,128)(...) custom-call(bf16[8,128,128]{2,1,0:T(8,128)(2,1)S(1)} %copy-done.1, ...), custom_call_target="tpu_custom_call" | custom-call | flops 67108864 | bytes 1181184 | tf_op jit(solution)/shard_map/project_left/pallas_call | solution.py:65
  13.2 0.9 %collective-permute-start.3 = (bf16[128,128]{1,0:T(8,128)(2,1)S(1)}, bf16[128,128]{1,0:T(8,128)(2,1)S(1)}, u32[]{:S(2)}, u32[]{:S(2)}) collective-permute-start(bf16[128,128]{1,0:T(8,128)(2,1)S(1)} %get-tuple-element.36), channel_id=1, source_target_pairs={{0,5},{1,4},{2,7},{3,6},{4,1},{5,0},{6,3},{7,2},{8,13},{9,12},{10,... | collective-permute-start | bytes 98312 | tf_op jit(solution)/shard_map/ppermute | solution.py:336
  14.1 1.5 %collective-permute-start.4 = (bf16[128,128]{1,0:T(8,128)(2,1)S(1)}, bf16[128,128]{1,0:T(8,128)(2,1)S(1)}, u32[]{:S(2)}, u32[]{:S(2)}) collective-permute-start(bf16[128,128]{1,0:T(8,128)(2,1)S(1)} %get-tuple-element.37), channel_id=1, source_target_pairs={{0,6},{1,7},{2,4},{3,5},{4,2},{5,3},{6,0},{7,1},{8,14},{9,15},{10,... | collective-permute-start | bytes 98312 | tf_op jit(solution)/shard_map/ppermute | solution.py:336
  15.6 1.5 %collective-permute-start.5 = (bf16[128,128]{1,0:T(8,128)(2,1)S(1)}, bf16[128,128]{1,0:T(8,128)(2,1)S(1)}, u32[]{:S(2)}, u32[]{:S(2)}) collective-permute-start(bf16[128,128]{1,0:T(8,128)(2,1)S(1)} %get-tuple-element.38), channel_id=1, source_target_pairs={{0,7},{1,6},{2,5},{3,4},{4,3},{5,2},{6,1},{7,0},{8,15},{9,14},{10,... | collective-permute-start | bytes 98312 | tf_op jit(solution)/shard_map/ppermute | solution.py:336
  17.1 1.3 %collective-permute-done.1.refs_2_ = bf16[128,128]{1,0:T(8,128)(2,1)S(1)} collective-permute-done((bf16[128,128]{1,0:T(8,128)(2,1)S(1)}, bf16[128,128]{1,0:T(8,128)(2,1)S(1)}, u32[]{:S(2)}, u32[]{:S(2)}) %collective-permute-start.1) | collective-permute-done | bytes 32800 | tf_op jit(solution)/shard_map/ppermute | solution.py:336
  19.0 0.8 %prepare.1 = (f32[8,128,128]{2,1,0:T(8,128)S(1)}, f32[8,128,128]{2,1,0:T(8,128)S(1)}) custom-call(bf16[8,128,128]{2,1,0:T(8,128)(2,1)S(1)} %copy-done.1, bf16[8,128,128]{2,1,0:T(8,128)(2,1)S(1)} %copy-done.3, f32[1,128]{1,0:T(1,128)S(1)} %bitcast.7, f32[1,128]{1,0:T(1,128)S(1)} %bitcast.11, bf16[128,128]{1,0:T(8,128)(2,1)S(1)} %copy-done.5, ...), custom_call_target="tpu_custom_call" | custom-call | flops 67108864 | bytes 1639936 | tf_op jit(solution)/shard_map/prepare/pallas_call | solution.py:65
  19.9 1.5 %collective-permute-done.2.refs_3_ = bf16[128,128]{1,0:T(8,128)(2,1)S(1)} collective-permute-done((bf16[128,128]{1,0:T(8,128)(2,1)S(1)}, bf16[128,128]{1,0:T(8,128)(2,1)S(1)}, u32[]{:S(2)}, u32[]{:S(2)}) %collective-permute-start.2) | collective-permute-done | bytes 32800 | tf_op jit(solution)/shard_map/ppermute | solution.py:336
  21.3 0.7 %collective-permute-done.3.refs_4_ = bf16[128,128]{1,0:T(8,128)(2,1)S(1)} collective-permute-done((bf16[128,128]{1,0:T(8,128)(2,1)S(1)}, bf16[128,128]{1,0:T(8,128)(2,1)S(1)}, u32[]{:S(2)}, u32[]{:S(2)}) %collective-permute-start.3) | collective-permute-done | bytes 32800 | tf_op jit(solution)/shard_map/ppermute | solution.py:336
  22.0 1.1 %collective-permute-done.4.refs_5_ = bf16[128,128]{1,0:T(8,128)(2,1)S(1)} collective-permute-done((bf16[128,128]{1,0:T(8,128)(2,1)S(1)}, bf16[128,128]{1,0:T(8,128)(2,1)S(1)}, u32[]{:S(2)}, u32[]{:S(2)}) %collective-permute-start.4) | collective-permute-done | bytes 32800 | tf_op jit(solution)/shard_map/ppermute | solution.py:336
  24.1 9.9 %all_to_all.20.refs_0_ = bf16[8,128,128]{2,1,0:T(8,128)(2,1)S(1)} all-to-all(bf16[8,128,128]{2,1,0:T(8,128)(2,1)S(1)} %get-tuple-element.41), channel_id=1, replica_groups={{0,1,2,3,4,5,6,7},{8,9,10,11,12,13,14,15},{16,17,18,19,20,21,22,23},{24..., dimensions={0} | all-to-all | bytes 524288 | tf_op jit(solution)/shard_map/all_to_all | solution.py:327
  34.3 8.6 %all_to_all.21.refs_0_ = bf16[8,128,128]{2,1,0:T(8,128)(2,1)S(1)} all-to-all(bf16[8,128,128]{2,1,0:T(8,128)(2,1)S(1)} %middle.1), channel_id=1, replica_groups={{0,1,2,3,4,5,6,7},{8,9,10,11,12,13,14,15},{16,17,18,19,20,21,22,23},{24..., dimensions={0} | all-to-all | bytes 524288 | tf_op jit(solution)/shard_map/all_to_all | solution.py:327
  42.9 1.5 %d_right.1 = (bf16[16,128,128]{2,1,0:T(8,128)(2,1)}, bf16[16,64,128]{2,1,0:T(8,128)(2,1)S(1)}) custom-call(bf16[8,128,128]{2,1,0:T(8,128)(2,1)S(1)} %all_to_all.21.refs_0_, bf16[16,64,128]{2,1,0:T(8,128)(2,1)S(1)} %sort_left.1.refs_1_), custom_call_target="tpu_custom_call" | custom-call | flops 33554432 | bytes 1310720 | tf_op jit(solution)/shard_map/d_right/pallas_call | solution.py:65
  44.4 4.9 %all-to-all-start.3 = ((bf16[16,128,128]{2,1,0:T(8,128)(2,1)}), bf16[16,128,128]{2,1,0:T(8,128)(2,1)S(1)}, u32[]{:S(2)}, u32[]{:S(2)}) async-start(bf16[16,128,128]{2,1,0:T(8,128)(2,1)} %get-tuple-element.42), calls=%async_computation.3 | async-start | bytes 1048576 | tf_op jit(solution)/shard_map/all_to_all | solution.py:319
  49.8 1.5 %collective-permute-start.8 = (bf16[128,128]{1,0:T(8,128)(2,1)S(1)}, bf16[128,128]{1,0:T(8,128)(2,1)S(1)}, u32[]{:S(2)}, u32[]{:S(2)}) collective-permute-start(bf16[128,128]{1,0:T(8,128)(2,1)S(1)} %get-tuple-element.47), channel_id=1, source_target_pairs={{0,2},{1,3},{2,0},{3,1},{4,6},{5,7},{6,4},{7,5},{8,10},{9,11},{10,... | collective-permute-start | bytes 98312 | tf_op jit(solution)/shard_map/ppermute | solution.py:336
  51.8 0.9 %collective-permute-start.10 = (bf16[128,128]{1,0:T(8,128)(2,1)S(1)}, bf16[128,128]{1,0:T(8,128)(2,1)S(1)}, u32[]{:S(2)}, u32[]{:S(2)}) collective-permute-start(bf16[128,128]{1,0:T(8,128)(2,1)S(1)} %get-tuple-element.49), channel_id=1, source_target_pairs={{0,5},{1,4},{2,7},{3,6},{4,1},{5,0},{6,3},{7,2},{8,13},{9,12},{10,... | collective-permute-start | bytes 98312 | tf_op jit(solution)/shard_map/ppermute | solution.py:336
  53.3 2.4 %collective-permute-start.12 = (bf16[128,128]{1,0:T(8,128)(2,1)S(1)}, bf16[128,128]{1,0:T(8,128)(2,1)S(1)}, u32[]{:S(2)}, u32[]{:S(2)}) collective-permute-start(bf16[128,128]{1,0:T(8,128)(2,1)S(1)} %get-tuple-element.51), channel_id=1, source_target_pairs={{0,7},{1,6},{2,5},{3,4},{4,3},{5,2},{6,1},{7,0},{8,15},{9,14},{10,... | collective-permute-start | bytes 98312 | tf_op jit(solution)/shard_map/ppermute | solution.py:336
  55.7 1.1 %collective-permute-done.8.refs_2_ = bf16[128,128]{1,0:T(8,128)(2,1)S(1)} collective-permute-done((bf16[128,128]{1,0:T(8,128)(2,1)S(1)}, bf16[128,128]{1,0:T(8,128)(2,1)S(1)}, u32[]{:S(2)}, u32[]{:S(2)}) %collective-permute-start.8) | collective-permute-done | bytes 32800 | tf_op jit(solution)/shard_map/ppermute | solution.py:336
  56.8 0.7 %copy-done.10 = f32[128]{0:T(128)S(1)} copy-done((f32[128]{0:T(128)S(1)}, f32[128]{0:T(128)}, u32[]{:S(2)}) %copy-start.10) | copy-done | bytes 536
  57.9 1.0 %slopes.1 = (bf16[8,512,128]{2,1,0:T(8,128)(2,1)S(1)}, bf16[8,128,128]{2,1,0:T(8,128)(2,1)S(1)}, f32[8,128]{1,0:T(8,128)S(1)}, f32[128,128]{1,0:T(8,128)S(1)}, bf16[128,640]{1,0:T(8,128)(2,1)S(1)}) custom-call(bf16[8,128,128]{2,1,0:T(8,128)(2,1)S(1)} %copy-done.1, s32[1,128]{1,0:T(1,128)S(1)} %bitcast.15, f32[1,128]{1,0:T(1,128)S(1)} %bitcast.8, ...), custom_call_target="tpu_custom_call" | custom-call | flops 134217728 | bytes 2233856 | tf_op jit(solution)/shard_map/slopes/pallas_call | solution.py:65
  59.6 0.7 %collective-permute-done.10.refs_4_ = bf16[128,128]{1,0:T(8,128)(2,1)S(1)} collective-permute-done((bf16[128,128]{1,0:T(8,128)(2,1)S(1)}, bf16[128,128]{1,0:T(8,128)(2,1)S(1)}, u32[]{:S(2)}, u32[]{:S(2)}) %collective-permute-start.10) | collective-permute-done | bytes 32800 | tf_op jit(solution)/shard_map/ppermute | solution.py:336
  60.3 2.5 %collective-permute-done.11.refs_5_ = bf16[128,128]{1,0:T(8,128)(2,1)S(1)} collective-permute-done((bf16[128,128]{1,0:T(8,128)(2,1)S(1)}, bf16[128,128]{1,0:T(8,128)(2,1)S(1)}, u32[]{:S(2)}, u32[]{:S(2)}) %collective-permute-start.11) | collective-permute-done | bytes 32800 | tf_op jit(solution)/shard_map/ppermute | solution.py:336
  62.8 1.4 %finish.1 = bf16[8,128,128]{2,1,0:T(8,128)(2,1)} custom-call(bf16[16,128,128]{2,1,0:T(8,128)(2,1)S(1)} %all-to-all-done.3.refs_0_, bf16[8,128,128]{2,1,0:T(8,128)(2,1)S(1)} %sort_d_left.1.refs_1_, bf16[8,512,128]{2,1,0:T(8,128)(2,1)S(1)} %get-tuple-element.54.refs_2_, bf16[8,128,128]{2,1,0:T(8,128)(2,1)S(1)} %gate_back.1.refs_6_.refs_3_, ...), custom_call_target="tpu_custom_call" | custom-call | flops 134217728 | bytes 2854912 | tf_op jit(solution)/shard_map/finish/pallas_call | solution.py:65
  (44 shorter events, 6.1 us)
Async XLA Ops:
  2.4 8.6 %copy-start = (bf16[16,128,128]{2,1,0:T(8,128)(2,1)S(1)}, bf16[16,128,128]{2,1,0:T(8,128)(2,1)}, u32[]{:S(2)}) copy-start(bf16[16,128,128]{2,1,0:T(8,128)(2,1)} %project_right.1.refs_5_) | copy-start | bytes 1572868
  2.4 8.6 %copy-start.1 = (bf16[8,128,128]{2,1,0:T(8,128)(2,1)S(1)}, bf16[8,128,128]{2,1,0:T(8,128)(2,1)}, u32[]{:S(2)}) copy-start(bf16[8,128,128]{2,1,0:T(8,128)(2,1)} %refs_0_.7) | copy-start | bytes 786436
  2.4 8.6 %copy-start.2 = (bf16[128,512]{1,0:T(8,128)(2,1)S(1)}, bf16[128,512]{1,0:T(8,128)(2,1)}, u32[]{:S(2)}) copy-start(bf16[128,512]{1,0:T(8,128)(2,1)} %refs_4_.9) | copy-start | bytes 393220
  2.4 8.6 %copy-start.6 = (f32[128]{0:T(128)S(1)}, f32[128]{0:T(128)}, u32[]{:S(2)}) copy-start(f32[128]{0:T(128)} %param.13) | copy-start | bytes 1540
  2.4 8.6 %copy-start.7 = (f32[128]{0:T(128)S(1)}, f32[128]{0:T(128)}, u32[]{:S(2)}) copy-start(f32[128]{0:T(128)} %param.14) | copy-start | bytes 1540
  2.5 8.6 %copy-start.8 = (s32[128]{0:T(128)S(1)}, s32[128]{0:T(128)}, u32[]{:S(2)}) copy-start(s32[128]{0:T(128)} %param.12) | copy-start | bytes 1540
  2.5 21.0 %all-to-all-start = ((bf16[16,128,128]{2,1,0:T(8,128)(2,1)}), bf16[16,128,128]{2,1,0:T(8,128)(2,1)S(1)}, u32[]{:S(2)}, u32[]{:S(2)}) async-start(bf16[16,128,128]{2,1,0:T(8,128)(2,1)} %project_right.1.refs_5_), calls=%async_computation | async-start | bytes 1048576 | tf_op jit(solution)/shard_map/all_to_all | solution.py:319
  11.0 7.3 %copy-start.3 = (bf16[8,128,128]{2,1,0:T(8,128)(2,1)S(1)}, bf16[8,128,128]{2,1,0:T(8,128)(2,1)}, u32[]{:S(2)}) copy-start(bf16[8,128,128]{2,1,0:T(8,128)(2,1)} %refs_1_.1) | copy-start | bytes 786436
  11.1 7.3 %copy-start.4 = (bf16[128,128]{1,0:T(8,128)(2,1)S(1)}, bf16[128,128]{1,0:T(8,128)(2,1)}, u32[]{:S(2)}) copy-start(bf16[128,128]{1,0:T(8,128)(2,1)} %refs_4_.8) | copy-start | bytes 98308
  11.9 3.7 %collective-permute-start = (bf16[128,128]{1,0:T(8,128)(2,1)S(1)}, bf16[128,128]{1,0:T(8,128)(2,1)S(1)}, u32[]{:S(2)}, u32[]{:S(2)}) collective-permute-start(bf16[128,128]{1,0:T(8,128)(2,1)S(1)} %get-tuple-element.33), channel_id=1, source_target_pairs={{0,1},{1,0},{2,3},{3,2},{4,5},{5,4},{6,7},{7,6},{8,9},{9,8},{10,11... | collective-permute-start | bytes 98312 | tf_op jit(solution)/shard_map/ppermute | solution.py:336
  12.1 6.3 %collective-permute-start.1 = (bf16[128,128]{1,0:T(8,128)(2,1)S(1)}, bf16[128,128]{1,0:T(8,128)(2,1)S(1)}, u32[]{:S(2)}, u32[]{:S(2)}) collective-permute-start(bf16[128,128]{1,0:T(8,128)(2,1)S(1)} %get-tuple-element.34), channel_id=1, source_target_pairs={{0,2},{1,3},{2,0},{3,1},{4,6},{5,7},{6,4},{7,5},{8,10},{9,11},{10,... | collective-permute-start | bytes 98312 | tf_op jit(solution)/shard_map/ppermute | solution.py:336
  12.7 8.6 %collective-permute-start.2 = (bf16[128,128]{1,0:T(8,128)(2,1)S(1)}, bf16[128,128]{1,0:T(8,128)(2,1)S(1)}, u32[]{:S(2)}, u32[]{:S(2)}) collective-permute-start(bf16[128,128]{1,0:T(8,128)(2,1)S(1)} %get-tuple-element.35), channel_id=1, source_target_pairs={{0,4},{1,5},{2,6},{3,7},{4,0},{5,1},{6,2},{7,3},{8,12},{9,13},{10,... | collective-permute-start | bytes 98312 | tf_op jit(solution)/shard_map/ppermute | solution.py:336
  13.2 8.8 %collective-permute-start.3 = (bf16[128,128]{1,0:T(8,128)(2,1)S(1)}, bf16[128,128]{1,0:T(8,128)(2,1)S(1)}, u32[]{:S(2)}, u32[]{:S(2)}) collective-permute-start(bf16[128,128]{1,0:T(8,128)(2,1)S(1)} %get-tuple-element.36), channel_id=1, source_target_pairs={{0,5},{1,4},{2,7},{3,6},{4,1},{5,0},{6,3},{7,2},{8,13},{9,12},{10,... | collective-permute-start | bytes 98312 | tf_op jit(solution)/shard_map/ppermute | solution.py:336
  14.1 9.0 %collective-permute-start.4 = (bf16[128,128]{1,0:T(8,128)(2,1)S(1)}, bf16[128,128]{1,0:T(8,128)(2,1)S(1)}, u32[]{:S(2)}, u32[]{:S(2)}) collective-permute-start(bf16[128,128]{1,0:T(8,128)(2,1)S(1)} %get-tuple-element.37), channel_id=1, source_target_pairs={{0,6},{1,7},{2,4},{3,5},{4,2},{5,3},{6,0},{7,1},{8,14},{9,15},{10,... | collective-permute-start | bytes 98312 | tf_op jit(solution)/shard_map/ppermute | solution.py:336
  15.6 7.5 %collective-permute-start.5 = (bf16[128,128]{1,0:T(8,128)(2,1)S(1)}, bf16[128,128]{1,0:T(8,128)(2,1)S(1)}, u32[]{:S(2)}, u32[]{:S(2)}) collective-permute-start(bf16[128,128]{1,0:T(8,128)(2,1)S(1)} %get-tuple-element.38), channel_id=1, source_target_pairs={{0,7},{1,6},{2,5},{3,4},{4,3},{5,2},{6,1},{7,0},{8,15},{9,14},{10,... | collective-permute-start | bytes 98312 | tf_op jit(solution)/shard_map/ppermute | solution.py:336
  18.4 4.9 %collective-permute-start.6 = (bf16[128,128]{1,0:T(8,128)(2,1)S(1)}, bf16[128,128]{1,0:T(8,128)(2,1)S(1)}, u32[]{:S(2)}, u32[]{:S(2)}) collective-permute-start(bf16[128,128]{1,0:T(8,128)(2,1)S(1)} %get-tuple-element.39), channel_id=1, source_target_pairs={{0,3},{1,2},{2,1},{3,0},{4,7},{5,6},{6,5},{7,4},{8,11},{9,10},{10,... | collective-permute-start | bytes 98312 | tf_op jit(solution)/shard_map/ppermute | solution.py:336
  44.4 18.4 %all-to-all-start.3 = ((bf16[16,128,128]{2,1,0:T(8,128)(2,1)}), bf16[16,128,128]{2,1,0:T(8,128)(2,1)S(1)}, u32[]{:S(2)}, u32[]{:S(2)}) async-start(bf16[16,128,128]{2,1,0:T(8,128)(2,1)} %get-tuple-element.42), calls=%async_computation.3 | async-start | bytes 1048576 | tf_op jit(solution)/shard_map/all_to_all | solution.py:319
  49.6 3.7 %collective-permute-start.7 = (bf16[128,128]{1,0:T(8,128)(2,1)S(1)}, bf16[128,128]{1,0:T(8,128)(2,1)S(1)}, u32[]{:S(2)}, u32[]{:S(2)}) collective-permute-start(bf16[128,128]{1,0:T(8,128)(2,1)S(1)} %get-tuple-element.46), channel_id=1, source_target_pairs={{0,1},{1,0},{2,3},{3,2},{4,5},{5,4},{6,7},{7,6},{8,9},{9,8},{10,11... | collective-permute-start | bytes 98312 | tf_op jit(solution)/shard_map/ppermute | solution.py:336
  49.8 7.0 %collective-permute-start.8 = (bf16[128,128]{1,0:T(8,128)(2,1)S(1)}, bf16[128,128]{1,0:T(8,128)(2,1)S(1)}, u32[]{:S(2)}, u32[]{:S(2)}) collective-permute-start(bf16[128,128]{1,0:T(8,128)(2,1)S(1)} %get-tuple-element.47), channel_id=1, source_target_pairs={{0,2},{1,3},{2,0},{3,1},{4,6},{5,7},{6,4},{7,5},{8,10},{9,11},{10,... | collective-permute-start | bytes 98312 | tf_op jit(solution)/shard_map/ppermute | solution.py:336
  51.3 8.3 %collective-permute-start.9 = (bf16[128,128]{1,0:T(8,128)(2,1)S(1)}, bf16[128,128]{1,0:T(8,128)(2,1)S(1)}, u32[]{:S(2)}, u32[]{:S(2)}) collective-permute-start(bf16[128,128]{1,0:T(8,128)(2,1)S(1)} %get-tuple-element.48), channel_id=1, source_target_pairs={{0,4},{1,5},{2,6},{3,7},{4,0},{5,1},{6,2},{7,3},{8,12},{9,13},{10,... | collective-permute-start | bytes 98312 | tf_op jit(solution)/shard_map/ppermute | solution.py:336
  51.8 8.5 %collective-permute-start.10 = (bf16[128,128]{1,0:T(8,128)(2,1)S(1)}, bf16[128,128]{1,0:T(8,128)(2,1)S(1)}, u32[]{:S(2)}, u32[]{:S(2)}) collective-permute-start(bf16[128,128]{1,0:T(8,128)(2,1)S(1)} %get-tuple-element.49), channel_id=1, source_target_pairs={{0,5},{1,4},{2,7},{3,6},{4,1},{5,0},{6,3},{7,2},{8,13},{9,12},{10,... | collective-permute-start | bytes 98312 | tf_op jit(solution)/shard_map/ppermute | solution.py:336
  52.7 10.0 %collective-permute-start.11 = (bf16[128,128]{1,0:T(8,128)(2,1)S(1)}, bf16[128,128]{1,0:T(8,128)(2,1)S(1)}, u32[]{:S(2)}, u32[]{:S(2)}) collective-permute-start(bf16[128,128]{1,0:T(8,128)(2,1)S(1)} %get-tuple-element.50), channel_id=1, source_target_pairs={{0,6},{1,7},{2,4},{3,5},{4,2},{5,3},{6,0},{7,1},{8,14},{9,15},{10,... | collective-permute-start | bytes 98312 | tf_op jit(solution)/shard_map/ppermute | solution.py:336
  53.3 9.5 %collective-permute-start.12 = (bf16[128,128]{1,0:T(8,128)(2,1)S(1)}, bf16[128,128]{1,0:T(8,128)(2,1)S(1)}, u32[]{:S(2)}, u32[]{:S(2)}) collective-permute-start(bf16[128,128]{1,0:T(8,128)(2,1)S(1)} %get-tuple-element.51), channel_id=1, source_target_pairs={{0,7},{1,6},{2,5},{3,4},{4,3},{5,2},{6,1},{7,0},{8,15},{9,14},{10,... | collective-permute-start | bytes 98312 | tf_op jit(solution)/shard_map/ppermute | solution.py:336
  56.8 6.0 %collective-permute-start.13 = (bf16[128,128]{1,0:T(8,128)(2,1)S(1)}, bf16[128,128]{1,0:T(8,128)(2,1)S(1)}, u32[]{:S(2)}, u32[]{:S(2)}) collective-permute-start(bf16[128,128]{1,0:T(8,128)(2,1)S(1)} %get-tuple-element.52), channel_id=1, source_target_pairs={{0,3},{1,2},{2,1},{3,0},{4,7},{5,6},{6,5},{7,4},{8,11},{9,10},{10,... | collective-permute-start | bytes 98312 | tf_op jit(solution)/shard_map/ppermute | solution.py:336
  (3 other events, 8.6 us)

commit v25 on v16

--- a/solution.py
+++ b/solution.py
@@ -176,7 +176,7 @@
 
 
 def sort_left_kernel(*refs):
-    *pieces, left_all, left_wide = refs
+    *pieces, left_all, left_pairs, left_wide = refs
     block, left_rows, _ = left_all.shape
     depth = pieces[0].shape[0]
     for step, piece in enumerate(pieces):
@@ -184,6 +184,10 @@
         left_wide[pl.ds(start, depth), :] = piece[...].astype(F32)
     for h in range(block):
         left_all[h] = left_wide[pl.ds(h, left_rows, stride=block), :].astype(BF16)
+    empty = jnp.zeros(left_all.shape[1:], BF16)
+    for n in range(block // 2):
+        left_pairs[n, :left_rows, :] = jnp.concatenate([left_all[2 * n], empty], axis=1)
+        left_pairs[n, left_rows:, :] = jnp.concatenate([empty, left_all[2 * n + 1]], axis=1)
 
 
 def tri_kernel(right_panel, left_all, after, products, right_all, left_wide, right_wide):
@@ -219,14 +223,20 @@
         ).astype(BF16)
 
 
-def d_right_kernel(d_products, left_all, d_right_panel, d_tri_all, left_wide, right_wide):
-    block, left_rows, _ = left_all.shape
+def d_right_kernel(d_products, left_pairs, d_right_panel, d_tri_all, left_wide, right_wide):
+    block, left_rows, width = d_tri_all.shape
     right_rows = right_wide.shape[0] // block
     spread(d_products, left_wide)
-    for h in range(block):
-        d_tri = left_wide[pl.ds(h, left_rows, stride=block), :].astype(BF16)
-        d_tri_all[h] = d_tri
-        right_wide[pl.ds(h, right_rows, stride=block), :] = dot(d_tri, left_all[h], 0, 0)
+    for n in range(block // 2):
+        pair = (2 * n, 2 * n + 1)
+        d_tri = [left_wide[pl.ds(h, left_rows, stride=block), :] for h in pair]
+        d_tri = jnp.concatenate(d_tri, axis=0).astype(BF16)
+        d_right = dot(d_tri, left_pairs[n], 0, 0)
+        for side, h in enumerate(pair):
+            d_tri_all[h] = d_tri[side * left_rows : (side + 1) * left_rows]
+            right_wide[pl.ds(h, right_rows, stride=block), :] = d_right[
+                :, side * width : (side + 1) * width
+            ]
     for rank, place in wide_places(d_right_panel, d_products.shape[0], True):
         d_right_panel[rank] = right_wide[place, :].astype(BF16)
 
@@ -389,10 +399,13 @@
         flops=2 * cells * channels * 2 * hidden,
     )
     pieces = swap_pieces(pieces)
-    (left_all,) = call(
+    left_all, left_pairs = call(
         sort_left_kernel,
         "sort_left",
-        [shape((block, left_rows, width), BF16)],
+        [
+            shape((block, left_rows, width), BF16),
+            shape((block // 2, 2 * left_rows, 2 * width), BF16),
+        ],
         pieces,
         scratch=[left_wide],
     )
@@ -426,7 +439,7 @@
         d_right_kernel,
         "d_right",
         [wide_panel, shape((block, left_rows, width), BF16)],
-        [d_products, left_all],
+        [d_products, left_pairs],
         scratch=[left_wide, right_wide],
         flops=2 * block * left_rows * width * right_rows,
     )

time: 62.7 us -> 62.7 us (level)
    unnamed x22 -> x26, local copies, waits for them, and re-layouts: 1.34 us -> 1.64 us
where the time goes in v25:
time: 62.7 us; the launch traced here: 62.2 us
  starting transfers between devices  24.7 us (39%)
  blocking collectives  17.3 us (28%)
  Pallas kernels  9.78 us (16%)
  waiting for transfers between devices  8.53 us (14%)
  local copies, waits for them, and re-layouts  1.64 us (3%)
    all_to_all x2, blocking collectives, swap_half(): lax.all_to_all(values, 'row', split_axis=0, concat_axis=0, tiled=True, ax...  17.3 us
    all_to_all x2, starting transfers between devices, swap(): lax.all_to_all(values, 'row', split_axis=0, concat_axis=0, tiled=True, ax...  13.4 us
    ppermute x14, starting transfers between devices, swap_pieces(): lax.ppermute(pieces[step], 'row', [(d, d ^ distance(step, count)) for d i...  11.3 us
    pallas_call x12, Pallas kernels, call(): pl.pallas_call(body, name=name, out_shape=outs, in_specs=[pl.BlockSpec(me...  9.78 us
    ppermute x14, waiting for transfers between devices, swap_pieces(): lax.ppermute(pieces[step], 'row', [(d, d ^ distance(step, count)) for d i...  8.08 us
    unnamed x26, local copies, waits for them, and re-layouts  1.64 us
  transfers between devices with their start and end apart: 16, of which 10 were waited for; matrix products, arithmetic and copies ran while one was open for 0% of the time, Pallas kernels for 6%

profile of v25, /device:TPU:0, one launch (start us, length us, event | category | flops | bytes accessed | tf_op | source)
XLA Modules:
  0.0 62.2 jit_solution(8845681864883545652)
XLA Ops:
  0.0 2.4 %project_right.1.refs_5_ = bf16[16,128,128]{2,1,0:T(8,128)(2,1)} custom-call(bf16[8,128,128]{2,1,0:T(8,128)(2,1)} %refs_0_.7, s32[1,128]{1,0:T(1,128)} %bitcast.13, f32[1,128]{1,0:T(1,128)} %bitcast.5, f32[1,128]{1,0:T(1,128)} %bitcast.9, bf16[128,512]{1,0:T(8,128)(2,1)} %refs_4_.9), custom_call_target="tpu_custom_call" | custom-call | flops 67108864 | bytes 919040 | tf_op jit(solution)/shard_map/project_right/pallas_call | solution.py:65
  2.5 8.5 %all-to-all-start = ((bf16[16,128,128]{2,1,0:T(8,128)(2,1)}), bf16[16,128,128]{2,1,0:T(8,128)(2,1)S(1)}, u32[]{:S(2)}, u32[]{:S(2)}) async-start(bf16[16,128,128]{2,1,0:T(8,128)(2,1)} %project_right.1.refs_5_), calls=%async_computation | async-start | bytes 1048576 | tf_op jit(solution)/shard_map/all_to_all | solution.py:329
  11.1 0.8 %project_left.1 = (bf16[128,128]{1,0:T(8,128)(2,1)S(1)}, bf16[128,128]{1,0:T(8,128)(2,1)S(1)}, bf16[128,128]{1,0:T(8,128)(2,1)S(1)}, bf16[128,128]{1,0:T(8,128)(...) custom-call(bf16[8,128,128]{2,1,0:T(8,128)(2,1)S(1)} %copy-done.1, ...), custom_call_target="tpu_custom_call" | custom-call | flops 67108864 | bytes 1181184 | tf_op jit(solution)/shard_map/project_left/pallas_call | solution.py:65
  12.7 1.4 %collective-permute-start.2 = (bf16[128,128]{1,0:T(8,128)(2,1)S(1)}, bf16[128,128]{1,0:T(8,128)(2,1)S(1)}, u32[]{:S(2)}, u32[]{:S(2)}) collective-permute-start(bf16[128,128]{1,0:T(8,128)(2,1)S(1)} %get-tuple-element.37), channel_id=1, source_target_pairs={{0,6},{1,7},{2,4},{3,5},{4,2},{5,3},{6,0},{7,1},{8,14},{9,15},{10,... | collective-permute-start | bytes 98312 | tf_op jit(solution)/shard_map/ppermute | solution.py:346
  14.1 0.9 %collective-permute-start.3 = (bf16[128,128]{1,0:T(8,128)(2,1)S(1)}, bf16[128,128]{1,0:T(8,128)(2,1)S(1)}, u32[]{:S(2)}, u32[]{:S(2)}) collective-permute-start(bf16[128,128]{1,0:T(8,128)(2,1)S(1)} %get-tuple-element.38), channel_id=1, source_target_pairs={{0,7},{1,6},{2,5},{3,4},{4,3},{5,2},{6,1},{7,0},{8,15},{9,14},{10,... | collective-permute-start | bytes 98312 | tf_op jit(solution)/shard_map/ppermute | solution.py:346
  15.6 1.5 %collective-permute-start.5 = (bf16[128,128]{1,0:T(8,128)(2,1)S(1)}, bf16[128,128]{1,0:T(8,128)(2,1)S(1)}, u32[]{:S(2)}, u32[]{:S(2)}) collective-permute-start(bf16[128,128]{1,0:T(8,128)(2,1)S(1)} %get-tuple-element.40), channel_id=1, source_target_pairs={{0,5},{1,4},{2,7},{3,6},{4,1},{5,0},{6,3},{7,2},{8,13},{9,12},{10,... | collective-permute-start | bytes 98312 | tf_op jit(solution)/shard_map/ppermute | solution.py:346
  17.1 1.3 %collective-permute-done.1.refs_2_ = bf16[128,128]{1,0:T(8,128)(2,1)S(1)} collective-permute-done((bf16[128,128]{1,0:T(8,128)(2,1)S(1)}, bf16[128,128]{1,0:T(8,128)(2,1)S(1)}, u32[]{:S(2)}, u32[]{:S(2)}) %collective-permute-start.1) | collective-permute-done | bytes 32800 | tf_op jit(solution)/shard_map/ppermute | solution.py:346
  19.0 0.8 %prepare.1 = (f32[8,128,128]{2,1,0:T(8,128)S(1)}, f32[8,128,128]{2,1,0:T(8,128)S(1)}) custom-call(bf16[8,128,128]{2,1,0:T(8,128)(2,1)S(1)} %copy-done.1, bf16[8,128,128]{2,1,0:T(8,128)(2,1)S(1)} %copy-done.3, f32[1,128]{1,0:T(1,128)S(1)} %bitcast.7, f32[1,128]{1,0:T(1,128)S(1)} %bitcast.11, bf16[128,128]{1,0:T(8,128)(2,1)S(1)} %copy-done.6, ...), custom_call_target="tpu_custom_call" | custom-call | flops 67108864 | bytes 1639936 | tf_op jit(solution)/shard_map/prepare/pallas_call | solution.py:65
  19.9 1.5 %collective-permute-done.2.refs_3_ = bf16[128,128]{1,0:T(8,128)(2,1)S(1)} collective-permute-done((bf16[128,128]{1,0:T(8,128)(2,1)S(1)}, bf16[128,128]{1,0:T(8,128)(2,1)S(1)}, u32[]{:S(2)}, u32[]{:S(2)}) %collective-permute-start.2) | collective-permute-done | bytes 32800 | tf_op jit(solution)/shard_map/ppermute | solution.py:346
  21.3 0.7 %collective-permute-done.3.refs_4_ = bf16[128,128]{1,0:T(8,128)(2,1)S(1)} collective-permute-done((bf16[128,128]{1,0:T(8,128)(2,1)S(1)}, bf16[128,128]{1,0:T(8,128)(2,1)S(1)}, u32[]{:S(2)}, u32[]{:S(2)}) %collective-permute-start.3) | collective-permute-done | bytes 32800 | tf_op jit(solution)/shard_map/ppermute | solution.py:346
  22.0 1.5 %collective-permute-done.4.refs_5_ = bf16[128,128]{1,0:T(8,128)(2,1)S(1)} collective-permute-done((bf16[128,128]{1,0:T(8,128)(2,1)S(1)}, bf16[128,128]{1,0:T(8,128)(2,1)S(1)}, u32[]{:S(2)}, u32[]{:S(2)}) %collective-permute-start.4) | collective-permute-done | bytes 32800 | tf_op jit(solution)/shard_map/ppermute | solution.py:346
  23.8 0.6 %tri.1 = (bf16[8,128,128]{2,1,0:T(8,128)(2,1)S(1)}, bf16[16,128,128]{2,1,0:T(8,128)(2,1)S(1)}) custom-call(bf16[16,128,128]{2,1,0:T(8,128)(2,1)S(1)} %all-to-all-done.refs_0_, bf16[16,64,128]{2,1,0:T(8,128)(2,1)S(1)} %get-tuple-element.42.refs_1_, f32[8,128,128]{2,1,0:T(8,128)S(1)} %get-tuple-element.43.refs_2_.refs_1_), custom_call_target="tpu_custom_call" | custom-call | flops 33554432 | bytes 2097152 | tf_op jit(solution)/shard_map/tri/pallas_call | solution.py:65
  24.5 8.7 %all_to_all.20.refs_0_ = bf16[8,128,128]{2,1,0:T(8,128)(2,1)S(1)} all-to-all(bf16[8,128,128]{2,1,0:T(8,128)(2,1)S(1)} %get-tuple-element.44), channel_id=1, replica_groups={{0,1,2,3,4,5,6,7},{8,9,10,11,12,13,14,15},{16,17,18,19,20,21,22,23},{24..., dimensions={0} | all-to-all | bytes 524288 | tf_op jit(solution)/shard_map/all_to_all | solution.py:337
  33.5 8.6 %all_to_all.21.refs_0_ = bf16[8,128,128]{2,1,0:T(8,128)(2,1)S(1)} all-to-all(bf16[8,128,128]{2,1,0:T(8,128)(2,1)S(1)} %middle.1), channel_id=1, replica_groups={{0,1,2,3,4,5,6,7},{8,9,10,11,12,13,14,15},{16,17,18,19,20,21,22,23},{24..., dimensions={0} | all-to-all | bytes 524288 | tf_op jit(solution)/shard_map/all_to_all | solution.py:337
  42.1 1.4 %d_right.1 = (bf16[16,128,128]{2,1,0:T(8,128)(2,1)}, bf16[16,64,128]{2,1,0:T(8,128)(2,1)S(1)}) custom-call(bf16[8,128,128]{2,1,0:T(8,128)(2,1)S(1)} %all_to_all.21.refs_0_, bf16[8,128,256]{2,1,0:T(8,128)(2,1)S(1)} %get-tuple-element.45.refs_1_), custom_call_target="tpu_custom_call" | custom-call | flops 33554432 | bytes 1572864 | tf_op jit(solution)/shard_map/d_right/pallas_call | solution.py:65
  43.5 4.9 %all-to-all-start.3 = ((bf16[16,128,128]{2,1,0:T(8,128)(2,1)}), bf16[16,128,128]{2,1,0:T(8,128)(2,1)S(1)}, u32[]{:S(2)}, u32[]{:S(2)}) async-start(bf16[16,128,128]{2,1,0:T(8,128)(2,1)} %get-tuple-element.46), calls=%async_computation.3 | async-start | bytes 1048576 | tf_op jit(solution)/shard_map/all_to_all | solution.py:329
  48.9 1.5 %collective-permute-start.8 = (bf16[128,128]{1,0:T(8,128)(2,1)S(1)}, bf16[128,128]{1,0:T(8,128)(2,1)S(1)}, u32[]{:S(2)}, u32[]{:S(2)}) collective-permute-start(bf16[128,128]{1,0:T(8,128)(2,1)S(1)} %get-tuple-element.51), channel_id=1, source_target_pairs={{0,2},{1,3},{2,0},{3,1},{4,6},{5,7},{6,4},{7,5},{8,10},{9,11},{10,... | collective-permute-start | bytes 98312 | tf_op jit(solution)/shard_map/ppermute | solution.py:346
  50.7 2.0 %collective-permute-start.10 = (bf16[128,128]{1,0:T(8,128)(2,1)S(1)}, bf16[128,128]{1,0:T(8,128)(2,1)S(1)}, u32[]{:S(2)}, u32[]{:S(2)}) collective-permute-start(bf16[128,128]{1,0:T(8,128)(2,1)S(1)} %get-tuple-element.53), channel_id=1, source_target_pairs={{0,7},{1,6},{2,5},{3,4},{4,3},{5,2},{6,1},{7,0},{8,15},{9,14},{10,... | collective-permute-start | bytes 98312 | tf_op jit(solution)/shard_map/ppermute | solution.py:346
  53.3 1.6 %collective-permute-start.12 = (bf16[128,128]{1,0:T(8,128)(2,1)S(1)}, bf16[128,128]{1,0:T(8,128)(2,1)S(1)}, u32[]{:S(2)}, u32[]{:S(2)}) collective-permute-start(bf16[128,128]{1,0:T(8,128)(2,1)S(1)} %get-tuple-element.55), channel_id=1, source_target_pairs={{0,5},{1,4},{2,7},{3,6},{4,1},{5,0},{6,3},{7,2},{8,13},{9,12},{10,... | collective-permute-start | bytes 98312 | tf_op jit(solution)/shard_map/ppermute | solution.py:346
  54.8 1.2 %collective-permute-done.8.refs_2_ = bf16[128,128]{1,0:T(8,128)(2,1)S(1)} collective-permute-done((bf16[128,128]{1,0:T(8,128)(2,1)S(1)}, bf16[128,128]{1,0:T(8,128)(2,1)S(1)}, u32[]{:S(2)}, u32[]{:S(2)}) %collective-permute-start.8) | collective-permute-done | bytes 32800 | tf_op jit(solution)/shard_map/ppermute | solution.py:346
  56.0 0.6 %copy-done.12 = f32[128]{0:T(128)S(1)} copy-done((f32[128]{0:T(128)S(1)}, f32[128]{0:T(128)}, u32[]{:S(2)}) %copy-start.12) | copy-done | bytes 536
  57.4 1.0 %slopes.1 = (bf16[8,512,128]{2,1,0:T(8,128)(2,1)S(1)}, bf16[8,128,128]{2,1,0:T(8,128)(2,1)S(1)}, f32[8,128]{1,0:T(8,128)S(1)}, f32[128,128]{1,0:T(8,128)S(1)}, bf16[128,640]{1,0:T(8,128)(2,1)S(1)}) custom-call(bf16[8,128,128]{2,1,0:T(8,128)(2,1)S(1)} %copy-done.1, s32[1,128]{1,0:T(1,128)S(1)} %bitcast.15, f32[1,128]{1,0:T(1,128)S(1)} %bitcast.8, ...), custom_call_target="tpu_custom_call" | custom-call | flops 134217728 | bytes 2233856 | tf_op jit(solution)/shard_map/slopes/pallas_call | solution.py:65
  58.7 0.7 %collective-permute-done.10.refs_4_ = bf16[128,128]{1,0:T(8,128)(2,1)S(1)} collective-permute-done((bf16[128,128]{1,0:T(8,128)(2,1)S(1)}, bf16[128,128]{1,0:T(8,128)(2,1)S(1)}, u32[]{:S(2)}, u32[]{:S(2)}) %collective-permute-start.10) | collective-permute-done | bytes 32800 | tf_op jit(solution)/shard_map/ppermute | solution.py:346
  60.8 1.4 %finish.1 = bf16[8,128,128]{2,1,0:T(8,128)(2,1)} custom-call(bf16[16,128,128]{2,1,0:T(8,128)(2,1)S(1)} %all-to-all-done.3.refs_0_, bf16[8,128,128]{2,1,0:T(8,128)(2,1)S(1)} %sort_d_left.1.refs_1_, bf16[8,512,128]{2,1,0:T(8,128)(2,1)S(1)} %get-tuple-element.58.refs_2_, bf16[8,128,128]{2,1,0:T(8,128)(2,1)S(1)} %gate_back.1.refs_6_.refs_3_, ...), custom_call_target="tpu_custom_call" | custom-call | flops 134217728 | bytes 2854912 | tf_op jit(solution)/shard_map/finish/pallas_call | solution.py:65
  (48 shorter events, 6.4 us)
Async XLA Ops:
  2.4 8.6 %copy-start = (bf16[16,128,128]{2,1,0:T(8,128)(2,1)S(1)}, bf16[16,128,128]{2,1,0:T(8,128)(2,1)}, u32[]{:S(2)}) copy-start(bf16[16,128,128]{2,1,0:T(8,128)(2,1)} %project_right.1.refs_5_) | copy-start | bytes 1572868
  2.4 8.6 %copy-start.1 = (bf16[8,128,128]{2,1,0:T(8,128)(2,1)S(1)}, bf16[8,128,128]{2,1,0:T(8,128)(2,1)}, u32[]{:S(2)}) copy-start(bf16[8,128,128]{2,1,0:T(8,128)(2,1)} %refs_0_.7) | copy-start | bytes 786436
  2.4 8.6 %copy-start.2 = (bf16[128,512]{1,0:T(8,128)(2,1)S(1)}, bf16[128,512]{1,0:T(8,128)(2,1)}, u32[]{:S(2)}) copy-start(bf16[128,512]{1,0:T(8,128)(2,1)} %refs_4_.9) | copy-start | bytes 393220
  2.4 8.6 %copy-start.8 = (f32[128]{0:T(128)S(1)}, f32[128]{0:T(128)}, u32[]{:S(2)}) copy-start(f32[128]{0:T(128)} %param.13) | copy-start | bytes 1540
  2.4 8.6 %copy-start.9 = (f32[128]{0:T(128)S(1)}, f32[128]{0:T(128)}, u32[]{:S(2)}) copy-start(f32[128]{0:T(128)} %param.14) | copy-start | bytes 1540
  2.5 8.6 %copy-start.10 = (s32[128]{0:T(128)S(1)}, s32[128]{0:T(128)}, u32[]{:S(2)}) copy-start(s32[128]{0:T(128)} %param.12) | copy-start | bytes 1540
  2.5 21.4 %all-to-all-start = ((bf16[16,128,128]{2,1,0:T(8,128)(2,1)}), bf16[16,128,128]{2,1,0:T(8,128)(2,1)S(1)}, u32[]{:S(2)}, u32[]{:S(2)}) async-start(bf16[16,128,128]{2,1,0:T(8,128)(2,1)} %project_right.1.refs_5_), calls=%async_computation | async-start | bytes 1048576 | tf_op jit(solution)/shard_map/all_to_all | solution.py:329
  11.0 7.4 %copy-start.3 = (bf16[8,128,128]{2,1,0:T(8,128)(2,1)S(1)}, bf16[8,128,128]{2,1,0:T(8,128)(2,1)}, u32[]{:S(2)}) copy-start(bf16[8,128,128]{2,1,0:T(8,128)(2,1)} %refs_1_.1) | copy-start | bytes 786436
  11.9 3.7 %collective-permute-start = (bf16[128,128]{1,0:T(8,128)(2,1)S(1)}, bf16[128,128]{1,0:T(8,128)(2,1)S(1)}, u32[]{:S(2)}, u32[]{:S(2)}) collective-permute-start(bf16[128,128]{1,0:T(8,128)(2,1)S(1)} %get-tuple-element.35), channel_id=1, source_target_pairs={{0,1},{1,0},{2,3},{3,2},{4,5},{5,4},{6,7},{7,6},{8,9},{9,8},{10,11... | collective-permute-start | bytes 98312 | tf_op jit(solution)/shard_map/ppermute | solution.py:346
  12.1 6.3 %collective-permute-start.1 = (bf16[128,128]{1,0:T(8,128)(2,1)S(1)}, bf16[128,128]{1,0:T(8,128)(2,1)S(1)}, u32[]{:S(2)}, u32[]{:S(2)}) collective-permute-start(bf16[128,128]{1,0:T(8,128)(2,1)S(1)} %get-tuple-element.36), channel_id=1, source_target_pairs={{0,2},{1,3},{2,0},{3,1},{4,6},{5,7},{6,4},{7,5},{8,10},{9,11},{10,... | collective-permute-start | bytes 98312 | tf_op jit(solution)/shard_map/ppermute | solution.py:346
  12.7 8.6 %collective-permute-start.2 = (bf16[128,128]{1,0:T(8,128)(2,1)S(1)}, bf16[128,128]{1,0:T(8,128)(2,1)S(1)}, u32[]{:S(2)}, u32[]{:S(2)}) collective-permute-start(bf16[128,128]{1,0:T(8,128)(2,1)S(1)} %get-tuple-element.37), channel_id=1, source_target_pairs={{0,6},{1,7},{2,4},{3,5},{4,2},{5,3},{6,0},{7,1},{8,14},{9,15},{10,... | collective-permute-start | bytes 98312 | tf_op jit(solution)/shard_map/ppermute | solution.py:346
  14.1 8.0 %collective-permute-start.3 = (bf16[128,128]{1,0:T(8,128)(2,1)S(1)}, bf16[128,128]{1,0:T(8,128)(2,1)S(1)}, u32[]{:S(2)}, u32[]{:S(2)}) collective-permute-start(bf16[128,128]{1,0:T(8,128)(2,1)S(1)} %get-tuple-element.38), channel_id=1, source_target_pairs={{0,7},{1,6},{2,5},{3,4},{4,3},{5,2},{6,1},{7,0},{8,15},{9,14},{10,... | collective-permute-start | bytes 98312 | tf_op jit(solution)/shard_map/ppermute | solution.py:346
  15.0 8.6 %collective-permute-start.4 = (bf16[128,128]{1,0:T(8,128)(2,1)S(1)}, bf16[128,128]{1,0:T(8,128)(2,1)S(1)}, u32[]{:S(2)}, u32[]{:S(2)}) collective-permute-start(bf16[128,128]{1,0:T(8,128)(2,1)S(1)} %get-tuple-element.39), channel_id=1, source_target_pairs={{0,4},{1,5},{2,6},{3,7},{4,0},{5,1},{6,2},{7,3},{8,12},{9,13},{10,... | collective-permute-start | bytes 98312 | tf_op jit(solution)/shard_map/ppermute | solution.py:346
  15.6 8.0 %collective-permute-start.5 = (bf16[128,128]{1,0:T(8,128)(2,1)S(1)}, bf16[128,128]{1,0:T(8,128)(2,1)S(1)}, u32[]{:S(2)}, u32[]{:S(2)}) collective-permute-start(bf16[128,128]{1,0:T(8,128)(2,1)S(1)} %get-tuple-element.40), channel_id=1, source_target_pairs={{0,5},{1,4},{2,7},{3,6},{4,1},{5,0},{6,3},{7,2},{8,13},{9,12},{10,... | collective-permute-start | bytes 98312 | tf_op jit(solution)/shard_map/ppermute | solution.py:346
  18.4 5.2 %collective-permute-start.6 = (bf16[128,128]{1,0:T(8,128)(2,1)S(1)}, bf16[128,128]{1,0:T(8,128)(2,1)S(1)}, u32[]{:S(2)}, u32[]{:S(2)}) collective-permute-start(bf16[128,128]{1,0:T(8,128)(2,1)S(1)} %get-tuple-element.41), channel_id=1, source_target_pairs={{0,3},{1,2},{2,1},{3,0},{4,7},{5,6},{6,5},{7,4},{8,11},{9,10},{10,... | collective-permute-start | bytes 98312 | tf_op jit(solution)/shard_map/ppermute | solution.py:346
  43.5 17.3 %all-to-all-start.3 = ((bf16[16,128,128]{2,1,0:T(8,128)(2,1)}), bf16[16,128,128]{2,1,0:T(8,128)(2,1)S(1)}, u32[]{:S(2)}, u32[]{:S(2)}) async-start(bf16[16,128,128]{2,1,0:T(8,128)(2,1)} %get-tuple-element.46), calls=%async_computation.3 | async-start | bytes 1048576 | tf_op jit(solution)/shard_map/all_to_all | solution.py:329
  48.4 7.7 %copy-start.5 = (bf16[128,128]{1,0:T(8,128)(2,1)S(1)}, bf16[128,128]{1,0:T(8,128)(2,1)}, u32[]{:S(2)}) copy-start(bf16[128,128]{1,0:T(8,128)(2,1)} %refs_4_.8) | copy-start | bytes 98308
  48.7 4.5 %collective-permute-start.7 = (bf16[128,128]{1,0:T(8,128)(2,1)S(1)}, bf16[128,128]{1,0:T(8,128)(2,1)S(1)}, u32[]{:S(2)}, u32[]{:S(2)}) collective-permute-start(bf16[128,128]{1,0:T(8,128)(2,1)S(1)} %get-tuple-element.50), channel_id=1, source_target_pairs={{0,1},{1,0},{2,3},{3,2},{4,5},{5,4},{6,7},{7,6},{8,9},{9,8},{10,11... | collective-permute-start | bytes 98312 | tf_op jit(solution)/shard_map/ppermute | solution.py:346
  48.9 7.1 %collective-permute-start.8 = (bf16[128,128]{1,0:T(8,128)(2,1)S(1)}, bf16[128,128]{1,0:T(8,128)(2,1)S(1)}, u32[]{:S(2)}, u32[]{:S(2)}) collective-permute-start(bf16[128,128]{1,0:T(8,128)(2,1)S(1)} %get-tuple-element.51), channel_id=1, source_target_pairs={{0,2},{1,3},{2,0},{3,1},{4,6},{5,7},{6,4},{7,5},{8,10},{9,11},{10,... | collective-permute-start | bytes 98312 | tf_op jit(solution)/shard_map/ppermute | solution.py:346
  50.4 8.3 %collective-permute-start.9 = (bf16[128,128]{1,0:T(8,128)(2,1)S(1)}, bf16[128,128]{1,0:T(8,128)(2,1)S(1)}, u32[]{:S(2)}, u32[]{:S(2)}) collective-permute-start(bf16[128,128]{1,0:T(8,128)(2,1)S(1)} %get-tuple-element.52), channel_id=1, source_target_pairs={{0,6},{1,7},{2,4},{3,5},{4,2},{5,3},{6,0},{7,1},{8,14},{9,15},{10,... | collective-permute-start | bytes 98312 | tf_op jit(solution)/shard_map/ppermute | solution.py:346
  50.7 8.7 %collective-permute-start.10 = (bf16[128,128]{1,0:T(8,128)(2,1)S(1)}, bf16[128,128]{1,0:T(8,128)(2,1)S(1)}, u32[]{:S(2)}, u32[]{:S(2)}) collective-permute-start(bf16[128,128]{1,0:T(8,128)(2,1)S(1)} %get-tuple-element.53), channel_id=1, source_target_pairs={{0,7},{1,6},{2,5},{3,4},{4,3},{5,2},{6,1},{7,0},{8,15},{9,14},{10,... | collective-permute-start | bytes 98312 | tf_op jit(solution)/shard_map/ppermute | solution.py:346
  52.8 7.2 %collective-permute-start.11 = (bf16[128,128]{1,0:T(8,128)(2,1)S(1)}, bf16[128,128]{1,0:T(8,128)(2,1)S(1)}, u32[]{:S(2)}, u32[]{:S(2)}) collective-permute-start(bf16[128,128]{1,0:T(8,128)(2,1)S(1)} %get-tuple-element.54), channel_id=1, source_target_pairs={{0,4},{1,5},{2,6},{3,7},{4,0},{5,1},{6,2},{7,3},{8,12},{9,13},{10,... | collective-permute-start | bytes 98312 | tf_op jit(solution)/shard_map/ppermute | solution.py:346
  53.3 7.1 %collective-permute-start.12 = (bf16[128,128]{1,0:T(8,128)(2,1)S(1)}, bf16[128,128]{1,0:T(8,128)(2,1)S(1)}, u32[]{:S(2)}, u32[]{:S(2)}) collective-permute-start(bf16[128,128]{1,0:T(8,128)(2,1)S(1)} %get-tuple-element.55), channel_id=1, source_target_pairs={{0,5},{1,4},{2,7},{3,6},{4,1},{5,0},{6,3},{7,2},{8,13},{9,12},{10,... | collective-permute-start | bytes 98312 | tf_op jit(solution)/shard_map/ppermute | solution.py:346
  56.0 4.3 %collective-permute-start.13 = (bf16[128,128]{1,0:T(8,128)(2,1)S(1)}, bf16[128,128]{1,0:T(8,128)(2,1)S(1)}, u32[]{:S(2)}, u32[]{:S(2)}) collective-permute-start(bf16[128,128]{1,0:T(8,128)(2,1)S(1)} %get-tuple-element.56), channel_id=1, source_target_pairs={{0,3},{1,2},{2,1},{3,0},{4,7},{5,6},{6,5},{7,4},{8,11},{9,10},{10,... | collective-permute-start | bytes 98312 | tf_op jit(solution)/shard_map/ppermute | solution.py:346
  (5 other events, 16.8 us)

commit v26 on v25

--- a/solution.py
+++ b/solution.py
@@ -102,7 +102,7 @@
 
 
 def distance(step, count):
-    far = sorted(range(3, count), key=lambda apart: -(apart // 2))
+    far = sorted(range(3, count), reverse=True)
     return [*range(min(3, count)), *far][step]
 
 

time: 62.7 us -> 63.1 us (level)
  transfers between devices with their start and end apart: 16 -> 16, of which waited for: 10 -> 11; matrix products, arithmetic and copies ran while one was open for 0% -> 0% of each run, Pallas kernels for 6% -> 6%
where the time goes in v26:
time: 63.1 us; the launch traced here: 62.6 us
  starting transfers between devices  24.7 us (39%)
  blocking collectives  17.3 us (27%)
  Pallas kernels  9.79 us (16%)
  waiting for transfers between devices  8.88 us (14%)
  local copies, waits for them, and re-layouts  1.64 us (3%)
    all_to_all x2, blocking collectives, swap_half(): lax.all_to_all(values, 'row', split_axis=0, concat_axis=0, tiled=True, ax...  17.3 us
    all_to_all x2, starting transfers between devices, swap(): lax.all_to_all(values, 'row', split_axis=0, concat_axis=0, tiled=True, ax...  13.4 us
    ppermute x14, starting transfers between devices, swap_pieces(): lax.ppermute(pieces[step], 'row', [(d, d ^ distance(step, count)) for d i...  11.3 us
    pallas_call x12, Pallas kernels, call(): pl.pallas_call(body, name=name, out_shape=outs, in_specs=[pl.BlockSpec(me...  9.79 us
    ppermute x14, waiting for transfers between devices, swap_pieces(): lax.ppermute(pieces[step], 'row', [(d, d ^ distance(step, count)) for d i...  8.42 us
    unnamed x26, local copies, waits for them, and re-layouts  1.64 us
  transfers between devices with their start and end apart: 16, of which 11 were waited for; matrix products, arithmetic and copies ran while one was open for 0% of the time, Pallas kernels for 6%

profile of v26, /device:TPU:0, one launch (start us, length us, event | category | flops | bytes accessed | tf_op | source)
XLA Modules:
  0.0 62.6 jit_solution(4120669794101258436)
XLA Ops:
  0.0 2.4 %project_right.1.refs_5_ = bf16[16,128,128]{2,1,0:T(8,128)(2,1)} custom-call(bf16[8,128,128]{2,1,0:T(8,128)(2,1)} %refs_0_.7, s32[1,128]{1,0:T(1,128)} %bitcast.13, f32[1,128]{1,0:T(1,128)} %bitcast.5, f32[1,128]{1,0:T(1,128)} %bitcast.9, bf16[128,512]{1,0:T(8,128)(2,1)} %refs_4_.9), custom_call_target="tpu_custom_call" | custom-call | flops 67108864 | bytes 919040 | tf_op jit(solution)/shard_map/project_right/pallas_call | solution.py:65
  2.5 8.5 %all-to-all-start = ((bf16[16,128,128]{2,1,0:T(8,128)(2,1)}), bf16[16,128,128]{2,1,0:T(8,128)(2,1)S(1)}, u32[]{:S(2)}, u32[]{:S(2)}) async-start(bf16[16,128,128]{2,1,0:T(8,128)(2,1)} %project_right.1.refs_5_), calls=%async_computation | async-start | bytes 1048576 | tf_op jit(solution)/shard_map/all_to_all | solution.py:329
  11.1 0.8 %project_left.1 = (bf16[128,128]{1,0:T(8,128)(2,1)S(1)}, bf16[128,128]{1,0:T(8,128)(2,1)S(1)}, bf16[128,128]{1,0:T(8,128)(2,1)S(1)}, bf16[128,128]{1,0:T(8,128)(...) custom-call(bf16[8,128,128]{2,1,0:T(8,128)(2,1)S(1)} %copy-done.1, ...), custom_call_target="tpu_custom_call" | custom-call | flops 67108864 | bytes 1181184 | tf_op jit(solution)/shard_map/project_left/pallas_call | solution.py:65
  12.7 1.0 %collective-permute-start.2 = (bf16[128,128]{1,0:T(8,128)(2,1)S(1)}, bf16[128,128]{1,0:T(8,128)(2,1)S(1)}, u32[]{:S(2)}, u32[]{:S(2)}) collective-permute-start(bf16[128,128]{1,0:T(8,128)(2,1)S(1)} %get-tuple-element.37), channel_id=1, source_target_pairs={{0,7},{1,6},{2,5},{3,4},{4,3},{5,2},{6,1},{7,0},{8,15},{9,14},{10,... | collective-permute-start | bytes 98312 | tf_op jit(solution)/shard_map/ppermute | solution.py:346
  13.7 1.5 %collective-permute-start.3 = (bf16[128,128]{1,0:T(8,128)(2,1)S(1)}, bf16[128,128]{1,0:T(8,128)(2,1)S(1)}, u32[]{:S(2)}, u32[]{:S(2)}) collective-permute-start(bf16[128,128]{1,0:T(8,128)(2,1)S(1)} %get-tuple-element.38), channel_id=1, source_target_pairs={{0,6},{1,7},{2,4},{3,5},{4,2},{5,3},{6,0},{7,1},{8,14},{9,15},{10,... | collective-permute-start | bytes 98312 | tf_op jit(solution)/shard_map/ppermute | solution.py:346
  15.6 1.5 %collective-permute-start.5 = (bf16[128,128]{1,0:T(8,128)(2,1)S(1)}, bf16[128,128]{1,0:T(8,128)(2,1)S(1)}, u32[]{:S(2)}, u32[]{:S(2)}) collective-permute-start(bf16[128,128]{1,0:T(8,128)(2,1)S(1)} %get-tuple-element.40), channel_id=1, source_target_pairs={{0,4},{1,5},{2,6},{3,7},{4,0},{5,1},{6,2},{7,3},{8,12},{9,13},{10,... | collective-permute-start | bytes 98312 | tf_op jit(solution)/shard_map/ppermute | solution.py:346
  17.1 1.3 %collective-permute-done.1.refs_2_ = bf16[128,128]{1,0:T(8,128)(2,1)S(1)} collective-permute-done((bf16[128,128]{1,0:T(8,128)(2,1)S(1)}, bf16[128,128]{1,0:T(8,128)(2,1)S(1)}, u32[]{:S(2)}, u32[]{:S(2)}) %collective-permute-start.1) | collective-permute-done | bytes 32800 | tf_op jit(solution)/shard_map/ppermute | solution.py:346
  19.0 0.8 %prepare.1 = (f32[8,128,128]{2,1,0:T(8,128)S(1)}, f32[8,128,128]{2,1,0:T(8,128)S(1)}) custom-call(bf16[8,128,128]{2,1,0:T(8,128)(2,1)S(1)} %copy-done.1, bf16[8,128,128]{2,1,0:T(8,128)(2,1)S(1)} %copy-done.3, f32[1,128]{1,0:T(1,128)S(1)} %bitcast.7, f32[1,128]{1,0:T(1,128)S(1)} %bitcast.11, bf16[128,128]{1,0:T(8,128)(2,1)S(1)} %copy-done.6, ...), custom_call_target="tpu_custom_call" | custom-call | flops 67108864 | bytes 1639936 | tf_op jit(solution)/shard_map/prepare/pallas_call | solution.py:65
  19.9 1.5 %collective-permute-done.2.refs_3_ = bf16[128,128]{1,0:T(8,128)(2,1)S(1)} collective-permute-done((bf16[128,128]{1,0:T(8,128)(2,1)S(1)}, bf16[128,128]{1,0:T(8,128)(2,1)S(1)}, u32[]{:S(2)}, u32[]{:S(2)}) %collective-permute-start.2) | collective-permute-done | bytes 32800 | tf_op jit(solution)/shard_map/ppermute | solution.py:346
  21.3 0.7 %collective-permute-done.3.refs_4_ = bf16[128,128]{1,0:T(8,128)(2,1)S(1)} collective-permute-done((bf16[128,128]{1,0:T(8,128)(2,1)S(1)}, bf16[128,128]{1,0:T(8,128)(2,1)S(1)}, u32[]{:S(2)}, u32[]{:S(2)}) %collective-permute-start.3) | collective-permute-done | bytes 32800 | tf_op jit(solution)/shard_map/ppermute | solution.py:346
  22.6 1.3 %collective-permute-done.5.refs_6_ = bf16[128,128]{1,0:T(8,128)(2,1)S(1)} collective-permute-done((bf16[128,128]{1,0:T(8,128)(2,1)S(1)}, bf16[128,128]{1,0:T(8,128)(2,1)S(1)}, u32[]{:S(2)}, u32[]{:S(2)}) %collective-permute-start.5) | collective-permute-done | bytes 32800 | tf_op jit(solution)/shard_map/ppermute | solution.py:346
  24.2 0.6 %tri.1 = (bf16[8,128,128]{2,1,0:T(8,128)(2,1)S(1)}, bf16[16,128,128]{2,1,0:T(8,128)(2,1)S(1)}) custom-call(bf16[16,128,128]{2,1,0:T(8,128)(2,1)S(1)} %all-to-all-done.refs_0_, bf16[16,64,128]{2,1,0:T(8,128)(2,1)S(1)} %get-tuple-element.42.refs_1_, f32[8,128,128]{2,1,0:T(8,128)S(1)} %get-tuple-element.43.refs_2_.refs_1_), custom_call_target="tpu_custom_call" | custom-call | flops 33554432 | bytes 2097152 | tf_op jit(solution)/shard_map/tri/pallas_call | solution.py:65
  24.8 8.7 %all_to_all.20.refs_0_ = bf16[8,128,128]{2,1,0:T(8,128)(2,1)S(1)} all-to-all(bf16[8,128,128]{2,1,0:T(8,128)(2,1)S(1)} %get-tuple-element.44), channel_id=1, replica_groups={{0,1,2,3,4,5,6,7},{8,9,10,11,12,13,14,15},{16,17,18,19,20,21,22,23},{24..., dimensions={0} | all-to-all | bytes 524288 | tf_op jit(solution)/shard_map/all_to_all | solution.py:337
  33.8 8.6 %all_to_all.21.refs_0_ = bf16[8,128,128]{2,1,0:T(8,128)(2,1)S(1)} all-to-all(bf16[8,128,128]{2,1,0:T(8,128)(2,1)S(1)} %middle.1), channel_id=1, replica_groups={{0,1,2,3,4,5,6,7},{8,9,10,11,12,13,14,15},{16,17,18,19,20,21,22,23},{24..., dimensions={0} | all-to-all | bytes 524288 | tf_op jit(solution)/shard_map/all_to_all | solution.py:337
  42.5 1.4 %d_right.1 = (bf16[16,128,128]{2,1,0:T(8,128)(2,1)}, bf16[16,64,128]{2,1,0:T(8,128)(2,1)S(1)}) custom-call(bf16[8,128,128]{2,1,0:T(8,128)(2,1)S(1)} %all_to_all.21.refs_0_, bf16[8,128,256]{2,1,0:T(8,128)(2,1)S(1)} %get-tuple-element.45.refs_1_), custom_call_target="tpu_custom_call" | custom-call | flops 33554432 | bytes 1572864 | tf_op jit(solution)/shard_map/d_right/pallas_call | solution.py:65
  43.9 4.9 %all-to-all-start.3 = ((bf16[16,128,128]{2,1,0:T(8,128)(2,1)}), bf16[16,128,128]{2,1,0:T(8,128)(2,1)S(1)}, u32[]{:S(2)}, u32[]{:S(2)}) async-start(bf16[16,128,128]{2,1,0:T(8,128)(2,1)} %get-tuple-element.46), calls=%async_computation.3 | async-start | bytes 1048576 | tf_op jit(solution)/shard_map/all_to_all | solution.py:329
  49.3 1.5 %collective-permute-start.8 = (bf16[128,128]{1,0:T(8,128)(2,1)S(1)}, bf16[128,128]{1,0:T(8,128)(2,1)S(1)}, u32[]{:S(2)}, u32[]{:S(2)}) collective-permute-start(bf16[128,128]{1,0:T(8,128)(2,1)S(1)} %get-tuple-element.51), channel_id=1, source_target_pairs={{0,2},{1,3},{2,0},{3,1},{4,6},{5,7},{6,4},{7,5},{8,10},{9,11},{10,... | collective-permute-start | bytes 98312 | tf_op jit(solution)/shard_map/ppermute | solution.py:346
  50.8 2.6 %collective-permute-start.10 = (bf16[128,128]{1,0:T(8,128)(2,1)S(1)}, bf16[128,128]{1,0:T(8,128)(2,1)S(1)}, u32[]{:S(2)}, u32[]{:S(2)}) collective-permute-start(bf16[128,128]{1,0:T(8,128)(2,1)S(1)} %get-tuple-element.53), channel_id=1, source_target_pairs={{0,6},{1,7},{2,4},{3,5},{4,2},{5,3},{6,0},{7,1},{8,14},{9,15},{10,... | collective-permute-start | bytes 98312 | tf_op jit(solution)/shard_map/ppermute | solution.py:346
  53.7 1.5 %collective-permute-start.12 = (bf16[128,128]{1,0:T(8,128)(2,1)S(1)}, bf16[128,128]{1,0:T(8,128)(2,1)S(1)}, u32[]{:S(2)}, u32[]{:S(2)}) collective-permute-start(bf16[128,128]{1,0:T(8,128)(2,1)S(1)} %get-tuple-element.55), channel_id=1, source_target_pairs={{0,4},{1,5},{2,6},{3,7},{4,0},{5,1},{6,2},{7,3},{8,12},{9,13},{10,... | collective-permute-start | bytes 98312 | tf_op jit(solution)/shard_map/ppermute | solution.py:346
  55.2 1.2 %collective-permute-done.8.refs_2_ = bf16[128,128]{1,0:T(8,128)(2,1)S(1)} collective-permute-done((bf16[128,128]{1,0:T(8,128)(2,1)S(1)}, bf16[128,128]{1,0:T(8,128)(2,1)S(1)}, u32[]{:S(2)}, u32[]{:S(2)}) %collective-permute-start.8) | collective-permute-done | bytes 32800 | tf_op jit(solution)/shard_map/ppermute | solution.py:346
  56.4 0.6 %copy-done.12 = f32[128]{0:T(128)S(1)} copy-done((f32[128]{0:T(128)S(1)}, f32[128]{0:T(128)}, u32[]{:S(2)}) %copy-start.12) | copy-done | bytes 536
  57.8 1.0 %slopes.1 = (bf16[8,512,128]{2,1,0:T(8,128)(2,1)S(1)}, bf16[8,128,128]{2,1,0:T(8,128)(2,1)S(1)}, f32[8,128]{1,0:T(8,128)S(1)}, f32[128,128]{1,0:T(8,128)S(1)}, bf16[128,640]{1,0:T(8,128)(2,1)S(1)}) custom-call(bf16[8,128,128]{2,1,0:T(8,128)(2,1)S(1)} %copy-done.1, s32[1,128]{1,0:T(1,128)S(1)} %bitcast.15, f32[1,128]{1,0:T(1,128)S(1)} %bitcast.8, ...), custom_call_target="tpu_custom_call" | custom-call | flops 134217728 | bytes 2233856 | tf_op jit(solution)/shard_map/slopes/pallas_call | solution.py:65
  59.1 1.1 %collective-permute-done.10.refs_4_ = bf16[128,128]{1,0:T(8,128)(2,1)S(1)} collective-permute-done((bf16[128,128]{1,0:T(8,128)(2,1)S(1)}, bf16[128,128]{1,0:T(8,128)(2,1)S(1)}, u32[]{:S(2)}, u32[]{:S(2)}) %collective-permute-start.10) | collective-permute-done | bytes 32800 | tf_op jit(solution)/shard_map/ppermute | solution.py:346
  61.2 1.4 %finish.1 = bf16[8,128,128]{2,1,0:T(8,128)(2,1)} custom-call(bf16[16,128,128]{2,1,0:T(8,128)(2,1)S(1)} %all-to-all-done.3.refs_0_, bf16[8,128,128]{2,1,0:T(8,128)(2,1)S(1)} %sort_d_left.1.refs_1_, bf16[8,512,128]{2,1,0:T(8,128)(2,1)S(1)} %get-tuple-element.58.refs_2_, bf16[8,128,128]{2,1,0:T(8,128)(2,1)S(1)} %gate_back.1.refs_6_.refs_3_, ...), custom_call_target="tpu_custom_call" | custom-call | flops 134217728 | bytes 2854912 | tf_op jit(solution)/shard_map/finish/pallas_call | solution.py:65
  (48 shorter events, 5.8 us)
Async XLA Ops:
  2.4 8.6 %copy-start = (bf16[16,128,128]{2,1,0:T(8,128)(2,1)S(1)}, bf16[16,128,128]{2,1,0:T(8,128)(2,1)}, u32[]{:S(2)}) copy-start(bf16[16,128,128]{2,1,0:T(8,128)(2,1)} %project_right.1.refs_5_) | copy-start | bytes 1572868
  2.4 8.6 %copy-start.1 = (bf16[8,128,128]{2,1,0:T(8,128)(2,1)S(1)}, bf16[8,128,128]{2,1,0:T(8,128)(2,1)}, u32[]{:S(2)}) copy-start(bf16[8,128,128]{2,1,0:T(8,128)(2,1)} %refs_0_.7) | copy-start | bytes 786436
  2.4 8.6 %copy-start.2 = (bf16[128,512]{1,0:T(8,128)(2,1)S(1)}, bf16[128,512]{1,0:T(8,128)(2,1)}, u32[]{:S(2)}) copy-start(bf16[128,512]{1,0:T(8,128)(2,1)} %refs_4_.9) | copy-start | bytes 393220
  2.4 8.6 %copy-start.8 = (f32[128]{0:T(128)S(1)}, f32[128]{0:T(128)}, u32[]{:S(2)}) copy-start(f32[128]{0:T(128)} %param.13) | copy-start | bytes 1540
  2.4 8.6 %copy-start.9 = (f32[128]{0:T(128)S(1)}, f32[128]{0:T(128)}, u32[]{:S(2)}) copy-start(f32[128]{0:T(128)} %param.14) | copy-start | bytes 1540
  2.5 8.6 %copy-start.10 = (s32[128]{0:T(128)S(1)}, s32[128]{0:T(128)}, u32[]{:S(2)}) copy-start(s32[128]{0:T(128)} %param.12) | copy-start | bytes 1540
  2.5 21.7 %all-to-all-start = ((bf16[16,128,128]{2,1,0:T(8,128)(2,1)}), bf16[16,128,128]{2,1,0:T(8,128)(2,1)S(1)}, u32[]{:S(2)}, u32[]{:S(2)}) async-start(bf16[16,128,128]{2,1,0:T(8,128)(2,1)} %project_right.1.refs_5_), calls=%async_computation | async-start | bytes 1048576 | tf_op jit(solution)/shard_map/all_to_all | solution.py:329
  11.0 7.4 %copy-start.3 = (bf16[8,128,128]{2,1,0:T(8,128)(2,1)S(1)}, bf16[8,128,128]{2,1,0:T(8,128)(2,1)}, u32[]{:S(2)}) copy-start(bf16[8,128,128]{2,1,0:T(8,128)(2,1)} %refs_1_.1) | copy-start | bytes 786436
  11.9 3.7 %collective-permute-start = (bf16[128,128]{1,0:T(8,128)(2,1)S(1)}, bf16[128,128]{1,0:T(8,128)(2,1)S(1)}, u32[]{:S(2)}, u32[]{:S(2)}) collective-permute-start(bf16[128,128]{1,0:T(8,128)(2,1)S(1)} %get-tuple-element.35), channel_id=1, source_target_pairs={{0,1},{1,0},{2,3},{3,2},{4,5},{5,4},{6,7},{7,6},{8,9},{9,8},{10,11... | collective-permute-start | bytes 98312 | tf_op jit(solution)/shard_map/ppermute | solution.py:346
  12.1 6.3 %collective-permute-start.1 = (bf16[128,128]{1,0:T(8,128)(2,1)S(1)}, bf16[128,128]{1,0:T(8,128)(2,1)S(1)}, u32[]{:S(2)}, u32[]{:S(2)}) collective-permute-start(bf16[128,128]{1,0:T(8,128)(2,1)S(1)} %get-tuple-element.36), channel_id=1, source_target_pairs={{0,2},{1,3},{2,0},{3,1},{4,6},{5,7},{6,4},{7,5},{8,10},{9,11},{10,... | collective-permute-start | bytes 98312 | tf_op jit(solution)/shard_map/ppermute | solution.py:346
  12.7 8.6 %collective-permute-start.2 = (bf16[128,128]{1,0:T(8,128)(2,1)S(1)}, bf16[128,128]{1,0:T(8,128)(2,1)S(1)}, u32[]{:S(2)}, u32[]{:S(2)}) collective-permute-start(bf16[128,128]{1,0:T(8,128)(2,1)S(1)} %get-tuple-element.37), channel_id=1, source_target_pairs={{0,7},{1,6},{2,5},{3,4},{4,3},{5,2},{6,1},{7,0},{8,15},{9,14},{10,... | collective-permute-start | bytes 98312 | tf_op jit(solution)/shard_map/ppermute | solution.py:346
  13.7 8.3 %collective-permute-start.3 = (bf16[128,128]{1,0:T(8,128)(2,1)S(1)}, bf16[128,128]{1,0:T(8,128)(2,1)S(1)}, u32[]{:S(2)}, u32[]{:S(2)}) collective-permute-start(bf16[128,128]{1,0:T(8,128)(2,1)S(1)} %get-tuple-element.38), channel_id=1, source_target_pairs={{0,6},{1,7},{2,4},{3,5},{4,2},{5,3},{6,0},{7,1},{8,14},{9,15},{10,... | collective-permute-start | bytes 98312 | tf_op jit(solution)/shard_map/ppermute | solution.py:346
  15.3 7.3 %collective-permute-start.4 = (bf16[128,128]{1,0:T(8,128)(2,1)S(1)}, bf16[128,128]{1,0:T(8,128)(2,1)S(1)}, u32[]{:S(2)}, u32[]{:S(2)}) collective-permute-start(bf16[128,128]{1,0:T(8,128)(2,1)S(1)} %get-tuple-element.39), channel_id=1, source_target_pairs={{0,5},{1,4},{2,7},{3,6},{4,1},{5,0},{6,3},{7,2},{8,13},{9,12},{10,... | collective-permute-start | bytes 98312 | tf_op jit(solution)/shard_map/ppermute | solution.py:346
  15.6 8.4 %collective-permute-start.5 = (bf16[128,128]{1,0:T(8,128)(2,1)S(1)}, bf16[128,128]{1,0:T(8,128)(2,1)S(1)}, u32[]{:S(2)}, u32[]{:S(2)}) collective-permute-start(bf16[128,128]{1,0:T(8,128)(2,1)S(1)} %get-tuple-element.40), channel_id=1, source_target_pairs={{0,4},{1,5},{2,6},{3,7},{4,0},{5,1},{6,2},{7,3},{8,12},{9,13},{10,... | collective-permute-start | bytes 98312 | tf_op jit(solution)/shard_map/ppermute | solution.py:346
  18.4 5.5 %collective-permute-start.6 = (bf16[128,128]{1,0:T(8,128)(2,1)S(1)}, bf16[128,128]{1,0:T(8,128)(2,1)S(1)}, u32[]{:S(2)}, u32[]{:S(2)}) collective-permute-start(bf16[128,128]{1,0:T(8,128)(2,1)S(1)} %get-tuple-element.41), channel_id=1, source_target_pairs={{0,3},{1,2},{2,1},{3,0},{4,7},{5,6},{6,5},{7,4},{8,11},{9,10},{10,... | collective-permute-start | bytes 98312 | tf_op jit(solution)/shard_map/ppermute | solution.py:346
  43.9 17.3 %all-to-all-start.3 = ((bf16[16,128,128]{2,1,0:T(8,128)(2,1)}), bf16[16,128,128]{2,1,0:T(8,128)(2,1)S(1)}, u32[]{:S(2)}, u32[]{:S(2)}) async-start(bf16[16,128,128]{2,1,0:T(8,128)(2,1)} %get-tuple-element.46), calls=%async_computation.3 | async-start | bytes 1048576 | tf_op jit(solution)/shard_map/all_to_all | solution.py:329
  48.7 7.7 %copy-start.5 = (bf16[128,128]{1,0:T(8,128)(2,1)S(1)}, bf16[128,128]{1,0:T(8,128)(2,1)}, u32[]{:S(2)}) copy-start(bf16[128,128]{1,0:T(8,128)(2,1)} %refs_4_.8) | copy-start | bytes 98308
  49.1 4.6 %collective-permute-start.7 = (bf16[128,128]{1,0:T(8,128)(2,1)S(1)}, bf16[128,128]{1,0:T(8,128)(2,1)S(1)}, u32[]{:S(2)}, u32[]{:S(2)}) collective-permute-start(bf16[128,128]{1,0:T(8,128)(2,1)S(1)} %get-tuple-element.50), channel_id=1, source_target_pairs={{0,1},{1,0},{2,3},{3,2},{4,5},{5,4},{6,7},{7,6},{8,9},{9,8},{10,11... | collective-permute-start | bytes 98312 | tf_op jit(solution)/shard_map/ppermute | solution.py:346
  49.3 7.1 %collective-permute-start.8 = (bf16[128,128]{1,0:T(8,128)(2,1)S(1)}, bf16[128,128]{1,0:T(8,128)(2,1)S(1)}, u32[]{:S(2)}, u32[]{:S(2)}) collective-permute-start(bf16[128,128]{1,0:T(8,128)(2,1)S(1)} %get-tuple-element.51), channel_id=1, source_target_pairs={{0,2},{1,3},{2,0},{3,1},{4,6},{5,7},{6,4},{7,5},{8,10},{9,11},{10,... | collective-permute-start | bytes 98312 | tf_op jit(solution)/shard_map/ppermute | solution.py:346
  50.8 8.3 %collective-permute-start.9 = (bf16[128,128]{1,0:T(8,128)(2,1)S(1)}, bf16[128,128]{1,0:T(8,128)(2,1)S(1)}, u32[]{:S(2)}, u32[]{:S(2)}) collective-permute-start(bf16[128,128]{1,0:T(8,128)(2,1)S(1)} %get-tuple-element.52), channel_id=1, source_target_pairs={{0,7},{1,6},{2,5},{3,4},{4,3},{5,2},{6,1},{7,0},{8,15},{9,14},{10,... | collective-permute-start | bytes 98312 | tf_op jit(solution)/shard_map/ppermute | solution.py:346
  50.8 9.3 %collective-permute-start.10 = (bf16[128,128]{1,0:T(8,128)(2,1)S(1)}, bf16[128,128]{1,0:T(8,128)(2,1)S(1)}, u32[]{:S(2)}, u32[]{:S(2)}) collective-permute-start(bf16[128,128]{1,0:T(8,128)(2,1)S(1)} %get-tuple-element.53), channel_id=1, source_target_pairs={{0,6},{1,7},{2,4},{3,5},{4,2},{5,3},{6,0},{7,1},{8,14},{9,15},{10,... | collective-permute-start | bytes 98312 | tf_op jit(solution)/shard_map/ppermute | solution.py:346
  53.4 7.0 %collective-permute-start.11 = (bf16[128,128]{1,0:T(8,128)(2,1)S(1)}, bf16[128,128]{1,0:T(8,128)(2,1)S(1)}, u32[]{:S(2)}, u32[]{:S(2)}) collective-permute-start(bf16[128,128]{1,0:T(8,128)(2,1)S(1)} %get-tuple-element.54), channel_id=1, source_target_pairs={{0,5},{1,4},{2,7},{3,6},{4,1},{5,0},{6,3},{7,2},{8,13},{9,12},{10,... | collective-permute-start | bytes 98312 | tf_op jit(solution)/shard_map/ppermute | solution.py:346
  53.7 7.0 %collective-permute-start.12 = (bf16[128,128]{1,0:T(8,128)(2,1)S(1)}, bf16[128,128]{1,0:T(8,128)(2,1)S(1)}, u32[]{:S(2)}, u32[]{:S(2)}) collective-permute-start(bf16[128,128]{1,0:T(8,128)(2,1)S(1)} %get-tuple-element.55), channel_id=1, source_target_pairs={{0,4},{1,5},{2,6},{3,7},{4,0},{5,1},{6,2},{7,3},{8,12},{9,13},{10,... | collective-permute-start | bytes 98312 | tf_op jit(solution)/shard_map/ppermute | solution.py:346
  56.4 4.3 %collective-permute-start.13 = (bf16[128,128]{1,0:T(8,128)(2,1)S(1)}, bf16[128,128]{1,0:T(8,128)(2,1)S(1)}, u32[]{:S(2)}, u32[]{:S(2)}) collective-permute-start(bf16[128,128]{1,0:T(8,128)(2,1)S(1)} %get-tuple-element.56), channel_id=1, source_target_pairs={{0,3},{1,2},{2,1},{3,0},{4,7},{5,6},{6,5},{7,4},{8,11},{9,10},{10,... | collective-permute-start | bytes 98312 | tf_op jit(solution)/shard_map/ppermute | solution.py:346
  (5 other events, 16.8 us)

commit v27 on v25

--- a/solution.py
+++ b/solution.py
@@ -39,7 +39,7 @@
 
 
 def call(
-    kernel, name, outs, args, fetched=(), unread=(), scratch=(), flops=0, limit=VMEM_LIMIT
+    kernel, name, outs, args, fetched=(), columns={}, unread=(), scratch=(), flops=0, limit=VMEM_LIMIT
 ):
     moved = sum(a.size * a.dtype.itemsize for a in args) + sum(
         o.size * jnp.dtype(o.dtype).itemsize for o in outs
@@ -51,7 +51,8 @@
         rest = refs[n_args + n_outs :]
         copies = []
         for n, place in enumerate(fetched):
-            copies.append(pltpu.make_async_copy(ins[place], rest[n], rest[n_fetched].at[n]))
+            source = ins[place].at[:, columns[place]] if place in columns else ins[place]
+            copies.append(pltpu.make_async_copy(source, rest[n], rest[n_fetched].at[n]))
             ins[place] = rest[n]
         for copy in copies:
             copy.start()
@@ -59,7 +60,13 @@
             copy.wait()
         kernel(*ins, *refs[n_args : n_args + n_outs], *rest[n_fetched + (n_fetched > 0) :])
 
-    buffers = [pltpu.VMEM(args[place].shape, args[place].dtype) for place in fetched]
+    buffers = [
+        pltpu.VMEM(
+            (*args[place].shape[:-1], columns[place].size) if place in columns else args[place].shape,
+            args[place].dtype,
+        )
+        for place in fetched
+    ]
     if fetched:
         buffers.append(pltpu.SemaphoreType.DMA((n_fetched,)))
     return pl.pallas_call(
@@ -110,10 +117,10 @@
     return lax.rem(lax.axis_index("row"), count) ^ distance(step, count)
 
 
-def gated_rows(pair, mask, gain, bias, w_proj, side):
+def gated_rows(pair, mask, gain, bias, w_side):
     rows = pair.shape[0]
-    hidden = w_proj.shape[1] // 4
-    w_flip = transposed(w_proj[:, 2 * side * hidden : 2 * (side + 1) * hidden])
+    hidden = w_side.shape[1] // 2
+    w_flip = transposed(w_side[...])
     gain_col, bias_col = column(gain[...]), column(bias[...])
     masks = cell_masks(mask, rows)
     for row in range(rows):
@@ -123,25 +130,25 @@
         yield row, masks[row] * sigmoid(proj[:hidden]) * proj[hidden:]
 
 
-def project_right_kernel(pair, mask, gain, bias, w_proj, right_panel):
+def project_right_kernel(pair, mask, gain, bias, w_side, right_panel):
     rows = pair.shape[0]
     devices, depth, width = right_panel.shape
     block = depth // rows
-    count = w_proj.shape[1] // 4 // block
-    for row, right in gated_rows(pair, mask, gain, bias, w_proj, 1):
+    count = w_side.shape[1] // 2 // block
+    for row, right in gated_rows(pair, mask, gain, bias, w_side):
         right = right.reshape(count, block, width).astype(BF16)
         for rank in range(devices):
             place = wide_order(devices, count, False)[rank] % count
             right_panel[rank, row * block : (row + 1) * block, :] = right[place]
 
 
-def project_left_kernel(pair, mask, gain, bias, w_proj, after, *refs):
+def project_left_kernel(pair, mask, gain, bias, w_side, after, *refs):
     del after
     *pieces, left_panel = refs
     rows = pair.shape[0]
     count, depth, width = left_panel.shape
     block = depth // rows
-    for row, left in gated_rows(pair, mask, gain, bias, w_proj, 0):
+    for row, left in gated_rows(pair, mask, gain, bias, w_side):
         left = left.reshape(count, block, width).astype(BF16)
         left_panel[:, row * block : (row + 1) * block, :] = left
     for step, piece in enumerate(pieces):
@@ -384,6 +391,7 @@
         [wide_panel],
         [pair, mask, gain, bias, w_proj],
         fetched=range(5),
+        columns={4: pl.ds(2 * hidden, 2 * hidden)},
         flops=2 * cells * channels * 2 * hidden,
         limit=64 * 1024 * 1024 - 640 * 1024,
     )
@@ -394,6 +402,7 @@
         [piece] * count,
         [pair, mask, gain, bias, w_proj, own_right],
         fetched=range(5),
+        columns={4: pl.ds(0, 2 * hidden)},
         unread=(5,),
         scratch=[left_panel],
         flops=2 * cells * channels * 2 * hidden,

time: 62.7 us -> 62.7 us (level)
  no operation moved by 1% of the time
where the time goes in v27:
time: 62.7 us; the launch traced here: 62.2 us
  starting transfers between devices  24.7 us (39%)
  blocking collectives  17.3 us (28%)
  Pallas kernels  9.55 us (15%)
  waiting for transfers between devices  8.69 us (14%)
  local copies, waits for them, and re-layouts  1.64 us (3%)
    all_to_all x2, blocking collectives, swap_half(): lax.all_to_all(values, 'row', split_axis=0, concat_axis=0, tiled=True, ax...  17.3 us
    all_to_all x2, starting transfers between devices, swap(): lax.all_to_all(values, 'row', split_axis=0, concat_axis=0, tiled=True, ax...  13.4 us
    ppermute x14, starting transfers between devices, swap_pieces(): lax.ppermute(pieces[step], 'row', [(d, d ^ distance(step, count)) for d i...  11.3 us
    pallas_call x12, Pallas kernels, call(): pl.pallas_call(body, name=name, out_shape=outs, in_specs=[pl.BlockSpec(me...  9.55 us
    ppermute x14, waiting for transfers between devices, swap_pieces(): lax.ppermute(pieces[step], 'row', [(d, d ^ distance(step, count)) for d i...  8.24 us
    unnamed x26, local copies, waits for them, and re-layouts  1.64 us
  transfers between devices with their start and end apart: 16, of which 10 were waited for; matrix products, arithmetic and copies ran while one was open for 0% of the time, Pallas kernels for 6%

profile of v27, /device:TPU:0, one launch (start us, length us, event | category | flops | bytes accessed | tf_op | source)
XLA Modules:
  0.0 62.2 jit_solution(4354021289316465768)
XLA Ops:
  0.0 2.3 %project_right.1.refs_5_ = bf16[16,128,128]{2,1,0:T(8,128)(2,1)} custom-call(bf16[8,128,128]{2,1,0:T(8,128)(2,1)} %refs_0_.7, s32[1,128]{1,0:T(1,128)} %bitcast.13, f32[1,128]{1,0:T(1,128)} %bitcast.5, f32[1,128]{1,0:T(1,128)} %bitcast.9, bf16[128,512]{1,0:T(8,128)(2,1)} %refs_4_.9), custom_call_target="tpu_custom_call" | custom-call | flops 67108864 | bytes 919040 | tf_op jit(solution)/shard_map/project_right/pallas_call | solution.py:72
  2.4 8.5 %all-to-all-start = ((bf16[16,128,128]{2,1,0:T(8,128)(2,1)}), bf16[16,128,128]{2,1,0:T(8,128)(2,1)S(1)}, u32[]{:S(2)}, u32[]{:S(2)}) async-start(bf16[16,128,128]{2,1,0:T(8,128)(2,1)} %project_right.1.refs_5_), calls=%async_computation | async-start | bytes 1048576 | tf_op jit(solution)/shard_map/all_to_all | solution.py:336
  12.5 1.4 %collective-permute-start.2 = (bf16[128,128]{1,0:T(8,128)(2,1)S(1)}, bf16[128,128]{1,0:T(8,128)(2,1)S(1)}, u32[]{:S(2)}, u32[]{:S(2)}) collective-permute-start(bf16[128,128]{1,0:T(8,128)(2,1)S(1)} %get-tuple-element.37), channel_id=1, source_target_pairs={{0,6},{1,7},{2,4},{3,5},{4,2},{5,3},{6,0},{7,1},{8,14},{9,15},{10,... | collective-permute-start | bytes 98312 | tf_op jit(solution)/shard_map/ppermute | solution.py:353
  13.8 0.9 %collective-permute-start.3 = (bf16[128,128]{1,0:T(8,128)(2,1)S(1)}, bf16[128,128]{1,0:T(8,128)(2,1)S(1)}, u32[]{:S(2)}, u32[]{:S(2)}) collective-permute-start(bf16[128,128]{1,0:T(8,128)(2,1)S(1)} %get-tuple-element.38), channel_id=1, source_target_pairs={{0,7},{1,6},{2,5},{3,4},{4,3},{5,2},{6,1},{7,0},{8,15},{9,14},{10,... | collective-permute-start | bytes 98312 | tf_op jit(solution)/shard_map/ppermute | solution.py:353
  15.4 1.5 %collective-permute-start.5 = (bf16[128,128]{1,0:T(8,128)(2,1)S(1)}, bf16[128,128]{1,0:T(8,128)(2,1)S(1)}, u32[]{:S(2)}, u32[]{:S(2)}) collective-permute-start(bf16[128,128]{1,0:T(8,128)(2,1)S(1)} %get-tuple-element.40), channel_id=1, source_target_pairs={{0,5},{1,4},{2,7},{3,6},{4,1},{5,0},{6,3},{7,2},{8,13},{9,12},{10,... | collective-permute-start | bytes 98312 | tf_op jit(solution)/shard_map/ppermute | solution.py:353
  16.9 1.5 %collective-permute-done.1.refs_2_ = bf16[128,128]{1,0:T(8,128)(2,1)S(1)} collective-permute-done((bf16[128,128]{1,0:T(8,128)(2,1)S(1)}, bf16[128,128]{1,0:T(8,128)(2,1)S(1)}, u32[]{:S(2)}, u32[]{:S(2)}) %collective-permute-start.1) | collective-permute-done | bytes 32800 | tf_op jit(solution)/shard_map/ppermute | solution.py:353
  18.4 0.6 %copy-done.11 = f32[128]{0:T(128)S(1)} copy-done((f32[128]{0:T(128)S(1)}, f32[128]{0:T(128)}, u32[]{:S(2)}) %copy-start.11) | copy-done | bytes 536
  19.0 0.8 %prepare.1 = (f32[8,128,128]{2,1,0:T(8,128)S(1)}, f32[8,128,128]{2,1,0:T(8,128)S(1)}) custom-call(bf16[8,128,128]{2,1,0:T(8,128)(2,1)S(1)} %copy-done.1, bf16[8,128,128]{2,1,0:T(8,128)(2,1)S(1)} %copy-done.3, f32[1,128]{1,0:T(1,128)S(1)} %bitcast.7, f32[1,128]{1,0:T(1,128)S(1)} %bitcast.11, bf16[128,128]{1,0:T(8,128)(2,1)S(1)} %copy-done.6, ...), custom_call_target="tpu_custom_call" | custom-call | flops 67108864 | bytes 1639936 | tf_op jit(solution)/shard_map/prepare/pallas_call | solution.py:72
  19.8 1.5 %collective-permute-done.2.refs_3_ = bf16[128,128]{1,0:T(8,128)(2,1)S(1)} collective-permute-done((bf16[128,128]{1,0:T(8,128)(2,1)S(1)}, bf16[128,128]{1,0:T(8,128)(2,1)S(1)}, u32[]{:S(2)}, u32[]{:S(2)}) %collective-permute-start.2) | collective-permute-done | bytes 32800 | tf_op jit(solution)/shard_map/ppermute | solution.py:353
  21.3 0.7 %collective-permute-done.3.refs_4_ = bf16[128,128]{1,0:T(8,128)(2,1)S(1)} collective-permute-done((bf16[128,128]{1,0:T(8,128)(2,1)S(1)}, bf16[128,128]{1,0:T(8,128)(2,1)S(1)}, u32[]{:S(2)}, u32[]{:S(2)}) %collective-permute-start.3) | collective-permute-done | bytes 32800 | tf_op jit(solution)/shard_map/ppermute | solution.py:353
  22.0 1.5 %collective-permute-done.4.refs_5_ = bf16[128,128]{1,0:T(8,128)(2,1)S(1)} collective-permute-done((bf16[128,128]{1,0:T(8,128)(2,1)S(1)}, bf16[128,128]{1,0:T(8,128)(2,1)S(1)}, u32[]{:S(2)}, u32[]{:S(2)}) %collective-permute-start.4) | collective-permute-done | bytes 32800 | tf_op jit(solution)/shard_map/ppermute | solution.py:353
  23.8 0.6 %tri.1 = (bf16[8,128,128]{2,1,0:T(8,128)(2,1)S(1)}, bf16[16,128,128]{2,1,0:T(8,128)(2,1)S(1)}) custom-call(bf16[16,128,128]{2,1,0:T(8,128)(2,1)S(1)} %all-to-all-done.refs_0_, bf16[16,64,128]{2,1,0:T(8,128)(2,1)S(1)} %get-tuple-element.42.refs_1_, f32[8,128,128]{2,1,0:T(8,128)S(1)} %get-tuple-element.43.refs_2_.refs_1_), custom_call_target="tpu_custom_call" | custom-call | flops 33554432 | bytes 2097152 | tf_op jit(solution)/shard_map/tri/pallas_call | solution.py:72
  24.4 8.7 %all_to_all.20.refs_0_ = bf16[8,128,128]{2,1,0:T(8,128)(2,1)S(1)} all-to-all(bf16[8,128,128]{2,1,0:T(8,128)(2,1)S(1)} %get-tuple-element.44), channel_id=1, replica_groups={{0,1,2,3,4,5,6,7},{8,9,10,11,12,13,14,15},{16,17,18,19,20,21,22,23},{24..., dimensions={0} | all-to-all | bytes 524288 | tf_op jit(solution)/shard_map/all_to_all | solution.py:344
  33.4 8.6 %all_to_all.21.refs_0_ = bf16[8,128,128]{2,1,0:T(8,128)(2,1)S(1)} all-to-all(bf16[8,128,128]{2,1,0:T(8,128)(2,1)S(1)} %middle.1), channel_id=1, replica_groups={{0,1,2,3,4,5,6,7},{8,9,10,11,12,13,14,15},{16,17,18,19,20,21,22,23},{24..., dimensions={0} | all-to-all | bytes 524288 | tf_op jit(solution)/shard_map/all_to_all | solution.py:344
  42.0 1.4 %d_right.1 = (bf16[16,128,128]{2,1,0:T(8,128)(2,1)}, bf16[16,64,128]{2,1,0:T(8,128)(2,1)S(1)}) custom-call(bf16[8,128,128]{2,1,0:T(8,128)(2,1)S(1)} %all_to_all.21.refs_0_, bf16[8,128,256]{2,1,0:T(8,128)(2,1)S(1)} %get-tuple-element.45.refs_1_), custom_call_target="tpu_custom_call" | custom-call | flops 33554432 | bytes 1572864 | tf_op jit(solution)/shard_map/d_right/pallas_call | solution.py:72
  43.5 4.9 %all-to-all-start.3 = ((bf16[16,128,128]{2,1,0:T(8,128)(2,1)}), bf16[16,128,128]{2,1,0:T(8,128)(2,1)S(1)}, u32[]{:S(2)}, u32[]{:S(2)}) async-start(bf16[16,128,128]{2,1,0:T(8,128)(2,1)} %get-tuple-element.46), calls=%async_computation.3 | async-start | bytes 1048576 | tf_op jit(solution)/shard_map/all_to_all | solution.py:336
  48.9 1.5 %collective-permute-start.8 = (bf16[128,128]{1,0:T(8,128)(2,1)S(1)}, bf16[128,128]{1,0:T(8,128)(2,1)S(1)}, u32[]{:S(2)}, u32[]{:S(2)}) collective-permute-start(bf16[128,128]{1,0:T(8,128)(2,1)S(1)} %get-tuple-element.51), channel_id=1, source_target_pairs={{0,2},{1,3},{2,0},{3,1},{4,6},{5,7},{6,4},{7,5},{8,10},{9,11},{10,... | collective-permute-start | bytes 98312 | tf_op jit(solution)/shard_map/ppermute | solution.py:353
  50.7 2.0 %collective-permute-start.10 = (bf16[128,128]{1,0:T(8,128)(2,1)S(1)}, bf16[128,128]{1,0:T(8,128)(2,1)S(1)}, u32[]{:S(2)}, u32[]{:S(2)}) collective-permute-start(bf16[128,128]{1,0:T(8,128)(2,1)S(1)} %get-tuple-element.53), channel_id=1, source_target_pairs={{0,7},{1,6},{2,5},{3,4},{4,3},{5,2},{6,1},{7,0},{8,15},{9,14},{10,... | collective-permute-start | bytes 98312 | tf_op jit(solution)/shard_map/ppermute | solution.py:353
  53.2 1.6 %collective-permute-start.12 = (bf16[128,128]{1,0:T(8,128)(2,1)S(1)}, bf16[128,128]{1,0:T(8,128)(2,1)S(1)}, u32[]{:S(2)}, u32[]{:S(2)}) collective-permute-start(bf16[128,128]{1,0:T(8,128)(2,1)S(1)} %get-tuple-element.55), channel_id=1, source_target_pairs={{0,5},{1,4},{2,7},{3,6},{4,1},{5,0},{6,3},{7,2},{8,13},{9,12},{10,... | collective-permute-start | bytes 98312 | tf_op jit(solution)/shard_map/ppermute | solution.py:353
  54.8 1.2 %collective-permute-done.8.refs_2_ = bf16[128,128]{1,0:T(8,128)(2,1)S(1)} collective-permute-done((bf16[128,128]{1,0:T(8,128)(2,1)S(1)}, bf16[128,128]{1,0:T(8,128)(2,1)S(1)}, u32[]{:S(2)}, u32[]{:S(2)}) %collective-permute-start.8) | collective-permute-done | bytes 32800 | tf_op jit(solution)/shard_map/ppermute | solution.py:353
  56.0 0.6 %copy-done.12 = f32[128]{0:T(128)S(1)} copy-done((f32[128]{0:T(128)S(1)}, f32[128]{0:T(128)}, u32[]{:S(2)}) %copy-start.12) | copy-done | bytes 536
  57.4 1.0 %slopes.1 = (bf16[8,512,128]{2,1,0:T(8,128)(2,1)S(1)}, bf16[8,128,128]{2,1,0:T(8,128)(2,1)S(1)}, f32[8,128]{1,0:T(8,128)S(1)}, f32[128,128]{1,0:T(8,128)S(1)}, bf16[128,640]{1,0:T(8,128)(2,1)S(1)}) custom-call(bf16[8,128,128]{2,1,0:T(8,128)(2,1)S(1)} %copy-done.1, s32[1,128]{1,0:T(1,128)S(1)} %bitcast.15, f32[1,128]{1,0:T(1,128)S(1)} %bitcast.8, ...), custom_call_target="tpu_custom_call" | custom-call | flops 134217728 | bytes 2233856 | tf_op jit(solution)/shard_map/slopes/pallas_call | solution.py:72
  58.7 0.7 %collective-permute-done.10.refs_4_ = bf16[128,128]{1,0:T(8,128)(2,1)S(1)} collective-permute-done((bf16[128,128]{1,0:T(8,128)(2,1)S(1)}, bf16[128,128]{1,0:T(8,128)(2,1)S(1)}, u32[]{:S(2)}, u32[]{:S(2)}) %collective-permute-start.10) | collective-permute-done | bytes 32800 | tf_op jit(solution)/shard_map/ppermute | solution.py:353
  60.8 1.4 %finish.1 = bf16[8,128,128]{2,1,0:T(8,128)(2,1)} custom-call(bf16[16,128,128]{2,1,0:T(8,128)(2,1)S(1)} %all-to-all-done.3.refs_0_, bf16[8,128,128]{2,1,0:T(8,128)(2,1)S(1)} %sort_d_left.1.refs_1_, bf16[8,512,128]{2,1,0:T(8,128)(2,1)S(1)} %get-tuple-element.58.refs_2_, bf16[8,128,128]{2,1,0:T(8,128)(2,1)S(1)} %gate_back.1.refs_6_.refs_3_, ...), custom_call_target="tpu_custom_call" | custom-call | flops 134217728 | bytes 2854912 | tf_op jit(solution)/shard_map/finish/pallas_call | solution.py:72
  (48 shorter events, 6.4 us)
Async XLA Ops:
  2.3 8.6 %copy-start = (bf16[16,128,128]{2,1,0:T(8,128)(2,1)S(1)}, bf16[16,128,128]{2,1,0:T(8,128)(2,1)}, u32[]{:S(2)}) copy-start(bf16[16,128,128]{2,1,0:T(8,128)(2,1)} %project_right.1.refs_5_) | copy-start | bytes 1572868
  2.3 8.6 %copy-start.1 = (bf16[8,128,128]{2,1,0:T(8,128)(2,1)S(1)}, bf16[8,128,128]{2,1,0:T(8,128)(2,1)}, u32[]{:S(2)}) copy-start(bf16[8,128,128]{2,1,0:T(8,128)(2,1)} %refs_0_.7) | copy-start | bytes 786436
  2.3 8.6 %copy-start.2 = (bf16[128,512]{1,0:T(8,128)(2,1)S(1)}, bf16[128,512]{1,0:T(8,128)(2,1)}, u32[]{:S(2)}) copy-start(bf16[128,512]{1,0:T(8,128)(2,1)} %refs_4_.9) | copy-start | bytes 393220
  2.4 8.6 %copy-start.8 = (f32[128]{0:T(128)S(1)}, f32[128]{0:T(128)}, u32[]{:S(2)}) copy-start(f32[128]{0:T(128)} %param.13) | copy-start | bytes 1540
  2.4 8.6 %copy-start.9 = (f32[128]{0:T(128)S(1)}, f32[128]{0:T(128)}, u32[]{:S(2)}) copy-start(f32[128]{0:T(128)} %param.14) | copy-start | bytes 1540
  2.4 8.6 %copy-start.10 = (s32[128]{0:T(128)S(1)}, s32[128]{0:T(128)}, u32[]{:S(2)}) copy-start(s32[128]{0:T(128)} %param.12) | copy-start | bytes 1540
  2.4 21.4 %all-to-all-start = ((bf16[16,128,128]{2,1,0:T(8,128)(2,1)}), bf16[16,128,128]{2,1,0:T(8,128)(2,1)S(1)}, u32[]{:S(2)}, u32[]{:S(2)}) async-start(bf16[16,128,128]{2,1,0:T(8,128)(2,1)} %project_right.1.refs_5_), calls=%async_computation | async-start | bytes 1048576 | tf_op jit(solution)/shard_map/all_to_all | solution.py:336
  11.0 7.4 %copy-start.3 = (bf16[8,128,128]{2,1,0:T(8,128)(2,1)S(1)}, bf16[8,128,128]{2,1,0:T(8,128)(2,1)}, u32[]{:S(2)}) copy-start(bf16[8,128,128]{2,1,0:T(8,128)(2,1)} %refs_1_.1) | copy-start | bytes 786436
  11.6 3.7 %collective-permute-start = (bf16[128,128]{1,0:T(8,128)(2,1)S(1)}, bf16[128,128]{1,0:T(8,128)(2,1)S(1)}, u32[]{:S(2)}, u32[]{:S(2)}) collective-permute-start(bf16[128,128]{1,0:T(8,128)(2,1)S(1)} %get-tuple-element.35), channel_id=1, source_target_pairs={{0,1},{1,0},{2,3},{3,2},{4,5},{5,4},{6,7},{7,6},{8,9},{9,8},{10,11... | collective-permute-start | bytes 98312 | tf_op jit(solution)/shard_map/ppermute | solution.py:353
  11.9 6.5 %collective-permute-start.1 = (bf16[128,128]{1,0:T(8,128)(2,1)S(1)}, bf16[128,128]{1,0:T(8,128)(2,1)S(1)}, u32[]{:S(2)}, u32[]{:S(2)}) collective-permute-start(bf16[128,128]{1,0:T(8,128)(2,1)S(1)} %get-tuple-element.36), channel_id=1, source_target_pairs={{0,2},{1,3},{2,0},{3,1},{4,6},{5,7},{6,4},{7,5},{8,10},{9,11},{10,... | collective-permute-start | bytes 98312 | tf_op jit(solution)/shard_map/ppermute | solution.py:353
  12.5 8.8 %collective-permute-start.2 = (bf16[128,128]{1,0:T(8,128)(2,1)S(1)}, bf16[128,128]{1,0:T(8,128)(2,1)S(1)}, u32[]{:S(2)}, u32[]{:S(2)}) collective-permute-start(bf16[128,128]{1,0:T(8,128)(2,1)S(1)} %get-tuple-element.37), channel_id=1, source_target_pairs={{0,6},{1,7},{2,4},{3,5},{4,2},{5,3},{6,0},{7,1},{8,14},{9,15},{10,... | collective-permute-start | bytes 98312 | tf_op jit(solution)/shard_map/ppermute | solution.py:353
  13.8 8.1 %collective-permute-start.3 = (bf16[128,128]{1,0:T(8,128)(2,1)S(1)}, bf16[128,128]{1,0:T(8,128)(2,1)S(1)}, u32[]{:S(2)}, u32[]{:S(2)}) collective-permute-start(bf16[128,128]{1,0:T(8,128)(2,1)S(1)} %get-tuple-element.38), channel_id=1, source_target_pairs={{0,7},{1,6},{2,5},{3,4},{4,3},{5,2},{6,1},{7,0},{8,15},{9,14},{10,... | collective-permute-start | bytes 98312 | tf_op jit(solution)/shard_map/ppermute | solution.py:353
  14.8 8.7 %collective-permute-start.4 = (bf16[128,128]{1,0:T(8,128)(2,1)S(1)}, bf16[128,128]{1,0:T(8,128)(2,1)S(1)}, u32[]{:S(2)}, u32[]{:S(2)}) collective-permute-start(bf16[128,128]{1,0:T(8,128)(2,1)S(1)} %get-tuple-element.39), channel_id=1, source_target_pairs={{0,4},{1,5},{2,6},{3,7},{4,0},{5,1},{6,2},{7,3},{8,12},{9,13},{10,... | collective-permute-start | bytes 98312 | tf_op jit(solution)/shard_map/ppermute | solution.py:353
  15.4 8.1 %collective-permute-start.5 = (bf16[128,128]{1,0:T(8,128)(2,1)S(1)}, bf16[128,128]{1,0:T(8,128)(2,1)S(1)}, u32[]{:S(2)}, u32[]{:S(2)}) collective-permute-start(bf16[128,128]{1,0:T(8,128)(2,1)S(1)} %get-tuple-element.40), channel_id=1, source_target_pairs={{0,5},{1,4},{2,7},{3,6},{4,1},{5,0},{6,3},{7,2},{8,13},{9,12},{10,... | collective-permute-start | bytes 98312 | tf_op jit(solution)/shard_map/ppermute | solution.py:353
  18.3 5.2 %collective-permute-start.6 = (bf16[128,128]{1,0:T(8,128)(2,1)S(1)}, bf16[128,128]{1,0:T(8,128)(2,1)S(1)}, u32[]{:S(2)}, u32[]{:S(2)}) collective-permute-start(bf16[128,128]{1,0:T(8,128)(2,1)S(1)} %get-tuple-element.41), channel_id=1, source_target_pairs={{0,3},{1,2},{2,1},{3,0},{4,7},{5,6},{6,5},{7,4},{8,11},{9,10},{10,... | collective-permute-start | bytes 98312 | tf_op jit(solution)/shard_map/ppermute | solution.py:353
  43.5 17.3 %all-to-all-start.3 = ((bf16[16,128,128]{2,1,0:T(8,128)(2,1)}), bf16[16,128,128]{2,1,0:T(8,128)(2,1)S(1)}, u32[]{:S(2)}, u32[]{:S(2)}) async-start(bf16[16,128,128]{2,1,0:T(8,128)(2,1)} %get-tuple-element.46), calls=%async_computation.3 | async-start | bytes 1048576 | tf_op jit(solution)/shard_map/all_to_all | solution.py:336
  48.3 7.7 %copy-start.5 = (bf16[128,128]{1,0:T(8,128)(2,1)S(1)}, bf16[128,128]{1,0:T(8,128)(2,1)}, u32[]{:S(2)}) copy-start(bf16[128,128]{1,0:T(8,128)(2,1)} %refs_4_.8) | copy-start | bytes 98308
  48.7 4.5 %collective-permute-start.7 = (bf16[128,128]{1,0:T(8,128)(2,1)S(1)}, bf16[128,128]{1,0:T(8,128)(2,1)S(1)}, u32[]{:S(2)}, u32[]{:S(2)}) collective-permute-start(bf16[128,128]{1,0:T(8,128)(2,1)S(1)} %get-tuple-element.50), channel_id=1, source_target_pairs={{0,1},{1,0},{2,3},{3,2},{4,5},{5,4},{6,7},{7,6},{8,9},{9,8},{10,11... | collective-permute-start | bytes 98312 | tf_op jit(solution)/shard_map/ppermute | solution.py:353
  48.9 7.1 %collective-permute-start.8 = (bf16[128,128]{1,0:T(8,128)(2,1)S(1)}, bf16[128,128]{1,0:T(8,128)(2,1)S(1)}, u32[]{:S(2)}, u32[]{:S(2)}) collective-permute-start(bf16[128,128]{1,0:T(8,128)(2,1)S(1)} %get-tuple-element.51), channel_id=1, source_target_pairs={{0,2},{1,3},{2,0},{3,1},{4,6},{5,7},{6,4},{7,5},{8,10},{9,11},{10,... | collective-permute-start | bytes 98312 | tf_op jit(solution)/shard_map/ppermute | solution.py:353
  50.4 8.3 %collective-permute-start.9 = (bf16[128,128]{1,0:T(8,128)(2,1)S(1)}, bf16[128,128]{1,0:T(8,128)(2,1)S(1)}, u32[]{:S(2)}, u32[]{:S(2)}) collective-permute-start(bf16[128,128]{1,0:T(8,128)(2,1)S(1)} %get-tuple-element.52), channel_id=1, source_target_pairs={{0,6},{1,7},{2,4},{3,5},{4,2},{5,3},{6,0},{7,1},{8,14},{9,15},{10,... | collective-permute-start | bytes 98312 | tf_op jit(solution)/shard_map/ppermute | solution.py:353
  50.7 8.7 %collective-permute-start.10 = (bf16[128,128]{1,0:T(8,128)(2,1)S(1)}, bf16[128,128]{1,0:T(8,128)(2,1)S(1)}, u32[]{:S(2)}, u32[]{:S(2)}) collective-permute-start(bf16[128,128]{1,0:T(8,128)(2,1)S(1)} %get-tuple-element.53), channel_id=1, source_target_pairs={{0,7},{1,6},{2,5},{3,4},{4,3},{5,2},{6,1},{7,0},{8,15},{9,14},{10,... | collective-permute-start | bytes 98312 | tf_op jit(solution)/shard_map/ppermute | solution.py:353
  52.7 7.2 %collective-permute-start.11 = (bf16[128,128]{1,0:T(8,128)(2,1)S(1)}, bf16[128,128]{1,0:T(8,128)(2,1)S(1)}, u32[]{:S(2)}, u32[]{:S(2)}) collective-permute-start(bf16[128,128]{1,0:T(8,128)(2,1)S(1)} %get-tuple-element.54), channel_id=1, source_target_pairs={{0,4},{1,5},{2,6},{3,7},{4,0},{5,1},{6,2},{7,3},{8,12},{9,13},{10,... | collective-permute-start | bytes 98312 | tf_op jit(solution)/shard_map/ppermute | solution.py:353
  53.2 7.1 %collective-permute-start.12 = (bf16[128,128]{1,0:T(8,128)(2,1)S(1)}, bf16[128,128]{1,0:T(8,128)(2,1)S(1)}, u32[]{:S(2)}, u32[]{:S(2)}) collective-permute-start(bf16[128,128]{1,0:T(8,128)(2,1)S(1)} %get-tuple-element.55), channel_id=1, source_target_pairs={{0,5},{1,4},{2,7},{3,6},{4,1},{5,0},{6,3},{7,2},{8,13},{9,12},{10,... | collective-permute-start | bytes 98312 | tf_op jit(solution)/shard_map/ppermute | solution.py:353
  56.0 4.3 %collective-permute-start.13 = (bf16[128,128]{1,0:T(8,128)(2,1)S(1)}, bf16[128,128]{1,0:T(8,128)(2,1)S(1)}, u32[]{:S(2)}, u32[]{:S(2)}) collective-permute-start(bf16[128,128]{1,0:T(8,128)(2,1)S(1)} %get-tuple-element.56), channel_id=1, source_target_pairs={{0,3},{1,2},{2,1},{3,0},{4,7},{5,6},{6,5},{7,4},{8,11},{9,10},{10,... | collective-permute-start | bytes 98312 | tf_op jit(solution)/shard_map/ppermute | solution.py:353
  (5 other events, 16.8 us)

commit v28 on v27

--- a/solution.py
+++ b/solution.py
@@ -101,10 +101,10 @@
 def wide_order(devices, count, back):
     order = []
     for place in range(count):
-        if back:
-            order += [place ^ (count // 2), count + place]
-        else:
+        if not back:
             order += [count + (place ^ 2), place ^ (count // 2)]
+        elif place < count // 2:
+            order += [place + count // 2, place + count, place, place + count + count // 2]
     return order
 
 

time: 62.7 us -> 64 us (1.021)
  waiting for transfers between devices: 8.69 us -> 9.44 us
    all_to_all x2, waiting for transfers between devices: 0.45 us -> 1.17 us  [swap(): lax.all_to_all(values, 'row', split_axis=0, concat_axis=0, tiled=True, ax...]
where the time goes in v28:
time: 64 us; the launch traced here: 62.9 us
  starting transfers between devices  24.7 us (39%)
  blocking collectives  17.3 us (27%)
  Pallas kernels  9.56 us (15%)
  waiting for transfers between devices  9.44 us (15%)
  local copies, waits for them, and re-layouts  1.64 us (3%)
    all_to_all x2, blocking collectives, swap_half(): lax.all_to_all(values, 'row', split_axis=0, concat_axis=0, tiled=True, ax...  17.3 us
    all_to_all x2, starting transfers between devices, swap(): lax.all_to_all(values, 'row', split_axis=0, concat_axis=0, tiled=True, ax...  13.3 us
    ppermute x14, starting transfers between devices, swap_pieces(): lax.ppermute(pieces[step], 'row', [(d, d ^ distance(step, count)) for d i...  11.3 us
    pallas_call x12, Pallas kernels, call(): pl.pallas_call(body, name=name, out_shape=outs, in_specs=[pl.BlockSpec(me...  9.56 us
    ppermute x14, waiting for transfers between devices, swap_pieces(): lax.ppermute(pieces[step], 'row', [(d, d ^ distance(step, count)) for d i...  8.28 us
    unnamed x26, local copies, waits for them, and re-layouts  1.64 us
  transfers between devices with their start and end apart: 16, of which 10 were waited for; matrix products, arithmetic and copies ran while one was open for 0% of the time, Pallas kernels for 6%

profile of v28, /device:TPU:0, one launch (start us, length us, event | category | flops | bytes accessed | tf_op | source)
XLA Modules:
  0.0 62.9 jit_solution(14610974802848385637)
XLA Ops:
  0.0 2.3 %project_right.1.refs_5_ = bf16[16,128,128]{2,1,0:T(8,128)(2,1)} custom-call(bf16[8,128,128]{2,1,0:T(8,128)(2,1)} %refs_0_.7, s32[1,128]{1,0:T(1,128)} %bitcast.13, f32[1,128]{1,0:T(1,128)} %bitcast.5, f32[1,128]{1,0:T(1,128)} %bitcast.9, bf16[128,512]{1,0:T(8,128)(2,1)} %refs_4_.9), custom_call_target="tpu_custom_call" | custom-call | flops 67108864 | bytes 919040 | tf_op jit(solution)/shard_map/project_right/pallas_call | solution.py:72
  2.4 8.5 %all-to-all-start = ((bf16[16,128,128]{2,1,0:T(8,128)(2,1)}), bf16[16,128,128]{2,1,0:T(8,128)(2,1)S(1)}, u32[]{:S(2)}, u32[]{:S(2)}) async-start(bf16[16,128,128]{2,1,0:T(8,128)(2,1)} %project_right.1.refs_5_), calls=%async_computation | async-start | bytes 1048576 | tf_op jit(solution)/shard_map/all_to_all | solution.py:336
  12.5 1.4 %collective-permute-start.2 = (bf16[128,128]{1,0:T(8,128)(2,1)S(1)}, bf16[128,128]{1,0:T(8,128)(2,1)S(1)}, u32[]{:S(2)}, u32[]{:S(2)}) collective-permute-start(bf16[128,128]{1,0:T(8,128)(2,1)S(1)} %get-tuple-element.37), channel_id=1, source_target_pairs={{0,6},{1,7},{2,4},{3,5},{4,2},{5,3},{6,0},{7,1},{8,14},{9,15},{10,... | collective-permute-start | bytes 98312 | tf_op jit(solution)/shard_map/ppermute | solution.py:353
  13.8 0.9 %collective-permute-start.3 = (bf16[128,128]{1,0:T(8,128)(2,1)S(1)}, bf16[128,128]{1,0:T(8,128)(2,1)S(1)}, u32[]{:S(2)}, u32[]{:S(2)}) collective-permute-start(bf16[128,128]{1,0:T(8,128)(2,1)S(1)} %get-tuple-element.38), channel_id=1, source_target_pairs={{0,7},{1,6},{2,5},{3,4},{4,3},{5,2},{6,1},{7,0},{8,15},{9,14},{10,... | collective-permute-start | bytes 98312 | tf_op jit(solution)/shard_map/ppermute | solution.py:353
  15.4 1.5 %collective-permute-start.5 = (bf16[128,128]{1,0:T(8,128)(2,1)S(1)}, bf16[128,128]{1,0:T(8,128)(2,1)S(1)}, u32[]{:S(2)}, u32[]{:S(2)}) collective-permute-start(bf16[128,128]{1,0:T(8,128)(2,1)S(1)} %get-tuple-element.40), channel_id=1, source_target_pairs={{0,5},{1,4},{2,7},{3,6},{4,1},{5,0},{6,3},{7,2},{8,13},{9,12},{10,... | collective-permute-start | bytes 98312 | tf_op jit(solution)/shard_map/ppermute | solution.py:353
  16.9 1.5 %collective-permute-done.1.refs_2_ = bf16[128,128]{1,0:T(8,128)(2,1)S(1)} collective-permute-done((bf16[128,128]{1,0:T(8,128)(2,1)S(1)}, bf16[128,128]{1,0:T(8,128)(2,1)S(1)}, u32[]{:S(2)}, u32[]{:S(2)}) %collective-permute-start.1) | collective-permute-done | bytes 32800 | tf_op jit(solution)/shard_map/ppermute | solution.py:353
  19.0 0.8 %prepare.1 = (f32[8,128,128]{2,1,0:T(8,128)S(1)}, f32[8,128,128]{2,1,0:T(8,128)S(1)}) custom-call(bf16[8,128,128]{2,1,0:T(8,128)(2,1)S(1)} %copy-done.1, bf16[8,128,128]{2,1,0:T(8,128)(2,1)S(1)} %copy-done.3, f32[1,128]{1,0:T(1,128)S(1)} %bitcast.7, f32[1,128]{1,0:T(1,128)S(1)} %bitcast.11, bf16[128,128]{1,0:T(8,128)(2,1)S(1)} %copy-done.6, ...), custom_call_target="tpu_custom_call" | custom-call | flops 67108864 | bytes 1639936 | tf_op jit(solution)/shard_map/prepare/pallas_call | solution.py:72
  19.8 1.5 %collective-permute-done.2.refs_3_ = bf16[128,128]{1,0:T(8,128)(2,1)S(1)} collective-permute-done((bf16[128,128]{1,0:T(8,128)(2,1)S(1)}, bf16[128,128]{1,0:T(8,128)(2,1)S(1)}, u32[]{:S(2)}, u32[]{:S(2)}) %collective-permute-start.2) | collective-permute-done | bytes 32800 | tf_op jit(solution)/shard_map/ppermute | solution.py:353
  21.3 0.7 %collective-permute-done.3.refs_4_ = bf16[128,128]{1,0:T(8,128)(2,1)S(1)} collective-permute-done((bf16[128,128]{1,0:T(8,128)(2,1)S(1)}, bf16[128,128]{1,0:T(8,128)(2,1)S(1)}, u32[]{:S(2)}, u32[]{:S(2)}) %collective-permute-start.3) | collective-permute-done | bytes 32800 | tf_op jit(solution)/shard_map/ppermute | solution.py:353
  22.0 1.5 %collective-permute-done.4.refs_5_ = bf16[128,128]{1,0:T(8,128)(2,1)S(1)} collective-permute-done((bf16[128,128]{1,0:T(8,128)(2,1)S(1)}, bf16[128,128]{1,0:T(8,128)(2,1)S(1)}, u32[]{:S(2)}, u32[]{:S(2)}) %collective-permute-start.4) | collective-permute-done | bytes 32800 | tf_op jit(solution)/shard_map/ppermute | solution.py:353
  23.8 0.6 %tri.1 = (bf16[8,128,128]{2,1,0:T(8,128)(2,1)S(1)}, bf16[16,128,128]{2,1,0:T(8,128)(2,1)S(1)}) custom-call(bf16[16,128,128]{2,1,0:T(8,128)(2,1)S(1)} %all-to-all-done.refs_0_, bf16[16,64,128]{2,1,0:T(8,128)(2,1)S(1)} %get-tuple-element.42.refs_1_, f32[8,128,128]{2,1,0:T(8,128)S(1)} %get-tuple-element.43.refs_2_.refs_1_), custom_call_target="tpu_custom_call" | custom-call | flops 33554432 | bytes 2097152 | tf_op jit(solution)/shard_map/tri/pallas_call | solution.py:72
  24.4 8.7 %all_to_all.20.refs_0_ = bf16[8,128,128]{2,1,0:T(8,128)(2,1)S(1)} all-to-all(bf16[8,128,128]{2,1,0:T(8,128)(2,1)S(1)} %get-tuple-element.44), channel_id=1, replica_groups={{0,1,2,3,4,5,6,7},{8,9,10,11,12,13,14,15},{16,17,18,19,20,21,22,23},{24..., dimensions={0} | all-to-all | bytes 524288 | tf_op jit(solution)/shard_map/all_to_all | solution.py:344
  33.4 8.6 %all_to_all.21.refs_0_ = bf16[8,128,128]{2,1,0:T(8,128)(2,1)S(1)} all-to-all(bf16[8,128,128]{2,1,0:T(8,128)(2,1)S(1)} %middle.1), channel_id=1, replica_groups={{0,1,2,3,4,5,6,7},{8,9,10,11,12,13,14,15},{16,17,18,19,20,21,22,23},{24..., dimensions={0} | all-to-all | bytes 524288 | tf_op jit(solution)/shard_map/all_to_all | solution.py:344
  42.0 1.4 %d_right.1 = (bf16[16,128,128]{2,1,0:T(8,128)(2,1)}, bf16[16,64,128]{2,1,0:T(8,128)(2,1)S(1)}) custom-call(bf16[8,128,128]{2,1,0:T(8,128)(2,1)S(1)} %all_to_all.21.refs_0_, bf16[8,128,256]{2,1,0:T(8,128)(2,1)S(1)} %get-tuple-element.45.refs_1_), custom_call_target="tpu_custom_call" | custom-call | flops 33554432 | bytes 1572864 | tf_op jit(solution)/shard_map/d_right/pallas_call | solution.py:72
  43.5 4.8 %all-to-all-start.3 = ((bf16[16,128,128]{2,1,0:T(8,128)(2,1)}), bf16[16,128,128]{2,1,0:T(8,128)(2,1)S(1)}, u32[]{:S(2)}, u32[]{:S(2)}) async-start(bf16[16,128,128]{2,1,0:T(8,128)(2,1)} %get-tuple-element.46), calls=%async_computation.3 | async-start | bytes 1048576 | tf_op jit(solution)/shard_map/all_to_all | solution.py:336
  48.8 1.5 %collective-permute-start.8 = (bf16[128,128]{1,0:T(8,128)(2,1)S(1)}, bf16[128,128]{1,0:T(8,128)(2,1)S(1)}, u32[]{:S(2)}, u32[]{:S(2)}) collective-permute-start(bf16[128,128]{1,0:T(8,128)(2,1)S(1)} %get-tuple-element.51), channel_id=1, source_target_pairs={{0,2},{1,3},{2,0},{3,1},{4,6},{5,7},{6,4},{7,5},{8,10},{9,11},{10,... | collective-permute-start | bytes 98312 | tf_op jit(solution)/shard_map/ppermute | solution.py:353
  50.7 2.0 %collective-permute-start.10 = (bf16[128,128]{1,0:T(8,128)(2,1)S(1)}, bf16[128,128]{1,0:T(8,128)(2,1)S(1)}, u32[]{:S(2)}, u32[]{:S(2)}) collective-permute-start(bf16[128,128]{1,0:T(8,128)(2,1)S(1)} %get-tuple-element.53), channel_id=1, source_target_pairs={{0,7},{1,6},{2,5},{3,4},{4,3},{5,2},{6,1},{7,0},{8,15},{9,14},{10,... | collective-permute-start | bytes 98312 | tf_op jit(solution)/shard_map/ppermute | solution.py:353
  53.2 1.5 %collective-permute-start.12 = (bf16[128,128]{1,0:T(8,128)(2,1)S(1)}, bf16[128,128]{1,0:T(8,128)(2,1)S(1)}, u32[]{:S(2)}, u32[]{:S(2)}) collective-permute-start(bf16[128,128]{1,0:T(8,128)(2,1)S(1)} %get-tuple-element.55), channel_id=1, source_target_pairs={{0,5},{1,4},{2,7},{3,6},{4,1},{5,0},{6,3},{7,2},{8,13},{9,12},{10,... | collective-permute-start | bytes 98312 | tf_op jit(solution)/shard_map/ppermute | solution.py:353
  55.0 0.6 %copy-done.12 = f32[128]{0:T(128)S(1)} copy-done((f32[128]{0:T(128)S(1)}, f32[128]{0:T(128)}, u32[]{:S(2)}) %copy-start.12) | copy-done | bytes 536
  56.4 1.0 %slopes.1 = (bf16[8,512,128]{2,1,0:T(8,128)(2,1)S(1)}, bf16[8,128,128]{2,1,0:T(8,128)(2,1)S(1)}, f32[8,128]{1,0:T(8,128)S(1)}, f32[128,128]{1,0:T(8,128)S(1)}, bf16[128,640]{1,0:T(8,128)(2,1)S(1)}) custom-call(bf16[8,128,128]{2,1,0:T(8,128)(2,1)S(1)} %copy-done.1, s32[1,128]{1,0:T(1,128)S(1)} %bitcast.15, f32[1,128]{1,0:T(1,128)S(1)} %bitcast.8, ...), custom_call_target="tpu_custom_call" | custom-call | flops 134217728 | bytes 2233856 | tf_op jit(solution)/shard_map/slopes/pallas_call | solution.py:72
  57.4 1.3 %collective-permute-done.9.refs_3_ = bf16[128,128]{1,0:T(8,128)(2,1)S(1)} collective-permute-done((bf16[128,128]{1,0:T(8,128)(2,1)S(1)}, bf16[128,128]{1,0:T(8,128)(2,1)S(1)}, u32[]{:S(2)}, u32[]{:S(2)}) %collective-permute-start.9) | collective-permute-done | bytes 32800 | tf_op jit(solution)/shard_map/ppermute | solution.py:353
  58.7 0.7 %collective-permute-done.10.refs_4_ = bf16[128,128]{1,0:T(8,128)(2,1)S(1)} collective-permute-done((bf16[128,128]{1,0:T(8,128)(2,1)S(1)}, bf16[128,128]{1,0:T(8,128)(2,1)S(1)}, u32[]{:S(2)}, u32[]{:S(2)}) %collective-permute-start.10) | collective-permute-done | bytes 32800 | tf_op jit(solution)/shard_map/ppermute | solution.py:353
  60.3 1.2 %all-to-all-done.3.refs_0_ = bf16[16,128,128]{2,1,0:T(8,128)(2,1)S(1)} async-done(((bf16[16,128,128]{2,1,0:T(8,128)(2,1)}), bf16[16,128,128]{2,1,0:T(8,128)(2,1)S(1)}, u32[]{:S(2)}, u32[]{:S(2)}) %all-to-all-start.3) | async-done | bytes 524320 | tf_op jit(solution)/shard_map/all_to_all | solution.py:336
  61.5 1.4 %finish.1 = bf16[8,128,128]{2,1,0:T(8,128)(2,1)} custom-call(bf16[16,128,128]{2,1,0:T(8,128)(2,1)S(1)} %all-to-all-done.3.refs_0_, bf16[8,128,128]{2,1,0:T(8,128)(2,1)S(1)} %sort_d_left.1.refs_1_, bf16[8,512,128]{2,1,0:T(8,128)(2,1)S(1)} %get-tuple-element.58.refs_2_, bf16[8,128,128]{2,1,0:T(8,128)(2,1)S(1)} %gate_back.1.refs_6_.refs_3_, ...), custom_call_target="tpu_custom_call" | custom-call | flops 134217728 | bytes 2854912 | tf_op jit(solution)/shard_map/finish/pallas_call | solution.py:72
  (48 shorter events, 6.6 us)
Async XLA Ops:
  2.3 8.6 %copy-start = (bf16[16,128,128]{2,1,0:T(8,128)(2,1)S(1)}, bf16[16,128,128]{2,1,0:T(8,128)(2,1)}, u32[]{:S(2)}) copy-start(bf16[16,128,128]{2,1,0:T(8,128)(2,1)} %project_right.1.refs_5_) | copy-start | bytes 1572868
  2.3 8.6 %copy-start.1 = (bf16[8,128,128]{2,1,0:T(8,128)(2,1)S(1)}, bf16[8,128,128]{2,1,0:T(8,128)(2,1)}, u32[]{:S(2)}) copy-start(bf16[8,128,128]{2,1,0:T(8,128)(2,1)} %refs_0_.7) | copy-start | bytes 786436
  2.3 8.6 %copy-start.2 = (bf16[128,512]{1,0:T(8,128)(2,1)S(1)}, bf16[128,512]{1,0:T(8,128)(2,1)}, u32[]{:S(2)}) copy-start(bf16[128,512]{1,0:T(8,128)(2,1)} %refs_4_.9) | copy-start | bytes 393220
  2.4 8.6 %copy-start.8 = (f32[128]{0:T(128)S(1)}, f32[128]{0:T(128)}, u32[]{:S(2)}) copy-start(f32[128]{0:T(128)} %param.13) | copy-start | bytes 1540
  2.4 8.6 %copy-start.9 = (f32[128]{0:T(128)S(1)}, f32[128]{0:T(128)}, u32[]{:S(2)}) copy-start(f32[128]{0:T(128)} %param.14) | copy-start | bytes 1540
  2.4 8.6 %copy-start.10 = (s32[128]{0:T(128)S(1)}, s32[128]{0:T(128)}, u32[]{:S(2)}) copy-start(s32[128]{0:T(128)} %param.12) | copy-start | bytes 1540
  2.4 21.4 %all-to-all-start = ((bf16[16,128,128]{2,1,0:T(8,128)(2,1)}), bf16[16,128,128]{2,1,0:T(8,128)(2,1)S(1)}, u32[]{:S(2)}, u32[]{:S(2)}) async-start(bf16[16,128,128]{2,1,0:T(8,128)(2,1)} %project_right.1.refs_5_), calls=%async_computation | async-start | bytes 1048576 | tf_op jit(solution)/shard_map/all_to_all | solution.py:336
  11.0 7.4 %copy-start.3 = (bf16[8,128,128]{2,1,0:T(8,128)(2,1)S(1)}, bf16[8,128,128]{2,1,0:T(8,128)(2,1)}, u32[]{:S(2)}) copy-start(bf16[8,128,128]{2,1,0:T(8,128)(2,1)} %refs_1_.1) | copy-start | bytes 786436
  11.0 7.3 %copy-start.4 = (bf16[128,128]{1,0:T(8,128)(2,1)S(1)}, bf16[128,128]{1,0:T(8,128)(2,1)}, u32[]{:S(2)}) copy-start(bf16[128,128]{1,0:T(8,128)(2,1)} %refs_4_.8) | copy-start | bytes 98308
  11.6 3.7 %collective-permute-start = (bf16[128,128]{1,0:T(8,128)(2,1)S(1)}, bf16[128,128]{1,0:T(8,128)(2,1)S(1)}, u32[]{:S(2)}, u32[]{:S(2)}) collective-permute-start(bf16[128,128]{1,0:T(8,128)(2,1)S(1)} %get-tuple-element.35), channel_id=1, source_target_pairs={{0,1},{1,0},{2,3},{3,2},{4,5},{5,4},{6,7},{7,6},{8,9},{9,8},{10,11... | collective-permute-start | bytes 98312 | tf_op jit(solution)/shard_map/ppermute | solution.py:353
  11.9 6.5 %collective-permute-start.1 = (bf16[128,128]{1,0:T(8,128)(2,1)S(1)}, bf16[128,128]{1,0:T(8,128)(2,1)S(1)}, u32[]{:S(2)}, u32[]{:S(2)}) collective-permute-start(bf16[128,128]{1,0:T(8,128)(2,1)S(1)} %get-tuple-element.36), channel_id=1, source_target_pairs={{0,2},{1,3},{2,0},{3,1},{4,6},{5,7},{6,4},{7,5},{8,10},{9,11},{10,... | collective-permute-start | bytes 98312 | tf_op jit(solution)/shard_map/ppermute | solution.py:353
  12.5 8.8 %collective-permute-start.2 = (bf16[128,128]{1,0:T(8,128)(2,1)S(1)}, bf16[128,128]{1,0:T(8,128)(2,1)S(1)}, u32[]{:S(2)}, u32[]{:S(2)}) collective-permute-start(bf16[128,128]{1,0:T(8,128)(2,1)S(1)} %get-tuple-element.37), channel_id=1, source_target_pairs={{0,6},{1,7},{2,4},{3,5},{4,2},{5,3},{6,0},{7,1},{8,14},{9,15},{10,... | collective-permute-start | bytes 98312 | tf_op jit(solution)/shard_map/ppermute | solution.py:353
  13.8 8.1 %collective-permute-start.3 = (bf16[128,128]{1,0:T(8,128)(2,1)S(1)}, bf16[128,128]{1,0:T(8,128)(2,1)S(1)}, u32[]{:S(2)}, u32[]{:S(2)}) collective-permute-start(bf16[128,128]{1,0:T(8,128)(2,1)S(1)} %get-tuple-element.38), channel_id=1, source_target_pairs={{0,7},{1,6},{2,5},{3,4},{4,3},{5,2},{6,1},{7,0},{8,15},{9,14},{10,... | collective-permute-start | bytes 98312 | tf_op jit(solution)/shard_map/ppermute | solution.py:353
  14.8 8.7 %collective-permute-start.4 = (bf16[128,128]{1,0:T(8,128)(2,1)S(1)}, bf16[128,128]{1,0:T(8,128)(2,1)S(1)}, u32[]{:S(2)}, u32[]{:S(2)}) collective-permute-start(bf16[128,128]{1,0:T(8,128)(2,1)S(1)} %get-tuple-element.39), channel_id=1, source_target_pairs={{0,4},{1,5},{2,6},{3,7},{4,0},{5,1},{6,2},{7,3},{8,12},{9,13},{10,... | collective-permute-start | bytes 98312 | tf_op jit(solution)/shard_map/ppermute | solution.py:353
  15.4 8.1 %collective-permute-start.5 = (bf16[128,128]{1,0:T(8,128)(2,1)S(1)}, bf16[128,128]{1,0:T(8,128)(2,1)S(1)}, u32[]{:S(2)}, u32[]{:S(2)}) collective-permute-start(bf16[128,128]{1,0:T(8,128)(2,1)S(1)} %get-tuple-element.40), channel_id=1, source_target_pairs={{0,5},{1,4},{2,7},{3,6},{4,1},{5,0},{6,3},{7,2},{8,13},{9,12},{10,... | collective-permute-start | bytes 98312 | tf_op jit(solution)/shard_map/ppermute | solution.py:353
  18.3 5.2 %collective-permute-start.6 = (bf16[128,128]{1,0:T(8,128)(2,1)S(1)}, bf16[128,128]{1,0:T(8,128)(2,1)S(1)}, u32[]{:S(2)}, u32[]{:S(2)}) collective-permute-start(bf16[128,128]{1,0:T(8,128)(2,1)S(1)} %get-tuple-element.41), channel_id=1, source_target_pairs={{0,3},{1,2},{2,1},{3,0},{4,7},{5,6},{6,5},{7,4},{8,11},{9,10},{10,... | collective-permute-start | bytes 98312 | tf_op jit(solution)/shard_map/ppermute | solution.py:353
  43.5 18.1 %all-to-all-start.3 = ((bf16[16,128,128]{2,1,0:T(8,128)(2,1)}), bf16[16,128,128]{2,1,0:T(8,128)(2,1)S(1)}, u32[]{:S(2)}, u32[]{:S(2)}) async-start(bf16[16,128,128]{2,1,0:T(8,128)(2,1)} %get-tuple-element.46), calls=%async_computation.3 | async-start | bytes 1048576 | tf_op jit(solution)/shard_map/all_to_all | solution.py:336
  48.6 4.6 %collective-permute-start.7 = (bf16[128,128]{1,0:T(8,128)(2,1)S(1)}, bf16[128,128]{1,0:T(8,128)(2,1)S(1)}, u32[]{:S(2)}, u32[]{:S(2)}) collective-permute-start(bf16[128,128]{1,0:T(8,128)(2,1)S(1)} %get-tuple-element.50), channel_id=1, source_target_pairs={{0,1},{1,0},{2,3},{3,2},{4,5},{5,4},{6,7},{7,6},{8,9},{9,8},{10,11... | collective-permute-start | bytes 98312 | tf_op jit(solution)/shard_map/ppermute | solution.py:353
  48.8 6.1 %collective-permute-start.8 = (bf16[128,128]{1,0:T(8,128)(2,1)S(1)}, bf16[128,128]{1,0:T(8,128)(2,1)S(1)}, u32[]{:S(2)}, u32[]{:S(2)}) collective-permute-start(bf16[128,128]{1,0:T(8,128)(2,1)S(1)} %get-tuple-element.51), channel_id=1, source_target_pairs={{0,2},{1,3},{2,0},{3,1},{4,6},{5,7},{6,4},{7,5},{8,10},{9,11},{10,... | collective-permute-start | bytes 98312 | tf_op jit(solution)/shard_map/ppermute | solution.py:353
  50.4 8.3 %collective-permute-start.9 = (bf16[128,128]{1,0:T(8,128)(2,1)S(1)}, bf16[128,128]{1,0:T(8,128)(2,1)S(1)}, u32[]{:S(2)}, u32[]{:S(2)}) collective-permute-start(bf16[128,128]{1,0:T(8,128)(2,1)S(1)} %get-tuple-element.52), channel_id=1, source_target_pairs={{0,6},{1,7},{2,4},{3,5},{4,2},{5,3},{6,0},{7,1},{8,14},{9,15},{10,... | collective-permute-start | bytes 98312 | tf_op jit(solution)/shard_map/ppermute | solution.py:353
  50.7 8.7 %collective-permute-start.10 = (bf16[128,128]{1,0:T(8,128)(2,1)S(1)}, bf16[128,128]{1,0:T(8,128)(2,1)S(1)}, u32[]{:S(2)}, u32[]{:S(2)}) collective-permute-start(bf16[128,128]{1,0:T(8,128)(2,1)S(1)} %get-tuple-element.53), channel_id=1, source_target_pairs={{0,7},{1,6},{2,5},{3,4},{4,3},{5,2},{6,1},{7,0},{8,15},{9,14},{10,... | collective-permute-start | bytes 98312 | tf_op jit(solution)/shard_map/ppermute | solution.py:353
  52.7 7.3 %collective-permute-start.11 = (bf16[128,128]{1,0:T(8,128)(2,1)S(1)}, bf16[128,128]{1,0:T(8,128)(2,1)S(1)}, u32[]{:S(2)}, u32[]{:S(2)}) collective-permute-start(bf16[128,128]{1,0:T(8,128)(2,1)S(1)} %get-tuple-element.54), channel_id=1, source_target_pairs={{0,4},{1,5},{2,6},{3,7},{4,0},{5,1},{6,2},{7,3},{8,12},{9,13},{10,... | collective-permute-start | bytes 98312 | tf_op jit(solution)/shard_map/ppermute | solution.py:353
  53.2 7.1 %collective-permute-start.12 = (bf16[128,128]{1,0:T(8,128)(2,1)S(1)}, bf16[128,128]{1,0:T(8,128)(2,1)S(1)}, u32[]{:S(2)}, u32[]{:S(2)}) collective-permute-start(bf16[128,128]{1,0:T(8,128)(2,1)S(1)} %get-tuple-element.55), channel_id=1, source_target_pairs={{0,5},{1,4},{2,7},{3,6},{4,1},{5,0},{6,3},{7,2},{8,13},{9,12},{10,... | collective-permute-start | bytes 98312 | tf_op jit(solution)/shard_map/ppermute | solution.py:353
  55.0 5.4 %collective-permute-start.13 = (bf16[128,128]{1,0:T(8,128)(2,1)S(1)}, bf16[128,128]{1,0:T(8,128)(2,1)S(1)}, u32[]{:S(2)}, u32[]{:S(2)}) collective-permute-start(bf16[128,128]{1,0:T(8,128)(2,1)S(1)} %get-tuple-element.56), channel_id=1, source_target_pairs={{0,3},{1,2},{2,1},{3,0},{4,7},{5,6},{6,5},{7,4},{8,11},{9,10},{10,... | collective-permute-start | bytes 98312 | tf_op jit(solution)/shard_map/ppermute | solution.py:353
  (5 other events, 16.1 us)

commit v29 on v27

--- a/solution.py
+++ b/solution.py
@@ -104,7 +104,7 @@
         if back:
             order += [place ^ (count // 2), count + place]
         else:
-            order += [count + (place ^ 2), place ^ (count // 2)]
+            order += [count + (place ^ 2), place ^ (count // 2) ^ 2]
     return order
 
 

time: 62.7 us -> 62.7 us (level)
  starting transfers between devices: 24.7 us -> 26.2 us
  waiting for transfers between devices: 8.69 us -> 7.86 us
    ppermute x14, starting transfers between devices: 11.3 us -> 12.8 us  [swap_pieces(): lax.ppermute(pieces[step], 'row', [(d, d ^ distance(step, count)) for d i...]
    ppermute x14, waiting for transfers between devices: 8.24 us -> 7.4 us  [swap_pieces(): lax.ppermute(pieces[step], 'row', [(d, d ^ distance(step, count)) for d i...]
  transfers between devices with their start and end apart: 16 -> 16, of which waited for: 10 -> 9; matrix products, arithmetic and copies ran while one was open for 0% -> 0% of each run, Pallas kernels for 6% -> 6%
where the time goes in v29:
time: 62.7 us; the launch traced here: 62.2 us
  starting transfers between devices  26.2 us (42%)
  blocking collectives  17.4 us (28%)
  Pallas kernels  9.56 us (15%)
  waiting for transfers between devices  7.86 us (13%)
  local copies, waits for them, and re-layouts  1.02 us (2%)
    all_to_all x2, blocking collectives, swap_half(): lax.all_to_all(values, 'row', split_axis=0, concat_axis=0, tiled=True, ax...  17.4 us
    all_to_all x2, starting transfers between devices, swap(): lax.all_to_all(values, 'row', split_axis=0, concat_axis=0, tiled=True, ax...  13.4 us
    ppermute x14, starting transfers between devices, swap_pieces(): lax.ppermute(pieces[step], 'row', [(d, d ^ distance(step, count)) for d i...  12.8 us
    pallas_call x12, Pallas kernels, call(): pl.pallas_call(body, name=name, out_shape=outs, in_specs=[pl.BlockSpec(me...  9.56 us
    ppermute x14, waiting for transfers between devices, swap_pieces(): lax.ppermute(pieces[step], 'row', [(d, d ^ distance(step, count)) for d i...  7.4 us
  transfers between devices with their start and end apart: 16, of which 9 were waited for; matrix products, arithmetic and copies ran while one was open for 0% of the time, Pallas kernels for 6%

profile of v29, /device:TPU:0, one launch (start us, length us, event | category | flops | bytes accessed | tf_op | source)
XLA Modules:
  0.0 62.2 jit_solution(6528006041727783788)
XLA Ops:
  0.0 2.3 %project_right.1.refs_5_ = bf16[16,128,128]{2,1,0:T(8,128)(2,1)} custom-call(bf16[8,128,128]{2,1,0:T(8,128)(2,1)} %refs_0_.7, s32[1,128]{1,0:T(1,128)} %bitcast.13, f32[1,128]{1,0:T(1,128)} %bitcast.5, f32[1,128]{1,0:T(1,128)} %bitcast.9, bf16[128,512]{1,0:T(8,128)(2,1)} %refs_4_.9), custom_call_target="tpu_custom_call" | custom-call | flops 67108864 | bytes 919040 | tf_op jit(solution)/shard_map/project_right/pallas_call | solution.py:72
  2.4 8.6 %all-to-all-start = ((bf16[16,128,128]{2,1,0:T(8,128)(2,1)}), bf16[16,128,128]{2,1,0:T(8,128)(2,1)S(1)}, u32[]{:S(2)}, u32[]{:S(2)}) async-start(bf16[16,128,128]{2,1,0:T(8,128)(2,1)} %project_right.1.refs_5_), calls=%async_computation | async-start | bytes 1048576 | tf_op jit(solution)/shard_map/all_to_all | solution.py:336
  12.4 1.4 %collective-permute-start.2 = (bf16[128,128]{1,0:T(8,128)(2,1)S(1)}, bf16[128,128]{1,0:T(8,128)(2,1)S(1)}, u32[]{:S(2)}, u32[]{:S(2)}) collective-permute-start(bf16[128,128]{1,0:T(8,128)(2,1)S(1)} %get-tuple-element.37), channel_id=1, source_target_pairs={{0,6},{1,7},{2,4},{3,5},{4,2},{5,3},{6,0},{7,1},{8,14},{9,15},{10,... | collective-permute-start | bytes 98312 | tf_op jit(solution)/shard_map/ppermute | solution.py:353
  13.9 0.9 %collective-permute-start.3 = (bf16[128,128]{1,0:T(8,128)(2,1)S(1)}, bf16[128,128]{1,0:T(8,128)(2,1)S(1)}, u32[]{:S(2)}, u32[]{:S(2)}) collective-permute-start(bf16[128,128]{1,0:T(8,128)(2,1)S(1)} %get-tuple-element.38), channel_id=1, source_target_pairs={{0,7},{1,6},{2,5},{3,4},{4,3},{5,2},{6,1},{7,0},{8,15},{9,14},{10,... | collective-permute-start | bytes 98312 | tf_op jit(solution)/shard_map/ppermute | solution.py:353
  14.8 0.6 %collective-permute-start.4 = (bf16[128,128]{1,0:T(8,128)(2,1)S(1)}, bf16[128,128]{1,0:T(8,128)(2,1)S(1)}, u32[]{:S(2)}, u32[]{:S(2)}) collective-permute-start(bf16[128,128]{1,0:T(8,128)(2,1)S(1)} %get-tuple-element.39), channel_id=1, source_target_pairs={{0,4},{1,5},{2,6},{3,7},{4,0},{5,1},{6,2},{7,3},{8,12},{9,13},{10,... | collective-permute-start | bytes 98312 | tf_op jit(solution)/shard_map/ppermute | solution.py:353
  15.4 1.4 %collective-permute-start.5 = (bf16[128,128]{1,0:T(8,128)(2,1)S(1)}, bf16[128,128]{1,0:T(8,128)(2,1)S(1)}, u32[]{:S(2)}, u32[]{:S(2)}) collective-permute-start(bf16[128,128]{1,0:T(8,128)(2,1)S(1)} %get-tuple-element.40), channel_id=1, source_target_pairs={{0,5},{1,4},{2,7},{3,6},{4,1},{5,0},{6,3},{7,2},{8,13},{9,12},{10,... | collective-permute-start | bytes 98312 | tf_op jit(solution)/shard_map/ppermute | solution.py:353
  16.8 1.5 %collective-permute-start.6 = (bf16[128,128]{1,0:T(8,128)(2,1)S(1)}, bf16[128,128]{1,0:T(8,128)(2,1)S(1)}, u32[]{:S(2)}, u32[]{:S(2)}) collective-permute-start(bf16[128,128]{1,0:T(8,128)(2,1)S(1)} %get-tuple-element.41), channel_id=1, source_target_pairs={{0,3},{1,2},{2,1},{3,0},{4,7},{5,6},{6,5},{7,4},{8,11},{9,10},{10,... | collective-permute-start | bytes 98312 | tf_op jit(solution)/shard_map/ppermute | solution.py:353
  18.4 0.8 %prepare.1 = (f32[8,128,128]{2,1,0:T(8,128)S(1)}, f32[8,128,128]{2,1,0:T(8,128)S(1)}) custom-call(bf16[8,128,128]{2,1,0:T(8,128)(2,1)S(1)} %copy-done.1, bf16[8,128,128]{2,1,0:T(8,128)(2,1)S(1)} %copy-done.3, f32[1,128]{1,0:T(1,128)S(1)} %bitcast.7, f32[1,128]{1,0:T(1,128)S(1)} %bitcast.11, bf16[128,128]{1,0:T(8,128)(2,1)S(1)} %copy-done.6, ...), custom_call_target="tpu_custom_call" | custom-call | flops 67108864 | bytes 1639936 | tf_op jit(solution)/shard_map/prepare/pallas_call | solution.py:72
  19.2 2.1 %collective-permute-done.2.refs_3_ = bf16[128,128]{1,0:T(8,128)(2,1)S(1)} collective-permute-done((bf16[128,128]{1,0:T(8,128)(2,1)S(1)}, bf16[128,128]{1,0:T(8,128)(2,1)S(1)}, u32[]{:S(2)}, u32[]{:S(2)}) %collective-permute-start.2) | collective-permute-done | bytes 32800 | tf_op jit(solution)/shard_map/ppermute | solution.py:353
  21.3 0.7 %collective-permute-done.3.refs_4_ = bf16[128,128]{1,0:T(8,128)(2,1)S(1)} collective-permute-done((bf16[128,128]{1,0:T(8,128)(2,1)S(1)}, bf16[128,128]{1,0:T(8,128)(2,1)S(1)}, u32[]{:S(2)}, u32[]{:S(2)}) %collective-permute-start.3) | collective-permute-done | bytes 32800 | tf_op jit(solution)/shard_map/ppermute | solution.py:353
  22.0 1.5 %collective-permute-done.4.refs_5_ = bf16[128,128]{1,0:T(8,128)(2,1)S(1)} collective-permute-done((bf16[128,128]{1,0:T(8,128)(2,1)S(1)}, bf16[128,128]{1,0:T(8,128)(2,1)S(1)}, u32[]{:S(2)}, u32[]{:S(2)}) %collective-permute-start.4) | collective-permute-done | bytes 32800 | tf_op jit(solution)/shard_map/ppermute | solution.py:353
  23.8 0.6 %tri.1 = (bf16[8,128,128]{2,1,0:T(8,128)(2,1)S(1)}, bf16[16,128,128]{2,1,0:T(8,128)(2,1)S(1)}) custom-call(bf16[16,128,128]{2,1,0:T(8,128)(2,1)S(1)} %all-to-all-done.refs_0_, bf16[16,64,128]{2,1,0:T(8,128)(2,1)S(1)} %get-tuple-element.42.refs_1_, f32[8,128,128]{2,1,0:T(8,128)S(1)} %get-tuple-element.43.refs_2_.refs_1_), custom_call_target="tpu_custom_call" | custom-call | flops 33554432 | bytes 2097152 | tf_op jit(solution)/shard_map/tri/pallas_call | solution.py:72
  24.4 8.7 %all_to_all.20.refs_0_ = bf16[8,128,128]{2,1,0:T(8,128)(2,1)S(1)} all-to-all(bf16[8,128,128]{2,1,0:T(8,128)(2,1)S(1)} %get-tuple-element.44), channel_id=1, replica_groups={{0,1,2,3,4,5,6,7},{8,9,10,11,12,13,14,15},{16,17,18,19,20,21,22,23},{24..., dimensions={0} | all-to-all | bytes 524288 | tf_op jit(solution)/shard_map/all_to_all | solution.py:344
  33.5 8.6 %all_to_all.21.refs_0_ = bf16[8,128,128]{2,1,0:T(8,128)(2,1)S(1)} all-to-all(bf16[8,128,128]{2,1,0:T(8,128)(2,1)S(1)} %middle.1), channel_id=1, replica_groups={{0,1,2,3,4,5,6,7},{8,9,10,11,12,13,14,15},{16,17,18,19,20,21,22,23},{24..., dimensions={0} | all-to-all | bytes 524288 | tf_op jit(solution)/shard_map/all_to_all | solution.py:344
  42.1 1.4 %d_right.1 = (bf16[16,128,128]{2,1,0:T(8,128)(2,1)}, bf16[16,64,128]{2,1,0:T(8,128)(2,1)S(1)}) custom-call(bf16[8,128,128]{2,1,0:T(8,128)(2,1)S(1)} %all_to_all.21.refs_0_, bf16[8,128,256]{2,1,0:T(8,128)(2,1)S(1)} %get-tuple-element.45.refs_1_), custom_call_target="tpu_custom_call" | custom-call | flops 33554432 | bytes 1572864 | tf_op jit(solution)/shard_map/d_right/pallas_call | solution.py:72
  43.5 4.9 %all-to-all-start.3 = ((bf16[16,128,128]{2,1,0:T(8,128)(2,1)}), bf16[16,128,128]{2,1,0:T(8,128)(2,1)S(1)}, u32[]{:S(2)}, u32[]{:S(2)}) async-start(bf16[16,128,128]{2,1,0:T(8,128)(2,1)} %get-tuple-element.46), calls=%async_computation.3 | async-start | bytes 1048576 | tf_op jit(solution)/shard_map/all_to_all | solution.py:336
  48.9 1.5 %collective-permute-start.8 = (bf16[128,128]{1,0:T(8,128)(2,1)S(1)}, bf16[128,128]{1,0:T(8,128)(2,1)S(1)}, u32[]{:S(2)}, u32[]{:S(2)}) collective-permute-start(bf16[128,128]{1,0:T(8,128)(2,1)S(1)} %get-tuple-element.51), channel_id=1, source_target_pairs={{0,2},{1,3},{2,0},{3,1},{4,6},{5,7},{6,4},{7,5},{8,10},{9,11},{10,... | collective-permute-start | bytes 98312 | tf_op jit(solution)/shard_map/ppermute | solution.py:353
  50.7 2.0 %collective-permute-start.10 = (bf16[128,128]{1,0:T(8,128)(2,1)S(1)}, bf16[128,128]{1,0:T(8,128)(2,1)S(1)}, u32[]{:S(2)}, u32[]{:S(2)}) collective-permute-start(bf16[128,128]{1,0:T(8,128)(2,1)S(1)} %get-tuple-element.53), channel_id=1, source_target_pairs={{0,7},{1,6},{2,5},{3,4},{4,3},{5,2},{6,1},{7,0},{8,15},{9,14},{10,... | collective-permute-start | bytes 98312 | tf_op jit(solution)/shard_map/ppermute | solution.py:353
  53.3 1.6 %collective-permute-start.12 = (bf16[128,128]{1,0:T(8,128)(2,1)S(1)}, bf16[128,128]{1,0:T(8,128)(2,1)S(1)}, u32[]{:S(2)}, u32[]{:S(2)}) collective-permute-start(bf16[128,128]{1,0:T(8,128)(2,1)S(1)} %get-tuple-element.55), channel_id=1, source_target_pairs={{0,5},{1,4},{2,7},{3,6},{4,1},{5,0},{6,3},{7,2},{8,13},{9,12},{10,... | collective-permute-start | bytes 98312 | tf_op jit(solution)/shard_map/ppermute | solution.py:353
  54.8 1.2 %collective-permute-done.8.refs_2_ = bf16[128,128]{1,0:T(8,128)(2,1)S(1)} collective-permute-done((bf16[128,128]{1,0:T(8,128)(2,1)S(1)}, bf16[128,128]{1,0:T(8,128)(2,1)S(1)}, u32[]{:S(2)}, u32[]{:S(2)}) %collective-permute-start.8) | collective-permute-done | bytes 32800 | tf_op jit(solution)/shard_map/ppermute | solution.py:353
  56.0 0.6 %copy-done.12 = f32[128]{0:T(128)S(1)} copy-done((f32[128]{0:T(128)S(1)}, f32[128]{0:T(128)}, u32[]{:S(2)}) %copy-start.12) | copy-done | bytes 536
  57.4 1.0 %slopes.1 = (bf16[8,512,128]{2,1,0:T(8,128)(2,1)S(1)}, bf16[8,128,128]{2,1,0:T(8,128)(2,1)S(1)}, f32[8,128]{1,0:T(8,128)S(1)}, f32[128,128]{1,0:T(8,128)S(1)}, bf16[128,640]{1,0:T(8,128)(2,1)S(1)}) custom-call(bf16[8,128,128]{2,1,0:T(8,128)(2,1)S(1)} %copy-done.1, s32[1,128]{1,0:T(1,128)S(1)} %bitcast.15, f32[1,128]{1,0:T(1,128)S(1)} %bitcast.8, ...), custom_call_target="tpu_custom_call" | custom-call | flops 134217728 | bytes 2233856 | tf_op jit(solution)/shard_map/slopes/pallas_call | solution.py:72
  58.7 0.7 %collective-permute-done.10.refs_4_ = bf16[128,128]{1,0:T(8,128)(2,1)S(1)} collective-permute-done((bf16[128,128]{1,0:T(8,128)(2,1)S(1)}, bf16[128,128]{1,0:T(8,128)(2,1)S(1)}, u32[]{:S(2)}, u32[]{:S(2)}) %collective-permute-start.10) | collective-permute-done | bytes 32800 | tf_op jit(solution)/shard_map/ppermute | solution.py:353
  60.8 1.4 %finish.1 = bf16[8,128,128]{2,1,0:T(8,128)(2,1)} custom-call(bf16[16,128,128]{2,1,0:T(8,128)(2,1)S(1)} %all-to-all-done.3.refs_0_, bf16[8,128,128]{2,1,0:T(8,128)(2,1)S(1)} %sort_d_left.1.refs_1_, bf16[8,512,128]{2,1,0:T(8,128)(2,1)S(1)} %get-tuple-element.58.refs_2_, bf16[8,128,128]{2,1,0:T(8,128)(2,1)S(1)} %gate_back.1.refs_6_.refs_3_, ...), custom_call_target="tpu_custom_call" | custom-call | flops 134217728 | bytes 2854912 | tf_op jit(solution)/shard_map/finish/pallas_call | solution.py:72
  (48 shorter events, 5.7 us)
Async XLA Ops:
  2.3 8.6 %copy-start = (bf16[16,128,128]{2,1,0:T(8,128)(2,1)S(1)}, bf16[16,128,128]{2,1,0:T(8,128)(2,1)}, u32[]{:S(2)}) copy-start(bf16[16,128,128]{2,1,0:T(8,128)(2,1)} %project_right.1.refs_5_) | copy-start | bytes 1572868
  2.3 8.6 %copy-start.1 = (bf16[8,128,128]{2,1,0:T(8,128)(2,1)S(1)}, bf16[8,128,128]{2,1,0:T(8,128)(2,1)}, u32[]{:S(2)}) copy-start(bf16[8,128,128]{2,1,0:T(8,128)(2,1)} %refs_0_.7) | copy-start | bytes 786436
  2.3 8.6 %copy-start.2 = (bf16[128,512]{1,0:T(8,128)(2,1)S(1)}, bf16[128,512]{1,0:T(8,128)(2,1)}, u32[]{:S(2)}) copy-start(bf16[128,512]{1,0:T(8,128)(2,1)} %refs_4_.9) | copy-start | bytes 393220
  2.4 8.6 %copy-start.8 = (f32[128]{0:T(128)S(1)}, f32[128]{0:T(128)}, u32[]{:S(2)}) copy-start(f32[128]{0:T(128)} %param.13) | copy-start | bytes 1540
  2.4 8.6 %copy-start.9 = (f32[128]{0:T(128)S(1)}, f32[128]{0:T(128)}, u32[]{:S(2)}) copy-start(f32[128]{0:T(128)} %param.14) | copy-start | bytes 1540
  2.4 8.6 %copy-start.10 = (s32[128]{0:T(128)S(1)}, s32[128]{0:T(128)}, u32[]{:S(2)}) copy-start(s32[128]{0:T(128)} %param.12) | copy-start | bytes 1540
  2.4 21.4 %all-to-all-start = ((bf16[16,128,128]{2,1,0:T(8,128)(2,1)}), bf16[16,128,128]{2,1,0:T(8,128)(2,1)S(1)}, u32[]{:S(2)}, u32[]{:S(2)}) async-start(bf16[16,128,128]{2,1,0:T(8,128)(2,1)} %project_right.1.refs_5_), calls=%async_computation | async-start | bytes 1048576 | tf_op jit(solution)/shard_map/all_to_all | solution.py:336
  11.0 7.4 %copy-start.3 = (bf16[8,128,128]{2,1,0:T(8,128)(2,1)S(1)}, bf16[8,128,128]{2,1,0:T(8,128)(2,1)}, u32[]{:S(2)}) copy-start(bf16[8,128,128]{2,1,0:T(8,128)(2,1)} %refs_1_.1) | copy-start | bytes 786436
  11.7 3.7 %collective-permute-start = (bf16[128,128]{1,0:T(8,128)(2,1)S(1)}, bf16[128,128]{1,0:T(8,128)(2,1)S(1)}, u32[]{:S(2)}, u32[]{:S(2)}) collective-permute-start(bf16[128,128]{1,0:T(8,128)(2,1)S(1)} %get-tuple-element.35), channel_id=1, source_target_pairs={{0,1},{1,0},{2,3},{3,2},{4,5},{5,4},{6,7},{7,6},{8,9},{9,8},{10,11... | collective-permute-start | bytes 98312 | tf_op jit(solution)/shard_map/ppermute | solution.py:353
  11.9 4.9 %collective-permute-start.1 = (bf16[128,128]{1,0:T(8,128)(2,1)S(1)}, bf16[128,128]{1,0:T(8,128)(2,1)S(1)}, u32[]{:S(2)}, u32[]{:S(2)}) collective-permute-start(bf16[128,128]{1,0:T(8,128)(2,1)S(1)} %get-tuple-element.36), channel_id=1, source_target_pairs={{0,2},{1,3},{2,0},{3,1},{4,6},{5,7},{6,4},{7,5},{8,10},{9,11},{10,... | collective-permute-start | bytes 98312 | tf_op jit(solution)/shard_map/ppermute | solution.py:353
  12.4 8.9 %collective-permute-start.2 = (bf16[128,128]{1,0:T(8,128)(2,1)S(1)}, bf16[128,128]{1,0:T(8,128)(2,1)S(1)}, u32[]{:S(2)}, u32[]{:S(2)}) collective-permute-start(bf16[128,128]{1,0:T(8,128)(2,1)S(1)} %get-tuple-element.37), channel_id=1, source_target_pairs={{0,6},{1,7},{2,4},{3,5},{4,2},{5,3},{6,0},{7,1},{8,14},{9,15},{10,... | collective-permute-start | bytes 98312 | tf_op jit(solution)/shard_map/ppermute | solution.py:353
  13.9 8.2 %collective-permute-start.3 = (bf16[128,128]{1,0:T(8,128)(2,1)S(1)}, bf16[128,128]{1,0:T(8,128)(2,1)S(1)}, u32[]{:S(2)}, u32[]{:S(2)}) collective-permute-start(bf16[128,128]{1,0:T(8,128)(2,1)S(1)} %get-tuple-element.38), channel_id=1, source_target_pairs={{0,7},{1,6},{2,5},{3,4},{4,3},{5,2},{6,1},{7,0},{8,15},{9,14},{10,... | collective-permute-start | bytes 98312 | tf_op jit(solution)/shard_map/ppermute | solution.py:353
  14.8 8.8 %collective-permute-start.4 = (bf16[128,128]{1,0:T(8,128)(2,1)S(1)}, bf16[128,128]{1,0:T(8,128)(2,1)S(1)}, u32[]{:S(2)}, u32[]{:S(2)}) collective-permute-start(bf16[128,128]{1,0:T(8,128)(2,1)S(1)} %get-tuple-element.39), channel_id=1, source_target_pairs={{0,4},{1,5},{2,6},{3,7},{4,0},{5,1},{6,2},{7,3},{8,12},{9,13},{10,... | collective-permute-start | bytes 98312 | tf_op jit(solution)/shard_map/ppermute | solution.py:353
  15.4 8.2 %collective-permute-start.5 = (bf16[128,128]{1,0:T(8,128)(2,1)S(1)}, bf16[128,128]{1,0:T(8,128)(2,1)S(1)}, u32[]{:S(2)}, u32[]{:S(2)}) collective-permute-start(bf16[128,128]{1,0:T(8,128)(2,1)S(1)} %get-tuple-element.40), channel_id=1, source_target_pairs={{0,5},{1,4},{2,7},{3,6},{4,1},{5,0},{6,3},{7,2},{8,13},{9,12},{10,... | collective-permute-start | bytes 98312 | tf_op jit(solution)/shard_map/ppermute | solution.py:353
  16.8 6.7 %collective-permute-start.6 = (bf16[128,128]{1,0:T(8,128)(2,1)S(1)}, bf16[128,128]{1,0:T(8,128)(2,1)S(1)}, u32[]{:S(2)}, u32[]{:S(2)}) collective-permute-start(bf16[128,128]{1,0:T(8,128)(2,1)S(1)} %get-tuple-element.41), channel_id=1, source_target_pairs={{0,3},{1,2},{2,1},{3,0},{4,7},{5,6},{6,5},{7,4},{8,11},{9,10},{10,... | collective-permute-start | bytes 98312 | tf_op jit(solution)/shard_map/ppermute | solution.py:353
  43.5 17.3 %all-to-all-start.3 = ((bf16[16,128,128]{2,1,0:T(8,128)(2,1)}), bf16[16,128,128]{2,1,0:T(8,128)(2,1)S(1)}, u32[]{:S(2)}, u32[]{:S(2)}) async-start(bf16[16,128,128]{2,1,0:T(8,128)(2,1)} %get-tuple-element.46), calls=%async_computation.3 | async-start | bytes 1048576 | tf_op jit(solution)/shard_map/all_to_all | solution.py:336
  48.4 7.7 %copy-start.5 = (bf16[128,128]{1,0:T(8,128)(2,1)S(1)}, bf16[128,128]{1,0:T(8,128)(2,1)}, u32[]{:S(2)}) copy-start(bf16[128,128]{1,0:T(8,128)(2,1)} %refs_4_.8) | copy-start | bytes 98308
  48.7 4.5 %collective-permute-start.7 = (bf16[128,128]{1,0:T(8,128)(2,1)S(1)}, bf16[128,128]{1,0:T(8,128)(2,1)S(1)}, u32[]{:S(2)}, u32[]{:S(2)}) collective-permute-start(bf16[128,128]{1,0:T(8,128)(2,1)S(1)} %get-tuple-element.50), channel_id=1, source_target_pairs={{0,1},{1,0},{2,3},{3,2},{4,5},{5,4},{6,7},{7,6},{8,9},{9,8},{10,11... | collective-permute-start | bytes 98312 | tf_op jit(solution)/shard_map/ppermute | solution.py:353
  48.9 7.1 %collective-permute-start.8 = (bf16[128,128]{1,0:T(8,128)(2,1)S(1)}, bf16[128,128]{1,0:T(8,128)(2,1)S(1)}, u32[]{:S(2)}, u32[]{:S(2)}) collective-permute-start(bf16[128,128]{1,0:T(8,128)(2,1)S(1)} %get-tuple-element.51), channel_id=1, source_target_pairs={{0,2},{1,3},{2,0},{3,1},{4,6},{5,7},{6,4},{7,5},{8,10},{9,11},{10,... | collective-permute-start | bytes 98312 | tf_op jit(solution)/shard_map/ppermute | solution.py:353
  50.4 8.3 %collective-permute-start.9 = (bf16[128,128]{1,0:T(8,128)(2,1)S(1)}, bf16[128,128]{1,0:T(8,128)(2,1)S(1)}, u32[]{:S(2)}, u32[]{:S(2)}) collective-permute-start(bf16[128,128]{1,0:T(8,128)(2,1)S(1)} %get-tuple-element.52), channel_id=1, source_target_pairs={{0,6},{1,7},{2,4},{3,5},{4,2},{5,3},{6,0},{7,1},{8,14},{9,15},{10,... | collective-permute-start | bytes 98312 | tf_op jit(solution)/shard_map/ppermute | solution.py:353
  50.7 8.7 %collective-permute-start.10 = (bf16[128,128]{1,0:T(8,128)(2,1)S(1)}, bf16[128,128]{1,0:T(8,128)(2,1)S(1)}, u32[]{:S(2)}, u32[]{:S(2)}) collective-permute-start(bf16[128,128]{1,0:T(8,128)(2,1)S(1)} %get-tuple-element.53), channel_id=1, source_target_pairs={{0,7},{1,6},{2,5},{3,4},{4,3},{5,2},{6,1},{7,0},{8,15},{9,14},{10,... | collective-permute-start | bytes 98312 | tf_op jit(solution)/shard_map/ppermute | solution.py:353
  52.8 7.2 %collective-permute-start.11 = (bf16[128,128]{1,0:T(8,128)(2,1)S(1)}, bf16[128,128]{1,0:T(8,128)(2,1)S(1)}, u32[]{:S(2)}, u32[]{:S(2)}) collective-permute-start(bf16[128,128]{1,0:T(8,128)(2,1)S(1)} %get-tuple-element.54), channel_id=1, source_target_pairs={{0,4},{1,5},{2,6},{3,7},{4,0},{5,1},{6,2},{7,3},{8,12},{9,13},{10,... | collective-permute-start | bytes 98312 | tf_op jit(solution)/shard_map/ppermute | solution.py:353
  53.3 7.1 %collective-permute-start.12 = (bf16[128,128]{1,0:T(8,128)(2,1)S(1)}, bf16[128,128]{1,0:T(8,128)(2,1)S(1)}, u32[]{:S(2)}, u32[]{:S(2)}) collective-permute-start(bf16[128,128]{1,0:T(8,128)(2,1)S(1)} %get-tuple-element.55), channel_id=1, source_target_pairs={{0,5},{1,4},{2,7},{3,6},{4,1},{5,0},{6,3},{7,2},{8,13},{9,12},{10,... | collective-permute-start | bytes 98312 | tf_op jit(solution)/shard_map/ppermute | solution.py:353
  56.0 4.3 %collective-permute-start.13 = (bf16[128,128]{1,0:T(8,128)(2,1)S(1)}, bf16[128,128]{1,0:T(8,128)(2,1)S(1)}, u32[]{:S(2)}, u32[]{:S(2)}) collective-permute-start(bf16[128,128]{1,0:T(8,128)(2,1)S(1)} %get-tuple-element.56), channel_id=1, source_target_pairs={{0,3},{1,2},{2,1},{3,0},{4,7},{5,6},{6,5},{7,4},{8,11},{9,10},{10,... | collective-permute-start | bytes 98312 | tf_op jit(solution)/shard_map/ppermute | solution.py:353
  (5 other events, 17.6 us)

commit v30 on v24

--- a/solution.py
+++ b/solution.py
@@ -102,8 +102,8 @@
 
 
 def distance(step, count):
-    far = sorted(range(3, count), key=lambda apart: apart < count // 2)
-    return [*range(min(3, count)), *far][step]
+    far = sorted(range(2, count), key=lambda apart: -(apart // 2))
+    return [0, 1, *far][step]
 
 
 def partner(step, count):

time: 64.6 us -> 67.4 us (1.043)
  waiting for transfers between devices: 9.6 us -> 11.1 us
  blocking collectives: 18.5 us -> 19.2 us
    ppermute x14, waiting for transfers between devices: 9.59 us -> 11.1 us  [swap_pieces(): lax.ppermute(pieces[step], 'row', [(d, d ^ distance(step, count)) for d i...]
    all_to_all x2, blocking collectives: 18.5 us -> 19.2 us  [swap_half(): lax.all_to_all(values, 'row', split_axis=0, concat_axis=0, tiled=True, ax...]
  transfers between devices with their start and end apart: 16 -> 16, of which waited for: 9 -> 5; matrix products, arithmetic and copies ran while one was open for 0% -> 0% of each run, Pallas kernels for 6% -> 5%
where the time goes in v30:
time: 67.4 us; the launch traced here: 66.8 us
  starting transfers between devices  25 us (37%)
  blocking collectives  19.2 us (28%)
  waiting for transfers between devices  11.1 us (16%)
  Pallas kernels  9.82 us (15%)
  local copies, waits for them, and re-layouts  1.34 us (2%)
    all_to_all x2, blocking collectives, swap_half(): lax.all_to_all(values, 'row', split_axis=0, concat_axis=0, tiled=True, ax...  19.2 us
    all_to_all x2, starting transfers between devices, swap(): lax.all_to_all(values, 'row', split_axis=0, concat_axis=0, tiled=True, ax...  13.4 us
    ppermute x14, starting transfers between devices, swap_pieces(): lax.ppermute(pieces[step], 'row', [(d, d ^ distance(step, count)) for d i...  11.6 us
    ppermute x14, waiting for transfers between devices, swap_pieces(): lax.ppermute(pieces[step], 'row', [(d, d ^ distance(step, count)) for d i...  11.1 us
    pallas_call x12, Pallas kernels, call(): pl.pallas_call(body, name=name, out_shape=outs, in_specs=[pl.BlockSpec(me...  9.82 us
  transfers between devices with their start and end apart: 16, of which 5 were waited for; matrix products, arithmetic and copies ran while one was open for 0% of the time, Pallas kernels for 5%

profile of v30, /device:TPU:0, one launch (start us, length us, event | category | flops | bytes accessed | tf_op | source)
XLA Modules:
  0.0 66.8 jit_solution(968503148114610695)
XLA Ops:
  0.0 2.4 %project_right.1.refs_5_ = bf16[16,128,128]{2,1,0:T(8,128)(2,1)} custom-call(bf16[8,128,128]{2,1,0:T(8,128)(2,1)} %refs_0_.7, s32[1,128]{1,0:T(1,128)} %bitcast.13, f32[1,128]{1,0:T(1,128)} %bitcast.5, f32[1,128]{1,0:T(1,128)} %bitcast.9, bf16[128,512]{1,0:T(8,128)(2,1)} %refs_4_.9), custom_call_target="tpu_custom_call" | custom-call | flops 67108864 | bytes 919040 | tf_op jit(solution)/shard_map/project_right/pallas_call | solution.py:65
  2.5 8.5 %all-to-all-start = ((bf16[16,128,128]{2,1,0:T(8,128)(2,1)}), bf16[16,128,128]{2,1,0:T(8,128)(2,1)S(1)}, u32[]{:S(2)}, u32[]{:S(2)}) async-start(bf16[16,128,128]{2,1,0:T(8,128)(2,1)} %project_right.1.refs_5_), calls=%async_computation | async-start | bytes 1048576 | tf_op jit(solution)/shard_map/all_to_all | solution.py:319
  11.1 0.8 %project_left.1 = (bf16[128,128]{1,0:T(8,128)(2,1)S(1)}, bf16[128,128]{1,0:T(8,128)(2,1)S(1)}, bf16[128,128]{1,0:T(8,128)(2,1)S(1)}, bf16[128,128]{1,0:T(8,128)(...) custom-call(bf16[8,128,128]{2,1,0:T(8,128)(2,1)S(1)} %copy-done.1, ...), custom_call_target="tpu_custom_call" | custom-call | flops 67108864 | bytes 1181184 | tf_op jit(solution)/shard_map/project_left/pallas_call | solution.py:65
  12.6 2.1 %collective-permute-start.2 = (bf16[128,128]{1,0:T(8,128)(2,1)S(1)}, bf16[128,128]{1,0:T(8,128)(2,1)S(1)}, u32[]{:S(2)}, u32[]{:S(2)}) collective-permute-start(bf16[128,128]{1,0:T(8,128)(2,1)S(1)} %get-tuple-element.35), channel_id=1, source_target_pairs={{0,7},{1,6},{2,5},{3,4},{4,3},{5,2},{6,1},{7,0},{8,15},{9,14},{10,... | collective-permute-start | bytes 98312 | tf_op jit(solution)/shard_map/ppermute | solution.py:336
  15.2 1.3 %collective-permute-start.4 = (bf16[128,128]{1,0:T(8,128)(2,1)S(1)}, bf16[128,128]{1,0:T(8,128)(2,1)S(1)}, u32[]{:S(2)}, u32[]{:S(2)}) collective-permute-start(bf16[128,128]{1,0:T(8,128)(2,1)S(1)} %get-tuple-element.37), channel_id=1, source_target_pairs={{0,5},{1,4},{2,7},{3,6},{4,1},{5,0},{6,3},{7,2},{8,13},{9,12},{10,... | collective-permute-start | bytes 98312 | tf_op jit(solution)/shard_map/ppermute | solution.py:336
  17.1 4.2 %collective-permute-done.1.refs_2_ = bf16[128,128]{1,0:T(8,128)(2,1)S(1)} collective-permute-done((bf16[128,128]{1,0:T(8,128)(2,1)S(1)}, bf16[128,128]{1,0:T(8,128)(2,1)S(1)}, u32[]{:S(2)}, u32[]{:S(2)}) %collective-permute-start.1) | collective-permute-done | bytes 32800 | tf_op jit(solution)/shard_map/ppermute | solution.py:336
  21.4 0.6 copy-done.9
  22.0 0.8 %prepare.1 = (f32[8,128,128]{2,1,0:T(8,128)S(1)}, f32[8,128,128]{2,1,0:T(8,128)S(1)}) custom-call(bf16[8,128,128]{2,1,0:T(8,128)(2,1)S(1)} %copy-done.1, bf16[8,128,128]{2,1,0:T(8,128)(2,1)S(1)} %copy-done.3, f32[1,128]{1,0:T(1,128)S(1)} %bitcast.7, f32[1,128]{1,0:T(1,128)S(1)} %bitcast.11, bf16[128,128]{1,0:T(8,128)(2,1)S(1)} %copy-done.5, ...), custom_call_target="tpu_custom_call" | custom-call | flops 67108864 | bytes 1639936 | tf_op jit(solution)/shard_map/prepare/pallas_call | solution.py:65
  22.8 0.8 %collective-permute-done.3.refs_4_ = bf16[128,128]{1,0:T(8,128)(2,1)S(1)} collective-permute-done((bf16[128,128]{1,0:T(8,128)(2,1)S(1)}, bf16[128,128]{1,0:T(8,128)(2,1)S(1)}, u32[]{:S(2)}, u32[]{:S(2)}) %collective-permute-start.3) | collective-permute-done | bytes 32800 | tf_op jit(solution)/shard_map/ppermute | solution.py:336
  23.6 1.1 %collective-permute-done.6.refs_7_ = bf16[128,128]{1,0:T(8,128)(2,1)S(1)} collective-permute-done((bf16[128,128]{1,0:T(8,128)(2,1)S(1)}, bf16[128,128]{1,0:T(8,128)(2,1)S(1)}, u32[]{:S(2)}, u32[]{:S(2)}) %collective-permute-start.6) | collective-permute-done | bytes 32800 | tf_op jit(solution)/shard_map/ppermute | solution.py:336
  24.9 0.6 tri.1
  25.5 10.6 %all_to_all.20.refs_0_ = bf16[8,128,128]{2,1,0:T(8,128)(2,1)S(1)} all-to-all(bf16[8,128,128]{2,1,0:T(8,128)(2,1)S(1)} %get-tuple-element.41), channel_id=1, replica_groups={{0,1,2,3,4,5,6,7},{8,9,10,11,12,13,14,15},{16,17,18,19,20,21,22,23},{24..., dimensions={0} | all-to-all | bytes 524288 | tf_op jit(solution)/shard_map/all_to_all | solution.py:327
  36.5 8.6 %all_to_all.21.refs_0_ = bf16[8,128,128]{2,1,0:T(8,128)(2,1)S(1)} all-to-all(bf16[8,128,128]{2,1,0:T(8,128)(2,1)S(1)} %middle.1), channel_id=1, replica_groups={{0,1,2,3,4,5,6,7},{8,9,10,11,12,13,14,15},{16,17,18,19,20,21,22,23},{24..., dimensions={0} | all-to-all | bytes 524288 | tf_op jit(solution)/shard_map/all_to_all | solution.py:327
  45.1 1.5 %d_right.1 = (bf16[16,128,128]{2,1,0:T(8,128)(2,1)}, bf16[16,64,128]{2,1,0:T(8,128)(2,1)S(1)}) custom-call(bf16[8,128,128]{2,1,0:T(8,128)(2,1)S(1)} %all_to_all.21.refs_0_, bf16[16,64,128]{2,1,0:T(8,128)(2,1)S(1)} %sort_left.1.refs_1_), custom_call_target="tpu_custom_call" | custom-call | flops 33554432 | bytes 1310720 | tf_op jit(solution)/shard_map/d_right/pallas_call | solution.py:65
  46.5 4.9 %all-to-all-start.3 = ((bf16[16,128,128]{2,1,0:T(8,128)(2,1)}), bf16[16,128,128]{2,1,0:T(8,128)(2,1)S(1)}, u32[]{:S(2)}, u32[]{:S(2)}) async-start(bf16[16,128,128]{2,1,0:T(8,128)(2,1)} %get-tuple-element.42), calls=%async_computation.3 | async-start | bytes 1048576 | tf_op jit(solution)/shard_map/all_to_all | solution.py:319
  52.0 1.5 %collective-permute-start.8 = (bf16[128,128]{1,0:T(8,128)(2,1)S(1)}, bf16[128,128]{1,0:T(8,128)(2,1)S(1)}, u32[]{:S(2)}, u32[]{:S(2)}) collective-permute-start(bf16[128,128]{1,0:T(8,128)(2,1)S(1)} %get-tuple-element.47), channel_id=1, source_target_pairs={{0,6},{1,7},{2,4},{3,5},{4,2},{5,3},{6,0},{7,1},{8,14},{9,15},{10,... | collective-permute-start | bytes 98312 | tf_op jit(solution)/shard_map/ppermute | solution.py:336
  53.4 1.2 %collective-permute-start.9 = (bf16[128,128]{1,0:T(8,128)(2,1)S(1)}, bf16[128,128]{1,0:T(8,128)(2,1)S(1)}, u32[]{:S(2)}, u32[]{:S(2)}) collective-permute-start(bf16[128,128]{1,0:T(8,128)(2,1)S(1)} %get-tuple-element.48), channel_id=1, source_target_pairs={{0,7},{1,6},{2,5},{3,4},{4,3},{5,2},{6,1},{7,0},{8,15},{9,14},{10,... | collective-permute-start | bytes 98312 | tf_op jit(solution)/shard_map/ppermute | solution.py:336
  55.0 1.4 %collective-permute-start.11 = (bf16[128,128]{1,0:T(8,128)(2,1)S(1)}, bf16[128,128]{1,0:T(8,128)(2,1)S(1)}, u32[]{:S(2)}, u32[]{:S(2)}) collective-permute-start(bf16[128,128]{1,0:T(8,128)(2,1)S(1)} %get-tuple-element.50), channel_id=1, source_target_pairs={{0,5},{1,4},{2,7},{3,6},{4,1},{5,0},{6,3},{7,2},{8,13},{9,12},{10,... | collective-permute-start | bytes 98312 | tf_op jit(solution)/shard_map/ppermute | solution.py:336
  56.4 1.5 %collective-permute-start.12 = (bf16[128,128]{1,0:T(8,128)(2,1)S(1)}, bf16[128,128]{1,0:T(8,128)(2,1)S(1)}, u32[]{:S(2)}, u32[]{:S(2)}) collective-permute-start(bf16[128,128]{1,0:T(8,128)(2,1)S(1)} %get-tuple-element.51), channel_id=1, source_target_pairs={{0,2},{1,3},{2,0},{3,1},{4,6},{5,7},{6,4},{7,5},{8,10},{9,11},{10,... | collective-permute-start | bytes 98312 | tf_op jit(solution)/shard_map/ppermute | solution.py:336
  57.9 3.9 %collective-permute-done.8.refs_2_ = bf16[128,128]{1,0:T(8,128)(2,1)S(1)} collective-permute-done((bf16[128,128]{1,0:T(8,128)(2,1)S(1)}, bf16[128,128]{1,0:T(8,128)(2,1)S(1)}, u32[]{:S(2)}, u32[]{:S(2)}) %collective-permute-start.8) | collective-permute-done | bytes 32800 | tf_op jit(solution)/shard_map/ppermute | solution.py:336
  62.1 0.7 copy-done.10
  63.2 1.0 %slopes.1 = (bf16[8,512,128]{2,1,0:T(8,128)(2,1)S(1)}, bf16[8,128,128]{2,1,0:T(8,128)(2,1)S(1)}, f32[8,128]{1,0:T(8,128)S(1)}, f32[128,128]{1,0:T(8,128)S(1)}, bf16[128,640]{1,0:T(8,128)(2,1)S(1)}) custom-call(bf16[8,128,128]{2,1,0:T(8,128)(2,1)S(1)} %copy-done.1, s32[1,128]{1,0:T(1,128)S(1)} %bitcast.15, f32[1,128]{1,0:T(1,128)S(1)} %bitcast.8, ...), custom_call_target="tpu_custom_call" | custom-call | flops 134217728 | bytes 2233856 | tf_op jit(solution)/shard_map/slopes/pallas_call | solution.py:65
  64.2 1.1 %collective-permute-done.13.refs_7_ = bf16[128,128]{1,0:T(8,128)(2,1)S(1)} collective-permute-done((bf16[128,128]{1,0:T(8,128)(2,1)S(1)}, bf16[128,128]{1,0:T(8,128)(2,1)S(1)}, u32[]{:S(2)}, u32[]{:S(2)}) %collective-permute-start.13) | collective-permute-done | bytes 32800 | tf_op jit(solution)/shard_map/ppermute | solution.py:336
  65.4 1.4 %finish.1 = bf16[8,128,128]{2,1,0:T(8,128)(2,1)} custom-call(bf16[16,128,128]{2,1,0:T(8,128)(2,1)S(1)} %all-to-all-done.3.refs_0_, bf16[8,128,128]{2,1,0:T(8,128)(2,1)S(1)} %sort_d_left.1.refs_1_, bf16[8,512,128]{2,1,0:T(8,128)(2,1)S(1)} %get-tuple-element.54.refs_2_, bf16[8,128,128]{2,1,0:T(8,128)(2,1)S(1)} %gate_back.1.refs_6_.refs_3_, ...), custom_call_target="tpu_custom_call" | custom-call | flops 134217728 | bytes 2854912 | tf_op jit(solution)/shard_map/finish/pallas_call | solution.py:65
  (44 shorter events, 4.1 us)
Async XLA Ops:
  2.4 8.6 %copy-start = (bf16[16,128,128]{2,1,0:T(8,128)(2,1)S(1)}, bf16[16,128,128]{2,1,0:T(8,128)(2,1)}, u32[]{:S(2)}) copy-start(bf16[16,128,128]{2,1,0:T(8,128)(2,1)} %project_right.1.refs_5_) | copy-start | bytes 1572868
  2.4 8.6 %copy-start.1 = (bf16[8,128,128]{2,1,0:T(8,128)(2,1)S(1)}, bf16[8,128,128]{2,1,0:T(8,128)(2,1)}, u32[]{:S(2)}) copy-start(bf16[8,128,128]{2,1,0:T(8,128)(2,1)} %refs_0_.7) | copy-start | bytes 786436
  2.4 8.6 %copy-start.2 = (bf16[128,512]{1,0:T(8,128)(2,1)S(1)}, bf16[128,512]{1,0:T(8,128)(2,1)}, u32[]{:S(2)}) copy-start(bf16[128,512]{1,0:T(8,128)(2,1)} %refs_4_.9) | copy-start | bytes 393220
  2.4 8.6 %copy-start.6 = (f32[128]{0:T(128)S(1)}, f32[128]{0:T(128)}, u32[]{:S(2)}) copy-start(f32[128]{0:T(128)} %param.13) | copy-start | bytes 1540
  2.4 8.6 %copy-start.7 = (f32[128]{0:T(128)S(1)}, f32[128]{0:T(128)}, u32[]{:S(2)}) copy-start(f32[128]{0:T(128)} %param.14) | copy-start | bytes 1540
  2.5 22.4 %all-to-all-start = ((bf16[16,128,128]{2,1,0:T(8,128)(2,1)}), bf16[16,128,128]{2,1,0:T(8,128)(2,1)S(1)}, u32[]{:S(2)}, u32[]{:S(2)}) async-start(bf16[16,128,128]{2,1,0:T(8,128)(2,1)} %project_right.1.refs_5_), calls=%async_computation | async-start | bytes 1048576 | tf_op jit(solution)/shard_map/all_to_all | solution.py:319
  11.0 10.3 %copy-start.3 = (bf16[8,128,128]{2,1,0:T(8,128)(2,1)S(1)}, bf16[8,128,128]{2,1,0:T(8,128)(2,1)}, u32[]{:S(2)}) copy-start(bf16[8,128,128]{2,1,0:T(8,128)(2,1)} %refs_1_.1) | copy-start | bytes 786436
  11.1 10.3 %copy-start.4 = (bf16[128,128]{1,0:T(8,128)(2,1)S(1)}, bf16[128,128]{1,0:T(8,128)(2,1)}, u32[]{:S(2)}) copy-start(bf16[128,128]{1,0:T(8,128)(2,1)} %refs_4_.8) | copy-start | bytes 98308
  11.1 10.3 %copy-start.5 = (bf16[128,128]{1,0:T(8,128)(2,1)S(1)}, bf16[128,128]{1,0:T(8,128)(2,1)}, u32[]{:S(2)}) copy-start(bf16[128,128]{1,0:T(8,128)(2,1)} %refs_5_.1) | copy-start | bytes 98308
  11.9 4.6 %collective-permute-start = (bf16[128,128]{1,0:T(8,128)(2,1)S(1)}, bf16[128,128]{1,0:T(8,128)(2,1)S(1)}, u32[]{:S(2)}, u32[]{:S(2)}) collective-permute-start(bf16[128,128]{1,0:T(8,128)(2,1)S(1)} %get-tuple-element.33), channel_id=1, source_target_pairs={{0,1},{1,0},{2,3},{3,2},{4,5},{5,4},{6,7},{7,6},{8,9},{9,8},{10,11... | collective-permute-start | bytes 98312 | tf_op jit(solution)/shard_map/ppermute | solution.py:336
  12.1 9.2 %collective-permute-start.1 = (bf16[128,128]{1,0:T(8,128)(2,1)S(1)}, bf16[128,128]{1,0:T(8,128)(2,1)S(1)}, u32[]{:S(2)}, u32[]{:S(2)}) collective-permute-start(bf16[128,128]{1,0:T(8,128)(2,1)S(1)} %get-tuple-element.34), channel_id=1, source_target_pairs={{0,6},{1,7},{2,4},{3,5},{4,2},{5,3},{6,0},{7,1},{8,14},{9,15},{10,... | collective-permute-start | bytes 98312 | tf_op jit(solution)/shard_map/ppermute | solution.py:336
  12.6 10.2 %collective-permute-start.2 = (bf16[128,128]{1,0:T(8,128)(2,1)S(1)}, bf16[128,128]{1,0:T(8,128)(2,1)S(1)}, u32[]{:S(2)}, u32[]{:S(2)}) collective-permute-start(bf16[128,128]{1,0:T(8,128)(2,1)S(1)} %get-tuple-element.35), channel_id=1, source_target_pairs={{0,7},{1,6},{2,5},{3,4},{4,3},{5,2},{6,1},{7,0},{8,15},{9,14},{10,... | collective-permute-start | bytes 98312 | tf_op jit(solution)/shard_map/ppermute | solution.py:336
  14.7 8.9 %collective-permute-start.3 = (bf16[128,128]{1,0:T(8,128)(2,1)S(1)}, bf16[128,128]{1,0:T(8,128)(2,1)S(1)}, u32[]{:S(2)}, u32[]{:S(2)}) collective-permute-start(bf16[128,128]{1,0:T(8,128)(2,1)S(1)} %get-tuple-element.36), channel_id=1, source_target_pairs={{0,4},{1,5},{2,6},{3,7},{4,0},{5,1},{6,2},{7,3},{8,12},{9,13},{10,... | collective-permute-start | bytes 98312 | tf_op jit(solution)/shard_map/ppermute | solution.py:336
  15.2 8.4 %collective-permute-start.4 = (bf16[128,128]{1,0:T(8,128)(2,1)S(1)}, bf16[128,128]{1,0:T(8,128)(2,1)S(1)}, u32[]{:S(2)}, u32[]{:S(2)}) collective-permute-start(bf16[128,128]{1,0:T(8,128)(2,1)S(1)} %get-tuple-element.37), channel_id=1, source_target_pairs={{0,5},{1,4},{2,7},{3,6},{4,1},{5,0},{6,3},{7,2},{8,13},{9,12},{10,... | collective-permute-start | bytes 98312 | tf_op jit(solution)/shard_map/ppermute | solution.py:336
  16.5 7.1 %collective-permute-start.5 = (bf16[128,128]{1,0:T(8,128)(2,1)S(1)}, bf16[128,128]{1,0:T(8,128)(2,1)S(1)}, u32[]{:S(2)}, u32[]{:S(2)}) collective-permute-start(bf16[128,128]{1,0:T(8,128)(2,1)S(1)} %get-tuple-element.38), channel_id=1, source_target_pairs={{0,2},{1,3},{2,0},{3,1},{4,6},{5,7},{6,4},{7,5},{8,10},{9,11},{10,... | collective-permute-start | bytes 98312 | tf_op jit(solution)/shard_map/ppermute | solution.py:336
  21.3 3.3 %collective-permute-start.6 = (bf16[128,128]{1,0:T(8,128)(2,1)S(1)}, bf16[128,128]{1,0:T(8,128)(2,1)S(1)}, u32[]{:S(2)}, u32[]{:S(2)}) collective-permute-start(bf16[128,128]{1,0:T(8,128)(2,1)S(1)} %get-tuple-element.39), channel_id=1, source_target_pairs={{0,3},{1,2},{2,1},{3,0},{4,7},{5,6},{6,5},{7,4},{8,11},{9,10},{10,... | collective-permute-start | bytes 98312 | tf_op jit(solution)/shard_map/ppermute | solution.py:336
  46.5 18.8 %all-to-all-start.3 = ((bf16[16,128,128]{2,1,0:T(8,128)(2,1)}), bf16[16,128,128]{2,1,0:T(8,128)(2,1)S(1)}, u32[]{:S(2)}, u32[]{:S(2)}) async-start(bf16[16,128,128]{2,1,0:T(8,128)(2,1)} %get-tuple-element.42), calls=%async_computation.3 | async-start | bytes 1048576 | tf_op jit(solution)/shard_map/all_to_all | solution.py:319
  51.7 4.6 %collective-permute-start.7 = (bf16[128,128]{1,0:T(8,128)(2,1)S(1)}, bf16[128,128]{1,0:T(8,128)(2,1)S(1)}, u32[]{:S(2)}, u32[]{:S(2)}) collective-permute-start(bf16[128,128]{1,0:T(8,128)(2,1)S(1)} %get-tuple-element.46), channel_id=1, source_target_pairs={{0,1},{1,0},{2,3},{3,2},{4,5},{5,4},{6,7},{7,6},{8,9},{9,8},{10,11... | collective-permute-start | bytes 98312 | tf_op jit(solution)/shard_map/ppermute | solution.py:336
  52.0 9.8 %collective-permute-start.8 = (bf16[128,128]{1,0:T(8,128)(2,1)S(1)}, bf16[128,128]{1,0:T(8,128)(2,1)S(1)}, u32[]{:S(2)}, u32[]{:S(2)}) collective-permute-start(bf16[128,128]{1,0:T(8,128)(2,1)S(1)} %get-tuple-element.47), channel_id=1, source_target_pairs={{0,6},{1,7},{2,4},{3,5},{4,2},{5,3},{6,0},{7,1},{8,14},{9,15},{10,... | collective-permute-start | bytes 98312 | tf_op jit(solution)/shard_map/ppermute | solution.py:336
  53.4 10.8 %collective-permute-start.9 = (bf16[128,128]{1,0:T(8,128)(2,1)S(1)}, bf16[128,128]{1,0:T(8,128)(2,1)S(1)}, u32[]{:S(2)}, u32[]{:S(2)}) collective-permute-start(bf16[128,128]{1,0:T(8,128)(2,1)S(1)} %get-tuple-element.48), channel_id=1, source_target_pairs={{0,7},{1,6},{2,5},{3,4},{4,3},{5,2},{6,1},{7,0},{8,15},{9,14},{10,... | collective-permute-start | bytes 98312 | tf_op jit(solution)/shard_map/ppermute | solution.py:336
  54.6 9.6 %collective-permute-start.10 = (bf16[128,128]{1,0:T(8,128)(2,1)S(1)}, bf16[128,128]{1,0:T(8,128)(2,1)S(1)}, u32[]{:S(2)}, u32[]{:S(2)}) collective-permute-start(bf16[128,128]{1,0:T(8,128)(2,1)S(1)} %get-tuple-element.49), channel_id=1, source_target_pairs={{0,4},{1,5},{2,6},{3,7},{4,0},{5,1},{6,2},{7,3},{8,12},{9,13},{10,... | collective-permute-start | bytes 98312 | tf_op jit(solution)/shard_map/ppermute | solution.py:336
  55.0 9.3 %collective-permute-start.11 = (bf16[128,128]{1,0:T(8,128)(2,1)S(1)}, bf16[128,128]{1,0:T(8,128)(2,1)S(1)}, u32[]{:S(2)}, u32[]{:S(2)}) collective-permute-start(bf16[128,128]{1,0:T(8,128)(2,1)S(1)} %get-tuple-element.50), channel_id=1, source_target_pairs={{0,5},{1,4},{2,7},{3,6},{4,1},{5,0},{6,3},{7,2},{8,13},{9,12},{10,... | collective-permute-start | bytes 98312 | tf_op jit(solution)/shard_map/ppermute | solution.py:336
  56.4 7.9 %collective-permute-start.12 = (bf16[128,128]{1,0:T(8,128)(2,1)S(1)}, bf16[128,128]{1,0:T(8,128)(2,1)S(1)}, u32[]{:S(2)}, u32[]{:S(2)}) collective-permute-start(bf16[128,128]{1,0:T(8,128)(2,1)S(1)} %get-tuple-element.51), channel_id=1, source_target_pairs={{0,2},{1,3},{2,0},{3,1},{4,6},{5,7},{6,4},{7,5},{8,10},{9,11},{10,... | collective-permute-start | bytes 98312 | tf_op jit(solution)/shard_map/ppermute | solution.py:336
  61.7 3.6 %collective-permute-start.13 = (bf16[128,128]{1,0:T(8,128)(2,1)S(1)}, bf16[128,128]{1,0:T(8,128)(2,1)S(1)}, u32[]{:S(2)}, u32[]{:S(2)}) collective-permute-start(bf16[128,128]{1,0:T(8,128)(2,1)S(1)} %get-tuple-element.52), channel_id=1, source_target_pairs={{0,3},{1,2},{2,1},{3,0},{4,7},{5,6},{6,5},{7,4},{8,11},{9,10},{10,... | collective-permute-start | bytes 98312 | tf_op jit(solution)/shard_map/ppermute | solution.py:336
  (3 other events, 9.9 us)

commit v31 on v16

--- a/solution.py
+++ b/solution.py
@@ -278,10 +278,25 @@
             slopes[row, base + hidden : base + 2 * hidden, :] = masked.astype(slopes.dtype)
 
 
-def sort_d_left_kernel(*refs):
-    *pieces, d_left_panel = refs
+def sloped(d_value, slopes, row, side):
+    hidden = d_value.shape[0]
+    parts = []
+    for base in (2 * side * hidden, (2 * side + 1) * hidden):
+        slope = slopes[row, base : base + hidden, :].astype(F32)
+        parts.append((d_value * slope).astype(BF16))
+    return jnp.concatenate(parts, axis=0)
+
+
+def finish_left_kernel(slopes, d_gate_pre, weights, *refs):
+    *pieces, d_zln_left, panel = refs
+    rows = d_zln_left.shape[0]
     for step, piece in enumerate(pieces):
-        d_left_panel[partner(step, len(pieces))] = piece[...]
+        panel[partner(step, len(pieces))] = piece[...]
+    half = slopes.shape[1] // 2
+    own = jnp.concatenate([weights[:, :half], weights[:, 2 * half :]], axis=1)
+    for row in range(rows):
+        d_proj = sloped(cell_row(panel, row, rows), slopes, row, 0)
+        d_zln_left[row] = dot(own, jnp.concatenate([d_proj, d_gate_pre[row]], axis=0), 1, 0)
 
 
 def both_halves(blocks, count):
@@ -292,21 +307,17 @@
 
 
 def finish_kernel(
-    d_right_panel, d_left_panel, slopes, d_gate_pre, normed_in, inv_in, gain_col, weights, grad
+    d_right_panel, d_zln_left, slopes, normed_in, inv_in, gain_col, weights, grad
 ):
     rows = grad.shape[0]
-    count, depth, width = d_left_panel.shape
-    hidden = count * depth // rows
+    devices, depth, width = d_right_panel.shape
+    half = slopes.shape[1] // 2
     for row in range(rows):
         d_right = cell_row(d_right_panel, row, rows)
-        d_right = both_halves(d_right.reshape(2 * count, depth // rows, width), count)
-        parts = []
-        for side, d_value in enumerate((cell_row(d_left_panel, row, rows), d_right.reshape(hidden, width))):
-            for base in (2 * side * hidden, (2 * side + 1) * hidden):
-                slope = slopes[row, base : base + hidden, :].astype(F32)
-                parts.append((d_value * slope).astype(BF16))
-        parts.append(d_gate_pre[row])
-        d_in = dot(weights[...], jnp.concatenate(parts, axis=0), 1, 0) * gain_col[...]
+        d_right = both_halves(d_right.reshape(devices, depth // rows, width), devices // 2)
+        d_proj = sloped(d_right.reshape(half // 2, width), slopes, row, 1)
+        d_zln = d_zln_left[row] + dot(weights[:, half : 2 * half], d_proj, 1, 0)
+        d_in = d_zln * gain_col[...]
         normed = normed_in[row].astype(F32)
         mean_grad = jnp.mean(d_in, axis=0, keepdims=True)
         mean_cross = jnp.mean(d_in * normed, axis=0, keepdims=True)
@@ -440,7 +451,6 @@
         flops=2 * block * left_rows * width * right_rows,
     )
     d_pieces = swap_pieces(d_pieces)
-    (d_left_panel,) = call(sort_d_left_kernel, "sort_d_left", [panel], d_pieces)
     (d_gate_pre,) = call(
         gate_back_kernel,
         "gate_back",
@@ -464,15 +474,22 @@
         unread=(6,),
         flops=2 * cells * channels * 4 * hidden,
     )
+    (d_zln_left,) = call(
+        finish_left_kernel,
+        "finish_left",
+        [shape((rows, channels, width), F32)],
+        [slopes, d_gate_pre, weights, *d_pieces],
+        scratch=[left_panel],
+        flops=2 * cells * channels * 3 * hidden,
+    )
     (grad,) = call(
         finish_kernel,
         "finish",
         [shape(pair.shape, BF16)],
         [
             d_right_panel,
-            d_left_panel,
+            d_zln_left,
             slopes,
-            d_gate_pre,
             normed_in,
             inv_in,
             gain_col,

time: 62.7 us -> 62.5 us (level)
  no operation moved by 1% of the time
where the time goes in v31:
time: 62.5 us; the launch traced here: 62.1 us
  starting transfers between devices  24.7 us (40%)
  blocking collectives  17.3 us (28%)
  Pallas kernels  9.99 us (16%)
  waiting for transfers between devices  8.51 us (14%)
  local copies, waits for them, and re-layouts  1.34 us (2%)
    all_to_all x2, blocking collectives, swap_half(): lax.all_to_all(values, 'row', split_axis=0, concat_axis=0, tiled=True, ax...  17.3 us
    all_to_all x2, starting transfers between devices, swap(): lax.all_to_all(values, 'row', split_axis=0, concat_axis=0, tiled=True, ax...  13.4 us
    ppermute x14, starting transfers between devices, swap_pieces(): lax.ppermute(pieces[step], 'row', [(d, d ^ distance(step, count)) for d i...  11.3 us
    pallas_call x12, Pallas kernels, call(): pl.pallas_call(body, name=name, out_shape=outs, in_specs=[pl.BlockSpec(me...  9.99 us
    ppermute x14, waiting for transfers between devices, swap_pieces(): lax.ppermute(pieces[step], 'row', [(d, d ^ distance(step, count)) for d i...  8.39 us
    unnamed x22, local copies, waits for them, and re-layouts  1.34 us
  transfers between devices with their start and end apart: 16, of which 10 were waited for; matrix products, arithmetic and copies ran while one was open for 0% of the time, Pallas kernels for 6%

profile of v31, /device:TPU:0, one launch (start us, length us, event | category | flops | bytes accessed | tf_op | source)
XLA Modules:
  0.0 62.1 jit_solution(7944706784561790829)
XLA Ops:
  0.0 2.4 %project_right.1.refs_5_ = bf16[16,128,128]{2,1,0:T(8,128)(2,1)} custom-call(bf16[8,128,128]{2,1,0:T(8,128)(2,1)} %refs_0_.7, s32[1,128]{1,0:T(1,128)} %bitcast.13, f32[1,128]{1,0:T(1,128)} %bitcast.5, f32[1,128]{1,0:T(1,128)} %bitcast.9, bf16[128,512]{1,0:T(8,128)(2,1)} %refs_4_.9), custom_call_target="tpu_custom_call" | custom-call | flops 67108864 | bytes 919040 | tf_op jit(solution)/shard_map/project_right/pallas_call | solution.py:65
  2.5 8.5 %all-to-all-start = ((bf16[16,128,128]{2,1,0:T(8,128)(2,1)}), bf16[16,128,128]{2,1,0:T(8,128)(2,1)S(1)}, u32[]{:S(2)}, u32[]{:S(2)}) async-start(bf16[16,128,128]{2,1,0:T(8,128)(2,1)} %project_right.1.refs_5_), calls=%async_computation | async-start | bytes 1048576 | tf_op jit(solution)/shard_map/all_to_all | solution.py:330
  11.1 0.8 %project_left.1 = (bf16[128,128]{1,0:T(8,128)(2,1)S(1)}, bf16[128,128]{1,0:T(8,128)(2,1)S(1)}, bf16[128,128]{1,0:T(8,128)(2,1)S(1)}, bf16[128,128]{1,0:T(8,128)(...) custom-call(bf16[8,128,128]{2,1,0:T(8,128)(2,1)S(1)} %copy-done.1, ...), custom_call_target="tpu_custom_call" | custom-call | flops 67108864 | bytes 1181184 | tf_op jit(solution)/shard_map/project_left/pallas_call | solution.py:65
  12.7 1.4 %collective-permute-start.2 = (bf16[128,128]{1,0:T(8,128)(2,1)S(1)}, bf16[128,128]{1,0:T(8,128)(2,1)S(1)}, u32[]{:S(2)}, u32[]{:S(2)}) collective-permute-start(bf16[128,128]{1,0:T(8,128)(2,1)S(1)} %get-tuple-element.35), channel_id=1, source_target_pairs={{0,6},{1,7},{2,4},{3,5},{4,2},{5,3},{6,0},{7,1},{8,14},{9,15},{10,... | collective-permute-start | bytes 98312 | tf_op jit(solution)/shard_map/ppermute | solution.py:347
  14.1 0.9 %collective-permute-start.3 = (bf16[128,128]{1,0:T(8,128)(2,1)S(1)}, bf16[128,128]{1,0:T(8,128)(2,1)S(1)}, u32[]{:S(2)}, u32[]{:S(2)}) collective-permute-start(bf16[128,128]{1,0:T(8,128)(2,1)S(1)} %get-tuple-element.36), channel_id=1, source_target_pairs={{0,7},{1,6},{2,5},{3,4},{4,3},{5,2},{6,1},{7,0},{8,15},{9,14},{10,... | collective-permute-start | bytes 98312 | tf_op jit(solution)/shard_map/ppermute | solution.py:347
  15.6 1.5 %collective-permute-start.5 = (bf16[128,128]{1,0:T(8,128)(2,1)S(1)}, bf16[128,128]{1,0:T(8,128)(2,1)S(1)}, u32[]{:S(2)}, u32[]{:S(2)}) collective-permute-start(bf16[128,128]{1,0:T(8,128)(2,1)S(1)} %get-tuple-element.38), channel_id=1, source_target_pairs={{0,5},{1,4},{2,7},{3,6},{4,1},{5,0},{6,3},{7,2},{8,13},{9,12},{10,... | collective-permute-start | bytes 98312 | tf_op jit(solution)/shard_map/ppermute | solution.py:347
  17.1 1.3 %collective-permute-done.1.refs_2_ = bf16[128,128]{1,0:T(8,128)(2,1)S(1)} collective-permute-done((bf16[128,128]{1,0:T(8,128)(2,1)S(1)}, bf16[128,128]{1,0:T(8,128)(2,1)S(1)}, u32[]{:S(2)}, u32[]{:S(2)}) %collective-permute-start.1) | collective-permute-done | bytes 32800 | tf_op jit(solution)/shard_map/ppermute | solution.py:347
  19.1 0.8 %prepare.1 = (f32[8,128,128]{2,1,0:T(8,128)S(1)}, f32[8,128,128]{2,1,0:T(8,128)S(1)}) custom-call(bf16[8,128,128]{2,1,0:T(8,128)(2,1)S(1)} %copy-done.1, bf16[8,128,128]{2,1,0:T(8,128)(2,1)S(1)} %copy-done.3, f32[1,128]{1,0:T(1,128)S(1)} %bitcast.7, f32[1,128]{1,0:T(1,128)S(1)} %bitcast.11, bf16[128,128]{1,0:T(8,128)(2,1)S(1)} %copy-done.5, ...), custom_call_target="tpu_custom_call" | custom-call | flops 67108864 | bytes 1639936 | tf_op jit(solution)/shard_map/prepare/pallas_call | solution.py:65
  19.9 1.5 %collective-permute-done.2.refs_3_ = bf16[128,128]{1,0:T(8,128)(2,1)S(1)} collective-permute-done((bf16[128,128]{1,0:T(8,128)(2,1)S(1)}, bf16[128,128]{1,0:T(8,128)(2,1)S(1)}, u32[]{:S(2)}, u32[]{:S(2)}) %collective-permute-start.2) | collective-permute-done | bytes 32800 | tf_op jit(solution)/shard_map/ppermute | solution.py:347
  21.3 0.7 %collective-permute-done.3.refs_4_ = bf16[128,128]{1,0:T(8,128)(2,1)S(1)} collective-permute-done((bf16[128,128]{1,0:T(8,128)(2,1)S(1)}, bf16[128,128]{1,0:T(8,128)(2,1)S(1)}, u32[]{:S(2)}, u32[]{:S(2)}) %collective-permute-start.3) | collective-permute-done | bytes 32800 | tf_op jit(solution)/shard_map/ppermute | solution.py:347
  22.0 1.5 %collective-permute-done.4.refs_5_ = bf16[128,128]{1,0:T(8,128)(2,1)S(1)} collective-permute-done((bf16[128,128]{1,0:T(8,128)(2,1)S(1)}, bf16[128,128]{1,0:T(8,128)(2,1)S(1)}, u32[]{:S(2)}, u32[]{:S(2)}) %collective-permute-start.4) | collective-permute-done | bytes 32800 | tf_op jit(solution)/shard_map/ppermute | solution.py:347
  23.8 0.6 %tri.1 = (bf16[8,128,128]{2,1,0:T(8,128)(2,1)S(1)}, bf16[16,128,128]{2,1,0:T(8,128)(2,1)S(1)}) custom-call(bf16[16,128,128]{2,1,0:T(8,128)(2,1)S(1)} %all-to-all-done.refs_0_, bf16[16,64,128]{2,1,0:T(8,128)(2,1)S(1)} %sort_left.1.refs_1_, f32[8,128,128]{2,1,0:T(8,128)S(1)} %get-tuple-element.40.refs_2_.refs_1_), custom_call_target="tpu_custom_call" | custom-call | flops 33554432 | bytes 2097152 | tf_op jit(solution)/shard_map/tri/pallas_call | solution.py:65
  24.5 8.7 %all_to_all.20.refs_0_ = bf16[8,128,128]{2,1,0:T(8,128)(2,1)S(1)} all-to-all(bf16[8,128,128]{2,1,0:T(8,128)(2,1)S(1)} %get-tuple-element.41), channel_id=1, replica_groups={{0,1,2,3,4,5,6,7},{8,9,10,11,12,13,14,15},{16,17,18,19,20,21,22,23},{24..., dimensions={0} | all-to-all | bytes 524288 | tf_op jit(solution)/shard_map/all_to_all | solution.py:338
  33.5 8.6 %all_to_all.21.refs_0_ = bf16[8,128,128]{2,1,0:T(8,128)(2,1)S(1)} all-to-all(bf16[8,128,128]{2,1,0:T(8,128)(2,1)S(1)} %middle.1), channel_id=1, replica_groups={{0,1,2,3,4,5,6,7},{8,9,10,11,12,13,14,15},{16,17,18,19,20,21,22,23},{24..., dimensions={0} | all-to-all | bytes 524288 | tf_op jit(solution)/shard_map/all_to_all | solution.py:338
  42.1 1.5 %d_right.1 = (bf16[16,128,128]{2,1,0:T(8,128)(2,1)}, bf16[16,64,128]{2,1,0:T(8,128)(2,1)S(1)}) custom-call(bf16[8,128,128]{2,1,0:T(8,128)(2,1)S(1)} %all_to_all.21.refs_0_, bf16[16,64,128]{2,1,0:T(8,128)(2,1)S(1)} %sort_left.1.refs_1_), custom_call_target="tpu_custom_call" | custom-call | flops 33554432 | bytes 1310720 | tf_op jit(solution)/shard_map/d_right/pallas_call | solution.py:65
  43.5 4.9 %all-to-all-start.3 = ((bf16[16,128,128]{2,1,0:T(8,128)(2,1)}), bf16[16,128,128]{2,1,0:T(8,128)(2,1)S(1)}, u32[]{:S(2)}, u32[]{:S(2)}) async-start(bf16[16,128,128]{2,1,0:T(8,128)(2,1)} %get-tuple-element.42), calls=%async_computation.3 | async-start | bytes 1048576 | tf_op jit(solution)/shard_map/all_to_all | solution.py:330
  49.0 1.5 %collective-permute-start.8 = (bf16[128,128]{1,0:T(8,128)(2,1)S(1)}, bf16[128,128]{1,0:T(8,128)(2,1)S(1)}, u32[]{:S(2)}, u32[]{:S(2)}) collective-permute-start(bf16[128,128]{1,0:T(8,128)(2,1)S(1)} %get-tuple-element.50), channel_id=1, source_target_pairs={{0,2},{1,3},{2,0},{3,1},{4,6},{5,7},{6,4},{7,5},{8,10},{9,11},{10,... | collective-permute-start | bytes 98312 | tf_op jit(solution)/shard_map/ppermute | solution.py:347
  50.8 2.0 %collective-permute-start.10 = (bf16[128,128]{1,0:T(8,128)(2,1)S(1)}, bf16[128,128]{1,0:T(8,128)(2,1)S(1)}, u32[]{:S(2)}, u32[]{:S(2)}) collective-permute-start(bf16[128,128]{1,0:T(8,128)(2,1)S(1)} %get-tuple-element.52), channel_id=1, source_target_pairs={{0,7},{1,6},{2,5},{3,4},{4,3},{5,2},{6,1},{7,0},{8,15},{9,14},{10,... | collective-permute-start | bytes 98312 | tf_op jit(solution)/shard_map/ppermute | solution.py:347
  53.3 1.6 %collective-permute-start.12 = (bf16[128,128]{1,0:T(8,128)(2,1)S(1)}, bf16[128,128]{1,0:T(8,128)(2,1)S(1)}, u32[]{:S(2)}, u32[]{:S(2)}) collective-permute-start(bf16[128,128]{1,0:T(8,128)(2,1)S(1)} %get-tuple-element.54), channel_id=1, source_target_pairs={{0,5},{1,4},{2,7},{3,6},{4,1},{5,0},{6,3},{7,2},{8,13},{9,12},{10,... | collective-permute-start | bytes 98312 | tf_op jit(solution)/shard_map/ppermute | solution.py:347
  54.9 1.2 %collective-permute-done.8.refs_5_ = bf16[128,128]{1,0:T(8,128)(2,1)S(1)} collective-permute-done((bf16[128,128]{1,0:T(8,128)(2,1)S(1)}, bf16[128,128]{1,0:T(8,128)(2,1)S(1)}, u32[]{:S(2)}, u32[]{:S(2)}) %collective-permute-start.8) | collective-permute-done | bytes 32800 | tf_op jit(solution)/shard_map/ppermute | solution.py:347
  56.1 0.7 %copy-done.10 = f32[128]{0:T(128)S(1)} copy-done((f32[128]{0:T(128)S(1)}, f32[128]{0:T(128)}, u32[]{:S(2)}) %copy-start.10) | copy-done | bytes 536
  57.2 1.0 %slopes.1 = (bf16[8,512,128]{2,1,0:T(8,128)(2,1)S(1)}, bf16[8,128,128]{2,1,0:T(8,128)(2,1)S(1)}, f32[8,128]{1,0:T(8,128)S(1)}, f32[128,128]{1,0:T(8,128)S(1)}, bf16[128,640]{1,0:T(8,128)(2,1)S(1)}) custom-call(bf16[8,128,128]{2,1,0:T(8,128)(2,1)S(1)} %copy-done.1, s32[1,128]{1,0:T(1,128)S(1)} %bitcast.15, f32[1,128]{1,0:T(1,128)S(1)} %bitcast.8, ...), custom_call_target="tpu_custom_call" | custom-call | flops 134217728 | bytes 2233856 | tf_op jit(solution)/shard_map/slopes/pallas_call | solution.py:65
  58.8 0.7 %collective-permute-done.10.refs_7_ = bf16[128,128]{1,0:T(8,128)(2,1)S(1)} collective-permute-done((bf16[128,128]{1,0:T(8,128)(2,1)S(1)}, bf16[128,128]{1,0:T(8,128)(2,1)S(1)}, u32[]{:S(2)}, u32[]{:S(2)}) %collective-permute-start.10) | collective-permute-done | bytes 32800 | tf_op jit(solution)/shard_map/ppermute | solution.py:347
  60.9 1.2 %finish.1 = bf16[8,128,128]{2,1,0:T(8,128)(2,1)} custom-call(bf16[16,128,128]{2,1,0:T(8,128)(2,1)S(1)} %all-to-all-done.3.refs_0_, f32[8,128,128]{2,1,0:T(8,128)S(1)} %finish_left.1.refs_1_, bf16[8,512,128]{2,1,0:T(8,128)(2,1)S(1)} %get-tuple-element.44.refs_0_.refs_2_, bf16[8,128,128]{2,1,0:T(8,128)(2,1)S(1)} %get-tuple-element.56.refs_3_, ...), custom_call_target="tpu_custom_call" | custom-call | flops 134217728 | bytes 2854912 | tf_op jit(solution)/shard_map/finish/pallas_call | solution.py:65
  (44 shorter events, 6.3 us)
Async XLA Ops:
  2.4 8.6 %copy-start = (bf16[16,128,128]{2,1,0:T(8,128)(2,1)S(1)}, bf16[16,128,128]{2,1,0:T(8,128)(2,1)}, u32[]{:S(2)}) copy-start(bf16[16,128,128]{2,1,0:T(8,128)(2,1)} %project_right.1.refs_5_) | copy-start | bytes 1572868
  2.4 8.6 %copy-start.1 = (bf16[8,128,128]{2,1,0:T(8,128)(2,1)S(1)}, bf16[8,128,128]{2,1,0:T(8,128)(2,1)}, u32[]{:S(2)}) copy-start(bf16[8,128,128]{2,1,0:T(8,128)(2,1)} %refs_0_.7) | copy-start | bytes 786436
  2.4 8.6 %copy-start.2 = (bf16[128,512]{1,0:T(8,128)(2,1)S(1)}, bf16[128,512]{1,0:T(8,128)(2,1)}, u32[]{:S(2)}) copy-start(bf16[128,512]{1,0:T(8,128)(2,1)} %refs_4_.9) | copy-start | bytes 393220
  2.4 8.6 %copy-start.6 = (f32[128]{0:T(128)S(1)}, f32[128]{0:T(128)}, u32[]{:S(2)}) copy-start(f32[128]{0:T(128)} %param.13) | copy-start | bytes 1540
  2.4 8.6 %copy-start.7 = (f32[128]{0:T(128)S(1)}, f32[128]{0:T(128)}, u32[]{:S(2)}) copy-start(f32[128]{0:T(128)} %param.14) | copy-start | bytes 1540
  2.5 8.6 %copy-start.8 = (s32[128]{0:T(128)S(1)}, s32[128]{0:T(128)}, u32[]{:S(2)}) copy-start(s32[128]{0:T(128)} %param.12) | copy-start | bytes 1540
  2.5 21.3 %all-to-all-start = ((bf16[16,128,128]{2,1,0:T(8,128)(2,1)}), bf16[16,128,128]{2,1,0:T(8,128)(2,1)S(1)}, u32[]{:S(2)}, u32[]{:S(2)}) async-start(bf16[16,128,128]{2,1,0:T(8,128)(2,1)} %project_right.1.refs_5_), calls=%async_computation | async-start | bytes 1048576 | tf_op jit(solution)/shard_map/all_to_all | solution.py:330
  11.0 7.4 %copy-start.3 = (bf16[8,128,128]{2,1,0:T(8,128)(2,1)S(1)}, bf16[8,128,128]{2,1,0:T(8,128)(2,1)}, u32[]{:S(2)}) copy-start(bf16[8,128,128]{2,1,0:T(8,128)(2,1)} %refs_1_.1) | copy-start | bytes 786436
  11.1 7.3 %copy-start.4 = (bf16[128,128]{1,0:T(8,128)(2,1)S(1)}, bf16[128,128]{1,0:T(8,128)(2,1)}, u32[]{:S(2)}) copy-start(bf16[128,128]{1,0:T(8,128)(2,1)} %refs_4_.8) | copy-start | bytes 98308
  11.9 3.7 %collective-permute-start = (bf16[128,128]{1,0:T(8,128)(2,1)S(1)}, bf16[128,128]{1,0:T(8,128)(2,1)S(1)}, u32[]{:S(2)}, u32[]{:S(2)}) collective-permute-start(bf16[128,128]{1,0:T(8,128)(2,1)S(1)} %get-tuple-element.33), channel_id=1, source_target_pairs={{0,1},{1,0},{2,3},{3,2},{4,5},{5,4},{6,7},{7,6},{8,9},{9,8},{10,11... | collective-permute-start | bytes 98312 | tf_op jit(solution)/shard_map/ppermute | solution.py:347
  12.1 6.3 %collective-permute-start.1 = (bf16[128,128]{1,0:T(8,128)(2,1)S(1)}, bf16[128,128]{1,0:T(8,128)(2,1)S(1)}, u32[]{:S(2)}, u32[]{:S(2)}) collective-permute-start(bf16[128,128]{1,0:T(8,128)(2,1)S(1)} %get-tuple-element.34), channel_id=1, source_target_pairs={{0,2},{1,3},{2,0},{3,1},{4,6},{5,7},{6,4},{7,5},{8,10},{9,11},{10,... | collective-permute-start | bytes 98312 | tf_op jit(solution)/shard_map/ppermute | solution.py:347
  12.7 8.6 %collective-permute-start.2 = (bf16[128,128]{1,0:T(8,128)(2,1)S(1)}, bf16[128,128]{1,0:T(8,128)(2,1)S(1)}, u32[]{:S(2)}, u32[]{:S(2)}) collective-permute-start(bf16[128,128]{1,0:T(8,128)(2,1)S(1)} %get-tuple-element.35), channel_id=1, source_target_pairs={{0,6},{1,7},{2,4},{3,5},{4,2},{5,3},{6,0},{7,1},{8,14},{9,15},{10,... | collective-permute-start | bytes 98312 | tf_op jit(solution)/shard_map/ppermute | solution.py:347
  14.1 8.0 %collective-permute-start.3 = (bf16[128,128]{1,0:T(8,128)(2,1)S(1)}, bf16[128,128]{1,0:T(8,128)(2,1)S(1)}, u32[]{:S(2)}, u32[]{:S(2)}) collective-permute-start(bf16[128,128]{1,0:T(8,128)(2,1)S(1)} %get-tuple-element.36), channel_id=1, source_target_pairs={{0,7},{1,6},{2,5},{3,4},{4,3},{5,2},{6,1},{7,0},{8,15},{9,14},{10,... | collective-permute-start | bytes 98312 | tf_op jit(solution)/shard_map/ppermute | solution.py:347
  15.0 8.6 %collective-permute-start.4 = (bf16[128,128]{1,0:T(8,128)(2,1)S(1)}, bf16[128,128]{1,0:T(8,128)(2,1)S(1)}, u32[]{:S(2)}, u32[]{:S(2)}) collective-permute-start(bf16[128,128]{1,0:T(8,128)(2,1)S(1)} %get-tuple-element.37), channel_id=1, source_target_pairs={{0,4},{1,5},{2,6},{3,7},{4,0},{5,1},{6,2},{7,3},{8,12},{9,13},{10,... | collective-permute-start | bytes 98312 | tf_op jit(solution)/shard_map/ppermute | solution.py:347
  15.6 8.0 %collective-permute-start.5 = (bf16[128,128]{1,0:T(8,128)(2,1)S(1)}, bf16[128,128]{1,0:T(8,128)(2,1)S(1)}, u32[]{:S(2)}, u32[]{:S(2)}) collective-permute-start(bf16[128,128]{1,0:T(8,128)(2,1)S(1)} %get-tuple-element.38), channel_id=1, source_target_pairs={{0,5},{1,4},{2,7},{3,6},{4,1},{5,0},{6,3},{7,2},{8,13},{9,12},{10,... | collective-permute-start | bytes 98312 | tf_op jit(solution)/shard_map/ppermute | solution.py:347
  18.4 5.2 %collective-permute-start.6 = (bf16[128,128]{1,0:T(8,128)(2,1)S(1)}, bf16[128,128]{1,0:T(8,128)(2,1)S(1)}, u32[]{:S(2)}, u32[]{:S(2)}) collective-permute-start(bf16[128,128]{1,0:T(8,128)(2,1)S(1)} %get-tuple-element.39), channel_id=1, source_target_pairs={{0,3},{1,2},{2,1},{3,0},{4,7},{5,6},{6,5},{7,4},{8,11},{9,10},{10,... | collective-permute-start | bytes 98312 | tf_op jit(solution)/shard_map/ppermute | solution.py:347
  43.5 17.3 %all-to-all-start.3 = ((bf16[16,128,128]{2,1,0:T(8,128)(2,1)}), bf16[16,128,128]{2,1,0:T(8,128)(2,1)S(1)}, u32[]{:S(2)}, u32[]{:S(2)}) async-start(bf16[16,128,128]{2,1,0:T(8,128)(2,1)} %get-tuple-element.42), calls=%async_computation.3 | async-start | bytes 1048576 | tf_op jit(solution)/shard_map/all_to_all | solution.py:330
  48.8 4.5 %collective-permute-start.7 = (bf16[128,128]{1,0:T(8,128)(2,1)S(1)}, bf16[128,128]{1,0:T(8,128)(2,1)S(1)}, u32[]{:S(2)}, u32[]{:S(2)}) collective-permute-start(bf16[128,128]{1,0:T(8,128)(2,1)S(1)} %get-tuple-element.49), channel_id=1, source_target_pairs={{0,1},{1,0},{2,3},{3,2},{4,5},{5,4},{6,7},{7,6},{8,9},{9,8},{10,11... | collective-permute-start | bytes 98312 | tf_op jit(solution)/shard_map/ppermute | solution.py:347
  49.0 7.1 %collective-permute-start.8 = (bf16[128,128]{1,0:T(8,128)(2,1)S(1)}, bf16[128,128]{1,0:T(8,128)(2,1)S(1)}, u32[]{:S(2)}, u32[]{:S(2)}) collective-permute-start(bf16[128,128]{1,0:T(8,128)(2,1)S(1)} %get-tuple-element.50), channel_id=1, source_target_pairs={{0,2},{1,3},{2,0},{3,1},{4,6},{5,7},{6,4},{7,5},{8,10},{9,11},{10,... | collective-permute-start | bytes 98312 | tf_op jit(solution)/shard_map/ppermute | solution.py:347
  50.5 8.3 %collective-permute-start.9 = (bf16[128,128]{1,0:T(8,128)(2,1)S(1)}, bf16[128,128]{1,0:T(8,128)(2,1)S(1)}, u32[]{:S(2)}, u32[]{:S(2)}) collective-permute-start(bf16[128,128]{1,0:T(8,128)(2,1)S(1)} %get-tuple-element.51), channel_id=1, source_target_pairs={{0,6},{1,7},{2,4},{3,5},{4,2},{5,3},{6,0},{7,1},{8,14},{9,15},{10,... | collective-permute-start | bytes 98312 | tf_op jit(solution)/shard_map/ppermute | solution.py:347
  50.8 8.7 %collective-permute-start.10 = (bf16[128,128]{1,0:T(8,128)(2,1)S(1)}, bf16[128,128]{1,0:T(8,128)(2,1)S(1)}, u32[]{:S(2)}, u32[]{:S(2)}) collective-permute-start(bf16[128,128]{1,0:T(8,128)(2,1)S(1)} %get-tuple-element.52), channel_id=1, source_target_pairs={{0,7},{1,6},{2,5},{3,4},{4,3},{5,2},{6,1},{7,0},{8,15},{9,14},{10,... | collective-permute-start | bytes 98312 | tf_op jit(solution)/shard_map/ppermute | solution.py:347
  52.8 7.2 %collective-permute-start.11 = (bf16[128,128]{1,0:T(8,128)(2,1)S(1)}, bf16[128,128]{1,0:T(8,128)(2,1)S(1)}, u32[]{:S(2)}, u32[]{:S(2)}) collective-permute-start(bf16[128,128]{1,0:T(8,128)(2,1)S(1)} %get-tuple-element.53), channel_id=1, source_target_pairs={{0,4},{1,5},{2,6},{3,7},{4,0},{5,1},{6,2},{7,3},{8,12},{9,13},{10,... | collective-permute-start | bytes 98312 | tf_op jit(solution)/shard_map/ppermute | solution.py:347
  53.3 7.1 %collective-permute-start.12 = (bf16[128,128]{1,0:T(8,128)(2,1)S(1)}, bf16[128,128]{1,0:T(8,128)(2,1)S(1)}, u32[]{:S(2)}, u32[]{:S(2)}) collective-permute-start(bf16[128,128]{1,0:T(8,128)(2,1)S(1)} %get-tuple-element.54), channel_id=1, source_target_pairs={{0,5},{1,4},{2,7},{3,6},{4,1},{5,0},{6,3},{7,2},{8,13},{9,12},{10,... | collective-permute-start | bytes 98312 | tf_op jit(solution)/shard_map/ppermute | solution.py:347
  56.1 4.3 %collective-permute-start.13 = (bf16[128,128]{1,0:T(8,128)(2,1)S(1)}, bf16[128,128]{1,0:T(8,128)(2,1)S(1)}, u32[]{:S(2)}, u32[]{:S(2)}) collective-permute-start(bf16[128,128]{1,0:T(8,128)(2,1)S(1)} %get-tuple-element.55), channel_id=1, source_target_pairs={{0,3},{1,2},{2,1},{3,0},{4,7},{5,6},{6,5},{7,4},{8,11},{9,10},{10,... | collective-permute-start | bytes 98312 | tf_op jit(solution)/shard_map/ppermute | solution.py:347
  (3 other events, 8.7 us)

commit v32 on v27

--- a/solution.py
+++ b/solution.py
@@ -295,10 +295,25 @@
             slopes[row, base + hidden : base + 2 * hidden, :] = masked.astype(slopes.dtype)
 
 
-def sort_d_left_kernel(*refs):
-    *pieces, d_left_panel = refs
+def sloped(d_value, slopes, row, side):
+    hidden = d_value.shape[0]
+    parts = []
+    for base in (2 * side * hidden, (2 * side + 1) * hidden):
+        slope = slopes[row, base : base + hidden, :].astype(F32)
+        parts.append((d_value * slope).astype(BF16))
+    return jnp.concatenate(parts, axis=0)
+
+
+def finish_left_kernel(slopes, d_gate_pre, weights, *refs):
+    *pieces, d_zln_left, panel = refs
+    rows = d_zln_left.shape[0]
     for step, piece in enumerate(pieces):
-        d_left_panel[partner(step, len(pieces))] = piece[...]
+        panel[partner(step, len(pieces))] = piece[...]
+    half = slopes.shape[1] // 2
+    own = jnp.concatenate([weights[:, :half], weights[:, 2 * half :]], axis=1)
+    for row in range(rows):
+        d_proj = sloped(cell_row(panel, row, rows), slopes, row, 0)
+        d_zln_left[row] = dot(own, jnp.concatenate([d_proj, d_gate_pre[row]], axis=0), 1, 0)
 
 
 def both_halves(blocks, count):
@@ -309,21 +324,17 @@
 
 
 def finish_kernel(
-    d_right_panel, d_left_panel, slopes, d_gate_pre, normed_in, inv_in, gain_col, weights, grad
+    d_right_panel, d_zln_left, slopes, normed_in, inv_in, gain_col, weights, grad
 ):
     rows = grad.shape[0]
-    count, depth, width = d_left_panel.shape
-    hidden = count * depth // rows
+    devices, depth, width = d_right_panel.shape
+    half = slopes.shape[1] // 2
     for row in range(rows):
         d_right = cell_row(d_right_panel, row, rows)
-        d_right = both_halves(d_right.reshape(2 * count, depth // rows, width), count)
-        parts = []
-        for side, d_value in enumerate((cell_row(d_left_panel, row, rows), d_right.reshape(hidden, width))):
-            for base in (2 * side * hidden, (2 * side + 1) * hidden):
-                slope = slopes[row, base : base + hidden, :].astype(F32)
-                parts.append((d_value * slope).astype(BF16))
-        parts.append(d_gate_pre[row])
-        d_in = dot(weights[...], jnp.concatenate(parts, axis=0), 1, 0) * gain_col[...]
+        d_right = both_halves(d_right.reshape(devices, depth // rows, width), devices // 2)
+        d_proj = sloped(d_right.reshape(half // 2, width), slopes, row, 1)
+        d_zln = d_zln_left[row] + dot(weights[:, half : 2 * half], d_proj, 1, 0)
+        d_in = d_zln * gain_col[...]
         normed = normed_in[row].astype(F32)
         mean_grad = jnp.mean(d_in, axis=0, keepdims=True)
         mean_cross = jnp.mean(d_in * normed, axis=0, keepdims=True)
@@ -462,7 +473,6 @@
         flops=2 * block * left_rows * width * right_rows,
     )
     d_pieces = swap_pieces(d_pieces)
-    (d_left_panel,) = call(sort_d_left_kernel, "sort_d_left", [panel], d_pieces)
     (d_gate_pre,) = call(
         gate_back_kernel,
         "gate_back",
@@ -486,15 +496,22 @@
         unread=(6,),
         flops=2 * cells * channels * 4 * hidden,
     )
+    (d_zln_left,) = call(
+        finish_left_kernel,
+        "finish_left",
+        [shape((rows, channels, width), F32)],
+        [slopes, d_gate_pre, weights, *d_pieces],
+        scratch=[left_panel],
+        flops=2 * cells * channels * 3 * hidden,
+    )
     (grad,) = call(
         finish_kernel,
         "finish",
         [shape(pair.shape, BF16)],
         [
             d_right_panel,
-            d_left_panel,
+            d_zln_left,
             slopes,
-            d_gate_pre,
             normed_in,
             inv_in,
             gain_col,

time: 62.7 us -> 63.4 us (1.011)
  no operation moved by 1% of the time
where the time goes in v32:
time: 63.4 us; the launch traced here: 62.9 us
  starting transfers between devices  24.7 us (39%)
  blocking collectives  17.5 us (28%)
  Pallas kernels  9.71 us (15%)
  waiting for transfers between devices  8.67 us (14%)
  local copies, waits for them, and re-layouts  2.14 us (3%)
    all_to_all x2, blocking collectives, swap_half(): lax.all_to_all(values, 'row', split_axis=0, concat_axis=0, tiled=True, ax...  17.5 us
    all_to_all x2, starting transfers between devices, swap(): lax.all_to_all(values, 'row', split_axis=0, concat_axis=0, tiled=True, ax...  13.4 us
    ppermute x14, starting transfers between devices, swap_pieces(): lax.ppermute(pieces[step], 'row', [(d, d ^ distance(step, count)) for d i...  11.3 us
    pallas_call x12, Pallas kernels, call(): pl.pallas_call(body, name=name, out_shape=outs, in_specs=[pl.BlockSpec(me...  9.71 us
    ppermute x14, waiting for transfers between devices, swap_pieces(): lax.ppermute(pieces[step], 'row', [(d, d ^ distance(step, count)) for d i...  8.56 us
    unnamed x26, local copies, waits for them, and re-layouts  2.14 us
  transfers between devices with their start and end apart: 16, of which 10 were waited for; matrix products, arithmetic and copies ran while one was open for 0% of the time, Pallas kernels for 6%

profile of v32, /device:TPU:0, one launch (start us, length us, event | category | flops | bytes accessed | tf_op | source)
XLA Modules:
  0.0 62.9 jit_solution(16418157489465368173)
XLA Ops:
  0.0 2.3 %project_right.1.refs_5_ = bf16[16,128,128]{2,1,0:T(8,128)(2,1)} custom-call(bf16[8,128,128]{2,1,0:T(8,128)(2,1)} %refs_0_.7, s32[1,128]{1,0:T(1,128)} %bitcast.13, f32[1,128]{1,0:T(1,128)} %bitcast.5, f32[1,128]{1,0:T(1,128)} %bitcast.9, bf16[128,512]{1,0:T(8,128)(2,1)} %refs_4_.9), custom_call_target="tpu_custom_call" | custom-call | flops 67108864 | bytes 919040 | tf_op jit(solution)/shard_map/project_right/pallas_call | solution.py:72
  2.4 8.5 %all-to-all-start = ((bf16[16,128,128]{2,1,0:T(8,128)(2,1)}), bf16[16,128,128]{2,1,0:T(8,128)(2,1)S(1)}, u32[]{:S(2)}, u32[]{:S(2)}) async-start(bf16[16,128,128]{2,1,0:T(8,128)(2,1)} %project_right.1.refs_5_), calls=%async_computation | async-start | bytes 1048576 | tf_op jit(solution)/shard_map/all_to_all | solution.py:347
  12.5 1.4 %collective-permute-start.2 = (bf16[128,128]{1,0:T(8,128)(2,1)S(1)}, bf16[128,128]{1,0:T(8,128)(2,1)S(1)}, u32[]{:S(2)}, u32[]{:S(2)}) collective-permute-start(bf16[128,128]{1,0:T(8,128)(2,1)S(1)} %get-tuple-element.37), channel_id=1, source_target_pairs={{0,6},{1,7},{2,4},{3,5},{4,2},{5,3},{6,0},{7,1},{8,14},{9,15},{10,... | collective-permute-start | bytes 98312 | tf_op jit(solution)/shard_map/ppermute | solution.py:364
  13.8 0.9 %collective-permute-start.3 = (bf16[128,128]{1,0:T(8,128)(2,1)S(1)}, bf16[128,128]{1,0:T(8,128)(2,1)S(1)}, u32[]{:S(2)}, u32[]{:S(2)}) collective-permute-start(bf16[128,128]{1,0:T(8,128)(2,1)S(1)} %get-tuple-element.38), channel_id=1, source_target_pairs={{0,7},{1,6},{2,5},{3,4},{4,3},{5,2},{6,1},{7,0},{8,15},{9,14},{10,... | collective-permute-start | bytes 98312 | tf_op jit(solution)/shard_map/ppermute | solution.py:364
  15.4 1.5 %collective-permute-start.5 = (bf16[128,128]{1,0:T(8,128)(2,1)S(1)}, bf16[128,128]{1,0:T(8,128)(2,1)S(1)}, u32[]{:S(2)}, u32[]{:S(2)}) collective-permute-start(bf16[128,128]{1,0:T(8,128)(2,1)S(1)} %get-tuple-element.40), channel_id=1, source_target_pairs={{0,5},{1,4},{2,7},{3,6},{4,1},{5,0},{6,3},{7,2},{8,13},{9,12},{10,... | collective-permute-start | bytes 98312 | tf_op jit(solution)/shard_map/ppermute | solution.py:364
  16.9 1.5 %collective-permute-done.1.refs_2_ = bf16[128,128]{1,0:T(8,128)(2,1)S(1)} collective-permute-done((bf16[128,128]{1,0:T(8,128)(2,1)S(1)}, bf16[128,128]{1,0:T(8,128)(2,1)S(1)}, u32[]{:S(2)}, u32[]{:S(2)}) %collective-permute-start.1) | collective-permute-done | bytes 32800 | tf_op jit(solution)/shard_map/ppermute | solution.py:364
  19.0 0.8 %prepare.1 = (f32[8,128,128]{2,1,0:T(8,128)S(1)}, f32[8,128,128]{2,1,0:T(8,128)S(1)}) custom-call(bf16[8,128,128]{2,1,0:T(8,128)(2,1)S(1)} %copy-done.1, bf16[8,128,128]{2,1,0:T(8,128)(2,1)S(1)} %copy-done.5, f32[1,128]{1,0:T(1,128)S(1)} %bitcast.7, f32[1,128]{1,0:T(1,128)S(1)} %bitcast.11, bf16[128,128]{1,0:T(8,128)(2,1)S(1)} %copy-done.7, ...), custom_call_target="tpu_custom_call" | custom-call | flops 67108864 | bytes 1639936 | tf_op jit(solution)/shard_map/prepare/pallas_call | solution.py:72
  19.8 1.5 %collective-permute-done.2.refs_3_ = bf16[128,128]{1,0:T(8,128)(2,1)S(1)} collective-permute-done((bf16[128,128]{1,0:T(8,128)(2,1)S(1)}, bf16[128,128]{1,0:T(8,128)(2,1)S(1)}, u32[]{:S(2)}, u32[]{:S(2)}) %collective-permute-start.2) | collective-permute-done | bytes 32800 | tf_op jit(solution)/shard_map/ppermute | solution.py:364
  21.3 0.7 %collective-permute-done.3.refs_4_ = bf16[128,128]{1,0:T(8,128)(2,1)S(1)} collective-permute-done((bf16[128,128]{1,0:T(8,128)(2,1)S(1)}, bf16[128,128]{1,0:T(8,128)(2,1)S(1)}, u32[]{:S(2)}, u32[]{:S(2)}) %collective-permute-start.3) | collective-permute-done | bytes 32800 | tf_op jit(solution)/shard_map/ppermute | solution.py:364
  22.0 1.5 %collective-permute-done.4.refs_5_ = bf16[128,128]{1,0:T(8,128)(2,1)S(1)} collective-permute-done((bf16[128,128]{1,0:T(8,128)(2,1)S(1)}, bf16[128,128]{1,0:T(8,128)(2,1)S(1)}, u32[]{:S(2)}, u32[]{:S(2)}) %collective-permute-start.4) | collective-permute-done | bytes 32800 | tf_op jit(solution)/shard_map/ppermute | solution.py:364
  23.8 0.8 %copy-done.3 = bf16[8,128,256]{2,1,0:T(8,128)(2,1)} copy-done((bf16[8,128,256]{2,1,0:T(8,128)(2,1)}, bf16[8,128,256]{2,1,0:T(8,128)(2,1)S(1)}, u32[]{:S(2)}) %copy-start.3) | copy-done | bytes 524312
  24.6 0.6 %tri.1 = (bf16[8,128,128]{2,1,0:T(8,128)(2,1)S(1)}, bf16[16,128,128]{2,1,0:T(8,128)(2,1)S(1)}) custom-call(bf16[16,128,128]{2,1,0:T(8,128)(2,1)S(1)} %all-to-all-done.refs_0_, bf16[16,64,128]{2,1,0:T(8,128)(2,1)S(1)} %get-tuple-element.42.refs_1_, f32[8,128,128]{2,1,0:T(8,128)S(1)} %get-tuple-element.43.refs_2_.refs_1_), custom_call_target="tpu_custom_call" | custom-call | flops 33554432 | bytes 2097152 | tf_op jit(solution)/shard_map/tri/pallas_call | solution.py:72
  25.2 8.7 %all_to_all.20.refs_0_ = bf16[8,128,128]{2,1,0:T(8,128)(2,1)S(1)} all-to-all(bf16[8,128,128]{2,1,0:T(8,128)(2,1)S(1)} %get-tuple-element.44), channel_id=1, replica_groups={{0,1,2,3,4,5,6,7},{8,9,10,11,12,13,14,15},{16,17,18,19,20,21,22,23},{24..., dimensions={0} | all-to-all | bytes 524288 | tf_op jit(solution)/shard_map/all_to_all | solution.py:355
  34.2 8.8 %all_to_all.21.refs_0_ = bf16[8,128,128]{2,1,0:T(8,128)(2,1)S(1)} all-to-all(bf16[8,128,128]{2,1,0:T(8,128)(2,1)S(1)} %middle.1), channel_id=1, replica_groups={{0,1,2,3,4,5,6,7},{8,9,10,11,12,13,14,15},{16,17,18,19,20,21,22,23},{24..., dimensions={0} | all-to-all | bytes 524288 | tf_op jit(solution)/shard_map/all_to_all | solution.py:355
  43.0 1.4 %d_right.1 = (bf16[16,128,128]{2,1,0:T(8,128)(2,1)}, bf16[16,64,128]{2,1,0:T(8,128)(2,1)S(1)}) custom-call(bf16[8,128,128]{2,1,0:T(8,128)(2,1)S(1)} %all_to_all.21.refs_0_, bf16[8,128,256]{2,1,0:T(8,128)(2,1)S(1)} %copy-done.4), custom_call_target="tpu_custom_call" | custom-call | flops 33554432 | bytes 1572864 | tf_op jit(solution)/shard_map/d_right/pallas_call | solution.py:72
  44.4 4.9 %all-to-all-start.3 = ((bf16[16,128,128]{2,1,0:T(8,128)(2,1)}), bf16[16,128,128]{2,1,0:T(8,128)(2,1)S(1)}, u32[]{:S(2)}, u32[]{:S(2)}) async-start(bf16[16,128,128]{2,1,0:T(8,128)(2,1)} %get-tuple-element.46), calls=%async_computation.3 | async-start | bytes 1048576 | tf_op jit(solution)/shard_map/all_to_all | solution.py:347
  49.8 1.5 %collective-permute-start.8 = (bf16[128,128]{1,0:T(8,128)(2,1)S(1)}, bf16[128,128]{1,0:T(8,128)(2,1)S(1)}, u32[]{:S(2)}, u32[]{:S(2)}) collective-permute-start(bf16[128,128]{1,0:T(8,128)(2,1)S(1)} %get-tuple-element.54), channel_id=1, source_target_pairs={{0,2},{1,3},{2,0},{3,1},{4,6},{5,7},{6,4},{7,5},{8,10},{9,11},{10,... | collective-permute-start | bytes 98312 | tf_op jit(solution)/shard_map/ppermute | solution.py:364
  51.6 2.0 %collective-permute-start.10 = (bf16[128,128]{1,0:T(8,128)(2,1)S(1)}, bf16[128,128]{1,0:T(8,128)(2,1)S(1)}, u32[]{:S(2)}, u32[]{:S(2)}) collective-permute-start(bf16[128,128]{1,0:T(8,128)(2,1)S(1)} %get-tuple-element.56), channel_id=1, source_target_pairs={{0,7},{1,6},{2,5},{3,4},{4,3},{5,2},{6,1},{7,0},{8,15},{9,14},{10,... | collective-permute-start | bytes 98312 | tf_op jit(solution)/shard_map/ppermute | solution.py:364
  54.1 1.6 %collective-permute-start.12 = (bf16[128,128]{1,0:T(8,128)(2,1)S(1)}, bf16[128,128]{1,0:T(8,128)(2,1)S(1)}, u32[]{:S(2)}, u32[]{:S(2)}) collective-permute-start(bf16[128,128]{1,0:T(8,128)(2,1)S(1)} %get-tuple-element.58), channel_id=1, source_target_pairs={{0,5},{1,4},{2,7},{3,6},{4,1},{5,0},{6,3},{7,2},{8,13},{9,12},{10,... | collective-permute-start | bytes 98312 | tf_op jit(solution)/shard_map/ppermute | solution.py:364
  55.7 1.2 %collective-permute-done.8.refs_5_ = bf16[128,128]{1,0:T(8,128)(2,1)S(1)} collective-permute-done((bf16[128,128]{1,0:T(8,128)(2,1)S(1)}, bf16[128,128]{1,0:T(8,128)(2,1)S(1)}, u32[]{:S(2)}, u32[]{:S(2)}) %collective-permute-start.8) | collective-permute-done | bytes 32800 | tf_op jit(solution)/shard_map/ppermute | solution.py:364
  56.9 0.7 %copy-done.12 = f32[128]{0:T(128)S(1)} copy-done((f32[128]{0:T(128)S(1)}, f32[128]{0:T(128)}, u32[]{:S(2)}) %copy-start.12) | copy-done | bytes 536
  58.0 1.0 %slopes.1 = (bf16[8,512,128]{2,1,0:T(8,128)(2,1)S(1)}, bf16[8,128,128]{2,1,0:T(8,128)(2,1)S(1)}, f32[8,128]{1,0:T(8,128)S(1)}, f32[128,128]{1,0:T(8,128)S(1)}, bf16[128,640]{1,0:T(8,128)(2,1)S(1)}) custom-call(bf16[8,128,128]{2,1,0:T(8,128)(2,1)S(1)} %copy-done.1, s32[1,128]{1,0:T(1,128)S(1)} %bitcast.15, f32[1,128]{1,0:T(1,128)S(1)} %bitcast.8, ...), custom_call_target="tpu_custom_call" | custom-call | flops 134217728 | bytes 2233856 | tf_op jit(solution)/shard_map/slopes/pallas_call | solution.py:72
  59.6 0.7 %collective-permute-done.10.refs_7_ = bf16[128,128]{1,0:T(8,128)(2,1)S(1)} collective-permute-done((bf16[128,128]{1,0:T(8,128)(2,1)S(1)}, bf16[128,128]{1,0:T(8,128)(2,1)S(1)}, u32[]{:S(2)}, u32[]{:S(2)}) %collective-permute-start.10) | collective-permute-done | bytes 32800 | tf_op jit(solution)/shard_map/ppermute | solution.py:364
  61.7 1.2 %finish.1 = bf16[8,128,128]{2,1,0:T(8,128)(2,1)} custom-call(bf16[16,128,128]{2,1,0:T(8,128)(2,1)S(1)} %all-to-all-done.3.refs_0_, f32[8,128,128]{2,1,0:T(8,128)S(1)} %finish_left.1.refs_1_, bf16[8,512,128]{2,1,0:T(8,128)(2,1)S(1)} %get-tuple-element.48.refs_0_.refs_2_, bf16[8,128,128]{2,1,0:T(8,128)(2,1)S(1)} %get-tuple-element.60.refs_3_, ...), custom_call_target="tpu_custom_call" | custom-call | flops 134217728 | bytes 2854912 | tf_op jit(solution)/shard_map/finish/pallas_call | solution.py:72
  (48 shorter events, 7.0 us)
Async XLA Ops:
  2.3 8.6 %copy-start = (bf16[16,128,128]{2,1,0:T(8,128)(2,1)S(1)}, bf16[16,128,128]{2,1,0:T(8,128)(2,1)}, u32[]{:S(2)}) copy-start(bf16[16,128,128]{2,1,0:T(8,128)(2,1)} %project_right.1.refs_5_) | copy-start | bytes 1572868
  2.3 8.6 %copy-start.1 = (bf16[8,128,128]{2,1,0:T(8,128)(2,1)S(1)}, bf16[8,128,128]{2,1,0:T(8,128)(2,1)}, u32[]{:S(2)}) copy-start(bf16[8,128,128]{2,1,0:T(8,128)(2,1)} %refs_0_.7) | copy-start | bytes 786436
  2.3 8.6 %copy-start.2 = (bf16[128,512]{1,0:T(8,128)(2,1)S(1)}, bf16[128,512]{1,0:T(8,128)(2,1)}, u32[]{:S(2)}) copy-start(bf16[128,512]{1,0:T(8,128)(2,1)} %refs_4_.9) | copy-start | bytes 393220
  2.4 8.6 %copy-start.8 = (f32[128]{0:T(128)S(1)}, f32[128]{0:T(128)}, u32[]{:S(2)}) copy-start(f32[128]{0:T(128)} %param.13) | copy-start | bytes 1540
  2.4 8.6 %copy-start.9 = (f32[128]{0:T(128)S(1)}, f32[128]{0:T(128)}, u32[]{:S(2)}) copy-start(f32[128]{0:T(128)} %param.14) | copy-start | bytes 1540
  2.4 8.6 %copy-start.10 = (s32[128]{0:T(128)S(1)}, s32[128]{0:T(128)}, u32[]{:S(2)}) copy-start(s32[128]{0:T(128)} %param.12) | copy-start | bytes 1540
  2.4 22.2 %all-to-all-start = ((bf16[16,128,128]{2,1,0:T(8,128)(2,1)}), bf16[16,128,128]{2,1,0:T(8,128)(2,1)S(1)}, u32[]{:S(2)}, u32[]{:S(2)}) async-start(bf16[16,128,128]{2,1,0:T(8,128)(2,1)} %project_right.1.refs_5_), calls=%async_computation | async-start | bytes 1048576 | tf_op jit(solution)/shard_map/all_to_all | solution.py:347
  11.0 7.4 %copy-start.5 = (bf16[8,128,128]{2,1,0:T(8,128)(2,1)S(1)}, bf16[8,128,128]{2,1,0:T(8,128)(2,1)}, u32[]{:S(2)}) copy-start(bf16[8,128,128]{2,1,0:T(8,128)(2,1)} %refs_1_.1) | copy-start | bytes 786436
  11.6 3.7 %collective-permute-start = (bf16[128,128]{1,0:T(8,128)(2,1)S(1)}, bf16[128,128]{1,0:T(8,128)(2,1)S(1)}, u32[]{:S(2)}, u32[]{:S(2)}) collective-permute-start(bf16[128,128]{1,0:T(8,128)(2,1)S(1)} %get-tuple-element.35), channel_id=1, source_target_pairs={{0,1},{1,0},{2,3},{3,2},{4,5},{5,4},{6,7},{7,6},{8,9},{9,8},{10,11... | collective-permute-start | bytes 98312 | tf_op jit(solution)/shard_map/ppermute | solution.py:364
  11.9 6.5 %collective-permute-start.1 = (bf16[128,128]{1,0:T(8,128)(2,1)S(1)}, bf16[128,128]{1,0:T(8,128)(2,1)S(1)}, u32[]{:S(2)}, u32[]{:S(2)}) collective-permute-start(bf16[128,128]{1,0:T(8,128)(2,1)S(1)} %get-tuple-element.36), channel_id=1, source_target_pairs={{0,2},{1,3},{2,0},{3,1},{4,6},{5,7},{6,4},{7,5},{8,10},{9,11},{10,... | collective-permute-start | bytes 98312 | tf_op jit(solution)/shard_map/ppermute | solution.py:364
  12.5 8.8 %collective-permute-start.2 = (bf16[128,128]{1,0:T(8,128)(2,1)S(1)}, bf16[128,128]{1,0:T(8,128)(2,1)S(1)}, u32[]{:S(2)}, u32[]{:S(2)}) collective-permute-start(bf16[128,128]{1,0:T(8,128)(2,1)S(1)} %get-tuple-element.37), channel_id=1, source_target_pairs={{0,6},{1,7},{2,4},{3,5},{4,2},{5,3},{6,0},{7,1},{8,14},{9,15},{10,... | collective-permute-start | bytes 98312 | tf_op jit(solution)/shard_map/ppermute | solution.py:364
  13.8 8.1 %collective-permute-start.3 = (bf16[128,128]{1,0:T(8,128)(2,1)S(1)}, bf16[128,128]{1,0:T(8,128)(2,1)S(1)}, u32[]{:S(2)}, u32[]{:S(2)}) collective-permute-start(bf16[128,128]{1,0:T(8,128)(2,1)S(1)} %get-tuple-element.38), channel_id=1, source_target_pairs={{0,7},{1,6},{2,5},{3,4},{4,3},{5,2},{6,1},{7,0},{8,15},{9,14},{10,... | collective-permute-start | bytes 98312 | tf_op jit(solution)/shard_map/ppermute | solution.py:364
  14.8 8.7 %collective-permute-start.4 = (bf16[128,128]{1,0:T(8,128)(2,1)S(1)}, bf16[128,128]{1,0:T(8,128)(2,1)S(1)}, u32[]{:S(2)}, u32[]{:S(2)}) collective-permute-start(bf16[128,128]{1,0:T(8,128)(2,1)S(1)} %get-tuple-element.39), channel_id=1, source_target_pairs={{0,4},{1,5},{2,6},{3,7},{4,0},{5,1},{6,2},{7,3},{8,12},{9,13},{10,... | collective-permute-start | bytes 98312 | tf_op jit(solution)/shard_map/ppermute | solution.py:364
  15.4 8.1 %collective-permute-start.5 = (bf16[128,128]{1,0:T(8,128)(2,1)S(1)}, bf16[128,128]{1,0:T(8,128)(2,1)S(1)}, u32[]{:S(2)}, u32[]{:S(2)}) collective-permute-start(bf16[128,128]{1,0:T(8,128)(2,1)S(1)} %get-tuple-element.40), channel_id=1, source_target_pairs={{0,5},{1,4},{2,7},{3,6},{4,1},{5,0},{6,3},{7,2},{8,13},{9,12},{10,... | collective-permute-start | bytes 98312 | tf_op jit(solution)/shard_map/ppermute | solution.py:364
  18.3 5.2 %collective-permute-start.6 = (bf16[128,128]{1,0:T(8,128)(2,1)S(1)}, bf16[128,128]{1,0:T(8,128)(2,1)S(1)}, u32[]{:S(2)}, u32[]{:S(2)}) collective-permute-start(bf16[128,128]{1,0:T(8,128)(2,1)S(1)} %get-tuple-element.41), channel_id=1, source_target_pairs={{0,3},{1,2},{2,1},{3,0},{4,7},{5,6},{6,5},{7,4},{8,11},{9,10},{10,... | collective-permute-start | bytes 98312 | tf_op jit(solution)/shard_map/ppermute | solution.py:364
  34.2 8.8 %copy-start.4 = (bf16[8,128,256]{2,1,0:T(8,128)(2,1)S(1)}, bf16[8,128,256]{2,1,0:T(8,128)(2,1)}, u32[]{:S(2)}) copy-start(bf16[8,128,256]{2,1,0:T(8,128)(2,1)} %copy-done.3) | copy-start | bytes 1572868
  44.4 17.3 %all-to-all-start.3 = ((bf16[16,128,128]{2,1,0:T(8,128)(2,1)}), bf16[16,128,128]{2,1,0:T(8,128)(2,1)S(1)}, u32[]{:S(2)}, u32[]{:S(2)}) async-start(bf16[16,128,128]{2,1,0:T(8,128)(2,1)} %get-tuple-element.46), calls=%async_computation.3 | async-start | bytes 1048576 | tf_op jit(solution)/shard_map/all_to_all | solution.py:347
  49.6 4.5 %collective-permute-start.7 = (bf16[128,128]{1,0:T(8,128)(2,1)S(1)}, bf16[128,128]{1,0:T(8,128)(2,1)S(1)}, u32[]{:S(2)}, u32[]{:S(2)}) collective-permute-start(bf16[128,128]{1,0:T(8,128)(2,1)S(1)} %get-tuple-element.53), channel_id=1, source_target_pairs={{0,1},{1,0},{2,3},{3,2},{4,5},{5,4},{6,7},{7,6},{8,9},{9,8},{10,11... | collective-permute-start | bytes 98312 | tf_op jit(solution)/shard_map/ppermute | solution.py:364
  49.8 7.1 %collective-permute-start.8 = (bf16[128,128]{1,0:T(8,128)(2,1)S(1)}, bf16[128,128]{1,0:T(8,128)(2,1)S(1)}, u32[]{:S(2)}, u32[]{:S(2)}) collective-permute-start(bf16[128,128]{1,0:T(8,128)(2,1)S(1)} %get-tuple-element.54), channel_id=1, source_target_pairs={{0,2},{1,3},{2,0},{3,1},{4,6},{5,7},{6,4},{7,5},{8,10},{9,11},{10,... | collective-permute-start | bytes 98312 | tf_op jit(solution)/shard_map/ppermute | solution.py:364
  51.3 8.3 %collective-permute-start.9 = (bf16[128,128]{1,0:T(8,128)(2,1)S(1)}, bf16[128,128]{1,0:T(8,128)(2,1)S(1)}, u32[]{:S(2)}, u32[]{:S(2)}) collective-permute-start(bf16[128,128]{1,0:T(8,128)(2,1)S(1)} %get-tuple-element.55), channel_id=1, source_target_pairs={{0,6},{1,7},{2,4},{3,5},{4,2},{5,3},{6,0},{7,1},{8,14},{9,15},{10,... | collective-permute-start | bytes 98312 | tf_op jit(solution)/shard_map/ppermute | solution.py:364
  51.6 8.7 %collective-permute-start.10 = (bf16[128,128]{1,0:T(8,128)(2,1)S(1)}, bf16[128,128]{1,0:T(8,128)(2,1)S(1)}, u32[]{:S(2)}, u32[]{:S(2)}) collective-permute-start(bf16[128,128]{1,0:T(8,128)(2,1)S(1)} %get-tuple-element.56), channel_id=1, source_target_pairs={{0,7},{1,6},{2,5},{3,4},{4,3},{5,2},{6,1},{7,0},{8,15},{9,14},{10,... | collective-permute-start | bytes 98312 | tf_op jit(solution)/shard_map/ppermute | solution.py:364
  53.6 7.2 %collective-permute-start.11 = (bf16[128,128]{1,0:T(8,128)(2,1)S(1)}, bf16[128,128]{1,0:T(8,128)(2,1)S(1)}, u32[]{:S(2)}, u32[]{:S(2)}) collective-permute-start(bf16[128,128]{1,0:T(8,128)(2,1)S(1)} %get-tuple-element.57), channel_id=1, source_target_pairs={{0,4},{1,5},{2,6},{3,7},{4,0},{5,1},{6,2},{7,3},{8,12},{9,13},{10,... | collective-permute-start | bytes 98312 | tf_op jit(solution)/shard_map/ppermute | solution.py:364
  54.1 7.1 %collective-permute-start.12 = (bf16[128,128]{1,0:T(8,128)(2,1)S(1)}, bf16[128,128]{1,0:T(8,128)(2,1)S(1)}, u32[]{:S(2)}, u32[]{:S(2)}) collective-permute-start(bf16[128,128]{1,0:T(8,128)(2,1)S(1)} %get-tuple-element.58), channel_id=1, source_target_pairs={{0,5},{1,4},{2,7},{3,6},{4,1},{5,0},{6,3},{7,2},{8,13},{9,12},{10,... | collective-permute-start | bytes 98312 | tf_op jit(solution)/shard_map/ppermute | solution.py:364
  56.9 4.3 %collective-permute-start.13 = (bf16[128,128]{1,0:T(8,128)(2,1)S(1)}, bf16[128,128]{1,0:T(8,128)(2,1)S(1)}, u32[]{:S(2)}, u32[]{:S(2)}) collective-permute-start(bf16[128,128]{1,0:T(8,128)(2,1)S(1)} %get-tuple-element.59), channel_id=1, source_target_pairs={{0,3},{1,2},{2,1},{3,0},{4,7},{5,6},{6,5},{7,4},{8,11},{9,10},{10,... | collective-permute-start | bytes 98312 | tf_op jit(solution)/shard_map/ppermute | solution.py:364
  (5 other events, 16.8 us)

commit v33 on v31

--- a/solution.py
+++ b/solution.py
@@ -39,7 +39,7 @@
 
 
 def call(
-    kernel, name, outs, args, fetched=(), unread=(), scratch=(), flops=0, limit=VMEM_LIMIT
+    kernel, name, outs, args, fetched=(), columns={}, unread=(), scratch=(), flops=0, limit=VMEM_LIMIT
 ):
     moved = sum(a.size * a.dtype.itemsize for a in args) + sum(
         o.size * jnp.dtype(o.dtype).itemsize for o in outs
@@ -51,7 +51,8 @@
         rest = refs[n_args + n_outs :]
         copies = []
         for n, place in enumerate(fetched):
-            copies.append(pltpu.make_async_copy(ins[place], rest[n], rest[n_fetched].at[n]))
+            source = ins[place].at[:, columns[place]] if place in columns else ins[place]
+            copies.append(pltpu.make_async_copy(source, rest[n], rest[n_fetched].at[n]))
             ins[place] = rest[n]
         for copy in copies:
             copy.start()
@@ -59,7 +60,13 @@
             copy.wait()
         kernel(*ins, *refs[n_args : n_args + n_outs], *rest[n_fetched + (n_fetched > 0) :])
 
-    buffers = [pltpu.VMEM(args[place].shape, args[place].dtype) for place in fetched]
+    buffers = [
+        pltpu.VMEM(
+            (*args[place].shape[:-1], columns[place].size) if place in columns else args[place].shape,
+            args[place].dtype,
+        )
+        for place in fetched
+    ]
     if fetched:
         buffers.append(pltpu.SemaphoreType.DMA((n_fetched,)))
     return pl.pallas_call(
@@ -110,10 +117,10 @@
     return lax.rem(lax.axis_index("row"), count) ^ distance(step, count)
 
 
-def gated_rows(pair, mask, gain, bias, w_proj, side):
+def gated_rows(pair, mask, gain, bias, w_side):
     rows = pair.shape[0]
-    hidden = w_proj.shape[1] // 4
-    w_flip = transposed(w_proj[:, 2 * side * hidden : 2 * (side + 1) * hidden])
+    hidden = w_side.shape[1] // 2
+    w_flip = transposed(w_side[...])
     gain_col, bias_col = column(gain[...]), column(bias[...])
     masks = cell_masks(mask, rows)
     for row in range(rows):
@@ -123,25 +130,25 @@
         yield row, masks[row] * sigmoid(proj[:hidden]) * proj[hidden:]
 
 
-def project_right_kernel(pair, mask, gain, bias, w_proj, right_panel):
+def project_right_kernel(pair, mask, gain, bias, w_side, right_panel):
     rows = pair.shape[0]
     devices, depth, width = right_panel.shape
     block = depth // rows
-    count = w_proj.shape[1] // 4 // block
-    for row, right in gated_rows(pair, mask, gain, bias, w_proj, 1):
+    count = w_side.shape[1] // 2 // block
+    for row, right in gated_rows(pair, mask, gain, bias, w_side):
         right = right.reshape(count, block, width).astype(BF16)
         for rank in range(devices):
             place = wide_order(devices, count, False)[rank] % count
             right_panel[rank, row * block : (row + 1) * block, :] = right[place]
 
 
-def project_left_kernel(pair, mask, gain, bias, w_proj, after, *refs):
+def project_left_kernel(pair, mask, gain, bias, w_side, after, *refs):
     del after
     *pieces, left_panel = refs
     rows = pair.shape[0]
     count, depth, width = left_panel.shape
     block = depth // rows
-    for row, left in gated_rows(pair, mask, gain, bias, w_proj, 0):
+    for row, left in gated_rows(pair, mask, gain, bias, w_side):
         left = left.reshape(count, block, width).astype(BF16)
         left_panel[:, row * block : (row + 1) * block, :] = left
     for step, piece in enumerate(pieces):
@@ -385,6 +392,7 @@
         [wide_panel],
         [pair, mask, gain, bias, w_proj],
         fetched=range(5),
+        columns={4: pl.ds(2 * hidden, 2 * hidden)},
         flops=2 * cells * channels * 2 * hidden,
         limit=64 * 1024 * 1024 - 640 * 1024,
     )
@@ -395,6 +403,7 @@
         [piece] * count,
         [pair, mask, gain, bias, w_proj, own_right],
         fetched=range(5),
+        columns={4: pl.ds(0, 2 * hidden)},
         unread=(5,),
         scratch=[left_panel],
         flops=2 * cells * channels * 2 * hidden,

time: 62.5 us -> 62.5 us (level)
  no operation moved by 1% of the time
where the time goes in v33:
time: 62.5 us; the launch traced here: 62 us
  starting transfers between devices  24.7 us (40%)
  blocking collectives  17.3 us (28%)
  Pallas kernels  9.76 us (16%)
  waiting for transfers between devices  8.67 us (14%)
  local copies, waits for them, and re-layouts  1.34 us (2%)
    all_to_all x2, blocking collectives, swap_half(): lax.all_to_all(values, 'row', split_axis=0, concat_axis=0, tiled=True, ax...  17.3 us
    all_to_all x2, starting transfers between devices, swap(): lax.all_to_all(values, 'row', split_axis=0, concat_axis=0, tiled=True, ax...  13.4 us
    ppermute x14, starting transfers between devices, swap_pieces(): lax.ppermute(pieces[step], 'row', [(d, d ^ distance(step, count)) for d i...  11.3 us
    pallas_call x12, Pallas kernels, call(): pl.pallas_call(body, name=name, out_shape=outs, in_specs=[pl.BlockSpec(me...  9.76 us
    ppermute x14, waiting for transfers between devices, swap_pieces(): lax.ppermute(pieces[step], 'row', [(d, d ^ distance(step, count)) for d i...  8.55 us
    unnamed x22, local copies, waits for them, and re-layouts  1.34 us
  transfers between devices with their start and end apart: 16, of which 10 were waited for; matrix products, arithmetic and copies ran while one was open for 0% of the time, Pallas kernels for 6%

profile of v33, /device:TPU:0, one launch (start us, length us, event | category | flops | bytes accessed | tf_op | source)
XLA Modules:
  0.0 62.0 jit_solution(1475097525003893778)
XLA Ops:
  0.0 2.3 %project_right.1.refs_5_ = bf16[16,128,128]{2,1,0:T(8,128)(2,1)} custom-call(bf16[8,128,128]{2,1,0:T(8,128)(2,1)} %refs_0_.7, s32[1,128]{1,0:T(1,128)} %bitcast.13, f32[1,128]{1,0:T(1,128)} %bitcast.5, f32[1,128]{1,0:T(1,128)} %bitcast.9, bf16[128,512]{1,0:T(8,128)(2,1)} %refs_4_.9), custom_call_target="tpu_custom_call" | custom-call | flops 67108864 | bytes 919040 | tf_op jit(solution)/shard_map/project_right/pallas_call | solution.py:72
  2.4 8.5 %all-to-all-start = ((bf16[16,128,128]{2,1,0:T(8,128)(2,1)}), bf16[16,128,128]{2,1,0:T(8,128)(2,1)S(1)}, u32[]{:S(2)}, u32[]{:S(2)}) async-start(bf16[16,128,128]{2,1,0:T(8,128)(2,1)} %project_right.1.refs_5_), calls=%async_computation | async-start | bytes 1048576 | tf_op jit(solution)/shard_map/all_to_all | solution.py:337
  12.5 1.4 %collective-permute-start.2 = (bf16[128,128]{1,0:T(8,128)(2,1)S(1)}, bf16[128,128]{1,0:T(8,128)(2,1)S(1)}, u32[]{:S(2)}, u32[]{:S(2)}) collective-permute-start(bf16[128,128]{1,0:T(8,128)(2,1)S(1)} %get-tuple-element.35), channel_id=1, source_target_pairs={{0,6},{1,7},{2,4},{3,5},{4,2},{5,3},{6,0},{7,1},{8,14},{9,15},{10,... | collective-permute-start | bytes 98312 | tf_op jit(solution)/shard_map/ppermute | solution.py:354
  13.8 0.9 %collective-permute-start.3 = (bf16[128,128]{1,0:T(8,128)(2,1)S(1)}, bf16[128,128]{1,0:T(8,128)(2,1)S(1)}, u32[]{:S(2)}, u32[]{:S(2)}) collective-permute-start(bf16[128,128]{1,0:T(8,128)(2,1)S(1)} %get-tuple-element.36), channel_id=1, source_target_pairs={{0,7},{1,6},{2,5},{3,4},{4,3},{5,2},{6,1},{7,0},{8,15},{9,14},{10,... | collective-permute-start | bytes 98312 | tf_op jit(solution)/shard_map/ppermute | solution.py:354
  15.4 1.5 %collective-permute-start.5 = (bf16[128,128]{1,0:T(8,128)(2,1)S(1)}, bf16[128,128]{1,0:T(8,128)(2,1)S(1)}, u32[]{:S(2)}, u32[]{:S(2)}) collective-permute-start(bf16[128,128]{1,0:T(8,128)(2,1)S(1)} %get-tuple-element.38), channel_id=1, source_target_pairs={{0,5},{1,4},{2,7},{3,6},{4,1},{5,0},{6,3},{7,2},{8,13},{9,12},{10,... | collective-permute-start | bytes 98312 | tf_op jit(solution)/shard_map/ppermute | solution.py:354
  16.9 1.5 %collective-permute-done.1.refs_2_ = bf16[128,128]{1,0:T(8,128)(2,1)S(1)} collective-permute-done((bf16[128,128]{1,0:T(8,128)(2,1)S(1)}, bf16[128,128]{1,0:T(8,128)(2,1)S(1)}, u32[]{:S(2)}, u32[]{:S(2)}) %collective-permute-start.1) | collective-permute-done | bytes 32800 | tf_op jit(solution)/shard_map/ppermute | solution.py:354
  18.4 0.6 %copy-done.9 = f32[128]{0:T(128)S(1)} copy-done((f32[128]{0:T(128)S(1)}, f32[128]{0:T(128)}, u32[]{:S(2)}) %copy-start.9) | copy-done | bytes 536
  19.0 0.8 %prepare.1 = (f32[8,128,128]{2,1,0:T(8,128)S(1)}, f32[8,128,128]{2,1,0:T(8,128)S(1)}) custom-call(bf16[8,128,128]{2,1,0:T(8,128)(2,1)S(1)} %copy-done.1, bf16[8,128,128]{2,1,0:T(8,128)(2,1)S(1)} %copy-done.3, f32[1,128]{1,0:T(1,128)S(1)} %bitcast.7, f32[1,128]{1,0:T(1,128)S(1)} %bitcast.11, bf16[128,128]{1,0:T(8,128)(2,1)S(1)} %copy-done.5, ...), custom_call_target="tpu_custom_call" | custom-call | flops 67108864 | bytes 1639936 | tf_op jit(solution)/shard_map/prepare/pallas_call | solution.py:72
  19.8 1.5 %collective-permute-done.2.refs_3_ = bf16[128,128]{1,0:T(8,128)(2,1)S(1)} collective-permute-done((bf16[128,128]{1,0:T(8,128)(2,1)S(1)}, bf16[128,128]{1,0:T(8,128)(2,1)S(1)}, u32[]{:S(2)}, u32[]{:S(2)}) %collective-permute-start.2) | collective-permute-done | bytes 32800 | tf_op jit(solution)/shard_map/ppermute | solution.py:354
  21.3 0.7 %collective-permute-done.3.refs_4_ = bf16[128,128]{1,0:T(8,128)(2,1)S(1)} collective-permute-done((bf16[128,128]{1,0:T(8,128)(2,1)S(1)}, bf16[128,128]{1,0:T(8,128)(2,1)S(1)}, u32[]{:S(2)}, u32[]{:S(2)}) %collective-permute-start.3) | collective-permute-done | bytes 32800 | tf_op jit(solution)/shard_map/ppermute | solution.py:354
  22.0 1.5 %collective-permute-done.4.refs_5_ = bf16[128,128]{1,0:T(8,128)(2,1)S(1)} collective-permute-done((bf16[128,128]{1,0:T(8,128)(2,1)S(1)}, bf16[128,128]{1,0:T(8,128)(2,1)S(1)}, u32[]{:S(2)}, u32[]{:S(2)}) %collective-permute-start.4) | collective-permute-done | bytes 32800 | tf_op jit(solution)/shard_map/ppermute | solution.py:354
  23.7 0.6 %tri.1 = (bf16[8,128,128]{2,1,0:T(8,128)(2,1)S(1)}, bf16[16,128,128]{2,1,0:T(8,128)(2,1)S(1)}) custom-call(bf16[16,128,128]{2,1,0:T(8,128)(2,1)S(1)} %all-to-all-done.refs_0_, bf16[16,64,128]{2,1,0:T(8,128)(2,1)S(1)} %sort_left.1.refs_1_, f32[8,128,128]{2,1,0:T(8,128)S(1)} %get-tuple-element.40.refs_2_.refs_1_), custom_call_target="tpu_custom_call" | custom-call | flops 33554432 | bytes 2097152 | tf_op jit(solution)/shard_map/tri/pallas_call | solution.py:72
  24.4 8.7 %all_to_all.20.refs_0_ = bf16[8,128,128]{2,1,0:T(8,128)(2,1)S(1)} all-to-all(bf16[8,128,128]{2,1,0:T(8,128)(2,1)S(1)} %get-tuple-element.41), channel_id=1, replica_groups={{0,1,2,3,4,5,6,7},{8,9,10,11,12,13,14,15},{16,17,18,19,20,21,22,23},{24..., dimensions={0} | all-to-all | bytes 524288 | tf_op jit(solution)/shard_map/all_to_all | solution.py:345
  33.4 8.6 %all_to_all.21.refs_0_ = bf16[8,128,128]{2,1,0:T(8,128)(2,1)S(1)} all-to-all(bf16[8,128,128]{2,1,0:T(8,128)(2,1)S(1)} %middle.1), channel_id=1, replica_groups={{0,1,2,3,4,5,6,7},{8,9,10,11,12,13,14,15},{16,17,18,19,20,21,22,23},{24..., dimensions={0} | all-to-all | bytes 524288 | tf_op jit(solution)/shard_map/all_to_all | solution.py:345
  42.0 1.5 %d_right.1 = (bf16[16,128,128]{2,1,0:T(8,128)(2,1)}, bf16[16,64,128]{2,1,0:T(8,128)(2,1)S(1)}) custom-call(bf16[8,128,128]{2,1,0:T(8,128)(2,1)S(1)} %all_to_all.21.refs_0_, bf16[16,64,128]{2,1,0:T(8,128)(2,1)S(1)} %sort_left.1.refs_1_), custom_call_target="tpu_custom_call" | custom-call | flops 33554432 | bytes 1310720 | tf_op jit(solution)/shard_map/d_right/pallas_call | solution.py:72
  43.5 4.9 %all-to-all-start.3 = ((bf16[16,128,128]{2,1,0:T(8,128)(2,1)}), bf16[16,128,128]{2,1,0:T(8,128)(2,1)S(1)}, u32[]{:S(2)}, u32[]{:S(2)}) async-start(bf16[16,128,128]{2,1,0:T(8,128)(2,1)} %get-tuple-element.42), calls=%async_computation.3 | async-start | bytes 1048576 | tf_op jit(solution)/shard_map/all_to_all | solution.py:337
  48.9 1.5 %collective-permute-start.8 = (bf16[128,128]{1,0:T(8,128)(2,1)S(1)}, bf16[128,128]{1,0:T(8,128)(2,1)S(1)}, u32[]{:S(2)}, u32[]{:S(2)}) collective-permute-start(bf16[128,128]{1,0:T(8,128)(2,1)S(1)} %get-tuple-element.50), channel_id=1, source_target_pairs={{0,2},{1,3},{2,0},{3,1},{4,6},{5,7},{6,4},{7,5},{8,10},{9,11},{10,... | collective-permute-start | bytes 98312 | tf_op jit(solution)/shard_map/ppermute | solution.py:354
  50.7 2.0 %collective-permute-start.10 = (bf16[128,128]{1,0:T(8,128)(2,1)S(1)}, bf16[128,128]{1,0:T(8,128)(2,1)S(1)}, u32[]{:S(2)}, u32[]{:S(2)}) collective-permute-start(bf16[128,128]{1,0:T(8,128)(2,1)S(1)} %get-tuple-element.52), channel_id=1, source_target_pairs={{0,7},{1,6},{2,5},{3,4},{4,3},{5,2},{6,1},{7,0},{8,15},{9,14},{10,... | collective-permute-start | bytes 98312 | tf_op jit(solution)/shard_map/ppermute | solution.py:354
  53.2 1.6 %collective-permute-start.12 = (bf16[128,128]{1,0:T(8,128)(2,1)S(1)}, bf16[128,128]{1,0:T(8,128)(2,1)S(1)}, u32[]{:S(2)}, u32[]{:S(2)}) collective-permute-start(bf16[128,128]{1,0:T(8,128)(2,1)S(1)} %get-tuple-element.54), channel_id=1, source_target_pairs={{0,5},{1,4},{2,7},{3,6},{4,1},{5,0},{6,3},{7,2},{8,13},{9,12},{10,... | collective-permute-start | bytes 98312 | tf_op jit(solution)/shard_map/ppermute | solution.py:354
  54.8 1.2 %collective-permute-done.8.refs_5_ = bf16[128,128]{1,0:T(8,128)(2,1)S(1)} collective-permute-done((bf16[128,128]{1,0:T(8,128)(2,1)S(1)}, bf16[128,128]{1,0:T(8,128)(2,1)S(1)}, u32[]{:S(2)}, u32[]{:S(2)}) %collective-permute-start.8) | collective-permute-done | bytes 32800 | tf_op jit(solution)/shard_map/ppermute | solution.py:354
  56.0 0.7 %copy-done.10 = f32[128]{0:T(128)S(1)} copy-done((f32[128]{0:T(128)S(1)}, f32[128]{0:T(128)}, u32[]{:S(2)}) %copy-start.10) | copy-done | bytes 536
  57.1 1.0 %slopes.1 = (bf16[8,512,128]{2,1,0:T(8,128)(2,1)S(1)}, bf16[8,128,128]{2,1,0:T(8,128)(2,1)S(1)}, f32[8,128]{1,0:T(8,128)S(1)}, f32[128,128]{1,0:T(8,128)S(1)}, bf16[128,640]{1,0:T(8,128)(2,1)S(1)}) custom-call(bf16[8,128,128]{2,1,0:T(8,128)(2,1)S(1)} %copy-done.1, s32[1,128]{1,0:T(1,128)S(1)} %bitcast.15, f32[1,128]{1,0:T(1,128)S(1)} %bitcast.8, ...), custom_call_target="tpu_custom_call" | custom-call | flops 134217728 | bytes 2233856 | tf_op jit(solution)/shard_map/slopes/pallas_call | solution.py:72
  58.7 0.7 %collective-permute-done.10.refs_7_ = bf16[128,128]{1,0:T(8,128)(2,1)S(1)} collective-permute-done((bf16[128,128]{1,0:T(8,128)(2,1)S(1)}, bf16[128,128]{1,0:T(8,128)(2,1)S(1)}, u32[]{:S(2)}, u32[]{:S(2)}) %collective-permute-start.10) | collective-permute-done | bytes 32800 | tf_op jit(solution)/shard_map/ppermute | solution.py:354
  60.8 1.2 %finish.1 = bf16[8,128,128]{2,1,0:T(8,128)(2,1)} custom-call(bf16[16,128,128]{2,1,0:T(8,128)(2,1)S(1)} %all-to-all-done.3.refs_0_, f32[8,128,128]{2,1,0:T(8,128)S(1)} %finish_left.1.refs_1_, bf16[8,512,128]{2,1,0:T(8,128)(2,1)S(1)} %get-tuple-element.44.refs_0_.refs_2_, bf16[8,128,128]{2,1,0:T(8,128)(2,1)S(1)} %get-tuple-element.56.refs_3_, ...), custom_call_target="tpu_custom_call" | custom-call | flops 134217728 | bytes 2854912 | tf_op jit(solution)/shard_map/finish/pallas_call | solution.py:72
  (44 shorter events, 6.3 us)
Async XLA Ops:
  2.3 8.6 %copy-start = (bf16[16,128,128]{2,1,0:T(8,128)(2,1)S(1)}, bf16[16,128,128]{2,1,0:T(8,128)(2,1)}, u32[]{:S(2)}) copy-start(bf16[16,128,128]{2,1,0:T(8,128)(2,1)} %project_right.1.refs_5_) | copy-start | bytes 1572868
  2.3 8.6 %copy-start.1 = (bf16[8,128,128]{2,1,0:T(8,128)(2,1)S(1)}, bf16[8,128,128]{2,1,0:T(8,128)(2,1)}, u32[]{:S(2)}) copy-start(bf16[8,128,128]{2,1,0:T(8,128)(2,1)} %refs_0_.7) | copy-start | bytes 786436
  2.4 8.6 %copy-start.2 = (bf16[128,512]{1,0:T(8,128)(2,1)S(1)}, bf16[128,512]{1,0:T(8,128)(2,1)}, u32[]{:S(2)}) copy-start(bf16[128,512]{1,0:T(8,128)(2,1)} %refs_4_.9) | copy-start | bytes 393220
  2.4 8.6 %copy-start.6 = (f32[128]{0:T(128)S(1)}, f32[128]{0:T(128)}, u32[]{:S(2)}) copy-start(f32[128]{0:T(128)} %param.13) | copy-start | bytes 1540
  2.4 8.6 %copy-start.7 = (f32[128]{0:T(128)S(1)}, f32[128]{0:T(128)}, u32[]{:S(2)}) copy-start(f32[128]{0:T(128)} %param.14) | copy-start | bytes 1540
  2.4 8.6 %copy-start.8 = (s32[128]{0:T(128)S(1)}, s32[128]{0:T(128)}, u32[]{:S(2)}) copy-start(s32[128]{0:T(128)} %param.12) | copy-start | bytes 1540
  2.4 21.3 %all-to-all-start = ((bf16[16,128,128]{2,1,0:T(8,128)(2,1)}), bf16[16,128,128]{2,1,0:T(8,128)(2,1)S(1)}, u32[]{:S(2)}, u32[]{:S(2)}) async-start(bf16[16,128,128]{2,1,0:T(8,128)(2,1)} %project_right.1.refs_5_), calls=%async_computation | async-start | bytes 1048576 | tf_op jit(solution)/shard_map/all_to_all | solution.py:337
  11.0 7.4 %copy-start.3 = (bf16[8,128,128]{2,1,0:T(8,128)(2,1)S(1)}, bf16[8,128,128]{2,1,0:T(8,128)(2,1)}, u32[]{:S(2)}) copy-start(bf16[8,128,128]{2,1,0:T(8,128)(2,1)} %refs_1_.1) | copy-start | bytes 786436
  11.0 7.3 %copy-start.4 = (bf16[128,128]{1,0:T(8,128)(2,1)S(1)}, bf16[128,128]{1,0:T(8,128)(2,1)}, u32[]{:S(2)}) copy-start(bf16[128,128]{1,0:T(8,128)(2,1)} %refs_4_.8) | copy-start | bytes 98308
  11.7 3.7 %collective-permute-start = (bf16[128,128]{1,0:T(8,128)(2,1)S(1)}, bf16[128,128]{1,0:T(8,128)(2,1)S(1)}, u32[]{:S(2)}, u32[]{:S(2)}) collective-permute-start(bf16[128,128]{1,0:T(8,128)(2,1)S(1)} %get-tuple-element.33), channel_id=1, source_target_pairs={{0,1},{1,0},{2,3},{3,2},{4,5},{5,4},{6,7},{7,6},{8,9},{9,8},{10,11... | collective-permute-start | bytes 98312 | tf_op jit(solution)/shard_map/ppermute | solution.py:354
  11.9 6.5 %collective-permute-start.1 = (bf16[128,128]{1,0:T(8,128)(2,1)S(1)}, bf16[128,128]{1,0:T(8,128)(2,1)S(1)}, u32[]{:S(2)}, u32[]{:S(2)}) collective-permute-start(bf16[128,128]{1,0:T(8,128)(2,1)S(1)} %get-tuple-element.34), channel_id=1, source_target_pairs={{0,2},{1,3},{2,0},{3,1},{4,6},{5,7},{6,4},{7,5},{8,10},{9,11},{10,... | collective-permute-start | bytes 98312 | tf_op jit(solution)/shard_map/ppermute | solution.py:354
  12.5 8.8 %collective-permute-start.2 = (bf16[128,128]{1,0:T(8,128)(2,1)S(1)}, bf16[128,128]{1,0:T(8,128)(2,1)S(1)}, u32[]{:S(2)}, u32[]{:S(2)}) collective-permute-start(bf16[128,128]{1,0:T(8,128)(2,1)S(1)} %get-tuple-element.35), channel_id=1, source_target_pairs={{0,6},{1,7},{2,4},{3,5},{4,2},{5,3},{6,0},{7,1},{8,14},{9,15},{10,... | collective-permute-start | bytes 98312 | tf_op jit(solution)/shard_map/ppermute | solution.py:354
  13.8 8.1 %collective-permute-start.3 = (bf16[128,128]{1,0:T(8,128)(2,1)S(1)}, bf16[128,128]{1,0:T(8,128)(2,1)S(1)}, u32[]{:S(2)}, u32[]{:S(2)}) collective-permute-start(bf16[128,128]{1,0:T(8,128)(2,1)S(1)} %get-tuple-element.36), channel_id=1, source_target_pairs={{0,7},{1,6},{2,5},{3,4},{4,3},{5,2},{6,1},{7,0},{8,15},{9,14},{10,... | collective-permute-start | bytes 98312 | tf_op jit(solution)/shard_map/ppermute | solution.py:354
  14.8 8.7 %collective-permute-start.4 = (bf16[128,128]{1,0:T(8,128)(2,1)S(1)}, bf16[128,128]{1,0:T(8,128)(2,1)S(1)}, u32[]{:S(2)}, u32[]{:S(2)}) collective-permute-start(bf16[128,128]{1,0:T(8,128)(2,1)S(1)} %get-tuple-element.37), channel_id=1, source_target_pairs={{0,4},{1,5},{2,6},{3,7},{4,0},{5,1},{6,2},{7,3},{8,12},{9,13},{10,... | collective-permute-start | bytes 98312 | tf_op jit(solution)/shard_map/ppermute | solution.py:354
  15.4 8.1 %collective-permute-start.5 = (bf16[128,128]{1,0:T(8,128)(2,1)S(1)}, bf16[128,128]{1,0:T(8,128)(2,1)S(1)}, u32[]{:S(2)}, u32[]{:S(2)}) collective-permute-start(bf16[128,128]{1,0:T(8,128)(2,1)S(1)} %get-tuple-element.38), channel_id=1, source_target_pairs={{0,5},{1,4},{2,7},{3,6},{4,1},{5,0},{6,3},{7,2},{8,13},{9,12},{10,... | collective-permute-start | bytes 98312 | tf_op jit(solution)/shard_map/ppermute | solution.py:354
  18.3 5.2 %collective-permute-start.6 = (bf16[128,128]{1,0:T(8,128)(2,1)S(1)}, bf16[128,128]{1,0:T(8,128)(2,1)S(1)}, u32[]{:S(2)}, u32[]{:S(2)}) collective-permute-start(bf16[128,128]{1,0:T(8,128)(2,1)S(1)} %get-tuple-element.39), channel_id=1, source_target_pairs={{0,3},{1,2},{2,1},{3,0},{4,7},{5,6},{6,5},{7,4},{8,11},{9,10},{10,... | collective-permute-start | bytes 98312 | tf_op jit(solution)/shard_map/ppermute | solution.py:354
  43.5 17.3 %all-to-all-start.3 = ((bf16[16,128,128]{2,1,0:T(8,128)(2,1)}), bf16[16,128,128]{2,1,0:T(8,128)(2,1)S(1)}, u32[]{:S(2)}, u32[]{:S(2)}) async-start(bf16[16,128,128]{2,1,0:T(8,128)(2,1)} %get-tuple-element.42), calls=%async_computation.3 | async-start | bytes 1048576 | tf_op jit(solution)/shard_map/all_to_all | solution.py:337
  48.7 4.5 %collective-permute-start.7 = (bf16[128,128]{1,0:T(8,128)(2,1)S(1)}, bf16[128,128]{1,0:T(8,128)(2,1)S(1)}, u32[]{:S(2)}, u32[]{:S(2)}) collective-permute-start(bf16[128,128]{1,0:T(8,128)(2,1)S(1)} %get-tuple-element.49), channel_id=1, source_target_pairs={{0,1},{1,0},{2,3},{3,2},{4,5},{5,4},{6,7},{7,6},{8,9},{9,8},{10,11... | collective-permute-start | bytes 98312 | tf_op jit(solution)/shard_map/ppermute | solution.py:354
  48.9 7.1 %collective-permute-start.8 = (bf16[128,128]{1,0:T(8,128)(2,1)S(1)}, bf16[128,128]{1,0:T(8,128)(2,1)S(1)}, u32[]{:S(2)}, u32[]{:S(2)}) collective-permute-start(bf16[128,128]{1,0:T(8,128)(2,1)S(1)} %get-tuple-element.50), channel_id=1, source_target_pairs={{0,2},{1,3},{2,0},{3,1},{4,6},{5,7},{6,4},{7,5},{8,10},{9,11},{10,... | collective-permute-start | bytes 98312 | tf_op jit(solution)/shard_map/ppermute | solution.py:354
  50.4 8.3 %collective-permute-start.9 = (bf16[128,128]{1,0:T(8,128)(2,1)S(1)}, bf16[128,128]{1,0:T(8,128)(2,1)S(1)}, u32[]{:S(2)}, u32[]{:S(2)}) collective-permute-start(bf16[128,128]{1,0:T(8,128)(2,1)S(1)} %get-tuple-element.51), channel_id=1, source_target_pairs={{0,6},{1,7},{2,4},{3,5},{4,2},{5,3},{6,0},{7,1},{8,14},{9,15},{10,... | collective-permute-start | bytes 98312 | tf_op jit(solution)/shard_map/ppermute | solution.py:354
  50.7 8.7 %collective-permute-start.10 = (bf16[128,128]{1,0:T(8,128)(2,1)S(1)}, bf16[128,128]{1,0:T(8,128)(2,1)S(1)}, u32[]{:S(2)}, u32[]{:S(2)}) collective-permute-start(bf16[128,128]{1,0:T(8,128)(2,1)S(1)} %get-tuple-element.52), channel_id=1, source_target_pairs={{0,7},{1,6},{2,5},{3,4},{4,3},{5,2},{6,1},{7,0},{8,15},{9,14},{10,... | collective-permute-start | bytes 98312 | tf_op jit(solution)/shard_map/ppermute | solution.py:354
  52.7 7.2 %collective-permute-start.11 = (bf16[128,128]{1,0:T(8,128)(2,1)S(1)}, bf16[128,128]{1,0:T(8,128)(2,1)S(1)}, u32[]{:S(2)}, u32[]{:S(2)}) collective-permute-start(bf16[128,128]{1,0:T(8,128)(2,1)S(1)} %get-tuple-element.53), channel_id=1, source_target_pairs={{0,4},{1,5},{2,6},{3,7},{4,0},{5,1},{6,2},{7,3},{8,12},{9,13},{10,... | collective-permute-start | bytes 98312 | tf_op jit(solution)/shard_map/ppermute | solution.py:354
  53.2 7.1 %collective-permute-start.12 = (bf16[128,128]{1,0:T(8,128)(2,1)S(1)}, bf16[128,128]{1,0:T(8,128)(2,1)S(1)}, u32[]{:S(2)}, u32[]{:S(2)}) collective-permute-start(bf16[128,128]{1,0:T(8,128)(2,1)S(1)} %get-tuple-element.54), channel_id=1, source_target_pairs={{0,5},{1,4},{2,7},{3,6},{4,1},{5,0},{6,3},{7,2},{8,13},{9,12},{10,... | collective-permute-start | bytes 98312 | tf_op jit(solution)/shard_map/ppermute | solution.py:354
  56.0 4.3 %collective-permute-start.13 = (bf16[128,128]{1,0:T(8,128)(2,1)S(1)}, bf16[128,128]{1,0:T(8,128)(2,1)S(1)}, u32[]{:S(2)}, u32[]{:S(2)}) collective-permute-start(bf16[128,128]{1,0:T(8,128)(2,1)S(1)} %get-tuple-element.55), channel_id=1, source_target_pairs={{0,3},{1,2},{2,1},{3,0},{4,7},{5,6},{6,5},{7,4},{8,11},{9,10},{10,... | collective-permute-start | bytes 98312 | tf_op jit(solution)/shard_map/ppermute | solution.py:354
  (3 other events, 8.7 us)

commit v34 on v32

--- a/solution.py
+++ b/solution.py
@@ -183,30 +183,39 @@
 
 
 def sort_left_kernel(*refs):
-    *pieces, left_all, left_pairs, left_wide = refs
-    block, left_rows, _ = left_all.shape
+    *pieces, left_pairs, left_wide = refs
+    pairs, both_rows, both_width = left_pairs.shape
+    left_rows, block = both_rows // 2, 2 * pairs
     depth = pieces[0].shape[0]
     for step, piece in enumerate(pieces):
         start = pl.multiple_of(partner(step, len(pieces)) * depth, depth)
         left_wide[pl.ds(start, depth), :] = piece[...].astype(F32)
-    for h in range(block):
-        left_all[h] = left_wide[pl.ds(h, left_rows, stride=block), :].astype(BF16)
-    empty = jnp.zeros(left_all.shape[1:], BF16)
-    for n in range(block // 2):
-        left_pairs[n, :left_rows, :] = jnp.concatenate([left_all[2 * n], empty], axis=1)
-        left_pairs[n, left_rows:, :] = jnp.concatenate([empty, left_all[2 * n + 1]], axis=1)
-
-
-def tri_kernel(right_panel, left_all, after, products, right_all, left_wide, right_wide):
+    empty = jnp.zeros((left_rows, both_width // 2), BF16)
+    for n in range(pairs):
+        left = [left_wide[pl.ds(h, left_rows, stride=block), :] for h in (2 * n, 2 * n + 1)]
+        left = [value.astype(BF16) for value in left]
+        left_pairs[n, :left_rows, :] = jnp.concatenate([left[0], empty], axis=1)
+        left_pairs[n, left_rows:, :] = jnp.concatenate([empty, left[1]], axis=1)
+
+
+def left_of(left_pairs, h):
+    _, both_rows, both_width = left_pairs.shape
+    rows, width, side = both_rows // 2, both_width // 2, h % 2
+    return left_pairs[
+        h // 2, side * rows : (side + 1) * rows, side * width : (side + 1) * width
+    ]
+
+
+def tri_kernel(right_panel, left_pairs, after, products, right_all, left_wide, right_wide):
     del after
-    block, left_rows, _ = left_all.shape
+    block, left_rows = 2 * left_pairs.shape[0], left_pairs.shape[1] // 2
     right_rows = right_all.shape[1]
     for rank, place in wide_places(right_panel, products.shape[0], False):
         right_wide[place, :] = right_panel[rank].astype(F32)
     for h in range(block):
         right = right_wide[pl.ds(h, right_rows, stride=block), :].astype(BF16)
         right_all[h] = right
-        left_wide[pl.ds(h, left_rows, stride=block), :] = dot(left_all[h], right, 1, 1)
+        left_wide[pl.ds(h, left_rows, stride=block), :] = dot(left_of(left_pairs, h), right, 1, 1)
     products[...] = left_wide[...].astype(BF16).reshape(products.shape)
 
 
@@ -419,13 +428,10 @@
         flops=2 * cells * channels * 2 * hidden,
     )
     pieces = swap_pieces(pieces)
-    left_all, left_pairs = call(
+    (left_pairs,) = call(
         sort_left_kernel,
         "sort_left",
-        [
-            shape((block, left_rows, width), BF16),
-            shape((block // 2, 2 * left_rows, 2 * width), BF16),
-        ],
+        [shape((block // 2, 2 * left_rows, 2 * width), BF16)],
         pieces,
         scratch=[left_wide],
     )
@@ -441,7 +447,7 @@
         tri_kernel,
         "tri",
         [panel, shape((block, right_rows, width), BF16)],
-        [right_panel, left_all, d_hat_centered],
+        [right_panel, left_pairs, d_hat_centered],
         unread=(2,),
         scratch=[left_wide, right_wide],
         flops=2 * block * left_rows * width * right_rows,

time: 63.4 us -> 62.5 us (0.986)
  no operation moved by 1% of the time
where the time goes in v34:
time: 62.5 us; the launch traced here: 62 us
  starting transfers between devices  24.7 us (40%)
  blocking collectives  17.3 us (28%)
  Pallas kernels  9.69 us (16%)
  waiting for transfers between devices  8.35 us (13%)
  local copies, waits for them, and re-layouts  1.64 us (3%)
    all_to_all x2, blocking collectives, swap_half(): lax.all_to_all(values, 'row', split_axis=0, concat_axis=0, tiled=True, ax...  17.3 us
    all_to_all x2, starting transfers between devices, swap(): lax.all_to_all(values, 'row', split_axis=0, concat_axis=0, tiled=True, ax...  13.4 us
    ppermute x14, starting transfers between devices, swap_pieces(): lax.ppermute(pieces[step], 'row', [(d, d ^ distance(step, count)) for d i...  11.3 us
    pallas_call x12, Pallas kernels, call(): pl.pallas_call(body, name=name, out_shape=outs, in_specs=[pl.BlockSpec(me...  9.69 us
    ppermute x14, waiting for transfers between devices, swap_pieces(): lax.ppermute(pieces[step], 'row', [(d, d ^ distance(step, count)) for d i...  8.24 us
    unnamed x26, local copies, waits for them, and re-layouts  1.64 us
  transfers between devices with their start and end apart: 16, of which 10 were waited for; matrix products, arithmetic and copies ran while one was open for 0% of the time, Pallas kernels for 6%

profile of v34, /device:TPU:0, one launch (start us, length us, event | category | flops | bytes accessed | tf_op | source)
XLA Modules:
  0.0 62.0 jit_solution(8998702123052413784)
XLA Ops:
  0.0 2.3 %project_right.1.refs_5_ = bf16[16,128,128]{2,1,0:T(8,128)(2,1)} custom-call(bf16[8,128,128]{2,1,0:T(8,128)(2,1)} %refs_0_.7, s32[1,128]{1,0:T(1,128)} %bitcast.13, f32[1,128]{1,0:T(1,128)} %bitcast.5, f32[1,128]{1,0:T(1,128)} %bitcast.9, bf16[128,512]{1,0:T(8,128)(2,1)} %refs_4_.9), custom_call_target="tpu_custom_call" | custom-call | flops 67108864 | bytes 919040 | tf_op jit(solution)/shard_map/project_right/pallas_call | solution.py:72
  2.4 8.5 %all-to-all-start = ((bf16[16,128,128]{2,1,0:T(8,128)(2,1)}), bf16[16,128,128]{2,1,0:T(8,128)(2,1)S(1)}, u32[]{:S(2)}, u32[]{:S(2)}) async-start(bf16[16,128,128]{2,1,0:T(8,128)(2,1)} %project_right.1.refs_5_), calls=%async_computation | async-start | bytes 1048576 | tf_op jit(solution)/shard_map/all_to_all | solution.py:356
  12.5 1.4 %collective-permute-start.2 = (bf16[128,128]{1,0:T(8,128)(2,1)S(1)}, bf16[128,128]{1,0:T(8,128)(2,1)S(1)}, u32[]{:S(2)}, u32[]{:S(2)}) collective-permute-start(bf16[128,128]{1,0:T(8,128)(2,1)S(1)} %get-tuple-element.35), channel_id=1, source_target_pairs={{0,6},{1,7},{2,4},{3,5},{4,2},{5,3},{6,0},{7,1},{8,14},{9,15},{10,... | collective-permute-start | bytes 98312 | tf_op jit(solution)/shard_map/ppermute | solution.py:373
  13.9 0.9 %collective-permute-start.3 = (bf16[128,128]{1,0:T(8,128)(2,1)S(1)}, bf16[128,128]{1,0:T(8,128)(2,1)S(1)}, u32[]{:S(2)}, u32[]{:S(2)}) collective-permute-start(bf16[128,128]{1,0:T(8,128)(2,1)S(1)} %get-tuple-element.36), channel_id=1, source_target_pairs={{0,7},{1,6},{2,5},{3,4},{4,3},{5,2},{6,1},{7,0},{8,15},{9,14},{10,... | collective-permute-start | bytes 98312 | tf_op jit(solution)/shard_map/ppermute | solution.py:373
  15.4 1.5 %collective-permute-start.5 = (bf16[128,128]{1,0:T(8,128)(2,1)S(1)}, bf16[128,128]{1,0:T(8,128)(2,1)S(1)}, u32[]{:S(2)}, u32[]{:S(2)}) collective-permute-start(bf16[128,128]{1,0:T(8,128)(2,1)S(1)} %get-tuple-element.38), channel_id=1, source_target_pairs={{0,5},{1,4},{2,7},{3,6},{4,1},{5,0},{6,3},{7,2},{8,13},{9,12},{10,... | collective-permute-start | bytes 98312 | tf_op jit(solution)/shard_map/ppermute | solution.py:373
  16.9 1.5 %collective-permute-done.1.refs_2_ = bf16[128,128]{1,0:T(8,128)(2,1)S(1)} collective-permute-done((bf16[128,128]{1,0:T(8,128)(2,1)S(1)}, bf16[128,128]{1,0:T(8,128)(2,1)S(1)}, u32[]{:S(2)}, u32[]{:S(2)}) %collective-permute-start.1) | collective-permute-done | bytes 32800 | tf_op jit(solution)/shard_map/ppermute | solution.py:373
  18.4 0.6 %copy-done.11 = f32[128]{0:T(128)S(1)} copy-done((f32[128]{0:T(128)S(1)}, f32[128]{0:T(128)}, u32[]{:S(2)}) %copy-start.11) | copy-done | bytes 536
  19.0 0.8 %prepare.1 = (f32[8,128,128]{2,1,0:T(8,128)S(1)}, f32[8,128,128]{2,1,0:T(8,128)S(1)}) custom-call(bf16[8,128,128]{2,1,0:T(8,128)(2,1)S(1)} %copy-done.1, bf16[8,128,128]{2,1,0:T(8,128)(2,1)S(1)} %copy-done.3, f32[1,128]{1,0:T(1,128)S(1)} %bitcast.7, f32[1,128]{1,0:T(1,128)S(1)} %bitcast.11, bf16[128,128]{1,0:T(8,128)(2,1)S(1)} %copy-done.6, ...), custom_call_target="tpu_custom_call" | custom-call | flops 67108864 | bytes 1639936 | tf_op jit(solution)/shard_map/prepare/pallas_call | solution.py:72
  19.8 1.5 %collective-permute-done.2.refs_3_ = bf16[128,128]{1,0:T(8,128)(2,1)S(1)} collective-permute-done((bf16[128,128]{1,0:T(8,128)(2,1)S(1)}, bf16[128,128]{1,0:T(8,128)(2,1)S(1)}, u32[]{:S(2)}, u32[]{:S(2)}) %collective-permute-start.2) | collective-permute-done | bytes 32800 | tf_op jit(solution)/shard_map/ppermute | solution.py:373
  21.3 0.7 %collective-permute-done.3.refs_4_ = bf16[128,128]{1,0:T(8,128)(2,1)S(1)} collective-permute-done((bf16[128,128]{1,0:T(8,128)(2,1)S(1)}, bf16[128,128]{1,0:T(8,128)(2,1)S(1)}, u32[]{:S(2)}, u32[]{:S(2)}) %collective-permute-start.3) | collective-permute-done | bytes 32800 | tf_op jit(solution)/shard_map/ppermute | solution.py:373
  22.0 1.5 %collective-permute-done.4.refs_5_ = bf16[128,128]{1,0:T(8,128)(2,1)S(1)} collective-permute-done((bf16[128,128]{1,0:T(8,128)(2,1)S(1)}, bf16[128,128]{1,0:T(8,128)(2,1)S(1)}, u32[]{:S(2)}, u32[]{:S(2)}) %collective-permute-start.4) | collective-permute-done | bytes 32800 | tf_op jit(solution)/shard_map/ppermute | solution.py:373
  23.7 0.6 %tri.1 = (bf16[8,128,128]{2,1,0:T(8,128)(2,1)S(1)}, bf16[16,128,128]{2,1,0:T(8,128)(2,1)S(1)}) custom-call(bf16[16,128,128]{2,1,0:T(8,128)(2,1)S(1)} %all-to-all-done.refs_0_, bf16[8,128,256]{2,1,0:T(8,128)(2,1)S(1)} %sort_left.1.refs_1_, f32[8,128,128]{2,1,0:T(8,128)S(1)} %get-tuple-element.40.refs_2_.refs_1_), custom_call_target="tpu_custom_call" | custom-call | flops 33554432 | bytes 2359296 | tf_op jit(solution)/shard_map/tri/pallas_call | solution.py:72
  24.4 8.7 %all_to_all.20.refs_0_ = bf16[8,128,128]{2,1,0:T(8,128)(2,1)S(1)} all-to-all(bf16[8,128,128]{2,1,0:T(8,128)(2,1)S(1)} %get-tuple-element.41), channel_id=1, replica_groups={{0,1,2,3,4,5,6,7},{8,9,10,11,12,13,14,15},{16,17,18,19,20,21,22,23},{24..., dimensions={0} | all-to-all | bytes 524288 | tf_op jit(solution)/shard_map/all_to_all | solution.py:364
  33.4 8.6 %all_to_all.21.refs_0_ = bf16[8,128,128]{2,1,0:T(8,128)(2,1)S(1)} all-to-all(bf16[8,128,128]{2,1,0:T(8,128)(2,1)S(1)} %middle.1), channel_id=1, replica_groups={{0,1,2,3,4,5,6,7},{8,9,10,11,12,13,14,15},{16,17,18,19,20,21,22,23},{24..., dimensions={0} | all-to-all | bytes 524288 | tf_op jit(solution)/shard_map/all_to_all | solution.py:364
  42.0 1.4 %d_right.1 = (bf16[16,128,128]{2,1,0:T(8,128)(2,1)}, bf16[16,64,128]{2,1,0:T(8,128)(2,1)S(1)}) custom-call(bf16[8,128,128]{2,1,0:T(8,128)(2,1)S(1)} %all_to_all.21.refs_0_, bf16[8,128,256]{2,1,0:T(8,128)(2,1)S(1)} %sort_left.1.refs_1_), custom_call_target="tpu_custom_call" | custom-call | flops 33554432 | bytes 1572864 | tf_op jit(solution)/shard_map/d_right/pallas_call | solution.py:72
  43.4 4.9 %all-to-all-start.3 = ((bf16[16,128,128]{2,1,0:T(8,128)(2,1)}), bf16[16,128,128]{2,1,0:T(8,128)(2,1)S(1)}, u32[]{:S(2)}, u32[]{:S(2)}) async-start(bf16[16,128,128]{2,1,0:T(8,128)(2,1)} %get-tuple-element.42), calls=%async_computation.3 | async-start | bytes 1048576 | tf_op jit(solution)/shard_map/all_to_all | solution.py:356
  48.8 1.5 %collective-permute-start.8 = (bf16[128,128]{1,0:T(8,128)(2,1)S(1)}, bf16[128,128]{1,0:T(8,128)(2,1)S(1)}, u32[]{:S(2)}, u32[]{:S(2)}) collective-permute-start(bf16[128,128]{1,0:T(8,128)(2,1)S(1)} %get-tuple-element.50), channel_id=1, source_target_pairs={{0,2},{1,3},{2,0},{3,1},{4,6},{5,7},{6,4},{7,5},{8,10},{9,11},{10,... | collective-permute-start | bytes 98312 | tf_op jit(solution)/shard_map/ppermute | solution.py:373
  50.6 2.0 %collective-permute-start.10 = (bf16[128,128]{1,0:T(8,128)(2,1)S(1)}, bf16[128,128]{1,0:T(8,128)(2,1)S(1)}, u32[]{:S(2)}, u32[]{:S(2)}) collective-permute-start(bf16[128,128]{1,0:T(8,128)(2,1)S(1)} %get-tuple-element.52), channel_id=1, source_target_pairs={{0,7},{1,6},{2,5},{3,4},{4,3},{5,2},{6,1},{7,0},{8,15},{9,14},{10,... | collective-permute-start | bytes 98312 | tf_op jit(solution)/shard_map/ppermute | solution.py:373
  53.2 1.6 %collective-permute-start.12 = (bf16[128,128]{1,0:T(8,128)(2,1)S(1)}, bf16[128,128]{1,0:T(8,128)(2,1)S(1)}, u32[]{:S(2)}, u32[]{:S(2)}) collective-permute-start(bf16[128,128]{1,0:T(8,128)(2,1)S(1)} %get-tuple-element.54), channel_id=1, source_target_pairs={{0,5},{1,4},{2,7},{3,6},{4,1},{5,0},{6,3},{7,2},{8,13},{9,12},{10,... | collective-permute-start | bytes 98312 | tf_op jit(solution)/shard_map/ppermute | solution.py:373
  54.7 1.2 %collective-permute-done.8.refs_5_ = bf16[128,128]{1,0:T(8,128)(2,1)S(1)} collective-permute-done((bf16[128,128]{1,0:T(8,128)(2,1)S(1)}, bf16[128,128]{1,0:T(8,128)(2,1)S(1)}, u32[]{:S(2)}, u32[]{:S(2)}) %collective-permute-start.8) | collective-permute-done | bytes 32800 | tf_op jit(solution)/shard_map/ppermute | solution.py:373
  55.9 0.6 %copy-done.12 = f32[128]{0:T(128)S(1)} copy-done((f32[128]{0:T(128)S(1)}, f32[128]{0:T(128)}, u32[]{:S(2)}) %copy-start.12) | copy-done | bytes 536
  57.3 1.0 %slopes.1 = (bf16[8,512,128]{2,1,0:T(8,128)(2,1)S(1)}, bf16[8,128,128]{2,1,0:T(8,128)(2,1)S(1)}, f32[8,128]{1,0:T(8,128)S(1)}, f32[128,128]{1,0:T(8,128)S(1)}, bf16[128,640]{1,0:T(8,128)(2,1)S(1)}) custom-call(bf16[8,128,128]{2,1,0:T(8,128)(2,1)S(1)} %copy-done.1, s32[1,128]{1,0:T(1,128)S(1)} %bitcast.15, f32[1,128]{1,0:T(1,128)S(1)} %bitcast.8, ...), custom_call_target="tpu_custom_call" | custom-call | flops 134217728 | bytes 2233856 | tf_op jit(solution)/shard_map/slopes/pallas_call | solution.py:72
  58.6 0.7 %collective-permute-done.10.refs_7_ = bf16[128,128]{1,0:T(8,128)(2,1)S(1)} collective-permute-done((bf16[128,128]{1,0:T(8,128)(2,1)S(1)}, bf16[128,128]{1,0:T(8,128)(2,1)S(1)}, u32[]{:S(2)}, u32[]{:S(2)}) %collective-permute-start.10) | collective-permute-done | bytes 32800 | tf_op jit(solution)/shard_map/ppermute | solution.py:373
  60.7 1.2 %finish.1 = bf16[8,128,128]{2,1,0:T(8,128)(2,1)} custom-call(bf16[16,128,128]{2,1,0:T(8,128)(2,1)S(1)} %all-to-all-done.3.refs_0_, f32[8,128,128]{2,1,0:T(8,128)S(1)} %finish_left.1.refs_1_, bf16[8,512,128]{2,1,0:T(8,128)(2,1)S(1)} %get-tuple-element.44.refs_0_.refs_2_, bf16[8,128,128]{2,1,0:T(8,128)(2,1)S(1)} %get-tuple-element.56.refs_3_, ...), custom_call_target="tpu_custom_call" | custom-call | flops 134217728 | bytes 2854912 | tf_op jit(solution)/shard_map/finish/pallas_call | solution.py:72
  (48 shorter events, 6.4 us)
Async XLA Ops:
  2.3 8.6 %copy-start = (bf16[16,128,128]{2,1,0:T(8,128)(2,1)S(1)}, bf16[16,128,128]{2,1,0:T(8,128)(2,1)}, u32[]{:S(2)}) copy-start(bf16[16,128,128]{2,1,0:T(8,128)(2,1)} %project_right.1.refs_5_) | copy-start | bytes 1572868
  2.3 8.6 %copy-start.1 = (bf16[8,128,128]{2,1,0:T(8,128)(2,1)S(1)}, bf16[8,128,128]{2,1,0:T(8,128)(2,1)}, u32[]{:S(2)}) copy-start(bf16[8,128,128]{2,1,0:T(8,128)(2,1)} %refs_0_.7) | copy-start | bytes 786436
  2.4 8.6 %copy-start.2 = (bf16[128,512]{1,0:T(8,128)(2,1)S(1)}, bf16[128,512]{1,0:T(8,128)(2,1)}, u32[]{:S(2)}) copy-start(bf16[128,512]{1,0:T(8,128)(2,1)} %refs_4_.9) | copy-start | bytes 393220
  2.4 8.6 %copy-start.8 = (f32[128]{0:T(128)S(1)}, f32[128]{0:T(128)}, u32[]{:S(2)}) copy-start(f32[128]{0:T(128)} %param.13) | copy-start | bytes 1540
  2.4 8.6 %copy-start.9 = (f32[128]{0:T(128)S(1)}, f32[128]{0:T(128)}, u32[]{:S(2)}) copy-start(f32[128]{0:T(128)} %param.14) | copy-start | bytes 1540
  2.4 8.6 %copy-start.10 = (s32[128]{0:T(128)S(1)}, s32[128]{0:T(128)}, u32[]{:S(2)}) copy-start(s32[128]{0:T(128)} %param.12) | copy-start | bytes 1540
  2.4 21.3 %all-to-all-start = ((bf16[16,128,128]{2,1,0:T(8,128)(2,1)}), bf16[16,128,128]{2,1,0:T(8,128)(2,1)S(1)}, u32[]{:S(2)}, u32[]{:S(2)}) async-start(bf16[16,128,128]{2,1,0:T(8,128)(2,1)} %project_right.1.refs_5_), calls=%async_computation | async-start | bytes 1048576 | tf_op jit(solution)/shard_map/all_to_all | solution.py:356
  11.0 7.4 %copy-start.3 = (bf16[8,128,128]{2,1,0:T(8,128)(2,1)S(1)}, bf16[8,128,128]{2,1,0:T(8,128)(2,1)}, u32[]{:S(2)}) copy-start(bf16[8,128,128]{2,1,0:T(8,128)(2,1)} %refs_1_.1) | copy-start | bytes 786436
  11.7 3.7 %collective-permute-start = (bf16[128,128]{1,0:T(8,128)(2,1)S(1)}, bf16[128,128]{1,0:T(8,128)(2,1)S(1)}, u32[]{:S(2)}, u32[]{:S(2)}) collective-permute-start(bf16[128,128]{1,0:T(8,128)(2,1)S(1)} %get-tuple-element.33), channel_id=1, source_target_pairs={{0,1},{1,0},{2,3},{3,2},{4,5},{5,4},{6,7},{7,6},{8,9},{9,8},{10,11... | collective-permute-start | bytes 98312 | tf_op jit(solution)/shard_map/ppermute | solution.py:373
  11.9 6.5 %collective-permute-start.1 = (bf16[128,128]{1,0:T(8,128)(2,1)S(1)}, bf16[128,128]{1,0:T(8,128)(2,1)S(1)}, u32[]{:S(2)}, u32[]{:S(2)}) collective-permute-start(bf16[128,128]{1,0:T(8,128)(2,1)S(1)} %get-tuple-element.34), channel_id=1, source_target_pairs={{0,2},{1,3},{2,0},{3,1},{4,6},{5,7},{6,4},{7,5},{8,10},{9,11},{10,... | collective-permute-start | bytes 98312 | tf_op jit(solution)/shard_map/ppermute | solution.py:373
  12.5 8.8 %collective-permute-start.2 = (bf16[128,128]{1,0:T(8,128)(2,1)S(1)}, bf16[128,128]{1,0:T(8,128)(2,1)S(1)}, u32[]{:S(2)}, u32[]{:S(2)}) collective-permute-start(bf16[128,128]{1,0:T(8,128)(2,1)S(1)} %get-tuple-element.35), channel_id=1, source_target_pairs={{0,6},{1,7},{2,4},{3,5},{4,2},{5,3},{6,0},{7,1},{8,14},{9,15},{10,... | collective-permute-start | bytes 98312 | tf_op jit(solution)/shard_map/ppermute | solution.py:373
  13.9 8.1 %collective-permute-start.3 = (bf16[128,128]{1,0:T(8,128)(2,1)S(1)}, bf16[128,128]{1,0:T(8,128)(2,1)S(1)}, u32[]{:S(2)}, u32[]{:S(2)}) collective-permute-start(bf16[128,128]{1,0:T(8,128)(2,1)S(1)} %get-tuple-element.36), channel_id=1, source_target_pairs={{0,7},{1,6},{2,5},{3,4},{4,3},{5,2},{6,1},{7,0},{8,15},{9,14},{10,... | collective-permute-start | bytes 98312 | tf_op jit(solution)/shard_map/ppermute | solution.py:373
  14.8 8.7 %collective-permute-start.4 = (bf16[128,128]{1,0:T(8,128)(2,1)S(1)}, bf16[128,128]{1,0:T(8,128)(2,1)S(1)}, u32[]{:S(2)}, u32[]{:S(2)}) collective-permute-start(bf16[128,128]{1,0:T(8,128)(2,1)S(1)} %get-tuple-element.37), channel_id=1, source_target_pairs={{0,4},{1,5},{2,6},{3,7},{4,0},{5,1},{6,2},{7,3},{8,12},{9,13},{10,... | collective-permute-start | bytes 98312 | tf_op jit(solution)/shard_map/ppermute | solution.py:373
  15.4 8.2 %collective-permute-start.5 = (bf16[128,128]{1,0:T(8,128)(2,1)S(1)}, bf16[128,128]{1,0:T(8,128)(2,1)S(1)}, u32[]{:S(2)}, u32[]{:S(2)}) collective-permute-start(bf16[128,128]{1,0:T(8,128)(2,1)S(1)} %get-tuple-element.38), channel_id=1, source_target_pairs={{0,5},{1,4},{2,7},{3,6},{4,1},{5,0},{6,3},{7,2},{8,13},{9,12},{10,... | collective-permute-start | bytes 98312 | tf_op jit(solution)/shard_map/ppermute | solution.py:373
  18.3 5.2 %collective-permute-start.6 = (bf16[128,128]{1,0:T(8,128)(2,1)S(1)}, bf16[128,128]{1,0:T(8,128)(2,1)S(1)}, u32[]{:S(2)}, u32[]{:S(2)}) collective-permute-start(bf16[128,128]{1,0:T(8,128)(2,1)S(1)} %get-tuple-element.39), channel_id=1, source_target_pairs={{0,3},{1,2},{2,1},{3,0},{4,7},{5,6},{6,5},{7,4},{8,11},{9,10},{10,... | collective-permute-start | bytes 98312 | tf_op jit(solution)/shard_map/ppermute | solution.py:373
  43.4 17.3 %all-to-all-start.3 = ((bf16[16,128,128]{2,1,0:T(8,128)(2,1)}), bf16[16,128,128]{2,1,0:T(8,128)(2,1)S(1)}, u32[]{:S(2)}, u32[]{:S(2)}) async-start(bf16[16,128,128]{2,1,0:T(8,128)(2,1)} %get-tuple-element.42), calls=%async_computation.3 | async-start | bytes 1048576 | tf_op jit(solution)/shard_map/all_to_all | solution.py:356
  48.3 7.7 %copy-start.5 = (bf16[128,128]{1,0:T(8,128)(2,1)S(1)}, bf16[128,128]{1,0:T(8,128)(2,1)}, u32[]{:S(2)}) copy-start(bf16[128,128]{1,0:T(8,128)(2,1)} %refs_4_.8) | copy-start | bytes 98308
  48.6 4.5 %collective-permute-start.7 = (bf16[128,128]{1,0:T(8,128)(2,1)S(1)}, bf16[128,128]{1,0:T(8,128)(2,1)S(1)}, u32[]{:S(2)}, u32[]{:S(2)}) collective-permute-start(bf16[128,128]{1,0:T(8,128)(2,1)S(1)} %get-tuple-element.49), channel_id=1, source_target_pairs={{0,1},{1,0},{2,3},{3,2},{4,5},{5,4},{6,7},{7,6},{8,9},{9,8},{10,11... | collective-permute-start | bytes 98312 | tf_op jit(solution)/shard_map/ppermute | solution.py:373
  48.8 7.1 %collective-permute-start.8 = (bf16[128,128]{1,0:T(8,128)(2,1)S(1)}, bf16[128,128]{1,0:T(8,128)(2,1)S(1)}, u32[]{:S(2)}, u32[]{:S(2)}) collective-permute-start(bf16[128,128]{1,0:T(8,128)(2,1)S(1)} %get-tuple-element.50), channel_id=1, source_target_pairs={{0,2},{1,3},{2,0},{3,1},{4,6},{5,7},{6,4},{7,5},{8,10},{9,11},{10,... | collective-permute-start | bytes 98312 | tf_op jit(solution)/shard_map/ppermute | solution.py:373
  50.4 8.3 %collective-permute-start.9 = (bf16[128,128]{1,0:T(8,128)(2,1)S(1)}, bf16[128,128]{1,0:T(8,128)(2,1)S(1)}, u32[]{:S(2)}, u32[]{:S(2)}) collective-permute-start(bf16[128,128]{1,0:T(8,128)(2,1)S(1)} %get-tuple-element.51), channel_id=1, source_target_pairs={{0,6},{1,7},{2,4},{3,5},{4,2},{5,3},{6,0},{7,1},{8,14},{9,15},{10,... | collective-permute-start | bytes 98312 | tf_op jit(solution)/shard_map/ppermute | solution.py:373
  50.6 8.7 %collective-permute-start.10 = (bf16[128,128]{1,0:T(8,128)(2,1)S(1)}, bf16[128,128]{1,0:T(8,128)(2,1)S(1)}, u32[]{:S(2)}, u32[]{:S(2)}) collective-permute-start(bf16[128,128]{1,0:T(8,128)(2,1)S(1)} %get-tuple-element.52), channel_id=1, source_target_pairs={{0,7},{1,6},{2,5},{3,4},{4,3},{5,2},{6,1},{7,0},{8,15},{9,14},{10,... | collective-permute-start | bytes 98312 | tf_op jit(solution)/shard_map/ppermute | solution.py:373
  52.7 7.2 %collective-permute-start.11 = (bf16[128,128]{1,0:T(8,128)(2,1)S(1)}, bf16[128,128]{1,0:T(8,128)(2,1)S(1)}, u32[]{:S(2)}, u32[]{:S(2)}) collective-permute-start(bf16[128,128]{1,0:T(8,128)(2,1)S(1)} %get-tuple-element.53), channel_id=1, source_target_pairs={{0,4},{1,5},{2,6},{3,7},{4,0},{5,1},{6,2},{7,3},{8,12},{9,13},{10,... | collective-permute-start | bytes 98312 | tf_op jit(solution)/shard_map/ppermute | solution.py:373
  53.2 7.1 %collective-permute-start.12 = (bf16[128,128]{1,0:T(8,128)(2,1)S(1)}, bf16[128,128]{1,0:T(8,128)(2,1)S(1)}, u32[]{:S(2)}, u32[]{:S(2)}) collective-permute-start(bf16[128,128]{1,0:T(8,128)(2,1)S(1)} %get-tuple-element.54), channel_id=1, source_target_pairs={{0,5},{1,4},{2,7},{3,6},{4,1},{5,0},{6,3},{7,2},{8,13},{9,12},{10,... | collective-permute-start | bytes 98312 | tf_op jit(solution)/shard_map/ppermute | solution.py:373
  55.9 4.3 %collective-permute-start.13 = (bf16[128,128]{1,0:T(8,128)(2,1)S(1)}, bf16[128,128]{1,0:T(8,128)(2,1)S(1)}, u32[]{:S(2)}, u32[]{:S(2)}) collective-permute-start(bf16[128,128]{1,0:T(8,128)(2,1)S(1)} %get-tuple-element.55), channel_id=1, source_target_pairs={{0,3},{1,2},{2,1},{3,0},{4,7},{5,6},{6,5},{7,4},{8,11},{9,10},{10,... | collective-permute-start | bytes 98312 | tf_op jit(solution)/shard_map/ppermute | solution.py:373
  (5 other events, 16.8 us)

commit v35 on v34

--- a/solution.py
+++ b/solution.py
@@ -127,7 +127,7 @@
         normed, _ = norm_rows(jnp.transpose(pair[row].astype(F32)))
         zln = (normed * gain_col + bias_col).astype(BF16)
         proj = dot(w_flip, zln, 1, 0)
-        yield row, masks[row] * sigmoid(proj[:hidden]) * proj[hidden:]
+        yield row, masks[row] * proj[hidden:] / (1.0 + jnp.exp(-proj[:hidden]))
 
 
 def project_right_kernel(pair, mask, gain, bias, w_side, right_panel):

time: 62.5 us -> 62.5 us (level)
  no operation moved by 1% of the time
where the time goes in v35:
time: 62.5 us; the launch traced here: 62 us
  starting transfers between devices  24.7 us (40%)
  blocking collectives  17.3 us (28%)
  Pallas kernels  9.68 us (15%)
  waiting for transfers between devices  8.35 us (13%)
  local copies, waits for them, and re-layouts  1.64 us (3%)
    all_to_all x2, blocking collectives, swap_half(): lax.all_to_all(values, 'row', split_axis=0, concat_axis=0, tiled=True, ax...  17.3 us
    all_to_all x2, starting transfers between devices, swap(): lax.all_to_all(values, 'row', split_axis=0, concat_axis=0, tiled=True, ax...  13.4 us
    ppermute x14, starting transfers between devices, swap_pieces(): lax.ppermute(pieces[step], 'row', [(d, d ^ distance(step, count)) for d i...  11.3 us
    pallas_call x12, Pallas kernels, call(): pl.pallas_call(body, name=name, out_shape=outs, in_specs=[pl.BlockSpec(me...  9.68 us
    ppermute x14, waiting for transfers between devices, swap_pieces(): lax.ppermute(pieces[step], 'row', [(d, d ^ distance(step, count)) for d i...  8.24 us
    unnamed x26, local copies, waits for them, and re-layouts  1.64 us
  transfers between devices with their start and end apart: 16, of which 10 were waited for; matrix products, arithmetic and copies ran while one was open for 0% of the time, Pallas kernels for 6%

profile of v35, /device:TPU:0, one launch (start us, length us, event | category | flops | bytes accessed | tf_op | source)
XLA Modules:
  0.0 62.0 jit_solution(3852144652378103604)
XLA Ops:
  0.0 2.3 %project_right.1.refs_5_ = bf16[16,128,128]{2,1,0:T(8,128)(2,1)} custom-call(bf16[8,128,128]{2,1,0:T(8,128)(2,1)} %refs_0_.7, s32[1,128]{1,0:T(1,128)} %bitcast.13, f32[1,128]{1,0:T(1,128)} %bitcast.5, f32[1,128]{1,0:T(1,128)} %bitcast.9, bf16[128,512]{1,0:T(8,128)(2,1)} %refs_4_.9), custom_call_target="tpu_custom_call" | custom-call | flops 67108864 | bytes 919040 | tf_op jit(solution)/shard_map/project_right/pallas_call | solution.py:72
  2.4 8.5 %all-to-all-start = ((bf16[16,128,128]{2,1,0:T(8,128)(2,1)}), bf16[16,128,128]{2,1,0:T(8,128)(2,1)S(1)}, u32[]{:S(2)}, u32[]{:S(2)}) async-start(bf16[16,128,128]{2,1,0:T(8,128)(2,1)} %project_right.1.refs_5_), calls=%async_computation | async-start | bytes 1048576 | tf_op jit(solution)/shard_map/all_to_all | solution.py:356
  11.0 0.6 %project_left.1 = (bf16[128,128]{1,0:T(8,128)(2,1)S(1)}, bf16[128,128]{1,0:T(8,128)(2,1)S(1)}, bf16[128,128]{1,0:T(8,128)(2,1)S(1)}, bf16[128,128]{1,0:T(8,128)(...) custom-call(bf16[8,128,128]{2,1,0:T(8,128)(2,1)S(1)} %copy-done.1, ...), custom_call_target="tpu_custom_call" | custom-call | flops 67108864 | bytes 1181184 | tf_op jit(solution)/shard_map/project_left/pallas_call | solution.py:72
  12.5 1.4 %collective-permute-start.2 = (bf16[128,128]{1,0:T(8,128)(2,1)S(1)}, bf16[128,128]{1,0:T(8,128)(2,1)S(1)}, u32[]{:S(2)}, u32[]{:S(2)}) collective-permute-start(bf16[128,128]{1,0:T(8,128)(2,1)S(1)} %get-tuple-element.35), channel_id=1, source_target_pairs={{0,6},{1,7},{2,4},{3,5},{4,2},{5,3},{6,0},{7,1},{8,14},{9,15},{10,... | collective-permute-start | bytes 98312 | tf_op jit(solution)/shard_map/ppermute | solution.py:373
  13.8 0.9 %collective-permute-start.3 = (bf16[128,128]{1,0:T(8,128)(2,1)S(1)}, bf16[128,128]{1,0:T(8,128)(2,1)S(1)}, u32[]{:S(2)}, u32[]{:S(2)}) collective-permute-start(bf16[128,128]{1,0:T(8,128)(2,1)S(1)} %get-tuple-element.36), channel_id=1, source_target_pairs={{0,7},{1,6},{2,5},{3,4},{4,3},{5,2},{6,1},{7,0},{8,15},{9,14},{10,... | collective-permute-start | bytes 98312 | tf_op jit(solution)/shard_map/ppermute | solution.py:373
  15.4 1.5 %collective-permute-start.5 = (bf16[128,128]{1,0:T(8,128)(2,1)S(1)}, bf16[128,128]{1,0:T(8,128)(2,1)S(1)}, u32[]{:S(2)}, u32[]{:S(2)}) collective-permute-start(bf16[128,128]{1,0:T(8,128)(2,1)S(1)} %get-tuple-element.38), channel_id=1, source_target_pairs={{0,5},{1,4},{2,7},{3,6},{4,1},{5,0},{6,3},{7,2},{8,13},{9,12},{10,... | collective-permute-start | bytes 98312 | tf_op jit(solution)/shard_map/ppermute | solution.py:373
  16.9 1.5 %collective-permute-done.1.refs_2_ = bf16[128,128]{1,0:T(8,128)(2,1)S(1)} collective-permute-done((bf16[128,128]{1,0:T(8,128)(2,1)S(1)}, bf16[128,128]{1,0:T(8,128)(2,1)S(1)}, u32[]{:S(2)}, u32[]{:S(2)}) %collective-permute-start.1) | collective-permute-done | bytes 32800 | tf_op jit(solution)/shard_map/ppermute | solution.py:373
  19.0 0.8 %prepare.1 = (f32[8,128,128]{2,1,0:T(8,128)S(1)}, f32[8,128,128]{2,1,0:T(8,128)S(1)}) custom-call(bf16[8,128,128]{2,1,0:T(8,128)(2,1)S(1)} %copy-done.1, bf16[8,128,128]{2,1,0:T(8,128)(2,1)S(1)} %copy-done.3, f32[1,128]{1,0:T(1,128)S(1)} %bitcast.7, f32[1,128]{1,0:T(1,128)S(1)} %bitcast.11, bf16[128,128]{1,0:T(8,128)(2,1)S(1)} %copy-done.6, ...), custom_call_target="tpu_custom_call" | custom-call | flops 67108864 | bytes 1639936 | tf_op jit(solution)/shard_map/prepare/pallas_call | solution.py:72
  19.8 1.5 %collective-permute-done.2.refs_3_ = bf16[128,128]{1,0:T(8,128)(2,1)S(1)} collective-permute-done((bf16[128,128]{1,0:T(8,128)(2,1)S(1)}, bf16[128,128]{1,0:T(8,128)(2,1)S(1)}, u32[]{:S(2)}, u32[]{:S(2)}) %collective-permute-start.2) | collective-permute-done | bytes 32800 | tf_op jit(solution)/shard_map/ppermute | solution.py:373
  21.3 0.7 %collective-permute-done.3.refs_4_ = bf16[128,128]{1,0:T(8,128)(2,1)S(1)} collective-permute-done((bf16[128,128]{1,0:T(8,128)(2,1)S(1)}, bf16[128,128]{1,0:T(8,128)(2,1)S(1)}, u32[]{:S(2)}, u32[]{:S(2)}) %collective-permute-start.3) | collective-permute-done | bytes 32800 | tf_op jit(solution)/shard_map/ppermute | solution.py:373
  22.0 1.5 %collective-permute-done.4.refs_5_ = bf16[128,128]{1,0:T(8,128)(2,1)S(1)} collective-permute-done((bf16[128,128]{1,0:T(8,128)(2,1)S(1)}, bf16[128,128]{1,0:T(8,128)(2,1)S(1)}, u32[]{:S(2)}, u32[]{:S(2)}) %collective-permute-start.4) | collective-permute-done | bytes 32800 | tf_op jit(solution)/shard_map/ppermute | solution.py:373
  23.7 0.6 %tri.1 = (bf16[8,128,128]{2,1,0:T(8,128)(2,1)S(1)}, bf16[16,128,128]{2,1,0:T(8,128)(2,1)S(1)}) custom-call(bf16[16,128,128]{2,1,0:T(8,128)(2,1)S(1)} %all-to-all-done.refs_0_, bf16[8,128,256]{2,1,0:T(8,128)(2,1)S(1)} %sort_left.1.refs_1_, f32[8,128,128]{2,1,0:T(8,128)S(1)} %get-tuple-element.40.refs_2_.refs_1_), custom_call_target="tpu_custom_call" | custom-call | flops 33554432 | bytes 2359296 | tf_op jit(solution)/shard_map/tri/pallas_call | solution.py:72
  24.4 8.7 %all_to_all.20.refs_0_ = bf16[8,128,128]{2,1,0:T(8,128)(2,1)S(1)} all-to-all(bf16[8,128,128]{2,1,0:T(8,128)(2,1)S(1)} %get-tuple-element.41), channel_id=1, replica_groups={{0,1,2,3,4,5,6,7},{8,9,10,11,12,13,14,15},{16,17,18,19,20,21,22,23},{24..., dimensions={0} | all-to-all | bytes 524288 | tf_op jit(solution)/shard_map/all_to_all | solution.py:364
  33.4 8.6 %all_to_all.21.refs_0_ = bf16[8,128,128]{2,1,0:T(8,128)(2,1)S(1)} all-to-all(bf16[8,128,128]{2,1,0:T(8,128)(2,1)S(1)} %middle.1), channel_id=1, replica_groups={{0,1,2,3,4,5,6,7},{8,9,10,11,12,13,14,15},{16,17,18,19,20,21,22,23},{24..., dimensions={0} | all-to-all | bytes 524288 | tf_op jit(solution)/shard_map/all_to_all | solution.py:364
  42.0 1.4 %d_right.1 = (bf16[16,128,128]{2,1,0:T(8,128)(2,1)}, bf16[16,64,128]{2,1,0:T(8,128)(2,1)S(1)}) custom-call(bf16[8,128,128]{2,1,0:T(8,128)(2,1)S(1)} %all_to_all.21.refs_0_, bf16[8,128,256]{2,1,0:T(8,128)(2,1)S(1)} %sort_left.1.refs_1_), custom_call_target="tpu_custom_call" | custom-call | flops 33554432 | bytes 1572864 | tf_op jit(solution)/shard_map/d_right/pallas_call | solution.py:72
  43.4 4.9 %all-to-all-start.3 = ((bf16[16,128,128]{2,1,0:T(8,128)(2,1)}), bf16[16,128,128]{2,1,0:T(8,128)(2,1)S(1)}, u32[]{:S(2)}, u32[]{:S(2)}) async-start(bf16[16,128,128]{2,1,0:T(8,128)(2,1)} %get-tuple-element.42), calls=%async_computation.3 | async-start | bytes 1048576 | tf_op jit(solution)/shard_map/all_to_all | solution.py:356
  48.8 1.5 %collective-permute-start.8 = (bf16[128,128]{1,0:T(8,128)(2,1)S(1)}, bf16[128,128]{1,0:T(8,128)(2,1)S(1)}, u32[]{:S(2)}, u32[]{:S(2)}) collective-permute-start(bf16[128,128]{1,0:T(8,128)(2,1)S(1)} %get-tuple-element.50), channel_id=1, source_target_pairs={{0,2},{1,3},{2,0},{3,1},{4,6},{5,7},{6,4},{7,5},{8,10},{9,11},{10,... | collective-permute-start | bytes 98312 | tf_op jit(solution)/shard_map/ppermute | solution.py:373
  50.6 2.0 %collective-permute-start.10 = (bf16[128,128]{1,0:T(8,128)(2,1)S(1)}, bf16[128,128]{1,0:T(8,128)(2,1)S(1)}, u32[]{:S(2)}, u32[]{:S(2)}) collective-permute-start(bf16[128,128]{1,0:T(8,128)(2,1)S(1)} %get-tuple-element.52), channel_id=1, source_target_pairs={{0,7},{1,6},{2,5},{3,4},{4,3},{5,2},{6,1},{7,0},{8,15},{9,14},{10,... | collective-permute-start | bytes 98312 | tf_op jit(solution)/shard_map/ppermute | solution.py:373
  53.2 1.6 %collective-permute-start.12 = (bf16[128,128]{1,0:T(8,128)(2,1)S(1)}, bf16[128,128]{1,0:T(8,128)(2,1)S(1)}, u32[]{:S(2)}, u32[]{:S(2)}) collective-permute-start(bf16[128,128]{1,0:T(8,128)(2,1)S(1)} %get-tuple-element.54), channel_id=1, source_target_pairs={{0,5},{1,4},{2,7},{3,6},{4,1},{5,0},{6,3},{7,2},{8,13},{9,12},{10,... | collective-permute-start | bytes 98312 | tf_op jit(solution)/shard_map/ppermute | solution.py:373
  54.7 1.2 %collective-permute-done.8.refs_5_ = bf16[128,128]{1,0:T(8,128)(2,1)S(1)} collective-permute-done((bf16[128,128]{1,0:T(8,128)(2,1)S(1)}, bf16[128,128]{1,0:T(8,128)(2,1)S(1)}, u32[]{:S(2)}, u32[]{:S(2)}) %collective-permute-start.8) | collective-permute-done | bytes 32800 | tf_op jit(solution)/shard_map/ppermute | solution.py:373
  55.9 0.6 %copy-done.12 = f32[128]{0:T(128)S(1)} copy-done((f32[128]{0:T(128)S(1)}, f32[128]{0:T(128)}, u32[]{:S(2)}) %copy-start.12) | copy-done | bytes 536
  57.3 1.0 %slopes.1 = (bf16[8,512,128]{2,1,0:T(8,128)(2,1)S(1)}, bf16[8,128,128]{2,1,0:T(8,128)(2,1)S(1)}, f32[8,128]{1,0:T(8,128)S(1)}, f32[128,128]{1,0:T(8,128)S(1)}, bf16[128,640]{1,0:T(8,128)(2,1)S(1)}) custom-call(bf16[8,128,128]{2,1,0:T(8,128)(2,1)S(1)} %copy-done.1, s32[1,128]{1,0:T(1,128)S(1)} %bitcast.15, f32[1,128]{1,0:T(1,128)S(1)} %bitcast.8, ...), custom_call_target="tpu_custom_call" | custom-call | flops 134217728 | bytes 2233856 | tf_op jit(solution)/shard_map/slopes/pallas_call | solution.py:72
  58.6 0.7 %collective-permute-done.10.refs_7_ = bf16[128,128]{1,0:T(8,128)(2,1)S(1)} collective-permute-done((bf16[128,128]{1,0:T(8,128)(2,1)S(1)}, bf16[128,128]{1,0:T(8,128)(2,1)S(1)}, u32[]{:S(2)}, u32[]{:S(2)}) %collective-permute-start.10) | collective-permute-done | bytes 32800 | tf_op jit(solution)/shard_map/ppermute | solution.py:373
  60.7 1.2 %finish.1 = bf16[8,128,128]{2,1,0:T(8,128)(2,1)} custom-call(bf16[16,128,128]{2,1,0:T(8,128)(2,1)S(1)} %all-to-all-done.3.refs_0_, f32[8,128,128]{2,1,0:T(8,128)S(1)} %finish_left.1.refs_1_, bf16[8,512,128]{2,1,0:T(8,128)(2,1)S(1)} %get-tuple-element.44.refs_0_.refs_2_, bf16[8,128,128]{2,1,0:T(8,128)(2,1)S(1)} %get-tuple-element.56.refs_3_, ...), custom_call_target="tpu_custom_call" | custom-call | flops 134217728 | bytes 2854912 | tf_op jit(solution)/shard_map/finish/pallas_call | solution.py:72
  (48 shorter events, 6.3 us)
Async XLA Ops:
  2.3 8.6 %copy-start = (bf16[16,128,128]{2,1,0:T(8,128)(2,1)S(1)}, bf16[16,128,128]{2,1,0:T(8,128)(2,1)}, u32[]{:S(2)}) copy-start(bf16[16,128,128]{2,1,0:T(8,128)(2,1)} %project_right.1.refs_5_) | copy-start | bytes 1572868
  2.3 8.6 %copy-start.1 = (bf16[8,128,128]{2,1,0:T(8,128)(2,1)S(1)}, bf16[8,128,128]{2,1,0:T(8,128)(2,1)}, u32[]{:S(2)}) copy-start(bf16[8,128,128]{2,1,0:T(8,128)(2,1)} %refs_0_.7) | copy-start | bytes 786436
  2.3 8.6 %copy-start.2 = (bf16[128,512]{1,0:T(8,128)(2,1)S(1)}, bf16[128,512]{1,0:T(8,128)(2,1)}, u32[]{:S(2)}) copy-start(bf16[128,512]{1,0:T(8,128)(2,1)} %refs_4_.9) | copy-start | bytes 393220
  2.4 8.6 %copy-start.8 = (f32[128]{0:T(128)S(1)}, f32[128]{0:T(128)}, u32[]{:S(2)}) copy-start(f32[128]{0:T(128)} %param.13) | copy-start | bytes 1540
  2.4 8.6 %copy-start.9 = (f32[128]{0:T(128)S(1)}, f32[128]{0:T(128)}, u32[]{:S(2)}) copy-start(f32[128]{0:T(128)} %param.14) | copy-start | bytes 1540
  2.4 8.6 %copy-start.10 = (s32[128]{0:T(128)S(1)}, s32[128]{0:T(128)}, u32[]{:S(2)}) copy-start(s32[128]{0:T(128)} %param.12) | copy-start | bytes 1540
  2.4 21.3 %all-to-all-start = ((bf16[16,128,128]{2,1,0:T(8,128)(2,1)}), bf16[16,128,128]{2,1,0:T(8,128)(2,1)S(1)}, u32[]{:S(2)}, u32[]{:S(2)}) async-start(bf16[16,128,128]{2,1,0:T(8,128)(2,1)} %project_right.1.refs_5_), calls=%async_computation | async-start | bytes 1048576 | tf_op jit(solution)/shard_map/all_to_all | solution.py:356
  11.0 7.4 %copy-start.3 = (bf16[8,128,128]{2,1,0:T(8,128)(2,1)S(1)}, bf16[8,128,128]{2,1,0:T(8,128)(2,1)}, u32[]{:S(2)}) copy-start(bf16[8,128,128]{2,1,0:T(8,128)(2,1)} %refs_1_.1) | copy-start | bytes 786436
  11.7 3.7 %collective-permute-start = (bf16[128,128]{1,0:T(8,128)(2,1)S(1)}, bf16[128,128]{1,0:T(8,128)(2,1)S(1)}, u32[]{:S(2)}, u32[]{:S(2)}) collective-permute-start(bf16[128,128]{1,0:T(8,128)(2,1)S(1)} %get-tuple-element.33), channel_id=1, source_target_pairs={{0,1},{1,0},{2,3},{3,2},{4,5},{5,4},{6,7},{7,6},{8,9},{9,8},{10,11... | collective-permute-start | bytes 98312 | tf_op jit(solution)/shard_map/ppermute | solution.py:373
  11.9 6.5 %collective-permute-start.1 = (bf16[128,128]{1,0:T(8,128)(2,1)S(1)}, bf16[128,128]{1,0:T(8,128)(2,1)S(1)}, u32[]{:S(2)}, u32[]{:S(2)}) collective-permute-start(bf16[128,128]{1,0:T(8,128)(2,1)S(1)} %get-tuple-element.34), channel_id=1, source_target_pairs={{0,2},{1,3},{2,0},{3,1},{4,6},{5,7},{6,4},{7,5},{8,10},{9,11},{10,... | collective-permute-start | bytes 98312 | tf_op jit(solution)/shard_map/ppermute | solution.py:373
  12.5 8.8 %collective-permute-start.2 = (bf16[128,128]{1,0:T(8,128)(2,1)S(1)}, bf16[128,128]{1,0:T(8,128)(2,1)S(1)}, u32[]{:S(2)}, u32[]{:S(2)}) collective-permute-start(bf16[128,128]{1,0:T(8,128)(2,1)S(1)} %get-tuple-element.35), channel_id=1, source_target_pairs={{0,6},{1,7},{2,4},{3,5},{4,2},{5,3},{6,0},{7,1},{8,14},{9,15},{10,... | collective-permute-start | bytes 98312 | tf_op jit(solution)/shard_map/ppermute | solution.py:373
  13.8 8.1 %collective-permute-start.3 = (bf16[128,128]{1,0:T(8,128)(2,1)S(1)}, bf16[128,128]{1,0:T(8,128)(2,1)S(1)}, u32[]{:S(2)}, u32[]{:S(2)}) collective-permute-start(bf16[128,128]{1,0:T(8,128)(2,1)S(1)} %get-tuple-element.36), channel_id=1, source_target_pairs={{0,7},{1,6},{2,5},{3,4},{4,3},{5,2},{6,1},{7,0},{8,15},{9,14},{10,... | collective-permute-start | bytes 98312 | tf_op jit(solution)/shard_map/ppermute | solution.py:373
  14.8 8.7 %collective-permute-start.4 = (bf16[128,128]{1,0:T(8,128)(2,1)S(1)}, bf16[128,128]{1,0:T(8,128)(2,1)S(1)}, u32[]{:S(2)}, u32[]{:S(2)}) collective-permute-start(bf16[128,128]{1,0:T(8,128)(2,1)S(1)} %get-tuple-element.37), channel_id=1, source_target_pairs={{0,4},{1,5},{2,6},{3,7},{4,0},{5,1},{6,2},{7,3},{8,12},{9,13},{10,... | collective-permute-start | bytes 98312 | tf_op jit(solution)/shard_map/ppermute | solution.py:373
  15.4 8.2 %collective-permute-start.5 = (bf16[128,128]{1,0:T(8,128)(2,1)S(1)}, bf16[128,128]{1,0:T(8,128)(2,1)S(1)}, u32[]{:S(2)}, u32[]{:S(2)}) collective-permute-start(bf16[128,128]{1,0:T(8,128)(2,1)S(1)} %get-tuple-element.38), channel_id=1, source_target_pairs={{0,5},{1,4},{2,7},{3,6},{4,1},{5,0},{6,3},{7,2},{8,13},{9,12},{10,... | collective-permute-start | bytes 98312 | tf_op jit(solution)/shard_map/ppermute | solution.py:373
  18.3 5.2 %collective-permute-start.6 = (bf16[128,128]{1,0:T(8,128)(2,1)S(1)}, bf16[128,128]{1,0:T(8,128)(2,1)S(1)}, u32[]{:S(2)}, u32[]{:S(2)}) collective-permute-start(bf16[128,128]{1,0:T(8,128)(2,1)S(1)} %get-tuple-element.39), channel_id=1, source_target_pairs={{0,3},{1,2},{2,1},{3,0},{4,7},{5,6},{6,5},{7,4},{8,11},{9,10},{10,... | collective-permute-start | bytes 98312 | tf_op jit(solution)/shard_map/ppermute | solution.py:373
  43.4 17.3 %all-to-all-start.3 = ((bf16[16,128,128]{2,1,0:T(8,128)(2,1)}), bf16[16,128,128]{2,1,0:T(8,128)(2,1)S(1)}, u32[]{:S(2)}, u32[]{:S(2)}) async-start(bf16[16,128,128]{2,1,0:T(8,128)(2,1)} %get-tuple-element.42), calls=%async_computation.3 | async-start | bytes 1048576 | tf_op jit(solution)/shard_map/all_to_all | solution.py:356
  48.3 7.7 %copy-start.5 = (bf16[128,128]{1,0:T(8,128)(2,1)S(1)}, bf16[128,128]{1,0:T(8,128)(2,1)}, u32[]{:S(2)}) copy-start(bf16[128,128]{1,0:T(8,128)(2,1)} %refs_4_.8) | copy-start | bytes 98308
  48.6 4.5 %collective-permute-start.7 = (bf16[128,128]{1,0:T(8,128)(2,1)S(1)}, bf16[128,128]{1,0:T(8,128)(2,1)S(1)}, u32[]{:S(2)}, u32[]{:S(2)}) collective-permute-start(bf16[128,128]{1,0:T(8,128)(2,1)S(1)} %get-tuple-element.49), channel_id=1, source_target_pairs={{0,1},{1,0},{2,3},{3,2},{4,5},{5,4},{6,7},{7,6},{8,9},{9,8},{10,11... | collective-permute-start | bytes 98312 | tf_op jit(solution)/shard_map/ppermute | solution.py:373
  48.8 7.1 %collective-permute-start.8 = (bf16[128,128]{1,0:T(8,128)(2,1)S(1)}, bf16[128,128]{1,0:T(8,128)(2,1)S(1)}, u32[]{:S(2)}, u32[]{:S(2)}) collective-permute-start(bf16[128,128]{1,0:T(8,128)(2,1)S(1)} %get-tuple-element.50), channel_id=1, source_target_pairs={{0,2},{1,3},{2,0},{3,1},{4,6},{5,7},{6,4},{7,5},{8,10},{9,11},{10,... | collective-permute-start | bytes 98312 | tf_op jit(solution)/shard_map/ppermute | solution.py:373
  50.4 8.3 %collective-permute-start.9 = (bf16[128,128]{1,0:T(8,128)(2,1)S(1)}, bf16[128,128]{1,0:T(8,128)(2,1)S(1)}, u32[]{:S(2)}, u32[]{:S(2)}) collective-permute-start(bf16[128,128]{1,0:T(8,128)(2,1)S(1)} %get-tuple-element.51), channel_id=1, source_target_pairs={{0,6},{1,7},{2,4},{3,5},{4,2},{5,3},{6,0},{7,1},{8,14},{9,15},{10,... | collective-permute-start | bytes 98312 | tf_op jit(solution)/shard_map/ppermute | solution.py:373
  50.6 8.7 %collective-permute-start.10 = (bf16[128,128]{1,0:T(8,128)(2,1)S(1)}, bf16[128,128]{1,0:T(8,128)(2,1)S(1)}, u32[]{:S(2)}, u32[]{:S(2)}) collective-permute-start(bf16[128,128]{1,0:T(8,128)(2,1)S(1)} %get-tuple-element.52), channel_id=1, source_target_pairs={{0,7},{1,6},{2,5},{3,4},{4,3},{5,2},{6,1},{7,0},{8,15},{9,14},{10,... | collective-permute-start | bytes 98312 | tf_op jit(solution)/shard_map/ppermute | solution.py:373
  52.7 7.2 %collective-permute-start.11 = (bf16[128,128]{1,0:T(8,128)(2,1)S(1)}, bf16[128,128]{1,0:T(8,128)(2,1)S(1)}, u32[]{:S(2)}, u32[]{:S(2)}) collective-permute-start(bf16[128,128]{1,0:T(8,128)(2,1)S(1)} %get-tuple-element.53), channel_id=1, source_target_pairs={{0,4},{1,5},{2,6},{3,7},{4,0},{5,1},{6,2},{7,3},{8,12},{9,13},{10,... | collective-permute-start | bytes 98312 | tf_op jit(solution)/shard_map/ppermute | solution.py:373
  53.2 7.1 %collective-permute-start.12 = (bf16[128,128]{1,0:T(8,128)(2,1)S(1)}, bf16[128,128]{1,0:T(8,128)(2,1)S(1)}, u32[]{:S(2)}, u32[]{:S(2)}) collective-permute-start(bf16[128,128]{1,0:T(8,128)(2,1)S(1)} %get-tuple-element.54), channel_id=1, source_target_pairs={{0,5},{1,4},{2,7},{3,6},{4,1},{5,0},{6,3},{7,2},{8,13},{9,12},{10,... | collective-permute-start | bytes 98312 | tf_op jit(solution)/shard_map/ppermute | solution.py:373
  55.9 4.3 %collective-permute-start.13 = (bf16[128,128]{1,0:T(8,128)(2,1)S(1)}, bf16[128,128]{1,0:T(8,128)(2,1)S(1)}, u32[]{:S(2)}, u32[]{:S(2)}) collective-permute-start(bf16[128,128]{1,0:T(8,128)(2,1)S(1)} %get-tuple-element.55), channel_id=1, source_target_pairs={{0,3},{1,2},{2,1},{3,0},{4,7},{5,6},{6,5},{7,4},{8,11},{9,10},{10,... | collective-permute-start | bytes 98312 | tf_op jit(solution)/shard_map/ppermute | solution.py:373
  (5 other events, 16.8 us)
